TPU v7x, 32 devices: a whole 2x2x4 slice. The times are simulated.
32 devices in a mesh: wide: 8 (over z, x), narrow: 4 (over y, core).
Axes of the slice: x: 2, y: 2, z: 4, core: 2. Of those that a mesh axis runs over, the one named last changes fastest.
Arguments:
- image_feats: bfloat16 [1536, 1152], P(('wide', 'narrow')), may hold values from -400 to 400
- proj_weight: bfloat16 [1152, 1152], replicated, may hold values from -0.1875 to 0.1875
- text_embed: bfloat16 [1536, 1152], P(('wide', 'narrow')), may hold values from -400 to 400
- log_scale: float32 [1], replicated, may hold values from 1.6 to 2.4
- logit_bias: float32 [1], replicated, may hold values from -7 to -4
Outputs:
- image_loss: float32 [1536], P(('wide', 'narrow'))
- d_text_unit: float32 [1536, 1152], P(('wide', 'narrow'))
- d_proj: float32 [1152, 1152], P('wide', 'narrow')
All inputs are finite; a program needn't handle non-finite values.
Results may differ from a plain program's by a relative error of at most 0.0037.
Values may be sent and summed in bfloat16 or wider, within the bound.
No kernel may reach another device: no remote copies, remote signals or barrier semaphores. Data moves between devices by JAX's collectives and lax.ppermute only.
A program may use at most 64 MiB of HBM per device.

v0:
```python
import jax
import jax.numpy as jnp
from jax import lax
from jax.sharding import PartitionSpec as P


def passed_along(value, axis, steps):
    count = lax.axis_size(axis)
    pairs = [(source, (source + steps) % count) for source in range(count)]
    return lax.ppermute(value, axis, pairs)


def unit_rows(values):
    inverse = lax.rsqrt(jnp.sum(values * values, axis=1, keepdims=True) + 1e-06)
    return (values * inverse, inverse)


def pair_terms(group_img, captions, own_pair, logit_scale, logit_shift):
    products = lax.dot_general(
        group_img, captions, (((1,), (1,)), ((), ())), preferred_element_type=jnp.float32
    )
    logits = logit_scale * products + logit_shift
    label_sign = jnp.where(own_pair, 1.0, -1.0).astype(jnp.float32)
    loss_rows = jnp.sum(jax.nn.softplus(-label_sign * logits), axis=1)
    grad_tile = (-logit_scale * label_sign * jax.nn.sigmoid(-label_sign * logits)).astype(
        jnp.bfloat16
    )
    return (loss_rows, grad_tile)


def transposed_product(grad_tile, group_img):
    return lax.dot_general(
        grad_tile, group_img, (((0,), (0,)), ((), ())), preferred_element_type=jnp.float32
    )


def local(image_feats, proj_weight, text_embed, log_scale, logit_bias):
    row_count = image_feats.shape[0]
    width = image_feats.shape[1]
    wide_count = lax.axis_size("wide")
    narrow_pos = lax.axis_index("narrow")
    zproj = jnp.dot(image_feats, proj_weight, preferred_element_type=jnp.float32)
    img_unit, img_inv = unit_rows(zproj)
    group_img = lax.all_gather(img_unit.astype(jnp.bfloat16), "narrow", axis=0, tiled=True)
    group_rows = group_img.shape[0]
    txt_unit, txt_inv = unit_rows(text_embed.astype(jnp.float32))
    txt_emb = txt_unit.astype(jnp.bfloat16)
    logit_scale = jnp.exp(log_scale[0])
    logit_shift = logit_bias[0]
    image_idx = lax.broadcasted_iota(jnp.int32, (group_rows, row_count), 0)
    caption_idx = lax.broadcasted_iota(jnp.int32, (group_rows, row_count), 1)
    diagonal = image_idx == narrow_pos * row_count + caption_idx

    def cycle_step(cycle_pos, state):
        caption_block, caption_grad, d_img, loss_total = state
        own_pair = jnp.logical_and(diagonal, cycle_pos == 0)
        loss_rows, grad_tile = pair_terms(
            group_img, caption_block, own_pair, logit_scale, logit_shift
        )
        d_img = d_img + jnp.dot(grad_tile, caption_block, preferred_element_type=jnp.float32)
        caption_grad = caption_grad + transposed_product(grad_tile, group_img)
        caption_block = passed_along(caption_block, "wide", 1)
        caption_grad = passed_along(caption_grad, "wide", 1)
        return (caption_block, caption_grad, d_img, loss_total + loss_rows)

    start_state = (
        txt_emb,
        jnp.zeros((row_count, width), jnp.float32),
        jnp.zeros((group_rows, width), jnp.float32),
        jnp.zeros((group_rows,), jnp.float32),
    )
    caption_block, caption_grad, d_img, loss_total = lax.fori_loop(
        0, wide_count - 1, cycle_step, start_state
    )
    last_pair = jnp.logical_and(diagonal, wide_count == 1)
    loss_rows, grad_tile = pair_terms(group_img, caption_block, last_pair, logit_scale, logit_shift)
    d_img = d_img + jnp.dot(grad_tile, caption_block, preferred_element_type=jnp.float32)
    caption_grad = caption_grad + transposed_product(grad_tile, group_img)
    loss_total = loss_total + loss_rows
    d_text_unit = passed_along(caption_grad, "wide", 1)
    img_grad, image_loss = (
        lax.psum_scatter(d_img, "narrow", scatter_dimension=0, tiled=True),
        lax.psum_scatter(loss_total, "narrow", scatter_dimension=0, tiled=True),
    )
    d_zproj = (
        img_inv * (img_grad - img_unit * jnp.sum(img_unit * img_grad, axis=1, keepdims=True))
    ).astype(jnp.bfloat16)
    shard_rows = lax.psum_scatter(
        transposed_product(image_feats, d_zproj), "wide", scatter_dimension=0, tiled=True
    )
    d_proj = lax.psum_scatter(shard_rows, "narrow", scatter_dimension=1, tiled=True)
    return (image_loss, d_text_unit, d_proj)


def solution(mesh):
    placed = (P(("wide", "narrow"), None), P(), P(("wide", "narrow"), None), P(), P())
    return jax.shard_map(
        local,
        mesh=mesh,
        in_specs=placed,
        out_specs=(P(("wide", "narrow")), P(("wide", "narrow"), None), P("wide", "narrow")),
        check_vma=False,
    )
```

profile of v0, /device:TPU:0, one launch (start us, length us, event | category | flops | bytes accessed | tf_op | source)
XLA Modules:
  0.0 308.8 jit_solution(1010229776399320710)
XLA Ops:
  13.8 8.7 %all_gather.3 = bf16[192,1152]{1,0:T(8,128)(2,1)} all-gather(bf16[48,1152]{1,0:T(8,128)(2,1)S(1)} %multiply_convert_fusion.1), channel_id=1, replica_groups=mesh['wide'=8,'narrow'=4] {'narrow'}, dimensions={0}, use_global_device_ids=true | all-gather | bytes 552960 | tf_op jit(solution)/shard_map/all_gather | solution.py:44
  23.2 105.3 %while.21 = (s32[]{:T(128)}, bf16[48,1152]{1,0:T(8,128)(2,1)}, f32[48,1152]{1,0:T(8,128)}, f32[192,1152]{1,0:T(8,128)S(1)}, f32[192]{0:T(256)S(1)}, /*index=5*/f...) while((s32[]{:T(128)}, bf16[48,1152]{1,0:T(8,128)(2,1)}, ...), condition=%wide.region_4.5_spmd.clone, body=%wide.region_2.4_spmd.clone.sunk | while | flops 64493760 | bytes 4980514 | solution.py:72
  28.2 2.0 convolution_add_fusion.6
  33.3 7.3 %collective-permute-done.1 = f32[48,1152]{1,0:T(8,128)} collective-permute-done((f32[48,1152]{1,0:T(8,128)}, f32[48,1152]{1,0:T(8,128)}, u32[]{:S(2)}, u32[]{:S(2)}) %collective-permute-start.1) | collective-permute-done | bytes 221216 | tf_op jit(solution)/shard_map/while/body/eval_jaxpr/ppermute | solution.py:10
  49.9 5.9 %collective-permute-done.1 = f32[48,1152]{1,0:T(8,128)} collective-permute-done((f32[48,1152]{1,0:T(8,128)}, f32[48,1152]{1,0:T(8,128)}, u32[]{:S(2)}, u32[]{:S(2)}) %collective-permute-start.1) | collective-permute-done | bytes 221216 | tf_op jit(solution)/shard_map/while/body/eval_jaxpr/ppermute | solution.py:10
  62.9 2.2 collective-permute-done
  65.1 5.2 %collective-permute-done.1 = f32[48,1152]{1,0:T(8,128)} collective-permute-done((f32[48,1152]{1,0:T(8,128)}, f32[48,1152]{1,0:T(8,128)}, u32[]{:S(2)}, u32[]{:S(2)}) %collective-permute-start.1) | collective-permute-done | bytes 221216 | tf_op jit(solution)/shard_map/while/body/eval_jaxpr/ppermute | solution.py:10
  77.4 3.1 %collective-permute-done = bf16[48,1152]{1,0:T(8,128)(2,1)} collective-permute-done((bf16[48,1152]{1,0:T(8,128)(2,1)}, bf16[48,1152]{1,0:T(8,128)(2,1)}, u32[]{:S(2)}, u32[]{:S(2)}) %collective-permute-start) | collective-permute-done | bytes 110624 | tf_op jit(solution)/shard_map/while/body/eval_jaxpr/ppermute | solution.py:10
  80.6 4.3 %collective-permute-done.1 = f32[48,1152]{1,0:T(8,128)} collective-permute-done((f32[48,1152]{1,0:T(8,128)}, f32[48,1152]{1,0:T(8,128)}, u32[]{:S(2)}, u32[]{:S(2)}) %collective-permute-start.1) | collective-permute-done | bytes 221216 | tf_op jit(solution)/shard_map/while/body/eval_jaxpr/ppermute | solution.py:10
  92.0 3.3 %collective-permute-done = bf16[48,1152]{1,0:T(8,128)(2,1)} collective-permute-done((bf16[48,1152]{1,0:T(8,128)(2,1)}, bf16[48,1152]{1,0:T(8,128)(2,1)}, u32[]{:S(2)}, u32[]{:S(2)}) %collective-permute-start) | collective-permute-done | bytes 110624 | tf_op jit(solution)/shard_map/while/body/eval_jaxpr/ppermute | solution.py:10
  95.3 4.1 %collective-permute-done.1 = f32[48,1152]{1,0:T(8,128)} collective-permute-done((f32[48,1152]{1,0:T(8,128)}, f32[48,1152]{1,0:T(8,128)}, u32[]{:S(2)}, u32[]{:S(2)}) %collective-permute-start.1) | collective-permute-done | bytes 221216 | tf_op jit(solution)/shard_map/while/body/eval_jaxpr/ppermute | solution.py:10
  102.9 2.0 convolution_add_fusion.6
  106.5 3.3 %collective-permute-done = bf16[48,1152]{1,0:T(8,128)(2,1)} collective-permute-done((bf16[48,1152]{1,0:T(8,128)(2,1)}, bf16[48,1152]{1,0:T(8,128)(2,1)}, u32[]{:S(2)}, u32[]{:S(2)}) %collective-permute-start) | collective-permute-done | bytes 110624 | tf_op jit(solution)/shard_map/while/body/eval_jaxpr/ppermute | solution.py:10
  109.8 4.1 %collective-permute-done.1 = f32[48,1152]{1,0:T(8,128)} collective-permute-done((f32[48,1152]{1,0:T(8,128)}, f32[48,1152]{1,0:T(8,128)}, u32[]{:S(2)}, u32[]{:S(2)}) %collective-permute-start.1) | collective-permute-done | bytes 221216 | tf_op jit(solution)/shard_map/while/body/eval_jaxpr/ppermute | solution.py:10
  121.0 3.3 %collective-permute-done = bf16[48,1152]{1,0:T(8,128)(2,1)} collective-permute-done((bf16[48,1152]{1,0:T(8,128)(2,1)}, bf16[48,1152]{1,0:T(8,128)(2,1)}, u32[]{:S(2)}, u32[]{:S(2)}) %collective-permute-start) | collective-permute-done | bytes 110624 | tf_op jit(solution)/shard_map/while/body/eval_jaxpr/ppermute | solution.py:10
  124.4 4.1 %collective-permute-done.1 = f32[48,1152]{1,0:T(8,128)} collective-permute-done((f32[48,1152]{1,0:T(8,128)}, f32[48,1152]{1,0:T(8,128)}, u32[]{:S(2)}, u32[]{:S(2)}) %collective-permute-start.1) | collective-permute-done | bytes 221216 | tf_op jit(solution)/shard_map/while/body/eval_jaxpr/ppermute | solution.py:10
  130.4 2.1 convolution_add_fusion.2
  132.6 22.3 %reduce-scatter.6.cloned.1.call-done = f32[48,1152]{1,0:T(8,128)} async-done(((f32[192,1152]{1,0:T(8,128)}), f32[48,1152]{1,0:T(8,128)}) %reduce-scatter.6.cloned.1.call-update) | async-done | bytes 221200 | tf_op jit(solution)/shard_map/reduce_scatter | solution.py:82
  156.2 4.4 %convolution_bitcast_fusion = f32[1152,1152]{0,1:T(8,128)} fusion(bf16[48,1152]{1,0:T(8,128)(2,1)} %param.7, f32[48,1152]{1,0:T(8,128)} %reduce-scatter.6.cloned.1.call-done, f32[48,1152]{1,0:T(8,128)} %copy-done.2, f32[48]{0:T(128)S(1)} %multiply_reduce_fusion, f32[48]{0:T(128)S(1)} %add_rsqrt_fusion), kind=kOutput, calls=%fused_computation.15 | convolution fusion | flops 127678464 | bytes 5861760 | tf_op jit(solution)/shard_map/dot_general | solution.py:32
  160.6 6.8 %copy.10 = f32[1152,1152]{1,0:T(8,128)} copy(f32[1152,1152]{0,1:T(8,128)} %convolution_bitcast_fusion) | data formatting | bytes 10616832
  167.5 104.2 %reduce-scatter.10.cloned.1.call-done = f32[144,1152]{1,0:T(8,128)} async-done(((f32[1152,1152]{1,0:T(8,128)}), f32[144,1152]{1,0:T(8,128)}) %reduce-scatter.10.cloned.1.call-update) | async-done | bytes 663568
  271.7 2.5 copy.11
  278.2 6.4 %all-reduce = f32[192]{0:T(256)S(1)} all-reduce(f32[192]{0:T(256)S(1)} %add.134), channel_id=2, replica_groups=mesh['wide'=8,'narrow'=4] {'narrow'}, use_global_device_ids=true, to_apply=%region_6.7.clone | all-reduce | flops 192 | bytes 1536
  285.2 14.7 %reduce-scatter.8.cloned.1.call-done = f32[144,288]{0,1:T(8,128)} async-done(((f32[144,1152]{0,1:T(8,128)}), f32[144,288]{0,1:T(8,128)}) %reduce-scatter.8.cloned.1.call-update) | async-done | bytes 165904 | tf_op jit(solution)/shard_map/reduce_scatter | solution.py:91
  (87 shorter events, 66.3 us)
Async XLA Ops:
  7.2 4.3 %copy-start = (bf16[1152,1152]{1,0:T(8,128)(2,1)S(1)}, bf16[1152,1152]{1,0:T(8,128)(2,1)}, u32[]{:S(2)}) copy-start(bf16[1152,1152]{1,0:T(8,128)(2,1)} %param.8) | copy-start | bytes 7962628
  7.2 147.7 %reduce-scatter.6.cloned.1.call-start = ((), (), s32[]{:S(2)}) async-start(), calls=%async_computation.3 | async-start | bytes 1105920 | tf_op jit(solution)/shard_map/reduce_scatter | solution.py:82
  13.0 0.7 copy-start.2
  24.7 8.6 %collective-permute-start = (bf16[48,1152]{1,0:T(8,128)(2,1)}, bf16[48,1152]{1,0:T(8,128)(2,1)}, u32[]{:S(2)}, u32[]{:S(2)}) collective-permute-start(bf16[48,1152]{1,0:T(8,128)(2,1)} %copy.18), channel_id=1, source_target_pairs={{0,4},{4,8},{8,12},{12,16},{16,20},{20,24},{24,28},{28,0},{1,5},{5... | collective-permute-start | bytes 331784 | tf_op jit(solution)/shard_map/while/body/eval_jaxpr/ppermute | solution.py:10
  30.2 10.4 %collective-permute-start.1 = (f32[48,1152]{1,0:T(8,128)}, f32[48,1152]{1,0:T(8,128)}, u32[]{:S(2)}, u32[]{:S(2)}) collective-permute-start(f32[48,1152]{1,0:T(8,128)} %convolution_add_fusion.6), channel_id=1, source_target_pairs={{0,4},{4,8},{8,12},{12,16},{16,20},{20,24},{24,28},{28,0},{1,5},{5... | collective-permute-start | bytes 663560 | tf_op jit(solution)/shard_map/while/body/eval_jaxpr/ppermute | solution.py:10
  42.2 7.8 %collective-permute-start = (bf16[48,1152]{1,0:T(8,128)(2,1)}, bf16[48,1152]{1,0:T(8,128)(2,1)}, u32[]{:S(2)}, u32[]{:S(2)}) collective-permute-start(bf16[48,1152]{1,0:T(8,128)(2,1)} %copy.18), channel_id=1, source_target_pairs={{0,4},{4,8},{8,12},{12,16},{16,20},{20,24},{24,28},{28,0},{1,5},{5... | collective-permute-start | bytes 331784 | tf_op jit(solution)/shard_map/while/body/eval_jaxpr/ppermute | solution.py:10
  46.2 9.6 %collective-permute-start.1 = (f32[48,1152]{1,0:T(8,128)}, f32[48,1152]{1,0:T(8,128)}, u32[]{:S(2)}, u32[]{:S(2)}) collective-permute-start(f32[48,1152]{1,0:T(8,128)} %convolution_add_fusion.6), channel_id=1, source_target_pairs={{0,4},{4,8},{8,12},{12,16},{16,20},{20,24},{24,28},{28,0},{1,5},{5... | collective-permute-start | bytes 663560 | tf_op jit(solution)/shard_map/while/body/eval_jaxpr/ppermute | solution.py:10
  57.3 7.8 %collective-permute-start = (bf16[48,1152]{1,0:T(8,128)(2,1)}, bf16[48,1152]{1,0:T(8,128)(2,1)}, u32[]{:S(2)}, u32[]{:S(2)}) collective-permute-start(bf16[48,1152]{1,0:T(8,128)(2,1)} %copy.18), channel_id=1, source_target_pairs={{0,4},{4,8},{8,12},{12,16},{16,20},{20,24},{24,28},{28,0},{1,5},{5... | collective-permute-start | bytes 331784 | tf_op jit(solution)/shard_map/while/body/eval_jaxpr/ppermute | solution.py:10
  61.4 8.9 %collective-permute-start.1 = (f32[48,1152]{1,0:T(8,128)}, f32[48,1152]{1,0:T(8,128)}, u32[]{:S(2)}, u32[]{:S(2)}) collective-permute-start(f32[48,1152]{1,0:T(8,128)} %convolution_add_fusion.6), channel_id=1, source_target_pairs={{0,4},{4,8},{8,12},{12,16},{16,20},{20,24},{24,28},{28,0},{1,5},{5... | collective-permute-start | bytes 663560 | tf_op jit(solution)/shard_map/while/body/eval_jaxpr/ppermute | solution.py:10
  71.9 8.7 %collective-permute-start = (bf16[48,1152]{1,0:T(8,128)(2,1)}, bf16[48,1152]{1,0:T(8,128)(2,1)}, u32[]{:S(2)}, u32[]{:S(2)}) collective-permute-start(bf16[48,1152]{1,0:T(8,128)(2,1)} %copy.18), channel_id=1, source_target_pairs={{0,4},{4,8},{8,12},{12,16},{16,20},{20,24},{24,28},{28,0},{1,5},{5... | collective-permute-start | bytes 331784 | tf_op jit(solution)/shard_map/while/body/eval_jaxpr/ppermute | solution.py:10
  75.9 8.9 %collective-permute-start.1 = (f32[48,1152]{1,0:T(8,128)}, f32[48,1152]{1,0:T(8,128)}, u32[]{:S(2)}, u32[]{:S(2)}) collective-permute-start(f32[48,1152]{1,0:T(8,128)} %convolution_add_fusion.6), channel_id=1, source_target_pairs={{0,4},{4,8},{8,12},{12,16},{16,20},{20,24},{24,28},{28,0},{1,5},{5... | collective-permute-start | bytes 663560 | tf_op jit(solution)/shard_map/while/body/eval_jaxpr/ppermute | solution.py:10
  86.4 8.9 %collective-permute-start = (bf16[48,1152]{1,0:T(8,128)(2,1)}, bf16[48,1152]{1,0:T(8,128)(2,1)}, u32[]{:S(2)}, u32[]{:S(2)}) collective-permute-start(bf16[48,1152]{1,0:T(8,128)(2,1)} %copy.18), channel_id=1, source_target_pairs={{0,4},{4,8},{8,12},{12,16},{16,20},{20,24},{24,28},{28,0},{1,5},{5... | collective-permute-start | bytes 331784 | tf_op jit(solution)/shard_map/while/body/eval_jaxpr/ppermute | solution.py:10
  90.4 8.9 %collective-permute-start.1 = (f32[48,1152]{1,0:T(8,128)}, f32[48,1152]{1,0:T(8,128)}, u32[]{:S(2)}, u32[]{:S(2)}) collective-permute-start(f32[48,1152]{1,0:T(8,128)} %convolution_add_fusion.6), channel_id=1, source_target_pairs={{0,4},{4,8},{8,12},{12,16},{16,20},{20,24},{24,28},{28,0},{1,5},{5... | collective-permute-start | bytes 663560 | tf_op jit(solution)/shard_map/while/body/eval_jaxpr/ppermute | solution.py:10
  100.9 8.9 %collective-permute-start = (bf16[48,1152]{1,0:T(8,128)(2,1)}, bf16[48,1152]{1,0:T(8,128)(2,1)}, u32[]{:S(2)}, u32[]{:S(2)}) collective-permute-start(bf16[48,1152]{1,0:T(8,128)(2,1)} %copy.18), channel_id=1, source_target_pairs={{0,4},{4,8},{8,12},{12,16},{16,20},{20,24},{24,28},{28,0},{1,5},{5... | collective-permute-start | bytes 331784 | tf_op jit(solution)/shard_map/while/body/eval_jaxpr/ppermute | solution.py:10
  105.0 8.9 %collective-permute-start.1 = (f32[48,1152]{1,0:T(8,128)}, f32[48,1152]{1,0:T(8,128)}, u32[]{:S(2)}, u32[]{:S(2)}) collective-permute-start(f32[48,1152]{1,0:T(8,128)} %convolution_add_fusion.6), channel_id=1, source_target_pairs={{0,4},{4,8},{8,12},{12,16},{16,20},{20,24},{24,28},{28,0},{1,5},{5... | collective-permute-start | bytes 663560 | tf_op jit(solution)/shard_map/while/body/eval_jaxpr/ppermute | solution.py:10
  115.5 8.9 %collective-permute-start = (bf16[48,1152]{1,0:T(8,128)(2,1)}, bf16[48,1152]{1,0:T(8,128)(2,1)}, u32[]{:S(2)}, u32[]{:S(2)}) collective-permute-start(bf16[48,1152]{1,0:T(8,128)(2,1)} %copy.18), channel_id=1, source_target_pairs={{0,4},{4,8},{8,12},{12,16},{16,20},{20,24},{24,28},{28,0},{1,5},{5... | collective-permute-start | bytes 331784 | tf_op jit(solution)/shard_map/while/body/eval_jaxpr/ppermute | solution.py:10
  119.5 8.9 %collective-permute-start.1 = (f32[48,1152]{1,0:T(8,128)}, f32[48,1152]{1,0:T(8,128)}, u32[]{:S(2)}, u32[]{:S(2)}) collective-permute-start(f32[48,1152]{1,0:T(8,128)} %convolution_add_fusion.6), channel_id=1, source_target_pairs={{0,4},{4,8},{8,12},{12,16},{16,20},{20,24},{24,28},{28,0},{1,5},{5... | collective-permute-start | bytes 663560 | tf_op jit(solution)/shard_map/while/body/eval_jaxpr/ppermute | solution.py:10
  129.8 0.6 copy-start.3
  132.6 139.1 %reduce-scatter.10.cloned.1.call-start = ((), (), s32[]{:S(2)}) async-start(), calls=%async_computation.5 | async-start | bytes 5971968
  167.4 106.8 %copy-start.1 = (bf16[192,1152]{1,0:T(8,128)(2,1)S(1)}, bf16[192,1152]{1,0:T(8,128)(2,1)}, u32[]{:S(2)}) copy-start(bf16[192,1152]{1,0:T(8,128)(2,1)} %get-tuple-element.383) | copy-start | bytes 1327108
  167.4 106.8 %copy-start.4 = (f32[192,48]{0,1:T(8,128)S(1)}, f32[192,48]{0,1:T(8,128)}, u32[]{:S(2)}) copy-start(f32[192,48]{0,1:T(8,128)} %copy-done.3) | copy-start | bytes 110596
  167.4 109.5 %copy-start.5 = (u32[32]{0:T(128)S(1)}, u32[32]{0:T(128)}, u32[]{:S(2)}) copy-start(u32[32]{0:T(128)} %constant.71) | copy-start | bytes 388
  167.5 132.4 %reduce-scatter.8.cloned.1.call-start = ((), (), s32[]{:S(2)}) async-start(), calls=%async_computation.4 | async-start | bytes 1474560 | tf_op jit(solution)/shard_map/reduce_scatter | solution.py:91
  275.4 9.8 %collective-permute-start.2 = (f32[48,1152]{1,0:T(8,128)S(1)}, f32[48,1152]{1,0:T(8,128)S(1)}, u32[]{:S(2)}, u32[]{:S(2)}) collective-permute-start(f32[48,1152]{1,0:T(8,128)S(1)} %convolution_add_fusion.3), channel_id=1, source_target_pairs={{0,4},{4,8},{8,12},{12,16},{16,20},{20,24},{24,28},{28,0},{1,5},{5... | collective-permute-start | bytes 663560 | tf_op jit(solution)/shard_map/ppermute | solution.py:10
Sparse Core Ops, SparseCore 0:
  132.7 22.1 reduce-scatter.5
  167.5 104.1 reduce-scatter.9
  274.4 25.4 reduce-scatter.7
where the time goes:
time: 310 us; the launch traced here: 309 us
  waiting for transfers between devices  192 us (62%)
  matrix products  49.4 us (16%)
  local copies, waits for them, and re-layouts  25.8 us (8%)
  between operations  16 us (5%)
  blocking collectives  15.1 us (5%)
  starting transfers between devices  5.94 us (2%)
  other arithmetic  4.08 us (1%)
    unnamed x4, waiting for transfers between devices  104 us
    ppermute x15, waiting for transfers between devices, passed_along(): return lax.ppermute(value, axis, pairs)  51.2 us
    reduce_scatter x1, waiting for transfers between devices, local(): lax.psum_scatter(d_img, 'narrow', scatter_dimension=0, tiled=True)  22.3 us
    dot_general x9, matrix products, transposed_product(): lax.dot_general(grad_tile, group_img, (((0,), (0,)), ((), ())), preferred...  19.7 us
    dot_general x8, matrix products, pair_terms(): lax.dot_general(group_img, captions, (((1,), (1,)), ((), ())), preferred_...  15.4 us
    reduce_scatter x1, waiting for transfers between devices, local(): lax.psum_scatter(shard_rows, 'narrow', scatter_dimension=1, tiled=True)  14.7 us
    unnamed x18, local copies, waits for them, and re-layouts  14.3 us
    while x7, local copies, waits for them, and re-layouts  10.8 us
  transfers between devices with their start and end apart: 18, of which 16 were waited for; matrix products, arithmetic and copies ran while one was open for 13% of the time, Pallas kernels for 0%

commit v1 on v0

v1 whole, which is shorter than its diff:
```python
import functools

import jax
import jax.numpy as jnp
from jax import lax
from jax.experimental import pallas as pl
from jax.experimental.pallas import tpu as pltpu
from jax.sharding import PartitionSpec as P

AXES = ("wide", "narrow")
F32 = jnp.float32
BF16 = jnp.bfloat16
LANES = 128
STAT_ROWS = 16
VMEM = pl.BlockSpec(memory_space=pltpu.VMEM)
SMEM = pl.BlockSpec(memory_space=pltpu.SMEM)
NT = (((1,), (1,)), ((), ()))
TN = (((0,), (0,)), ((), ()))
PARAMS = pltpu.CompilerParams(vmem_limit_bytes=40 * 1024 * 1024)


def swapped(value, total, mask):
    return lax.ppermute(value, AXES, [(source, source ^ mask) for source in range(total)])


def split_pair(values):
    high = values.astype(BF16)
    return high, (values - high.astype(F32)).astype(BF16)


def column_block(member, narrow):
    return (member % narrow) * 2 + member // narrow


def pair_kernel(narrow, group, spread, *refs):
    member_ref, log_scale_ref, bias_ref, weight_ref = refs[:4]
    feats = refs[4 : 4 + group]
    texts = refs[4 + group : 4 + group + spread]
    outs = refs[4 + group + spread :]
    feats_out, unit_out, inv_out, emb_out, grad_out, own_out = outs[:6]
    send_out = outs[6 : 5 + group]
    unit_all, text_all, d_all = outs[5 + group :]
    rows, width = feats[0].shape
    images = group * rows
    share = width // group
    member = member_ref[0]

    for step in range(group):
        place = pl.multiple_of((member ^ step) * rows, rows)
        feats_out[pl.ds(place, rows), :] = feats[step][...]
    for start in range(0, images, LANES):
        cols = slice(start, start + LANES)
        proj = jnp.dot(feats_out[cols, :], weight_ref[...], preferred_element_type=F32)
        turned = proj.T
        inverse = lax.rsqrt(jnp.sum(turned * turned, axis=0, keepdims=True) + 1e-06)
        unit = turned * inverse
        inv_out[:, cols] = inverse
        unit_all[:, cols] = unit
        emb_out[:, cols] = unit.astype(BF16)
    block = pl.multiple_of(column_block(member, narrow) * share, share)
    unit_out[...] = unit_all[pl.ds(block, share), :]

    for step in range(spread):
        values = texts[step][...].astype(F32)
        inverse = lax.rsqrt(jnp.sum(values * values, axis=1, keepdims=True) + 1e-06)
        text_all[step * rows : (step + 1) * rows, :] = (values * inverse).astype(BF16)

    scale = jnp.exp(jnp.full((1, 1), log_scale_ref[0], F32))
    shift = bias_ref[0]
    count = 4 * rows if spread % 4 == 0 else rows
    chunks = spread * rows // count

    def one_chunk(chunk, loss_sum, dot_sum, first):
        here = pl.ds(pl.multiple_of(chunk * count, count), count)
        text = text_all[here, :]
        products = jnp.dot(text, emb_out[...], preferred_element_type=F32)
        logits = scale * products + shift
        caption = lax.broadcasted_iota(jnp.int32, (count, images), 0) + chunk * count
        image = lax.broadcasted_iota(jnp.int32, (count, images), 1)
        own = jnp.logical_and(caption < rows, image == member * rows + caption)
        sign = jnp.where(own, 1.0, -1.0).astype(F32)
        away = -sign * logits
        small = jnp.exp(-jnp.abs(away))
        loss = jnp.maximum(away, 0.0) + jnp.log1p(small)
        chance = jnp.where(away >= 0.0, 1.0, small) / (1.0 + small)
        grad = (-scale * sign * chance).astype(BF16)
        grad_out[here, :] = grad
        loss_sum = loss_sum + jnp.sum(loss, axis=0, keepdims=True)
        dot_sum = dot_sum + jnp.sum(grad.astype(F32) * products, axis=0, keepdims=True)
        d_img = lax.dot_general(text, grad, TN, preferred_element_type=F32)
        if first:
            d_all[...] = d_img
        else:
            d_all[...] += d_img
        return loss_sum, dot_sum

    zero = jnp.zeros((1, images), F32)
    sums = one_chunk(0, zero, zero, True)
    if chunks > 1:
        sums = lax.fori_loop(1, chunks, lambda c, s: one_chunk(c, *s, False), sums)
    loss_sum, dot_sum = sums

    own_out[:share, :] = d_all[pl.ds(block, share), :]
    own_out[share : share + 1, :] = loss_sum
    own_out[share + 1 : share + 2, :] = dot_sum
    loss_high, loss_low = split_pair(loss_sum)
    dot_high, dot_low = split_pair(dot_sum)
    row = lax.broadcasted_iota(jnp.int32, (STAT_ROWS, images), 0)
    stats = jnp.zeros((STAT_ROWS, images), F32)
    for place, line in enumerate((loss_high, loss_low, dot_high, dot_low)):
        stats = jnp.where(row == place, line.astype(F32), stats)
    stats = stats.astype(BF16)
    for step in range(1, group):
        part = pl.multiple_of(column_block(member ^ step, narrow) * share, share)
        send_out[step - 1][:share, :] = d_all[pl.ds(part, share), :].astype(BF16)
        send_out[step - 1][share:, :] = stats


def caption_kernel(rows, grad_ref, emb_ref, feats_ref, *outs):
    feats_t, own_out = outs[:2]
    for step in range(len(outs) - 1):
        grad = grad_ref[step * rows : (step + 1) * rows, :]
        product = lax.dot_general(grad, emb_ref[...], NT, preferred_element_type=F32)
        target = outs[1 + step]
        target[...] = product.astype(target.dtype)
    for start in range(0, feats_ref.shape[0], LANES):
        cols = slice(start, start + LANES)
        feats_t[:, cols] = feats_ref[cols, :].astype(F32).T.astype(BF16)


def gathered_gradient(own_ref, got, unit_ref, inv_ref, loss_out):
    share = unit_ref.shape[0]
    total = own_ref[:share, :]
    loss = own_ref[share : share + 1, :]
    along = own_ref[share + 1 : share + 2, :]
    for block in got:
        total = total + block[:share, :].astype(F32)
        stats = block[share:, :].astype(F32)
        loss = loss + (stats[0:1, :] + stats[1:2, :])
        along = along + (stats[2:3, :] + stats[3:4, :])
    loss_out[...] = loss
    return inv_ref[...] * (total - unit_ref[...] * along)


def weight_kernel(group, wide, *refs):
    wide_ref, own_ref = refs[:2]
    got = refs[2 : 1 + group]
    unit_ref, inv_ref, feats_ref, feats_t_ref = refs[1 + group : 5 + group]
    loss_out, own_out = refs[5 + group : 7 + group]
    send_out = refs[7 + group : 6 + group + wide]
    main_all, rest_all = refs[6 + group + wide :]
    share = unit_ref.shape[0]
    rest = share - LANES
    rows = feats_t_ref.shape[0] // wide
    d_zproj = gathered_gradient(own_ref, got, unit_ref, inv_ref, loss_out)
    high, low = split_pair(d_zproj)
    main_all[...] = lax.dot_general(
        feats_t_ref[...], high[:LANES, :], NT, preferred_element_type=F32
    ) + lax.dot_general(feats_t_ref[...], low[:LANES, :], NT, preferred_element_type=F32)
    tail = jnp.dot(high[LANES:, :], feats_ref[...], preferred_element_type=F32) + jnp.dot(
        low[LANES:, :], feats_ref[...], preferred_element_type=F32
    )
    rest_all[...] = jnp.zeros_like(rest_all)
    for place in range(wide):
        begin = place * rows
        rest_all[place, :rest, :] = tail[:, begin : begin + LANES]
        rest_all[place, rest:, : rows - LANES] = tail[:, begin + LANES : begin + rows]
    here = wide_ref[0]
    for step in range(wide):
        place = here ^ step
        begin = pl.multiple_of(place * rows, rows)
        target = own_out if step == 0 else send_out[step - 1]
        target[:rows, :] = main_all[pl.ds(begin, rows), :].astype(target.dtype)
        target[rows:, :] = rest_all[place].astype(target.dtype)


def total_kernel(rest, wide_ref, *refs):
    blocks, out = refs[:-1], refs[-1]
    rows = out.shape[0]
    even = blocks[0][...]
    for block in blocks[2::2]:
        even = even + block[...].astype(F32)
    odd = blocks[1][...].astype(F32)
    for block in blocks[3::2]:
        odd = odd + block[...].astype(F32)
    mine = (wide_ref[0] & 1) == 0
    halves = (jnp.where(mine, even, odd), jnp.where(mine, odd, even))
    for side, half in enumerate(halves):
        left = side * (LANES + rest)
        out[:, left : left + LANES] = half[:rows, :]
        upper = half[rows : rows + rest, :].T
        lower = half[rows + rest :, :].T
        out[:LANES, left + LANES : left + LANES + rest] = upper
        out[LANES:, left + LANES : left + LANES + rest] = lower[: rows - LANES, :]


def sum_kernel(*refs):
    total = refs[0][...]
    for block in refs[1:-1]:
        total = total + block[...].astype(F32)
    refs[-1][...] = total


def local(wide, narrow, image_feats, proj_weight, text_embed, log_scale, logit_bias):
    rows, width = image_feats.shape
    total = wide * narrow
    group = 2 * narrow
    spread = wide // 2
    share = width // group
    images = group * rows
    wide_pos = lax.axis_index("wide").astype(jnp.int32)
    member = (wide_pos & 1) * narrow + lax.axis_index("narrow").astype(jnp.int32)
    wide_pos, member = wide_pos.reshape(1), member.reshape(1)

    feats = [image_feats] + [swapped(image_feats, total, step) for step in range(1, group)]
    texts = [text_embed] + [swapped(text_embed, total, step * group) for step in range(1, spread)]

    sent = jax.ShapeDtypeStruct((share + STAT_ROWS, images), BF16)
    results = pl.pallas_call(
        functools.partial(pair_kernel, narrow, group, spread),
        in_specs=[SMEM] * 3 + [VMEM] * (1 + group + spread),
        out_specs=[VMEM] * (5 + group),
        out_shape=[
            jax.ShapeDtypeStruct((images, width), BF16),
            jax.ShapeDtypeStruct((share, images), F32),
            jax.ShapeDtypeStruct((1, images), F32),
            jax.ShapeDtypeStruct((width, images), BF16),
            jax.ShapeDtypeStruct((spread * rows, images), BF16),
            jax.ShapeDtypeStruct((share + 8, images), F32),
        ]
        + [sent] * (group - 1),
        scratch_shapes=[
            pltpu.VMEM((width, images), F32),
            pltpu.VMEM((spread * rows, width), BF16),
            pltpu.VMEM((width, images), F32),
        ],
        compiler_params=PARAMS,
        name="pairs",
    )(member, log_scale, logit_bias, proj_weight, *feats, *texts)
    all_feats, unit_part, inv_part, img_emb, grad_tile, own_part = results[:6]
    got = [swapped(value, total, step) for step, value in enumerate(results[6:], 1)]

    results = pl.pallas_call(
        functools.partial(caption_kernel, rows),
        in_specs=[VMEM] * 3,
        out_specs=[VMEM] * (1 + spread),
        out_shape=[jax.ShapeDtypeStruct((width, images), BF16), jax.ShapeDtypeStruct((rows, width), F32)]
        + [jax.ShapeDtypeStruct((rows, width), BF16)] * (spread - 1),
        compiler_params=PARAMS,
        name="captions",
    )(grad_tile, img_emb, all_feats)
    feats_t, own_text = results[:2]
    got_text = [swapped(value, total, step * group) for step, value in enumerate(results[2:], 1)]

    out_rows = width // wide
    rest = share - LANES
    packed = out_rows + 2 * rest
    direct = LANES < out_rows <= 2 * LANES and out_rows % 16 == 0 and rest % 16 == 0
    if direct:
        results = pl.pallas_call(
            functools.partial(weight_kernel, group, wide),
            in_specs=[SMEM] + [VMEM] * (4 + group),
            out_specs=[VMEM] * (1 + wide),
            out_shape=[
                jax.ShapeDtypeStruct((1, images), F32),
                jax.ShapeDtypeStruct((packed, LANES), F32),
            ]
            + [jax.ShapeDtypeStruct((packed, LANES), BF16)] * (wide - 1),
            scratch_shapes=[
                pltpu.VMEM((width, LANES), F32),
                pltpu.VMEM((wide, 2 * rest, LANES), F32),
            ],
            compiler_params=PARAMS,
            name="weights",
        )(wide_pos, own_part, *got, unit_part, inv_part, all_feats, feats_t)
        loss_line, own_weight = results[:2]
        got_weight = [swapped(value, total, step * narrow) for step, value in enumerate(results[2:], 1)]
        d_proj = pl.pallas_call(
            functools.partial(total_kernel, rest),
            in_specs=[SMEM] + [VMEM] * wide,
            out_specs=VMEM,
            out_shape=jax.ShapeDtypeStruct((out_rows, 2 * share), F32),
            compiler_params=PARAMS,
            name="weight_total",
        )(wide_pos, own_weight, *got_weight)
    else:

        def gradient_kernel(*refs):
            own_ref, blocks = refs[0], refs[1:group]
            unit_ref, inv_ref, loss_out, d_out = refs[group:]
            d_out[...] = gathered_gradient(own_ref, blocks, unit_ref, inv_ref, loss_out)

        loss_line, d_zproj = pl.pallas_call(
            gradient_kernel,
            in_specs=[VMEM] * (2 + group),
            out_specs=[VMEM] * 2,
            out_shape=[jax.ShapeDtypeStruct((1, images), F32), jax.ShapeDtypeStruct((share, images), F32)],
            compiler_params=PARAMS,
            name="gradient",
        )(own_part, *got, unit_part, inv_part)
        partial = sum(
            lax.dot_general(feats_t, part, NT, preferred_element_type=F32) for part in split_pair(d_zproj)
        )
        left = (wide_pos[0] & 1) == 0
        both = jnp.concatenate([jnp.where(left, partial, 0.0), jnp.where(left, 0.0, partial)], axis=1)
        d_proj = lax.psum_scatter(both, "wide", scatter_dimension=0, tiled=True)

    d_text_unit = pl.pallas_call(
        sum_kernel,
        in_specs=[VMEM] * spread,
        out_specs=VMEM,
        out_shape=jax.ShapeDtypeStruct((rows, width), F32),
        compiler_params=PARAMS,
        name="caption_total",
    )(own_text, *got_text)
    image_loss = lax.dynamic_slice_in_dim(loss_line[0], member[0] * rows, rows, 0)
    return (image_loss, d_text_unit, d_proj)


def solution(mesh):
    placed = (P(AXES, None), P(), P(AXES, None), P(), P())
    return jax.shard_map(
        functools.partial(local, mesh.shape["wide"], mesh.shape["narrow"]),
        mesh=mesh,
        in_specs=placed,
        out_specs=(P(AXES), P(AXES, None), P("wide", "narrow")),
        check_vma=False,
    )
```

time: 310 us -> 69.3 us (0.22)
  waiting for transfers between devices: 192 us -> 22 us
  matrix products: 49.4 us -> 0 us
  starting transfers between devices: 5.94 us -> 34.1 us
  local copies, waits for them, and re-layouts: 25.8 us -> 4.12 us
  blocking collectives: 15.1 us -> 0 us
  between operations: 16 us -> 1.99 us
  Pallas kernels: 0 us -> 6.91 us
  other arithmetic: 4.08 us -> 0 us
    unnamed x4 -> x0, waiting for transfers between devices: 104 us -> none
    dot_general x26 -> x0, matrix products: 49.4 us -> none  [the longest x9 19.7 us: transposed_product(): lax.dot_general(grad_tile, group_img, (((0,), (0,)), ((), ())), preferred...]
    reduce_scatter x2 -> x0, waiting for transfers between devices: 36.9 us -> none  [the longest x1 22.3 us: local(): lax.psum_scatter(d_img, 'narrow', scatter_dimension=0, tiled=True)]
    ppermute x15 -> x27, waiting for transfers between devices: 51.2 us -> 22 us  [swapped(): lax.ppermute(value, AXES, [(source, source ^ mask) for source in range(to...]
    ppermute x15 -> x27, starting transfers between devices: 5.82 us -> 34.1 us  [swapped(): lax.ppermute(value, AXES, [(source, source ^ mask) for source in range(to...]
    while x7 -> x0, local copies, waits for them, and re-layouts: 10.8 us -> none
    unnamed x18 -> x6, local copies, waits for them, and re-layouts: 14.3 us -> 3.54 us
    all_gather x1 -> x0, blocking collectives: 8.65 us -> none  [local(): lax.all_gather(img_unit.astype(jnp.bfloat16), 'narrow', axis=0, tiled=True)]
  transfers between devices with their start and end apart: 18 -> 27, of which waited for: 16 -> 12; matrix products, arithmetic and copies ran while one was open for 13% -> 1% of each run, Pallas kernels for 0% -> 4%
where the time goes in v1:
time: 69.3 us; the launch traced here: 69.1 us
  starting transfers between devices  34.1 us (49%)
  waiting for transfers between devices  22 us (32%)
  Pallas kernels  6.91 us (10%)
  local copies, waits for them, and re-layouts  4.12 us (6%)
  between operations  1.99 us (3%)
    ppermute x27, starting transfers between devices, swapped(): lax.ppermute(value, AXES, [(source, source ^ mask) for source in range(to...  34.1 us
    ppermute x27, waiting for transfers between devices, swapped(): lax.ppermute(value, AXES, [(source, source ^ mask) for source in range(to...  22 us
    unnamed x6, local copies, waits for them, and re-layouts  3.54 us
    pallas_call x1, Pallas kernels, local(): pl.pallas_call(functools.partial(pair_kernel, narrow, group, spread), in_...  2.99 us
  transfers between devices with their start and end apart: 27, of which 12 were waited for; matrix products, arithmetic and copies ran while one was open for 1% of the time, Pallas kernels for 4%

profile of v1, /device:TPU:0, one launch (start us, length us, event | category | flops | bytes accessed | tf_op | source)
XLA Modules:
  0.0 69.1 jit_solution(12492247170070298444)
XLA Ops:
  0.6 4.1 %collective-permute-start.8 = (bf16[48,1152]{1,0:T(8,128)(2,1)}, bf16[48,1152]{1,0:T(8,128)(2,1)S(1)}, u32[]{:S(2)}, u32[]{:S(2)}) collective-permute-start(bf16[48,1152]{1,0:T(8,128)(2,1)} %refs_12_.1), channel_id=1, source_target_pairs={{0,16},{1,17},{2,18},{3,19},{4,20},{5,21},{6,22},{7,23},{8,24},{9,... | collective-permute-start | bytes 331784 | tf_op jit(solution)/shard_map/ppermute | solution.py:23
  4.7 1.6 %collective-permute-start.7 = (bf16[48,1152]{1,0:T(8,128)(2,1)}, bf16[48,1152]{1,0:T(8,128)(2,1)S(1)}, u32[]{:S(2)}, u32[]{:S(2)}) collective-permute-start(bf16[48,1152]{1,0:T(8,128)(2,1)} %refs_12_.1), channel_id=1, source_target_pairs={{0,8},{1,9},{2,10},{3,11},{4,12},{5,13},{6,14},{7,15},{8,0},{9,1},... | collective-permute-start | bytes 331784 | tf_op jit(solution)/shard_map/ppermute | solution.py:23
  6.3 2.7 %collective-permute-start.5 = (bf16[48,1152]{1,0:T(8,128)(2,1)}, bf16[48,1152]{1,0:T(8,128)(2,1)S(1)}, u32[]{:S(2)}, u32[]{:S(2)}) collective-permute-start(bf16[48,1152]{1,0:T(8,128)(2,1)} %refs_4_.1), channel_id=1, source_target_pairs={{0,6},{1,7},{2,4},{3,5},{4,2},{5,3},{6,0},{7,1},{8,14},{9,15},{10,... | collective-permute-start | bytes 331784 | tf_op jit(solution)/shard_map/ppermute | solution.py:23
  9.0 3.0 %collective-permute-done.8.refs_14_ = bf16[48,1152]{1,0:T(8,128)(2,1)S(1)} collective-permute-done((bf16[48,1152]{1,0:T(8,128)(2,1)}, bf16[48,1152]{1,0:T(8,128)(2,1)S(1)}, u32[]{:S(2)}, u32[]{:S(2)}) %collective-permute-start.8) | collective-permute-done | bytes 110624 | tf_op jit(solution)/shard_map/ppermute | solution.py:23
  12.0 3.4 %collective-permute-start.3 = (bf16[48,1152]{1,0:T(8,128)(2,1)}, bf16[48,1152]{1,0:T(8,128)(2,1)S(1)}, u32[]{:S(2)}, u32[]{:S(2)}) collective-permute-start(bf16[48,1152]{1,0:T(8,128)(2,1)} %refs_4_.1), channel_id=1, source_target_pairs={{0,4},{1,5},{2,6},{3,7},{4,0},{5,1},{6,2},{7,3},{8,12},{9,13},{10,... | collective-permute-start | bytes 331784 | tf_op jit(solution)/shard_map/ppermute | solution.py:23
  15.4 1.6 %collective-permute-start.1 = (bf16[48,1152]{1,0:T(8,128)(2,1)}, bf16[48,1152]{1,0:T(8,128)(2,1)S(1)}, u32[]{:S(2)}, u32[]{:S(2)}) collective-permute-start(bf16[48,1152]{1,0:T(8,128)(2,1)} %refs_4_.1), channel_id=1, source_target_pairs={{0,2},{1,3},{2,0},{3,1},{4,6},{5,7},{6,4},{7,5},{8,10},{9,11},{10,... | collective-permute-start | bytes 331784 | tf_op jit(solution)/shard_map/ppermute | solution.py:23
  17.3 1.2 %collective-permute-start.6 = (bf16[48,1152]{1,0:T(8,128)(2,1)}, bf16[48,1152]{1,0:T(8,128)(2,1)S(1)}, u32[]{:S(2)}, u32[]{:S(2)}) collective-permute-start(bf16[48,1152]{1,0:T(8,128)(2,1)} %refs_4_.1), channel_id=1, source_target_pairs={{0,7},{1,6},{2,5},{3,4},{4,3},{5,2},{6,1},{7,0},{8,15},{9,14},{10,... | collective-permute-start | bytes 331784 | tf_op jit(solution)/shard_map/ppermute | solution.py:23
  19.8 1.1 %collective-permute-done.2.refs_7_ = bf16[48,1152]{1,0:T(8,128)(2,1)S(1)} collective-permute-done((bf16[48,1152]{1,0:T(8,128)(2,1)}, bf16[48,1152]{1,0:T(8,128)(2,1)S(1)}, u32[]{:S(2)}, u32[]{:S(2)}) %collective-permute-start.2) | collective-permute-done | bytes 110624 | tf_op jit(solution)/shard_map/ppermute | solution.py:23
  20.9 4.8 %collective-permute-done.1.refs_6_ = bf16[48,1152]{1,0:T(8,128)(2,1)S(1)} collective-permute-done((bf16[48,1152]{1,0:T(8,128)(2,1)}, bf16[48,1152]{1,0:T(8,128)(2,1)S(1)}, u32[]{:S(2)}, u32[]{:S(2)}) %collective-permute-start.1) | collective-permute-done | bytes 110624 | tf_op jit(solution)/shard_map/ppermute | solution.py:23
  25.7 1.7 %copy-done = bf16[1152,1152]{1,0:T(8,128)(2,1)S(1)} copy-done((bf16[1152,1152]{1,0:T(8,128)(2,1)S(1)}, bf16[1152,1152]{1,0:T(8,128)(2,1)}, u32[]{:S(2)}) %copy-start) | copy-done | bytes 2654232
  29.3 3.0 %pairs.1 = (bf16[384,1152]{1,0:T(8,128)(2,1)S(1)}, f32[144,384]{1,0:T(8,128)S(1)}, f32[1,384]{1,0:T(1,128)S(1)}, bf16[1152,384]{1,0:T(8,128)(2,1)S(1)}, bf16[192...) custom-call(s32[1]{0:T(128)} %bitcast.1.refs_0_, ...), custom_call_target="tpu_custom_call" | custom-call | tf_op jit(solution)/shard_map/pairs/pallas_call | solution.py:219
  32.8 1.4 %collective-permute-start.12 = (bf16[160,384]{1,0:T(8,128)(2,1)S(1)}, bf16[160,384]{1,0:T(8,128)(2,1)S(1)}, u32[]{:S(2)}, u32[]{:S(2)}) collective-permute-start(bf16[160,384]{1,0:T(8,128)(2,1)S(1)} %get-tuple-element.33), channel_id=1, source_target_pairs={{0,3},{1,2},{2,1},{3,0},{4,7},{5,6},{6,5},{7,4},{8,11},{9,10},{10,... | collective-permute-start | bytes 368648 | tf_op jit(solution)/shard_map/ppermute | solution.py:23
  34.2 1.7 %collective-permute-start.14 = (bf16[160,384]{1,0:T(8,128)(2,1)S(1)}, bf16[160,384]{1,0:T(8,128)(2,1)S(1)}, u32[]{:S(2)}, u32[]{:S(2)}) collective-permute-start(bf16[160,384]{1,0:T(8,128)(2,1)S(1)} %get-tuple-element.35), channel_id=1, source_target_pairs={{0,5},{1,4},{2,7},{3,6},{4,1},{5,0},{6,3},{7,2},{8,13},{9,12},{10,... | collective-permute-start | bytes 368648 | tf_op jit(solution)/shard_map/ppermute | solution.py:23
  36.0 2.5 %collective-permute-done.11.refs_3_ = bf16[160,384]{1,0:T(8,128)(2,1)S(1)} collective-permute-done((bf16[160,384]{1,0:T(8,128)(2,1)S(1)}, bf16[160,384]{1,0:T(8,128)(2,1)S(1)}, u32[]{:S(2)}, u32[]{:S(2)}) %collective-permute-start.11) | collective-permute-done | bytes 122912 | tf_op jit(solution)/shard_map/ppermute | solution.py:23
  38.6 1.2 %captions.1 = (bf16[1152,384]{1,0:T(8,128)(2,1)S(1)}, f32[48,1152]{1,0:T(8,128)S(1)}, bf16[48,1152]{1,0:T(8,128)(2,1)S(1)}, bf16[48,1152]{1,0:T(8,128)(2,1)S(1)}, bf16[48,1152]{1,0:T(8,128)(2,1)S(1)}) custom-call(bf16[192,384]{1,0:T(8,128)(2,1)S(1)} %get-tuple-element.41.grad_ref, bf16[1152,384]{1,0:T(8,128)(2,1)S(1)} %get-tuple-element.42.emb_ref, ...), custom_call_target="tpu_custom_call" | custom-call | tf_op jit(solution)/shard_map/captions/pallas_call | solution.py:243
  40.4 2.9 %collective-permute-start.18 = (bf16[48,1152]{1,0:T(8,128)(2,1)S(1)}, bf16[48,1152]{1,0:T(8,128)(2,1)S(1)}, u32[]{:S(2)}, u32[]{:S(2)}) collective-permute-start(bf16[48,1152]{1,0:T(8,128)(2,1)S(1)} %get-tuple-element.47), channel_id=1, source_target_pairs={{0,16},{1,17},{2,18},{3,19},{4,20},{5,21},{6,22},{7,23},{8,24},{9,... | collective-permute-start | bytes 331784 | tf_op jit(solution)/shard_map/ppermute | solution.py:23
  43.3 1.4 %collective-permute-start.19 = (bf16[48,1152]{1,0:T(8,128)(2,1)S(1)}, bf16[48,1152]{1,0:T(8,128)(2,1)S(1)}, u32[]{:S(2)}, u32[]{:S(2)}) collective-permute-start(bf16[48,1152]{1,0:T(8,128)(2,1)S(1)} %get-tuple-element.48), channel_id=1, source_target_pairs={{0,24},{1,25},{2,26},{3,27},{4,28},{5,29},{6,30},{7,31},{8,16},{9,... | collective-permute-start | bytes 331784 | tf_op jit(solution)/shard_map/ppermute | solution.py:23
  45.3 1.7 %collective-permute-done.16.refs_8_ = bf16[160,384]{1,0:T(8,128)(2,1)S(1)} collective-permute-done((bf16[160,384]{1,0:T(8,128)(2,1)S(1)}, bf16[160,384]{1,0:T(8,128)(2,1)S(1)}, u32[]{:S(2)}, u32[]{:S(2)}) %collective-permute-start.16) | collective-permute-done | bytes 122912 | tf_op jit(solution)/shard_map/ppermute | solution.py:23
  48.6 3.3 %collective-permute-done.18.refs_2_ = bf16[48,1152]{1,0:T(8,128)(2,1)S(1)} collective-permute-done((bf16[48,1152]{1,0:T(8,128)(2,1)S(1)}, bf16[48,1152]{1,0:T(8,128)(2,1)S(1)}, u32[]{:S(2)}, u32[]{:S(2)}) %collective-permute-start.18) | collective-permute-done | bytes 110624 | tf_op jit(solution)/shard_map/ppermute | solution.py:23
  52.6 3.0 %collective-permute-start.22 = (bf16[176,128]{1,0:T(8,128)(2,1)S(1)}, bf16[176,128]{1,0:T(8,128)(2,1)S(1)}, u32[]{:S(2)}, u32[]{:S(2)}) collective-permute-start(bf16[176,128]{1,0:T(8,128)(2,1)S(1)} %get-tuple-element.52), channel_id=1, source_target_pairs={{0,12},{1,13},{2,14},{3,15},{4,8},{5,9},{6,10},{7,11},{8,4},{9,5},... | collective-permute-start | bytes 135176 | tf_op jit(solution)/shard_map/ppermute | solution.py:23
  56.2 2.9 %collective-permute-start.24 = (bf16[176,128]{1,0:T(8,128)(2,1)S(1)}, bf16[176,128]{1,0:T(8,128)(2,1)S(1)}, u32[]{:S(2)}, u32[]{:S(2)}) collective-permute-start(bf16[176,128]{1,0:T(8,128)(2,1)S(1)} %get-tuple-element.54), channel_id=1, source_target_pairs={{0,20},{1,21},{2,22},{3,23},{4,16},{5,17},{6,18},{7,19},{8,28},{9,... | collective-permute-start | bytes 135176 | tf_op jit(solution)/shard_map/ppermute | solution.py:23
  59.1 2.4 %collective-permute-start.25 = (bf16[176,128]{1,0:T(8,128)(2,1)S(1)}, bf16[176,128]{1,0:T(8,128)(2,1)S(1)}, u32[]{:S(2)}, u32[]{:S(2)}) collective-permute-start(bf16[176,128]{1,0:T(8,128)(2,1)S(1)} %get-tuple-element.55), channel_id=1, source_target_pairs={{0,24},{1,25},{2,26},{3,27},{4,28},{5,29},{6,30},{7,31},{8,16},{9,... | collective-permute-start | bytes 135176 | tf_op jit(solution)/shard_map/ppermute | solution.py:23
  61.5 1.8 %collective-permute-start.26 = (bf16[176,128]{1,0:T(8,128)(2,1)S(1)}, bf16[176,128]{1,0:T(8,128)(2,1)S(1)}, u32[]{:S(2)}, u32[]{:S(2)}) collective-permute-start(bf16[176,128]{1,0:T(8,128)(2,1)S(1)} %get-tuple-element.56), channel_id=1, source_target_pairs={{0,28},{1,29},{2,30},{3,31},{4,24},{5,25},{6,26},{7,27},{8,20},{9,... | collective-permute-start | bytes 135176 | tf_op jit(solution)/shard_map/ppermute | solution.py:23
  65.0 3.2 %collective-permute-done.26.refs_7_ = bf16[176,128]{1,0:T(8,128)(2,1)S(1)} collective-permute-done((bf16[176,128]{1,0:T(8,128)(2,1)S(1)}, bf16[176,128]{1,0:T(8,128)(2,1)S(1)}, u32[]{:S(2)}, u32[]{:S(2)}) %collective-permute-start.26) | collective-permute-done | bytes 45088 | tf_op jit(solution)/shard_map/ppermute | solution.py:23
  (42 shorter events, 9.5 us)
Async XLA Ops:
  0.6 11.4 %collective-permute-start.8 = (bf16[48,1152]{1,0:T(8,128)(2,1)}, bf16[48,1152]{1,0:T(8,128)(2,1)S(1)}, u32[]{:S(2)}, u32[]{:S(2)}) collective-permute-start(bf16[48,1152]{1,0:T(8,128)(2,1)} %refs_12_.1), channel_id=1, source_target_pairs={{0,16},{1,17},{2,18},{3,19},{4,20},{5,21},{6,22},{7,23},{8,24},{9,... | collective-permute-start | bytes 331784 | tf_op jit(solution)/shard_map/ppermute | solution.py:23
  4.7 10.7 %collective-permute-start.7 = (bf16[48,1152]{1,0:T(8,128)(2,1)}, bf16[48,1152]{1,0:T(8,128)(2,1)S(1)}, u32[]{:S(2)}, u32[]{:S(2)}) collective-permute-start(bf16[48,1152]{1,0:T(8,128)(2,1)} %refs_12_.1), channel_id=1, source_target_pairs={{0,8},{1,9},{2,10},{3,11},{4,12},{5,13},{6,14},{7,15},{8,0},{9,1},... | collective-permute-start | bytes 331784 | tf_op jit(solution)/shard_map/ppermute | solution.py:23
  6.3 9.1 %collective-permute-start.9 = (bf16[48,1152]{1,0:T(8,128)(2,1)}, bf16[48,1152]{1,0:T(8,128)(2,1)S(1)}, u32[]{:S(2)}, u32[]{:S(2)}) collective-permute-start(bf16[48,1152]{1,0:T(8,128)(2,1)} %refs_12_.1), channel_id=1, source_target_pairs={{0,24},{1,25},{2,26},{3,27},{4,28},{5,29},{6,30},{7,31},{8,16},{9,... | collective-permute-start | bytes 331784 | tf_op jit(solution)/shard_map/ppermute | solution.py:23
  6.3 10.7 %collective-permute-start.5 = (bf16[48,1152]{1,0:T(8,128)(2,1)}, bf16[48,1152]{1,0:T(8,128)(2,1)S(1)}, u32[]{:S(2)}, u32[]{:S(2)}) collective-permute-start(bf16[48,1152]{1,0:T(8,128)(2,1)} %refs_4_.1), channel_id=1, source_target_pairs={{0,6},{1,7},{2,4},{3,5},{4,2},{5,3},{6,0},{7,1},{8,14},{9,15},{10,... | collective-permute-start | bytes 331784 | tf_op jit(solution)/shard_map/ppermute | solution.py:23
  9.0 8.3 %collective-permute-start.4 = (bf16[48,1152]{1,0:T(8,128)(2,1)}, bf16[48,1152]{1,0:T(8,128)(2,1)S(1)}, u32[]{:S(2)}, u32[]{:S(2)}) collective-permute-start(bf16[48,1152]{1,0:T(8,128)(2,1)} %refs_4_.1), channel_id=1, source_target_pairs={{0,5},{1,4},{2,7},{3,6},{4,1},{5,0},{6,3},{7,2},{8,13},{9,12},{10,... | collective-permute-start | bytes 331784 | tf_op jit(solution)/shard_map/ppermute | solution.py:23
  12.0 7.7 %collective-permute-start.3 = (bf16[48,1152]{1,0:T(8,128)(2,1)}, bf16[48,1152]{1,0:T(8,128)(2,1)S(1)}, u32[]{:S(2)}, u32[]{:S(2)}) collective-permute-start(bf16[48,1152]{1,0:T(8,128)(2,1)} %refs_4_.1), channel_id=1, source_target_pairs={{0,4},{1,5},{2,6},{3,7},{4,0},{5,1},{6,2},{7,3},{8,12},{9,13},{10,... | collective-permute-start | bytes 331784 | tf_op jit(solution)/shard_map/ppermute | solution.py:23
  15.4 10.3 %collective-permute-start.1 = (bf16[48,1152]{1,0:T(8,128)(2,1)}, bf16[48,1152]{1,0:T(8,128)(2,1)S(1)}, u32[]{:S(2)}, u32[]{:S(2)}) collective-permute-start(bf16[48,1152]{1,0:T(8,128)(2,1)} %refs_4_.1), channel_id=1, source_target_pairs={{0,2},{1,3},{2,0},{3,1},{4,6},{5,7},{6,4},{7,5},{8,10},{9,11},{10,... | collective-permute-start | bytes 331784 | tf_op jit(solution)/shard_map/ppermute | solution.py:23
  17.0 8.7 %collective-permute-start = (bf16[48,1152]{1,0:T(8,128)(2,1)}, bf16[48,1152]{1,0:T(8,128)(2,1)S(1)}, u32[]{:S(2)}, u32[]{:S(2)}) collective-permute-start(bf16[48,1152]{1,0:T(8,128)(2,1)} %refs_4_.1), channel_id=1, source_target_pairs={{0,1},{1,0},{2,3},{3,2},{4,5},{5,4},{6,7},{7,6},{8,9},{9,8},{10,11... | collective-permute-start | bytes 331784 | tf_op jit(solution)/shard_map/ppermute | solution.py:23
  17.3 8.4 %collective-permute-start.6 = (bf16[48,1152]{1,0:T(8,128)(2,1)}, bf16[48,1152]{1,0:T(8,128)(2,1)S(1)}, u32[]{:S(2)}, u32[]{:S(2)}) collective-permute-start(bf16[48,1152]{1,0:T(8,128)(2,1)} %refs_4_.1), channel_id=1, source_target_pairs={{0,7},{1,6},{2,5},{3,4},{4,3},{5,2},{6,1},{7,0},{8,15},{9,14},{10,... | collective-permute-start | bytes 331784 | tf_op jit(solution)/shard_map/ppermute | solution.py:23
  32.3 6.2 %collective-permute-start.11 = (bf16[160,384]{1,0:T(8,128)(2,1)S(1)}, bf16[160,384]{1,0:T(8,128)(2,1)S(1)}, u32[]{:S(2)}, u32[]{:S(2)}) collective-permute-start(bf16[160,384]{1,0:T(8,128)(2,1)S(1)} %get-tuple-element.32), channel_id=1, source_target_pairs={{0,2},{1,3},{2,0},{3,1},{4,6},{5,7},{6,4},{7,5},{8,10},{9,11},{10,... | collective-permute-start | bytes 368648 | tf_op jit(solution)/shard_map/ppermute | solution.py:23
  32.8 7.5 %collective-permute-start.12 = (bf16[160,384]{1,0:T(8,128)(2,1)S(1)}, bf16[160,384]{1,0:T(8,128)(2,1)S(1)}, u32[]{:S(2)}, u32[]{:S(2)}) collective-permute-start(bf16[160,384]{1,0:T(8,128)(2,1)S(1)} %get-tuple-element.33), channel_id=1, source_target_pairs={{0,3},{1,2},{2,1},{3,0},{4,7},{5,6},{6,5},{7,4},{8,11},{9,10},{10,... | collective-permute-start | bytes 368648 | tf_op jit(solution)/shard_map/ppermute | solution.py:23
  34.2 6.2 %collective-permute-start.13 = (bf16[160,384]{1,0:T(8,128)(2,1)S(1)}, bf16[160,384]{1,0:T(8,128)(2,1)S(1)}, u32[]{:S(2)}, u32[]{:S(2)}) collective-permute-start(bf16[160,384]{1,0:T(8,128)(2,1)S(1)} %get-tuple-element.34), channel_id=1, source_target_pairs={{0,4},{1,5},{2,6},{3,7},{4,0},{5,1},{6,2},{7,3},{8,12},{9,13},{10,... | collective-permute-start | bytes 368648 | tf_op jit(solution)/shard_map/ppermute | solution.py:23
  34.2 9.1 %collective-permute-start.14 = (bf16[160,384]{1,0:T(8,128)(2,1)S(1)}, bf16[160,384]{1,0:T(8,128)(2,1)S(1)}, u32[]{:S(2)}, u32[]{:S(2)}) collective-permute-start(bf16[160,384]{1,0:T(8,128)(2,1)S(1)} %get-tuple-element.35), channel_id=1, source_target_pairs={{0,5},{1,4},{2,7},{3,6},{4,1},{5,0},{6,3},{7,2},{8,13},{9,12},{10,... | collective-permute-start | bytes 368648 | tf_op jit(solution)/shard_map/ppermute | solution.py:23
  35.9 9.4 %collective-permute-start.15 = (bf16[160,384]{1,0:T(8,128)(2,1)S(1)}, bf16[160,384]{1,0:T(8,128)(2,1)S(1)}, u32[]{:S(2)}, u32[]{:S(2)}) collective-permute-start(bf16[160,384]{1,0:T(8,128)(2,1)S(1)} %get-tuple-element.36), channel_id=1, source_target_pairs={{0,6},{1,7},{2,4},{3,5},{4,2},{5,3},{6,0},{7,1},{8,14},{9,15},{10,... | collective-permute-start | bytes 368648 | tf_op jit(solution)/shard_map/ppermute | solution.py:23
  38.5 8.5 %collective-permute-start.16 = (bf16[160,384]{1,0:T(8,128)(2,1)S(1)}, bf16[160,384]{1,0:T(8,128)(2,1)S(1)}, u32[]{:S(2)}, u32[]{:S(2)}) collective-permute-start(bf16[160,384]{1,0:T(8,128)(2,1)S(1)} %get-tuple-element.37), channel_id=1, source_target_pairs={{0,7},{1,6},{2,5},{3,4},{4,3},{5,2},{6,1},{7,0},{8,15},{9,14},{10,... | collective-permute-start | bytes 368648 | tf_op jit(solution)/shard_map/ppermute | solution.py:23
  40.3 8.4 %collective-permute-start.17 = (bf16[48,1152]{1,0:T(8,128)(2,1)S(1)}, bf16[48,1152]{1,0:T(8,128)(2,1)S(1)}, u32[]{:S(2)}, u32[]{:S(2)}) collective-permute-start(bf16[48,1152]{1,0:T(8,128)(2,1)S(1)} %get-tuple-element.46), channel_id=1, source_target_pairs={{0,8},{1,9},{2,10},{3,11},{4,12},{5,13},{6,14},{7,15},{8,0},{9,1},... | collective-permute-start | bytes 331784 | tf_op jit(solution)/shard_map/ppermute | solution.py:23
  40.4 11.5 %collective-permute-start.18 = (bf16[48,1152]{1,0:T(8,128)(2,1)S(1)}, bf16[48,1152]{1,0:T(8,128)(2,1)S(1)}, u32[]{:S(2)}, u32[]{:S(2)}) collective-permute-start(bf16[48,1152]{1,0:T(8,128)(2,1)S(1)} %get-tuple-element.47), channel_id=1, source_target_pairs={{0,16},{1,17},{2,18},{3,19},{4,20},{5,21},{6,22},{7,23},{8,24},{9,... | collective-permute-start | bytes 331784 | tf_op jit(solution)/shard_map/ppermute | solution.py:23
  43.3 8.6 %collective-permute-start.19 = (bf16[48,1152]{1,0:T(8,128)(2,1)S(1)}, bf16[48,1152]{1,0:T(8,128)(2,1)S(1)}, u32[]{:S(2)}, u32[]{:S(2)}) collective-permute-start(bf16[48,1152]{1,0:T(8,128)(2,1)S(1)} %get-tuple-element.48), channel_id=1, source_target_pairs={{0,24},{1,25},{2,26},{3,27},{4,28},{5,29},{6,30},{7,31},{8,16},{9,... | collective-permute-start | bytes 331784 | tf_op jit(solution)/shard_map/ppermute | solution.py:23
  48.1 11.0 %collective-permute-start.20 = (bf16[176,128]{1,0:T(8,128)(2,1)S(1)}, bf16[176,128]{1,0:T(8,128)(2,1)S(1)}, u32[]{:S(2)}, u32[]{:S(2)}) collective-permute-start(bf16[176,128]{1,0:T(8,128)(2,1)S(1)} %get-tuple-element.50), channel_id=1, source_target_pairs={{0,4},{1,5},{2,6},{3,7},{4,0},{5,1},{6,2},{7,3},{8,12},{9,13},{10,... | collective-permute-start | bytes 135176 | tf_op jit(solution)/shard_map/ppermute | solution.py:23
  48.6 12.8 %collective-permute-start.21 = (bf16[176,128]{1,0:T(8,128)(2,1)S(1)}, bf16[176,128]{1,0:T(8,128)(2,1)S(1)}, u32[]{:S(2)}, u32[]{:S(2)}) collective-permute-start(bf16[176,128]{1,0:T(8,128)(2,1)S(1)} %get-tuple-element.51), channel_id=1, source_target_pairs={{0,8},{1,9},{2,10},{3,11},{4,12},{5,13},{6,14},{7,15},{8,0},{9,1},... | collective-permute-start | bytes 135176 | tf_op jit(solution)/shard_map/ppermute | solution.py:23
  52.6 11.2 %collective-permute-start.22 = (bf16[176,128]{1,0:T(8,128)(2,1)S(1)}, bf16[176,128]{1,0:T(8,128)(2,1)S(1)}, u32[]{:S(2)}, u32[]{:S(2)}) collective-permute-start(bf16[176,128]{1,0:T(8,128)(2,1)S(1)} %get-tuple-element.52), channel_id=1, source_target_pairs={{0,12},{1,13},{2,14},{3,15},{4,8},{5,9},{6,10},{7,11},{8,4},{9,5},... | collective-permute-start | bytes 135176 | tf_op jit(solution)/shard_map/ppermute | solution.py:23
  55.6 8.2 %collective-permute-start.23 = (bf16[176,128]{1,0:T(8,128)(2,1)S(1)}, bf16[176,128]{1,0:T(8,128)(2,1)S(1)}, u32[]{:S(2)}, u32[]{:S(2)}) collective-permute-start(bf16[176,128]{1,0:T(8,128)(2,1)S(1)} %get-tuple-element.53), channel_id=1, source_target_pairs={{0,16},{1,17},{2,18},{3,19},{4,20},{5,21},{6,22},{7,23},{8,24},{9,... | collective-permute-start | bytes 135176 | tf_op jit(solution)/shard_map/ppermute | solution.py:23
  56.2 8.2 %collective-permute-start.24 = (bf16[176,128]{1,0:T(8,128)(2,1)S(1)}, bf16[176,128]{1,0:T(8,128)(2,1)S(1)}, u32[]{:S(2)}, u32[]{:S(2)}) collective-permute-start(bf16[176,128]{1,0:T(8,128)(2,1)S(1)} %get-tuple-element.54), channel_id=1, source_target_pairs={{0,20},{1,21},{2,22},{3,23},{4,16},{5,17},{6,18},{7,19},{8,28},{9,... | collective-permute-start | bytes 135176 | tf_op jit(solution)/shard_map/ppermute | solution.py:23
  61.5 6.7 %collective-permute-start.26 = (bf16[176,128]{1,0:T(8,128)(2,1)S(1)}, bf16[176,128]{1,0:T(8,128)(2,1)S(1)}, u32[]{:S(2)}, u32[]{:S(2)}) collective-permute-start(bf16[176,128]{1,0:T(8,128)(2,1)S(1)} %get-tuple-element.56), channel_id=1, source_target_pairs={{0,28},{1,29},{2,30},{3,31},{4,24},{5,25},{6,26},{7,27},{8,20},{9,... | collective-permute-start | bytes 135176 | tf_op jit(solution)/shard_map/ppermute | solution.py:23
  (6 other events, 18.6 us)

commit v2 on v1

v2 whole, which is shorter than its diff:
```python
import functools

import jax
import jax.numpy as jnp
from jax import lax
from jax.experimental import pallas as pl
from jax.experimental.pallas import tpu as pltpu
from jax.sharding import PartitionSpec as P

AXES = ("outer", "inner", "narrow")
F32 = jnp.float32
BF16 = jnp.bfloat16
LANES = 128
STAT_ROWS = 16
VMEM = pl.BlockSpec(memory_space=pltpu.VMEM)
SMEM = pl.BlockSpec(memory_space=pltpu.SMEM)
NT = (((1,), (1,)), ((), ()))
TN = (((0,), (0,)), ((), ()))
PARAMS = pltpu.CompilerParams(vmem_limit_bytes=40 * 1024 * 1024)


def split_pair(values):
    high = values.astype(BF16)
    return high, (values - high.astype(F32)).astype(BF16)


def column_block(member, narrow):
    return (member % narrow) * 2 + member // narrow


def pair_kernel(
    narrow,
    rows,
    place_ref,
    log_scale_ref,
    bias_ref,
    weight_ref,
    feats_ref,
    texts_ref,
    unit_out,
    inv_out,
    emb_out,
    grad_out,
    send_out,
    unit_all,
    text_all,
    d_all,
):
    images, width = feats_ref.shape
    group, spread = images // rows, texts_ref.shape[0] // rows
    share = width // group
    line, member = place_ref[0], place_ref[1]

    for start in range(0, images, LANES):
        cols = slice(start, start + LANES)
        proj = jnp.dot(feats_ref[cols, :], weight_ref[...], preferred_element_type=F32)
        turned = proj.T
        inverse = lax.rsqrt(jnp.sum(turned * turned, axis=0, keepdims=True) + 1e-06)
        unit = turned * inverse
        inv_out[:, cols] = inverse
        unit_all[:, cols] = unit
        emb_out[:, cols] = unit.astype(BF16)
    block = pl.multiple_of(column_block(member, narrow) * share, share)
    unit_out[...] = unit_all[pl.ds(block, share), :]

    for step in range(spread):
        here = slice(step * rows, (step + 1) * rows)
        values = texts_ref[here, :].astype(F32)
        inverse = lax.rsqrt(jnp.sum(values * values, axis=1, keepdims=True) + 1e-06)
        text_all[here, :] = (values * inverse).astype(BF16)

    scale = jnp.exp(jnp.full((1, 1), log_scale_ref[0], F32))
    shift = bias_ref[0]
    count = 4 * rows if spread % 4 == 0 else rows
    chunks = spread * rows // count

    def one_chunk(chunk, loss_sum, dot_sum, first):
        here = pl.ds(pl.multiple_of(chunk * count, count), count)
        text = text_all[here, :]
        products = jnp.dot(text, emb_out[...], preferred_element_type=F32)
        logits = scale * products + shift
        caption = lax.broadcasted_iota(jnp.int32, (count, images), 0) + (chunk * count - line * rows)
        image = lax.broadcasted_iota(jnp.int32, (count, images), 1)
        here_too = jnp.logical_and(caption >= 0, caption < rows)
        own = jnp.logical_and(here_too, image == member * rows + caption)
        sign = jnp.where(own, 1.0, -1.0).astype(F32)
        away = -sign * logits
        small = jnp.exp(-jnp.abs(away))
        loss = jnp.maximum(away, 0.0) + jnp.log1p(small)
        chance = jnp.where(away >= 0.0, 1.0, small) / (1.0 + small)
        grad = (-scale * sign * chance).astype(BF16)
        grad_out[here, :] = grad
        loss_sum = loss_sum + jnp.sum(loss, axis=0, keepdims=True)
        dot_sum = dot_sum + jnp.sum(grad.astype(F32) * products, axis=0, keepdims=True)
        d_img = lax.dot_general(text, grad, TN, preferred_element_type=F32)
        if first:
            d_all[...] = d_img
        else:
            d_all[...] += d_img
        return loss_sum, dot_sum

    zero = jnp.zeros((1, images), F32)
    sums = one_chunk(0, zero, zero, True)
    if chunks > 1:
        sums = lax.fori_loop(1, chunks, lambda c, s: one_chunk(c, *s, False), sums)
    loss_sum, dot_sum = sums

    loss_high, loss_low = split_pair(loss_sum)
    dot_high, dot_low = split_pair(dot_sum)
    row = lax.broadcasted_iota(jnp.int32, (STAT_ROWS, images), 0)
    stats = jnp.zeros((STAT_ROWS, images), F32)
    for place, line in enumerate((loss_high, loss_low, dot_high, dot_low)):
        stats = jnp.where(row == place, line.astype(F32), stats)
    stats = stats.astype(BF16)
    for place in range(group):
        part = column_block(place, narrow) * share
        send_out[place, :share, :] = d_all[part : part + share, :].astype(BF16)
        send_out[place, share:, :] = stats


def caption_kernel(rows, grad_ref, emb_ref, feats_ref, feats_t, send_out):
    for step in range(send_out.shape[0]):
        grad = grad_ref[step * rows : (step + 1) * rows, :]
        product = lax.dot_general(grad, emb_ref[...], NT, preferred_element_type=F32)
        send_out[step] = product.astype(BF16)
    for start in range(0, feats_ref.shape[0], LANES):
        cols = slice(start, start + LANES)
        feats_t[:, cols] = feats_ref[cols, :].astype(F32).T.astype(BF16)


def gathered_gradient(got_ref, unit_ref, inv_ref, loss_out):
    share = unit_ref.shape[0]
    total = got_ref[0].astype(F32)
    for place in range(1, got_ref.shape[0]):
        total = total + got_ref[place].astype(F32)
    loss_out[...] = total[share : share + 1, :] + total[share + 1 : share + 2, :]
    along = total[share + 2 : share + 3, :] + total[share + 3 : share + 4, :]
    return inv_ref[...] * (total[:share, :] - unit_ref[...] * along)


def weight_kernel(wide, got_ref, unit_ref, inv_ref, feats_ref, feats_t_ref, loss_out, send_out):
    share = unit_ref.shape[0]
    rest = share - LANES
    rows = feats_t_ref.shape[0] // wide
    high, low = split_pair(gathered_gradient(got_ref, unit_ref, inv_ref, loss_out))
    main = lax.dot_general(
        feats_t_ref[...], high[:LANES, :], NT, preferred_element_type=F32
    ) + lax.dot_general(feats_t_ref[...], low[:LANES, :], NT, preferred_element_type=F32)
    tail = jnp.dot(high[LANES:, :], feats_ref[...], preferred_element_type=F32) + jnp.dot(
        low[LANES:, :], feats_ref[...], preferred_element_type=F32
    )
    main, tail = main.astype(BF16), tail.astype(BF16)
    for place in range(wide):
        begin = place * rows
        send_out[place, :rows, :] = main[begin : begin + rows, :]
        send_out[place, rows : rows + rest, :] = tail[:, begin : begin + LANES]
        send_out[place, rows + rest :, :] = jnp.zeros((rest, LANES), BF16)
        send_out[place, rows + rest :, : rows - LANES] = tail[:, begin + LANES : begin + rows]


def total_kernel(rest, got_ref, out):
    rows = out.shape[0]
    for side in range(2):
        half = got_ref[side].astype(F32)
        for place in range(side + 2, got_ref.shape[0], 2):
            half = half + got_ref[place].astype(F32)
        left = side * (LANES + rest)
        out[:, left : left + LANES] = half[:rows, :]
        out[:LANES, left + LANES : left + LANES + rest] = half[rows : rows + rest, :].T
        out[LANES:, left + LANES : left + LANES + rest] = half[rows + rest :, :].T[: rows - LANES, :]


def sum_kernel(got_ref, out):
    total = got_ref[0].astype(F32)
    for place in range(1, got_ref.shape[0]):
        total = total + got_ref[place].astype(F32)
    out[...] = total


def local(wide, narrow, image_feats, proj_weight, text_embed, log_scale, logit_bias):
    rows, width = image_feats.shape
    group = 2 * narrow
    spread = wide // 2
    share = width // group
    images = group * rows
    line = lax.axis_index("outer").astype(jnp.int32)
    member = lax.axis_index(("inner", "narrow")).astype(jnp.int32)

    all_feats = lax.all_gather(image_feats, ("inner", "narrow"), axis=0, tiled=True)
    texts = lax.all_gather(text_embed, "outer", axis=0, tiled=True)

    unit_part, inv_part, img_emb, grad_tile, sent = pl.pallas_call(
        functools.partial(pair_kernel, narrow, rows),
        in_specs=[SMEM] * 3 + [VMEM] * 3,
        out_specs=[VMEM] * 5,
        out_shape=[
            jax.ShapeDtypeStruct((share, images), F32),
            jax.ShapeDtypeStruct((1, images), F32),
            jax.ShapeDtypeStruct((width, images), BF16),
            jax.ShapeDtypeStruct((spread * rows, images), BF16),
            jax.ShapeDtypeStruct((group, share + STAT_ROWS, images), BF16),
        ],
        scratch_shapes=[
            pltpu.VMEM((width, images), F32),
            pltpu.VMEM((spread * rows, width), BF16),
            pltpu.VMEM((width, images), F32),
        ],
        compiler_params=PARAMS,
        name="pairs",
    )(jnp.stack([line, member]), log_scale, logit_bias, proj_weight, all_feats, texts)
    got = lax.all_to_all(sent, ("inner", "narrow"), 0, 0)

    feats_t, sent_text = pl.pallas_call(
        functools.partial(caption_kernel, rows),
        in_specs=[VMEM] * 3,
        out_specs=[VMEM] * 2,
        out_shape=[
            jax.ShapeDtypeStruct((width, images), BF16),
            jax.ShapeDtypeStruct((spread, rows, width), BF16),
        ],
        compiler_params=PARAMS,
        name="captions",
    )(grad_tile, img_emb, all_feats)
    got_text = lax.all_to_all(sent_text, "outer", 0, 0)

    out_rows = width // wide
    rest = share - LANES
    if LANES < out_rows <= 2 * LANES and out_rows % 16 == 0 and rest % 16 == 0:
        loss_line, sent_weight = pl.pallas_call(
            functools.partial(weight_kernel, wide),
            in_specs=[VMEM] * 5,
            out_specs=[VMEM] * 2,
            out_shape=[
                jax.ShapeDtypeStruct((1, images), F32),
                jax.ShapeDtypeStruct((wide, out_rows + 2 * rest, LANES), BF16),
            ],
            compiler_params=PARAMS,
            name="weights",
        )(got, unit_part, inv_part, all_feats, feats_t)
        got_weight = lax.all_to_all(sent_weight, ("outer", "inner"), 0, 0)
        d_proj = pl.pallas_call(
            functools.partial(total_kernel, rest),
            in_specs=[VMEM],
            out_specs=VMEM,
            out_shape=jax.ShapeDtypeStruct((out_rows, 2 * share), F32),
            compiler_params=PARAMS,
            name="weight_total",
        )(got_weight)
    else:

        def gradient_kernel(got_ref, unit_ref, inv_ref, loss_out, d_out):
            d_out[...] = gathered_gradient(got_ref, unit_ref, inv_ref, loss_out)

        loss_line, d_zproj = pl.pallas_call(
            gradient_kernel,
            in_specs=[VMEM] * 3,
            out_specs=[VMEM] * 2,
            out_shape=[jax.ShapeDtypeStruct((1, images), F32), jax.ShapeDtypeStruct((share, images), F32)],
            compiler_params=PARAMS,
            name="gradient",
        )(got, unit_part, inv_part)
        partial = sum(
            lax.dot_general(feats_t, part, NT, preferred_element_type=F32) for part in split_pair(d_zproj)
        )
        left = lax.axis_index("inner") == 0
        both = jnp.concatenate([jnp.where(left, partial, 0.0), jnp.where(left, 0.0, partial)], axis=1)
        d_proj = lax.psum_scatter(both, ("outer", "inner"), scatter_dimension=0, tiled=True)

    d_text_unit = pl.pallas_call(
        sum_kernel,
        in_specs=[VMEM],
        out_specs=VMEM,
        out_shape=jax.ShapeDtypeStruct((rows, width), F32),
        compiler_params=PARAMS,
        name="caption_total",
    )(got_text)
    image_loss = lax.dynamic_slice_in_dim(loss_line[0], member * rows, rows, 0)
    return (image_loss, d_text_unit, d_proj)


def solution(mesh):
    wide, narrow = mesh.shape["wide"], mesh.shape["narrow"]
    cut = jax.sharding.Mesh(mesh.devices.reshape(wide // 2, 2, narrow), AXES)
    placed = (P(AXES, None), P(), P(AXES, None), P(), P())
    return jax.shard_map(
        functools.partial(local, wide, narrow),
        mesh=cut,
        in_specs=placed,
        out_specs=(P(AXES), P(AXES, None), P(AXES[:2], "narrow")),
        check_vma=False,
    )
```

time: 69.3 us -> 88 us (1.27)
  blocking collectives: 0 us -> 27.9 us
  starting transfers between devices: 34.1 us -> 12.4 us
  waiting for transfers between devices: 22 us -> 29.5 us
  local copies, waits for them, and re-layouts: 4.12 us -> 6.82 us
  Pallas kernels: 6.91 us -> 8.91 us
    ppermute x27 -> x0, starting transfers between devices: 34.1 us -> none  [swapped(): lax.ppermute(value, AXES, [(source, source ^ mask) for source in range(to...]
    all_to_all x0 -> x3, waiting for transfers between devices: none -> 29.5 us  [the longest x1 10.8 us: local(): got_text = lax.all_to_all(sent_text, 'outer', 0, 0)]
    all_gather x0 -> x2, blocking collectives: none -> 27.9 us  [the longest x1 16.9 us: local(): texts = lax.all_gather(text_embed, 'outer', axis=0, tiled=True)]
    ppermute x27 -> x0, waiting for transfers between devices: 22 us -> none  [swapped(): lax.ppermute(value, AXES, [(source, source ^ mask) for source in range(to...]
    all_to_all x0 -> x3, starting transfers between devices: none -> 12.4 us  [the longest x1 5.38 us: local(): got_text = lax.all_to_all(sent_text, 'outer', 0, 0)]
    unnamed x6 -> x12, local copies, waits for them, and re-layouts: 3.54 us -> 6.24 us
    pallas_call x4, Pallas kernels: 5.68 us -> 7.71 us  [the longest x1 4.35 us: local(): pl.pallas_call(functools.partial(pair_kernel, narrow, rows), in_specs=[SM...]
  transfers between devices with their start and end apart: 27 -> 3, of which waited for: 12 -> 3; matrix products, arithmetic and copies ran while one was open for 1% -> 1% of each run, Pallas kernels for 4% -> 4%
where the time goes in v2:
time: 88 us; the launch traced here: 87.5 us
  waiting for transfers between devices  29.5 us (34%)
  blocking collectives  27.9 us (32%)
  starting transfers between devices  12.4 us (14%)
  Pallas kernels  8.91 us (10%)
  local copies, waits for them, and re-layouts  6.82 us (8%)
  between operations  1.97 us (2%)
    all_gather x1, blocking collectives, local(): texts = lax.all_gather(text_embed, 'outer', axis=0, tiled=True)  16.9 us
    all_gather x1, blocking collectives, local(): lax.all_gather(image_feats, ('inner', 'narrow'), axis=0, tiled=True)  11 us
    all_to_all x1, waiting for transfers between devices, local(): got_text = lax.all_to_all(sent_text, 'outer', 0, 0)  10.8 us
    all_to_all x1, waiting for transfers between devices, local(): got = lax.all_to_all(sent, ('inner', 'narrow'), 0, 0)  9.6 us
    all_to_all x1, waiting for transfers between devices, local(): got_weight = lax.all_to_all(sent_weight, ('outer', 'inner'), 0, 0)  9.07 us
    unnamed x12, local copies, waits for them, and re-layouts  6.24 us
    all_to_all x1, starting transfers between devices, local(): got_text = lax.all_to_all(sent_text, 'outer', 0, 0)  5.38 us
    pallas_call x1, Pallas kernels, local(): pl.pallas_call(functools.partial(pair_kernel, narrow, rows), in_specs=[SM...  4.35 us
  transfers between devices with their start and end apart: 3, of which 3 were waited for; matrix products, arithmetic and copies ran while one was open for 1% of the time, Pallas kernels for 4%

profile of v2, /device:TPU:0, one launch (start us, length us, event | category | flops | bytes accessed | tf_op | source)
XLA Modules:
  0.0 87.5 jit_solution(9220994540485362801)
XLA Ops:
  1.9 16.9 %all_gather.7.texts_ref = bf16[192,1152]{1,0:T(8,128)(2,1)S(1)} all-gather(bf16[48,1152]{1,0:T(8,128)(2,1)} %param.7), channel_id=1, replica_groups=mesh['outer'=4,'inner'=2,'narrow'=4] {'outer'}, dimensions={0}, use_global_device_ids=true | all-gather | bytes 552960 | tf_op jit(solution)/shard_map/all_gather | solution.py:190
  18.8 11.0 %all_gather.6.feats_ref = bf16[384,1152]{1,0:T(8,128)(2,1)S(1)} all-gather(bf16[48,1152]{1,0:T(8,128)(2,1)} %param.5), channel_id=1, replica_groups=mesh['outer'=4,'inner'=2,'narrow'=4] {'inner','narrow'}, dimensions={0}, use_global_device_ids=true | all-gather | bytes 995328 | tf_op jit(solution)/shard_map/all_gather | solution.py:189
  29.8 0.1 pad_add_fusion.place_ref
  29.9 0.0 copy-start
  29.9 1.7 %copy-done = bf16[1152,1152]{1,0:T(8,128)(2,1)S(1)} copy-done((bf16[1152,1152]{1,0:T(8,128)(2,1)S(1)}, bf16[1152,1152]{1,0:T(8,128)(2,1)}, u32[]{:S(2)}) %copy-start) | copy-done | bytes 2654232
  31.6 4.3 %pairs.1 = (f32[144,384]{1,0:T(8,128)S(1)}, f32[1,384]{1,0:T(1,128)S(1)}, bf16[1152,384]{1,0:T(8,128)(2,1)S(1)}, bf16[192,384]{1,0:T(8,128)(2,1)S(1)}, bf16[8,160,384]{2,1,0:T(8,128)(2,1)}) custom-call(s32[2]{0:T(128)S(1)} %pad_add_fusion.place_ref, f32[1]{0:T(128)S(6)} %copy.8.log_scale_ref, f32[1]{0:T(128)S(6)} %copy.9.bias_ref, ...), custom_call_target="tpu_custom_call" | custom-call | tf_op jit(solution)/shard_map/pairs/pallas_call | solution.py:192
  36.0 0.0 copy-start.1
  36.0 1.0 %copy-done.1 = bf16[1152,384]{1,0:T(8,128)(2,1)} copy-done((bf16[1152,384]{1,0:T(8,128)(2,1)}, bf16[1152,384]{1,0:T(8,128)(2,1)S(1)}, u32[]{:S(2)}) %copy-start.1) | copy-done | bytes 884760
  37.0 0.7 copy-done.4
  37.6 3.6 %all-to-all-start = ((bf16[8,160,384]{2,1,0:T(8,128)(2,1)}), bf16[8,160,384]{2,1,0:T(8,128)(2,1)S(1)}, u32[]{:S(2)}, u32[]{:S(2)}) async-start(bf16[8,160,384]{2,1,0:T(8,128)(2,1)} %get-tuple-element.12), calls=%async_computation | async-start | bytes 1966080 | tf_op jit(solution)/shard_map/all_to_all | solution.py:211
  41.2 0.0 copy-start.2
  41.2 1.2 %copy-done.2 = bf16[1152,384]{1,0:T(8,128)(2,1)S(1)} copy-done((bf16[1152,384]{1,0:T(8,128)(2,1)S(1)}, bf16[1152,384]{1,0:T(8,128)(2,1)}, u32[]{:S(2)}) %copy-start.2) | copy-done | bytes 884760
  42.4 0.9 %copy-done.5 = bf16[192,384]{1,0:T(8,128)(2,1)S(1)} copy-done((bf16[192,384]{1,0:T(8,128)(2,1)S(1)}, bf16[192,384]{1,0:T(8,128)(2,1)}, u32[]{:S(2)}) %copy-start.5) | copy-done | bytes 147480
  43.3 1.2 %captions.1 = (bf16[1152,384]{1,0:T(8,128)(2,1)S(1)}, bf16[4,48,1152]{2,1,0:T(8,128)(2,1)S(1)}) custom-call(bf16[192,384]{1,0:T(8,128)(2,1)S(1)} %copy-done.5, bf16[1152,384]{1,0:T(8,128)(2,1)S(1)} %copy-done.2, bf16[384,1152]{1,0:T(8,128)(2,1)S(1)} %all_gather.6.feats_ref), custom_call_target="tpu_custom_call" | custom-call | tf_op jit(solution)/shard_map/captions/pallas_call | solution.py:213
  44.5 0.8 copy-done.3
  45.3 9.6 %all-to-all-done.got_ref = bf16[8,160,384]{2,1,0:T(8,128)(2,1)S(1)} async-done(((bf16[8,160,384]{2,1,0:T(8,128)(2,1)}), bf16[8,160,384]{2,1,0:T(8,128)(2,1)S(1)}, u32[]{:S(2)}, u32[]{:S(2)}) %all-to-all-start) | async-done | bytes 983072 | tf_op jit(solution)/shard_map/all_to_all | solution.py:211
  54.9 5.4 %all-to-all-start.1 = ((bf16[4,48,1152]{2,1,0:T(8,128)(2,1)}), bf16[4,48,1152]{2,1,0:T(8,128)(2,1)S(1)}, u32[]{:S(2)}, u32[]{:S(2)}) async-start(bf16[4,48,1152]{2,1,0:T(8,128)(2,1)} %copy-done.3), calls=%async_computation.1 | async-start | bytes 884736 | tf_op jit(solution)/shard_map/all_to_all | solution.py:224
  60.2 1.8 %weights.1 = (f32[1,384]{1,0:T(1,128)S(1)}, bf16[8,176,128]{2,1,0:T(8,128)(2,1)}) custom-call(bf16[8,160,384]{2,1,0:T(8,128)(2,1)S(1)} %all-to-all-done.got_ref, f32[144,384]{1,0:T(8,128)S(1)} %get-tuple-element.13.unit_ref, f32[1,384]{1,0:T(1,128)S(1)} %get-tuple-element.14.inv_ref, bf16[384,1152]{1,0:T(8,128)(2,1)S(1)} %all_gather.6.feats_ref, ...), custom_call_target="tpu_custom_call" | custom-call | tf_op jit(solution)/shard_map/weights/pallas_call | solution.py:229
  62.0 10.8 %all-to-all-done.1.got_ref = bf16[4,48,1152]{2,1,0:T(8,128)(2,1)S(1)} async-done(((bf16[4,48,1152]{2,1,0:T(8,128)(2,1)}), bf16[4,48,1152]{2,1,0:T(8,128)(2,1)S(1)}, u32[]{:S(2)}, u32[]{:S(2)}) %all-to-all-start.1) | async-done | bytes 442400 | tf_op jit(solution)/shard_map/all_to_all | solution.py:224
  72.8 3.4 %all-to-all-start.2 = ((bf16[8,176,128]{2,1,0:T(8,128)(2,1)}), bf16[8,176,128]{2,1,0:T(8,128)(2,1)S(1)}, u32[]{:S(2)}, u32[]{:S(2)}) async-start(bf16[8,176,128]{2,1,0:T(8,128)(2,1)} %get-tuple-element.20), calls=%async_computation.2 | async-start | bytes 720896 | tf_op jit(solution)/shard_map/all_to_all | solution.py:240
  76.2 0.7 caption_total.1
  77.0 0.6 dynamic-slice_bitcast_fusion
  77.5 9.1 %all-to-all-done.2.got_ref = bf16[8,176,128]{2,1,0:T(8,128)(2,1)S(1)} async-done(((bf16[8,176,128]{2,1,0:T(8,128)(2,1)}), bf16[8,176,128]{2,1,0:T(8,128)(2,1)S(1)}, u32[]{:S(2)}, u32[]{:S(2)}) %all-to-all-start.2) | async-done | bytes 360480 | tf_op jit(solution)/shard_map/all_to_all | solution.py:240
  86.6 0.9 weight_total.1
  (3 shorter events, 0.0 us)
Async XLA Ops:
  29.9 1.7 %copy-start = (bf16[1152,1152]{1,0:T(8,128)(2,1)S(1)}, bf16[1152,1152]{1,0:T(8,128)(2,1)}, u32[]{:S(2)}) copy-start(bf16[1152,1152]{1,0:T(8,128)(2,1)} %weight_ref.1) | copy-start | bytes 7962628
  36.0 1.0 %copy-start.1 = (bf16[1152,384]{1,0:T(8,128)(2,1)}, bf16[1152,384]{1,0:T(8,128)(2,1)S(1)}, u32[]{:S(2)}) copy-start(bf16[1152,384]{1,0:T(8,128)(2,1)S(1)} %get-tuple-element.16.emb_ref) | copy-start | bytes 2654212
  37.0 0.7 copy-start.4
  37.6 17.2 %all-to-all-start = ((bf16[8,160,384]{2,1,0:T(8,128)(2,1)}), bf16[8,160,384]{2,1,0:T(8,128)(2,1)S(1)}, u32[]{:S(2)}, u32[]{:S(2)}) async-start(bf16[8,160,384]{2,1,0:T(8,128)(2,1)} %get-tuple-element.12), calls=%async_computation | async-start | bytes 1966080 | tf_op jit(solution)/shard_map/all_to_all | solution.py:211
  41.2 1.2 %copy-start.2 = (bf16[1152,384]{1,0:T(8,128)(2,1)S(1)}, bf16[1152,384]{1,0:T(8,128)(2,1)}, u32[]{:S(2)}) copy-start(bf16[1152,384]{1,0:T(8,128)(2,1)} %copy-done.1) | copy-start | bytes 2654212
  42.3 0.9 %copy-start.5 = (bf16[192,384]{1,0:T(8,128)(2,1)S(1)}, bf16[192,384]{1,0:T(8,128)(2,1)}, u32[]{:S(2)}) copy-start(bf16[192,384]{1,0:T(8,128)(2,1)} %copy-done.4) | copy-start | bytes 442372
  44.5 0.8 copy-start.3
  54.9 17.9 %all-to-all-start.1 = ((bf16[4,48,1152]{2,1,0:T(8,128)(2,1)}), bf16[4,48,1152]{2,1,0:T(8,128)(2,1)S(1)}, u32[]{:S(2)}, u32[]{:S(2)}) async-start(bf16[4,48,1152]{2,1,0:T(8,128)(2,1)} %copy-done.3), calls=%async_computation.1 | async-start | bytes 884736 | tf_op jit(solution)/shard_map/all_to_all | solution.py:224
  72.8 13.8 %all-to-all-start.2 = ((bf16[8,176,128]{2,1,0:T(8,128)(2,1)}), bf16[8,176,128]{2,1,0:T(8,128)(2,1)S(1)}, u32[]{:S(2)}, u32[]{:S(2)}) async-start(bf16[8,176,128]{2,1,0:T(8,128)(2,1)} %get-tuple-element.20), calls=%async_computation.2 | async-start | bytes 720896 | tf_op jit(solution)/shard_map/all_to_all | solution.py:240

commit v3 on v1

--- a/solution.py
+++ b/solution.py
@@ -7,7 +7,7 @@
 from jax.experimental.pallas import tpu as pltpu
 from jax.sharding import PartitionSpec as P
 
-AXES = ("wide", "narrow")
+AXES = ("outer", "inner", "narrow")
 F32 = jnp.float32
 BF16 = jnp.bfloat16
 LANES = 128
@@ -32,25 +32,25 @@
     return (member % narrow) * 2 + member // narrow
 
 
+def load_kernel(weight_ref, out):
+    pltpu.sync_copy(weight_ref, out)
+
+
 def pair_kernel(narrow, group, spread, *refs):
-    member_ref, log_scale_ref, bias_ref, weight_ref = refs[:4]
-    feats = refs[4 : 4 + group]
-    texts = refs[4 + group : 4 + group + spread]
-    outs = refs[4 + group + spread :]
-    feats_out, unit_out, inv_out, emb_out, grad_out, own_out = outs[:6]
-    send_out = outs[6 : 5 + group]
-    unit_all, text_all, d_all = outs[5 + group :]
-    rows, width = feats[0].shape
+    member_ref, log_scale_ref, bias_ref, weight_ref, feats_ref = refs[:5]
+    texts = refs[5 : 5 + spread]
+    outs = refs[5 + spread :]
+    unit_out, inv_out, emb_out, grad_out, own_out = outs[:5]
+    send_out = outs[5 : 4 + group]
+    unit_all, text_all, d_all = outs[4 + group :]
+    rows, width = texts[0].shape
     images = group * rows
     share = width // group
     member = member_ref[0]
 
-    for step in range(group):
-        place = pl.multiple_of((member ^ step) * rows, rows)
-        feats_out[pl.ds(place, rows), :] = feats[step][...]
     for start in range(0, images, LANES):
         cols = slice(start, start + LANES)
-        proj = jnp.dot(feats_out[cols, :], weight_ref[...], preferred_element_type=F32)
+        proj = jnp.dot(feats_ref[cols, :], weight_ref[...], preferred_element_type=F32)
         turned = proj.T
         inverse = lax.rsqrt(jnp.sum(turned * turned, axis=0, keepdims=True) + 1e-06)
         unit = turned * inverse
@@ -208,20 +208,28 @@
     spread = wide // 2
     share = width // group
     images = group * rows
-    wide_pos = lax.axis_index("wide").astype(jnp.int32)
-    member = (wide_pos & 1) * narrow + lax.axis_index("narrow").astype(jnp.int32)
+    wide_pos = lax.axis_index(AXES[:2]).astype(jnp.int32)
+    member = lax.axis_index(AXES[1:]).astype(jnp.int32)
     wide_pos, member = wide_pos.reshape(1), member.reshape(1)
 
-    feats = [image_feats] + [swapped(image_feats, total, step) for step in range(1, group)]
     texts = [text_embed] + [swapped(text_embed, total, step * group) for step in range(1, spread)]
+
+    all_feats = lax.all_gather(image_feats, AXES[1:], axis=0, tiled=True)
+    weight = pl.pallas_call(
+        load_kernel,
+        in_specs=[pl.BlockSpec(memory_space=pl.ANY)],
+        out_specs=VMEM,
+        out_shape=jax.ShapeDtypeStruct((width, width), BF16),
+        compiler_params=PARAMS,
+        name="load_weight",
+    )(proj_weight)
 
     sent = jax.ShapeDtypeStruct((share + STAT_ROWS, images), BF16)
     results = pl.pallas_call(
         functools.partial(pair_kernel, narrow, group, spread),
-        in_specs=[SMEM] * 3 + [VMEM] * (1 + group + spread),
-        out_specs=[VMEM] * (5 + group),
+        in_specs=[SMEM] * 3 + [VMEM] * (2 + spread),
+        out_specs=[VMEM] * (4 + group),
         out_shape=[
-            jax.ShapeDtypeStruct((images, width), BF16),
             jax.ShapeDtypeStruct((share, images), F32),
             jax.ShapeDtypeStruct((1, images), F32),
             jax.ShapeDtypeStruct((width, images), BF16),
@@ -236,9 +244,9 @@
         ],
         compiler_params=PARAMS,
         name="pairs",
-    )(member, log_scale, logit_bias, proj_weight, *feats, *texts)
-    all_feats, unit_part, inv_part, img_emb, grad_tile, own_part = results[:6]
-    got = [swapped(value, total, step) for step, value in enumerate(results[6:], 1)]
+    )(member, log_scale, logit_bias, weight, all_feats, *texts)
+    unit_part, inv_part, img_emb, grad_tile, own_part = results[:5]
+    got = [swapped(value, total, step) for step, value in enumerate(results[5:], 1)]
 
     results = pl.pallas_call(
         functools.partial(caption_kernel, rows),
@@ -303,7 +311,7 @@
         )
         left = (wide_pos[0] & 1) == 0
         both = jnp.concatenate([jnp.where(left, partial, 0.0), jnp.where(left, 0.0, partial)], axis=1)
-        d_proj = lax.psum_scatter(both, "wide", scatter_dimension=0, tiled=True)
+        d_proj = lax.psum_scatter(both, AXES[:2], scatter_dimension=0, tiled=True)
 
     d_text_unit = pl.pallas_call(
         sum_kernel,
@@ -318,11 +326,13 @@
 
 
 def solution(mesh):
+    wide, narrow = mesh.shape["wide"], mesh.shape["narrow"]
+    cut = jax.sharding.Mesh(mesh.devices.reshape(wide // 2, 2, narrow), AXES)
     placed = (P(AXES, None), P(), P(AXES, None), P(), P())
     return jax.shard_map(
-        functools.partial(local, mesh.shape["wide"], mesh.shape["narrow"]),
-        mesh=mesh,
+        functools.partial(local, wide, narrow),
+        mesh=cut,
         in_specs=placed,
-        out_specs=(P(AXES), P(AXES, None), P("wide", "narrow")),
+        out_specs=(P(AXES), P(AXES, None), P(AXES[:2], "narrow")),
         check_vma=False,
     )

time: 69.3 us -> 67.3 us (0.971)
  waiting for transfers between devices: 22 us -> 8.84 us
  blocking collectives: 0 us -> 11.3 us
  starting transfers between devices: 34.1 us -> 27.5 us
  local copies, waits for them, and re-layouts: 4.12 us -> 7.55 us
  Pallas kernels: 6.91 us -> 9.77 us
    ppermute x27 -> x20, waiting for transfers between devices: 22 us -> 8.84 us  [swapped(): lax.ppermute(value, AXES, [(source, source ^ mask) for source in range(to...]
    all_gather x0 -> x1, blocking collectives: none -> 11.3 us  [local(): all_feats = lax.all_gather(image_feats, AXES[1:], axis=0, tiled=True)]
    ppermute x27 -> x20, starting transfers between devices: 34.1 us -> 27.5 us  [swapped(): lax.ppermute(value, AXES, [(source, source ^ mask) for source in range(to...]
    unnamed x6 -> x20, local copies, waits for them, and re-layouts: 3.54 us -> 6.97 us
    pallas_call x1, Pallas kernels: 2.99 us -> 4.59 us  [local(): pl.pallas_call(functools.partial(pair_kernel, narrow, group, spread), in_...]
  transfers between devices with their start and end apart: 27 -> 20, of which waited for: 12 -> 5; matrix products, arithmetic and copies ran while one was open for 1% -> 1% of each run, Pallas kernels for 4% -> 6%
where the time goes in v3:
time: 67.3 us; the launch traced here: 66.9 us
  starting transfers between devices  27.5 us (41%)
  blocking collectives  11.3 us (17%)
  Pallas kernels  9.77 us (15%)
  waiting for transfers between devices  8.84 us (13%)
  local copies, waits for them, and re-layouts  7.55 us (11%)
  between operations  2 us (3%)
    ppermute x20, starting transfers between devices, swapped(): lax.ppermute(value, AXES, [(source, source ^ mask) for source in range(to...  27.5 us
    all_gather x1, blocking collectives, local(): all_feats = lax.all_gather(image_feats, AXES[1:], axis=0, tiled=True)  11.3 us
    ppermute x20, waiting for transfers between devices, swapped(): lax.ppermute(value, AXES, [(source, source ^ mask) for source in range(to...  8.84 us
    unnamed x20, local copies, waits for them, and re-layouts  6.97 us
    pallas_call x1, Pallas kernels, local(): pl.pallas_call(functools.partial(pair_kernel, narrow, group, spread), in_...  4.59 us
    pallas_call x1, Pallas kernels, local(): pl.pallas_call(functools.partial(weight_kernel, group, wide), in_specs=[S...  1.7 us
    pallas_call x1, Pallas kernels, local(): pl.pallas_call(functools.partial(caption_kernel, rows), in_specs=[VMEM] *...  1.65 us
  transfers between devices with their start and end apart: 20, of which 5 were waited for; matrix products, arithmetic and copies ran while one was open for 1% of the time, Pallas kernels for 6%

profile of v3, /device:TPU:0, one launch (start us, length us, event | category | flops | bytes accessed | tf_op | source)
XLA Modules:
  0.0 66.9 jit_solution(16744743364774962412)
XLA Ops:
  0.6 3.1 %collective-permute-start = (bf16[48,1152]{1,0:T(8,128)(2,1)}, bf16[48,1152]{1,0:T(8,128)(2,1)}, u32[]{:S(2)}, u32[]{:S(2)}) collective-permute-start(bf16[48,1152]{1,0:T(8,128)(2,1)} %refs_5_.1), channel_id=1, source_target_pairs={{0,8},{1,9},{2,10},{3,11},{4,12},{5,13},{6,14},{7,15},{8,0},{9,1},... | collective-permute-start | bytes 331784 | tf_op jit(solution)/shard_map/ppermute | solution.py:23
  3.7 2.6 %collective-permute-start.1 = (bf16[48,1152]{1,0:T(8,128)(2,1)}, bf16[48,1152]{1,0:T(8,128)(2,1)}, u32[]{:S(2)}, u32[]{:S(2)}) collective-permute-start(bf16[48,1152]{1,0:T(8,128)(2,1)} %refs_5_.1), channel_id=1, source_target_pairs={{0,16},{1,17},{2,18},{3,19},{4,20},{5,21},{6,22},{7,23},{8,24},{9,... | collective-permute-start | bytes 331784 | tf_op jit(solution)/shard_map/ppermute | solution.py:23
  7.6 1.7 %copy-done = bf16[1152,1152]{1,0:T(8,128)(2,1)S(1)} copy-done((bf16[1152,1152]{1,0:T(8,128)(2,1)S(1)}, bf16[1152,1152]{1,0:T(8,128)(2,1)}, u32[]{:S(2)}) %copy-start) | copy-done | bytes 2654232
  9.6 11.3 %all_gather.3.refs_4_.feats_ref.refs_11_ = bf16[384,1152]{1,0:T(8,128)(2,1)S(1)} all-gather(bf16[48,1152]{1,0:T(8,128)(2,1)} %param.5), channel_id=1, replica_groups=mesh['outer'=4,'inner'=2,'narrow'=4] {'inner','narrow'}, dimensions={0}, use_global_device_ids=true | all-gather | bytes 995328 | tf_op jit(solution)/shard_map/all_gather | solution.py:217
  20.9 0.9 %copy-done.5 = bf16[48,1152]{1,0:T(8,128)(2,1)S(1)} copy-done((bf16[48,1152]{1,0:T(8,128)(2,1)S(1)}, bf16[48,1152]{1,0:T(8,128)(2,1)}, u32[]{:S(2)}) %copy-start.5) | copy-done | bytes 110616
  21.8 4.6 %pairs.1 = (f32[144,384]{1,0:T(8,128)S(1)}, f32[1,384]{1,0:T(1,128)S(1)}, bf16[1152,384]{1,0:T(8,128)(2,1)S(1)}, bf16[192,384]{1,0:T(8,128)(2,1)S(1)}, f32[152,3...) custom-call(s32[1]{0:T(128)} %bitcast.1.refs_0_, ...), custom_call_target="tpu_custom_call" | custom-call | tf_op jit(solution)/shard_map/pairs/pallas_call | solution.py:228
  26.7 1.1 %collective-permute-start.4 = (bf16[160,384]{1,0:T(8,128)(2,1)S(1)}, bf16[160,384]{1,0:T(8,128)(2,1)S(1)}, u32[]{:S(2)}, u32[]{:S(2)}) collective-permute-start(bf16[160,384]{1,0:T(8,128)(2,1)S(1)} %get-tuple-element.31), channel_id=1, source_target_pairs={{0,2},{1,3},{2,0},{3,1},{4,6},{5,7},{6,4},{7,5},{8,10},{9,11},{10,... | collective-permute-start | bytes 368648 | tf_op jit(solution)/shard_map/ppermute | solution.py:23
  28.2 1.1 %collective-permute-start.6 = (bf16[160,384]{1,0:T(8,128)(2,1)S(1)}, bf16[160,384]{1,0:T(8,128)(2,1)S(1)}, u32[]{:S(2)}, u32[]{:S(2)}) collective-permute-start(bf16[160,384]{1,0:T(8,128)(2,1)S(1)} %get-tuple-element.33), channel_id=1, source_target_pairs={{0,4},{1,5},{2,6},{3,7},{4,0},{5,1},{6,2},{7,3},{8,12},{9,13},{10,... | collective-permute-start | bytes 368648 | tf_op jit(solution)/shard_map/ppermute | solution.py:23
  30.2 1.4 %collective-permute-start.8 = (bf16[160,384]{1,0:T(8,128)(2,1)}, bf16[160,384]{1,0:T(8,128)(2,1)S(1)}, u32[]{:S(2)}, u32[]{:S(2)}) collective-permute-start(bf16[160,384]{1,0:T(8,128)(2,1)} %get-tuple-element.35), channel_id=1, source_target_pairs={{0,6},{1,7},{2,4},{3,5},{4,2},{5,3},{6,0},{7,1},{8,14},{9,15},{10,... | collective-permute-start | bytes 368648 | tf_op jit(solution)/shard_map/ppermute | solution.py:23
  31.6 1.2 %collective-permute-done.4.refs_3_ = bf16[160,384]{1,0:T(8,128)(2,1)S(1)} collective-permute-done((bf16[160,384]{1,0:T(8,128)(2,1)S(1)}, bf16[160,384]{1,0:T(8,128)(2,1)S(1)}, u32[]{:S(2)}, u32[]{:S(2)}) %collective-permute-start.4) | collective-permute-done | bytes 122912 | tf_op jit(solution)/shard_map/ppermute | solution.py:23
  32.9 1.7 %captions.1 = (bf16[1152,384]{1,0:T(8,128)(2,1)S(1)}, f32[48,1152]{1,0:T(8,128)S(1)}, bf16[48,1152]{1,0:T(8,128)(2,1)}, bf16[48,1152]{1,0:T(8,128)(2,1)S(1)}, bf16[48,1152]{1,0:T(8,128)(2,1)S(1)}) custom-call(bf16[192,384]{1,0:T(8,128)(2,1)S(1)} %get-tuple-element.39.grad_ref, bf16[1152,384]{1,0:T(8,128)(2,1)S(1)} %get-tuple-element.40.emb_ref, ...), custom_call_target="tpu_custom_call" | custom-call | tf_op jit(solution)/shard_map/captions/pallas_call | solution.py:251
  35.3 3.5 %collective-permute-start.11 = (bf16[48,1152]{1,0:T(8,128)(2,1)S(1)}, bf16[48,1152]{1,0:T(8,128)(2,1)S(1)}, u32[]{:S(2)}, u32[]{:S(2)}) collective-permute-start(bf16[48,1152]{1,0:T(8,128)(2,1)S(1)} %get-tuple-element.45), channel_id=1, source_target_pairs={{0,16},{1,17},{2,18},{3,19},{4,20},{5,21},{6,22},{7,23},{8,24},{9,... | collective-permute-start | bytes 331784 | tf_op jit(solution)/shard_map/ppermute | solution.py:23
  38.8 1.2 %collective-permute-start.12 = (bf16[48,1152]{1,0:T(8,128)(2,1)S(1)}, bf16[48,1152]{1,0:T(8,128)(2,1)S(1)}, u32[]{:S(2)}, u32[]{:S(2)}) collective-permute-start(bf16[48,1152]{1,0:T(8,128)(2,1)S(1)} %get-tuple-element.46), channel_id=1, source_target_pairs={{0,24},{1,25},{2,26},{3,27},{4,28},{5,29},{6,30},{7,31},{8,16},{9,... | collective-permute-start | bytes 331784 | tf_op jit(solution)/shard_map/ppermute | solution.py:23
  40.3 2.0 %collective-permute-done.9.refs_8_ = bf16[160,384]{1,0:T(8,128)(2,1)S(1)} collective-permute-done((bf16[160,384]{1,0:T(8,128)(2,1)}, bf16[160,384]{1,0:T(8,128)(2,1)S(1)}, u32[]{:S(2)}, u32[]{:S(2)}) %collective-permute-start.9) | collective-permute-done | bytes 122912 | tf_op jit(solution)/shard_map/ppermute | solution.py:23
  42.2 0.9 %copy-done.2 = f32[152,384]{1,0:T(8,128)S(1)} copy-done((f32[152,384]{1,0:T(8,128)S(1)}, f32[152,384]{1,0:T(8,128)}, u32[]{:S(2)}) %copy-start.2) | copy-done | bytes 233496
  43.2 0.9 %copy-done.4 = f32[144,384]{1,0:T(8,128)S(1)} copy-done((f32[144,384]{1,0:T(8,128)S(1)}, f32[144,384]{1,0:T(8,128)}, u32[]{:S(2)}) %copy-start.4) | copy-done | bytes 221208
  44.1 1.7 %weights.1 = (f32[1,384]{1,0:T(1,128)S(1)}, f32[176,128]{1,0:T(8,128)S(1)}, bf16[176,128]{1,0:T(8,128)(2,1)}, bf16[176,128]{1,0:T(8,128)(2,1)}, bf16[176,128]{1,...) custom-call(s32[1]{0:T(128)} %bitcast.refs_0_.wide_ref, ...), custom_call_target="tpu_custom_call" | custom-call | tf_op jit(solution)/shard_map/weights/pallas_call | solution.py:268
  50.6 1.9 %collective-permute-start.15 = (bf16[176,128]{1,0:T(8,128)(2,1)}, bf16[176,128]{1,0:T(8,128)(2,1)S(1)}, u32[]{:S(2)}, u32[]{:S(2)}) collective-permute-start(bf16[176,128]{1,0:T(8,128)(2,1)} %copy-done.9), channel_id=1, source_target_pairs={{0,12},{1,13},{2,14},{3,15},{4,8},{5,9},{6,10},{7,11},{8,4},{9,5},... | collective-permute-start | bytes 135176 | tf_op jit(solution)/shard_map/ppermute | solution.py:23
  52.5 2.2 %collective-permute-start.16 = (bf16[176,128]{1,0:T(8,128)(2,1)}, bf16[176,128]{1,0:T(8,128)(2,1)S(1)}, u32[]{:S(2)}, u32[]{:S(2)}) collective-permute-start(bf16[176,128]{1,0:T(8,128)(2,1)} %copy-done.8), channel_id=1, source_target_pairs={{0,16},{1,17},{2,18},{3,19},{4,20},{5,21},{6,22},{7,23},{8,24},{9,... | collective-permute-start | bytes 135176 | tf_op jit(solution)/shard_map/ppermute | solution.py:23
  54.7 1.1 %collective-permute-start.17 = (bf16[176,128]{1,0:T(8,128)(2,1)}, bf16[176,128]{1,0:T(8,128)(2,1)S(1)}, u32[]{:S(2)}, u32[]{:S(2)}) collective-permute-start(bf16[176,128]{1,0:T(8,128)(2,1)} %copy-done.7), channel_id=1, source_target_pairs={{0,20},{1,21},{2,22},{3,23},{4,16},{5,17},{6,18},{7,19},{8,28},{9,... | collective-permute-start | bytes 135176 | tf_op jit(solution)/shard_map/ppermute | solution.py:23
  55.7 3.6 %collective-permute-start.18 = (bf16[176,128]{1,0:T(8,128)(2,1)}, bf16[176,128]{1,0:T(8,128)(2,1)S(1)}, u32[]{:S(2)}, u32[]{:S(2)}) collective-permute-start(bf16[176,128]{1,0:T(8,128)(2,1)} %copy-done.6), channel_id=1, source_target_pairs={{0,24},{1,25},{2,26},{3,27},{4,28},{5,29},{6,30},{7,31},{8,16},{9,... | collective-permute-start | bytes 135176 | tf_op jit(solution)/shard_map/ppermute | solution.py:23
  60.7 2.2 %collective-permute-done.17.refs_5_ = bf16[176,128]{1,0:T(8,128)(2,1)S(1)} collective-permute-done((bf16[176,128]{1,0:T(8,128)(2,1)}, bf16[176,128]{1,0:T(8,128)(2,1)S(1)}, u32[]{:S(2)}, u32[]{:S(2)}) %collective-permute-start.17) | collective-permute-done | bytes 45088 | tf_op jit(solution)/shard_map/ppermute | solution.py:23
  63.0 3.1 %collective-permute-done.19.refs_7_ = bf16[176,128]{1,0:T(8,128)(2,1)S(1)} collective-permute-done((bf16[176,128]{1,0:T(8,128)(2,1)S(1)}, bf16[176,128]{1,0:T(8,128)(2,1)S(1)}, u32[]{:S(2)}, u32[]{:S(2)}) %collective-permute-start.19) | collective-permute-done | bytes 45088 | tf_op jit(solution)/shard_map/ppermute | solution.py:23
  66.1 0.9 %weight_total.1 = f32[144,288]{1,0:T(8,128)} custom-call(s32[1]{0:T(128)} %bitcast.refs_0_.wide_ref, f32[176,128]{1,0:T(8,128)S(1)} %get-tuple-element.47.refs_0_, bf16[176,128]{1,0:T(8,128)(2,1)S(1)} %collective-permute-done.13.refs_1_, bf16[176,128]{1,0:T(8,128)(2,1)S(1)} %collective-permute-done.14.refs_2_, ...), custom_call_target="tpu_custom_call" | custom-call | tf_op jit(solution)/shard_map/weight_total/pallas_call | solution.py:286
  (44 shorter events, 9.0 us)
Async XLA Ops:
  0.6 20.2 %collective-permute-start = (bf16[48,1152]{1,0:T(8,128)(2,1)}, bf16[48,1152]{1,0:T(8,128)(2,1)}, u32[]{:S(2)}, u32[]{:S(2)}) collective-permute-start(bf16[48,1152]{1,0:T(8,128)(2,1)} %refs_5_.1), channel_id=1, source_target_pairs={{0,8},{1,9},{2,10},{3,11},{4,12},{5,13},{6,14},{7,15},{8,0},{9,1},... | collective-permute-start | bytes 331784 | tf_op jit(solution)/shard_map/ppermute | solution.py:23
  3.7 17.1 %collective-permute-start.1 = (bf16[48,1152]{1,0:T(8,128)(2,1)}, bf16[48,1152]{1,0:T(8,128)(2,1)}, u32[]{:S(2)}, u32[]{:S(2)}) collective-permute-start(bf16[48,1152]{1,0:T(8,128)(2,1)} %refs_5_.1), channel_id=1, source_target_pairs={{0,16},{1,17},{2,18},{3,19},{4,20},{5,21},{6,22},{7,23},{8,24},{9,... | collective-permute-start | bytes 331784 | tf_op jit(solution)/shard_map/ppermute | solution.py:23
  6.3 14.5 %collective-permute-start.2 = (bf16[48,1152]{1,0:T(8,128)(2,1)}, bf16[48,1152]{1,0:T(8,128)(2,1)}, u32[]{:S(2)}, u32[]{:S(2)}) collective-permute-start(bf16[48,1152]{1,0:T(8,128)(2,1)} %refs_5_.1), channel_id=1, source_target_pairs={{0,24},{1,25},{2,26},{3,27},{4,28},{5,29},{6,30},{7,31},{8,16},{9,... | collective-permute-start | bytes 331784 | tf_op jit(solution)/shard_map/ppermute | solution.py:23
  7.6 1.8 %copy-start = (bf16[1152,1152]{1,0:T(8,128)(2,1)S(1)}, bf16[1152,1152]{1,0:T(8,128)(2,1)}, u32[]{:S(2)}) copy-start(bf16[1152,1152]{1,0:T(8,128)(2,1)} %weight_ref.1) | copy-start | bytes 7962628
  26.4 8.2 %copy-start.1 = (f32[152,384]{1,0:T(8,128)}, f32[152,384]{1,0:T(8,128)S(1)}, u32[]{:S(2)}) copy-start(f32[152,384]{1,0:T(8,128)S(1)} %get-tuple-element.29.refs_1_) | copy-start | bytes 700420
  26.4 8.2 %copy-start.3 = (f32[144,384]{1,0:T(8,128)}, f32[144,384]{1,0:T(8,128)S(1)}, u32[]{:S(2)}) copy-start(f32[144,384]{1,0:T(8,128)S(1)} %get-tuple-element.37.refs_9_) | copy-start | bytes 663556
  26.4 3.9 %collective-permute-start.3 = (bf16[160,384]{1,0:T(8,128)(2,1)S(1)}, bf16[160,384]{1,0:T(8,128)(2,1)S(1)}, u32[]{:S(2)}, u32[]{:S(2)}) collective-permute-start(bf16[160,384]{1,0:T(8,128)(2,1)S(1)} %get-tuple-element.30), channel_id=1, source_target_pairs={{0,1},{1,0},{2,3},{3,2},{4,5},{5,4},{6,7},{7,6},{8,9},{9,8},{10,11... | collective-permute-start | bytes 368648 | tf_op jit(solution)/shard_map/ppermute | solution.py:23
  26.7 6.2 %collective-permute-start.4 = (bf16[160,384]{1,0:T(8,128)(2,1)S(1)}, bf16[160,384]{1,0:T(8,128)(2,1)S(1)}, u32[]{:S(2)}, u32[]{:S(2)}) collective-permute-start(bf16[160,384]{1,0:T(8,128)(2,1)S(1)} %get-tuple-element.31), channel_id=1, source_target_pairs={{0,2},{1,3},{2,0},{3,1},{4,6},{5,7},{6,4},{7,5},{8,10},{9,11},{10,... | collective-permute-start | bytes 368648 | tf_op jit(solution)/shard_map/ppermute | solution.py:23
  27.9 6.7 %collective-permute-start.5 = (bf16[160,384]{1,0:T(8,128)(2,1)S(1)}, bf16[160,384]{1,0:T(8,128)(2,1)S(1)}, u32[]{:S(2)}, u32[]{:S(2)}) collective-permute-start(bf16[160,384]{1,0:T(8,128)(2,1)S(1)} %get-tuple-element.32), channel_id=1, source_target_pairs={{0,3},{1,2},{2,1},{3,0},{4,7},{5,6},{6,5},{7,4},{8,11},{9,10},{10,... | collective-permute-start | bytes 368648 | tf_op jit(solution)/shard_map/ppermute | solution.py:23
  28.2 7.1 %collective-permute-start.6 = (bf16[160,384]{1,0:T(8,128)(2,1)S(1)}, bf16[160,384]{1,0:T(8,128)(2,1)S(1)}, u32[]{:S(2)}, u32[]{:S(2)}) collective-permute-start(bf16[160,384]{1,0:T(8,128)(2,1)S(1)} %get-tuple-element.33), channel_id=1, source_target_pairs={{0,4},{1,5},{2,6},{3,7},{4,0},{5,1},{6,2},{7,3},{8,12},{9,13},{10,... | collective-permute-start | bytes 368648 | tf_op jit(solution)/shard_map/ppermute | solution.py:23
  29.4 9.4 %collective-permute-start.7 = (bf16[160,384]{1,0:T(8,128)(2,1)S(1)}, bf16[160,384]{1,0:T(8,128)(2,1)S(1)}, u32[]{:S(2)}, u32[]{:S(2)}) collective-permute-start(bf16[160,384]{1,0:T(8,128)(2,1)S(1)} %get-tuple-element.34), channel_id=1, source_target_pairs={{0,5},{1,4},{2,7},{3,6},{4,1},{5,0},{6,3},{7,2},{8,13},{9,12},{10,... | collective-permute-start | bytes 368648 | tf_op jit(solution)/shard_map/ppermute | solution.py:23
  30.2 10.0 %collective-permute-start.8 = (bf16[160,384]{1,0:T(8,128)(2,1)}, bf16[160,384]{1,0:T(8,128)(2,1)S(1)}, u32[]{:S(2)}, u32[]{:S(2)}) collective-permute-start(bf16[160,384]{1,0:T(8,128)(2,1)} %get-tuple-element.35), channel_id=1, source_target_pairs={{0,6},{1,7},{2,4},{3,5},{4,2},{5,3},{6,0},{7,1},{8,14},{9,15},{10,... | collective-permute-start | bytes 368648 | tf_op jit(solution)/shard_map/ppermute | solution.py:23
  32.9 9.3 %collective-permute-start.9 = (bf16[160,384]{1,0:T(8,128)(2,1)}, bf16[160,384]{1,0:T(8,128)(2,1)S(1)}, u32[]{:S(2)}, u32[]{:S(2)}) collective-permute-start(bf16[160,384]{1,0:T(8,128)(2,1)} %get-tuple-element.36), channel_id=1, source_target_pairs={{0,7},{1,6},{2,5},{3,4},{4,3},{5,2},{6,1},{7,0},{8,15},{9,14},{10,... | collective-permute-start | bytes 368648 | tf_op jit(solution)/shard_map/ppermute | solution.py:23
  34.5 15.3 %collective-permute-start.10 = (bf16[48,1152]{1,0:T(8,128)(2,1)}, bf16[48,1152]{1,0:T(8,128)(2,1)S(1)}, u32[]{:S(2)}, u32[]{:S(2)}) collective-permute-start(bf16[48,1152]{1,0:T(8,128)(2,1)} %get-tuple-element.44), channel_id=1, source_target_pairs={{0,8},{1,9},{2,10},{3,11},{4,12},{5,13},{6,14},{7,15},{8,0},{9,1},... | collective-permute-start | bytes 331784 | tf_op jit(solution)/shard_map/ppermute | solution.py:23
  35.3 14.5 %collective-permute-start.11 = (bf16[48,1152]{1,0:T(8,128)(2,1)S(1)}, bf16[48,1152]{1,0:T(8,128)(2,1)S(1)}, u32[]{:S(2)}, u32[]{:S(2)}) collective-permute-start(bf16[48,1152]{1,0:T(8,128)(2,1)S(1)} %get-tuple-element.45), channel_id=1, source_target_pairs={{0,16},{1,17},{2,18},{3,19},{4,20},{5,21},{6,22},{7,23},{8,24},{9,... | collective-permute-start | bytes 331784 | tf_op jit(solution)/shard_map/ppermute | solution.py:23
  38.8 11.0 %collective-permute-start.12 = (bf16[48,1152]{1,0:T(8,128)(2,1)S(1)}, bf16[48,1152]{1,0:T(8,128)(2,1)S(1)}, u32[]{:S(2)}, u32[]{:S(2)}) collective-permute-start(bf16[48,1152]{1,0:T(8,128)(2,1)S(1)} %get-tuple-element.46), channel_id=1, source_target_pairs={{0,24},{1,25},{2,26},{3,27},{4,28},{5,29},{6,30},{7,31},{8,16},{9,... | collective-permute-start | bytes 331784 | tf_op jit(solution)/shard_map/ppermute | solution.py:23
  42.2 0.9 %copy-start.2 = (f32[152,384]{1,0:T(8,128)S(1)}, f32[152,384]{1,0:T(8,128)}, u32[]{:S(2)}) copy-start(f32[152,384]{1,0:T(8,128)} %copy-done.1) | copy-start | bytes 700420
  48.3 7.5 %collective-permute-start.13 = (bf16[176,128]{1,0:T(8,128)(2,1)}, bf16[176,128]{1,0:T(8,128)(2,1)S(1)}, u32[]{:S(2)}, u32[]{:S(2)}) collective-permute-start(bf16[176,128]{1,0:T(8,128)(2,1)} %get-tuple-element.48), channel_id=1, source_target_pairs={{0,4},{1,5},{2,6},{3,7},{4,0},{5,1},{6,2},{7,3},{8,12},{9,13},{10,... | collective-permute-start | bytes 135176 | tf_op jit(solution)/shard_map/ppermute | solution.py:23
  49.1 10.2 %collective-permute-start.14 = (bf16[176,128]{1,0:T(8,128)(2,1)}, bf16[176,128]{1,0:T(8,128)(2,1)S(1)}, u32[]{:S(2)}, u32[]{:S(2)}) collective-permute-start(bf16[176,128]{1,0:T(8,128)(2,1)} %get-tuple-element.49), channel_id=1, source_target_pairs={{0,8},{1,9},{2,10},{3,11},{4,12},{5,13},{6,14},{7,15},{8,0},{9,1},... | collective-permute-start | bytes 135176 | tf_op jit(solution)/shard_map/ppermute | solution.py:23
  50.6 10.2 %collective-permute-start.15 = (bf16[176,128]{1,0:T(8,128)(2,1)}, bf16[176,128]{1,0:T(8,128)(2,1)S(1)}, u32[]{:S(2)}, u32[]{:S(2)}) collective-permute-start(bf16[176,128]{1,0:T(8,128)(2,1)} %copy-done.9), channel_id=1, source_target_pairs={{0,12},{1,13},{2,14},{3,15},{4,8},{5,9},{6,10},{7,11},{8,4},{9,5},... | collective-permute-start | bytes 135176 | tf_op jit(solution)/shard_map/ppermute | solution.py:23
  52.5 8.2 %collective-permute-start.16 = (bf16[176,128]{1,0:T(8,128)(2,1)}, bf16[176,128]{1,0:T(8,128)(2,1)S(1)}, u32[]{:S(2)}, u32[]{:S(2)}) collective-permute-start(bf16[176,128]{1,0:T(8,128)(2,1)} %copy-done.8), channel_id=1, source_target_pairs={{0,16},{1,17},{2,18},{3,19},{4,20},{5,21},{6,22},{7,23},{8,24},{9,... | collective-permute-start | bytes 135176 | tf_op jit(solution)/shard_map/ppermute | solution.py:23
  54.7 8.3 %collective-permute-start.17 = (bf16[176,128]{1,0:T(8,128)(2,1)}, bf16[176,128]{1,0:T(8,128)(2,1)S(1)}, u32[]{:S(2)}, u32[]{:S(2)}) collective-permute-start(bf16[176,128]{1,0:T(8,128)(2,1)} %copy-done.7), channel_id=1, source_target_pairs={{0,20},{1,21},{2,22},{3,23},{4,16},{5,17},{6,18},{7,19},{8,28},{9,... | collective-permute-start | bytes 135176 | tf_op jit(solution)/shard_map/ppermute | solution.py:23
  55.7 7.2 %collective-permute-start.18 = (bf16[176,128]{1,0:T(8,128)(2,1)}, bf16[176,128]{1,0:T(8,128)(2,1)S(1)}, u32[]{:S(2)}, u32[]{:S(2)}) collective-permute-start(bf16[176,128]{1,0:T(8,128)(2,1)} %copy-done.6), channel_id=1, source_target_pairs={{0,24},{1,25},{2,26},{3,27},{4,28},{5,29},{6,30},{7,31},{8,16},{9,... | collective-permute-start | bytes 135176 | tf_op jit(solution)/shard_map/ppermute | solution.py:23
  59.3 6.7 %collective-permute-start.19 = (bf16[176,128]{1,0:T(8,128)(2,1)S(1)}, bf16[176,128]{1,0:T(8,128)(2,1)S(1)}, u32[]{:S(2)}, u32[]{:S(2)}) collective-permute-start(bf16[176,128]{1,0:T(8,128)(2,1)S(1)} %get-tuple-element.54), channel_id=1, source_target_pairs={{0,28},{1,29},{2,30},{3,31},{4,24},{5,25},{6,26},{7,27},{8,20},{9,... | collective-permute-start | bytes 135176 | tf_op jit(solution)/shard_map/ppermute | solution.py:23
  (6 other events, 4.3 us)

commit v4 on v3

--- a/solution.py
+++ b/solution.py
@@ -16,7 +16,12 @@
 SMEM = pl.BlockSpec(memory_space=pltpu.SMEM)
 NT = (((1,), (1,)), ((), ()))
 TN = (((0,), (0,)), ((), ()))
-PARAMS = pltpu.CompilerParams(vmem_limit_bytes=40 * 1024 * 1024)
+ANY = pl.BlockSpec(memory_space=pl.ANY)
+MIB = 1024 * 1024
+
+
+def limit(mebibytes):
+    return pltpu.CompilerParams(vmem_limit_bytes=mebibytes * MIB)
 
 
 def swapped(value, total, mask):
@@ -30,10 +35,6 @@
 
 def column_block(member, narrow):
     return (member % narrow) * 2 + member // narrow
-
-
-def load_kernel(weight_ref, out):
-    pltpu.sync_copy(weight_ref, out)
 
 
 def pair_kernel(narrow, group, spread, *refs):
@@ -42,15 +43,27 @@
     outs = refs[5 + spread :]
     unit_out, inv_out, emb_out, grad_out, own_out = outs[:5]
     send_out = outs[5 : 4 + group]
-    unit_all, text_all, d_all = outs[4 + group :]
+    unit_all, text_all, d_all, weight, own_text, sems = outs[4 + group :]
     rows, width = texts[0].shape
     images = group * rows
     share = width // group
     member = member_ref[0]
-
+    text_copy = pltpu.make_async_copy(texts[0], own_text, sems.at[0])
+    weight_copy = pltpu.make_async_copy(weight_ref, weight, sems.at[1])
+    text_copy.start()
+    weight_copy.start()
+
+    for step in [*range(1, spread), 0]:
+        if step == 0:
+            text_copy.wait()
+        values = (texts[step] if step else own_text)[...].astype(F32)
+        inverse = lax.rsqrt(jnp.sum(values * values, axis=1, keepdims=True) + 1e-06)
+        text_all[step * rows : (step + 1) * rows, :] = (values * inverse).astype(BF16)
+
+    weight_copy.wait()
     for start in range(0, images, LANES):
         cols = slice(start, start + LANES)
-        proj = jnp.dot(feats_ref[cols, :], weight_ref[...], preferred_element_type=F32)
+        proj = jnp.dot(feats_ref[cols, :], weight[...], preferred_element_type=F32)
         turned = proj.T
         inverse = lax.rsqrt(jnp.sum(turned * turned, axis=0, keepdims=True) + 1e-06)
         unit = turned * inverse
@@ -59,11 +72,6 @@
         emb_out[:, cols] = unit.astype(BF16)
     block = pl.multiple_of(column_block(member, narrow) * share, share)
     unit_out[...] = unit_all[pl.ds(block, share), :]
-
-    for step in range(spread):
-        values = texts[step][...].astype(F32)
-        inverse = lax.rsqrt(jnp.sum(values * values, axis=1, keepdims=True) + 1e-06)
-        text_all[step * rows : (step + 1) * rows, :] = (values * inverse).astype(BF16)
 
     scale = jnp.exp(jnp.full((1, 1), log_scale_ref[0], F32))
     shift = bias_ref[0]
@@ -143,55 +151,38 @@
 
 
 def weight_kernel(group, wide, *refs):
-    wide_ref, own_ref = refs[:2]
-    got = refs[2 : 1 + group]
-    unit_ref, inv_ref, feats_ref, feats_t_ref = refs[1 + group : 5 + group]
-    loss_out, own_out = refs[5 + group : 7 + group]
-    send_out = refs[7 + group : 6 + group + wide]
-    main_all, rest_all = refs[6 + group + wide :]
+    own_ref = refs[0]
+    got = refs[1:group]
+    unit_ref, inv_ref, feats_ref, feats_t_ref, loss_out, send_out = refs[group:]
     share = unit_ref.shape[0]
     rest = share - LANES
     rows = feats_t_ref.shape[0] // wide
-    d_zproj = gathered_gradient(own_ref, got, unit_ref, inv_ref, loss_out)
-    high, low = split_pair(d_zproj)
-    main_all[...] = lax.dot_general(
+    high, low = split_pair(gathered_gradient(own_ref, got, unit_ref, inv_ref, loss_out))
+    main = lax.dot_general(
         feats_t_ref[...], high[:LANES, :], NT, preferred_element_type=F32
     ) + lax.dot_general(feats_t_ref[...], low[:LANES, :], NT, preferred_element_type=F32)
     tail = jnp.dot(high[LANES:, :], feats_ref[...], preferred_element_type=F32) + jnp.dot(
         low[LANES:, :], feats_ref[...], preferred_element_type=F32
     )
-    rest_all[...] = jnp.zeros_like(rest_all)
+    main, tail = main.astype(BF16), tail.astype(BF16)
     for place in range(wide):
         begin = place * rows
-        rest_all[place, :rest, :] = tail[:, begin : begin + LANES]
-        rest_all[place, rest:, : rows - LANES] = tail[:, begin + LANES : begin + rows]
-    here = wide_ref[0]
-    for step in range(wide):
-        place = here ^ step
-        begin = pl.multiple_of(place * rows, rows)
-        target = own_out if step == 0 else send_out[step - 1]
-        target[:rows, :] = main_all[pl.ds(begin, rows), :].astype(target.dtype)
-        target[rows:, :] = rest_all[place].astype(target.dtype)
-
-
-def total_kernel(rest, wide_ref, *refs):
-    blocks, out = refs[:-1], refs[-1]
+        send_out[place, :rows, :] = main[begin : begin + rows, :]
+        send_out[place, rows : rows + rest, :] = tail[:, begin : begin + LANES]
+        send_out[place, rows + rest :, :] = jnp.zeros((rest, LANES), BF16)
+        send_out[place, rows + rest :, : rows - LANES] = tail[:, begin + LANES : begin + rows]
+
+
+def total_kernel(rest, got_ref, out):
     rows = out.shape[0]
-    even = blocks[0][...]
-    for block in blocks[2::2]:
-        even = even + block[...].astype(F32)
-    odd = blocks[1][...].astype(F32)
-    for block in blocks[3::2]:
-        odd = odd + block[...].astype(F32)
-    mine = (wide_ref[0] & 1) == 0
-    halves = (jnp.where(mine, even, odd), jnp.where(mine, odd, even))
-    for side, half in enumerate(halves):
+    for side in range(2):
+        half = got_ref[side].astype(F32)
+        for place in range(side + 2, got_ref.shape[0], 2):
+            half = half + got_ref[place].astype(F32)
         left = side * (LANES + rest)
         out[:, left : left + LANES] = half[:rows, :]
-        upper = half[rows : rows + rest, :].T
-        lower = half[rows + rest :, :].T
-        out[:LANES, left + LANES : left + LANES + rest] = upper
-        out[LANES:, left + LANES : left + LANES + rest] = lower[: rows - LANES, :]
+        out[:LANES, left + LANES : left + LANES + rest] = half[rows : rows + rest, :].T
+        out[LANES:, left + LANES : left + LANES + rest] = half[rows + rest :, :].T[: rows - LANES, :]
 
 
 def sum_kernel(*refs):
@@ -208,26 +199,15 @@
     spread = wide // 2
     share = width // group
     images = group * rows
-    wide_pos = lax.axis_index(AXES[:2]).astype(jnp.int32)
-    member = lax.axis_index(AXES[1:]).astype(jnp.int32)
-    wide_pos, member = wide_pos.reshape(1), member.reshape(1)
+    member = lax.axis_index(AXES[1:]).astype(jnp.int32).reshape(1)
 
     texts = [text_embed] + [swapped(text_embed, total, step * group) for step in range(1, spread)]
 
     all_feats = lax.all_gather(image_feats, AXES[1:], axis=0, tiled=True)
-    weight = pl.pallas_call(
-        load_kernel,
-        in_specs=[pl.BlockSpec(memory_space=pl.ANY)],
-        out_specs=VMEM,
-        out_shape=jax.ShapeDtypeStruct((width, width), BF16),
-        compiler_params=PARAMS,
-        name="load_weight",
-    )(proj_weight)
-
     sent = jax.ShapeDtypeStruct((share + STAT_ROWS, images), BF16)
     results = pl.pallas_call(
         functools.partial(pair_kernel, narrow, group, spread),
-        in_specs=[SMEM] * 3 + [VMEM] * (2 + spread),
+        in_specs=[SMEM] * 3 + [ANY, VMEM, ANY] + [VMEM] * (spread - 1),
         out_specs=[VMEM] * (4 + group),
         out_shape=[
             jax.ShapeDtypeStruct((share, images), F32),
@@ -241,10 +221,13 @@
             pltpu.VMEM((width, images), F32),
             pltpu.VMEM((spread * rows, width), BF16),
             pltpu.VMEM((width, images), F32),
+            pltpu.VMEM((width, width), BF16),
+            pltpu.VMEM((rows, width), BF16),
+            pltpu.SemaphoreType.DMA((2,)),
         ],
-        compiler_params=PARAMS,
+        compiler_params=limit(24 if spread <= 4 else 40),
         name="pairs",
-    )(member, log_scale, logit_bias, weight, all_feats, *texts)
+    )(member, log_scale, logit_bias, proj_weight, all_feats, *texts)
     unit_part, inv_part, img_emb, grad_tile, own_part = results[:5]
     got = [swapped(value, total, step) for step, value in enumerate(results[5:], 1)]
 
@@ -254,7 +237,7 @@
         out_specs=[VMEM] * (1 + spread),
         out_shape=[jax.ShapeDtypeStruct((width, images), BF16), jax.ShapeDtypeStruct((rows, width), F32)]
         + [jax.ShapeDtypeStruct((rows, width), BF16)] * (spread - 1),
-        compiler_params=PARAMS,
+        compiler_params=limit(12 if spread <= 4 else 24),
         name="captions",
     )(grad_tile, img_emb, all_feats)
     feats_t, own_text = results[:2]
@@ -265,32 +248,26 @@
     packed = out_rows + 2 * rest
     direct = LANES < out_rows <= 2 * LANES and out_rows % 16 == 0 and rest % 16 == 0
     if direct:
-        results = pl.pallas_call(
+        loss_line, sent_weight = pl.pallas_call(
             functools.partial(weight_kernel, group, wide),
-            in_specs=[SMEM] + [VMEM] * (4 + group),
-            out_specs=[VMEM] * (1 + wide),
+            in_specs=[VMEM] * (4 + group),
+            out_specs=[VMEM] * 2,
             out_shape=[
                 jax.ShapeDtypeStruct((1, images), F32),
-                jax.ShapeDtypeStruct((packed, LANES), F32),
-            ]
-            + [jax.ShapeDtypeStruct((packed, LANES), BF16)] * (wide - 1),
-            scratch_shapes=[
-                pltpu.VMEM((width, LANES), F32),
-                pltpu.VMEM((wide, 2 * rest, LANES), F32),
+                jax.ShapeDtypeStruct((wide, packed, LANES), BF16),
             ],
-            compiler_params=PARAMS,
+            compiler_params=limit(12),
             name="weights",
-        )(wide_pos, own_part, *got, unit_part, inv_part, all_feats, feats_t)
-        loss_line, own_weight = results[:2]
-        got_weight = [swapped(value, total, step * narrow) for step, value in enumerate(results[2:], 1)]
+        )(own_part, *got, unit_part, inv_part, all_feats, feats_t)
+        got_weight = lax.all_to_all(sent_weight, AXES[:2], 0, 0)
         d_proj = pl.pallas_call(
             functools.partial(total_kernel, rest),
-            in_specs=[SMEM] + [VMEM] * wide,
+            in_specs=[VMEM],
             out_specs=VMEM,
             out_shape=jax.ShapeDtypeStruct((out_rows, 2 * share), F32),
-            compiler_params=PARAMS,
+            compiler_params=limit(4),
             name="weight_total",
-        )(wide_pos, own_weight, *got_weight)
+        )(got_weight)
     else:
 
         def gradient_kernel(*refs):
@@ -303,13 +280,13 @@
             in_specs=[VMEM] * (2 + group),
             out_specs=[VMEM] * 2,
             out_shape=[jax.ShapeDtypeStruct((1, images), F32), jax.ShapeDtypeStruct((share, images), F32)],
-            compiler_params=PARAMS,
+            compiler_params=limit(12),
             name="gradient",
         )(own_part, *got, unit_part, inv_part)
         partial = sum(
             lax.dot_general(feats_t, part, NT, preferred_element_type=F32) for part in split_pair(d_zproj)
         )
-        left = (wide_pos[0] & 1) == 0
+        left = lax.axis_index("inner") == 0
         both = jnp.concatenate([jnp.where(left, partial, 0.0), jnp.where(left, 0.0, partial)], axis=1)
         d_proj = lax.psum_scatter(both, AXES[:2], scatter_dimension=0, tiled=True)
 
@@ -318,7 +295,7 @@
         in_specs=[VMEM] * spread,
         out_specs=VMEM,
         out_shape=jax.ShapeDtypeStruct((rows, width), F32),
-        compiler_params=PARAMS,
+        compiler_params=limit(4 if spread <= 4 else 12),
         name="caption_total",
     )(own_text, *got_text)
     image_loss = lax.dynamic_slice_in_dim(loss_line[0], member[0] * rows, rows, 0)

time: 67.3 us -> 70 us (1.040)
  waiting for transfers between devices: 8.84 us -> 24.5 us
  starting transfers between devices: 27.5 us -> 20.6 us
  local copies, waits for them, and re-layouts: 7.55 us -> 3.22 us
  Pallas kernels: 9.77 us -> 8.14 us
    ppermute x20 -> x13, waiting for transfers between devices: 8.84 us -> 24.5 us  [swapped(): lax.ppermute(value, AXES, [(source, source ^ mask) for source in range(to...]
    ppermute x20 -> x13, starting transfers between devices: 27.5 us -> 15.4 us  [swapped(): lax.ppermute(value, AXES, [(source, source ^ mask) for source in range(to...]
    all_to_all x0 -> x1, starting transfers between devices: none -> 5.16 us  [local(): got_weight = lax.all_to_all(sent_weight, AXES[:2], 0, 0)]
    unnamed x20 -> x4, local copies, waits for them, and re-layouts: 6.97 us -> 2.64 us
    pallas_call x1, Pallas kernels: 4.59 us -> 3.5 us  [local(): pl.pallas_call(functools.partial(pair_kernel, narrow, group, spread), in_...]
    pallas_call x3 -> x2, Pallas kernels: 2.78 us -> 2.67 us  [the longest x1 1.8 us: local(): pl.pallas_call(functools.partial(weight_kernel, group, wide), in_specs=[V...]
  transfers between devices with their start and end apart: 20 -> 14, of which waited for: 5 -> 7; matrix products, arithmetic and copies ran while one was open for 1% -> 1% of each run, Pallas kernels for 6% -> 3%
where the time goes in v4:
time: 70 us; the launch traced here: 69.6 us
  waiting for transfers between devices  24.5 us (35%)
  starting transfers between devices  20.6 us (29%)
  blocking collectives  11.3 us (16%)
  Pallas kernels  8.14 us (12%)
  local copies, waits for them, and re-layouts  3.22 us (5%)
  between operations  1.97 us (3%)
    ppermute x13, waiting for transfers between devices, swapped(): lax.ppermute(value, AXES, [(source, source ^ mask) for source in range(to...  24.5 us
    ppermute x13, starting transfers between devices, swapped(): lax.ppermute(value, AXES, [(source, source ^ mask) for source in range(to...  15.4 us
    all_gather x1, blocking collectives, local(): all_feats = lax.all_gather(image_feats, AXES[1:], axis=0, tiled=True)  11.3 us
    all_to_all x1, starting transfers between devices, local(): got_weight = lax.all_to_all(sent_weight, AXES[:2], 0, 0)  5.16 us
    pallas_call x1, Pallas kernels, local(): pl.pallas_call(functools.partial(pair_kernel, narrow, group, spread), in_...  3.5 us
    unnamed x4, local copies, waits for them, and re-layouts  2.64 us
    pallas_call x1, Pallas kernels, local(): pl.pallas_call(functools.partial(weight_kernel, group, wide), in_specs=[V...  1.8 us
  transfers between devices with their start and end apart: 14, of which 7 were waited for; matrix products, arithmetic and copies ran while one was open for 1% of the time, Pallas kernels for 3%

profile of v4, /device:TPU:0, one launch (start us, length us, event | category | flops | bytes accessed | tf_op | source)
XLA Modules:
  0.0 69.6 jit_solution(11884113642654708545)
XLA Ops:
  0.6 4.1 %collective-permute-start.1 = (bf16[48,1152]{1,0:T(8,128)(2,1)}, bf16[48,1152]{1,0:T(8,128)(2,1)S(1)}, u32[]{:S(2)}, u32[]{:S(2)}) collective-permute-start(bf16[48,1152]{1,0:T(8,128)(2,1)} %refs_5_.1), channel_id=1, source_target_pairs={{0,16},{1,17},{2,18},{3,19},{4,20},{5,21},{6,22},{7,23},{8,24},{9,... | collective-permute-start | bytes 331784 | tf_op jit(solution)/shard_map/ppermute | solution.py:28
  4.7 1.6 %collective-permute-start = (bf16[48,1152]{1,0:T(8,128)(2,1)}, bf16[48,1152]{1,0:T(8,128)(2,1)S(1)}, u32[]{:S(2)}, u32[]{:S(2)}) collective-permute-start(bf16[48,1152]{1,0:T(8,128)(2,1)} %refs_5_.1), channel_id=1, source_target_pairs={{0,8},{1,9},{2,10},{3,11},{4,12},{5,13},{6,14},{7,15},{8,0},{9,1},... | collective-permute-start | bytes 331784 | tf_op jit(solution)/shard_map/ppermute | solution.py:28
  7.6 11.3 %all_gather.3.refs_4_.feats_ref.refs_10_ = bf16[384,1152]{1,0:T(8,128)(2,1)S(1)} all-gather(bf16[48,1152]{1,0:T(8,128)(2,1)} %param.5), channel_id=1, replica_groups=mesh['outer'=4,'inner'=2,'narrow'=4] {'inner','narrow'}, dimensions={0}, use_global_device_ids=true | all-gather | bytes 995328 | tf_op jit(solution)/shard_map/all_gather | solution.py:206
  18.9 1.7 %copy-done = bf16[1152,1152]{1,0:T(8,128)(2,1)S(1)} copy-done((bf16[1152,1152]{1,0:T(8,128)(2,1)S(1)}, bf16[1152,1152]{1,0:T(8,128)(2,1)}, u32[]{:S(2)}) %copy-start) | copy-done | bytes 2654232
  20.6 0.9 %copy-done.1 = bf16[48,1152]{1,0:T(8,128)(2,1)S(1)} copy-done((bf16[48,1152]{1,0:T(8,128)(2,1)S(1)}, bf16[48,1152]{1,0:T(8,128)(2,1)}, u32[]{:S(2)}) %copy-start.1) | copy-done | bytes 110616
  21.5 3.5 %pairs.1 = (f32[144,384]{1,0:T(8,128)S(1)}, f32[1,384]{1,0:T(1,128)S(1)}, bf16[1152,384]{1,0:T(8,128)(2,1)S(1)}, bf16[192,384]{1,0:T(8,128)(2,1)S(1)}, f32[152,3...) custom-call(s32[1]{0:T(128)} %bitcast.refs_0_, ...), custom_call_target="tpu_custom_call" | custom-call | tf_op jit(solution)/shard_map/pairs/pallas_call | solution.py:208
  25.4 1.1 %collective-permute-start.4 = (bf16[160,384]{1,0:T(8,128)(2,1)S(1)}, bf16[160,384]{1,0:T(8,128)(2,1)S(1)}, u32[]{:S(2)}, u32[]{:S(2)}) collective-permute-start(bf16[160,384]{1,0:T(8,128)(2,1)S(1)} %get-tuple-element.24), channel_id=1, source_target_pairs={{0,2},{1,3},{2,0},{3,1},{4,6},{5,7},{6,4},{7,5},{8,10},{9,11},{10,... | collective-permute-start | bytes 368648 | tf_op jit(solution)/shard_map/ppermute | solution.py:28
  27.0 1.1 %collective-permute-start.6 = (bf16[160,384]{1,0:T(8,128)(2,1)S(1)}, bf16[160,384]{1,0:T(8,128)(2,1)S(1)}, u32[]{:S(2)}, u32[]{:S(2)}) collective-permute-start(bf16[160,384]{1,0:T(8,128)(2,1)S(1)} %get-tuple-element.26), channel_id=1, source_target_pairs={{0,4},{1,5},{2,6},{3,7},{4,0},{5,1},{6,2},{7,3},{8,12},{9,13},{10,... | collective-permute-start | bytes 368648 | tf_op jit(solution)/shard_map/ppermute | solution.py:28
  28.1 0.8 %collective-permute-start.7 = (bf16[160,384]{1,0:T(8,128)(2,1)S(1)}, bf16[160,384]{1,0:T(8,128)(2,1)S(1)}, u32[]{:S(2)}, u32[]{:S(2)}) collective-permute-start(bf16[160,384]{1,0:T(8,128)(2,1)S(1)} %get-tuple-element.27), channel_id=1, source_target_pairs={{0,5},{1,4},{2,7},{3,6},{4,1},{5,0},{6,3},{7,2},{8,13},{9,12},{10,... | collective-permute-start | bytes 368648 | tf_op jit(solution)/shard_map/ppermute | solution.py:28
  28.9 1.4 %collective-permute-start.8 = (bf16[160,384]{1,0:T(8,128)(2,1)S(1)}, bf16[160,384]{1,0:T(8,128)(2,1)S(1)}, u32[]{:S(2)}, u32[]{:S(2)}) collective-permute-start(bf16[160,384]{1,0:T(8,128)(2,1)S(1)} %get-tuple-element.28), channel_id=1, source_target_pairs={{0,6},{1,7},{2,4},{3,5},{4,2},{5,3},{6,0},{7,1},{8,14},{9,15},{10,... | collective-permute-start | bytes 368648 | tf_op jit(solution)/shard_map/ppermute | solution.py:28
  30.4 1.2 %collective-permute-done.4.refs_2_ = bf16[160,384]{1,0:T(8,128)(2,1)S(1)} collective-permute-done((bf16[160,384]{1,0:T(8,128)(2,1)S(1)}, bf16[160,384]{1,0:T(8,128)(2,1)S(1)}, u32[]{:S(2)}, u32[]{:S(2)}) %collective-permute-start.4) | collective-permute-done | bytes 122912 | tf_op jit(solution)/shard_map/ppermute | solution.py:28
  31.6 1.2 %captions.1 = (bf16[1152,384]{1,0:T(8,128)(2,1)S(1)}, f32[48,1152]{1,0:T(8,128)S(1)}, bf16[48,1152]{1,0:T(8,128)(2,1)S(1)}, bf16[48,1152]{1,0:T(8,128)(2,1)S(1)}, bf16[48,1152]{1,0:T(8,128)(2,1)S(1)}) custom-call(bf16[192,384]{1,0:T(8,128)(2,1)S(1)} %get-tuple-element.32.grad_ref, bf16[1152,384]{1,0:T(8,128)(2,1)S(1)} %get-tuple-element.33.emb_ref, ...), custom_call_target="tpu_custom_call" | custom-call | tf_op jit(solution)/shard_map/captions/pallas_call | solution.py:234
  33.2 2.0 %collective-permute-done.7.refs_5_ = bf16[160,384]{1,0:T(8,128)(2,1)S(1)} collective-permute-done((bf16[160,384]{1,0:T(8,128)(2,1)S(1)}, bf16[160,384]{1,0:T(8,128)(2,1)S(1)}, u32[]{:S(2)}, u32[]{:S(2)}) %collective-permute-start.7) | collective-permute-done | bytes 122912 | tf_op jit(solution)/shard_map/ppermute | solution.py:28
  35.1 3.9 %collective-permute-done.8.refs_6_ = bf16[160,384]{1,0:T(8,128)(2,1)S(1)} collective-permute-done((bf16[160,384]{1,0:T(8,128)(2,1)S(1)}, bf16[160,384]{1,0:T(8,128)(2,1)S(1)}, u32[]{:S(2)}, u32[]{:S(2)}) %collective-permute-start.8) | collective-permute-done | bytes 122912 | tf_op jit(solution)/shard_map/ppermute | solution.py:28
  39.0 2.0 %collective-permute-done.9.refs_7_ = bf16[160,384]{1,0:T(8,128)(2,1)S(1)} collective-permute-done((bf16[160,384]{1,0:T(8,128)(2,1)S(1)}, bf16[160,384]{1,0:T(8,128)(2,1)S(1)}, u32[]{:S(2)}, u32[]{:S(2)}) %collective-permute-start.9) | collective-permute-done | bytes 122912 | tf_op jit(solution)/shard_map/ppermute | solution.py:28
  41.0 1.8 %weights.1 = (f32[1,384]{1,0:T(1,128)S(1)}, bf16[8,176,128]{2,1,0:T(8,128)(2,1)}) custom-call(f32[152,384]{1,0:T(8,128)S(1)} %get-tuple-element.22.refs_0_, bf16[160,384]{1,0:T(8,128)(2,1)S(1)} %collective-permute-done.3.refs_1_, bf16[160,384]{1,0:T(8,128)(2,1)S(1)} %collective-permute-done.4.refs_2_, bf16[160,384]{1,0:T(8,128)(2,1)S(1)} %collective-permute-done.5.refs_3_, ...), custom_call_target="tpu_custom_call" | custom-call | tf_op jit(solution)/shard_map/weights/pallas_call | solution.py:251
  42.8 5.2 %all-to-all-start = ((bf16[8,176,128]{2,1,0:T(8,128)(2,1)}), bf16[8,176,128]{2,1,0:T(8,128)(2,1)S(1)}, u32[]{:S(2)}, u32[]{:S(2)}) async-start(bf16[8,176,128]{2,1,0:T(8,128)(2,1)} %get-tuple-element.40), calls=%async_computation | async-start | bytes 720896 | tf_op jit(solution)/shard_map/all_to_all | solution.py:262
  47.9 2.0 %collective-permute-start.10 = (bf16[48,1152]{1,0:T(8,128)(2,1)S(1)}, bf16[48,1152]{1,0:T(8,128)(2,1)S(1)}, u32[]{:S(2)}, u32[]{:S(2)}) collective-permute-start(bf16[48,1152]{1,0:T(8,128)(2,1)S(1)} %get-tuple-element.37), channel_id=1, source_target_pairs={{0,8},{1,9},{2,10},{3,11},{4,12},{5,13},{6,14},{7,15},{8,0},{9,1},... | collective-permute-start | bytes 331784 | tf_op jit(solution)/shard_map/ppermute | solution.py:28
  50.0 2.4 %collective-permute-start.11 = (bf16[48,1152]{1,0:T(8,128)(2,1)S(1)}, bf16[48,1152]{1,0:T(8,128)(2,1)S(1)}, u32[]{:S(2)}, u32[]{:S(2)}) collective-permute-start(bf16[48,1152]{1,0:T(8,128)(2,1)S(1)} %get-tuple-element.38), channel_id=1, source_target_pairs={{0,16},{1,17},{2,18},{3,19},{4,20},{5,21},{6,22},{7,23},{8,24},{9,... | collective-permute-start | bytes 331784 | tf_op jit(solution)/shard_map/ppermute | solution.py:28
  52.4 6.1 %collective-permute-done.10.refs_1_ = bf16[48,1152]{1,0:T(8,128)(2,1)S(1)} collective-permute-done((bf16[48,1152]{1,0:T(8,128)(2,1)S(1)}, bf16[48,1152]{1,0:T(8,128)(2,1)S(1)}, u32[]{:S(2)}, u32[]{:S(2)}) %collective-permute-start.10) | collective-permute-done | bytes 110624 | tf_op jit(solution)/shard_map/ppermute | solution.py:28
  58.4 9.0 %collective-permute-done.11.refs_2_ = bf16[48,1152]{1,0:T(8,128)(2,1)S(1)} collective-permute-done((bf16[48,1152]{1,0:T(8,128)(2,1)S(1)}, bf16[48,1152]{1,0:T(8,128)(2,1)S(1)}, u32[]{:S(2)}, u32[]{:S(2)}) %collective-permute-start.11) | collective-permute-done | bytes 110624 | tf_op jit(solution)/shard_map/ppermute | solution.py:28
  67.4 0.7 %caption_total.1 = f32[48,1152]{1,0:T(8,128)} custom-call(f32[48,1152]{1,0:T(8,128)S(1)} %get-tuple-element.36.refs_0_, bf16[48,1152]{1,0:T(8,128)(2,1)S(1)} %collective-permute-done.10.refs_1_, bf16[48,1152]{1,0:T(8,128)(2,1)S(1)} %collective-permute-done.11.refs_2_, bf16[48,1152]{1,0:T(8,128)(2,1)S(1)} %collective-permute-done.12.refs_3_), custom_call_target="tpu_custom_call" | custom-call | tf_op jit(solution)/shard_map/caption_total/pallas_call | solution.py:293
  68.2 0.6 dynamic-slice_bitcast_fusion
  68.8 0.9 %weight_total.1 = f32[144,288]{1,0:T(8,128)} custom-call(bf16[8,176,128]{2,1,0:T(8,128)(2,1)S(1)} %all-to-all-done.got_ref), custom_call_target="tpu_custom_call" | custom-call | tf_op jit(solution)/shard_map/weight_total/pallas_call | solution.py:263
  (15 shorter events, 1.1 us)
Async XLA Ops:
  0.6 18.2 %collective-permute-start.1 = (bf16[48,1152]{1,0:T(8,128)(2,1)}, bf16[48,1152]{1,0:T(8,128)(2,1)S(1)}, u32[]{:S(2)}, u32[]{:S(2)}) collective-permute-start(bf16[48,1152]{1,0:T(8,128)(2,1)} %refs_5_.1), channel_id=1, source_target_pairs={{0,16},{1,17},{2,18},{3,19},{4,20},{5,21},{6,22},{7,23},{8,24},{9,... | collective-permute-start | bytes 331784 | tf_op jit(solution)/shard_map/ppermute | solution.py:28
  4.7 14.1 %collective-permute-start = (bf16[48,1152]{1,0:T(8,128)(2,1)}, bf16[48,1152]{1,0:T(8,128)(2,1)S(1)}, u32[]{:S(2)}, u32[]{:S(2)}) collective-permute-start(bf16[48,1152]{1,0:T(8,128)(2,1)} %refs_5_.1), channel_id=1, source_target_pairs={{0,8},{1,9},{2,10},{3,11},{4,12},{5,13},{6,14},{7,15},{8,0},{9,1},... | collective-permute-start | bytes 331784 | tf_op jit(solution)/shard_map/ppermute | solution.py:28
  6.3 12.6 %collective-permute-start.2 = (bf16[48,1152]{1,0:T(8,128)(2,1)}, bf16[48,1152]{1,0:T(8,128)(2,1)S(1)}, u32[]{:S(2)}, u32[]{:S(2)}) collective-permute-start(bf16[48,1152]{1,0:T(8,128)(2,1)} %refs_5_.1), channel_id=1, source_target_pairs={{0,24},{1,25},{2,26},{3,27},{4,28},{5,29},{6,30},{7,31},{8,16},{9,... | collective-permute-start | bytes 331784 | tf_op jit(solution)/shard_map/ppermute | solution.py:28
  18.9 1.8 %copy-start = (bf16[1152,1152]{1,0:T(8,128)(2,1)S(1)}, bf16[1152,1152]{1,0:T(8,128)(2,1)}, u32[]{:S(2)}) copy-start(bf16[1152,1152]{1,0:T(8,128)(2,1)} %refs_3_.1) | copy-start | bytes 7962628
  20.6 0.9 %copy-start.1 = (bf16[48,1152]{1,0:T(8,128)(2,1)S(1)}, bf16[48,1152]{1,0:T(8,128)(2,1)}, u32[]{:S(2)}) copy-start(bf16[48,1152]{1,0:T(8,128)(2,1)} %refs_5_.1) | copy-start | bytes 331780
  25.0 3.9 %collective-permute-start.3 = (bf16[160,384]{1,0:T(8,128)(2,1)S(1)}, bf16[160,384]{1,0:T(8,128)(2,1)S(1)}, u32[]{:S(2)}, u32[]{:S(2)}) collective-permute-start(bf16[160,384]{1,0:T(8,128)(2,1)S(1)} %get-tuple-element.23), channel_id=1, source_target_pairs={{0,1},{1,0},{2,3},{3,2},{4,5},{5,4},{6,7},{7,6},{8,9},{9,8},{10,11... | collective-permute-start | bytes 368648 | tf_op jit(solution)/shard_map/ppermute | solution.py:28
  25.4 6.2 %collective-permute-start.4 = (bf16[160,384]{1,0:T(8,128)(2,1)S(1)}, bf16[160,384]{1,0:T(8,128)(2,1)S(1)}, u32[]{:S(2)}, u32[]{:S(2)}) collective-permute-start(bf16[160,384]{1,0:T(8,128)(2,1)S(1)} %get-tuple-element.24), channel_id=1, source_target_pairs={{0,2},{1,3},{2,0},{3,1},{4,6},{5,7},{6,4},{7,5},{8,10},{9,11},{10,... | collective-permute-start | bytes 368648 | tf_op jit(solution)/shard_map/ppermute | solution.py:28
  26.6 6.3 %collective-permute-start.5 = (bf16[160,384]{1,0:T(8,128)(2,1)S(1)}, bf16[160,384]{1,0:T(8,128)(2,1)S(1)}, u32[]{:S(2)}, u32[]{:S(2)}) collective-permute-start(bf16[160,384]{1,0:T(8,128)(2,1)S(1)} %get-tuple-element.25), channel_id=1, source_target_pairs={{0,3},{1,2},{2,1},{3,0},{4,7},{5,6},{6,5},{7,4},{8,11},{9,10},{10,... | collective-permute-start | bytes 368648 | tf_op jit(solution)/shard_map/ppermute | solution.py:28
  27.0 6.2 %collective-permute-start.6 = (bf16[160,384]{1,0:T(8,128)(2,1)S(1)}, bf16[160,384]{1,0:T(8,128)(2,1)S(1)}, u32[]{:S(2)}, u32[]{:S(2)}) collective-permute-start(bf16[160,384]{1,0:T(8,128)(2,1)S(1)} %get-tuple-element.26), channel_id=1, source_target_pairs={{0,4},{1,5},{2,6},{3,7},{4,0},{5,1},{6,2},{7,3},{8,12},{9,13},{10,... | collective-permute-start | bytes 368648 | tf_op jit(solution)/shard_map/ppermute | solution.py:28
  28.1 7.0 %collective-permute-start.7 = (bf16[160,384]{1,0:T(8,128)(2,1)S(1)}, bf16[160,384]{1,0:T(8,128)(2,1)S(1)}, u32[]{:S(2)}, u32[]{:S(2)}) collective-permute-start(bf16[160,384]{1,0:T(8,128)(2,1)S(1)} %get-tuple-element.27), channel_id=1, source_target_pairs={{0,5},{1,4},{2,7},{3,6},{4,1},{5,0},{6,3},{7,2},{8,13},{9,12},{10,... | collective-permute-start | bytes 368648 | tf_op jit(solution)/shard_map/ppermute | solution.py:28
  28.9 10.1 %collective-permute-start.8 = (bf16[160,384]{1,0:T(8,128)(2,1)S(1)}, bf16[160,384]{1,0:T(8,128)(2,1)S(1)}, u32[]{:S(2)}, u32[]{:S(2)}) collective-permute-start(bf16[160,384]{1,0:T(8,128)(2,1)S(1)} %get-tuple-element.28), channel_id=1, source_target_pairs={{0,6},{1,7},{2,4},{3,5},{4,2},{5,3},{6,0},{7,1},{8,14},{9,15},{10,... | collective-permute-start | bytes 368648 | tf_op jit(solution)/shard_map/ppermute | solution.py:28
  31.6 9.4 %collective-permute-start.9 = (bf16[160,384]{1,0:T(8,128)(2,1)S(1)}, bf16[160,384]{1,0:T(8,128)(2,1)S(1)}, u32[]{:S(2)}, u32[]{:S(2)}) collective-permute-start(bf16[160,384]{1,0:T(8,128)(2,1)S(1)} %get-tuple-element.29), channel_id=1, source_target_pairs={{0,7},{1,6},{2,5},{3,4},{4,3},{5,2},{6,1},{7,0},{8,15},{9,14},{10,... | collective-permute-start | bytes 368648 | tf_op jit(solution)/shard_map/ppermute | solution.py:28
  42.8 26.0 %all-to-all-start = ((bf16[8,176,128]{2,1,0:T(8,128)(2,1)}), bf16[8,176,128]{2,1,0:T(8,128)(2,1)S(1)}, u32[]{:S(2)}, u32[]{:S(2)}) async-start(bf16[8,176,128]{2,1,0:T(8,128)(2,1)} %get-tuple-element.40), calls=%async_computation | async-start | bytes 720896 | tf_op jit(solution)/shard_map/all_to_all | solution.py:262
  47.9 10.5 %collective-permute-start.10 = (bf16[48,1152]{1,0:T(8,128)(2,1)S(1)}, bf16[48,1152]{1,0:T(8,128)(2,1)S(1)}, u32[]{:S(2)}, u32[]{:S(2)}) collective-permute-start(bf16[48,1152]{1,0:T(8,128)(2,1)S(1)} %get-tuple-element.37), channel_id=1, source_target_pairs={{0,8},{1,9},{2,10},{3,11},{4,12},{5,13},{6,14},{7,15},{8,0},{9,1},... | collective-permute-start | bytes 331784 | tf_op jit(solution)/shard_map/ppermute | solution.py:28
  50.0 17.5 %collective-permute-start.11 = (bf16[48,1152]{1,0:T(8,128)(2,1)S(1)}, bf16[48,1152]{1,0:T(8,128)(2,1)S(1)}, u32[]{:S(2)}, u32[]{:S(2)}) collective-permute-start(bf16[48,1152]{1,0:T(8,128)(2,1)S(1)} %get-tuple-element.38), channel_id=1, source_target_pairs={{0,16},{1,17},{2,18},{3,19},{4,20},{5,21},{6,22},{7,23},{8,24},{9,... | collective-permute-start | bytes 331784 | tf_op jit(solution)/shard_map/ppermute | solution.py:28
  52.3 15.1 %collective-permute-start.12 = (bf16[48,1152]{1,0:T(8,128)(2,1)S(1)}, bf16[48,1152]{1,0:T(8,128)(2,1)S(1)}, u32[]{:S(2)}, u32[]{:S(2)}) collective-permute-start(bf16[48,1152]{1,0:T(8,128)(2,1)S(1)} %get-tuple-element.39), channel_id=1, source_target_pairs={{0,24},{1,25},{2,26},{3,27},{4,28},{5,29},{6,30},{7,31},{8,16},{9,... | collective-permute-start | bytes 331784 | tf_op jit(solution)/shard_map/ppermute | solution.py:28

commit v5 on v4

--- a/solution.py
+++ b/solution.py
@@ -16,7 +16,7 @@
 SMEM = pl.BlockSpec(memory_space=pltpu.SMEM)
 NT = (((1,), (1,)), ((), ()))
 TN = (((0,), (0,)), ((), ()))
-ANY = pl.BlockSpec(memory_space=pl.ANY)
+HBM = pl.BlockSpec(memory_space=pltpu.HBM)
 MIB = 1024 * 1024
 
 
@@ -31,6 +31,19 @@
 def split_pair(values):
     high = values.astype(BF16)
     return high, (values - high.astype(F32)).astype(BF16)
+
+
+def stat_rows(loss, along):
+    row = lax.broadcasted_iota(jnp.int32, (STAT_ROWS, loss.shape[1]), 0)
+    stats = jnp.zeros(row.shape, F32)
+    for place, line in enumerate(split_pair(loss) + split_pair(along)):
+        stats = jnp.where(row == place, line.astype(F32), stats)
+    return stats.astype(BF16)
+
+
+def stat_sums(stats):
+    stats = stats.astype(F32)
+    return stats[0:1, :] + stats[1:2, :], stats[2:3, :] + stats[3:4, :]
 
 
 def column_block(member, narrow):
@@ -41,17 +54,18 @@
     member_ref, log_scale_ref, bias_ref, weight_ref, feats_ref = refs[:5]
     texts = refs[5 : 5 + spread]
     outs = refs[5 + spread :]
-    unit_out, inv_out, emb_out, grad_out, own_out = outs[:5]
-    send_out = outs[5 : 4 + group]
-    unit_all, text_all, d_all, weight, own_text, sems = outs[4 + group :]
+    unit_out, inv_out, emb_out, grad_out, own_out, send_out = outs[:6]
+    unit_all, text_all, d_all, weight, own_text, scalars, sems = outs[6:]
     rows, width = texts[0].shape
     images = group * rows
     share = width // group
     member = member_ref[0]
     text_copy = pltpu.make_async_copy(texts[0], own_text, sems.at[0])
     weight_copy = pltpu.make_async_copy(weight_ref, weight, sems.at[1])
-    text_copy.start()
-    weight_copy.start()
+    scale_copy = pltpu.make_async_copy(log_scale_ref, scalars.at[0], sems.at[2])
+    bias_copy = pltpu.make_async_copy(bias_ref, scalars.at[1], sems.at[3])
+    for copy in (text_copy, scale_copy, bias_copy, weight_copy):
+        copy.start()
 
     for step in [*range(1, spread), 0]:
         if step == 0:
@@ -73,8 +87,10 @@
     block = pl.multiple_of(column_block(member, narrow) * share, share)
     unit_out[...] = unit_all[pl.ds(block, share), :]
 
-    scale = jnp.exp(jnp.full((1, 1), log_scale_ref[0], F32))
-    shift = bias_ref[0]
+    scale_copy.wait()
+    bias_copy.wait()
+    scale = jnp.exp(jnp.full((1, 1), scalars[0, 0], F32))
+    shift = scalars[1, 0]
     count = 4 * rows if spread % 4 == 0 else rows
     chunks = spread * rows // count
 
@@ -108,32 +124,47 @@
         sums = lax.fori_loop(1, chunks, lambda c, s: one_chunk(c, *s, False), sums)
     loss_sum, dot_sum = sums
 
-    own_out[:share, :] = d_all[pl.ds(block, share), :]
-    own_out[share : share + 1, :] = loss_sum
-    own_out[share + 1 : share + 2, :] = dot_sum
-    loss_high, loss_low = split_pair(loss_sum)
-    dot_high, dot_low = split_pair(dot_sum)
-    row = lax.broadcasted_iota(jnp.int32, (STAT_ROWS, images), 0)
-    stats = jnp.zeros((STAT_ROWS, images), F32)
-    for place, line in enumerate((loss_high, loss_low, dot_high, dot_low)):
-        stats = jnp.where(row == place, line.astype(F32), stats)
-    stats = stats.astype(BF16)
-    for step in range(1, group):
-        part = pl.multiple_of(column_block(member ^ step, narrow) * share, share)
-        send_out[step - 1][:share, :] = d_all[pl.ds(part, share), :].astype(BF16)
-        send_out[step - 1][share:, :] = stats
-
-
-def caption_kernel(rows, grad_ref, emb_ref, feats_ref, *outs):
-    feats_t, own_out = outs[:2]
-    for step in range(len(outs) - 1):
+    stats = stat_rows(loss_sum, dot_sum)
+    for index in range(group // 2):
+        part = pl.multiple_of(column_block(member ^ (2 * index), narrow) * share, share)
+        own_out[index, :share, :] = d_all[pl.ds(part, share), :]
+        part = pl.multiple_of(column_block(member ^ (2 * index + 1), narrow) * share, share)
+        send_out[index, :share, :] = d_all[pl.ds(part, share), :].astype(BF16)
+        send_out[index, share:, :] = stats
+    own_out[0, share : share + 1, :] = loss_sum
+    own_out[0, share + 1 : share + 2, :] = dot_sum
+
+
+def chip_kernel(own_ref, got_ref, own_out, *send_out):
+    share = own_out.shape[0] - 8
+    loss, along = stat_sums(got_ref[0, share:, :])
+    loss = loss + own_ref[0, share : share + 1, :]
+    along = along + own_ref[0, share + 1 : share + 2, :]
+    own_out[:share, :] = own_ref[0, :share, :] + got_ref[0, :share, :].astype(F32)
+    own_out[share : share + 1, :] = loss
+    own_out[share + 1 : share + 2, :] = along
+    stats = stat_rows(loss, along)
+    for index, target in enumerate(send_out, 1):
+        target[:share, :] = (own_ref[index, :share, :] + got_ref[index, :share, :].astype(F32)).astype(BF16)
+        target[share:, :] = stats
+
+
+def caption_kernel(rows, grad_ref, emb_ref, feats_ref, feats_t, own_out, send_out):
+    for step in range(grad_ref.shape[0] // rows):
         grad = grad_ref[step * rows : (step + 1) * rows, :]
         product = lax.dot_general(grad, emb_ref[...], NT, preferred_element_type=F32)
-        target = outs[1 + step]
-        target[...] = product.astype(target.dtype)
+        target = send_out if step & 1 else own_out
+        target[step // 2] = product.astype(target.dtype)
     for start in range(0, feats_ref.shape[0], LANES):
         cols = slice(start, start + LANES)
         feats_t[:, cols] = feats_ref[cols, :].astype(F32).T.astype(BF16)
+
+
+def halving_kernel(own_ref, got_ref, own_out, send_out):
+    for step in range(own_ref.shape[0]):
+        total = own_ref[step] + got_ref[step].astype(F32)
+        target = send_out if step & 1 else own_out
+        target[step // 2] = total.astype(target.dtype)
 
 
 def gathered_gradient(own_ref, got, unit_ref, inv_ref, loss_out):
@@ -143,17 +174,17 @@
     along = own_ref[share + 1 : share + 2, :]
     for block in got:
         total = total + block[:share, :].astype(F32)
-        stats = block[share:, :].astype(F32)
-        loss = loss + (stats[0:1, :] + stats[1:2, :])
-        along = along + (stats[2:3, :] + stats[3:4, :])
+        more_loss, more_along = stat_sums(block[share:, :])
+        loss = loss + more_loss
+        along = along + more_along
     loss_out[...] = loss
     return inv_ref[...] * (total - unit_ref[...] * along)
 
 
 def weight_kernel(group, wide, *refs):
     own_ref = refs[0]
-    got = refs[1:group]
-    unit_ref, inv_ref, feats_ref, feats_t_ref, loss_out, send_out = refs[group:]
+    got = refs[1 : group // 2]
+    unit_ref, inv_ref, feats_ref, feats_t_ref, loss_out, send_out = refs[group // 2 :]
     share = unit_ref.shape[0]
     rest = share - LANES
     rows = feats_t_ref.shape[0] // wide
@@ -185,11 +216,8 @@
         out[LANES:, left + LANES : left + LANES + rest] = half[rows + rest :, :].T[: rows - LANES, :]
 
 
-def sum_kernel(*refs):
-    total = refs[0][...]
-    for block in refs[1:-1]:
-        total = total + block[...].astype(F32)
-    refs[-1][...] = total
+def sum_kernel(own_ref, got_ref, out):
+    out[...] = own_ref[0] + got_ref[0].astype(F32)
 
 
 def local(wide, narrow, image_feats, proj_weight, text_embed, log_scale, logit_bias):
@@ -204,44 +232,67 @@
     texts = [text_embed] + [swapped(text_embed, total, step * group) for step in range(1, spread)]
 
     all_feats = lax.all_gather(image_feats, AXES[1:], axis=0, tiled=True)
-    sent = jax.ShapeDtypeStruct((share + STAT_ROWS, images), BF16)
     results = pl.pallas_call(
         functools.partial(pair_kernel, narrow, group, spread),
-        in_specs=[SMEM] * 3 + [ANY, VMEM, ANY] + [VMEM] * (spread - 1),
-        out_specs=[VMEM] * (4 + group),
+        in_specs=[SMEM, HBM, HBM, HBM, VMEM, HBM] + [VMEM] * (spread - 1),
+        out_specs=[VMEM] * 6,
         out_shape=[
             jax.ShapeDtypeStruct((share, images), F32),
             jax.ShapeDtypeStruct((1, images), F32),
             jax.ShapeDtypeStruct((width, images), BF16),
             jax.ShapeDtypeStruct((spread * rows, images), BF16),
-            jax.ShapeDtypeStruct((share + 8, images), F32),
-        ]
-        + [sent] * (group - 1),
+            jax.ShapeDtypeStruct((group // 2, share + 8, images), F32),
+            jax.ShapeDtypeStruct((group // 2, share + STAT_ROWS, images), BF16),
+        ],
         scratch_shapes=[
             pltpu.VMEM((width, images), F32),
             pltpu.VMEM((spread * rows, width), BF16),
             pltpu.VMEM((width, images), F32),
             pltpu.VMEM((width, width), BF16),
             pltpu.VMEM((rows, width), BF16),
-            pltpu.SemaphoreType.DMA((2,)),
+            pltpu.SMEM((2, 1), F32),
+            pltpu.SemaphoreType.DMA((4,)),
         ],
         compiler_params=limit(24 if spread <= 4 else 40),
         name="pairs",
     )(member, log_scale, logit_bias, proj_weight, all_feats, *texts)
-    unit_part, inv_part, img_emb, grad_tile, own_part = results[:5]
-    got = [swapped(value, total, step) for step, value in enumerate(results[5:], 1)]
-
-    results = pl.pallas_call(
+    unit_part, inv_part, img_emb, grad_tile, own_part, sent_part = results
+    got_part = swapped(sent_part, total, 1)
+    feats_t, own_text, sent_text = pl.pallas_call(
         functools.partial(caption_kernel, rows),
         in_specs=[VMEM] * 3,
-        out_specs=[VMEM] * (1 + spread),
-        out_shape=[jax.ShapeDtypeStruct((width, images), BF16), jax.ShapeDtypeStruct((rows, width), F32)]
-        + [jax.ShapeDtypeStruct((rows, width), BF16)] * (spread - 1),
+        out_specs=[VMEM] * 3,
+        out_shape=[jax.ShapeDtypeStruct((width, images), BF16)]
+        + [jax.ShapeDtypeStruct((spread // 2, rows, width), kind) for kind in (F32, BF16)],
         compiler_params=limit(12 if spread <= 4 else 24),
         name="captions",
     )(grad_tile, img_emb, all_feats)
-    feats_t, own_text = results[:2]
-    got_text = [swapped(value, total, step * group) for step, value in enumerate(results[2:], 1)]
+    own_part, *chip_parts = pl.pallas_call(
+        chip_kernel,
+        in_specs=[VMEM] * 2,
+        out_specs=[VMEM] * (group // 2),
+        out_shape=[jax.ShapeDtypeStruct((share + 8, images), F32)]
+        + [jax.ShapeDtypeStruct((share + STAT_ROWS, images), BF16)] * (group // 2 - 1),
+        compiler_params=limit(12),
+        name="chip_sum",
+    )(own_part, got_part)
+    got = [swapped(value, total, 2 * index) for index, value in enumerate(chip_parts, 1)]
+
+    mask = group
+    got_text = swapped(sent_text, total, mask)
+    while own_text.shape[0] > 1:
+        mask *= 2
+        own_text, sent_text = pl.pallas_call(
+            halving_kernel,
+            in_specs=[VMEM] * 2,
+            out_specs=[VMEM] * 2,
+            out_shape=[
+                jax.ShapeDtypeStruct((own_text.shape[0] // 2, rows, width), kind) for kind in (F32, BF16)
+            ],
+            compiler_params=limit(6 if spread <= 4 else 24),
+            name="caption_half",
+        )(own_text, got_text)
+        got_text = swapped(sent_text, total, mask)
 
     out_rows = width // wide
     rest = share - LANES
@@ -250,7 +301,7 @@
     if direct:
         loss_line, sent_weight = pl.pallas_call(
             functools.partial(weight_kernel, group, wide),
-            in_specs=[VMEM] * (4 + group),
+            in_specs=[VMEM] * (4 + group // 2),
             out_specs=[VMEM] * 2,
             out_shape=[
                 jax.ShapeDtypeStruct((1, images), F32),
@@ -271,13 +322,13 @@
     else:
 
         def gradient_kernel(*refs):
-            own_ref, blocks = refs[0], refs[1:group]
-            unit_ref, inv_ref, loss_out, d_out = refs[group:]
+            own_ref, blocks = refs[0], refs[1 : group // 2]
+            unit_ref, inv_ref, loss_out, d_out = refs[group // 2 :]
             d_out[...] = gathered_gradient(own_ref, blocks, unit_ref, inv_ref, loss_out)
 
         loss_line, d_zproj = pl.pallas_call(
             gradient_kernel,
-            in_specs=[VMEM] * (2 + group),
+            in_specs=[VMEM] * (2 + group // 2),
             out_specs=[VMEM] * 2,
             out_shape=[jax.ShapeDtypeStruct((1, images), F32), jax.ShapeDtypeStruct((share, images), F32)],
             compiler_params=limit(12),
@@ -292,12 +343,12 @@
 
     d_text_unit = pl.pallas_call(
         sum_kernel,
-        in_specs=[VMEM] * spread,
+        in_specs=[VMEM] * 2,
         out_specs=VMEM,
         out_shape=jax.ShapeDtypeStruct((rows, width), F32),
-        compiler_params=limit(4 if spread <= 4 else 12),
+        compiler_params=limit(4),
         name="caption_total",
-    )(own_text, *got_text)
+    )(own_text, got_text)
     image_loss = lax.dynamic_slice_in_dim(loss_line[0], member[0] * rows, rows, 0)
     return (image_loss, d_text_unit, d_proj)
 

time: 70 us -> 65.4 us (0.934)
  waiting for transfers between devices: 24.5 us -> 20.7 us
  starting transfers between devices: 20.6 us -> 19.6 us
    ppermute x13 -> x9, waiting for transfers between devices: 24.5 us -> 20.6 us  [swapped(): lax.ppermute(value, AXES, [(source, source ^ mask) for source in range(to...]
    ppermute x13 -> x9, starting transfers between devices: 15.4 us -> 14.1 us  [swapped(): lax.ppermute(value, AXES, [(source, source ^ mask) for source in range(to...]
  transfers between devices with their start and end apart: 14 -> 10, of which waited for: 7 -> 6; matrix products, arithmetic and copies ran while one was open for 1% -> 1% of each run, Pallas kernels for 3% -> 3%
where the time goes in v5:
time: 65.4 us; the launch traced here: 65.1 us
  waiting for transfers between devices  20.7 us (32%)
  starting transfers between devices  19.6 us (30%)
  blocking collectives  11.3 us (17%)
  Pallas kernels  8.39 us (13%)
  local copies, waits for them, and re-layouts  3.22 us (5%)
  between operations  1.97 us (3%)
    ppermute x9, waiting for transfers between devices, swapped(): lax.ppermute(value, AXES, [(source, source ^ mask) for source in range(to...  20.6 us
    ppermute x9, starting transfers between devices, swapped(): lax.ppermute(value, AXES, [(source, source ^ mask) for source in range(to...  14.1 us
    all_gather x1, blocking collectives, local(): all_feats = lax.all_gather(image_feats, AXES[1:], axis=0, tiled=True)  11.3 us
    all_to_all x1, starting transfers between devices, local(): got_weight = lax.all_to_all(sent_weight, AXES[:2], 0, 0)  5.48 us
    pallas_call x1, Pallas kernels, local(): pl.pallas_call(functools.partial(pair_kernel, narrow, group, spread), in_...  3.71 us
    unnamed x4, local copies, waits for them, and re-layouts  2.64 us
    pallas_call x1, Pallas kernels, local(): pl.pallas_call(functools.partial(weight_kernel, group, wide), in_specs=[V...  1.73 us
  transfers between devices with their start and end apart: 10, of which 6 were waited for; matrix products, arithmetic and copies ran while one was open for 1% of the time, Pallas kernels for 3%

profile of v5, /device:TPU:0, one launch (start us, length us, event | category | flops | bytes accessed | tf_op | source)
XLA Modules:
  0.0 65.1 jit_solution(8946632238703489848)
XLA Ops:
  0.6 4.1 %collective-permute-start.1 = (bf16[48,1152]{1,0:T(8,128)(2,1)}, bf16[48,1152]{1,0:T(8,128)(2,1)S(1)}, u32[]{:S(2)}, u32[]{:S(2)}) collective-permute-start(bf16[48,1152]{1,0:T(8,128)(2,1)} %refs_5_.1), channel_id=1, source_target_pairs={{0,16},{1,17},{2,18},{3,19},{4,20},{5,21},{6,22},{7,23},{8,24},{9,... | collective-permute-start | bytes 331784 | tf_op jit(solution)/shard_map/ppermute | solution.py:28
  4.7 1.6 %collective-permute-start = (bf16[48,1152]{1,0:T(8,128)(2,1)}, bf16[48,1152]{1,0:T(8,128)(2,1)S(1)}, u32[]{:S(2)}, u32[]{:S(2)}) collective-permute-start(bf16[48,1152]{1,0:T(8,128)(2,1)} %refs_5_.1), channel_id=1, source_target_pairs={{0,8},{1,9},{2,10},{3,11},{4,12},{5,13},{6,14},{7,15},{8,0},{9,1},... | collective-permute-start | bytes 331784 | tf_op jit(solution)/shard_map/ppermute | solution.py:28
  7.6 11.3 %all_gather.3.refs_4_.feats_ref.refs_6_ = bf16[384,1152]{1,0:T(8,128)(2,1)S(1)} all-gather(bf16[48,1152]{1,0:T(8,128)(2,1)} %param.5), channel_id=1, replica_groups=mesh['outer'=4,'inner'=2,'narrow'=4] {'inner','narrow'}, dimensions={0}, use_global_device_ids=true | all-gather | bytes 995328 | tf_op jit(solution)/shard_map/all_gather | solution.py:234
  18.9 1.7 %copy-done = bf16[1152,1152]{1,0:T(8,128)(2,1)S(1)} copy-done((bf16[1152,1152]{1,0:T(8,128)(2,1)S(1)}, bf16[1152,1152]{1,0:T(8,128)(2,1)}, u32[]{:S(2)}) %copy-start) | copy-done | bytes 2654232
  20.6 0.9 %copy-done.1 = bf16[48,1152]{1,0:T(8,128)(2,1)S(1)} copy-done((bf16[48,1152]{1,0:T(8,128)(2,1)S(1)}, bf16[48,1152]{1,0:T(8,128)(2,1)}, u32[]{:S(2)}) %copy-start.1) | copy-done | bytes 110616
  21.5 3.7 %pairs.1 = (f32[144,384]{1,0:T(8,128)S(1)}, f32[1,384]{1,0:T(1,128)S(1)}, bf16[1152,384]{1,0:T(8,128)(2,1)S(1)}, bf16[192,384]{1,0:T(8,128)(2,1)S(1)}, f32[4,152...) custom-call(s32[1]{0:T(128)} %bitcast.refs_0_, f32[1]{0:T(128)S(6)} %copy.8.refs_1_, f32[1]{0:T(128)S(6)} %copy.9.refs_2_, ...), custom_call_target="tpu_custom_call" | custom-call | tf_op jit(solution)/shard_map/pairs/pallas_call | solution.py:235
  25.2 0.4 collective-permute-start.3
  25.7 1.5 %collective-permute-done.3.got_ref = bf16[4,160,384]{2,1,0:T(8,128)(2,1)S(1)} collective-permute-done((bf16[4,160,384]{2,1,0:T(8,128)(2,1)S(1)}, bf16[4,160,384]{2,1,0:T(8,128)(2,1)S(1)}, u32[]{:S(2)}, u32[]{:S(2)}) %collective-permute-start.3) | collective-permute-done | bytes 491552 | tf_op jit(solution)/shard_map/ppermute | solution.py:28
  27.3 1.2 %collective-permute-start.4 = (bf16[160,384]{1,0:T(8,128)(2,1)S(1)}, bf16[160,384]{1,0:T(8,128)(2,1)S(1)}, u32[]{:S(2)}, u32[]{:S(2)}) collective-permute-start(bf16[160,384]{1,0:T(8,128)(2,1)S(1)} %get-tuple-element.23), channel_id=1, source_target_pairs={{0,2},{1,3},{2,0},{3,1},{4,6},{5,7},{6,4},{7,5},{8,10},{9,11},{10,... | collective-permute-start | bytes 368648 | tf_op jit(solution)/shard_map/ppermute | solution.py:28
  28.5 0.8 %collective-permute-start.5 = (bf16[160,384]{1,0:T(8,128)(2,1)S(1)}, bf16[160,384]{1,0:T(8,128)(2,1)S(1)}, u32[]{:S(2)}, u32[]{:S(2)}) collective-permute-start(bf16[160,384]{1,0:T(8,128)(2,1)S(1)} %get-tuple-element.24), channel_id=1, source_target_pairs={{0,4},{1,5},{2,6},{3,7},{4,0},{5,1},{6,2},{7,3},{8,12},{9,13},{10,... | collective-permute-start | bytes 368648 | tf_op jit(solution)/shard_map/ppermute | solution.py:28
  29.3 1.5 %collective-permute-start.6 = (bf16[160,384]{1,0:T(8,128)(2,1)S(1)}, bf16[160,384]{1,0:T(8,128)(2,1)S(1)}, u32[]{:S(2)}, u32[]{:S(2)}) collective-permute-start(bf16[160,384]{1,0:T(8,128)(2,1)S(1)} %get-tuple-element.25), channel_id=1, source_target_pairs={{0,6},{1,7},{2,4},{3,5},{4,2},{5,3},{6,0},{7,1},{8,14},{9,15},{10,... | collective-permute-start | bytes 368648 | tf_op jit(solution)/shard_map/ppermute | solution.py:28
  30.8 1.2 %captions.1 = (bf16[1152,384]{1,0:T(8,128)(2,1)S(1)}, f32[2,48,1152]{2,1,0:T(8,128)S(1)}, bf16[2,48,1152]{2,1,0:T(8,128)(2,1)S(1)}) custom-call(bf16[192,384]{1,0:T(8,128)(2,1)S(1)} %get-tuple-element.28.grad_ref, bf16[1152,384]{1,0:T(8,128)(2,1)S(1)} %get-tuple-element.29.emb_ref, bf16[384,1152]{1,0:T(8,128)(2,1)S(1)} %all_gather.3.refs_4_.feats_ref.refs_6_), custom_call_target="tpu_custom_call" | custom-call | tf_op jit(solution)/shard_map/captions/pallas_call | solution.py:261
  32.1 0.9 %collective-permute-done.4.refs_1_ = bf16[160,384]{1,0:T(8,128)(2,1)S(1)} collective-permute-done((bf16[160,384]{1,0:T(8,128)(2,1)S(1)}, bf16[160,384]{1,0:T(8,128)(2,1)S(1)}, u32[]{:S(2)}, u32[]{:S(2)}) %collective-permute-start.4) | collective-permute-done | bytes 122912 | tf_op jit(solution)/shard_map/ppermute | solution.py:28
  32.9 1.7 %collective-permute-done.5.refs_2_ = bf16[160,384]{1,0:T(8,128)(2,1)S(1)} collective-permute-done((bf16[160,384]{1,0:T(8,128)(2,1)S(1)}, bf16[160,384]{1,0:T(8,128)(2,1)S(1)}, u32[]{:S(2)}, u32[]{:S(2)}) %collective-permute-start.5) | collective-permute-done | bytes 122912 | tf_op jit(solution)/shard_map/ppermute | solution.py:28
  34.7 2.1 %collective-permute-done.6.refs_3_ = bf16[160,384]{1,0:T(8,128)(2,1)S(1)} collective-permute-done((bf16[160,384]{1,0:T(8,128)(2,1)S(1)}, bf16[160,384]{1,0:T(8,128)(2,1)S(1)}, u32[]{:S(2)}, u32[]{:S(2)}) %collective-permute-start.6) | collective-permute-done | bytes 122912 | tf_op jit(solution)/shard_map/ppermute | solution.py:28
  36.7 1.7 %weights.1 = (f32[1,384]{1,0:T(1,128)S(1)}, bf16[8,176,128]{2,1,0:T(8,128)(2,1)}) custom-call(f32[152,384]{1,0:T(8,128)S(1)} %get-tuple-element.22.refs_0_, bf16[160,384]{1,0:T(8,128)(2,1)S(1)} %collective-permute-done.4.refs_1_, bf16[160,384]{1,0:T(8,128)(2,1)S(1)} %collective-permute-done.5.refs_2_, bf16[160,384]{1,0:T(8,128)(2,1)S(1)} %collective-permute-done.6.refs_3_, ...), custom_call_target="tpu_custom_call" | custom-call | tf_op jit(solution)/shard_map/weights/pallas_call | solution.py:302
  38.5 5.5 %all-to-all-start = ((bf16[8,176,128]{2,1,0:T(8,128)(2,1)}), bf16[8,176,128]{2,1,0:T(8,128)(2,1)S(1)}, u32[]{:S(2)}, u32[]{:S(2)}) async-start(bf16[8,176,128]{2,1,0:T(8,128)(2,1)} %get-tuple-element.36), calls=%async_computation | async-start | bytes 720896 | tf_op jit(solution)/shard_map/all_to_all | solution.py:313
  44.0 2.0 %collective-permute-start.7 = (bf16[2,48,1152]{2,1,0:T(8,128)(2,1)S(1)}, bf16[2,48,1152]{2,1,0:T(8,128)(2,1)S(1)}, u32[]{:S(2)}, u32[]{:S(2)}) collective-permute-start(bf16[2,48,1152]{2,1,0:T(8,128)(2,1)S(1)} %get-tuple-element.33), channel_id=1, source_target_pairs={{0,8},{1,9},{2,10},{3,11},{4,12},{5,13},{6,14},{7,15},{8,0},{9,1},... | collective-permute-start | bytes 663560 | tf_op jit(solution)/shard_map/ppermute | solution.py:28
  46.0 10.3 %collective-permute-done.7.got_ref = bf16[2,48,1152]{2,1,0:T(8,128)(2,1)S(1)} collective-permute-done((bf16[2,48,1152]{2,1,0:T(8,128)(2,1)S(1)}, bf16[2,48,1152]{2,1,0:T(8,128)(2,1)S(1)}, u32[]{:S(2)}, u32[]{:S(2)}) %collective-permute-start.7) | collective-permute-done | bytes 221216 | tf_op jit(solution)/shard_map/ppermute | solution.py:28
  56.3 2.4 %collective-permute-start.8 = (bf16[1,48,1152]{2,1,0:T(8,128)(2,1)S(1)}, bf16[1,48,1152]{2,1,0:T(8,128)(2,1)S(1)}, u32[]{:S(2)}, u32[]{:S(2)}) collective-permute-start(bf16[1,48,1152]{2,1,0:T(8,128)(2,1)S(1)} %get-tuple-element.35), channel_id=1, source_target_pairs={{0,16},{1,17},{2,18},{3,19},{4,20},{5,21},{6,22},{7,23},{8,24},{9,... | collective-permute-start | bytes 331784 | tf_op jit(solution)/shard_map/ppermute | solution.py:28
  58.7 4.2 %collective-permute-done.8.got_ref = bf16[1,48,1152]{2,1,0:T(8,128)(2,1)S(1)} collective-permute-done((bf16[1,48,1152]{2,1,0:T(8,128)(2,1)S(1)}, bf16[1,48,1152]{2,1,0:T(8,128)(2,1)S(1)}, u32[]{:S(2)}, u32[]{:S(2)}) %collective-permute-start.8) | collective-permute-done | bytes 110624 | tf_op jit(solution)/shard_map/ppermute | solution.py:28
  62.9 0.7 %caption_total.1 = f32[48,1152]{1,0:T(8,128)} custom-call(f32[1,48,1152]{2,1,0:T(8,128)S(1)} %get-tuple-element.34.own_ref, bf16[1,48,1152]{2,1,0:T(8,128)(2,1)S(1)} %collective-permute-done.8.got_ref), custom_call_target="tpu_custom_call" | custom-call | tf_op jit(solution)/shard_map/caption_total/pallas_call | solution.py:344
  63.6 0.6 dynamic-slice_bitcast_fusion
  64.2 0.9 %weight_total.1 = f32[144,288]{1,0:T(8,128)} custom-call(bf16[8,176,128]{2,1,0:T(8,128)(2,1)S(1)} %all-to-all-done.got_ref), custom_call_target="tpu_custom_call" | custom-call | tf_op jit(solution)/shard_map/weight_total/pallas_call | solution.py:314
  (9 shorter events, 0.2 us)
Async XLA Ops:
  0.6 18.2 %collective-permute-start.1 = (bf16[48,1152]{1,0:T(8,128)(2,1)}, bf16[48,1152]{1,0:T(8,128)(2,1)S(1)}, u32[]{:S(2)}, u32[]{:S(2)}) collective-permute-start(bf16[48,1152]{1,0:T(8,128)(2,1)} %refs_5_.1), channel_id=1, source_target_pairs={{0,16},{1,17},{2,18},{3,19},{4,20},{5,21},{6,22},{7,23},{8,24},{9,... | collective-permute-start | bytes 331784 | tf_op jit(solution)/shard_map/ppermute | solution.py:28
  4.7 14.1 %collective-permute-start = (bf16[48,1152]{1,0:T(8,128)(2,1)}, bf16[48,1152]{1,0:T(8,128)(2,1)S(1)}, u32[]{:S(2)}, u32[]{:S(2)}) collective-permute-start(bf16[48,1152]{1,0:T(8,128)(2,1)} %refs_5_.1), channel_id=1, source_target_pairs={{0,8},{1,9},{2,10},{3,11},{4,12},{5,13},{6,14},{7,15},{8,0},{9,1},... | collective-permute-start | bytes 331784 | tf_op jit(solution)/shard_map/ppermute | solution.py:28
  6.3 12.6 %collective-permute-start.2 = (bf16[48,1152]{1,0:T(8,128)(2,1)}, bf16[48,1152]{1,0:T(8,128)(2,1)S(1)}, u32[]{:S(2)}, u32[]{:S(2)}) collective-permute-start(bf16[48,1152]{1,0:T(8,128)(2,1)} %refs_5_.1), channel_id=1, source_target_pairs={{0,24},{1,25},{2,26},{3,27},{4,28},{5,29},{6,30},{7,31},{8,16},{9,... | collective-permute-start | bytes 331784 | tf_op jit(solution)/shard_map/ppermute | solution.py:28
  18.9 1.8 %copy-start = (bf16[1152,1152]{1,0:T(8,128)(2,1)S(1)}, bf16[1152,1152]{1,0:T(8,128)(2,1)}, u32[]{:S(2)}) copy-start(bf16[1152,1152]{1,0:T(8,128)(2,1)} %refs_3_.1) | copy-start | bytes 7962628
  20.6 0.9 %copy-start.1 = (bf16[48,1152]{1,0:T(8,128)(2,1)S(1)}, bf16[48,1152]{1,0:T(8,128)(2,1)}, u32[]{:S(2)}) copy-start(bf16[48,1152]{1,0:T(8,128)(2,1)} %refs_5_.1) | copy-start | bytes 331780
  25.2 1.9 %collective-permute-start.3 = (bf16[4,160,384]{2,1,0:T(8,128)(2,1)S(1)}, bf16[4,160,384]{2,1,0:T(8,128)(2,1)S(1)}, u32[]{:S(2)}, u32[]{:S(2)}) collective-permute-start(bf16[4,160,384]{2,1,0:T(8,128)(2,1)S(1)} %get-tuple-element.21), channel_id=1, source_target_pairs={{0,1},{1,0},{2,3},{3,2},{4,5},{5,4},{6,7},{7,6},{8,9},{9,8},{10,11... | collective-permute-start | bytes 1474568 | tf_op jit(solution)/shard_map/ppermute | solution.py:28
  27.3 5.6 %collective-permute-start.4 = (bf16[160,384]{1,0:T(8,128)(2,1)S(1)}, bf16[160,384]{1,0:T(8,128)(2,1)S(1)}, u32[]{:S(2)}, u32[]{:S(2)}) collective-permute-start(bf16[160,384]{1,0:T(8,128)(2,1)S(1)} %get-tuple-element.23), channel_id=1, source_target_pairs={{0,2},{1,3},{2,0},{3,1},{4,6},{5,7},{6,4},{7,5},{8,10},{9,11},{10,... | collective-permute-start | bytes 368648 | tf_op jit(solution)/shard_map/ppermute | solution.py:28
  28.5 6.2 %collective-permute-start.5 = (bf16[160,384]{1,0:T(8,128)(2,1)S(1)}, bf16[160,384]{1,0:T(8,128)(2,1)S(1)}, u32[]{:S(2)}, u32[]{:S(2)}) collective-permute-start(bf16[160,384]{1,0:T(8,128)(2,1)S(1)} %get-tuple-element.24), channel_id=1, source_target_pairs={{0,4},{1,5},{2,6},{3,7},{4,0},{5,1},{6,2},{7,3},{8,12},{9,13},{10,... | collective-permute-start | bytes 368648 | tf_op jit(solution)/shard_map/ppermute | solution.py:28
  29.3 7.4 %collective-permute-start.6 = (bf16[160,384]{1,0:T(8,128)(2,1)S(1)}, bf16[160,384]{1,0:T(8,128)(2,1)S(1)}, u32[]{:S(2)}, u32[]{:S(2)}) collective-permute-start(bf16[160,384]{1,0:T(8,128)(2,1)S(1)} %get-tuple-element.25), channel_id=1, source_target_pairs={{0,6},{1,7},{2,4},{3,5},{4,2},{5,3},{6,0},{7,1},{8,14},{9,15},{10,... | collective-permute-start | bytes 368648 | tf_op jit(solution)/shard_map/ppermute | solution.py:28
  38.5 25.7 %all-to-all-start = ((bf16[8,176,128]{2,1,0:T(8,128)(2,1)}), bf16[8,176,128]{2,1,0:T(8,128)(2,1)S(1)}, u32[]{:S(2)}, u32[]{:S(2)}) async-start(bf16[8,176,128]{2,1,0:T(8,128)(2,1)} %get-tuple-element.36), calls=%async_computation | async-start | bytes 720896 | tf_op jit(solution)/shard_map/all_to_all | solution.py:313
  44.0 12.3 %collective-permute-start.7 = (bf16[2,48,1152]{2,1,0:T(8,128)(2,1)S(1)}, bf16[2,48,1152]{2,1,0:T(8,128)(2,1)S(1)}, u32[]{:S(2)}, u32[]{:S(2)}) collective-permute-start(bf16[2,48,1152]{2,1,0:T(8,128)(2,1)S(1)} %get-tuple-element.33), channel_id=1, source_target_pairs={{0,8},{1,9},{2,10},{3,11},{4,12},{5,13},{6,14},{7,15},{8,0},{9,1},... | collective-permute-start | bytes 663560 | tf_op jit(solution)/shard_map/ppermute | solution.py:28
  56.3 6.6 %collective-permute-start.8 = (bf16[1,48,1152]{2,1,0:T(8,128)(2,1)S(1)}, bf16[1,48,1152]{2,1,0:T(8,128)(2,1)S(1)}, u32[]{:S(2)}, u32[]{:S(2)}) collective-permute-start(bf16[1,48,1152]{2,1,0:T(8,128)(2,1)S(1)} %get-tuple-element.35), channel_id=1, source_target_pairs={{0,16},{1,17},{2,18},{3,19},{4,20},{5,21},{6,22},{7,23},{8,24},{9,... | collective-permute-start | bytes 331784 | tf_op jit(solution)/shard_map/ppermute | solution.py:28

commit v6 on v5

--- a/solution.py
+++ b/solution.py
@@ -16,7 +16,6 @@
 SMEM = pl.BlockSpec(memory_space=pltpu.SMEM)
 NT = (((1,), (1,)), ((), ()))
 TN = (((0,), (0,)), ((), ()))
-HBM = pl.BlockSpec(memory_space=pltpu.HBM)
 MIB = 1024 * 1024
 
 
@@ -51,34 +50,23 @@
 
 
 def pair_kernel(narrow, group, spread, *refs):
-    member_ref, log_scale_ref, bias_ref, weight_ref, feats_ref = refs[:5]
-    texts = refs[5 : 5 + spread]
-    outs = refs[5 + spread :]
+    member_ref, log_scale_ref, bias_ref, proj_ref = refs[:4]
+    texts = refs[4 : 4 + spread]
+    outs = refs[4 + spread :]
     unit_out, inv_out, emb_out, grad_out, own_out, send_out = outs[:6]
-    unit_all, text_all, d_all, weight, own_text, scalars, sems = outs[6:]
+    unit_all, text_all, d_all = outs[6:]
     rows, width = texts[0].shape
     images = group * rows
     share = width // group
     member = member_ref[0]
-    text_copy = pltpu.make_async_copy(texts[0], own_text, sems.at[0])
-    weight_copy = pltpu.make_async_copy(weight_ref, weight, sems.at[1])
-    scale_copy = pltpu.make_async_copy(log_scale_ref, scalars.at[0], sems.at[2])
-    bias_copy = pltpu.make_async_copy(bias_ref, scalars.at[1], sems.at[3])
-    for copy in (text_copy, scale_copy, bias_copy, weight_copy):
-        copy.start()
-
-    for step in [*range(1, spread), 0]:
-        if step == 0:
-            text_copy.wait()
-        values = (texts[step] if step else own_text)[...].astype(F32)
+
+    for step in range(spread):
+        values = texts[step][...].astype(F32)
         inverse = lax.rsqrt(jnp.sum(values * values, axis=1, keepdims=True) + 1e-06)
         text_all[step * rows : (step + 1) * rows, :] = (values * inverse).astype(BF16)
-
-    weight_copy.wait()
     for start in range(0, images, LANES):
         cols = slice(start, start + LANES)
-        proj = jnp.dot(feats_ref[cols, :], weight[...], preferred_element_type=F32)
-        turned = proj.T
+        turned = proj_ref[cols, :].T
         inverse = lax.rsqrt(jnp.sum(turned * turned, axis=0, keepdims=True) + 1e-06)
         unit = turned * inverse
         inv_out[:, cols] = inverse
@@ -87,10 +75,8 @@
     block = pl.multiple_of(column_block(member, narrow) * share, share)
     unit_out[...] = unit_all[pl.ds(block, share), :]
 
-    scale_copy.wait()
-    bias_copy.wait()
-    scale = jnp.exp(jnp.full((1, 1), scalars[0, 0], F32))
-    shift = scalars[1, 0]
+    scale = jnp.exp(jnp.full((1, 1), log_scale_ref[0], F32))
+    shift = bias_ref[0]
     count = 4 * rows if spread % 4 == 0 else rows
     chunks = spread * rows // count
 
@@ -232,9 +218,10 @@
     texts = [text_embed] + [swapped(text_embed, total, step * group) for step in range(1, spread)]
 
     all_feats = lax.all_gather(image_feats, AXES[1:], axis=0, tiled=True)
+    zproj = jnp.dot(all_feats, proj_weight, preferred_element_type=F32)
     results = pl.pallas_call(
         functools.partial(pair_kernel, narrow, group, spread),
-        in_specs=[SMEM, HBM, HBM, HBM, VMEM, HBM] + [VMEM] * (spread - 1),
+        in_specs=[SMEM] * 3 + [VMEM] * (1 + spread),
         out_specs=[VMEM] * 6,
         out_shape=[
             jax.ShapeDtypeStruct((share, images), F32),
@@ -248,14 +235,10 @@
             pltpu.VMEM((width, images), F32),
             pltpu.VMEM((spread * rows, width), BF16),
             pltpu.VMEM((width, images), F32),
-            pltpu.VMEM((width, width), BF16),
-            pltpu.VMEM((rows, width), BF16),
-            pltpu.SMEM((2, 1), F32),
-            pltpu.SemaphoreType.DMA((4,)),
         ],
         compiler_params=limit(24 if spread <= 4 else 40),
         name="pairs",
-    )(member, log_scale, logit_bias, proj_weight, all_feats, *texts)
+    )(member, log_scale, logit_bias, zproj, *texts)
     unit_part, inv_part, img_emb, grad_tile, own_part, sent_part = results
     got_part = swapped(sent_part, total, 1)
     feats_t, own_text, sent_text = pl.pallas_call(
@@ -267,6 +250,8 @@
         compiler_params=limit(12 if spread <= 4 else 24),
         name="captions",
     )(grad_tile, img_emb, all_feats)
+    own_part, got_part, sent_text = lax.optimization_barrier((own_part, got_part, sent_text))
+    got_text = swapped(sent_text, total, group)
     own_part, *chip_parts = pl.pallas_call(
         chip_kernel,
         in_specs=[VMEM] * 2,
@@ -277,9 +262,9 @@
         name="chip_sum",
     )(own_part, got_part)
     got = [swapped(value, total, 2 * index) for index, value in enumerate(chip_parts, 1)]
+    got, got_text = lax.optimization_barrier((got, got_text))
 
     mask = group
-    got_text = swapped(sent_text, total, mask)
     while own_text.shape[0] > 1:
         mask *= 2
         own_text, sent_text = pl.pallas_call(

time: 65.4 us -> 63.4 us (0.969)
  waiting for transfers between devices: 20.7 us -> 15.1 us
  local copies, waits for them, and re-layouts: 3.22 us -> 6.32 us
  matrix products: 0 us -> 2.65 us
  Pallas kernels: 8.39 us -> 6.92 us
  starting transfers between devices: 19.6 us -> 18.7 us
    ppermute x9, waiting for transfers between devices: 20.6 us -> 15.1 us  [swapped(): lax.ppermute(value, AXES, [(source, source ^ mask) for source in range(to...]
    unnamed x4 -> x16, local copies, waits for them, and re-layouts: 2.64 us -> 5.74 us
    dot_general x0 -> x1, matrix products: none -> 2.65 us  [local(): zproj = jnp.dot(all_feats, proj_weight, preferred_element_type=F32)]
    ppermute x9, starting transfers between devices: 14.1 us -> 13.3 us  [swapped(): lax.ppermute(value, AXES, [(source, source ^ mask) for source in range(to...]
    pallas_call x1, Pallas kernels: 1.73 us -> 0.97 us  [local(): pl.pallas_call(functools.partial(weight_kernel, group, wide), in_specs=[V...]
    pallas_call x1, Pallas kernels: 3.71 us -> 3.03 us  [local(): pl.pallas_call(functools.partial(pair_kernel, narrow, group, spread), in_...]
  transfers between devices with their start and end apart: 10 -> 10, of which waited for: 6 -> 5; matrix products, arithmetic and copies ran while one was open for 1% -> 5% of each run, Pallas kernels for 3% -> 3%
where the time goes in v6:
time: 63.4 us; the launch traced here: 63 us
  starting transfers between devices  18.7 us (29%)
  waiting for transfers between devices  15.1 us (24%)
  blocking collectives  11.2 us (18%)
  Pallas kernels  6.92 us (11%)
  local copies, waits for them, and re-layouts  6.32 us (10%)
  matrix products  2.65 us (4%)
  between operations  2.03 us (3%)
    ppermute x9, waiting for transfers between devices, swapped(): lax.ppermute(value, AXES, [(source, source ^ mask) for source in range(to...  15.1 us
    ppermute x9, starting transfers between devices, swapped(): lax.ppermute(value, AXES, [(source, source ^ mask) for source in range(to...  13.3 us
    all_gather x1, blocking collectives, local(): all_feats = lax.all_gather(image_feats, AXES[1:], axis=0, tiled=True)  11.2 us
    unnamed x16, local copies, waits for them, and re-layouts  5.74 us
    all_to_all x1, starting transfers between devices, local(): got_weight = lax.all_to_all(sent_weight, AXES[:2], 0, 0)  5.35 us
    pallas_call x1, Pallas kernels, local(): pl.pallas_call(functools.partial(pair_kernel, narrow, group, spread), in_...  3.03 us
    dot_general x1, matrix products, local(): zproj = jnp.dot(all_feats, proj_weight, preferred_element_type=F32)  2.65 us
  transfers between devices with their start and end apart: 10, of which 5 were waited for; matrix products, arithmetic and copies ran while one was open for 5% of the time, Pallas kernels for 3%

profile of v6, /device:TPU:0, one launch (start us, length us, event | category | flops | bytes accessed | tf_op | source)
XLA Modules:
  0.0 63.0 jit_solution(2254874309226169383)
XLA Ops:
  0.6 3.1 %collective-permute-start = (bf16[48,1152]{1,0:T(8,128)(2,1)}, bf16[48,1152]{1,0:T(8,128)(2,1)}, u32[]{:S(2)}, u32[]{:S(2)}) collective-permute-start(bf16[48,1152]{1,0:T(8,128)(2,1)} %refs_4_.1), channel_id=1, source_target_pairs={{0,8},{1,9},{2,10},{3,11},{4,12},{5,13},{6,14},{7,15},{8,0},{9,1},... | collective-permute-start | bytes 331784 | tf_op jit(solution)/shard_map/ppermute | solution.py:27
  3.7 2.6 %collective-permute-start.1 = (bf16[48,1152]{1,0:T(8,128)(2,1)}, bf16[48,1152]{1,0:T(8,128)(2,1)}, u32[]{:S(2)}, u32[]{:S(2)}) collective-permute-start(bf16[48,1152]{1,0:T(8,128)(2,1)} %refs_4_.1), channel_id=1, source_target_pairs={{0,16},{1,17},{2,18},{3,19},{4,20},{5,21},{6,22},{7,23},{8,24},{9,... | collective-permute-start | bytes 331784 | tf_op jit(solution)/shard_map/ppermute | solution.py:27
  6.3 11.2 %all_gather.3.feats_ref.refs_6_ = bf16[384,1152]{1,0:T(8,128)(2,1)S(1)} all-gather(bf16[48,1152]{1,0:T(8,128)(2,1)} %param.5), channel_id=1, replica_groups=mesh['outer'=4,'inner'=2,'narrow'=4] {'inner','narrow'}, dimensions={0}, use_global_device_ids=true | all-gather | bytes 995328 | tf_op jit(solution)/shard_map/all_gather | solution.py:220
  17.6 2.6 %fusion.refs_3_ = f32[384,1152]{1,0:T(8,128)} fusion(bf16[384,1152]{1,0:T(8,128)(2,1)S(1)} %all_gather.3.feats_ref.refs_6_, bf16[1152,1152]{1,0:T(8,128)(2,1)S(1)} %copy-done), kind=kOutput, calls=%fused_computation.1 | convolution fusion | flops 1019215872 | bytes 5308416 | tf_op jit(solution)/shard_map/dot_general | solution.py:221
  21.6 1.5 %copy-done.1 = f32[384,1152]{1,0:T(8,128)S(1)} copy-done((f32[384,1152]{1,0:T(8,128)S(1)}, f32[384,1152]{1,0:T(8,128)}, u32[]{:S(2)}) %copy-start.1) | copy-done | bytes 1769496
  23.0 0.9 %copy-done.7 = bf16[48,1152]{1,0:T(8,128)(2,1)S(1)} copy-done((bf16[48,1152]{1,0:T(8,128)(2,1)S(1)}, bf16[48,1152]{1,0:T(8,128)(2,1)}, u32[]{:S(2)}) %copy-start.7) | copy-done | bytes 110616
  23.9 3.0 %pairs.1 = (f32[144,384]{1,0:T(8,128)S(1)}, f32[1,384]{1,0:T(1,128)S(1)}, bf16[1152,384]{1,0:T(8,128)(2,1)S(1)}, bf16[192,384]{1,0:T(8,128)(2,1)S(1)}, f32[4,152...) custom-call(s32[1]{0:T(128)} %bitcast.refs_0_, f32[1]{0:T(128)S(6)} %copy.8.refs_1_, f32[1]{0:T(128)S(6)} %copy.9.refs_2_, ...), custom_call_target="tpu_custom_call" | custom-call | tf_op jit(solution)/shard_map/pairs/pallas_call | solution.py:222
  27.4 1.2 %captions.1 = (bf16[1152,384]{1,0:T(8,128)(2,1)S(1)}, f32[2,48,1152]{2,1,0:T(8,128)S(1)}, bf16[2,48,1152]{2,1,0:T(8,128)(2,1)S(1)}) custom-call(bf16[192,384]{1,0:T(8,128)(2,1)S(1)} %get-tuple-element.29.grad_ref, bf16[1152,384]{1,0:T(8,128)(2,1)S(1)} %get-tuple-element.30.emb_ref, bf16[384,1152]{1,0:T(8,128)(2,1)S(1)} %all_gather.3.feats_ref.refs_6_), custom_call_target="tpu_custom_call" | custom-call | tf_op jit(solution)/shard_map/captions/pallas_call | solution.py:244
  28.9 0.7 %collective-permute-start.7 = (bf16[2,48,1152]{2,1,0:T(8,128)(2,1)S(1)}, bf16[2,48,1152]{2,1,0:T(8,128)(2,1)S(1)}, u32[]{:S(2)}, u32[]{:S(2)}) collective-permute-start(bf16[2,48,1152]{2,1,0:T(8,128)(2,1)S(1)} %get-tuple-element.38), channel_id=1, source_target_pairs={{0,8},{1,9},{2,10},{3,11},{4,12},{5,13},{6,14},{7,15},{8,0},{9,1},... | collective-permute-start | bytes 663560 | tf_op jit(solution)/shard_map/ppermute | solution.py:27
  29.7 1.2 %collective-permute-start.4 = (bf16[160,384]{1,0:T(8,128)(2,1)S(1)}, bf16[160,384]{1,0:T(8,128)(2,1)S(1)}, u32[]{:S(2)}, u32[]{:S(2)}) collective-permute-start(bf16[160,384]{1,0:T(8,128)(2,1)S(1)} %get-tuple-element.35), channel_id=1, source_target_pairs={{0,2},{1,3},{2,0},{3,1},{4,6},{5,7},{6,4},{7,5},{8,10},{9,11},{10,... | collective-permute-start | bytes 368648 | tf_op jit(solution)/shard_map/ppermute | solution.py:27
  30.9 0.9 %collective-permute-start.5 = (bf16[160,384]{1,0:T(8,128)(2,1)S(1)}, bf16[160,384]{1,0:T(8,128)(2,1)S(1)}, u32[]{:S(2)}, u32[]{:S(2)}) collective-permute-start(bf16[160,384]{1,0:T(8,128)(2,1)S(1)} %get-tuple-element.36), channel_id=1, source_target_pairs={{0,4},{1,5},{2,6},{3,7},{4,0},{5,1},{6,2},{7,3},{8,12},{9,13},{10,... | collective-permute-start | bytes 368648 | tf_op jit(solution)/shard_map/ppermute | solution.py:27
  31.7 1.5 %collective-permute-start.6 = (bf16[160,384]{1,0:T(8,128)(2,1)S(1)}, bf16[160,384]{1,0:T(8,128)(2,1)S(1)}, u32[]{:S(2)}, u32[]{:S(2)}) collective-permute-start(bf16[160,384]{1,0:T(8,128)(2,1)S(1)} %get-tuple-element.37), channel_id=1, source_target_pairs={{0,6},{1,7},{2,4},{3,5},{4,2},{5,3},{6,0},{7,1},{8,14},{9,15},{10,... | collective-permute-start | bytes 368648 | tf_op jit(solution)/shard_map/ppermute | solution.py:27
  33.2 1.8 %collective-permute-done.4.refs_1_ = bf16[160,384]{1,0:T(8,128)(2,1)S(1)} collective-permute-done((bf16[160,384]{1,0:T(8,128)(2,1)S(1)}, bf16[160,384]{1,0:T(8,128)(2,1)S(1)}, u32[]{:S(2)}, u32[]{:S(2)}) %collective-permute-start.4) | collective-permute-done | bytes 122912 | tf_op jit(solution)/shard_map/ppermute | solution.py:27
  35.1 2.0 %collective-permute-done.5.refs_2_ = bf16[160,384]{1,0:T(8,128)(2,1)S(1)} collective-permute-done((bf16[160,384]{1,0:T(8,128)(2,1)S(1)}, bf16[160,384]{1,0:T(8,128)(2,1)S(1)}, u32[]{:S(2)}, u32[]{:S(2)}) %collective-permute-start.5) | collective-permute-done | bytes 122912 | tf_op jit(solution)/shard_map/ppermute | solution.py:27
  37.1 1.8 %collective-permute-done.6.refs_3_ = bf16[160,384]{1,0:T(8,128)(2,1)S(1)} collective-permute-done((bf16[160,384]{1,0:T(8,128)(2,1)S(1)}, bf16[160,384]{1,0:T(8,128)(2,1)S(1)}, u32[]{:S(2)}, u32[]{:S(2)}) %collective-permute-start.6) | collective-permute-done | bytes 122912 | tf_op jit(solution)/shard_map/ppermute | solution.py:27
  39.5 1.0 %weights.1 = (f32[1,384]{1,0:T(1,128)S(1)}, bf16[8,176,128]{2,1,0:T(8,128)(2,1)S(1)}) custom-call(f32[152,384]{1,0:T(8,128)S(1)} %get-tuple-element.34.refs_0_, bf16[160,384]{1,0:T(8,128)(2,1)S(1)} %collective-permute-done.4.refs_1_, bf16[160,384]{1,0:T(8,128)(2,1)S(1)} %collective-permute-done.5.refs_2_, ...), custom_call_target="tpu_custom_call" | custom-call | tf_op jit(solution)/shard_map/weights/pallas_call | solution.py:287
  40.5 0.7 %copy-done.4 = bf16[8,176,128]{2,1,0:T(8,128)(2,1)} copy-done((bf16[8,176,128]{2,1,0:T(8,128)(2,1)}, bf16[8,176,128]{2,1,0:T(8,128)(2,1)S(1)}, u32[]{:S(2)}) %copy-start.4) | copy-done | bytes 360472
  41.2 5.3 %all-to-all-start = ((bf16[8,176,128]{2,1,0:T(8,128)(2,1)}), bf16[8,176,128]{2,1,0:T(8,128)(2,1)S(1)}, u32[]{:S(2)}, u32[]{:S(2)}) async-start(bf16[8,176,128]{2,1,0:T(8,128)(2,1)} %copy-done.4), calls=%async_computation | async-start | bytes 720896 | tf_op jit(solution)/shard_map/all_to_all | solution.py:298
  46.6 1.0 %copy-done.3 = f32[2,48,1152]{2,1,0:T(8,128)S(1)} copy-done((f32[2,48,1152]{2,1,0:T(8,128)S(1)}, f32[2,48,1152]{2,1,0:T(8,128)}, u32[]{:S(2)}) %copy-start.3) | copy-done | bytes 442392
  47.6 0.9 %copy-done.6 = bf16[2,48,1152]{2,1,0:T(8,128)(2,1)S(1)} copy-done((bf16[2,48,1152]{2,1,0:T(8,128)(2,1)S(1)}, bf16[2,48,1152]{2,1,0:T(8,128)(2,1)}, u32[]{:S(2)}) %copy-start.6) | copy-done | bytes 221208
  48.6 3.0 %collective-permute-start.8 = (bf16[1,48,1152]{2,1,0:T(8,128)(2,1)S(1)}, bf16[1,48,1152]{2,1,0:T(8,128)(2,1)S(1)}, u32[]{:S(2)}, u32[]{:S(2)}) collective-permute-start(bf16[1,48,1152]{2,1,0:T(8,128)(2,1)S(1)} %get-tuple-element.49), channel_id=1, source_target_pairs={{0,16},{1,17},{2,18},{3,19},{4,20},{5,21},{6,22},{7,23},{8,24},{9,... | collective-permute-start | bytes 331784 | tf_op jit(solution)/shard_map/ppermute | solution.py:27
  52.2 9.2 %collective-permute-done.8.got_ref = bf16[1,48,1152]{2,1,0:T(8,128)(2,1)S(1)} collective-permute-done((bf16[1,48,1152]{2,1,0:T(8,128)(2,1)S(1)}, bf16[1,48,1152]{2,1,0:T(8,128)(2,1)S(1)}, u32[]{:S(2)}, u32[]{:S(2)}) %collective-permute-start.8) | collective-permute-done | bytes 110624 | tf_op jit(solution)/shard_map/ppermute | solution.py:27
  61.4 0.7 %caption_total.1 = f32[48,1152]{1,0:T(8,128)} custom-call(f32[1,48,1152]{2,1,0:T(8,128)S(1)} %get-tuple-element.48.own_ref, bf16[1,48,1152]{2,1,0:T(8,128)(2,1)S(1)} %collective-permute-done.8.got_ref), custom_call_target="tpu_custom_call" | custom-call | tf_op jit(solution)/shard_map/caption_total/pallas_call | solution.py:329
  62.1 0.9 %weight_total.1 = f32[144,288]{1,0:T(8,128)} custom-call(bf16[8,176,128]{2,1,0:T(8,128)(2,1)S(1)} %all-to-all-done.got_ref), custom_call_target="tpu_custom_call" | custom-call | tf_op jit(solution)/shard_map/weight_total/pallas_call | solution.py:299
  (22 shorter events, 2.1 us)
Async XLA Ops:
  0.6 16.9 %copy-start = (bf16[1152,1152]{1,0:T(8,128)(2,1)S(1)}, bf16[1152,1152]{1,0:T(8,128)(2,1)}, u32[]{:S(2)}) copy-start(bf16[1152,1152]{1,0:T(8,128)(2,1)} %param.6) | copy-start | bytes 7962628
  0.6 20.9 %collective-permute-start = (bf16[48,1152]{1,0:T(8,128)(2,1)}, bf16[48,1152]{1,0:T(8,128)(2,1)}, u32[]{:S(2)}, u32[]{:S(2)}) collective-permute-start(bf16[48,1152]{1,0:T(8,128)(2,1)} %refs_4_.1), channel_id=1, source_target_pairs={{0,8},{1,9},{2,10},{3,11},{4,12},{5,13},{6,14},{7,15},{8,0},{9,1},... | collective-permute-start | bytes 331784 | tf_op jit(solution)/shard_map/ppermute | solution.py:27
  3.7 17.8 %collective-permute-start.1 = (bf16[48,1152]{1,0:T(8,128)(2,1)}, bf16[48,1152]{1,0:T(8,128)(2,1)}, u32[]{:S(2)}, u32[]{:S(2)}) collective-permute-start(bf16[48,1152]{1,0:T(8,128)(2,1)} %refs_4_.1), channel_id=1, source_target_pairs={{0,16},{1,17},{2,18},{3,19},{4,20},{5,21},{6,22},{7,23},{8,24},{9,... | collective-permute-start | bytes 331784 | tf_op jit(solution)/shard_map/ppermute | solution.py:27
  6.3 15.2 %collective-permute-start.2 = (bf16[48,1152]{1,0:T(8,128)(2,1)}, bf16[48,1152]{1,0:T(8,128)(2,1)}, u32[]{:S(2)}, u32[]{:S(2)}) collective-permute-start(bf16[48,1152]{1,0:T(8,128)(2,1)} %refs_4_.1), channel_id=1, source_target_pairs={{0,24},{1,25},{2,26},{3,27},{4,28},{5,29},{6,30},{7,31},{8,16},{9,... | collective-permute-start | bytes 331784 | tf_op jit(solution)/shard_map/ppermute | solution.py:27
  21.5 1.5 %copy-start.1 = (f32[384,1152]{1,0:T(8,128)S(1)}, f32[384,1152]{1,0:T(8,128)}, u32[]{:S(2)}) copy-start(f32[384,1152]{1,0:T(8,128)} %fusion.refs_3_) | copy-start | bytes 5308420
  23.0 0.9 %copy-start.7 = (bf16[48,1152]{1,0:T(8,128)(2,1)S(1)}, bf16[48,1152]{1,0:T(8,128)(2,1)}, u32[]{:S(2)}) copy-start(bf16[48,1152]{1,0:T(8,128)(2,1)} %refs_4_.1) | copy-start | bytes 331780
  27.0 1.9 %collective-permute-start.3 = (bf16[4,160,384]{2,1,0:T(8,128)(2,1)S(1)}, bf16[4,160,384]{2,1,0:T(8,128)(2,1)S(1)}, u32[]{:S(2)}, u32[]{:S(2)}) collective-permute-start(bf16[4,160,384]{2,1,0:T(8,128)(2,1)S(1)} %get-tuple-element.28), channel_id=1, source_target_pairs={{0,1},{1,0},{2,3},{3,2},{4,5},{5,4},{6,7},{7,6},{8,9},{9,8},{10,11... | collective-permute-start | bytes 1474568 | tf_op jit(solution)/shard_map/ppermute | solution.py:27
  28.6 1.1 %copy-start.2 = (f32[2,48,1152]{2,1,0:T(8,128)}, f32[2,48,1152]{2,1,0:T(8,128)S(1)}, u32[]{:S(2)}) copy-start(f32[2,48,1152]{2,1,0:T(8,128)S(1)} %get-tuple-element.46.own_ref) | copy-start | bytes 1327108
  28.9 10.0 %collective-permute-start.7 = (bf16[2,48,1152]{2,1,0:T(8,128)(2,1)S(1)}, bf16[2,48,1152]{2,1,0:T(8,128)(2,1)S(1)}, u32[]{:S(2)}, u32[]{:S(2)}) collective-permute-start(bf16[2,48,1152]{2,1,0:T(8,128)(2,1)S(1)} %get-tuple-element.38), channel_id=1, source_target_pairs={{0,8},{1,9},{2,10},{3,11},{4,12},{5,13},{6,14},{7,15},{8,0},{9,1},... | collective-permute-start | bytes 663560 | tf_op jit(solution)/shard_map/ppermute | solution.py:27
  29.7 5.4 %collective-permute-start.4 = (bf16[160,384]{1,0:T(8,128)(2,1)S(1)}, bf16[160,384]{1,0:T(8,128)(2,1)S(1)}, u32[]{:S(2)}, u32[]{:S(2)}) collective-permute-start(bf16[160,384]{1,0:T(8,128)(2,1)S(1)} %get-tuple-element.35), channel_id=1, source_target_pairs={{0,2},{1,3},{2,0},{3,1},{4,6},{5,7},{6,4},{7,5},{8,10},{9,11},{10,... | collective-permute-start | bytes 368648 | tf_op jit(solution)/shard_map/ppermute | solution.py:27
  30.9 6.2 %collective-permute-start.5 = (bf16[160,384]{1,0:T(8,128)(2,1)S(1)}, bf16[160,384]{1,0:T(8,128)(2,1)S(1)}, u32[]{:S(2)}, u32[]{:S(2)}) collective-permute-start(bf16[160,384]{1,0:T(8,128)(2,1)S(1)} %get-tuple-element.36), channel_id=1, source_target_pairs={{0,4},{1,5},{2,6},{3,7},{4,0},{5,1},{6,2},{7,3},{8,12},{9,13},{10,... | collective-permute-start | bytes 368648 | tf_op jit(solution)/shard_map/ppermute | solution.py:27
  31.7 7.1 %collective-permute-start.6 = (bf16[160,384]{1,0:T(8,128)(2,1)S(1)}, bf16[160,384]{1,0:T(8,128)(2,1)S(1)}, u32[]{:S(2)}, u32[]{:S(2)}) collective-permute-start(bf16[160,384]{1,0:T(8,128)(2,1)S(1)} %get-tuple-element.37), channel_id=1, source_target_pairs={{0,6},{1,7},{2,4},{3,5},{4,2},{5,3},{6,0},{7,1},{8,14},{9,15},{10,... | collective-permute-start | bytes 368648 | tf_op jit(solution)/shard_map/ppermute | solution.py:27
  38.9 0.7 %copy-start.5 = (bf16[2,48,1152]{2,1,0:T(8,128)(2,1)}, bf16[2,48,1152]{2,1,0:T(8,128)(2,1)S(1)}, u32[]{:S(2)}) copy-start(bf16[2,48,1152]{2,1,0:T(8,128)(2,1)S(1)} %collective-permute-done.7.got_ref) | copy-start | bytes 663556
  40.5 0.7 %copy-start.4 = (bf16[8,176,128]{2,1,0:T(8,128)(2,1)}, bf16[8,176,128]{2,1,0:T(8,128)(2,1)S(1)}, u32[]{:S(2)}) copy-start(bf16[8,176,128]{2,1,0:T(8,128)(2,1)S(1)} %get-tuple-element.50) | copy-start | bytes 1081348
  41.2 20.8 %all-to-all-start = ((bf16[8,176,128]{2,1,0:T(8,128)(2,1)}), bf16[8,176,128]{2,1,0:T(8,128)(2,1)S(1)}, u32[]{:S(2)}, u32[]{:S(2)}) async-start(bf16[8,176,128]{2,1,0:T(8,128)(2,1)} %copy-done.4), calls=%async_computation | async-start | bytes 720896 | tf_op jit(solution)/shard_map/all_to_all | solution.py:298
  46.6 1.0 %copy-start.3 = (f32[2,48,1152]{2,1,0:T(8,128)S(1)}, f32[2,48,1152]{2,1,0:T(8,128)}, u32[]{:S(2)}) copy-start(f32[2,48,1152]{2,1,0:T(8,128)} %copy-done.2) | copy-start | bytes 1327108
  47.6 0.9 %copy-start.6 = (bf16[2,48,1152]{2,1,0:T(8,128)(2,1)S(1)}, bf16[2,48,1152]{2,1,0:T(8,128)(2,1)}, u32[]{:S(2)}) copy-start(bf16[2,48,1152]{2,1,0:T(8,128)(2,1)} %copy-done.5) | copy-start | bytes 663556
  48.6 12.8 %collective-permute-start.8 = (bf16[1,48,1152]{2,1,0:T(8,128)(2,1)S(1)}, bf16[1,48,1152]{2,1,0:T(8,128)(2,1)S(1)}, u32[]{:S(2)}, u32[]{:S(2)}) collective-permute-start(bf16[1,48,1152]{2,1,0:T(8,128)(2,1)S(1)} %get-tuple-element.49), channel_id=1, source_target_pairs={{0,16},{1,17},{2,18},{3,19},{4,20},{5,21},{6,22},{7,23},{8,24},{9,... | collective-permute-start | bytes 331784 | tf_op jit(solution)/shard_map/ppermute | solution.py:27

commit v7 on v6

--- a/solution.py
+++ b/solution.py
@@ -49,24 +49,71 @@
     return (member % narrow) * 2 + member // narrow
 
 
-def pair_kernel(narrow, group, spread, *refs):
-    member_ref, log_scale_ref, bias_ref, proj_ref = refs[:4]
-    texts = refs[4 : 4 + spread]
-    outs = refs[4 + spread :]
-    unit_out, inv_out, emb_out, grad_out, own_out, send_out = outs[:6]
-    unit_all, text_all, d_all = outs[6:]
-    rows, width = texts[0].shape
-    images = group * rows
+def load_kernel(log_scale_ref, bias_ref, weight_ref, feats_ref, text_ref, weight_out, feats_out, text_out, scalars_out):
+    weight_out[...] = weight_ref[...]
+    feats_out[...] = feats_ref[...]
+    text_out[...] = text_ref[...]
+    row = lax.broadcasted_iota(jnp.int32, scalars_out.shape, 0)
+    scale = jnp.exp(jnp.full(scalars_out.shape, log_scale_ref[0], F32))
+    scalars_out[...] = jnp.where(row == 0, scale, bias_ref[0])
+
+
+def stack_kernel(member_ref, *refs):
+    blocks, out = refs[:-1], refs[-1]
+    rows = blocks[0].shape[0]
+    chip = member_ref[0] // 2
+    for step, block in enumerate(blocks):
+        place = pl.multiple_of((chip ^ step) * rows, rows)
+        out[pl.ds(place, rows), :] = block[...]
+
+
+def text_kernel(*refs):
+    texts, out = refs[:-1], refs[-1]
+    rows = texts[0].shape[0]
+    for step, text in enumerate(texts):
+        values = text[...].astype(F32)
+        inverse = lax.rsqrt(jnp.sum(values * values, axis=1, keepdims=True) + 1e-06)
+        out[step * rows : (step + 1) * rows, :] = (values * inverse).astype(BF16)
+
+
+def first_image(member, rows, group):
+    return (member % 2) * (group // 2 * rows) + (member // 2) * rows
+
+
+def pair_kernel(
+    narrow,
+    group,
+    member_ref,
+    scalars_ref,
+    weight,
+    own_half,
+    got_half,
+    text_all,
+    feats_ref,
+    unit_out,
+    inv_out,
+    emb_out,
+    grad_out,
+    own_out,
+    send_out,
+    unit_all,
+    d_all,
+):
+    images, width = feats_ref.shape
+    rows = images // group
+    spread = text_all.shape[0] // rows
+    half = images // 2
     share = width // group
     member = member_ref[0]
 
-    for step in range(spread):
-        values = texts[step][...].astype(F32)
-        inverse = lax.rsqrt(jnp.sum(values * values, axis=1, keepdims=True) + 1e-06)
-        text_all[step * rows : (step + 1) * rows, :] = (values * inverse).astype(BF16)
+    place = pl.multiple_of((member % 2) * half, half)
+    feats_ref[pl.ds(place, half), :] = own_half[...]
+    place = pl.multiple_of((1 - member % 2) * half, half)
+    feats_ref[pl.ds(place, half), :] = got_half[...]
     for start in range(0, images, LANES):
         cols = slice(start, start + LANES)
-        turned = proj_ref[cols, :].T
+        proj = jnp.dot(feats_ref[cols, :], weight[...], preferred_element_type=F32)
+        turned = proj.T
         inverse = lax.rsqrt(jnp.sum(turned * turned, axis=0, keepdims=True) + 1e-06)
         unit = turned * inverse
         inv_out[:, cols] = inverse
@@ -75,8 +122,8 @@
     block = pl.multiple_of(column_block(member, narrow) * share, share)
     unit_out[...] = unit_all[pl.ds(block, share), :]
 
-    scale = jnp.exp(jnp.full((1, 1), log_scale_ref[0], F32))
-    shift = bias_ref[0]
+    scale = scalars_ref[0:1, 0:1]
+    shift = scalars_ref[1:2, 0:1]
     count = 4 * rows if spread % 4 == 0 else rows
     chunks = spread * rows // count
 
@@ -87,7 +134,7 @@
         logits = scale * products + shift
         caption = lax.broadcasted_iota(jnp.int32, (count, images), 0) + chunk * count
         image = lax.broadcasted_iota(jnp.int32, (count, images), 1)
-        own = jnp.logical_and(caption < rows, image == member * rows + caption)
+        own = jnp.logical_and(caption < rows, image == first_image(member, rows, group) + caption)
         sign = jnp.where(own, 1.0, -1.0).astype(F32)
         away = -sign * logits
         small = jnp.exp(-jnp.abs(away))
@@ -135,22 +182,14 @@
         target[share:, :] = stats
 
 
-def caption_kernel(rows, grad_ref, emb_ref, feats_ref, feats_t, own_out, send_out):
-    for step in range(grad_ref.shape[0] // rows):
+def caption_kernel(rows, grad_ref, emb_ref, feats_ref, feats_t, *outs):
+    for step, target in enumerate(outs):
         grad = grad_ref[step * rows : (step + 1) * rows, :]
         product = lax.dot_general(grad, emb_ref[...], NT, preferred_element_type=F32)
-        target = send_out if step & 1 else own_out
-        target[step // 2] = product.astype(target.dtype)
+        target[...] = product.astype(target.dtype)
     for start in range(0, feats_ref.shape[0], LANES):
         cols = slice(start, start + LANES)
         feats_t[:, cols] = feats_ref[cols, :].astype(F32).T.astype(BF16)
-
-
-def halving_kernel(own_ref, got_ref, own_out, send_out):
-    for step in range(own_ref.shape[0]):
-        total = own_ref[step] + got_ref[step].astype(F32)
-        target = send_out if step & 1 else own_out
-        target[step // 2] = total.astype(target.dtype)
 
 
 def gathered_gradient(own_ref, got, unit_ref, inv_ref, loss_out):
@@ -190,7 +229,16 @@
         send_out[place, rows + rest :, : rows - LANES] = tail[:, begin + LANES : begin + rows]
 
 
-def total_kernel(rest, got_ref, out):
+def total_text(refs, out):
+    total = refs[0][...]
+    for block in refs[1:]:
+        total = total + block[...].astype(F32)
+    out[...] = total
+
+
+def total_kernel(rest, *refs):
+    got_ref, out, text_out = refs[0], refs[-2], refs[-1]
+    total_text(refs[1:-2], text_out)
     rows = out.shape[0]
     for side in range(2):
         half = got_ref[side].astype(F32)
@@ -202,8 +250,8 @@
         out[LANES:, left + LANES : left + LANES + rest] = half[rows + rest :, :].T[: rows - LANES, :]
 
 
-def sum_kernel(own_ref, got_ref, out):
-    out[...] = own_ref[0] + got_ref[0].astype(F32)
+def sum_kernel(*refs):
+    total_text(refs[:-1], refs[-1])
 
 
 def local(wide, narrow, image_feats, proj_weight, text_embed, log_scale, logit_bias):
@@ -215,15 +263,48 @@
     images = group * rows
     member = lax.axis_index(AXES[1:]).astype(jnp.int32).reshape(1)
 
-    texts = [text_embed] + [swapped(text_embed, total, step * group) for step in range(1, spread)]
-
-    all_feats = lax.all_gather(image_feats, AXES[1:], axis=0, tiled=True)
-    zproj = jnp.dot(all_feats, proj_weight, preferred_element_type=F32)
+    texts = [swapped(text_embed, total, step * group) for step in range(1, spread)]
+    got_feats = [swapped(image_feats, total, 2 * step) for step in range(1, group // 2)]
+    arrived = lax.optimization_barrier([got_feats[0], *texts[:0:-1], got_feats[-1], texts[0], *got_feats[1:-1]])
+    got_feats = [arrived[0], *arrived[spread + 1 :], arrived[spread - 1]]
+    texts = [arrived[spread], *arrived[spread - 2 : 0 : -1]]
+    weight, own_feats, own_text, scalars = pl.pallas_call(
+        load_kernel,
+        in_specs=[SMEM] * 2 + [VMEM] * 3,
+        out_specs=[VMEM] * 4,
+        out_shape=[
+            jax.ShapeDtypeStruct((width, width), BF16),
+            jax.ShapeDtypeStruct((rows, width), BF16),
+            jax.ShapeDtypeStruct((rows, width), BF16),
+            jax.ShapeDtypeStruct((8, LANES), F32),
+        ],
+        compiler_params=limit(8),
+        name="load",
+    )(log_scale, logit_bias, proj_weight, image_feats, text_embed)
+    own_half = pl.pallas_call(
+        stack_kernel,
+        in_specs=[SMEM] + [VMEM] * (group // 2),
+        out_specs=VMEM,
+        out_shape=jax.ShapeDtypeStruct((images // 2, width), BF16),
+        compiler_params=limit(4),
+        name="stack",
+    )(member, own_feats, *got_feats)
+    got_half = swapped(own_half, total, 1)
+    text_emb = pl.pallas_call(
+        text_kernel,
+        in_specs=[VMEM] * spread,
+        out_specs=VMEM,
+        out_shape=jax.ShapeDtypeStruct((spread * rows, width), BF16),
+        compiler_params=limit(4 if spread <= 4 else 16),
+        name="text_unit",
+    )(own_text, *texts)
+
     results = pl.pallas_call(
-        functools.partial(pair_kernel, narrow, group, spread),
-        in_specs=[SMEM] * 3 + [VMEM] * (1 + spread),
-        out_specs=[VMEM] * 6,
+        functools.partial(pair_kernel, narrow, group),
+        in_specs=[SMEM] + [VMEM] * 5,
+        out_specs=[VMEM] * 7,
         out_shape=[
+            jax.ShapeDtypeStruct((images, width), BF16),
             jax.ShapeDtypeStruct((share, images), F32),
             jax.ShapeDtypeStruct((1, images), F32),
             jax.ShapeDtypeStruct((width, images), BF16),
@@ -233,25 +314,24 @@
         ],
         scratch_shapes=[
             pltpu.VMEM((width, images), F32),
-            pltpu.VMEM((spread * rows, width), BF16),
             pltpu.VMEM((width, images), F32),
         ],
         compiler_params=limit(24 if spread <= 4 else 40),
         name="pairs",
-    )(member, log_scale, logit_bias, zproj, *texts)
-    unit_part, inv_part, img_emb, grad_tile, own_part, sent_part = results
+    )(member, scalars, weight, own_half, got_half, text_emb)
+    all_feats, unit_part, inv_part, img_emb, grad_tile, own_part, sent_part = results
     got_part = swapped(sent_part, total, 1)
-    feats_t, own_text, sent_text = pl.pallas_call(
+    feats_t, own_text, *sent_text = pl.pallas_call(
         functools.partial(caption_kernel, rows),
         in_specs=[VMEM] * 3,
-        out_specs=[VMEM] * 3,
-        out_shape=[jax.ShapeDtypeStruct((width, images), BF16)]
-        + [jax.ShapeDtypeStruct((spread // 2, rows, width), kind) for kind in (F32, BF16)],
+        out_specs=[VMEM] * (1 + spread),
+        out_shape=[jax.ShapeDtypeStruct((width, images), BF16), jax.ShapeDtypeStruct((rows, width), F32)]
+        + [jax.ShapeDtypeStruct((rows, width), BF16)] * (spread - 1),
         compiler_params=limit(12 if spread <= 4 else 24),
         name="captions",
     )(grad_tile, img_emb, all_feats)
     own_part, got_part, sent_text = lax.optimization_barrier((own_part, got_part, sent_text))
-    got_text = swapped(sent_text, total, group)
+    got_text = [swapped(value, total, step * group) for step, value in enumerate(sent_text, 1)]
     own_part, *chip_parts = pl.pallas_call(
         chip_kernel,
         in_specs=[VMEM] * 2,
@@ -262,22 +342,6 @@
         name="chip_sum",
     )(own_part, got_part)
     got = [swapped(value, total, 2 * index) for index, value in enumerate(chip_parts, 1)]
-    got, got_text = lax.optimization_barrier((got, got_text))
-
-    mask = group
-    while own_text.shape[0] > 1:
-        mask *= 2
-        own_text, sent_text = pl.pallas_call(
-            halving_kernel,
-            in_specs=[VMEM] * 2,
-            out_specs=[VMEM] * 2,
-            out_shape=[
-                jax.ShapeDtypeStruct((own_text.shape[0] // 2, rows, width), kind) for kind in (F32, BF16)
-            ],
-            compiler_params=limit(6 if spread <= 4 else 24),
-            name="caption_half",
-        )(own_text, got_text)
-        got_text = swapped(sent_text, total, mask)
 
     out_rows = width // wide
     rest = share - LANES
@@ -296,14 +360,18 @@
             name="weights",
         )(own_part, *got, unit_part, inv_part, all_feats, feats_t)
         got_weight = lax.all_to_all(sent_weight, AXES[:2], 0, 0)
-        d_proj = pl.pallas_call(
+        got_weight, got_text = lax.optimization_barrier((got_weight, got_text))
+        d_proj, d_text_unit = pl.pallas_call(
             functools.partial(total_kernel, rest),
-            in_specs=[VMEM],
-            out_specs=VMEM,
-            out_shape=jax.ShapeDtypeStruct((out_rows, 2 * share), F32),
-            compiler_params=limit(4),
-            name="weight_total",
-        )(got_weight)
+            in_specs=[VMEM] * (1 + spread),
+            out_specs=[VMEM] * 2,
+            out_shape=[
+                jax.ShapeDtypeStruct((out_rows, 2 * share), F32),
+                jax.ShapeDtypeStruct((rows, width), F32),
+            ],
+            compiler_params=limit(6),
+            name="totals",
+        )(got_weight, own_text, *got_text)
     else:
 
         def gradient_kernel(*refs):
@@ -325,16 +393,15 @@
         left = lax.axis_index("inner") == 0
         both = jnp.concatenate([jnp.where(left, partial, 0.0), jnp.where(left, 0.0, partial)], axis=1)
         d_proj = lax.psum_scatter(both, AXES[:2], scatter_dimension=0, tiled=True)
-
-    d_text_unit = pl.pallas_call(
-        sum_kernel,
-        in_specs=[VMEM] * 2,
-        out_specs=VMEM,
-        out_shape=jax.ShapeDtypeStruct((rows, width), F32),
-        compiler_params=limit(4),
-        name="caption_total",
-    )(own_text, got_text)
-    image_loss = lax.dynamic_slice_in_dim(loss_line[0], member[0] * rows, rows, 0)
+        d_text_unit = pl.pallas_call(
+            sum_kernel,
+            in_specs=[VMEM] * spread,
+            out_specs=VMEM,
+            out_shape=jax.ShapeDtypeStruct((rows, width), F32),
+            compiler_params=limit(12),
+            name="caption_total",
+        )(own_text, *got_text)
+    image_loss = lax.dynamic_slice_in_dim(loss_line[0], first_image(member[0], rows, group), rows, 0)
     return (image_loss, d_text_unit, d_proj)
 
 

time: 63.4 us -> 59.6 us (0.940)
  blocking collectives: 11.2 us -> 0 us
  waiting for transfers between devices: 15.1 us -> 23.6 us
  starting transfers between devices: 18.7 us -> 22.1 us
  matrix products: 2.65 us -> 0 us
  local copies, waits for them, and re-layouts: 6.32 us -> 4.12 us
    all_gather x1 -> x0, blocking collectives: 11.2 us -> none  [local(): all_feats = lax.all_gather(image_feats, AXES[1:], axis=0, tiled=True)]
    ppermute x9 -> x14, waiting for transfers between devices: 15.1 us -> 23.6 us  [swapped(): lax.ppermute(value, AXES, [(source, source ^ mask) for source in range(to...]
    ppermute x9 -> x14, starting transfers between devices: 13.3 us -> 17.4 us  [swapped(): lax.ppermute(value, AXES, [(source, source ^ mask) for source in range(to...]
    dot_general x1 -> x0, matrix products: 2.65 us -> none  [local(): zproj = jnp.dot(all_feats, proj_weight, preferred_element_type=F32)]
    unnamed x16 -> x6, local copies, waits for them, and re-layouts: 5.74 us -> 3.54 us
    pallas_call x1, Pallas kernels: 0.97 us -> 1.74 us  [local(): pl.pallas_call(functools.partial(weight_kernel, group, wide), in_specs=[V...]
    all_to_all x1, starting transfers between devices: 5.35 us -> 4.69 us  [local(): got_weight = lax.all_to_all(sent_weight, AXES[:2], 0, 0)]
    pallas_call x4 -> x5, Pallas kernels: 4.64 us -> 4.37 us  [the longest x1 2.99 us: local(): pl.pallas_call(functools.partial(pair_kernel, narrow, group), in_specs=[S...]
  transfers between devices with their start and end apart: 10 -> 15, of which waited for: 5 -> 7; matrix products, arithmetic and copies ran while one was open for 5% -> 1% of each run, Pallas kernels for 3% -> 3%
where the time goes in v7:
time: 59.6 us; the launch traced here: 59.3 us
  waiting for transfers between devices  23.6 us (40%)
  starting transfers between devices  22.1 us (37%)
  Pallas kernels  7.45 us (12%)
  local copies, waits for them, and re-layouts  4.12 us (7%)
  between operations  2 us (3%)
    ppermute x14, waiting for transfers between devices, swapped(): lax.ppermute(value, AXES, [(source, source ^ mask) for source in range(to...  23.6 us
    ppermute x14, starting transfers between devices, swapped(): lax.ppermute(value, AXES, [(source, source ^ mask) for source in range(to...  17.4 us
    all_to_all x1, starting transfers between devices, local(): got_weight = lax.all_to_all(sent_weight, AXES[:2], 0, 0)  4.69 us
    unnamed x6, local copies, waits for them, and re-layouts  3.54 us
    pallas_call x1, Pallas kernels, local(): pl.pallas_call(functools.partial(pair_kernel, narrow, group), in_specs=[S...  2.99 us
    pallas_call x1, Pallas kernels, local(): pl.pallas_call(functools.partial(weight_kernel, group, wide), in_specs=[V...  1.74 us
    pallas_call x1, Pallas kernels, local(): pl.pallas_call(functools.partial(caption_kernel, rows), in_specs=[VMEM] *...  1.22 us
  transfers between devices with their start and end apart: 15, of which 7 were waited for; matrix products, arithmetic and copies ran while one was open for 1% of the time, Pallas kernels for 3%

profile of v7, /device:TPU:0, one launch (start us, length us, event | category | flops | bytes accessed | tf_op | source)
XLA Modules:
  0.0 59.3 jit_solution(3874640176198095877)
XLA Ops:
  0.6 3.0 %collective-permute-start = (bf16[48,1152]{1,0:T(8,128)(2,1)}, bf16[48,1152]{1,0:T(8,128)(2,1)S(1)}, u32[]{:S(2)}, u32[]{:S(2)}) collective-permute-start(bf16[48,1152]{1,0:T(8,128)(2,1)} %feats_ref.1), channel_id=1, source_target_pairs={{0,2},{1,3},{2,0},{3,1},{4,6},{5,7},{6,4},{7,5},{8,10},{9,11},{10,... | collective-permute-start | bytes 331784 | tf_op jit(solution)/shard_map/ppermute | solution.py:27
  3.7 3.6 %collective-permute-start.1 = (bf16[48,1152]{1,0:T(8,128)(2,1)}, bf16[48,1152]{1,0:T(8,128)(2,1)S(1)}, u32[]{:S(2)}, u32[]{:S(2)}) collective-permute-start(bf16[48,1152]{1,0:T(8,128)(2,1)} %text_ref.1), channel_id=1, source_target_pairs={{0,24},{1,25},{2,26},{3,27},{4,28},{5,29},{6,30},{7,31},{8,16},{9,... | collective-permute-start | bytes 331784 | tf_op jit(solution)/shard_map/ppermute | solution.py:27
  7.3 1.4 %collective-permute-start.3 = (bf16[48,1152]{1,0:T(8,128)(2,1)}, bf16[48,1152]{1,0:T(8,128)(2,1)S(1)}, u32[]{:S(2)}, u32[]{:S(2)}) collective-permute-start(bf16[48,1152]{1,0:T(8,128)(2,1)} %feats_ref.1), channel_id=1, source_target_pairs={{0,6},{1,7},{2,4},{3,5},{4,2},{5,3},{6,0},{7,1},{8,14},{9,15},{10,... | collective-permute-start | bytes 331784 | tf_op jit(solution)/shard_map/ppermute | solution.py:27
  8.7 0.8 %collective-permute-start.4 = (bf16[48,1152]{1,0:T(8,128)(2,1)}, bf16[48,1152]{1,0:T(8,128)(2,1)S(1)}, u32[]{:S(2)}, u32[]{:S(2)}) collective-permute-start(bf16[48,1152]{1,0:T(8,128)(2,1)} %text_ref.1), channel_id=1, source_target_pairs={{0,8},{1,9},{2,10},{3,11},{4,12},{5,13},{6,14},{7,15},{8,0},{9,1},... | collective-permute-start | bytes 331784 | tf_op jit(solution)/shard_map/ppermute | solution.py:27
  11.1 1.7 %copy-done = bf16[1152,1152]{1,0:T(8,128)(2,1)S(1)} copy-done((bf16[1152,1152]{1,0:T(8,128)(2,1)S(1)}, bf16[1152,1152]{1,0:T(8,128)(2,1)}, u32[]{:S(2)}) %copy-start) | copy-done | bytes 2654232
  12.9 0.9 %copy-done.1 = bf16[48,1152]{1,0:T(8,128)(2,1)S(1)} copy-done((bf16[48,1152]{1,0:T(8,128)(2,1)S(1)}, bf16[48,1152]{1,0:T(8,128)(2,1)}, u32[]{:S(2)}) %copy-start.1) | copy-done | bytes 110616
  13.8 0.9 %copy-done.2 = bf16[48,1152]{1,0:T(8,128)(2,1)S(1)} copy-done((bf16[48,1152]{1,0:T(8,128)(2,1)S(1)}, bf16[48,1152]{1,0:T(8,128)(2,1)}, u32[]{:S(2)}) %copy-start.2) | copy-done | bytes 110616
  14.9 1.6 %collective-permute-done.2.refs_2_ = bf16[48,1152]{1,0:T(8,128)(2,1)S(1)} collective-permute-done((bf16[48,1152]{1,0:T(8,128)(2,1)}, bf16[48,1152]{1,0:T(8,128)(2,1)S(1)}, u32[]{:S(2)}, u32[]{:S(2)}) %collective-permute-start.2) | collective-permute-done | bytes 110624 | tf_op jit(solution)/shard_map/ppermute | solution.py:27
  16.8 1.6 %collective-permute-done.6.got_half = bf16[192,1152]{1,0:T(8,128)(2,1)S(1)} collective-permute-done((bf16[192,1152]{1,0:T(8,128)(2,1)S(1)}, bf16[192,1152]{1,0:T(8,128)(2,1)S(1)}, u32[]{:S(2)}, u32[]{:S(2)}) %collective-permute-start.6) | collective-permute-done | bytes 442400 | tf_op jit(solution)/shard_map/ppermute | solution.py:27
  18.4 3.0 %pairs.1 = (bf16[384,1152]{1,0:T(8,128)(2,1)S(1)}, f32[144,384]{1,0:T(8,128)S(1)}, f32[1,384]{1,0:T(1,128)S(1)}, bf16[1152,384]{1,0:T(8,128)(2,1)S(1)}, bf16[192...) custom-call(s32[1]{0:T(128)} %bitcast.member_ref, ...), custom_call_target="tpu_custom_call" | custom-call | tf_op jit(solution)/shard_map/pairs/pallas_call | solution.py:302
  21.6 1.2 %captions.1 = (bf16[1152,384]{1,0:T(8,128)(2,1)S(1)}, f32[48,1152]{1,0:T(8,128)S(1)}, bf16[48,1152]{1,0:T(8,128)(2,1)S(1)}, bf16[48,1152]{1,0:T(8,128)(2,1)S(1)}, bf16[48,1152]{1,0:T(8,128)(2,1)S(1)}) custom-call(bf16[192,384]{1,0:T(8,128)(2,1)S(1)} %get-tuple-element.54.grad_ref, bf16[1152,384]{1,0:T(8,128)(2,1)S(1)} %get-tuple-element.55.emb_ref, ...), custom_call_target="tpu_custom_call" | custom-call | tf_op jit(solution)/shard_map/captions/pallas_call | solution.py:324
  23.5 1.5 %collective-permute-start.10 = (bf16[160,384]{1,0:T(8,128)(2,1)S(1)}, bf16[160,384]{1,0:T(8,128)(2,1)S(1)}, u32[]{:S(2)}, u32[]{:S(2)}) collective-permute-start(bf16[160,384]{1,0:T(8,128)(2,1)S(1)} %get-tuple-element.65), channel_id=1, source_target_pairs={{0,6},{1,7},{2,4},{3,5},{4,2},{5,3},{6,0},{7,1},{8,14},{9,15},{10,... | collective-permute-start | bytes 368648 | tf_op jit(solution)/shard_map/ppermute | solution.py:27
  25.0 1.5 %collective-permute-start.8 = (bf16[160,384]{1,0:T(8,128)(2,1)S(1)}, bf16[160,384]{1,0:T(8,128)(2,1)S(1)}, u32[]{:S(2)}, u32[]{:S(2)}) collective-permute-start(bf16[160,384]{1,0:T(8,128)(2,1)S(1)} %get-tuple-element.63), channel_id=1, source_target_pairs={{0,2},{1,3},{2,0},{3,1},{4,6},{5,7},{6,4},{7,5},{8,10},{9,11},{10,... | collective-permute-start | bytes 368648 | tf_op jit(solution)/shard_map/ppermute | solution.py:27
  26.5 0.5 collective-permute-start.9
  27.0 3.6 %collective-permute-done.10.refs_3_ = bf16[160,384]{1,0:T(8,128)(2,1)S(1)} collective-permute-done((bf16[160,384]{1,0:T(8,128)(2,1)S(1)}, bf16[160,384]{1,0:T(8,128)(2,1)S(1)}, u32[]{:S(2)}, u32[]{:S(2)}) %collective-permute-start.10) | collective-permute-done | bytes 122912 | tf_op jit(solution)/shard_map/ppermute | solution.py:27
  30.6 1.8 %collective-permute-done.8.refs_1_ = bf16[160,384]{1,0:T(8,128)(2,1)S(1)} collective-permute-done((bf16[160,384]{1,0:T(8,128)(2,1)S(1)}, bf16[160,384]{1,0:T(8,128)(2,1)S(1)}, u32[]{:S(2)}, u32[]{:S(2)}) %collective-permute-start.8) | collective-permute-done | bytes 122912 | tf_op jit(solution)/shard_map/ppermute | solution.py:27
  32.5 1.7 %weights.1 = (f32[1,384]{1,0:T(1,128)S(1)}, bf16[8,176,128]{2,1,0:T(8,128)(2,1)}) custom-call(f32[152,384]{1,0:T(8,128)S(1)} %get-tuple-element.62.refs_0_, bf16[160,384]{1,0:T(8,128)(2,1)S(1)} %collective-permute-done.8.refs_1_, bf16[160,384]{1,0:T(8,128)(2,1)S(1)} %collective-permute-done.9.refs_2_, bf16[160,384]{1,0:T(8,128)(2,1)S(1)} %collective-permute-done.10.refs_3_, ...), custom_call_target="tpu_custom_call" | custom-call | tf_op jit(solution)/shard_map/weights/pallas_call | solution.py:351
  34.2 4.7 %all-to-all-start = ((bf16[8,176,128]{2,1,0:T(8,128)(2,1)}), bf16[8,176,128]{2,1,0:T(8,128)(2,1)S(1)}, u32[]{:S(2)}, u32[]{:S(2)}) async-start(bf16[8,176,128]{2,1,0:T(8,128)(2,1)} %get-tuple-element.70), calls=%async_computation | async-start | bytes 720896 | tf_op jit(solution)/shard_map/all_to_all | solution.py:362
  38.9 2.0 %collective-permute-start.11 = (bf16[48,1152]{1,0:T(8,128)(2,1)S(1)}, bf16[48,1152]{1,0:T(8,128)(2,1)S(1)}, u32[]{:S(2)}, u32[]{:S(2)}) collective-permute-start(bf16[48,1152]{1,0:T(8,128)(2,1)S(1)} %get-tuple-element.71), channel_id=1, source_target_pairs={{0,8},{1,9},{2,10},{3,11},{4,12},{5,13},{6,14},{7,15},{8,0},{9,1},... | collective-permute-start | bytes 331784 | tf_op jit(solution)/shard_map/ppermute | solution.py:27
  40.9 2.4 %collective-permute-start.12 = (bf16[48,1152]{1,0:T(8,128)(2,1)S(1)}, bf16[48,1152]{1,0:T(8,128)(2,1)S(1)}, u32[]{:S(2)}, u32[]{:S(2)}) collective-permute-start(bf16[48,1152]{1,0:T(8,128)(2,1)S(1)} %get-tuple-element.72), channel_id=1, source_target_pairs={{0,16},{1,17},{2,18},{3,19},{4,20},{5,21},{6,22},{7,23},{8,24},{9,... | collective-permute-start | bytes 331784 | tf_op jit(solution)/shard_map/ppermute | solution.py:27
  43.3 0.6 dynamic-slice_bitcast_fusion
  43.9 5.5 %collective-permute-done.11.refs_2_ = bf16[48,1152]{1,0:T(8,128)(2,1)S(1)} collective-permute-done((bf16[48,1152]{1,0:T(8,128)(2,1)S(1)}, bf16[48,1152]{1,0:T(8,128)(2,1)S(1)}, u32[]{:S(2)}, u32[]{:S(2)}) %collective-permute-start.11) | collective-permute-done | bytes 110624 | tf_op jit(solution)/shard_map/ppermute | solution.py:27
  49.4 8.9 %collective-permute-done.12.refs_3_ = bf16[48,1152]{1,0:T(8,128)(2,1)S(1)} collective-permute-done((bf16[48,1152]{1,0:T(8,128)(2,1)S(1)}, bf16[48,1152]{1,0:T(8,128)(2,1)S(1)}, u32[]{:S(2)}, u32[]{:S(2)}) %collective-permute-start.12) | collective-permute-done | bytes 110624 | tf_op jit(solution)/shard_map/ppermute | solution.py:27
  58.3 0.9 %totals.1 = (f32[144,288]{1,0:T(8,128)}, f32[48,1152]{1,0:T(8,128)}) custom-call(bf16[8,176,128]{2,1,0:T(8,128)(2,1)S(1)} %all-to-all-done.refs_0_, f32[48,1152]{1,0:T(8,128)S(1)} %get-tuple-element.75.refs_1_, bf16[48,1152]{1,0:T(8,128)(2,1)S(1)} %collective-permute-done.11.refs_2_, bf16[48,1152]{1,0:T(8,128)(2,1)S(1)} %collective-permute-done.12.refs_3_, ...), custom_call_target="tpu_custom_call" | custom-call | tf_op jit(solution)/shard_map/totals/pallas_call | solution.py:364
  (21 shorter events, 1.7 us)
Async XLA Ops:
  0.6 8.9 %collective-permute-start = (bf16[48,1152]{1,0:T(8,128)(2,1)}, bf16[48,1152]{1,0:T(8,128)(2,1)S(1)}, u32[]{:S(2)}, u32[]{:S(2)}) collective-permute-start(bf16[48,1152]{1,0:T(8,128)(2,1)} %feats_ref.1), channel_id=1, source_target_pairs={{0,2},{1,3},{2,0},{3,1},{4,6},{5,7},{6,4},{7,5},{8,10},{9,11},{10,... | collective-permute-start | bytes 331784 | tf_op jit(solution)/shard_map/ppermute | solution.py:27
  3.7 11.2 %collective-permute-start.1 = (bf16[48,1152]{1,0:T(8,128)(2,1)}, bf16[48,1152]{1,0:T(8,128)(2,1)S(1)}, u32[]{:S(2)}, u32[]{:S(2)}) collective-permute-start(bf16[48,1152]{1,0:T(8,128)(2,1)} %text_ref.1), channel_id=1, source_target_pairs={{0,24},{1,25},{2,26},{3,27},{4,28},{5,29},{6,30},{7,31},{8,16},{9,... | collective-permute-start | bytes 331784 | tf_op jit(solution)/shard_map/ppermute | solution.py:27
  7.3 9.2 %collective-permute-start.2 = (bf16[48,1152]{1,0:T(8,128)(2,1)}, bf16[48,1152]{1,0:T(8,128)(2,1)S(1)}, u32[]{:S(2)}, u32[]{:S(2)}) collective-permute-start(bf16[48,1152]{1,0:T(8,128)(2,1)} %text_ref.1), channel_id=1, source_target_pairs={{0,16},{1,17},{2,18},{3,19},{4,20},{5,21},{6,22},{7,23},{8,24},{9,... | collective-permute-start | bytes 331784 | tf_op jit(solution)/shard_map/ppermute | solution.py:27
  7.3 9.2 %collective-permute-start.3 = (bf16[48,1152]{1,0:T(8,128)(2,1)}, bf16[48,1152]{1,0:T(8,128)(2,1)S(1)}, u32[]{:S(2)}, u32[]{:S(2)}) collective-permute-start(bf16[48,1152]{1,0:T(8,128)(2,1)} %feats_ref.1), channel_id=1, source_target_pairs={{0,6},{1,7},{2,4},{3,5},{4,2},{5,3},{6,0},{7,1},{8,14},{9,15},{10,... | collective-permute-start | bytes 331784 | tf_op jit(solution)/shard_map/ppermute | solution.py:27
  8.7 7.8 %collective-permute-start.4 = (bf16[48,1152]{1,0:T(8,128)(2,1)}, bf16[48,1152]{1,0:T(8,128)(2,1)S(1)}, u32[]{:S(2)}, u32[]{:S(2)}) collective-permute-start(bf16[48,1152]{1,0:T(8,128)(2,1)} %text_ref.1), channel_id=1, source_target_pairs={{0,8},{1,9},{2,10},{3,11},{4,12},{5,13},{6,14},{7,15},{8,0},{9,1},... | collective-permute-start | bytes 331784 | tf_op jit(solution)/shard_map/ppermute | solution.py:27
  9.5 7.0 %collective-permute-start.5 = (bf16[48,1152]{1,0:T(8,128)(2,1)}, bf16[48,1152]{1,0:T(8,128)(2,1)S(1)}, u32[]{:S(2)}, u32[]{:S(2)}) collective-permute-start(bf16[48,1152]{1,0:T(8,128)(2,1)} %feats_ref.1), channel_id=1, source_target_pairs={{0,4},{1,5},{2,6},{3,7},{4,0},{5,1},{6,2},{7,3},{8,12},{9,13},{10,... | collective-permute-start | bytes 331784 | tf_op jit(solution)/shard_map/ppermute | solution.py:27
  11.1 1.8 %copy-start = (bf16[1152,1152]{1,0:T(8,128)(2,1)S(1)}, bf16[1152,1152]{1,0:T(8,128)(2,1)}, u32[]{:S(2)}) copy-start(bf16[1152,1152]{1,0:T(8,128)(2,1)} %weight_ref.1) | copy-start | bytes 7962628
  12.9 0.9 %copy-start.1 = (bf16[48,1152]{1,0:T(8,128)(2,1)S(1)}, bf16[48,1152]{1,0:T(8,128)(2,1)}, u32[]{:S(2)}) copy-start(bf16[48,1152]{1,0:T(8,128)(2,1)} %text_ref.1) | copy-start | bytes 331780
  13.8 0.9 %copy-start.2 = (bf16[48,1152]{1,0:T(8,128)(2,1)S(1)}, bf16[48,1152]{1,0:T(8,128)(2,1)}, u32[]{:S(2)}) copy-start(bf16[48,1152]{1,0:T(8,128)(2,1)} %feats_ref.1) | copy-start | bytes 331780
  16.6 1.9 %collective-permute-start.6 = (bf16[192,1152]{1,0:T(8,128)(2,1)S(1)}, bf16[192,1152]{1,0:T(8,128)(2,1)S(1)}, u32[]{:S(2)}, u32[]{:S(2)}) collective-permute-start(bf16[192,1152]{1,0:T(8,128)(2,1)S(1)} %stack.1.own_half), channel_id=1, source_target_pairs={{0,1},{1,0},{2,3},{3,2},{4,5},{5,4},{6,7},{7,6},{8,9},{9,8},{10,11... | collective-permute-start | bytes 1327112 | tf_op jit(solution)/shard_map/ppermute | solution.py:27
  21.4 1.9 %collective-permute-start.7 = (bf16[4,160,384]{2,1,0:T(8,128)(2,1)S(1)}, bf16[4,160,384]{2,1,0:T(8,128)(2,1)S(1)}, u32[]{:S(2)}, u32[]{:S(2)}) collective-permute-start(bf16[4,160,384]{2,1,0:T(8,128)(2,1)S(1)} %get-tuple-element.53), channel_id=1, source_target_pairs={{0,1},{1,0},{2,3},{3,2},{4,5},{5,4},{6,7},{7,6},{8,9},{9,8},{10,11... | collective-permute-start | bytes 1474568 | tf_op jit(solution)/shard_map/ppermute | solution.py:27
  23.5 7.1 %collective-permute-start.10 = (bf16[160,384]{1,0:T(8,128)(2,1)S(1)}, bf16[160,384]{1,0:T(8,128)(2,1)S(1)}, u32[]{:S(2)}, u32[]{:S(2)}) collective-permute-start(bf16[160,384]{1,0:T(8,128)(2,1)S(1)} %get-tuple-element.65), channel_id=1, source_target_pairs={{0,6},{1,7},{2,4},{3,5},{4,2},{5,3},{6,0},{7,1},{8,14},{9,15},{10,... | collective-permute-start | bytes 368648 | tf_op jit(solution)/shard_map/ppermute | solution.py:27
  25.0 7.5 %collective-permute-start.8 = (bf16[160,384]{1,0:T(8,128)(2,1)S(1)}, bf16[160,384]{1,0:T(8,128)(2,1)S(1)}, u32[]{:S(2)}, u32[]{:S(2)}) collective-permute-start(bf16[160,384]{1,0:T(8,128)(2,1)S(1)} %get-tuple-element.63), channel_id=1, source_target_pairs={{0,2},{1,3},{2,0},{3,1},{4,6},{5,7},{6,4},{7,5},{8,10},{9,11},{10,... | collective-permute-start | bytes 368648 | tf_op jit(solution)/shard_map/ppermute | solution.py:27
  26.5 5.9 %collective-permute-start.9 = (bf16[160,384]{1,0:T(8,128)(2,1)S(1)}, bf16[160,384]{1,0:T(8,128)(2,1)S(1)}, u32[]{:S(2)}, u32[]{:S(2)}) collective-permute-start(bf16[160,384]{1,0:T(8,128)(2,1)S(1)} %get-tuple-element.64), channel_id=1, source_target_pairs={{0,4},{1,5},{2,6},{3,7},{4,0},{5,1},{6,2},{7,3},{8,12},{9,13},{10,... | collective-permute-start | bytes 368648 | tf_op jit(solution)/shard_map/ppermute | solution.py:27
  34.2 24.2 %all-to-all-start = ((bf16[8,176,128]{2,1,0:T(8,128)(2,1)}), bf16[8,176,128]{2,1,0:T(8,128)(2,1)S(1)}, u32[]{:S(2)}, u32[]{:S(2)}) async-start(bf16[8,176,128]{2,1,0:T(8,128)(2,1)} %get-tuple-element.70), calls=%async_computation | async-start | bytes 720896 | tf_op jit(solution)/shard_map/all_to_all | solution.py:362
  38.9 10.5 %collective-permute-start.11 = (bf16[48,1152]{1,0:T(8,128)(2,1)S(1)}, bf16[48,1152]{1,0:T(8,128)(2,1)S(1)}, u32[]{:S(2)}, u32[]{:S(2)}) collective-permute-start(bf16[48,1152]{1,0:T(8,128)(2,1)S(1)} %get-tuple-element.71), channel_id=1, source_target_pairs={{0,8},{1,9},{2,10},{3,11},{4,12},{5,13},{6,14},{7,15},{8,0},{9,1},... | collective-permute-start | bytes 331784 | tf_op jit(solution)/shard_map/ppermute | solution.py:27
  40.9 17.4 %collective-permute-start.12 = (bf16[48,1152]{1,0:T(8,128)(2,1)S(1)}, bf16[48,1152]{1,0:T(8,128)(2,1)S(1)}, u32[]{:S(2)}, u32[]{:S(2)}) collective-permute-start(bf16[48,1152]{1,0:T(8,128)(2,1)S(1)} %get-tuple-element.72), channel_id=1, source_target_pairs={{0,16},{1,17},{2,18},{3,19},{4,20},{5,21},{6,22},{7,23},{8,24},{9,... | collective-permute-start | bytes 331784 | tf_op jit(solution)/shard_map/ppermute | solution.py:27
  43.3 15.1 %collective-permute-start.13 = (bf16[48,1152]{1,0:T(8,128)(2,1)S(1)}, bf16[48,1152]{1,0:T(8,128)(2,1)S(1)}, u32[]{:S(2)}, u32[]{:S(2)}) collective-permute-start(bf16[48,1152]{1,0:T(8,128)(2,1)S(1)} %get-tuple-element.73), channel_id=1, source_target_pairs={{0,24},{1,25},{2,26},{3,27},{4,28},{5,29},{6,30},{7,31},{8,16},{9,... | collective-permute-start | bytes 331784 | tf_op jit(solution)/shard_map/ppermute | solution.py:27

commit v8 on v7

--- a/solution.py
+++ b/solution.py
@@ -229,16 +229,7 @@
         send_out[place, rows + rest :, : rows - LANES] = tail[:, begin + LANES : begin + rows]
 
 
-def total_text(refs, out):
-    total = refs[0][...]
-    for block in refs[1:]:
-        total = total + block[...].astype(F32)
-    out[...] = total
-
-
-def total_kernel(rest, *refs):
-    got_ref, out, text_out = refs[0], refs[-2], refs[-1]
-    total_text(refs[1:-2], text_out)
+def total_kernel(rest, got_ref, out):
     rows = out.shape[0]
     for side in range(2):
         half = got_ref[side].astype(F32)
@@ -251,7 +242,10 @@
 
 
 def sum_kernel(*refs):
-    total_text(refs[:-1], refs[-1])
+    total = refs[0][...]
+    for block in refs[1:-1]:
+        total = total + block[...].astype(F32)
+    refs[-1][...] = total
 
 
 def local(wide, narrow, image_feats, proj_weight, text_embed, log_scale, logit_bias):
@@ -359,19 +353,18 @@
             compiler_params=limit(12),
             name="weights",
         )(own_part, *got, unit_part, inv_part, all_feats, feats_t)
+        order = [*got_text[1:], got_text[0]]
+        sent_weight, *order = lax.optimization_barrier((sent_weight, *order))
+        got_text = [order[-1], *order[:-1]]
         got_weight = lax.all_to_all(sent_weight, AXES[:2], 0, 0)
-        got_weight, got_text = lax.optimization_barrier((got_weight, got_text))
-        d_proj, d_text_unit = pl.pallas_call(
+        d_proj = pl.pallas_call(
             functools.partial(total_kernel, rest),
-            in_specs=[VMEM] * (1 + spread),
-            out_specs=[VMEM] * 2,
-            out_shape=[
-                jax.ShapeDtypeStruct((out_rows, 2 * share), F32),
-                jax.ShapeDtypeStruct((rows, width), F32),
-            ],
-            compiler_params=limit(6),
-            name="totals",
-        )(got_weight, own_text, *got_text)
+            in_specs=[VMEM],
+            out_specs=VMEM,
+            out_shape=jax.ShapeDtypeStruct((out_rows, 2 * share), F32),
+            compiler_params=limit(4),
+            name="weight_total",
+        )(got_weight)
     else:
 
         def gradient_kernel(*refs):
@@ -393,14 +386,15 @@
         left = lax.axis_index("inner") == 0
         both = jnp.concatenate([jnp.where(left, partial, 0.0), jnp.where(left, 0.0, partial)], axis=1)
         d_proj = lax.psum_scatter(both, AXES[:2], scatter_dimension=0, tiled=True)
-        d_text_unit = pl.pallas_call(
-            sum_kernel,
-            in_specs=[VMEM] * spread,
-            out_specs=VMEM,
-            out_shape=jax.ShapeDtypeStruct((rows, width), F32),
-            compiler_params=limit(12),
-            name="caption_total",
-        )(own_text, *got_text)
+
+    d_text_unit = pl.pallas_call(
+        sum_kernel,
+        in_specs=[VMEM] * spread,
+        out_specs=VMEM,
+        out_shape=jax.ShapeDtypeStruct((rows, width), F32),
+        compiler_params=limit(12),
+        name="caption_total",
+    )(own_text, *got_text)
     image_loss = lax.dynamic_slice_in_dim(loss_line[0], first_image(member[0], rows, group), rows, 0)
     return (image_loss, d_text_unit, d_proj)
 

time: 59.6 us -> 54.1 us (0.908)
  waiting for transfers between devices: 23.6 us -> 19.7 us
  starting transfers between devices: 22.1 us -> 19.9 us
  Pallas kernels: 7.45 us -> 8.1 us
    ppermute x14, waiting for transfers between devices: 23.6 us -> 10.6 us  [swapped(): lax.ppermute(value, AXES, [(source, source ^ mask) for source in range(to...]
    all_to_all x1, waiting for transfers between devices: 0.01 us -> 9.1 us  [local(): got_weight = lax.all_to_all(sent_weight, AXES[:2], 0, 0)]
    ppermute x14, starting transfers between devices: 17.4 us -> 15.6 us  [swapped(): lax.ppermute(value, AXES, [(source, source ^ mask) for source in range(to...]
    pallas_call x1 -> x2, Pallas kernels: 0.95 us -> 1.61 us  [the longest x1 0.86 us: local(): pl.pallas_call(functools.partial(total_kernel, rest), in_specs=[VMEM], ou...]
  transfers between devices with their start and end apart: 15 -> 15, of which waited for: 7 -> 8; matrix products, arithmetic and copies ran while one was open for 1% -> 1% of each run, Pallas kernels for 3% -> 8%
where the time goes in v8:
time: 54.1 us; the launch traced here: 53.8 us
  starting transfers between devices  19.9 us (37%)
  waiting for transfers between devices  19.7 us (36%)
  Pallas kernels  8.1 us (15%)
  local copies, waits for them, and re-layouts  4.12 us (8%)
  between operations  2 us (4%)
    ppermute x14, starting transfers between devices, swapped(): lax.ppermute(value, AXES, [(source, source ^ mask) for source in range(to...  15.6 us
    ppermute x14, waiting for transfers between devices, swapped(): lax.ppermute(value, AXES, [(source, source ^ mask) for source in range(to...  10.6 us
    all_to_all x1, waiting for transfers between devices, local(): got_weight = lax.all_to_all(sent_weight, AXES[:2], 0, 0)  9.1 us
    all_to_all x1, starting transfers between devices, local(): got_weight = lax.all_to_all(sent_weight, AXES[:2], 0, 0)  4.26 us
    unnamed x6, local copies, waits for them, and re-layouts  3.54 us
    pallas_call x1, Pallas kernels, local(): pl.pallas_call(functools.partial(pair_kernel, narrow, group), in_specs=[S...  2.99 us
    pallas_call x1, Pallas kernels, local(): pl.pallas_call(functools.partial(weight_kernel, group, wide), in_specs=[V...  1.73 us
    pallas_call x1, Pallas kernels, local(): pl.pallas_call(functools.partial(caption_kernel, rows), in_specs=[VMEM] *...  1.22 us
  transfers between devices with their start and end apart: 15, of which 8 were waited for; matrix products, arithmetic and copies ran while one was open for 1% of the time, Pallas kernels for 8%

profile of v8, /device:TPU:0, one launch (start us, length us, event | category | flops | bytes accessed | tf_op | source)
XLA Modules:
  0.0 53.8 jit_solution(5751476839233238742)
XLA Ops:
  0.6 3.0 %collective-permute-start = (bf16[48,1152]{1,0:T(8,128)(2,1)}, bf16[48,1152]{1,0:T(8,128)(2,1)S(1)}, u32[]{:S(2)}, u32[]{:S(2)}) collective-permute-start(bf16[48,1152]{1,0:T(8,128)(2,1)} %feats_ref.1), channel_id=1, source_target_pairs={{0,2},{1,3},{2,0},{3,1},{4,6},{5,7},{6,4},{7,5},{8,10},{9,11},{10,... | collective-permute-start | bytes 331784 | tf_op jit(solution)/shard_map/ppermute | solution.py:27
  3.7 3.6 %collective-permute-start.1 = (bf16[48,1152]{1,0:T(8,128)(2,1)}, bf16[48,1152]{1,0:T(8,128)(2,1)S(1)}, u32[]{:S(2)}, u32[]{:S(2)}) collective-permute-start(bf16[48,1152]{1,0:T(8,128)(2,1)} %text_ref.1), channel_id=1, source_target_pairs={{0,24},{1,25},{2,26},{3,27},{4,28},{5,29},{6,30},{7,31},{8,16},{9,... | collective-permute-start | bytes 331784 | tf_op jit(solution)/shard_map/ppermute | solution.py:27
  7.3 1.4 %collective-permute-start.3 = (bf16[48,1152]{1,0:T(8,128)(2,1)}, bf16[48,1152]{1,0:T(8,128)(2,1)S(1)}, u32[]{:S(2)}, u32[]{:S(2)}) collective-permute-start(bf16[48,1152]{1,0:T(8,128)(2,1)} %feats_ref.1), channel_id=1, source_target_pairs={{0,6},{1,7},{2,4},{3,5},{4,2},{5,3},{6,0},{7,1},{8,14},{9,15},{10,... | collective-permute-start | bytes 331784 | tf_op jit(solution)/shard_map/ppermute | solution.py:27
  8.7 0.8 %collective-permute-start.4 = (bf16[48,1152]{1,0:T(8,128)(2,1)}, bf16[48,1152]{1,0:T(8,128)(2,1)S(1)}, u32[]{:S(2)}, u32[]{:S(2)}) collective-permute-start(bf16[48,1152]{1,0:T(8,128)(2,1)} %text_ref.1), channel_id=1, source_target_pairs={{0,8},{1,9},{2,10},{3,11},{4,12},{5,13},{6,14},{7,15},{8,0},{9,1},... | collective-permute-start | bytes 331784 | tf_op jit(solution)/shard_map/ppermute | solution.py:27
  11.1 1.7 %copy-done = bf16[1152,1152]{1,0:T(8,128)(2,1)S(1)} copy-done((bf16[1152,1152]{1,0:T(8,128)(2,1)S(1)}, bf16[1152,1152]{1,0:T(8,128)(2,1)}, u32[]{:S(2)}) %copy-start) | copy-done | bytes 2654232
  12.9 0.9 %copy-done.1 = bf16[48,1152]{1,0:T(8,128)(2,1)S(1)} copy-done((bf16[48,1152]{1,0:T(8,128)(2,1)S(1)}, bf16[48,1152]{1,0:T(8,128)(2,1)}, u32[]{:S(2)}) %copy-start.1) | copy-done | bytes 110616
  13.8 0.9 %copy-done.2 = bf16[48,1152]{1,0:T(8,128)(2,1)S(1)} copy-done((bf16[48,1152]{1,0:T(8,128)(2,1)S(1)}, bf16[48,1152]{1,0:T(8,128)(2,1)}, u32[]{:S(2)}) %copy-start.2) | copy-done | bytes 110616
  14.9 1.6 %collective-permute-done.2.refs_2_ = bf16[48,1152]{1,0:T(8,128)(2,1)S(1)} collective-permute-done((bf16[48,1152]{1,0:T(8,128)(2,1)}, bf16[48,1152]{1,0:T(8,128)(2,1)S(1)}, u32[]{:S(2)}, u32[]{:S(2)}) %collective-permute-start.2) | collective-permute-done | bytes 110624 | tf_op jit(solution)/shard_map/ppermute | solution.py:27
  16.8 1.6 %collective-permute-done.6.got_half = bf16[192,1152]{1,0:T(8,128)(2,1)S(1)} collective-permute-done((bf16[192,1152]{1,0:T(8,128)(2,1)S(1)}, bf16[192,1152]{1,0:T(8,128)(2,1)S(1)}, u32[]{:S(2)}, u32[]{:S(2)}) %collective-permute-start.6) | collective-permute-done | bytes 442400 | tf_op jit(solution)/shard_map/ppermute | solution.py:27
  18.4 3.0 %pairs.1 = (bf16[384,1152]{1,0:T(8,128)(2,1)S(1)}, f32[144,384]{1,0:T(8,128)S(1)}, f32[1,384]{1,0:T(1,128)S(1)}, bf16[1152,384]{1,0:T(8,128)(2,1)S(1)}, bf16[192...) custom-call(s32[1]{0:T(128)} %bitcast.member_ref, ...), custom_call_target="tpu_custom_call" | custom-call | tf_op jit(solution)/shard_map/pairs/pallas_call | solution.py:296
  21.6 1.2 %captions.1 = (bf16[1152,384]{1,0:T(8,128)(2,1)S(1)}, f32[48,1152]{1,0:T(8,128)S(1)}, bf16[48,1152]{1,0:T(8,128)(2,1)S(1)}, bf16[48,1152]{1,0:T(8,128)(2,1)S(1)}, bf16[48,1152]{1,0:T(8,128)(2,1)S(1)}) custom-call(bf16[192,384]{1,0:T(8,128)(2,1)S(1)} %get-tuple-element.52.grad_ref, bf16[1152,384]{1,0:T(8,128)(2,1)S(1)} %get-tuple-element.53.emb_ref, ...), custom_call_target="tpu_custom_call" | custom-call | tf_op jit(solution)/shard_map/captions/pallas_call | solution.py:318
  23.5 1.5 %collective-permute-start.10 = (bf16[160,384]{1,0:T(8,128)(2,1)S(1)}, bf16[160,384]{1,0:T(8,128)(2,1)S(1)}, u32[]{:S(2)}, u32[]{:S(2)}) collective-permute-start(bf16[160,384]{1,0:T(8,128)(2,1)S(1)} %get-tuple-element.63), channel_id=1, source_target_pairs={{0,6},{1,7},{2,4},{3,5},{4,2},{5,3},{6,0},{7,1},{8,14},{9,15},{10,... | collective-permute-start | bytes 368648 | tf_op jit(solution)/shard_map/ppermute | solution.py:27
  25.0 1.5 %collective-permute-start.8 = (bf16[160,384]{1,0:T(8,128)(2,1)S(1)}, bf16[160,384]{1,0:T(8,128)(2,1)S(1)}, u32[]{:S(2)}, u32[]{:S(2)}) collective-permute-start(bf16[160,384]{1,0:T(8,128)(2,1)S(1)} %get-tuple-element.61), channel_id=1, source_target_pairs={{0,2},{1,3},{2,0},{3,1},{4,6},{5,7},{6,4},{7,5},{8,10},{9,11},{10,... | collective-permute-start | bytes 368648 | tf_op jit(solution)/shard_map/ppermute | solution.py:27
  27.0 0.7 %collective-permute-start.11 = (bf16[48,1152]{1,0:T(8,128)(2,1)S(1)}, bf16[48,1152]{1,0:T(8,128)(2,1)S(1)}, u32[]{:S(2)}, u32[]{:S(2)}) collective-permute-start(bf16[48,1152]{1,0:T(8,128)(2,1)S(1)} %get-tuple-element.70), channel_id=1, source_target_pairs={{0,16},{1,17},{2,18},{3,19},{4,20},{5,21},{6,22},{7,23},{8,24},{9,... | collective-permute-start | bytes 331784 | tf_op jit(solution)/shard_map/ppermute | solution.py:27
  27.8 1.9 %collective-permute-start.12 = (bf16[48,1152]{1,0:T(8,128)(2,1)S(1)}, bf16[48,1152]{1,0:T(8,128)(2,1)S(1)}, u32[]{:S(2)}, u32[]{:S(2)}) collective-permute-start(bf16[48,1152]{1,0:T(8,128)(2,1)S(1)} %get-tuple-element.71), channel_id=1, source_target_pairs={{0,24},{1,25},{2,26},{3,27},{4,28},{5,29},{6,30},{7,31},{8,16},{9,... | collective-permute-start | bytes 331784 | tf_op jit(solution)/shard_map/ppermute | solution.py:27
  29.7 1.0 %collective-permute-done.10.refs_3_ = bf16[160,384]{1,0:T(8,128)(2,1)S(1)} collective-permute-done((bf16[160,384]{1,0:T(8,128)(2,1)S(1)}, bf16[160,384]{1,0:T(8,128)(2,1)S(1)}, u32[]{:S(2)}, u32[]{:S(2)}) %collective-permute-start.10) | collective-permute-done | bytes 122912 | tf_op jit(solution)/shard_map/ppermute | solution.py:27
  30.6 1.8 %collective-permute-done.8.refs_1_ = bf16[160,384]{1,0:T(8,128)(2,1)S(1)} collective-permute-done((bf16[160,384]{1,0:T(8,128)(2,1)S(1)}, bf16[160,384]{1,0:T(8,128)(2,1)S(1)}, u32[]{:S(2)}, u32[]{:S(2)}) %collective-permute-start.8) | collective-permute-done | bytes 122912 | tf_op jit(solution)/shard_map/ppermute | solution.py:27
  32.5 1.7 %weights.1 = (f32[1,384]{1,0:T(1,128)S(1)}, bf16[8,176,128]{2,1,0:T(8,128)(2,1)}) custom-call(f32[152,384]{1,0:T(8,128)S(1)} %get-tuple-element.60.refs_0_, bf16[160,384]{1,0:T(8,128)(2,1)S(1)} %collective-permute-done.8.refs_1_, bf16[160,384]{1,0:T(8,128)(2,1)S(1)} %collective-permute-done.9.refs_2_, bf16[160,384]{1,0:T(8,128)(2,1)S(1)} %collective-permute-done.10.refs_3_, ...), custom_call_target="tpu_custom_call" | custom-call | tf_op jit(solution)/shard_map/weights/pallas_call | solution.py:345
  34.2 3.0 %collective-permute-done.11.refs_2_ = bf16[48,1152]{1,0:T(8,128)(2,1)S(1)} collective-permute-done((bf16[48,1152]{1,0:T(8,128)(2,1)S(1)}, bf16[48,1152]{1,0:T(8,128)(2,1)S(1)}, u32[]{:S(2)}, u32[]{:S(2)}) %collective-permute-start.11) | collective-permute-done | bytes 110624 | tf_op jit(solution)/shard_map/ppermute | solution.py:27
  37.2 1.1 %collective-permute-done.13.refs_1_ = bf16[48,1152]{1,0:T(8,128)(2,1)S(1)} collective-permute-done((bf16[48,1152]{1,0:T(8,128)(2,1)S(1)}, bf16[48,1152]{1,0:T(8,128)(2,1)S(1)}, u32[]{:S(2)}, u32[]{:S(2)}) %collective-permute-start.13) | collective-permute-done | bytes 110624 | tf_op jit(solution)/shard_map/ppermute | solution.py:27
  38.2 4.3 %all-to-all-start = ((bf16[8,176,128]{2,1,0:T(8,128)(2,1)}), bf16[8,176,128]{2,1,0:T(8,128)(2,1)S(1)}, u32[]{:S(2)}, u32[]{:S(2)}) async-start(bf16[8,176,128]{2,1,0:T(8,128)(2,1)} %get-tuple-element.76), calls=%async_computation | async-start | bytes 720896 | tf_op jit(solution)/shard_map/all_to_all | solution.py:359
  42.5 0.7 %caption_total.1 = f32[48,1152]{1,0:T(8,128)} custom-call(f32[48,1152]{1,0:T(8,128)S(1)} %get-tuple-element.68.refs_0_, bf16[48,1152]{1,0:T(8,128)(2,1)S(1)} %collective-permute-done.13.refs_1_, bf16[48,1152]{1,0:T(8,128)(2,1)S(1)} %collective-permute-done.11.refs_2_, bf16[48,1152]{1,0:T(8,128)(2,1)S(1)} %collective-permute-done.12.refs_3_), custom_call_target="tpu_custom_call" | custom-call | tf_op jit(solution)/shard_map/caption_total/pallas_call | solution.py:390
  43.8 9.1 %all-to-all-done.got_ref = bf16[8,176,128]{2,1,0:T(8,128)(2,1)S(1)} async-done(((bf16[8,176,128]{2,1,0:T(8,128)(2,1)}), bf16[8,176,128]{2,1,0:T(8,128)(2,1)S(1)}, u32[]{:S(2)}, u32[]{:S(2)}) %all-to-all-start) | async-done | bytes 360480 | tf_op jit(solution)/shard_map/all_to_all | solution.py:359
  52.9 0.9 %weight_total.1 = f32[144,288]{1,0:T(8,128)} custom-call(bf16[8,176,128]{2,1,0:T(8,128)(2,1)S(1)} %all-to-all-done.got_ref), custom_call_target="tpu_custom_call" | custom-call | tf_op jit(solution)/shard_map/weight_total/pallas_call | solution.py:360
  (22 shorter events, 2.8 us)
Async XLA Ops:
  0.6 8.9 %collective-permute-start = (bf16[48,1152]{1,0:T(8,128)(2,1)}, bf16[48,1152]{1,0:T(8,128)(2,1)S(1)}, u32[]{:S(2)}, u32[]{:S(2)}) collective-permute-start(bf16[48,1152]{1,0:T(8,128)(2,1)} %feats_ref.1), channel_id=1, source_target_pairs={{0,2},{1,3},{2,0},{3,1},{4,6},{5,7},{6,4},{7,5},{8,10},{9,11},{10,... | collective-permute-start | bytes 331784 | tf_op jit(solution)/shard_map/ppermute | solution.py:27
  3.7 11.2 %collective-permute-start.1 = (bf16[48,1152]{1,0:T(8,128)(2,1)}, bf16[48,1152]{1,0:T(8,128)(2,1)S(1)}, u32[]{:S(2)}, u32[]{:S(2)}) collective-permute-start(bf16[48,1152]{1,0:T(8,128)(2,1)} %text_ref.1), channel_id=1, source_target_pairs={{0,24},{1,25},{2,26},{3,27},{4,28},{5,29},{6,30},{7,31},{8,16},{9,... | collective-permute-start | bytes 331784 | tf_op jit(solution)/shard_map/ppermute | solution.py:27
  7.3 9.2 %collective-permute-start.2 = (bf16[48,1152]{1,0:T(8,128)(2,1)}, bf16[48,1152]{1,0:T(8,128)(2,1)S(1)}, u32[]{:S(2)}, u32[]{:S(2)}) collective-permute-start(bf16[48,1152]{1,0:T(8,128)(2,1)} %text_ref.1), channel_id=1, source_target_pairs={{0,16},{1,17},{2,18},{3,19},{4,20},{5,21},{6,22},{7,23},{8,24},{9,... | collective-permute-start | bytes 331784 | tf_op jit(solution)/shard_map/ppermute | solution.py:27
  7.3 9.2 %collective-permute-start.3 = (bf16[48,1152]{1,0:T(8,128)(2,1)}, bf16[48,1152]{1,0:T(8,128)(2,1)S(1)}, u32[]{:S(2)}, u32[]{:S(2)}) collective-permute-start(bf16[48,1152]{1,0:T(8,128)(2,1)} %feats_ref.1), channel_id=1, source_target_pairs={{0,6},{1,7},{2,4},{3,5},{4,2},{5,3},{6,0},{7,1},{8,14},{9,15},{10,... | collective-permute-start | bytes 331784 | tf_op jit(solution)/shard_map/ppermute | solution.py:27
  8.7 7.8 %collective-permute-start.4 = (bf16[48,1152]{1,0:T(8,128)(2,1)}, bf16[48,1152]{1,0:T(8,128)(2,1)S(1)}, u32[]{:S(2)}, u32[]{:S(2)}) collective-permute-start(bf16[48,1152]{1,0:T(8,128)(2,1)} %text_ref.1), channel_id=1, source_target_pairs={{0,8},{1,9},{2,10},{3,11},{4,12},{5,13},{6,14},{7,15},{8,0},{9,1},... | collective-permute-start | bytes 331784 | tf_op jit(solution)/shard_map/ppermute | solution.py:27
  9.5 7.0 %collective-permute-start.5 = (bf16[48,1152]{1,0:T(8,128)(2,1)}, bf16[48,1152]{1,0:T(8,128)(2,1)S(1)}, u32[]{:S(2)}, u32[]{:S(2)}) collective-permute-start(bf16[48,1152]{1,0:T(8,128)(2,1)} %feats_ref.1), channel_id=1, source_target_pairs={{0,4},{1,5},{2,6},{3,7},{4,0},{5,1},{6,2},{7,3},{8,12},{9,13},{10,... | collective-permute-start | bytes 331784 | tf_op jit(solution)/shard_map/ppermute | solution.py:27
  11.1 1.8 %copy-start = (bf16[1152,1152]{1,0:T(8,128)(2,1)S(1)}, bf16[1152,1152]{1,0:T(8,128)(2,1)}, u32[]{:S(2)}) copy-start(bf16[1152,1152]{1,0:T(8,128)(2,1)} %weight_ref.1) | copy-start | bytes 7962628
  12.9 0.9 %copy-start.1 = (bf16[48,1152]{1,0:T(8,128)(2,1)S(1)}, bf16[48,1152]{1,0:T(8,128)(2,1)}, u32[]{:S(2)}) copy-start(bf16[48,1152]{1,0:T(8,128)(2,1)} %text_ref.1) | copy-start | bytes 331780
  13.8 0.9 %copy-start.2 = (bf16[48,1152]{1,0:T(8,128)(2,1)S(1)}, bf16[48,1152]{1,0:T(8,128)(2,1)}, u32[]{:S(2)}) copy-start(bf16[48,1152]{1,0:T(8,128)(2,1)} %feats_ref.1) | copy-start | bytes 331780
  16.6 1.9 %collective-permute-start.6 = (bf16[192,1152]{1,0:T(8,128)(2,1)S(1)}, bf16[192,1152]{1,0:T(8,128)(2,1)S(1)}, u32[]{:S(2)}, u32[]{:S(2)}) collective-permute-start(bf16[192,1152]{1,0:T(8,128)(2,1)S(1)} %stack.1.own_half), channel_id=1, source_target_pairs={{0,1},{1,0},{2,3},{3,2},{4,5},{5,4},{6,7},{7,6},{8,9},{9,8},{10,11... | collective-permute-start | bytes 1327112 | tf_op jit(solution)/shard_map/ppermute | solution.py:27
  21.4 1.9 %collective-permute-start.7 = (bf16[4,160,384]{2,1,0:T(8,128)(2,1)S(1)}, bf16[4,160,384]{2,1,0:T(8,128)(2,1)S(1)}, u32[]{:S(2)}, u32[]{:S(2)}) collective-permute-start(bf16[4,160,384]{2,1,0:T(8,128)(2,1)S(1)} %get-tuple-element.51), channel_id=1, source_target_pairs={{0,1},{1,0},{2,3},{3,2},{4,5},{5,4},{6,7},{7,6},{8,9},{9,8},{10,11... | collective-permute-start | bytes 1474568 | tf_op jit(solution)/shard_map/ppermute | solution.py:27
  23.5 7.1 %collective-permute-start.10 = (bf16[160,384]{1,0:T(8,128)(2,1)S(1)}, bf16[160,384]{1,0:T(8,128)(2,1)S(1)}, u32[]{:S(2)}, u32[]{:S(2)}) collective-permute-start(bf16[160,384]{1,0:T(8,128)(2,1)S(1)} %get-tuple-element.63), channel_id=1, source_target_pairs={{0,6},{1,7},{2,4},{3,5},{4,2},{5,3},{6,0},{7,1},{8,14},{9,15},{10,... | collective-permute-start | bytes 368648 | tf_op jit(solution)/shard_map/ppermute | solution.py:27
  25.0 7.5 %collective-permute-start.8 = (bf16[160,384]{1,0:T(8,128)(2,1)S(1)}, bf16[160,384]{1,0:T(8,128)(2,1)S(1)}, u32[]{:S(2)}, u32[]{:S(2)}) collective-permute-start(bf16[160,384]{1,0:T(8,128)(2,1)S(1)} %get-tuple-element.61), channel_id=1, source_target_pairs={{0,2},{1,3},{2,0},{3,1},{4,6},{5,7},{6,4},{7,5},{8,10},{9,11},{10,... | collective-permute-start | bytes 368648 | tf_op jit(solution)/shard_map/ppermute | solution.py:27
  26.5 5.9 %collective-permute-start.9 = (bf16[160,384]{1,0:T(8,128)(2,1)S(1)}, bf16[160,384]{1,0:T(8,128)(2,1)S(1)}, u32[]{:S(2)}, u32[]{:S(2)}) collective-permute-start(bf16[160,384]{1,0:T(8,128)(2,1)S(1)} %get-tuple-element.62), channel_id=1, source_target_pairs={{0,4},{1,5},{2,6},{3,7},{4,0},{5,1},{6,2},{7,3},{8,12},{9,13},{10,... | collective-permute-start | bytes 368648 | tf_op jit(solution)/shard_map/ppermute | solution.py:27
  27.0 10.1 %collective-permute-start.11 = (bf16[48,1152]{1,0:T(8,128)(2,1)S(1)}, bf16[48,1152]{1,0:T(8,128)(2,1)S(1)}, u32[]{:S(2)}, u32[]{:S(2)}) collective-permute-start(bf16[48,1152]{1,0:T(8,128)(2,1)S(1)} %get-tuple-element.70), channel_id=1, source_target_pairs={{0,16},{1,17},{2,18},{3,19},{4,20},{5,21},{6,22},{7,23},{8,24},{9,... | collective-permute-start | bytes 331784 | tf_op jit(solution)/shard_map/ppermute | solution.py:27
  27.8 9.4 %collective-permute-start.12 = (bf16[48,1152]{1,0:T(8,128)(2,1)S(1)}, bf16[48,1152]{1,0:T(8,128)(2,1)S(1)}, u32[]{:S(2)}, u32[]{:S(2)}) collective-permute-start(bf16[48,1152]{1,0:T(8,128)(2,1)S(1)} %get-tuple-element.71), channel_id=1, source_target_pairs={{0,24},{1,25},{2,26},{3,27},{4,28},{5,29},{6,30},{7,31},{8,16},{9,... | collective-permute-start | bytes 331784 | tf_op jit(solution)/shard_map/ppermute | solution.py:27
  30.6 7.6 %collective-permute-start.13 = (bf16[48,1152]{1,0:T(8,128)(2,1)S(1)}, bf16[48,1152]{1,0:T(8,128)(2,1)S(1)}, u32[]{:S(2)}, u32[]{:S(2)}) collective-permute-start(bf16[48,1152]{1,0:T(8,128)(2,1)S(1)} %get-tuple-element.72), channel_id=1, source_target_pairs={{0,8},{1,9},{2,10},{3,11},{4,12},{5,13},{6,14},{7,15},{8,0},{9,1},... | collective-permute-start | bytes 331784 | tf_op jit(solution)/shard_map/ppermute | solution.py:27
  38.2 14.7 %all-to-all-start = ((bf16[8,176,128]{2,1,0:T(8,128)(2,1)}), bf16[8,176,128]{2,1,0:T(8,128)(2,1)S(1)}, u32[]{:S(2)}, u32[]{:S(2)}) async-start(bf16[8,176,128]{2,1,0:T(8,128)(2,1)} %get-tuple-element.76), calls=%async_computation | async-start | bytes 720896 | tf_op jit(solution)/shard_map/all_to_all | solution.py:359

commit v9 on v8

--- a/solution.py
+++ b/solution.py
@@ -76,6 +76,10 @@
         out[step * rows : (step + 1) * rows, :] = (values * inverse).astype(BF16)
 
 
+def project_kernel(feats_ref, weight_ref, out):
+    out[...] = jnp.dot(feats_ref[...], weight_ref[...], preferred_element_type=F32)
+
+
 def first_image(member, rows, group):
     return (member % 2) * (group // 2 * rows) + (member // 2) * rows
 
@@ -87,6 +91,7 @@
     scalars_ref,
     weight,
     own_half,
+    own_proj,
     got_half,
     text_all,
     feats_ref,
@@ -98,6 +103,7 @@
     send_out,
     unit_all,
     d_all,
+    proj_all,
 ):
     images, width = feats_ref.shape
     rows = images // group
@@ -108,12 +114,13 @@
 
     place = pl.multiple_of((member % 2) * half, half)
     feats_ref[pl.ds(place, half), :] = own_half[...]
+    proj_all[pl.ds(place, half), :] = own_proj[...]
     place = pl.multiple_of((1 - member % 2) * half, half)
     feats_ref[pl.ds(place, half), :] = got_half[...]
+    proj_all[pl.ds(place, half), :] = jnp.dot(got_half[...], weight[...], preferred_element_type=F32)
     for start in range(0, images, LANES):
         cols = slice(start, start + LANES)
-        proj = jnp.dot(feats_ref[cols, :], weight[...], preferred_element_type=F32)
-        turned = proj.T
+        turned = proj_all[cols, :].T
         inverse = lax.rsqrt(jnp.sum(turned * turned, axis=0, keepdims=True) + 1e-06)
         unit = turned * inverse
         inv_out[:, cols] = inverse
@@ -257,11 +264,15 @@
     images = group * rows
     member = lax.axis_index(AXES[1:]).astype(jnp.int32).reshape(1)
 
-    texts = [swapped(text_embed, total, step * group) for step in range(1, spread)]
+    far = swapped(text_embed, total, 2 * group)
+    near = swapped(text_embed, total, group)
     got_feats = [swapped(image_feats, total, 2 * step) for step in range(1, group // 2)]
-    arrived = lax.optimization_barrier([got_feats[0], *texts[:0:-1], got_feats[-1], texts[0], *got_feats[1:-1]])
-    got_feats = [arrived[0], *arrived[spread + 1 :], arrived[spread - 1]]
-    texts = [arrived[spread], *arrived[spread - 2 : 0 : -1]]
+    far, last, near, *rest_feats = lax.optimization_barrier([far, got_feats[-1], near, *got_feats[-2::-1]])
+    got_feats = [*rest_feats[::-1], last]
+    texts = [near, far, swapped(far, total, group)]
+    while len(texts) + 1 < spread:
+        mask = (len(texts) + 1) * group
+        texts += [swapped(text, total, mask) for text in [text_embed, *texts]]
     weight, own_feats, own_text, scalars = pl.pallas_call(
         load_kernel,
         in_specs=[SMEM] * 2 + [VMEM] * 3,
@@ -284,6 +295,14 @@
         name="stack",
     )(member, own_feats, *got_feats)
     got_half = swapped(own_half, total, 1)
+    own_proj = pl.pallas_call(
+        project_kernel,
+        in_specs=[VMEM] * 2,
+        out_specs=VMEM,
+        out_shape=jax.ShapeDtypeStruct((images // 2, width), F32),
+        compiler_params=limit(8),
+        name="own_projection",
+    )(own_half, weight)
     text_emb = pl.pallas_call(
         text_kernel,
         in_specs=[VMEM] * spread,
@@ -295,7 +314,7 @@
 
     results = pl.pallas_call(
         functools.partial(pair_kernel, narrow, group),
-        in_specs=[SMEM] + [VMEM] * 5,
+        in_specs=[SMEM] + [VMEM] * 6,
         out_specs=[VMEM] * 7,
         out_shape=[
             jax.ShapeDtypeStruct((images, width), BF16),
@@ -309,10 +328,11 @@
         scratch_shapes=[
             pltpu.VMEM((width, images), F32),
             pltpu.VMEM((width, images), F32),
+            pltpu.VMEM((images, width), F32),
         ],
         compiler_params=limit(24 if spread <= 4 else 40),
         name="pairs",
-    )(member, scalars, weight, own_half, got_half, text_emb)
+    )(member, scalars, weight, own_half, own_proj, got_half, text_emb)
     all_feats, unit_part, inv_part, img_emb, grad_tile, own_part, sent_part = results
     got_part = swapped(sent_part, total, 1)
     feats_t, own_text, *sent_text = pl.pallas_call(
@@ -336,6 +356,7 @@
         name="chip_sum",
     )(own_part, got_part)
     got = [swapped(value, total, 2 * index) for index, value in enumerate(chip_parts, 1)]
+    got_text[1], got = lax.optimization_barrier((got_text[1], got))
 
     out_rows = width // wide
     rest = share - LANES

time: 54.1 us -> 54.4 us (level)
  Pallas kernels: 8.1 us -> 8.65 us
    all_to_all x1, waiting for transfers between devices: 9.1 us -> 7.61 us  [local(): got_weight = lax.all_to_all(sent_weight, AXES[:2], 0, 0)]
    ppermute x14, waiting for transfers between devices: 10.6 us -> 12 us  [swapped(): lax.ppermute(value, AXES, [(source, source ^ mask) for source in range(to...]
    all_to_all x1, starting transfers between devices: 4.26 us -> 3.44 us  [local(): got_weight = lax.all_to_all(sent_weight, AXES[:2], 0, 0)]
    pallas_call x0 -> x1, Pallas kernels: none -> 0.8 us  [local(): pl.pallas_call(project_kernel, in_specs=[VMEM] * 2, out_specs=VMEM, out_s...]
    ppermute x14, starting transfers between devices: 15.6 us -> 16.2 us  [swapped(): lax.ppermute(value, AXES, [(source, source ^ mask) for source in range(to...]
  transfers between devices with their start and end apart: 15 -> 15, of which waited for: 8 -> 5; matrix products, arithmetic and copies ran while one was open for 1% -> 1% of each run, Pallas kernels for 8% -> 9%
where the time goes in v9:
time: 54.4 us; the launch traced here: 54.1 us
  starting transfers between devices  19.6 us (36%)
  waiting for transfers between devices  19.6 us (36%)
  Pallas kernels  8.65 us (16%)
  local copies, waits for them, and re-layouts  4.12 us (8%)
  between operations  2.09 us (4%)
    ppermute x14, starting transfers between devices, swapped(): lax.ppermute(value, AXES, [(source, source ^ mask) for source in range(to...  16.2 us
    ppermute x14, waiting for transfers between devices, swapped(): lax.ppermute(value, AXES, [(source, source ^ mask) for source in range(to...  12 us
    all_to_all x1, waiting for transfers between devices, local(): got_weight = lax.all_to_all(sent_weight, AXES[:2], 0, 0)  7.61 us
    unnamed x6, local copies, waits for them, and re-layouts  3.54 us
    all_to_all x1, starting transfers between devices, local(): got_weight = lax.all_to_all(sent_weight, AXES[:2], 0, 0)  3.44 us
    pallas_call x1, Pallas kernels, local(): pl.pallas_call(functools.partial(pair_kernel, narrow, group), in_specs=[S...  2.74 us
    pallas_call x1, Pallas kernels, local(): pl.pallas_call(functools.partial(weight_kernel, group, wide), in_specs=[V...  1.73 us
    pallas_call x1, Pallas kernels, local(): pl.pallas_call(functools.partial(caption_kernel, rows), in_specs=[VMEM] *...  1.23 us
  transfers between devices with their start and end apart: 15, of which 5 were waited for; matrix products, arithmetic and copies ran while one was open for 1% of the time, Pallas kernels for 9%

profile of v9, /device:TPU:0, one launch (start us, length us, event | category | flops | bytes accessed | tf_op | source)
XLA Modules:
  0.0 54.1 jit_solution(8751548612520913764)
XLA Ops:
  0.6 4.1 %collective-permute-start = (bf16[48,1152]{1,0:T(8,128)(2,1)}, bf16[48,1152]{1,0:T(8,128)(2,1)S(1)}, u32[]{:S(2)}, u32[]{:S(2)}) collective-permute-start(bf16[48,1152]{1,0:T(8,128)(2,1)} %text_ref.1), channel_id=1, source_target_pairs={{0,16},{1,17},{2,18},{3,19},{4,20},{5,21},{6,22},{7,23},{8,24},{9,... | collective-permute-start | bytes 331784 | tf_op jit(solution)/shard_map/ppermute | solution.py:27
  4.7 2.4 %collective-permute-start.1 = (bf16[48,1152]{1,0:T(8,128)(2,1)}, bf16[48,1152]{1,0:T(8,128)(2,1)S(1)}, u32[]{:S(2)}, u32[]{:S(2)}) collective-permute-start(bf16[48,1152]{1,0:T(8,128)(2,1)} %feats_ref.1), channel_id=1, source_target_pairs={{0,6},{1,7},{2,4},{3,5},{4,2},{5,3},{6,0},{7,1},{8,14},{9,15},{10,... | collective-permute-start | bytes 331784 | tf_op jit(solution)/shard_map/ppermute | solution.py:27
  7.2 1.6 %collective-permute-start.2 = (bf16[48,1152]{1,0:T(8,128)(2,1)}, bf16[48,1152]{1,0:T(8,128)(2,1)S(1)}, u32[]{:S(2)}, u32[]{:S(2)}) collective-permute-start(bf16[48,1152]{1,0:T(8,128)(2,1)} %text_ref.1), channel_id=1, source_target_pairs={{0,8},{1,9},{2,10},{3,11},{4,12},{5,13},{6,14},{7,15},{8,0},{9,1},... | collective-permute-start | bytes 331784 | tf_op jit(solution)/shard_map/ppermute | solution.py:27
  8.8 0.5 collective-permute-start.3
  11.1 1.7 %copy-done = bf16[1152,1152]{1,0:T(8,128)(2,1)S(1)} copy-done((bf16[1152,1152]{1,0:T(8,128)(2,1)S(1)}, bf16[1152,1152]{1,0:T(8,128)(2,1)}, u32[]{:S(2)}) %copy-start) | copy-done | bytes 2654232
  12.9 0.9 %copy-done.1 = bf16[48,1152]{1,0:T(8,128)(2,1)S(1)} copy-done((bf16[48,1152]{1,0:T(8,128)(2,1)S(1)}, bf16[48,1152]{1,0:T(8,128)(2,1)}, u32[]{:S(2)}) %copy-start.1) | copy-done | bytes 110616
  13.7 0.9 %copy-done.2 = bf16[48,1152]{1,0:T(8,128)(2,1)S(1)} copy-done((bf16[48,1152]{1,0:T(8,128)(2,1)S(1)}, bf16[48,1152]{1,0:T(8,128)(2,1)}, u32[]{:S(2)}) %copy-start.2) | copy-done | bytes 110616
  15.0 0.5 collective-permute-start.6
  15.6 0.8 %own_projection.1.own_proj = f32[192,1152]{1,0:T(8,128)S(1)} custom-call(bf16[192,1152]{1,0:T(8,128)(2,1)S(1)} %stack.1.feats_ref.own_half, bf16[1152,1152]{1,0:T(8,128)(2,1)S(1)} %get-tuple-element.44.weight_ref.weight), custom_call_target="tpu_custom_call" | custom-call | tf_op jit(solution)/shard_map/own_projection/pallas_call | solution.py:298
  16.4 4.2 %collective-permute-done.6.refs_3_ = bf16[48,1152]{1,0:T(8,128)(2,1)S(1)} collective-permute-done((bf16[48,1152]{1,0:T(8,128)(2,1)S(1)}, bf16[48,1152]{1,0:T(8,128)(2,1)S(1)}, u32[]{:S(2)}, u32[]{:S(2)}) %collective-permute-start.6) | collective-permute-done | bytes 110624 | tf_op jit(solution)/shard_map/ppermute | solution.py:27
  20.7 2.7 %pairs.1 = (bf16[384,1152]{1,0:T(8,128)(2,1)S(1)}, f32[144,384]{1,0:T(8,128)S(1)}, f32[1,384]{1,0:T(1,128)S(1)}, bf16[1152,384]{1,0:T(8,128)(2,1)S(1)}, bf16[192...) custom-call(s32[1]{0:T(128)} %bitcast.member_ref, ...), custom_call_target="tpu_custom_call" | custom-call | tf_op jit(solution)/shard_map/pairs/pallas_call | solution.py:315
  23.5 1.2 %captions.1 = (bf16[1152,384]{1,0:T(8,128)(2,1)S(1)}, f32[48,1152]{1,0:T(8,128)S(1)}, bf16[48,1152]{1,0:T(8,128)(2,1)S(1)}, bf16[48,1152]{1,0:T(8,128)(2,1)S(1)}, bf16[48,1152]{1,0:T(8,128)(2,1)S(1)}) custom-call(bf16[192,384]{1,0:T(8,128)(2,1)S(1)} %get-tuple-element.54.grad_ref, bf16[1152,384]{1,0:T(8,128)(2,1)S(1)} %get-tuple-element.55.emb_ref, ...), custom_call_target="tpu_custom_call" | custom-call | tf_op jit(solution)/shard_map/captions/pallas_call | solution.py:338
  24.8 0.6 %collective-permute-done.7.got_ref = bf16[4,160,384]{2,1,0:T(8,128)(2,1)S(1)} collective-permute-done((bf16[4,160,384]{2,1,0:T(8,128)(2,1)S(1)}, bf16[4,160,384]{2,1,0:T(8,128)(2,1)S(1)}, u32[]{:S(2)}, u32[]{:S(2)}) %collective-permute-start.7) | collective-permute-done | bytes 491552 | tf_op jit(solution)/shard_map/ppermute | solution.py:27
  25.8 1.6 %collective-permute-start.10 = (bf16[160,384]{1,0:T(8,128)(2,1)S(1)}, bf16[160,384]{1,0:T(8,128)(2,1)S(1)}, u32[]{:S(2)}, u32[]{:S(2)}) collective-permute-start(bf16[160,384]{1,0:T(8,128)(2,1)S(1)} %get-tuple-element.65), channel_id=1, source_target_pairs={{0,4},{1,5},{2,6},{3,7},{4,0},{5,1},{6,2},{7,3},{8,12},{9,13},{10,... | collective-permute-start | bytes 368648 | tf_op jit(solution)/shard_map/ppermute | solution.py:27
  27.4 1.5 %collective-permute-start.11 = (bf16[160,384]{1,0:T(8,128)(2,1)S(1)}, bf16[160,384]{1,0:T(8,128)(2,1)S(1)}, u32[]{:S(2)}, u32[]{:S(2)}) collective-permute-start(bf16[160,384]{1,0:T(8,128)(2,1)S(1)} %get-tuple-element.66), channel_id=1, source_target_pairs={{0,6},{1,7},{2,4},{3,5},{4,2},{5,3},{6,0},{7,1},{8,14},{9,15},{10,... | collective-permute-start | bytes 368648 | tf_op jit(solution)/shard_map/ppermute | solution.py:27
  29.4 2.5 %collective-permute-start.12 = (bf16[48,1152]{1,0:T(8,128)(2,1)S(1)}, bf16[48,1152]{1,0:T(8,128)(2,1)S(1)}, u32[]{:S(2)}, u32[]{:S(2)}) collective-permute-start(bf16[48,1152]{1,0:T(8,128)(2,1)S(1)} %get-tuple-element.77), channel_id=1, source_target_pairs={{0,24},{1,25},{2,26},{3,27},{4,28},{5,29},{6,30},{7,31},{8,16},{9,... | collective-permute-start | bytes 331784 | tf_op jit(solution)/shard_map/ppermute | solution.py:27
  31.9 4.2 %collective-permute-done.8.refs_2_ = bf16[48,1152]{1,0:T(8,128)(2,1)S(1)} collective-permute-done((bf16[48,1152]{1,0:T(8,128)(2,1)S(1)}, bf16[48,1152]{1,0:T(8,128)(2,1)S(1)}, u32[]{:S(2)}, u32[]{:S(2)}) %collective-permute-start.8) | collective-permute-done | bytes 110624 | tf_op jit(solution)/shard_map/ppermute | solution.py:27
  36.1 1.7 %weights.1 = (f32[1,384]{1,0:T(1,128)S(1)}, bf16[8,176,128]{2,1,0:T(8,128)(2,1)}) custom-call(f32[152,384]{1,0:T(8,128)S(1)} %get-tuple-element.62.refs_0_, bf16[160,384]{1,0:T(8,128)(2,1)S(1)} %collective-permute-done.9.refs_1_, bf16[160,384]{1,0:T(8,128)(2,1)S(1)} %collective-permute-done.10.refs_2_, bf16[160,384]{1,0:T(8,128)(2,1)S(1)} %collective-permute-done.11.refs_3_, ...), custom_call_target="tpu_custom_call" | custom-call | tf_op jit(solution)/shard_map/weights/pallas_call | solution.py:366
  37.8 3.0 %collective-permute-done.13.refs_1_ = bf16[48,1152]{1,0:T(8,128)(2,1)S(1)} collective-permute-done((bf16[48,1152]{1,0:T(8,128)(2,1)S(1)}, bf16[48,1152]{1,0:T(8,128)(2,1)S(1)}, u32[]{:S(2)}, u32[]{:S(2)}) %collective-permute-start.13) | collective-permute-done | bytes 110624 | tf_op jit(solution)/shard_map/ppermute | solution.py:27
  40.8 3.4 %all-to-all-start = ((bf16[8,176,128]{2,1,0:T(8,128)(2,1)}), bf16[8,176,128]{2,1,0:T(8,128)(2,1)S(1)}, u32[]{:S(2)}, u32[]{:S(2)}) async-start(bf16[8,176,128]{2,1,0:T(8,128)(2,1)} %get-tuple-element.82), calls=%async_computation | async-start | bytes 720896 | tf_op jit(solution)/shard_map/all_to_all | solution.py:380
  44.3 0.7 %caption_total.1 = f32[48,1152]{1,0:T(8,128)} custom-call(f32[48,1152]{1,0:T(8,128)S(1)} %get-tuple-element.74.refs_0_, bf16[48,1152]{1,0:T(8,128)(2,1)S(1)} %collective-permute-done.13.refs_1_, bf16[48,1152]{1,0:T(8,128)(2,1)S(1)} %collective-permute-done.8.refs_2_, bf16[48,1152]{1,0:T(8,128)(2,1)S(1)} %collective-permute-done.12.refs_3_), custom_call_target="tpu_custom_call" | custom-call | tf_op jit(solution)/shard_map/caption_total/pallas_call | solution.py:411
  45.0 0.6 %dynamic-slice_bitcast_fusion = f32[48]{0:T(128)} fusion(f32[1,384]{1,0:T(1,128)S(1)} %get-tuple-element.73, s32[]{:T(128)S(6)} %select_n.16), kind=kLoop, calls=%fused_computation | loop fusion | bytes 388 | tf_op jit(solution)/shard_map/dynamic_slice | solution.py:419
  45.6 7.6 %all-to-all-done.got_ref = bf16[8,176,128]{2,1,0:T(8,128)(2,1)S(1)} async-done(((bf16[8,176,128]{2,1,0:T(8,128)(2,1)}), bf16[8,176,128]{2,1,0:T(8,128)(2,1)S(1)}, u32[]{:S(2)}, u32[]{:S(2)}) %all-to-all-start) | async-done | bytes 360480 | tf_op jit(solution)/shard_map/all_to_all | solution.py:380
  53.2 0.9 %weight_total.1 = f32[144,288]{1,0:T(8,128)} custom-call(bf16[8,176,128]{2,1,0:T(8,128)(2,1)S(1)} %all-to-all-done.got_ref), custom_call_target="tpu_custom_call" | custom-call | tf_op jit(solution)/shard_map/weight_total/pallas_call | solution.py:381
  (23 shorter events, 2.1 us)
Async XLA Ops:
  0.6 14.2 %collective-permute-start = (bf16[48,1152]{1,0:T(8,128)(2,1)}, bf16[48,1152]{1,0:T(8,128)(2,1)S(1)}, u32[]{:S(2)}, u32[]{:S(2)}) collective-permute-start(bf16[48,1152]{1,0:T(8,128)(2,1)} %text_ref.1), channel_id=1, source_target_pairs={{0,16},{1,17},{2,18},{3,19},{4,20},{5,21},{6,22},{7,23},{8,24},{9,... | collective-permute-start | bytes 331784 | tf_op jit(solution)/shard_map/ppermute | solution.py:27
  4.7 10.1 %collective-permute-start.1 = (bf16[48,1152]{1,0:T(8,128)(2,1)}, bf16[48,1152]{1,0:T(8,128)(2,1)S(1)}, u32[]{:S(2)}, u32[]{:S(2)}) collective-permute-start(bf16[48,1152]{1,0:T(8,128)(2,1)} %feats_ref.1), channel_id=1, source_target_pairs={{0,6},{1,7},{2,4},{3,5},{4,2},{5,3},{6,0},{7,1},{8,14},{9,15},{10,... | collective-permute-start | bytes 331784 | tf_op jit(solution)/shard_map/ppermute | solution.py:27
  7.2 7.7 %collective-permute-start.2 = (bf16[48,1152]{1,0:T(8,128)(2,1)}, bf16[48,1152]{1,0:T(8,128)(2,1)S(1)}, u32[]{:S(2)}, u32[]{:S(2)}) collective-permute-start(bf16[48,1152]{1,0:T(8,128)(2,1)} %text_ref.1), channel_id=1, source_target_pairs={{0,8},{1,9},{2,10},{3,11},{4,12},{5,13},{6,14},{7,15},{8,0},{9,1},... | collective-permute-start | bytes 331784 | tf_op jit(solution)/shard_map/ppermute | solution.py:27
  8.8 6.1 %collective-permute-start.3 = (bf16[48,1152]{1,0:T(8,128)(2,1)}, bf16[48,1152]{1,0:T(8,128)(2,1)S(1)}, u32[]{:S(2)}, u32[]{:S(2)}) collective-permute-start(bf16[48,1152]{1,0:T(8,128)(2,1)} %feats_ref.1), channel_id=1, source_target_pairs={{0,4},{1,5},{2,6},{3,7},{4,0},{5,1},{6,2},{7,3},{8,12},{9,13},{10,... | collective-permute-start | bytes 331784 | tf_op jit(solution)/shard_map/ppermute | solution.py:27
  9.3 5.6 %collective-permute-start.4 = (bf16[48,1152]{1,0:T(8,128)(2,1)}, bf16[48,1152]{1,0:T(8,128)(2,1)S(1)}, u32[]{:S(2)}, u32[]{:S(2)}) collective-permute-start(bf16[48,1152]{1,0:T(8,128)(2,1)} %feats_ref.1), channel_id=1, source_target_pairs={{0,2},{1,3},{2,0},{3,1},{4,6},{5,7},{6,4},{7,5},{8,10},{9,11},{10,... | collective-permute-start | bytes 331784 | tf_op jit(solution)/shard_map/ppermute | solution.py:27
  11.1 1.8 %copy-start = (bf16[1152,1152]{1,0:T(8,128)(2,1)S(1)}, bf16[1152,1152]{1,0:T(8,128)(2,1)}, u32[]{:S(2)}) copy-start(bf16[1152,1152]{1,0:T(8,128)(2,1)} %weight_ref.1) | copy-start | bytes 7962628
  12.8 0.9 %copy-start.1 = (bf16[48,1152]{1,0:T(8,128)(2,1)S(1)}, bf16[48,1152]{1,0:T(8,128)(2,1)}, u32[]{:S(2)}) copy-start(bf16[48,1152]{1,0:T(8,128)(2,1)} %text_ref.1) | copy-start | bytes 331780
  13.7 0.9 %copy-start.2 = (bf16[48,1152]{1,0:T(8,128)(2,1)S(1)}, bf16[48,1152]{1,0:T(8,128)(2,1)}, u32[]{:S(2)}) copy-start(bf16[48,1152]{1,0:T(8,128)(2,1)} %feats_ref.1) | copy-start | bytes 331780
  15.0 5.7 %collective-permute-start.5 = (bf16[192,1152]{1,0:T(8,128)(2,1)S(1)}, bf16[192,1152]{1,0:T(8,128)(2,1)S(1)}, u32[]{:S(2)}, u32[]{:S(2)}) collective-permute-start(bf16[192,1152]{1,0:T(8,128)(2,1)S(1)} %stack.1.feats_ref.own_half), channel_id=1, source_target_pairs={{0,1},{1,0},{2,3},{3,2},{4,5},{5,4},{6,7},{7,6},{8,9},{9,8},{10,11... | collective-permute-start | bytes 1327112 | tf_op jit(solution)/shard_map/ppermute | solution.py:27
  15.0 5.5 %collective-permute-start.6 = (bf16[48,1152]{1,0:T(8,128)(2,1)S(1)}, bf16[48,1152]{1,0:T(8,128)(2,1)S(1)}, u32[]{:S(2)}, u32[]{:S(2)}) collective-permute-start(bf16[48,1152]{1,0:T(8,128)(2,1)S(1)} %collective-permute-done.refs_2_), channel_id=1, source_target_pairs={{0,8},{1,9},{2,10},{3,11},{4,12},{5,13},{6,14},{7,15},{8,0},{9,1},... | collective-permute-start | bytes 331784 | tf_op jit(solution)/shard_map/ppermute | solution.py:27
  23.4 1.9 %collective-permute-start.7 = (bf16[4,160,384]{2,1,0:T(8,128)(2,1)S(1)}, bf16[4,160,384]{2,1,0:T(8,128)(2,1)S(1)}, u32[]{:S(2)}, u32[]{:S(2)}) collective-permute-start(bf16[4,160,384]{2,1,0:T(8,128)(2,1)S(1)} %get-tuple-element.53), channel_id=1, source_target_pairs={{0,1},{1,0},{2,3},{3,2},{4,5},{5,4},{6,7},{7,6},{8,9},{9,8},{10,11... | collective-permute-start | bytes 1474568 | tf_op jit(solution)/shard_map/ppermute | solution.py:27
  25.4 10.7 %collective-permute-start.8 = (bf16[48,1152]{1,0:T(8,128)(2,1)S(1)}, bf16[48,1152]{1,0:T(8,128)(2,1)S(1)}, u32[]{:S(2)}, u32[]{:S(2)}) collective-permute-start(bf16[48,1152]{1,0:T(8,128)(2,1)S(1)} %get-tuple-element.63), channel_id=1, source_target_pairs={{0,16},{1,17},{2,18},{3,19},{4,20},{5,21},{6,22},{7,23},{8,24},{9,... | collective-permute-start | bytes 331784 | tf_op jit(solution)/shard_map/ppermute | solution.py:27
  25.8 10.2 %collective-permute-start.10 = (bf16[160,384]{1,0:T(8,128)(2,1)S(1)}, bf16[160,384]{1,0:T(8,128)(2,1)S(1)}, u32[]{:S(2)}, u32[]{:S(2)}) collective-permute-start(bf16[160,384]{1,0:T(8,128)(2,1)S(1)} %get-tuple-element.65), channel_id=1, source_target_pairs={{0,4},{1,5},{2,6},{3,7},{4,0},{5,1},{6,2},{7,3},{8,12},{9,13},{10,... | collective-permute-start | bytes 368648 | tf_op jit(solution)/shard_map/ppermute | solution.py:27
  27.4 8.7 %collective-permute-start.11 = (bf16[160,384]{1,0:T(8,128)(2,1)S(1)}, bf16[160,384]{1,0:T(8,128)(2,1)S(1)}, u32[]{:S(2)}, u32[]{:S(2)}) collective-permute-start(bf16[160,384]{1,0:T(8,128)(2,1)S(1)} %get-tuple-element.66), channel_id=1, source_target_pairs={{0,6},{1,7},{2,4},{3,5},{4,2},{5,3},{6,0},{7,1},{8,14},{9,15},{10,... | collective-permute-start | bytes 368648 | tf_op jit(solution)/shard_map/ppermute | solution.py:27
  28.9 7.2 %collective-permute-start.9 = (bf16[160,384]{1,0:T(8,128)(2,1)S(1)}, bf16[160,384]{1,0:T(8,128)(2,1)S(1)}, u32[]{:S(2)}, u32[]{:S(2)}) collective-permute-start(bf16[160,384]{1,0:T(8,128)(2,1)S(1)} %get-tuple-element.64), channel_id=1, source_target_pairs={{0,2},{1,3},{2,0},{3,1},{4,6},{5,7},{6,4},{7,5},{8,10},{9,11},{10,... | collective-permute-start | bytes 368648 | tf_op jit(solution)/shard_map/ppermute | solution.py:27
  29.4 8.4 %collective-permute-start.12 = (bf16[48,1152]{1,0:T(8,128)(2,1)S(1)}, bf16[48,1152]{1,0:T(8,128)(2,1)S(1)}, u32[]{:S(2)}, u32[]{:S(2)}) collective-permute-start(bf16[48,1152]{1,0:T(8,128)(2,1)S(1)} %get-tuple-element.77), channel_id=1, source_target_pairs={{0,24},{1,25},{2,26},{3,27},{4,28},{5,29},{6,30},{7,31},{8,16},{9,... | collective-permute-start | bytes 331784 | tf_op jit(solution)/shard_map/ppermute | solution.py:27
  36.1 4.7 %collective-permute-start.13 = (bf16[48,1152]{1,0:T(8,128)(2,1)S(1)}, bf16[48,1152]{1,0:T(8,128)(2,1)S(1)}, u32[]{:S(2)}, u32[]{:S(2)}) collective-permute-start(bf16[48,1152]{1,0:T(8,128)(2,1)S(1)} %get-tuple-element.78), channel_id=1, source_target_pairs={{0,8},{1,9},{2,10},{3,11},{4,12},{5,13},{6,14},{7,15},{8,0},{9,1},... | collective-permute-start | bytes 331784 | tf_op jit(solution)/shard_map/ppermute | solution.py:27
  40.8 12.4 %all-to-all-start = ((bf16[8,176,128]{2,1,0:T(8,128)(2,1)}), bf16[8,176,128]{2,1,0:T(8,128)(2,1)S(1)}, u32[]{:S(2)}, u32[]{:S(2)}) async-start(bf16[8,176,128]{2,1,0:T(8,128)(2,1)} %get-tuple-element.82), calls=%async_computation | async-start | bytes 720896 | tf_op jit(solution)/shard_map/all_to_all | solution.py:380

commit v10 on v9

--- a/solution.py
+++ b/solution.py
@@ -23,6 +23,10 @@
     return pltpu.CompilerParams(vmem_limit_bytes=mebibytes * MIB)
 
 
+def hint(flops):
+    return pl.CostEstimate(flops=flops, bytes_accessed=0, transcendentals=0)
+
+
 def swapped(value, total, mask):
     return lax.ppermute(value, AXES, [(source, source ^ mask) for source in range(total)])
 
@@ -49,31 +53,35 @@
     return (member % narrow) * 2 + member // narrow
 
 
-def load_kernel(log_scale_ref, bias_ref, weight_ref, feats_ref, text_ref, weight_out, feats_out, text_out, scalars_out):
-    weight_out[...] = weight_ref[...]
-    feats_out[...] = feats_ref[...]
-    text_out[...] = text_ref[...]
+def unit_text(text):
+    values = text.astype(F32)
+    inverse = lax.rsqrt(jnp.sum(values * values, axis=1, keepdims=True) + 1e-06)
+    return (values * inverse).astype(BF16)
+
+
+def own_kernel(log_scale_ref, bias_ref, text_ref, text_out, scalars_out):
+    text_out[...] = unit_text(text_ref[...])
     row = lax.broadcasted_iota(jnp.int32, scalars_out.shape, 0)
     scale = jnp.exp(jnp.full(scalars_out.shape, log_scale_ref[0], F32))
     scalars_out[...] = jnp.where(row == 0, scale, bias_ref[0])
 
 
 def stack_kernel(member_ref, *refs):
-    blocks, out = refs[:-1], refs[-1]
+    blocks, half_out = refs[:-1], refs[-1]
     rows = blocks[0].shape[0]
     chip = member_ref[0] // 2
     for step, block in enumerate(blocks):
         place = pl.multiple_of((chip ^ step) * rows, rows)
-        out[pl.ds(place, rows), :] = block[...]
+        half_out[pl.ds(place, rows), :] = block[...]
 
 
 def text_kernel(*refs):
     texts, out = refs[:-1], refs[-1]
     rows = texts[0].shape[0]
-    for step, text in enumerate(texts):
-        values = text[...].astype(F32)
-        inverse = lax.rsqrt(jnp.sum(values * values, axis=1, keepdims=True) + 1e-06)
-        out[step * rows : (step + 1) * rows, :] = (values * inverse).astype(BF16)
+    out[:rows, :] = texts[0][...]
+    for place, text in enumerate(texts[1:], 1):
+        step = len(texts) - place
+        out[step * rows : (step + 1) * rows, :] = unit_text(text[...])
 
 
 def project_kernel(feats_ref, weight_ref, out):
@@ -264,28 +272,17 @@
     images = group * rows
     member = lax.axis_index(AXES[1:]).astype(jnp.int32).reshape(1)
 
-    far = swapped(text_embed, total, 2 * group)
-    near = swapped(text_embed, total, group)
+    texts = [swapped(text_embed, total, step * group) for step in range(1, spread)]
     got_feats = [swapped(image_feats, total, 2 * step) for step in range(1, group // 2)]
-    far, last, near, *rest_feats = lax.optimization_barrier([far, got_feats[-1], near, *got_feats[-2::-1]])
-    got_feats = [*rest_feats[::-1], last]
-    texts = [near, far, swapped(far, total, group)]
-    while len(texts) + 1 < spread:
-        mask = (len(texts) + 1) * group
-        texts += [swapped(text, total, mask) for text in [text_embed, *texts]]
-    weight, own_feats, own_text, scalars = pl.pallas_call(
-        load_kernel,
-        in_specs=[SMEM] * 2 + [VMEM] * 3,
-        out_specs=[VMEM] * 4,
-        out_shape=[
-            jax.ShapeDtypeStruct((width, width), BF16),
-            jax.ShapeDtypeStruct((rows, width), BF16),
-            jax.ShapeDtypeStruct((rows, width), BF16),
-            jax.ShapeDtypeStruct((8, LANES), F32),
-        ],
-        compiler_params=limit(8),
-        name="load",
-    )(log_scale, logit_bias, proj_weight, image_feats, text_embed)
+    own_text, scalars = pl.pallas_call(
+        own_kernel,
+        in_specs=[SMEM] * 2 + [VMEM],
+        out_specs=[VMEM] * 2,
+        out_shape=[jax.ShapeDtypeStruct((rows, width), BF16), jax.ShapeDtypeStruct((8, LANES), F32)],
+        compiler_params=limit(4),
+        cost_estimate=hint(10**10),
+        name="own_text",
+    )(log_scale, logit_bias, text_embed)
     own_half = pl.pallas_call(
         stack_kernel,
         in_specs=[SMEM] + [VMEM] * (group // 2),
@@ -293,7 +290,7 @@
         out_shape=jax.ShapeDtypeStruct((images // 2, width), BF16),
         compiler_params=limit(4),
         name="stack",
-    )(member, own_feats, *got_feats)
+    )(member, image_feats, *got_feats)
     got_half = swapped(own_half, total, 1)
     own_proj = pl.pallas_call(
         project_kernel,
@@ -302,13 +299,15 @@
         out_shape=jax.ShapeDtypeStruct((images // 2, width), F32),
         compiler_params=limit(8),
         name="own_projection",
-    )(own_half, weight)
+    )(own_half, proj_weight)
+    own_proj, *texts = lax.optimization_barrier((own_proj, *texts[::-1]))
     text_emb = pl.pallas_call(
         text_kernel,
         in_specs=[VMEM] * spread,
         out_specs=VMEM,
         out_shape=jax.ShapeDtypeStruct((spread * rows, width), BF16),
         compiler_params=limit(4 if spread <= 4 else 16),
+        cost_estimate=hint(10**10),
         name="text_unit",
     )(own_text, *texts)
 
@@ -332,7 +331,7 @@
         ],
         compiler_params=limit(24 if spread <= 4 else 40),
         name="pairs",
-    )(member, scalars, weight, own_half, own_proj, got_half, text_emb)
+    )(member, scalars, proj_weight, own_half, own_proj, got_half, text_emb)
     all_feats, unit_part, inv_part, img_emb, grad_tile, own_part, sent_part = results
     got_part = swapped(sent_part, total, 1)
     feats_t, own_text, *sent_text = pl.pallas_call(
@@ -356,7 +355,6 @@
         name="chip_sum",
     )(own_part, got_part)
     got = [swapped(value, total, 2 * index) for index, value in enumerate(chip_parts, 1)]
-    got_text[1], got = lax.optimization_barrier((got_text[1], got))
 
     out_rows = width // wide
     rest = share - LANES
@@ -374,9 +372,6 @@
             compiler_params=limit(12),
             name="weights",
         )(own_part, *got, unit_part, inv_part, all_feats, feats_t)
-        order = [*got_text[1:], got_text[0]]
-        sent_weight, *order = lax.optimization_barrier((sent_weight, *order))
-        got_text = [order[-1], *order[:-1]]
         got_weight = lax.all_to_all(sent_weight, AXES[:2], 0, 0)
         d_proj = pl.pallas_call(
             functools.partial(total_kernel, rest),
@@ -414,6 +409,7 @@
         out_specs=VMEM,
         out_shape=jax.ShapeDtypeStruct((rows, width), F32),
         compiler_params=limit(12),
+        cost_estimate=hint(5 * 10**9),
         name="caption_total",
     )(own_text, *got_text)
     image_loss = lax.dynamic_slice_in_dim(loss_line[0], first_image(member[0], rows, group), rows, 0)

time: 54.4 us -> 50.6 us (0.930)
  waiting for transfers between devices: 19.6 us -> 13.8 us
  starting transfers between devices: 19.6 us -> 22.9 us
  local copies, waits for them, and re-layouts: 4.12 us -> 2.98 us
    ppermute x14, waiting for transfers between devices: 12 us -> 4.06 us  [swapped(): lax.ppermute(value, AXES, [(source, source ^ mask) for source in range(to...]
    all_to_all x1, waiting for transfers between devices: 7.61 us -> 9.7 us  [local(): got_weight = lax.all_to_all(sent_weight, AXES[:2], 0, 0)]
    ppermute x14, starting transfers between devices: 16.2 us -> 18.2 us  [swapped(): lax.ppermute(value, AXES, [(source, source ^ mask) for source in range(to...]
    all_to_all x1, starting transfers between devices: 3.44 us -> 4.68 us  [local(): got_weight = lax.all_to_all(sent_weight, AXES[:2], 0, 0)]
    unnamed x6, local copies, waits for them, and re-layouts: 3.54 us -> 2.4 us
  transfers between devices with their start and end apart: 15 -> 15, of which waited for: 5 -> 5; matrix products, arithmetic and copies ran while one was open for 1% -> 1% of each run, Pallas kernels for 9% -> 10%
where the time goes in v10:
time: 50.6 us; the launch traced here: 50.3 us
  starting transfers between devices  22.9 us (45%)
  waiting for transfers between devices  13.8 us (27%)
  Pallas kernels  8.54 us (17%)
  local copies, waits for them, and re-layouts  2.98 us (6%)
  between operations  2.07 us (4%)
    ppermute x14, starting transfers between devices, swapped(): lax.ppermute(value, AXES, [(source, source ^ mask) for source in range(to...  18.2 us
    all_to_all x1, waiting for transfers between devices, local(): got_weight = lax.all_to_all(sent_weight, AXES[:2], 0, 0)  9.7 us
    all_to_all x1, starting transfers between devices, local(): got_weight = lax.all_to_all(sent_weight, AXES[:2], 0, 0)  4.68 us
    ppermute x14, waiting for transfers between devices, swapped(): lax.ppermute(value, AXES, [(source, source ^ mask) for source in range(to...  4.06 us
    pallas_call x1, Pallas kernels, local(): pl.pallas_call(functools.partial(pair_kernel, narrow, group), in_specs=[S...  2.74 us
    unnamed x6, local copies, waits for them, and re-layouts  2.4 us
    pallas_call x1, Pallas kernels, local(): pl.pallas_call(functools.partial(weight_kernel, group, wide), in_specs=[V...  1.73 us
    pallas_call x1, Pallas kernels, local(): pl.pallas_call(functools.partial(caption_kernel, rows), in_specs=[VMEM] *...  1.23 us
  transfers between devices with their start and end apart: 15, of which 5 were waited for; matrix products, arithmetic and copies ran while one was open for 1% of the time, Pallas kernels for 10%

profile of v10, /device:TPU:0, one launch (start us, length us, event | category | flops | bytes accessed | tf_op | source)
XLA Modules:
  0.0 50.3 jit_solution(14843504223511198900)
XLA Ops:
  0.6 3.0 %collective-permute-start = (bf16[48,1152]{1,0:T(8,128)(2,1)}, bf16[48,1152]{1,0:T(8,128)(2,1)S(1)}, u32[]{:S(2)}, u32[]{:S(2)}) collective-permute-start(bf16[48,1152]{1,0:T(8,128)(2,1)} %refs_0_.1), channel_id=1, source_target_pairs={{0,2},{1,3},{2,0},{3,1},{4,6},{5,7},{6,4},{7,5},{8,10},{9,11},{10,... | collective-permute-start | bytes 331784 | tf_op jit(solution)/shard_map/ppermute | solution.py:31
  3.7 1.5 %collective-permute-start.1 = (bf16[48,1152]{1,0:T(8,128)(2,1)}, bf16[48,1152]{1,0:T(8,128)(2,1)S(1)}, u32[]{:S(2)}, u32[]{:S(2)}) collective-permute-start(bf16[48,1152]{1,0:T(8,128)(2,1)} %refs_0_.1), channel_id=1, source_target_pairs={{0,4},{1,5},{2,6},{3,7},{4,0},{5,1},{6,2},{7,3},{8,12},{9,13},{10,... | collective-permute-start | bytes 331784 | tf_op jit(solution)/shard_map/ppermute | solution.py:31
  5.2 4.0 %collective-permute-start.3 = (bf16[48,1152]{1,0:T(8,128)(2,1)}, bf16[48,1152]{1,0:T(8,128)(2,1)S(1)}, u32[]{:S(2)}, u32[]{:S(2)}) collective-permute-start(bf16[48,1152]{1,0:T(8,128)(2,1)} %text_ref.1), channel_id=1, source_target_pairs={{0,24},{1,25},{2,26},{3,27},{4,28},{5,29},{6,30},{7,31},{8,16},{9,... | collective-permute-start | bytes 331784 | tf_op jit(solution)/shard_map/ppermute | solution.py:31
  10.6 0.6 %collective-permute-start.5 = (bf16[48,1152]{1,0:T(8,128)(2,1)}, bf16[48,1152]{1,0:T(8,128)(2,1)S(1)}, u32[]{:S(2)}, u32[]{:S(2)}) collective-permute-start(bf16[48,1152]{1,0:T(8,128)(2,1)} %text_ref.1), channel_id=1, source_target_pairs={{0,8},{1,9},{2,10},{3,11},{4,12},{5,13},{6,14},{7,15},{8,0},{9,1},... | collective-permute-start | bytes 331784 | tf_op jit(solution)/shard_map/ppermute | solution.py:31
  11.2 0.9 %copy-done.2 = bf16[48,1152]{1,0:T(8,128)(2,1)S(1)} copy-done((bf16[48,1152]{1,0:T(8,128)(2,1)S(1)}, bf16[48,1152]{1,0:T(8,128)(2,1)}, u32[]{:S(2)}) %copy-start.2) | copy-done | bytes 110616
  12.4 1.5 %copy-done = bf16[1152,1152]{1,0:T(8,128)(2,1)S(1)} copy-done((bf16[1152,1152]{1,0:T(8,128)(2,1)S(1)}, bf16[1152,1152]{1,0:T(8,128)(2,1)}, u32[]{:S(2)}) %copy-start) | copy-done | bytes 2654232
  13.9 0.8 %own_projection.1.own_proj = f32[192,1152]{1,0:T(8,128)S(1)} custom-call(bf16[192,1152]{1,0:T(8,128)(2,1)S(1)} %stack.1.feats_ref.own_half, bf16[1152,1152]{1,0:T(8,128)(2,1)S(1)} %copy-done), custom_call_target="tpu_custom_call" | custom-call | tf_op jit(solution)/shard_map/own_projection/pallas_call | solution.py:295
  14.7 3.3 %collective-permute-done.4.refs_2_ = bf16[48,1152]{1,0:T(8,128)(2,1)S(1)} collective-permute-done((bf16[48,1152]{1,0:T(8,128)(2,1)}, bf16[48,1152]{1,0:T(8,128)(2,1)S(1)}, u32[]{:S(2)}, u32[]{:S(2)}) %collective-permute-start.4) | collective-permute-done | bytes 110624 | tf_op jit(solution)/shard_map/ppermute | solution.py:31
  18.0 0.2 text_unit.1.text_all
  18.1 2.7 %pairs.1 = (bf16[384,1152]{1,0:T(8,128)(2,1)S(1)}, f32[144,384]{1,0:T(8,128)S(1)}, f32[1,384]{1,0:T(1,128)S(1)}, bf16[1152,384]{1,0:T(8,128)(2,1)S(1)}, bf16[192...) custom-call(s32[1]{0:T(128)} %bitcast.member_ref, ...), custom_call_target="tpu_custom_call" | custom-call | tf_op jit(solution)/shard_map/pairs/pallas_call | solution.py:314
  21.0 1.2 %captions.1 = (bf16[1152,384]{1,0:T(8,128)(2,1)S(1)}, f32[48,1152]{1,0:T(8,128)S(1)}, bf16[48,1152]{1,0:T(8,128)(2,1)S(1)}, bf16[48,1152]{1,0:T(8,128)(2,1)S(1)}, bf16[48,1152]{1,0:T(8,128)(2,1)S(1)}) custom-call(bf16[192,384]{1,0:T(8,128)(2,1)S(1)} %get-tuple-element.40.grad_ref, bf16[1152,384]{1,0:T(8,128)(2,1)S(1)} %get-tuple-element.41.emb_ref, ...), custom_call_target="tpu_custom_call" | custom-call | tf_op jit(solution)/shard_map/captions/pallas_call | solution.py:337
  22.2 0.6 %collective-permute-done.7.got_ref = bf16[4,160,384]{2,1,0:T(8,128)(2,1)S(1)} collective-permute-done((bf16[4,160,384]{2,1,0:T(8,128)(2,1)S(1)}, bf16[4,160,384]{2,1,0:T(8,128)(2,1)S(1)}, u32[]{:S(2)}, u32[]{:S(2)}) %collective-permute-start.7) | collective-permute-done | bytes 491552 | tf_op jit(solution)/shard_map/ppermute | solution.py:31
  22.9 2.5 %collective-permute-start.10 = (bf16[160,384]{1,0:T(8,128)(2,1)S(1)}, bf16[160,384]{1,0:T(8,128)(2,1)S(1)}, u32[]{:S(2)}, u32[]{:S(2)}) collective-permute-start(bf16[160,384]{1,0:T(8,128)(2,1)S(1)} %get-tuple-element.51), channel_id=1, source_target_pairs={{0,6},{1,7},{2,4},{3,5},{4,2},{5,3},{6,0},{7,1},{8,14},{9,15},{10,... | collective-permute-start | bytes 368648 | tf_op jit(solution)/shard_map/ppermute | solution.py:31
  25.4 0.5 %collective-permute-start.8 = (bf16[160,384]{1,0:T(8,128)(2,1)S(1)}, bf16[160,384]{1,0:T(8,128)(2,1)S(1)}, u32[]{:S(2)}, u32[]{:S(2)}) collective-permute-start(bf16[160,384]{1,0:T(8,128)(2,1)S(1)} %get-tuple-element.49), channel_id=1, source_target_pairs={{0,2},{1,3},{2,0},{3,1},{4,6},{5,7},{6,4},{7,5},{8,10},{9,11},{10,... | collective-permute-start | bytes 368648 | tf_op jit(solution)/shard_map/ppermute | solution.py:31
  25.9 0.5 %collective-permute-start.9 = (bf16[160,384]{1,0:T(8,128)(2,1)S(1)}, bf16[160,384]{1,0:T(8,128)(2,1)S(1)}, u32[]{:S(2)}, u32[]{:S(2)}) collective-permute-start(bf16[160,384]{1,0:T(8,128)(2,1)S(1)} %get-tuple-element.50), channel_id=1, source_target_pairs={{0,4},{1,5},{2,6},{3,7},{4,0},{5,1},{6,2},{7,3},{8,12},{9,13},{10,... | collective-permute-start | bytes 368648 | tf_op jit(solution)/shard_map/ppermute | solution.py:31
  26.5 0.2 collective-permute-start.11
  26.7 2.8 %collective-permute-start.12 = (bf16[48,1152]{1,0:T(8,128)(2,1)S(1)}, bf16[48,1152]{1,0:T(8,128)(2,1)S(1)}, u32[]{:S(2)}, u32[]{:S(2)}) collective-permute-start(bf16[48,1152]{1,0:T(8,128)(2,1)S(1)} %get-tuple-element.58), channel_id=1, source_target_pairs={{0,16},{1,17},{2,18},{3,19},{4,20},{5,21},{6,22},{7,23},{8,24},{9,... | collective-permute-start | bytes 331784 | tf_op jit(solution)/shard_map/ppermute | solution.py:31
  29.5 2.3 %collective-permute-start.13 = (bf16[48,1152]{1,0:T(8,128)(2,1)S(1)}, bf16[48,1152]{1,0:T(8,128)(2,1)S(1)}, u32[]{:S(2)}, u32[]{:S(2)}) collective-permute-start(bf16[48,1152]{1,0:T(8,128)(2,1)S(1)} %get-tuple-element.59), channel_id=1, source_target_pairs={{0,24},{1,25},{2,26},{3,27},{4,28},{5,29},{6,30},{7,31},{8,16},{9,... | collective-permute-start | bytes 331784 | tf_op jit(solution)/shard_map/ppermute | solution.py:31
  32.0 1.7 %weights.1 = (f32[1,384]{1,0:T(1,128)S(1)}, bf16[8,176,128]{2,1,0:T(8,128)(2,1)}) custom-call(f32[152,384]{1,0:T(8,128)S(1)} %get-tuple-element.48.refs_0_, bf16[160,384]{1,0:T(8,128)(2,1)S(1)} %collective-permute-done.8.refs_1_, bf16[160,384]{1,0:T(8,128)(2,1)S(1)} %collective-permute-done.9.refs_2_, bf16[160,384]{1,0:T(8,128)(2,1)S(1)} %collective-permute-done.10.refs_3_, ...), custom_call_target="tpu_custom_call" | custom-call | tf_op jit(solution)/shard_map/weights/pallas_call | solution.py:364
  33.7 4.7 %all-to-all-start = ((bf16[8,176,128]{2,1,0:T(8,128)(2,1)}), bf16[8,176,128]{2,1,0:T(8,128)(2,1)S(1)}, u32[]{:S(2)}, u32[]{:S(2)}) async-start(bf16[8,176,128]{2,1,0:T(8,128)(2,1)} %get-tuple-element.60), calls=%async_computation | async-start | bytes 720896 | tf_op jit(solution)/shard_map/all_to_all | solution.py:375
  38.4 0.7 %caption_total.1 = f32[48,1152]{1,0:T(8,128)} custom-call(f32[48,1152]{1,0:T(8,128)S(1)} %get-tuple-element.56.refs_0_, bf16[48,1152]{1,0:T(8,128)(2,1)S(1)} %collective-permute-done.11.refs_1_, bf16[48,1152]{1,0:T(8,128)(2,1)S(1)} %collective-permute-done.12.refs_2_, bf16[48,1152]{1,0:T(8,128)(2,1)S(1)} %collective-permute-done.13.refs_3_), custom_call_target="tpu_custom_call" | custom-call | flops 5000000000 | tf_op jit(solution)/shard_map/caption_total/pallas_call | solution.py:406
  39.1 0.6 %dynamic-slice_bitcast_fusion = f32[48]{0:T(128)} fusion(f32[1,384]{1,0:T(1,128)S(1)} %get-tuple-element.55, s32[]{:T(128)S(6)} %select_n.16), kind=kLoop, calls=%fused_computation | loop fusion | bytes 388 | tf_op jit(solution)/shard_map/dynamic_slice | solution.py:415
  39.7 9.7 %all-to-all-done.got_ref = bf16[8,176,128]{2,1,0:T(8,128)(2,1)S(1)} async-done(((bf16[8,176,128]{2,1,0:T(8,128)(2,1)}), bf16[8,176,128]{2,1,0:T(8,128)(2,1)S(1)}, u32[]{:S(2)}, u32[]{:S(2)}) %all-to-all-start) | async-done | bytes 360480 | tf_op jit(solution)/shard_map/all_to_all | solution.py:375
  49.4 0.9 %weight_total.1 = f32[144,288]{1,0:T(8,128)} custom-call(bf16[8,176,128]{2,1,0:T(8,128)(2,1)S(1)} %all-to-all-done.got_ref), custom_call_target="tpu_custom_call" | custom-call | tf_op jit(solution)/shard_map/weight_total/pallas_call | solution.py:376
  (23 shorter events, 0.7 us)
Async XLA Ops:
  0.6 9.9 %collective-permute-start = (bf16[48,1152]{1,0:T(8,128)(2,1)}, bf16[48,1152]{1,0:T(8,128)(2,1)S(1)}, u32[]{:S(2)}, u32[]{:S(2)}) collective-permute-start(bf16[48,1152]{1,0:T(8,128)(2,1)} %refs_0_.1), channel_id=1, source_target_pairs={{0,2},{1,3},{2,0},{3,1},{4,6},{5,7},{6,4},{7,5},{8,10},{9,11},{10,... | collective-permute-start | bytes 331784 | tf_op jit(solution)/shard_map/ppermute | solution.py:31
  3.7 8.6 %collective-permute-start.1 = (bf16[48,1152]{1,0:T(8,128)(2,1)}, bf16[48,1152]{1,0:T(8,128)(2,1)S(1)}, u32[]{:S(2)}, u32[]{:S(2)}) collective-permute-start(bf16[48,1152]{1,0:T(8,128)(2,1)} %refs_0_.1), channel_id=1, source_target_pairs={{0,4},{1,5},{2,6},{3,7},{4,0},{5,1},{6,2},{7,3},{8,12},{9,13},{10,... | collective-permute-start | bytes 331784 | tf_op jit(solution)/shard_map/ppermute | solution.py:31
  5.2 7.1 %collective-permute-start.2 = (bf16[48,1152]{1,0:T(8,128)(2,1)}, bf16[48,1152]{1,0:T(8,128)(2,1)S(1)}, u32[]{:S(2)}, u32[]{:S(2)}) collective-permute-start(bf16[48,1152]{1,0:T(8,128)(2,1)} %refs_0_.1), channel_id=1, source_target_pairs={{0,6},{1,7},{2,4},{3,5},{4,2},{5,3},{6,0},{7,1},{8,14},{9,15},{10,... | collective-permute-start | bytes 331784 | tf_op jit(solution)/shard_map/ppermute | solution.py:31
  5.2 9.5 %collective-permute-start.3 = (bf16[48,1152]{1,0:T(8,128)(2,1)}, bf16[48,1152]{1,0:T(8,128)(2,1)S(1)}, u32[]{:S(2)}, u32[]{:S(2)}) collective-permute-start(bf16[48,1152]{1,0:T(8,128)(2,1)} %text_ref.1), channel_id=1, source_target_pairs={{0,24},{1,25},{2,26},{3,27},{4,28},{5,29},{6,30},{7,31},{8,16},{9,... | collective-permute-start | bytes 331784 | tf_op jit(solution)/shard_map/ppermute | solution.py:31
  9.2 8.7 %collective-permute-start.4 = (bf16[48,1152]{1,0:T(8,128)(2,1)}, bf16[48,1152]{1,0:T(8,128)(2,1)S(1)}, u32[]{:S(2)}, u32[]{:S(2)}) collective-permute-start(bf16[48,1152]{1,0:T(8,128)(2,1)} %text_ref.1), channel_id=1, source_target_pairs={{0,16},{1,17},{2,18},{3,19},{4,20},{5,21},{6,22},{7,23},{8,24},{9,... | collective-permute-start | bytes 331784 | tf_op jit(solution)/shard_map/ppermute | solution.py:31
  10.5 1.7 %copy-start.1 = (bf16[48,1152]{1,0:T(8,128)(2,1)S(1)}, bf16[48,1152]{1,0:T(8,128)(2,1)}, u32[]{:S(2)}) copy-start(bf16[48,1152]{1,0:T(8,128)(2,1)} %refs_0_.1) | copy-start | bytes 331780
  10.6 7.4 %collective-permute-start.5 = (bf16[48,1152]{1,0:T(8,128)(2,1)}, bf16[48,1152]{1,0:T(8,128)(2,1)S(1)}, u32[]{:S(2)}, u32[]{:S(2)}) collective-permute-start(bf16[48,1152]{1,0:T(8,128)(2,1)} %text_ref.1), channel_id=1, source_target_pairs={{0,8},{1,9},{2,10},{3,11},{4,12},{5,13},{6,14},{7,15},{8,0},{9,1},... | collective-permute-start | bytes 331784 | tf_op jit(solution)/shard_map/ppermute | solution.py:31
  11.2 0.9 %copy-start.2 = (bf16[48,1152]{1,0:T(8,128)(2,1)S(1)}, bf16[48,1152]{1,0:T(8,128)(2,1)}, u32[]{:S(2)}) copy-start(bf16[48,1152]{1,0:T(8,128)(2,1)} %text_ref.1) | copy-start | bytes 331780
  12.1 1.7 %copy-start = (bf16[1152,1152]{1,0:T(8,128)(2,1)S(1)}, bf16[1152,1152]{1,0:T(8,128)(2,1)}, u32[]{:S(2)}) copy-start(bf16[1152,1152]{1,0:T(8,128)(2,1)} %weight.1) | copy-start | bytes 7962628
  12.3 5.8 %collective-permute-start.6 = (bf16[192,1152]{1,0:T(8,128)(2,1)S(1)}, bf16[192,1152]{1,0:T(8,128)(2,1)S(1)}, u32[]{:S(2)}, u32[]{:S(2)}) collective-permute-start(bf16[192,1152]{1,0:T(8,128)(2,1)S(1)} %stack.1.feats_ref.own_half), channel_id=1, source_target_pairs={{0,1},{1,0},{2,3},{3,2},{4,5},{5,4},{6,7},{7,6},{8,9},{9,8},{10,11... | collective-permute-start | bytes 1327112 | tf_op jit(solution)/shard_map/ppermute | solution.py:31
  20.9 1.9 %collective-permute-start.7 = (bf16[4,160,384]{2,1,0:T(8,128)(2,1)S(1)}, bf16[4,160,384]{2,1,0:T(8,128)(2,1)S(1)}, u32[]{:S(2)}, u32[]{:S(2)}) collective-permute-start(bf16[4,160,384]{2,1,0:T(8,128)(2,1)S(1)} %get-tuple-element.39), channel_id=1, source_target_pairs={{0,1},{1,0},{2,3},{3,2},{4,5},{5,4},{6,7},{7,6},{8,9},{9,8},{10,11... | collective-permute-start | bytes 1474568 | tf_op jit(solution)/shard_map/ppermute | solution.py:31
  22.9 6.6 %collective-permute-start.10 = (bf16[160,384]{1,0:T(8,128)(2,1)S(1)}, bf16[160,384]{1,0:T(8,128)(2,1)S(1)}, u32[]{:S(2)}, u32[]{:S(2)}) collective-permute-start(bf16[160,384]{1,0:T(8,128)(2,1)S(1)} %get-tuple-element.51), channel_id=1, source_target_pairs={{0,6},{1,7},{2,4},{3,5},{4,2},{5,3},{6,0},{7,1},{8,14},{9,15},{10,... | collective-permute-start | bytes 368648 | tf_op jit(solution)/shard_map/ppermute | solution.py:31
  25.4 6.5 %collective-permute-start.8 = (bf16[160,384]{1,0:T(8,128)(2,1)S(1)}, bf16[160,384]{1,0:T(8,128)(2,1)S(1)}, u32[]{:S(2)}, u32[]{:S(2)}) collective-permute-start(bf16[160,384]{1,0:T(8,128)(2,1)S(1)} %get-tuple-element.49), channel_id=1, source_target_pairs={{0,2},{1,3},{2,0},{3,1},{4,6},{5,7},{6,4},{7,5},{8,10},{9,11},{10,... | collective-permute-start | bytes 368648 | tf_op jit(solution)/shard_map/ppermute | solution.py:31
  25.9 6.0 %collective-permute-start.9 = (bf16[160,384]{1,0:T(8,128)(2,1)S(1)}, bf16[160,384]{1,0:T(8,128)(2,1)S(1)}, u32[]{:S(2)}, u32[]{:S(2)}) collective-permute-start(bf16[160,384]{1,0:T(8,128)(2,1)S(1)} %get-tuple-element.50), channel_id=1, source_target_pairs={{0,4},{1,5},{2,6},{3,7},{4,0},{5,1},{6,2},{7,3},{8,12},{9,13},{10,... | collective-permute-start | bytes 368648 | tf_op jit(solution)/shard_map/ppermute | solution.py:31
  26.5 11.9 %collective-permute-start.11 = (bf16[48,1152]{1,0:T(8,128)(2,1)S(1)}, bf16[48,1152]{1,0:T(8,128)(2,1)S(1)}, u32[]{:S(2)}, u32[]{:S(2)}) collective-permute-start(bf16[48,1152]{1,0:T(8,128)(2,1)S(1)} %get-tuple-element.57), channel_id=1, source_target_pairs={{0,8},{1,9},{2,10},{3,11},{4,12},{5,13},{6,14},{7,15},{8,0},{9,1},... | collective-permute-start | bytes 331784 | tf_op jit(solution)/shard_map/ppermute | solution.py:31
  26.7 11.7 %collective-permute-start.12 = (bf16[48,1152]{1,0:T(8,128)(2,1)S(1)}, bf16[48,1152]{1,0:T(8,128)(2,1)S(1)}, u32[]{:S(2)}, u32[]{:S(2)}) collective-permute-start(bf16[48,1152]{1,0:T(8,128)(2,1)S(1)} %get-tuple-element.58), channel_id=1, source_target_pairs={{0,16},{1,17},{2,18},{3,19},{4,20},{5,21},{6,22},{7,23},{8,24},{9,... | collective-permute-start | bytes 331784 | tf_op jit(solution)/shard_map/ppermute | solution.py:31
  29.5 8.9 %collective-permute-start.13 = (bf16[48,1152]{1,0:T(8,128)(2,1)S(1)}, bf16[48,1152]{1,0:T(8,128)(2,1)S(1)}, u32[]{:S(2)}, u32[]{:S(2)}) collective-permute-start(bf16[48,1152]{1,0:T(8,128)(2,1)S(1)} %get-tuple-element.59), channel_id=1, source_target_pairs={{0,24},{1,25},{2,26},{3,27},{4,28},{5,29},{6,30},{7,31},{8,16},{9,... | collective-permute-start | bytes 331784 | tf_op jit(solution)/shard_map/ppermute | solution.py:31
  33.7 15.7 %all-to-all-start = ((bf16[8,176,128]{2,1,0:T(8,128)(2,1)}), bf16[8,176,128]{2,1,0:T(8,128)(2,1)S(1)}, u32[]{:S(2)}, u32[]{:S(2)}) async-start(bf16[8,176,128]{2,1,0:T(8,128)(2,1)} %get-tuple-element.60), calls=%async_computation | async-start | bytes 720896 | tf_op jit(solution)/shard_map/all_to_all | solution.py:375

commit v11 on v10

--- a/solution.py
+++ b/solution.py
@@ -222,34 +222,44 @@
 
 
 def weight_kernel(group, wide, *refs):
-    own_ref = refs[0]
-    got = refs[1 : group // 2]
-    unit_ref, inv_ref, feats_ref, feats_t_ref, loss_out, send_out = refs[group // 2 :]
+    wide_ref, own_ref = refs[:2]
+    got = refs[2 : 1 + group // 2]
+    unit_ref, inv_ref, feats_ref, feats_t_ref, loss_out, own_out = refs[1 + group // 2 : 7 + group // 2]
+    send_out = refs[7 + group // 2 : 6 + group // 2 + wide]
+    main_all, rest_all = refs[6 + group // 2 + wide :]
     share = unit_ref.shape[0]
     rest = share - LANES
     rows = feats_t_ref.shape[0] // wide
     high, low = split_pair(gathered_gradient(own_ref, got, unit_ref, inv_ref, loss_out))
-    main = lax.dot_general(
-        feats_t_ref[...], high[:LANES, :], NT, preferred_element_type=F32
-    ) + lax.dot_general(feats_t_ref[...], low[:LANES, :], NT, preferred_element_type=F32)
-    tail = jnp.dot(high[LANES:, :], feats_ref[...], preferred_element_type=F32) + jnp.dot(
-        low[LANES:, :], feats_ref[...], preferred_element_type=F32
-    )
-    main, tail = main.astype(BF16), tail.astype(BF16)
+    both = jnp.concatenate([high[:LANES, :], low[:LANES, :]], axis=0)
+    main = lax.dot_general(feats_t_ref[...], both, NT, preferred_element_type=F32)
+    main_all[...] = main[:, :LANES] + main[:, LANES:]
+    both = jnp.concatenate([high[LANES:, :], low[LANES:, :]], axis=0)
+    tail = jnp.dot(both, feats_ref[...], preferred_element_type=F32)
+    tail = tail[:rest, :] + tail[rest:, :]
     for place in range(wide):
         begin = place * rows
-        send_out[place, :rows, :] = main[begin : begin + rows, :]
-        send_out[place, rows : rows + rest, :] = tail[:, begin : begin + LANES]
-        send_out[place, rows + rest :, :] = jnp.zeros((rest, LANES), BF16)
-        send_out[place, rows + rest :, : rows - LANES] = tail[:, begin + LANES : begin + rows]
-
-
-def total_kernel(rest, got_ref, out):
+        rest_all[place, :rest, :] = tail[:, begin : begin + LANES]
+        rest_all[place, rest:, :] = jnp.zeros((rest, LANES), F32)
+        rest_all[place, rest:, : rows - LANES] = tail[:, begin + LANES : begin + rows]
+    for step in range(wide):
+        place = wide_ref[0] ^ step
+        target = own_out if step == 0 else send_out[step - 1]
+        target[:rows, :] = main_all[pl.ds(pl.multiple_of(place * rows, rows), rows), :].astype(target.dtype)
+        target[rows:, :] = rest_all[place].astype(target.dtype)
+
+
+def total_kernel(rest, wide_ref, *refs):
+    blocks, out = refs[:-1], refs[-1]
     rows = out.shape[0]
-    for side in range(2):
-        half = got_ref[side].astype(F32)
-        for place in range(side + 2, got_ref.shape[0], 2):
-            half = half + got_ref[place].astype(F32)
+    same, other = blocks[0][...], blocks[1][...].astype(F32)
+    for block in blocks[2::2]:
+        same = same + block[...].astype(F32)
+    for block in blocks[3::2]:
+        other = other + block[...].astype(F32)
+    left_is_same = wide_ref[0] % 2 == 0
+    halves = (jnp.where(left_is_same, same, other), jnp.where(left_is_same, other, same))
+    for side, half in enumerate(halves):
         left = side * (LANES + rest)
         out[:, left : left + LANES] = half[:rows, :]
         out[:LANES, left + LANES : left + LANES + rest] = half[rows : rows + rest, :].T
@@ -361,26 +371,27 @@
     packed = out_rows + 2 * rest
     direct = LANES < out_rows <= 2 * LANES and out_rows % 16 == 0 and rest % 16 == 0
     if direct:
-        loss_line, sent_weight = pl.pallas_call(
+        wide_pos = lax.axis_index(AXES[:2]).astype(jnp.int32).reshape(1)
+        loss_line, own_weight, *sent_weight = pl.pallas_call(
             functools.partial(weight_kernel, group, wide),
-            in_specs=[VMEM] * (4 + group // 2),
-            out_specs=[VMEM] * 2,
-            out_shape=[
-                jax.ShapeDtypeStruct((1, images), F32),
-                jax.ShapeDtypeStruct((wide, packed, LANES), BF16),
-            ],
+            in_specs=[SMEM] + [VMEM] * (4 + group // 2),
+            out_specs=[VMEM] * (1 + wide),
+            out_shape=[jax.ShapeDtypeStruct((1, images), F32), jax.ShapeDtypeStruct((packed, LANES), F32)]
+            + [jax.ShapeDtypeStruct((packed, LANES), BF16)] * (wide - 1),
+            scratch_shapes=[pltpu.VMEM((width, LANES), F32), pltpu.VMEM((wide, 2 * rest, LANES), F32)],
             compiler_params=limit(12),
             name="weights",
-        )(own_part, *got, unit_part, inv_part, all_feats, feats_t)
-        got_weight = lax.all_to_all(sent_weight, AXES[:2], 0, 0)
+        )(wide_pos, own_part, *got, unit_part, inv_part, all_feats, feats_t)
+        got_weight = [swapped(value, total, step * narrow) for step, value in enumerate(sent_weight, 1)]
+        got_weight = lax.optimization_barrier(got_weight[::-1])[::-1]
         d_proj = pl.pallas_call(
             functools.partial(total_kernel, rest),
-            in_specs=[VMEM],
+            in_specs=[SMEM] + [VMEM] * wide,
             out_specs=VMEM,
             out_shape=jax.ShapeDtypeStruct((out_rows, 2 * share), F32),
             compiler_params=limit(4),
             name="weight_total",
-        )(got_weight)
+        )(wide_pos, own_weight, *got_weight)
     else:
 
         def gradient_kernel(*refs):
@@ -411,7 +422,7 @@
         compiler_params=limit(12),
         cost_estimate=hint(5 * 10**9),
         name="caption_total",
-    )(own_text, *got_text)
+    )(own_text, *got_text[::-1])
     image_loss = lax.dynamic_slice_in_dim(loss_line[0], first_image(member[0], rows, group), rows, 0)
     return (image_loss, d_text_unit, d_proj)
 

time: 50.6 us -> 50.8 us (level)
  starting transfers between devices: 22.9 us -> 29.5 us
  waiting for transfers between devices: 13.8 us -> 7.58 us
  Pallas kernels: 8.54 us -> 7.55 us
  local copies, waits for them, and re-layouts: 2.98 us -> 3.92 us
    ppermute x14 -> x21, starting transfers between devices: 18.2 us -> 29.5 us  [swapped(): lax.ppermute(value, AXES, [(source, source ^ mask) for source in range(to...]
    all_to_all x1 -> x0, waiting for transfers between devices: 9.7 us -> none  [local(): got_weight = lax.all_to_all(sent_weight, AXES[:2], 0, 0)]
    all_to_all x1 -> x0, starting transfers between devices: 4.68 us -> none  [local(): got_weight = lax.all_to_all(sent_weight, AXES[:2], 0, 0)]
    ppermute x14 -> x21, waiting for transfers between devices: 4.06 us -> 7.58 us  [swapped(): lax.ppermute(value, AXES, [(source, source ^ mask) for source in range(to...]
    pallas_call x2, Pallas kernels: 2.59 us -> 1.59 us  [the longest x1 0.87 us: local(): pl.pallas_call(functools.partial(total_kernel, rest), in_specs=[SMEM] + [...]
    unnamed x6 -> x10, local copies, waits for them, and re-layouts: 2.4 us -> 3.34 us
  transfers between devices with their start and end apart: 15 -> 21, of which waited for: 5 -> 6; matrix products, arithmetic and copies ran while one was open for 1% -> 1% of each run, Pallas kernels for 10% -> 8%
where the time goes in v11:
time: 50.8 us; the launch traced here: 50.6 us
  starting transfers between devices  29.5 us (58%)
  waiting for transfers between devices  7.58 us (15%)
  Pallas kernels  7.55 us (15%)
  local copies, waits for them, and re-layouts  3.92 us (8%)
  between operations  2.09 us (4%)
    ppermute x21, starting transfers between devices, swapped(): lax.ppermute(value, AXES, [(source, source ^ mask) for source in range(to...  29.5 us
    ppermute x21, waiting for transfers between devices, swapped(): lax.ppermute(value, AXES, [(source, source ^ mask) for source in range(to...  7.58 us
    unnamed x10, local copies, waits for them, and re-layouts  3.34 us
    pallas_call x1, Pallas kernels, local(): pl.pallas_call(functools.partial(pair_kernel, narrow, group), in_specs=[S...  2.74 us
    pallas_call x1, Pallas kernels, local(): pl.pallas_call(functools.partial(caption_kernel, rows), in_specs=[VMEM] *...  1.23 us
  transfers between devices with their start and end apart: 21, of which 6 were waited for; matrix products, arithmetic and copies ran while one was open for 1% of the time, Pallas kernels for 8%

profile of v11, /device:TPU:0, one launch (start us, length us, event | category | flops | bytes accessed | tf_op | source)
XLA Modules:
  0.0 50.6 jit_solution(16179494228356000016)
XLA Ops:
  0.6 3.0 %collective-permute-start = (bf16[48,1152]{1,0:T(8,128)(2,1)}, bf16[48,1152]{1,0:T(8,128)(2,1)S(1)}, u32[]{:S(2)}, u32[]{:S(2)}) collective-permute-start(bf16[48,1152]{1,0:T(8,128)(2,1)} %refs_0_.1), channel_id=1, source_target_pairs={{0,2},{1,3},{2,0},{3,1},{4,6},{5,7},{6,4},{7,5},{8,10},{9,11},{10,... | collective-permute-start | bytes 331784 | tf_op jit(solution)/shard_map/ppermute | solution.py:31
  3.7 1.5 %collective-permute-start.1 = (bf16[48,1152]{1,0:T(8,128)(2,1)}, bf16[48,1152]{1,0:T(8,128)(2,1)S(1)}, u32[]{:S(2)}, u32[]{:S(2)}) collective-permute-start(bf16[48,1152]{1,0:T(8,128)(2,1)} %refs_0_.1), channel_id=1, source_target_pairs={{0,4},{1,5},{2,6},{3,7},{4,0},{5,1},{6,2},{7,3},{8,12},{9,13},{10,... | collective-permute-start | bytes 331784 | tf_op jit(solution)/shard_map/ppermute | solution.py:31
  5.2 4.0 %collective-permute-start.3 = (bf16[48,1152]{1,0:T(8,128)(2,1)}, bf16[48,1152]{1,0:T(8,128)(2,1)S(1)}, u32[]{:S(2)}, u32[]{:S(2)}) collective-permute-start(bf16[48,1152]{1,0:T(8,128)(2,1)} %text_ref.1), channel_id=1, source_target_pairs={{0,24},{1,25},{2,26},{3,27},{4,28},{5,29},{6,30},{7,31},{8,16},{9,... | collective-permute-start | bytes 331784 | tf_op jit(solution)/shard_map/ppermute | solution.py:31
  11.2 0.9 %copy-done.4 = bf16[48,1152]{1,0:T(8,128)(2,1)S(1)} copy-done((bf16[48,1152]{1,0:T(8,128)(2,1)S(1)}, bf16[48,1152]{1,0:T(8,128)(2,1)}, u32[]{:S(2)}) %copy-start.4) | copy-done | bytes 110616
  12.4 1.5 %copy-done = bf16[1152,1152]{1,0:T(8,128)(2,1)S(1)} copy-done((bf16[1152,1152]{1,0:T(8,128)(2,1)S(1)}, bf16[1152,1152]{1,0:T(8,128)(2,1)}, u32[]{:S(2)}) %copy-start) | copy-done | bytes 2654232
  13.9 0.8 %own_projection.1.own_proj = f32[192,1152]{1,0:T(8,128)S(1)} custom-call(bf16[192,1152]{1,0:T(8,128)(2,1)S(1)} %stack.1.feats_ref.own_half, bf16[1152,1152]{1,0:T(8,128)(2,1)S(1)} %copy-done), custom_call_target="tpu_custom_call" | custom-call | tf_op jit(solution)/shard_map/own_projection/pallas_call | solution.py:305
  14.7 3.3 %collective-permute-done.4.refs_2_ = bf16[48,1152]{1,0:T(8,128)(2,1)S(1)} collective-permute-done((bf16[48,1152]{1,0:T(8,128)(2,1)}, bf16[48,1152]{1,0:T(8,128)(2,1)S(1)}, u32[]{:S(2)}, u32[]{:S(2)}) %collective-permute-start.4) | collective-permute-done | bytes 110624 | tf_op jit(solution)/shard_map/ppermute | solution.py:31
  18.1 2.7 %pairs.1 = (bf16[384,1152]{1,0:T(8,128)(2,1)S(1)}, f32[144,384]{1,0:T(8,128)S(1)}, f32[1,384]{1,0:T(1,128)S(1)}, bf16[1152,384]{1,0:T(8,128)(2,1)S(1)}, bf16[192...) custom-call(s32[1]{0:T(128)} %bitcast.1.member_ref, ...), custom_call_target="tpu_custom_call" | custom-call | tf_op jit(solution)/shard_map/pairs/pallas_call | solution.py:324
  21.0 1.2 %captions.1 = (bf16[1152,384]{1,0:T(8,128)(2,1)S(1)}, f32[48,1152]{1,0:T(8,128)S(1)}, bf16[48,1152]{1,0:T(8,128)(2,1)S(1)}, bf16[48,1152]{1,0:T(8,128)(2,1)S(1)}, bf16[48,1152]{1,0:T(8,128)(2,1)S(1)}) custom-call(bf16[192,384]{1,0:T(8,128)(2,1)S(1)} %get-tuple-element.54.grad_ref, bf16[1152,384]{1,0:T(8,128)(2,1)S(1)} %get-tuple-element.55.emb_ref, ...), custom_call_target="tpu_custom_call" | custom-call | tf_op jit(solution)/shard_map/captions/pallas_call | solution.py:347
  22.9 1.6 %collective-permute-start.8 = (bf16[160,384]{1,0:T(8,128)(2,1)S(1)}, bf16[160,384]{1,0:T(8,128)(2,1)S(1)}, u32[]{:S(2)}, u32[]{:S(2)}) collective-permute-start(bf16[160,384]{1,0:T(8,128)(2,1)S(1)} %get-tuple-element.63), channel_id=1, source_target_pairs={{0,2},{1,3},{2,0},{3,1},{4,6},{5,7},{6,4},{7,5},{8,10},{9,11},{10,... | collective-permute-start | bytes 368648 | tf_op jit(solution)/shard_map/ppermute | solution.py:31
  24.5 1.5 %collective-permute-start.9 = (bf16[160,384]{1,0:T(8,128)(2,1)S(1)}, bf16[160,384]{1,0:T(8,128)(2,1)S(1)}, u32[]{:S(2)}, u32[]{:S(2)}) collective-permute-start(bf16[160,384]{1,0:T(8,128)(2,1)S(1)} %get-tuple-element.64), channel_id=1, source_target_pairs={{0,4},{1,5},{2,6},{3,7},{4,0},{5,1},{6,2},{7,3},{8,12},{9,13},{10,... | collective-permute-start | bytes 368648 | tf_op jit(solution)/shard_map/ppermute | solution.py:31
  26.5 2.4 %collective-permute-start.11 = (bf16[48,1152]{1,0:T(8,128)(2,1)S(1)}, bf16[48,1152]{1,0:T(8,128)(2,1)S(1)}, u32[]{:S(2)}, u32[]{:S(2)}) collective-permute-start(bf16[48,1152]{1,0:T(8,128)(2,1)S(1)} %get-tuple-element.71), channel_id=1, source_target_pairs={{0,24},{1,25},{2,26},{3,27},{4,28},{5,29},{6,30},{7,31},{8,16},{9,... | collective-permute-start | bytes 331784 | tf_op jit(solution)/shard_map/ppermute | solution.py:31
  29.0 1.9 %collective-permute-start.13 = (bf16[48,1152]{1,0:T(8,128)(2,1)S(1)}, bf16[48,1152]{1,0:T(8,128)(2,1)S(1)}, u32[]{:S(2)}, u32[]{:S(2)}) collective-permute-start(bf16[48,1152]{1,0:T(8,128)(2,1)S(1)} %get-tuple-element.73), channel_id=1, source_target_pairs={{0,8},{1,9},{2,10},{3,11},{4,12},{5,13},{6,14},{7,15},{8,0},{9,1},... | collective-permute-start | bytes 331784 | tf_op jit(solution)/shard_map/ppermute | solution.py:31
  30.9 1.3 %collective-permute-done.10.refs_4_ = bf16[160,384]{1,0:T(8,128)(2,1)S(1)} collective-permute-done((bf16[160,384]{1,0:T(8,128)(2,1)S(1)}, bf16[160,384]{1,0:T(8,128)(2,1)S(1)}, u32[]{:S(2)}, u32[]{:S(2)}) %collective-permute-start.10) | collective-permute-done | bytes 122912 | tf_op jit(solution)/shard_map/ppermute | solution.py:31
  32.2 0.9 %copy-done.2 = f32[144,384]{1,0:T(8,128)S(1)} copy-done((f32[144,384]{1,0:T(8,128)S(1)}, f32[144,384]{1,0:T(8,128)}, u32[]{:S(2)}) %copy-start.2) | copy-done | bytes 221208
  33.9 3.4 %collective-permute-start.14 = (bf16[176,128]{1,0:T(8,128)(2,1)S(1)}, bf16[176,128]{1,0:T(8,128)(2,1)S(1)}, u32[]{:S(2)}, u32[]{:S(2)}) collective-permute-start(bf16[176,128]{1,0:T(8,128)(2,1)S(1)} %get-tuple-element.75), channel_id=1, source_target_pairs={{0,28},{1,29},{2,30},{3,31},{4,24},{5,25},{6,26},{7,27},{8,20},{9,... | collective-permute-start | bytes 135176 | tf_op jit(solution)/shard_map/ppermute | solution.py:31
  37.3 1.4 %collective-permute-start.15 = (bf16[176,128]{1,0:T(8,128)(2,1)S(1)}, bf16[176,128]{1,0:T(8,128)(2,1)S(1)}, u32[]{:S(2)}, u32[]{:S(2)}) collective-permute-start(bf16[176,128]{1,0:T(8,128)(2,1)S(1)} %get-tuple-element.76), channel_id=1, source_target_pairs={{0,24},{1,25},{2,26},{3,27},{4,28},{5,29},{6,30},{7,31},{8,16},{9,... | collective-permute-start | bytes 135176 | tf_op jit(solution)/shard_map/ppermute | solution.py:31
  39.1 0.7 %caption_total.1 = f32[48,1152]{1,0:T(8,128)} custom-call(f32[48,1152]{1,0:T(8,128)S(1)} %get-tuple-element.70.refs_0_, bf16[48,1152]{1,0:T(8,128)(2,1)S(1)} %collective-permute-done.11.refs_1_, bf16[48,1152]{1,0:T(8,128)(2,1)S(1)} %collective-permute-done.12.refs_2_, bf16[48,1152]{1,0:T(8,128)(2,1)S(1)} %collective-permute-done.13.refs_3_), custom_call_target="tpu_custom_call" | custom-call | flops 5000000000 | tf_op jit(solution)/shard_map/caption_total/pallas_call | solution.py:417
  40.3 3.4 %collective-permute-start.17 = (bf16[176,128]{1,0:T(8,128)(2,1)S(1)}, bf16[176,128]{1,0:T(8,128)(2,1)S(1)}, u32[]{:S(2)}, u32[]{:S(2)}) collective-permute-start(bf16[176,128]{1,0:T(8,128)(2,1)S(1)} %get-tuple-element.78), channel_id=1, source_target_pairs={{0,16},{1,17},{2,18},{3,19},{4,20},{5,21},{6,22},{7,23},{8,24},{9,... | collective-permute-start | bytes 135176 | tf_op jit(solution)/shard_map/ppermute | solution.py:31
  43.7 2.0 %collective-permute-start.19 = (bf16[176,128]{1,0:T(8,128)(2,1)S(1)}, bf16[176,128]{1,0:T(8,128)(2,1)S(1)}, u32[]{:S(2)}, u32[]{:S(2)}) collective-permute-start(bf16[176,128]{1,0:T(8,128)(2,1)S(1)} %get-tuple-element.80), channel_id=1, source_target_pairs={{0,8},{1,9},{2,10},{3,11},{4,12},{5,13},{6,14},{7,15},{8,0},{9,1},... | collective-permute-start | bytes 135176 | tf_op jit(solution)/shard_map/ppermute | solution.py:31
  45.7 1.5 %collective-permute-start.20 = (bf16[176,128]{1,0:T(8,128)(2,1)S(1)}, bf16[176,128]{1,0:T(8,128)(2,1)S(1)}, u32[]{:S(2)}, u32[]{:S(2)}) collective-permute-start(bf16[176,128]{1,0:T(8,128)(2,1)S(1)} %get-tuple-element.81), channel_id=1, source_target_pairs={{0,4},{1,5},{2,6},{3,7},{4,0},{5,1},{6,2},{7,3},{8,12},{9,13},{10,... | collective-permute-start | bytes 135176 | tf_op jit(solution)/shard_map/ppermute | solution.py:31
  47.8 0.9 %collective-permute-done.18.refs_3_ = bf16[176,128]{1,0:T(8,128)(2,1)S(1)} collective-permute-done((bf16[176,128]{1,0:T(8,128)(2,1)S(1)}, bf16[176,128]{1,0:T(8,128)(2,1)S(1)}, u32[]{:S(2)}, u32[]{:S(2)}) %collective-permute-start.18) | collective-permute-done | bytes 45088 | tf_op jit(solution)/shard_map/ppermute | solution.py:31
  48.6 1.1 %collective-permute-done.20.refs_1_ = bf16[176,128]{1,0:T(8,128)(2,1)S(1)} collective-permute-done((bf16[176,128]{1,0:T(8,128)(2,1)S(1)}, bf16[176,128]{1,0:T(8,128)(2,1)S(1)}, u32[]{:S(2)}, u32[]{:S(2)}) %collective-permute-start.20) | collective-permute-done | bytes 45088 | tf_op jit(solution)/shard_map/ppermute | solution.py:31
  49.7 0.9 %weight_total.1 = f32[144,288]{1,0:T(8,128)} custom-call(s32[1]{0:T(128)} %bitcast.refs_0_.wide_ref, f32[176,128]{1,0:T(8,128)S(1)} %get-tuple-element.74.refs_0_, bf16[176,128]{1,0:T(8,128)(2,1)S(1)} %collective-permute-done.20.refs_1_, bf16[176,128]{1,0:T(8,128)(2,1)S(1)} %collective-permute-done.19.refs_2_, ...), custom_call_target="tpu_custom_call" | custom-call | tf_op jit(solution)/shard_map/weight_total/pallas_call | solution.py:387
  (39 shorter events, 4.6 us)
Async XLA Ops:
  0.6 9.9 %collective-permute-start = (bf16[48,1152]{1,0:T(8,128)(2,1)}, bf16[48,1152]{1,0:T(8,128)(2,1)S(1)}, u32[]{:S(2)}, u32[]{:S(2)}) collective-permute-start(bf16[48,1152]{1,0:T(8,128)(2,1)} %refs_0_.1), channel_id=1, source_target_pairs={{0,2},{1,3},{2,0},{3,1},{4,6},{5,7},{6,4},{7,5},{8,10},{9,11},{10,... | collective-permute-start | bytes 331784 | tf_op jit(solution)/shard_map/ppermute | solution.py:31
  3.7 8.6 %collective-permute-start.1 = (bf16[48,1152]{1,0:T(8,128)(2,1)}, bf16[48,1152]{1,0:T(8,128)(2,1)S(1)}, u32[]{:S(2)}, u32[]{:S(2)}) collective-permute-start(bf16[48,1152]{1,0:T(8,128)(2,1)} %refs_0_.1), channel_id=1, source_target_pairs={{0,4},{1,5},{2,6},{3,7},{4,0},{5,1},{6,2},{7,3},{8,12},{9,13},{10,... | collective-permute-start | bytes 331784 | tf_op jit(solution)/shard_map/ppermute | solution.py:31
  5.2 7.1 %collective-permute-start.2 = (bf16[48,1152]{1,0:T(8,128)(2,1)}, bf16[48,1152]{1,0:T(8,128)(2,1)S(1)}, u32[]{:S(2)}, u32[]{:S(2)}) collective-permute-start(bf16[48,1152]{1,0:T(8,128)(2,1)} %refs_0_.1), channel_id=1, source_target_pairs={{0,6},{1,7},{2,4},{3,5},{4,2},{5,3},{6,0},{7,1},{8,14},{9,15},{10,... | collective-permute-start | bytes 331784 | tf_op jit(solution)/shard_map/ppermute | solution.py:31
  5.2 9.5 %collective-permute-start.3 = (bf16[48,1152]{1,0:T(8,128)(2,1)}, bf16[48,1152]{1,0:T(8,128)(2,1)S(1)}, u32[]{:S(2)}, u32[]{:S(2)}) collective-permute-start(bf16[48,1152]{1,0:T(8,128)(2,1)} %text_ref.1), channel_id=1, source_target_pairs={{0,24},{1,25},{2,26},{3,27},{4,28},{5,29},{6,30},{7,31},{8,16},{9,... | collective-permute-start | bytes 331784 | tf_op jit(solution)/shard_map/ppermute | solution.py:31
  9.2 8.7 %collective-permute-start.4 = (bf16[48,1152]{1,0:T(8,128)(2,1)}, bf16[48,1152]{1,0:T(8,128)(2,1)S(1)}, u32[]{:S(2)}, u32[]{:S(2)}) collective-permute-start(bf16[48,1152]{1,0:T(8,128)(2,1)} %text_ref.1), channel_id=1, source_target_pairs={{0,16},{1,17},{2,18},{3,19},{4,20},{5,21},{6,22},{7,23},{8,24},{9,... | collective-permute-start | bytes 331784 | tf_op jit(solution)/shard_map/ppermute | solution.py:31
  10.5 1.7 %copy-start.3 = (bf16[48,1152]{1,0:T(8,128)(2,1)S(1)}, bf16[48,1152]{1,0:T(8,128)(2,1)}, u32[]{:S(2)}) copy-start(bf16[48,1152]{1,0:T(8,128)(2,1)} %refs_0_.1) | copy-start | bytes 331780
  10.6 7.4 %collective-permute-start.5 = (bf16[48,1152]{1,0:T(8,128)(2,1)}, bf16[48,1152]{1,0:T(8,128)(2,1)S(1)}, u32[]{:S(2)}, u32[]{:S(2)}) collective-permute-start(bf16[48,1152]{1,0:T(8,128)(2,1)} %text_ref.1), channel_id=1, source_target_pairs={{0,8},{1,9},{2,10},{3,11},{4,12},{5,13},{6,14},{7,15},{8,0},{9,1},... | collective-permute-start | bytes 331784 | tf_op jit(solution)/shard_map/ppermute | solution.py:31
  12.1 1.7 %copy-start = (bf16[1152,1152]{1,0:T(8,128)(2,1)S(1)}, bf16[1152,1152]{1,0:T(8,128)(2,1)}, u32[]{:S(2)}) copy-start(bf16[1152,1152]{1,0:T(8,128)(2,1)} %weight.1) | copy-start | bytes 7962628
  12.3 5.8 %collective-permute-start.6 = (bf16[192,1152]{1,0:T(8,128)(2,1)S(1)}, bf16[192,1152]{1,0:T(8,128)(2,1)S(1)}, u32[]{:S(2)}, u32[]{:S(2)}) collective-permute-start(bf16[192,1152]{1,0:T(8,128)(2,1)S(1)} %stack.1.feats_ref.own_half), channel_id=1, source_target_pairs={{0,1},{1,0},{2,3},{3,2},{4,5},{5,4},{6,7},{7,6},{8,9},{9,8},{10,11... | collective-permute-start | bytes 1327112 | tf_op jit(solution)/shard_map/ppermute | solution.py:31
  20.9 2.1 %copy-start.1 = (f32[144,384]{1,0:T(8,128)}, f32[144,384]{1,0:T(8,128)S(1)}, u32[]{:S(2)}) copy-start(f32[144,384]{1,0:T(8,128)S(1)} %get-tuple-element.66.refs_5_) | copy-start | bytes 663556
  20.9 1.9 %collective-permute-start.7 = (bf16[4,160,384]{2,1,0:T(8,128)(2,1)S(1)}, bf16[4,160,384]{2,1,0:T(8,128)(2,1)S(1)}, u32[]{:S(2)}, u32[]{:S(2)}) collective-permute-start(bf16[4,160,384]{2,1,0:T(8,128)(2,1)S(1)} %get-tuple-element.53), channel_id=1, source_target_pairs={{0,1},{1,0},{2,3},{3,2},{4,5},{5,4},{6,7},{7,6},{8,9},{9,8},{10,11... | collective-permute-start | bytes 1474568 | tf_op jit(solution)/shard_map/ppermute | solution.py:31
  22.9 6.0 %collective-permute-start.8 = (bf16[160,384]{1,0:T(8,128)(2,1)S(1)}, bf16[160,384]{1,0:T(8,128)(2,1)S(1)}, u32[]{:S(2)}, u32[]{:S(2)}) collective-permute-start(bf16[160,384]{1,0:T(8,128)(2,1)S(1)} %get-tuple-element.63), channel_id=1, source_target_pairs={{0,2},{1,3},{2,0},{3,1},{4,6},{5,7},{6,4},{7,5},{8,10},{9,11},{10,... | collective-permute-start | bytes 368648 | tf_op jit(solution)/shard_map/ppermute | solution.py:31
  24.5 6.4 %collective-permute-start.9 = (bf16[160,384]{1,0:T(8,128)(2,1)S(1)}, bf16[160,384]{1,0:T(8,128)(2,1)S(1)}, u32[]{:S(2)}, u32[]{:S(2)}) collective-permute-start(bf16[160,384]{1,0:T(8,128)(2,1)S(1)} %get-tuple-element.64), channel_id=1, source_target_pairs={{0,4},{1,5},{2,6},{3,7},{4,0},{5,1},{6,2},{7,3},{8,12},{9,13},{10,... | collective-permute-start | bytes 368648 | tf_op jit(solution)/shard_map/ppermute | solution.py:31
  26.0 6.2 %collective-permute-start.10 = (bf16[160,384]{1,0:T(8,128)(2,1)S(1)}, bf16[160,384]{1,0:T(8,128)(2,1)S(1)}, u32[]{:S(2)}, u32[]{:S(2)}) collective-permute-start(bf16[160,384]{1,0:T(8,128)(2,1)S(1)} %get-tuple-element.65), channel_id=1, source_target_pairs={{0,6},{1,7},{2,4},{3,5},{4,2},{5,3},{6,0},{7,1},{8,14},{9,15},{10,... | collective-permute-start | bytes 368648 | tf_op jit(solution)/shard_map/ppermute | solution.py:31
  26.5 12.2 %collective-permute-start.11 = (bf16[48,1152]{1,0:T(8,128)(2,1)S(1)}, bf16[48,1152]{1,0:T(8,128)(2,1)S(1)}, u32[]{:S(2)}, u32[]{:S(2)}) collective-permute-start(bf16[48,1152]{1,0:T(8,128)(2,1)S(1)} %get-tuple-element.71), channel_id=1, source_target_pairs={{0,24},{1,25},{2,26},{3,27},{4,28},{5,29},{6,30},{7,31},{8,16},{9,... | collective-permute-start | bytes 331784 | tf_op jit(solution)/shard_map/ppermute | solution.py:31
  28.9 10.1 %collective-permute-start.12 = (bf16[48,1152]{1,0:T(8,128)(2,1)S(1)}, bf16[48,1152]{1,0:T(8,128)(2,1)S(1)}, u32[]{:S(2)}, u32[]{:S(2)}) collective-permute-start(bf16[48,1152]{1,0:T(8,128)(2,1)S(1)} %get-tuple-element.72), channel_id=1, source_target_pairs={{0,16},{1,17},{2,18},{3,19},{4,20},{5,21},{6,22},{7,23},{8,24},{9,... | collective-permute-start | bytes 331784 | tf_op jit(solution)/shard_map/ppermute | solution.py:31
  29.0 10.1 %collective-permute-start.13 = (bf16[48,1152]{1,0:T(8,128)(2,1)S(1)}, bf16[48,1152]{1,0:T(8,128)(2,1)S(1)}, u32[]{:S(2)}, u32[]{:S(2)}) collective-permute-start(bf16[48,1152]{1,0:T(8,128)(2,1)S(1)} %get-tuple-element.73), channel_id=1, source_target_pairs={{0,8},{1,9},{2,10},{3,11},{4,12},{5,13},{6,14},{7,15},{8,0},{9,1},... | collective-permute-start | bytes 331784 | tf_op jit(solution)/shard_map/ppermute | solution.py:31
  33.9 9.8 %collective-permute-start.14 = (bf16[176,128]{1,0:T(8,128)(2,1)S(1)}, bf16[176,128]{1,0:T(8,128)(2,1)S(1)}, u32[]{:S(2)}, u32[]{:S(2)}) collective-permute-start(bf16[176,128]{1,0:T(8,128)(2,1)S(1)} %get-tuple-element.75), channel_id=1, source_target_pairs={{0,28},{1,29},{2,30},{3,31},{4,24},{5,25},{6,26},{7,27},{8,20},{9,... | collective-permute-start | bytes 135176 | tf_op jit(solution)/shard_map/ppermute | solution.py:31
  37.3 8.4 %collective-permute-start.15 = (bf16[176,128]{1,0:T(8,128)(2,1)S(1)}, bf16[176,128]{1,0:T(8,128)(2,1)S(1)}, u32[]{:S(2)}, u32[]{:S(2)}) collective-permute-start(bf16[176,128]{1,0:T(8,128)(2,1)S(1)} %get-tuple-element.76), channel_id=1, source_target_pairs={{0,24},{1,25},{2,26},{3,27},{4,28},{5,29},{6,30},{7,31},{8,16},{9,... | collective-permute-start | bytes 135176 | tf_op jit(solution)/shard_map/ppermute | solution.py:31
  39.8 7.9 %collective-permute-start.16 = (bf16[176,128]{1,0:T(8,128)(2,1)S(1)}, bf16[176,128]{1,0:T(8,128)(2,1)S(1)}, u32[]{:S(2)}, u32[]{:S(2)}) collective-permute-start(bf16[176,128]{1,0:T(8,128)(2,1)S(1)} %get-tuple-element.77), channel_id=1, source_target_pairs={{0,20},{1,21},{2,22},{3,23},{4,16},{5,17},{6,18},{7,19},{8,28},{9,... | collective-permute-start | bytes 135176 | tf_op jit(solution)/shard_map/ppermute | solution.py:31
  40.3 7.5 %collective-permute-start.17 = (bf16[176,128]{1,0:T(8,128)(2,1)S(1)}, bf16[176,128]{1,0:T(8,128)(2,1)S(1)}, u32[]{:S(2)}, u32[]{:S(2)}) collective-permute-start(bf16[176,128]{1,0:T(8,128)(2,1)S(1)} %get-tuple-element.78), channel_id=1, source_target_pairs={{0,16},{1,17},{2,18},{3,19},{4,20},{5,21},{6,22},{7,23},{8,24},{9,... | collective-permute-start | bytes 135176 | tf_op jit(solution)/shard_map/ppermute | solution.py:31
  43.7 4.9 %collective-permute-start.18 = (bf16[176,128]{1,0:T(8,128)(2,1)S(1)}, bf16[176,128]{1,0:T(8,128)(2,1)S(1)}, u32[]{:S(2)}, u32[]{:S(2)}) collective-permute-start(bf16[176,128]{1,0:T(8,128)(2,1)S(1)} %get-tuple-element.79), channel_id=1, source_target_pairs={{0,12},{1,13},{2,14},{3,15},{4,8},{5,9},{6,10},{7,11},{8,4},{9,5},... | collective-permute-start | bytes 135176 | tf_op jit(solution)/shard_map/ppermute | solution.py:31
  43.7 4.9 %collective-permute-start.19 = (bf16[176,128]{1,0:T(8,128)(2,1)S(1)}, bf16[176,128]{1,0:T(8,128)(2,1)S(1)}, u32[]{:S(2)}, u32[]{:S(2)}) collective-permute-start(bf16[176,128]{1,0:T(8,128)(2,1)S(1)} %get-tuple-element.80), channel_id=1, source_target_pairs={{0,8},{1,9},{2,10},{3,11},{4,12},{5,13},{6,14},{7,15},{8,0},{9,1},... | collective-permute-start | bytes 135176 | tf_op jit(solution)/shard_map/ppermute | solution.py:31
  45.7 4.0 %collective-permute-start.20 = (bf16[176,128]{1,0:T(8,128)(2,1)S(1)}, bf16[176,128]{1,0:T(8,128)(2,1)S(1)}, u32[]{:S(2)}, u32[]{:S(2)}) collective-permute-start(bf16[176,128]{1,0:T(8,128)(2,1)S(1)} %get-tuple-element.81), channel_id=1, source_target_pairs={{0,4},{1,5},{2,6},{3,7},{4,0},{5,1},{6,2},{7,3},{8,12},{9,13},{10,... | collective-permute-start | bytes 135176 | tf_op jit(solution)/shard_map/ppermute | solution.py:31
  (2 other events, 1.9 us)

commit v12 on v11

--- a/solution.py
+++ b/solution.py
@@ -36,17 +36,16 @@
     return high, (values - high.astype(F32)).astype(BF16)
 
 
-def stat_rows(loss, along):
+def loss_rows(loss):
     row = lax.broadcasted_iota(jnp.int32, (STAT_ROWS, loss.shape[1]), 0)
-    stats = jnp.zeros(row.shape, F32)
-    for place, line in enumerate(split_pair(loss) + split_pair(along)):
-        stats = jnp.where(row == place, line.astype(F32), stats)
-    return stats.astype(BF16)
-
-
-def stat_sums(stats):
-    stats = stats.astype(F32)
-    return stats[0:1, :] + stats[1:2, :], stats[2:3, :] + stats[3:4, :]
+    high, low = split_pair(loss)
+    rows = jnp.where(row == 0, high.astype(F32), jnp.where(row == 1, low.astype(F32), 0.0))
+    return rows.astype(BF16)
+
+
+def loss_of(rows):
+    rows = rows.astype(F32)
+    return rows[0:1, :] + rows[1:2, :]
 
 
 def column_block(member, narrow):
@@ -103,7 +102,6 @@
     got_half,
     text_all,
     feats_ref,
-    unit_out,
     inv_out,
     emb_out,
     grad_out,
@@ -134,8 +132,6 @@
         inv_out[:, cols] = inverse
         unit_all[:, cols] = unit
         emb_out[:, cols] = unit.astype(BF16)
-    block = pl.multiple_of(column_block(member, narrow) * share, share)
-    unit_out[...] = unit_all[pl.ds(block, share), :]
 
     scale = scalars_ref[0:1, 0:1]
     shift = scalars_ref[1:2, 0:1]
@@ -172,29 +168,27 @@
         sums = lax.fori_loop(1, chunks, lambda c, s: one_chunk(c, *s, False), sums)
     loss_sum, dot_sum = sums
 
-    stats = stat_rows(loss_sum, dot_sum)
+    def projected(index):
+        part = pl.ds(pl.multiple_of(column_block(member ^ index, narrow) * share, share), share)
+        return d_all[part, :] - unit_all[part, :] * dot_sum
+
+    losses = loss_rows(loss_sum)
     for index in range(group // 2):
-        part = pl.multiple_of(column_block(member ^ (2 * index), narrow) * share, share)
-        own_out[index, :share, :] = d_all[pl.ds(part, share), :]
-        part = pl.multiple_of(column_block(member ^ (2 * index + 1), narrow) * share, share)
-        send_out[index, :share, :] = d_all[pl.ds(part, share), :].astype(BF16)
-        send_out[index, share:, :] = stats
+        own_out[index, :share, :] = projected(2 * index)
+        send_out[index, :share, :] = projected(2 * index + 1).astype(BF16)
+        send_out[index, share:, :] = losses
     own_out[0, share : share + 1, :] = loss_sum
-    own_out[0, share + 1 : share + 2, :] = dot_sum
 
 
 def chip_kernel(own_ref, got_ref, own_out, *send_out):
     share = own_out.shape[0] - 8
-    loss, along = stat_sums(got_ref[0, share:, :])
-    loss = loss + own_ref[0, share : share + 1, :]
-    along = along + own_ref[0, share + 1 : share + 2, :]
+    loss = own_ref[0, share : share + 1, :] + loss_of(got_ref[0, share:, :])
     own_out[:share, :] = own_ref[0, :share, :] + got_ref[0, :share, :].astype(F32)
     own_out[share : share + 1, :] = loss
-    own_out[share + 1 : share + 2, :] = along
-    stats = stat_rows(loss, along)
+    losses = loss_rows(loss)
     for index, target in enumerate(send_out, 1):
         target[:share, :] = (own_ref[index, :share, :] + got_ref[index, :share, :].astype(F32)).astype(BF16)
-        target[share:, :] = stats
+        target[share:, :] = losses
 
 
 def caption_kernel(rows, grad_ref, emb_ref, feats_ref, feats_t, *outs):
@@ -207,30 +201,27 @@
         feats_t[:, cols] = feats_ref[cols, :].astype(F32).T.astype(BF16)
 
 
-def gathered_gradient(own_ref, got, unit_ref, inv_ref, loss_out):
-    share = unit_ref.shape[0]
+def gathered_gradient(own_ref, got, inv_ref, loss_out):
+    share = own_ref.shape[0] - 8
     total = own_ref[:share, :]
     loss = own_ref[share : share + 1, :]
-    along = own_ref[share + 1 : share + 2, :]
     for block in got:
         total = total + block[:share, :].astype(F32)
-        more_loss, more_along = stat_sums(block[share:, :])
-        loss = loss + more_loss
-        along = along + more_along
+        loss = loss + loss_of(block[share:, :])
     loss_out[...] = loss
-    return inv_ref[...] * (total - unit_ref[...] * along)
-
-
-def weight_kernel(group, wide, *refs):
+    return inv_ref[...] * total
+
+
+def weight_kernel(group, spread, *refs):
     wide_ref, own_ref = refs[:2]
     got = refs[2 : 1 + group // 2]
-    unit_ref, inv_ref, feats_ref, feats_t_ref, loss_out, own_out = refs[1 + group // 2 : 7 + group // 2]
-    send_out = refs[7 + group // 2 : 6 + group // 2 + wide]
-    main_all, rest_all = refs[6 + group // 2 + wide :]
-    share = unit_ref.shape[0]
-    rest = share - LANES
+    inv_ref, feats_ref, feats_t_ref, loss_out, own_out = refs[1 + group // 2 : 6 + group // 2]
+    send_out = refs[6 + group // 2 : 5 + group // 2 + spread]
+    main_all, rest_all = refs[5 + group // 2 + spread :]
+    wide = 2 * spread
     rows = feats_t_ref.shape[0] // wide
-    high, low = split_pair(gathered_gradient(own_ref, got, unit_ref, inv_ref, loss_out))
+    high, low = split_pair(gathered_gradient(own_ref, got, inv_ref, loss_out))
+    rest = high.shape[0] - LANES
     both = jnp.concatenate([high[:LANES, :], low[:LANES, :]], axis=0)
     main = lax.dot_general(feats_t_ref[...], both, NT, preferred_element_type=F32)
     main_all[...] = main[:, :LANES] + main[:, LANES:]
@@ -242,21 +233,29 @@
         rest_all[place, :rest, :] = tail[:, begin : begin + LANES]
         rest_all[place, rest:, :] = jnp.zeros((rest, LANES), F32)
         rest_all[place, rest:, : rows - LANES] = tail[:, begin + LANES : begin + rows]
-    for step in range(wide):
-        place = wide_ref[0] ^ step
-        target = own_out if step == 0 else send_out[step - 1]
-        target[:rows, :] = main_all[pl.ds(pl.multiple_of(place * rows, rows), rows), :].astype(target.dtype)
-        target[rows:, :] = rest_all[place].astype(target.dtype)
-
-
-def total_kernel(rest, wide_ref, *refs):
-    blocks, out = refs[:-1], refs[-1]
+    for step in range(spread):
+        target = send_out[step - 1] if step else own_out
+        for side in range(2):
+            place = wide_ref[0] ^ (2 * step + side)
+            begin = side * (rows + 2 * rest)
+            part = main_all[pl.ds(pl.multiple_of(place * rows, rows), rows), :]
+            target[begin : begin + rows, :] = part.astype(target.dtype)
+            target[begin + rows : begin + rows + 2 * rest, :] = rest_all[place].astype(target.dtype)
+
+
+def line_kernel(*refs):
+    blocks, (own_out, send_out) = refs[:-2], refs[-2:]
+    total = blocks[0][...]
+    for block in blocks[1:]:
+        total = total + block[...].astype(F32)
+    packed = own_out.shape[0]
+    own_out[...] = total[:packed, :]
+    send_out[...] = total[packed:, :].astype(BF16)
+
+
+def total_kernel(rest, wide_ref, same_ref, other_ref, out):
     rows = out.shape[0]
-    same, other = blocks[0][...], blocks[1][...].astype(F32)
-    for block in blocks[2::2]:
-        same = same + block[...].astype(F32)
-    for block in blocks[3::2]:
-        other = other + block[...].astype(F32)
+    same, other = same_ref[...], other_ref[...].astype(F32)
     left_is_same = wide_ref[0] % 2 == 0
     halves = (jnp.where(left_is_same, same, other), jnp.where(left_is_same, other, same))
     for side, half in enumerate(halves):
@@ -324,10 +323,9 @@
     results = pl.pallas_call(
         functools.partial(pair_kernel, narrow, group),
         in_specs=[SMEM] + [VMEM] * 6,
-        out_specs=[VMEM] * 7,
+        out_specs=[VMEM] * 6,
         out_shape=[
             jax.ShapeDtypeStruct((images, width), BF16),
-            jax.ShapeDtypeStruct((share, images), F32),
             jax.ShapeDtypeStruct((1, images), F32),
             jax.ShapeDtypeStruct((width, images), BF16),
             jax.ShapeDtypeStruct((spread * rows, images), BF16),
@@ -342,7 +340,7 @@
         compiler_params=limit(24 if spread <= 4 else 40),
         name="pairs",
     )(member, scalars, proj_weight, own_half, own_proj, got_half, text_emb)
-    all_feats, unit_part, inv_part, img_emb, grad_tile, own_part, sent_part = results
+    all_feats, inv_part, img_emb, grad_tile, own_part, sent_part = results
     got_part = swapped(sent_part, total, 1)
     feats_t, own_text, *sent_text = pl.pallas_call(
         functools.partial(caption_kernel, rows),
@@ -373,40 +371,48 @@
     if direct:
         wide_pos = lax.axis_index(AXES[:2]).astype(jnp.int32).reshape(1)
         loss_line, own_weight, *sent_weight = pl.pallas_call(
-            functools.partial(weight_kernel, group, wide),
-            in_specs=[SMEM] + [VMEM] * (4 + group // 2),
-            out_specs=[VMEM] * (1 + wide),
-            out_shape=[jax.ShapeDtypeStruct((1, images), F32), jax.ShapeDtypeStruct((packed, LANES), F32)]
-            + [jax.ShapeDtypeStruct((packed, LANES), BF16)] * (wide - 1),
+            functools.partial(weight_kernel, group, spread),
+            in_specs=[SMEM] + [VMEM] * (3 + group // 2),
+            out_specs=[VMEM] * (1 + spread),
+            out_shape=[jax.ShapeDtypeStruct((1, images), F32), jax.ShapeDtypeStruct((2 * packed, LANES), F32)]
+            + [jax.ShapeDtypeStruct((2 * packed, LANES), BF16)] * (spread - 1),
             scratch_shapes=[pltpu.VMEM((width, LANES), F32), pltpu.VMEM((wide, 2 * rest, LANES), F32)],
             compiler_params=limit(12),
             name="weights",
-        )(wide_pos, own_part, *got, unit_part, inv_part, all_feats, feats_t)
-        got_weight = [swapped(value, total, step * narrow) for step, value in enumerate(sent_weight, 1)]
-        got_weight = lax.optimization_barrier(got_weight[::-1])[::-1]
+        )(wide_pos, own_part, *got, inv_part, all_feats, feats_t)
+        got_weight = [swapped(value, total, step * group) for step, value in enumerate(sent_weight, 1)]
+        own_weight, sent_weight = pl.pallas_call(
+            line_kernel,
+            in_specs=[VMEM] * spread,
+            out_specs=[VMEM] * 2,
+            out_shape=[jax.ShapeDtypeStruct((packed, LANES), kind) for kind in (F32, BF16)],
+            compiler_params=limit(4),
+            name="weight_line",
+        )(own_weight, *got_weight[::-1])
+        got_weight = swapped(sent_weight, total, narrow)
         d_proj = pl.pallas_call(
             functools.partial(total_kernel, rest),
-            in_specs=[SMEM] + [VMEM] * wide,
+            in_specs=[SMEM] + [VMEM] * 2,
             out_specs=VMEM,
             out_shape=jax.ShapeDtypeStruct((out_rows, 2 * share), F32),
             compiler_params=limit(4),
             name="weight_total",
-        )(wide_pos, own_weight, *got_weight)
+        )(wide_pos, own_weight, got_weight)
     else:
 
         def gradient_kernel(*refs):
             own_ref, blocks = refs[0], refs[1 : group // 2]
-            unit_ref, inv_ref, loss_out, d_out = refs[group // 2 :]
-            d_out[...] = gathered_gradient(own_ref, blocks, unit_ref, inv_ref, loss_out)
+            inv_ref, loss_out, d_out = refs[group // 2 :]
+            d_out[...] = gathered_gradient(own_ref, blocks, inv_ref, loss_out)
 
         loss_line, d_zproj = pl.pallas_call(
             gradient_kernel,
-            in_specs=[VMEM] * (2 + group // 2),
+            in_specs=[VMEM] * (1 + group // 2),
             out_specs=[VMEM] * 2,
             out_shape=[jax.ShapeDtypeStruct((1, images), F32), jax.ShapeDtypeStruct((share, images), F32)],
             compiler_params=limit(12),
             name="gradient",
-        )(own_part, *got, unit_part, inv_part)
+        )(own_part, *got, inv_part)
         partial = sum(
             lax.dot_general(feats_t, part, NT, preferred_element_type=F32) for part in split_pair(d_zproj)
         )

time: 50.8 us -> 51.1 us (level)
  waiting for transfers between devices: 7.58 us -> 14.8 us
  starting transfers between devices: 29.5 us -> 23.3 us
  local copies, waits for them, and re-layouts: 3.92 us -> 2.98 us
    ppermute x21 -> x18, waiting for transfers between devices: 7.58 us -> 14.8 us  [swapped(): lax.ppermute(value, AXES, [(source, source ^ mask) for source in range(to...]
    ppermute x21 -> x18, starting transfers between devices: 29.5 us -> 23.3 us  [swapped(): lax.ppermute(value, AXES, [(source, source ^ mask) for source in range(to...]
    unnamed x10 -> x6, local copies, waits for them, and re-layouts: 3.34 us -> 2.4 us
  transfers between devices with their start and end apart: 21 -> 18, of which waited for: 6 -> 6; matrix products, arithmetic and copies ran while one was open for 1% -> 1% of each run, Pallas kernels for 8% -> 7%
where the time goes in v12:
time: 51.1 us; the launch traced here: 50.9 us
  starting transfers between devices  23.3 us (46%)
  waiting for transfers between devices  14.8 us (29%)
  Pallas kernels  7.68 us (15%)
  local copies, waits for them, and re-layouts  2.98 us (6%)
  between operations  2.07 us (4%)
    ppermute x18, starting transfers between devices, swapped(): lax.ppermute(value, AXES, [(source, source ^ mask) for source in range(to...  23.3 us
    ppermute x18, waiting for transfers between devices, swapped(): lax.ppermute(value, AXES, [(source, source ^ mask) for source in range(to...  14.8 us
    pallas_call x1, Pallas kernels, local(): pl.pallas_call(functools.partial(pair_kernel, narrow, group), in_specs=[S...  2.89 us
    unnamed x6, local copies, waits for them, and re-layouts  2.4 us
    pallas_call x1, Pallas kernels, local(): pl.pallas_call(functools.partial(caption_kernel, rows), in_specs=[VMEM] *...  1.23 us
  transfers between devices with their start and end apart: 18, of which 6 were waited for; matrix products, arithmetic and copies ran while one was open for 1% of the time, Pallas kernels for 7%

profile of v12, /device:TPU:0, one launch (start us, length us, event | category | flops | bytes accessed | tf_op | source)
XLA Modules:
  0.0 50.9 jit_solution(8498026998143035428)
XLA Ops:
  0.6 3.0 %collective-permute-start = (bf16[48,1152]{1,0:T(8,128)(2,1)}, bf16[48,1152]{1,0:T(8,128)(2,1)S(1)}, u32[]{:S(2)}, u32[]{:S(2)}) collective-permute-start(bf16[48,1152]{1,0:T(8,128)(2,1)} %refs_0_.1), channel_id=1, source_target_pairs={{0,2},{1,3},{2,0},{3,1},{4,6},{5,7},{6,4},{7,5},{8,10},{9,11},{10,... | collective-permute-start | bytes 331784 | tf_op jit(solution)/shard_map/ppermute | solution.py:31
  3.7 1.5 %collective-permute-start.1 = (bf16[48,1152]{1,0:T(8,128)(2,1)}, bf16[48,1152]{1,0:T(8,128)(2,1)S(1)}, u32[]{:S(2)}, u32[]{:S(2)}) collective-permute-start(bf16[48,1152]{1,0:T(8,128)(2,1)} %refs_0_.1), channel_id=1, source_target_pairs={{0,4},{1,5},{2,6},{3,7},{4,0},{5,1},{6,2},{7,3},{8,12},{9,13},{10,... | collective-permute-start | bytes 331784 | tf_op jit(solution)/shard_map/ppermute | solution.py:31
  5.2 4.0 %collective-permute-start.3 = (bf16[48,1152]{1,0:T(8,128)(2,1)}, bf16[48,1152]{1,0:T(8,128)(2,1)S(1)}, u32[]{:S(2)}, u32[]{:S(2)}) collective-permute-start(bf16[48,1152]{1,0:T(8,128)(2,1)} %text_ref.1), channel_id=1, source_target_pairs={{0,24},{1,25},{2,26},{3,27},{4,28},{5,29},{6,30},{7,31},{8,16},{9,... | collective-permute-start | bytes 331784 | tf_op jit(solution)/shard_map/ppermute | solution.py:31
  10.6 0.6 %collective-permute-start.5 = (bf16[48,1152]{1,0:T(8,128)(2,1)}, bf16[48,1152]{1,0:T(8,128)(2,1)S(1)}, u32[]{:S(2)}, u32[]{:S(2)}) collective-permute-start(bf16[48,1152]{1,0:T(8,128)(2,1)} %text_ref.1), channel_id=1, source_target_pairs={{0,8},{1,9},{2,10},{3,11},{4,12},{5,13},{6,14},{7,15},{8,0},{9,1},... | collective-permute-start | bytes 331784 | tf_op jit(solution)/shard_map/ppermute | solution.py:31
  11.2 0.9 %copy-done.2 = bf16[48,1152]{1,0:T(8,128)(2,1)S(1)} copy-done((bf16[48,1152]{1,0:T(8,128)(2,1)S(1)}, bf16[48,1152]{1,0:T(8,128)(2,1)}, u32[]{:S(2)}) %copy-start.2) | copy-done | bytes 110616
  12.4 1.5 %copy-done = bf16[1152,1152]{1,0:T(8,128)(2,1)S(1)} copy-done((bf16[1152,1152]{1,0:T(8,128)(2,1)S(1)}, bf16[1152,1152]{1,0:T(8,128)(2,1)}, u32[]{:S(2)}) %copy-start) | copy-done | bytes 2654232
  13.9 0.8 %own_projection.1.own_proj = f32[192,1152]{1,0:T(8,128)S(1)} custom-call(bf16[192,1152]{1,0:T(8,128)(2,1)S(1)} %stack.1.feats_ref.own_half, bf16[1152,1152]{1,0:T(8,128)(2,1)S(1)} %copy-done), custom_call_target="tpu_custom_call" | custom-call | tf_op jit(solution)/shard_map/own_projection/pallas_call | solution.py:304
  14.7 3.3 %collective-permute-done.4.refs_2_ = bf16[48,1152]{1,0:T(8,128)(2,1)S(1)} collective-permute-done((bf16[48,1152]{1,0:T(8,128)(2,1)}, bf16[48,1152]{1,0:T(8,128)(2,1)S(1)}, u32[]{:S(2)}, u32[]{:S(2)}) %collective-permute-start.4) | collective-permute-done | bytes 110624 | tf_op jit(solution)/shard_map/ppermute | solution.py:31
  18.1 2.9 %pairs.1 = (bf16[384,1152]{1,0:T(8,128)(2,1)S(1)}, f32[1,384]{1,0:T(1,128)S(1)}, bf16[1152,384]{1,0:T(8,128)(2,1)S(1)}, bf16[192,384]{1,0:T(8,128)(2,1)S(1)}, f3...) custom-call(s32[1]{0:T(128)} %bitcast.1.member_ref, f32[8,128]{1,0:T(8,128)S(1)} %get-tuple-element.36.scalars_ref, ...), custom_call_target="tpu_custom_call" | custom-call | tf_op jit(solution)/shard_map/pairs/pallas_call | solution.py:323
  21.1 1.2 %captions.1 = (bf16[1152,384]{1,0:T(8,128)(2,1)S(1)}, f32[48,1152]{1,0:T(8,128)S(1)}, bf16[48,1152]{1,0:T(8,128)(2,1)S(1)}, bf16[48,1152]{1,0:T(8,128)(2,1)S(1)}, bf16[48,1152]{1,0:T(8,128)(2,1)S(1)}) custom-call(bf16[192,384]{1,0:T(8,128)(2,1)S(1)} %get-tuple-element.44.grad_ref, bf16[1152,384]{1,0:T(8,128)(2,1)S(1)} %get-tuple-element.45.emb_ref, ...), custom_call_target="tpu_custom_call" | custom-call | tf_op jit(solution)/shard_map/captions/pallas_call | solution.py:345
  23.0 1.6 %collective-permute-start.8 = (bf16[160,384]{1,0:T(8,128)(2,1)S(1)}, bf16[160,384]{1,0:T(8,128)(2,1)S(1)}, u32[]{:S(2)}, u32[]{:S(2)}) collective-permute-start(bf16[160,384]{1,0:T(8,128)(2,1)S(1)} %get-tuple-element.53), channel_id=1, source_target_pairs={{0,2},{1,3},{2,0},{3,1},{4,6},{5,7},{6,4},{7,5},{8,10},{9,11},{10,... | collective-permute-start | bytes 368648 | tf_op jit(solution)/shard_map/ppermute | solution.py:31
  24.6 1.5 %collective-permute-start.9 = (bf16[160,384]{1,0:T(8,128)(2,1)S(1)}, bf16[160,384]{1,0:T(8,128)(2,1)S(1)}, u32[]{:S(2)}, u32[]{:S(2)}) collective-permute-start(bf16[160,384]{1,0:T(8,128)(2,1)S(1)} %get-tuple-element.54), channel_id=1, source_target_pairs={{0,4},{1,5},{2,6},{3,7},{4,0},{5,1},{6,2},{7,3},{8,12},{9,13},{10,... | collective-permute-start | bytes 368648 | tf_op jit(solution)/shard_map/ppermute | solution.py:31
  26.6 2.4 %collective-permute-start.11 = (bf16[48,1152]{1,0:T(8,128)(2,1)S(1)}, bf16[48,1152]{1,0:T(8,128)(2,1)S(1)}, u32[]{:S(2)}, u32[]{:S(2)}) collective-permute-start(bf16[48,1152]{1,0:T(8,128)(2,1)S(1)} %get-tuple-element.60), channel_id=1, source_target_pairs={{0,24},{1,25},{2,26},{3,27},{4,28},{5,29},{6,30},{7,31},{8,16},{9,... | collective-permute-start | bytes 331784 | tf_op jit(solution)/shard_map/ppermute | solution.py:31
  29.0 1.9 %collective-permute-start.13 = (bf16[48,1152]{1,0:T(8,128)(2,1)S(1)}, bf16[48,1152]{1,0:T(8,128)(2,1)S(1)}, u32[]{:S(2)}, u32[]{:S(2)}) collective-permute-start(bf16[48,1152]{1,0:T(8,128)(2,1)S(1)} %get-tuple-element.62), channel_id=1, source_target_pairs={{0,8},{1,9},{2,10},{3,11},{4,12},{5,13},{6,14},{7,15},{8,0},{9,1},... | collective-permute-start | bytes 331784 | tf_op jit(solution)/shard_map/ppermute | solution.py:31
  31.0 1.3 %collective-permute-done.10.refs_4_ = bf16[160,384]{1,0:T(8,128)(2,1)S(1)} collective-permute-done((bf16[160,384]{1,0:T(8,128)(2,1)S(1)}, bf16[160,384]{1,0:T(8,128)(2,1)S(1)}, u32[]{:S(2)}, u32[]{:S(2)}) %collective-permute-start.10) | collective-permute-done | bytes 122912 | tf_op jit(solution)/shard_map/ppermute | solution.py:31
  32.3 0.7 %weights.1 = (f32[1,384]{1,0:T(1,128)S(1)}, f32[352,128]{1,0:T(8,128)S(1)}, bf16[352,128]{1,0:T(8,128)(2,1)S(1)}, bf16[352,128]{1,0:T(8,128)(2,1)S(1)}, bf16[352,128]{1,0:T(8,128)(2,1)S(1)}) custom-call(s32[1]{0:T(128)} %bitcast.refs_0_.wide_ref, f32[152,384]{1,0:T(8,128)S(1)} %get-tuple-element.52.refs_1_, ...), custom_call_target="tpu_custom_call" | custom-call | tf_op jit(solution)/shard_map/weights/pallas_call | solution.py:373
  33.0 2.5 %collective-permute-start.14 = (bf16[352,128]{1,0:T(8,128)(2,1)S(1)}, bf16[352,128]{1,0:T(8,128)(2,1)S(1)}, u32[]{:S(2)}, u32[]{:S(2)}) collective-permute-start(bf16[352,128]{1,0:T(8,128)(2,1)S(1)} %get-tuple-element.64), channel_id=1, source_target_pairs={{0,24},{1,25},{2,26},{3,27},{4,28},{5,29},{6,30},{7,31},{8,16},{9,... | collective-permute-start | bytes 270344 | tf_op jit(solution)/shard_map/ppermute | solution.py:31
  35.5 1.9 %collective-permute-start.16 = (bf16[352,128]{1,0:T(8,128)(2,1)S(1)}, bf16[352,128]{1,0:T(8,128)(2,1)S(1)}, u32[]{:S(2)}, u32[]{:S(2)}) collective-permute-start(bf16[352,128]{1,0:T(8,128)(2,1)S(1)} %get-tuple-element.66), channel_id=1, source_target_pairs={{0,8},{1,9},{2,10},{3,11},{4,12},{5,13},{6,14},{7,15},{8,0},{9,1},... | collective-permute-start | bytes 270344 | tf_op jit(solution)/shard_map/ppermute | solution.py:31
  37.5 5.1 %collective-permute-done.12.refs_2_ = bf16[48,1152]{1,0:T(8,128)(2,1)S(1)} collective-permute-done((bf16[48,1152]{1,0:T(8,128)(2,1)S(1)}, bf16[48,1152]{1,0:T(8,128)(2,1)S(1)}, u32[]{:S(2)}, u32[]{:S(2)}) %collective-permute-start.12) | collective-permute-done | bytes 110624 | tf_op jit(solution)/shard_map/ppermute | solution.py:31
  42.5 0.7 %caption_total.1 = f32[48,1152]{1,0:T(8,128)} custom-call(f32[48,1152]{1,0:T(8,128)S(1)} %get-tuple-element.59.refs_0_, bf16[48,1152]{1,0:T(8,128)(2,1)S(1)} %collective-permute-done.11.refs_1_, bf16[48,1152]{1,0:T(8,128)(2,1)S(1)} %collective-permute-done.12.refs_2_, bf16[48,1152]{1,0:T(8,128)(2,1)S(1)} %collective-permute-done.13.refs_3_), custom_call_target="tpu_custom_call" | custom-call | flops 5000000000 | tf_op jit(solution)/shard_map/caption_total/pallas_call | solution.py:423
  43.3 2.5 %collective-permute-done.15.refs_2_ = bf16[352,128]{1,0:T(8,128)(2,1)S(1)} collective-permute-done((bf16[352,128]{1,0:T(8,128)(2,1)S(1)}, bf16[352,128]{1,0:T(8,128)(2,1)S(1)}, u32[]{:S(2)}, u32[]{:S(2)}) %collective-permute-start.15) | collective-permute-done | bytes 90144 | tf_op jit(solution)/shard_map/ppermute | solution.py:31
  45.9 1.6 %collective-permute-start.17 = (bf16[176,128]{1,0:T(8,128)(2,1)S(1)}, bf16[176,128]{1,0:T(8,128)(2,1)S(1)}, u32[]{:S(2)}, u32[]{:S(2)}) collective-permute-start(bf16[176,128]{1,0:T(8,128)(2,1)S(1)} %get-tuple-element.68), channel_id=1, source_target_pairs={{0,4},{1,5},{2,6},{3,7},{4,0},{5,1},{6,2},{7,3},{8,12},{9,13},{10,... | collective-permute-start | bytes 135176 | tf_op jit(solution)/shard_map/ppermute | solution.py:31
  48.1 2.0 %collective-permute-done.17.other_ref = bf16[176,128]{1,0:T(8,128)(2,1)S(1)} collective-permute-done((bf16[176,128]{1,0:T(8,128)(2,1)S(1)}, bf16[176,128]{1,0:T(8,128)(2,1)S(1)}, u32[]{:S(2)}, u32[]{:S(2)}) %collective-permute-start.17) | collective-permute-done | bytes 45088 | tf_op jit(solution)/shard_map/ppermute | solution.py:31
  50.0 0.9 %weight_total.1 = f32[144,288]{1,0:T(8,128)} custom-call(s32[1]{0:T(128)} %bitcast.refs_0_.wide_ref, f32[176,128]{1,0:T(8,128)S(1)} %get-tuple-element.67.same_ref, bf16[176,128]{1,0:T(8,128)(2,1)S(1)} %collective-permute-done.17.other_ref), custom_call_target="tpu_custom_call" | custom-call | tf_op jit(solution)/shard_map/weight_total/pallas_call | solution.py:393
  (30 shorter events, 2.4 us)
Async XLA Ops:
  0.6 9.9 %collective-permute-start = (bf16[48,1152]{1,0:T(8,128)(2,1)}, bf16[48,1152]{1,0:T(8,128)(2,1)S(1)}, u32[]{:S(2)}, u32[]{:S(2)}) collective-permute-start(bf16[48,1152]{1,0:T(8,128)(2,1)} %refs_0_.1), channel_id=1, source_target_pairs={{0,2},{1,3},{2,0},{3,1},{4,6},{5,7},{6,4},{7,5},{8,10},{9,11},{10,... | collective-permute-start | bytes 331784 | tf_op jit(solution)/shard_map/ppermute | solution.py:31
  3.7 8.6 %collective-permute-start.1 = (bf16[48,1152]{1,0:T(8,128)(2,1)}, bf16[48,1152]{1,0:T(8,128)(2,1)S(1)}, u32[]{:S(2)}, u32[]{:S(2)}) collective-permute-start(bf16[48,1152]{1,0:T(8,128)(2,1)} %refs_0_.1), channel_id=1, source_target_pairs={{0,4},{1,5},{2,6},{3,7},{4,0},{5,1},{6,2},{7,3},{8,12},{9,13},{10,... | collective-permute-start | bytes 331784 | tf_op jit(solution)/shard_map/ppermute | solution.py:31
  5.2 7.1 %collective-permute-start.2 = (bf16[48,1152]{1,0:T(8,128)(2,1)}, bf16[48,1152]{1,0:T(8,128)(2,1)S(1)}, u32[]{:S(2)}, u32[]{:S(2)}) collective-permute-start(bf16[48,1152]{1,0:T(8,128)(2,1)} %refs_0_.1), channel_id=1, source_target_pairs={{0,6},{1,7},{2,4},{3,5},{4,2},{5,3},{6,0},{7,1},{8,14},{9,15},{10,... | collective-permute-start | bytes 331784 | tf_op jit(solution)/shard_map/ppermute | solution.py:31
  5.2 9.5 %collective-permute-start.3 = (bf16[48,1152]{1,0:T(8,128)(2,1)}, bf16[48,1152]{1,0:T(8,128)(2,1)S(1)}, u32[]{:S(2)}, u32[]{:S(2)}) collective-permute-start(bf16[48,1152]{1,0:T(8,128)(2,1)} %text_ref.1), channel_id=1, source_target_pairs={{0,24},{1,25},{2,26},{3,27},{4,28},{5,29},{6,30},{7,31},{8,16},{9,... | collective-permute-start | bytes 331784 | tf_op jit(solution)/shard_map/ppermute | solution.py:31
  9.2 8.7 %collective-permute-start.4 = (bf16[48,1152]{1,0:T(8,128)(2,1)}, bf16[48,1152]{1,0:T(8,128)(2,1)S(1)}, u32[]{:S(2)}, u32[]{:S(2)}) collective-permute-start(bf16[48,1152]{1,0:T(8,128)(2,1)} %text_ref.1), channel_id=1, source_target_pairs={{0,16},{1,17},{2,18},{3,19},{4,20},{5,21},{6,22},{7,23},{8,24},{9,... | collective-permute-start | bytes 331784 | tf_op jit(solution)/shard_map/ppermute | solution.py:31
  10.5 1.7 %copy-start.1 = (bf16[48,1152]{1,0:T(8,128)(2,1)S(1)}, bf16[48,1152]{1,0:T(8,128)(2,1)}, u32[]{:S(2)}) copy-start(bf16[48,1152]{1,0:T(8,128)(2,1)} %refs_0_.1) | copy-start | bytes 331780
  10.6 7.4 %collective-permute-start.5 = (bf16[48,1152]{1,0:T(8,128)(2,1)}, bf16[48,1152]{1,0:T(8,128)(2,1)S(1)}, u32[]{:S(2)}, u32[]{:S(2)}) collective-permute-start(bf16[48,1152]{1,0:T(8,128)(2,1)} %text_ref.1), channel_id=1, source_target_pairs={{0,8},{1,9},{2,10},{3,11},{4,12},{5,13},{6,14},{7,15},{8,0},{9,1},... | collective-permute-start | bytes 331784 | tf_op jit(solution)/shard_map/ppermute | solution.py:31
  11.2 0.9 %copy-start.2 = (bf16[48,1152]{1,0:T(8,128)(2,1)S(1)}, bf16[48,1152]{1,0:T(8,128)(2,1)}, u32[]{:S(2)}) copy-start(bf16[48,1152]{1,0:T(8,128)(2,1)} %text_ref.1) | copy-start | bytes 331780
  12.1 1.7 %copy-start = (bf16[1152,1152]{1,0:T(8,128)(2,1)S(1)}, bf16[1152,1152]{1,0:T(8,128)(2,1)}, u32[]{:S(2)}) copy-start(bf16[1152,1152]{1,0:T(8,128)(2,1)} %weight.1) | copy-start | bytes 7962628
  12.3 5.8 %collective-permute-start.6 = (bf16[192,1152]{1,0:T(8,128)(2,1)S(1)}, bf16[192,1152]{1,0:T(8,128)(2,1)S(1)}, u32[]{:S(2)}, u32[]{:S(2)}) collective-permute-start(bf16[192,1152]{1,0:T(8,128)(2,1)S(1)} %stack.1.feats_ref.own_half), channel_id=1, source_target_pairs={{0,1},{1,0},{2,3},{3,2},{4,5},{5,4},{6,7},{7,6},{8,9},{9,8},{10,11... | collective-permute-start | bytes 1327112 | tf_op jit(solution)/shard_map/ppermute | solution.py:31
  21.0 1.9 %collective-permute-start.7 = (bf16[4,160,384]{2,1,0:T(8,128)(2,1)S(1)}, bf16[4,160,384]{2,1,0:T(8,128)(2,1)S(1)}, u32[]{:S(2)}, u32[]{:S(2)}) collective-permute-start(bf16[4,160,384]{2,1,0:T(8,128)(2,1)S(1)} %get-tuple-element.43), channel_id=1, source_target_pairs={{0,1},{1,0},{2,3},{3,2},{4,5},{5,4},{6,7},{7,6},{8,9},{9,8},{10,11... | collective-permute-start | bytes 1474568 | tf_op jit(solution)/shard_map/ppermute | solution.py:31
  23.0 6.0 %collective-permute-start.8 = (bf16[160,384]{1,0:T(8,128)(2,1)S(1)}, bf16[160,384]{1,0:T(8,128)(2,1)S(1)}, u32[]{:S(2)}, u32[]{:S(2)}) collective-permute-start(bf16[160,384]{1,0:T(8,128)(2,1)S(1)} %get-tuple-element.53), channel_id=1, source_target_pairs={{0,2},{1,3},{2,0},{3,1},{4,6},{5,7},{6,4},{7,5},{8,10},{9,11},{10,... | collective-permute-start | bytes 368648 | tf_op jit(solution)/shard_map/ppermute | solution.py:31
  24.6 6.4 %collective-permute-start.9 = (bf16[160,384]{1,0:T(8,128)(2,1)S(1)}, bf16[160,384]{1,0:T(8,128)(2,1)S(1)}, u32[]{:S(2)}, u32[]{:S(2)}) collective-permute-start(bf16[160,384]{1,0:T(8,128)(2,1)S(1)} %get-tuple-element.54), channel_id=1, source_target_pairs={{0,4},{1,5},{2,6},{3,7},{4,0},{5,1},{6,2},{7,3},{8,12},{9,13},{10,... | collective-permute-start | bytes 368648 | tf_op jit(solution)/shard_map/ppermute | solution.py:31
  26.1 6.2 %collective-permute-start.10 = (bf16[160,384]{1,0:T(8,128)(2,1)S(1)}, bf16[160,384]{1,0:T(8,128)(2,1)S(1)}, u32[]{:S(2)}, u32[]{:S(2)}) collective-permute-start(bf16[160,384]{1,0:T(8,128)(2,1)S(1)} %get-tuple-element.55), channel_id=1, source_target_pairs={{0,6},{1,7},{2,4},{3,5},{4,2},{5,3},{6,0},{7,1},{8,14},{9,15},{10,... | collective-permute-start | bytes 368648 | tf_op jit(solution)/shard_map/ppermute | solution.py:31
  26.6 8.9 %collective-permute-start.11 = (bf16[48,1152]{1,0:T(8,128)(2,1)S(1)}, bf16[48,1152]{1,0:T(8,128)(2,1)S(1)}, u32[]{:S(2)}, u32[]{:S(2)}) collective-permute-start(bf16[48,1152]{1,0:T(8,128)(2,1)S(1)} %get-tuple-element.60), channel_id=1, source_target_pairs={{0,24},{1,25},{2,26},{3,27},{4,28},{5,29},{6,30},{7,31},{8,16},{9,... | collective-permute-start | bytes 331784 | tf_op jit(solution)/shard_map/ppermute | solution.py:31
  29.0 13.5 %collective-permute-start.12 = (bf16[48,1152]{1,0:T(8,128)(2,1)S(1)}, bf16[48,1152]{1,0:T(8,128)(2,1)S(1)}, u32[]{:S(2)}, u32[]{:S(2)}) collective-permute-start(bf16[48,1152]{1,0:T(8,128)(2,1)S(1)} %get-tuple-element.61), channel_id=1, source_target_pairs={{0,16},{1,17},{2,18},{3,19},{4,20},{5,21},{6,22},{7,23},{8,24},{9,... | collective-permute-start | bytes 331784 | tf_op jit(solution)/shard_map/ppermute | solution.py:31
  29.0 13.5 %collective-permute-start.13 = (bf16[48,1152]{1,0:T(8,128)(2,1)S(1)}, bf16[48,1152]{1,0:T(8,128)(2,1)S(1)}, u32[]{:S(2)}, u32[]{:S(2)}) collective-permute-start(bf16[48,1152]{1,0:T(8,128)(2,1)S(1)} %get-tuple-element.62), channel_id=1, source_target_pairs={{0,8},{1,9},{2,10},{3,11},{4,12},{5,13},{6,14},{7,15},{8,0},{9,1},... | collective-permute-start | bytes 331784 | tf_op jit(solution)/shard_map/ppermute | solution.py:31
  33.0 10.3 %collective-permute-start.14 = (bf16[352,128]{1,0:T(8,128)(2,1)S(1)}, bf16[352,128]{1,0:T(8,128)(2,1)S(1)}, u32[]{:S(2)}, u32[]{:S(2)}) collective-permute-start(bf16[352,128]{1,0:T(8,128)(2,1)S(1)} %get-tuple-element.64), channel_id=1, source_target_pairs={{0,24},{1,25},{2,26},{3,27},{4,28},{5,29},{6,30},{7,31},{8,16},{9,... | collective-permute-start | bytes 270344 | tf_op jit(solution)/shard_map/ppermute | solution.py:31
  35.5 10.3 %collective-permute-start.15 = (bf16[352,128]{1,0:T(8,128)(2,1)S(1)}, bf16[352,128]{1,0:T(8,128)(2,1)S(1)}, u32[]{:S(2)}, u32[]{:S(2)}) collective-permute-start(bf16[352,128]{1,0:T(8,128)(2,1)S(1)} %get-tuple-element.65), channel_id=1, source_target_pairs={{0,16},{1,17},{2,18},{3,19},{4,20},{5,21},{6,22},{7,23},{8,24},{9,... | collective-permute-start | bytes 270344 | tf_op jit(solution)/shard_map/ppermute | solution.py:31
  35.5 10.3 %collective-permute-start.16 = (bf16[352,128]{1,0:T(8,128)(2,1)S(1)}, bf16[352,128]{1,0:T(8,128)(2,1)S(1)}, u32[]{:S(2)}, u32[]{:S(2)}) collective-permute-start(bf16[352,128]{1,0:T(8,128)(2,1)S(1)} %get-tuple-element.66), channel_id=1, source_target_pairs={{0,8},{1,9},{2,10},{3,11},{4,12},{5,13},{6,14},{7,15},{8,0},{9,1},... | collective-permute-start | bytes 270344 | tf_op jit(solution)/shard_map/ppermute | solution.py:31
  45.9 4.1 %collective-permute-start.17 = (bf16[176,128]{1,0:T(8,128)(2,1)S(1)}, bf16[176,128]{1,0:T(8,128)(2,1)S(1)}, u32[]{:S(2)}, u32[]{:S(2)}) collective-permute-start(bf16[176,128]{1,0:T(8,128)(2,1)S(1)} %get-tuple-element.68), channel_id=1, source_target_pairs={{0,4},{1,5},{2,6},{3,7},{4,0},{5,1},{6,2},{7,3},{8,12},{9,13},{10,... | collective-permute-start | bytes 135176 | tf_op jit(solution)/shard_map/ppermute | solution.py:31

commit v13 on v12

--- a/solution.py
+++ b/solution.py
@@ -212,13 +212,12 @@
     return inv_ref[...] * total
 
 
-def weight_kernel(group, spread, *refs):
+def weight_kernel(group, wide, *refs):
     wide_ref, own_ref = refs[:2]
     got = refs[2 : 1 + group // 2]
     inv_ref, feats_ref, feats_t_ref, loss_out, own_out = refs[1 + group // 2 : 6 + group // 2]
-    send_out = refs[6 + group // 2 : 5 + group // 2 + spread]
-    main_all, rest_all = refs[5 + group // 2 + spread :]
-    wide = 2 * spread
+    send_out = refs[6 + group // 2 : 5 + group // 2 + wide]
+    main_all, rest_all = refs[5 + group // 2 + wide :]
     rows = feats_t_ref.shape[0] // wide
     high, low = split_pair(gathered_gradient(own_ref, got, inv_ref, loss_out))
     rest = high.shape[0] - LANES
@@ -233,29 +232,21 @@
         rest_all[place, :rest, :] = tail[:, begin : begin + LANES]
         rest_all[place, rest:, :] = jnp.zeros((rest, LANES), F32)
         rest_all[place, rest:, : rows - LANES] = tail[:, begin + LANES : begin + rows]
-    for step in range(spread):
-        target = send_out[step - 1] if step else own_out
-        for side in range(2):
-            place = wide_ref[0] ^ (2 * step + side)
-            begin = side * (rows + 2 * rest)
-            part = main_all[pl.ds(pl.multiple_of(place * rows, rows), rows), :]
-            target[begin : begin + rows, :] = part.astype(target.dtype)
-            target[begin + rows : begin + rows + 2 * rest, :] = rest_all[place].astype(target.dtype)
-
-
-def line_kernel(*refs):
-    blocks, (own_out, send_out) = refs[:-2], refs[-2:]
-    total = blocks[0][...]
-    for block in blocks[1:]:
-        total = total + block[...].astype(F32)
-    packed = own_out.shape[0]
-    own_out[...] = total[:packed, :]
-    send_out[...] = total[packed:, :].astype(BF16)
-
-
-def total_kernel(rest, wide_ref, same_ref, other_ref, out):
+    for step in range(wide):
+        place = wide_ref[0] ^ step
+        target = own_out if step == 0 else send_out[step - 1]
+        target[:rows, :] = main_all[pl.ds(pl.multiple_of(place * rows, rows), rows), :].astype(target.dtype)
+        target[rows:, :] = rest_all[place].astype(target.dtype)
+
+
+def total_kernel(rest, wide_ref, *refs):
+    blocks, out = refs[:-1], refs[-1]
     rows = out.shape[0]
-    same, other = same_ref[...], other_ref[...].astype(F32)
+    same, other = blocks[0][...], blocks[1][...].astype(F32)
+    for block in blocks[2::2]:
+        same = same + block[...].astype(F32)
+    for block in blocks[3::2]:
+        other = other + block[...].astype(F32)
     left_is_same = wide_ref[0] % 2 == 0
     halves = (jnp.where(left_is_same, same, other), jnp.where(left_is_same, other, same))
     for side, half in enumerate(halves):
@@ -371,33 +362,25 @@
     if direct:
         wide_pos = lax.axis_index(AXES[:2]).astype(jnp.int32).reshape(1)
         loss_line, own_weight, *sent_weight = pl.pallas_call(
-            functools.partial(weight_kernel, group, spread),
+            functools.partial(weight_kernel, group, wide),
             in_specs=[SMEM] + [VMEM] * (3 + group // 2),
-            out_specs=[VMEM] * (1 + spread),
-            out_shape=[jax.ShapeDtypeStruct((1, images), F32), jax.ShapeDtypeStruct((2 * packed, LANES), F32)]
-            + [jax.ShapeDtypeStruct((2 * packed, LANES), BF16)] * (spread - 1),
+            out_specs=[VMEM] * (1 + wide),
+            out_shape=[jax.ShapeDtypeStruct((1, images), F32), jax.ShapeDtypeStruct((packed, LANES), F32)]
+            + [jax.ShapeDtypeStruct((packed, LANES), BF16)] * (wide - 1),
             scratch_shapes=[pltpu.VMEM((width, LANES), F32), pltpu.VMEM((wide, 2 * rest, LANES), F32)],
             compiler_params=limit(12),
             name="weights",
         )(wide_pos, own_part, *got, inv_part, all_feats, feats_t)
-        got_weight = [swapped(value, total, step * group) for step, value in enumerate(sent_weight, 1)]
-        own_weight, sent_weight = pl.pallas_call(
-            line_kernel,
-            in_specs=[VMEM] * spread,
-            out_specs=[VMEM] * 2,
-            out_shape=[jax.ShapeDtypeStruct((packed, LANES), kind) for kind in (F32, BF16)],
-            compiler_params=limit(4),
-            name="weight_line",
-        )(own_weight, *got_weight[::-1])
-        got_weight = swapped(sent_weight, total, narrow)
+        got_weight = [swapped(value, total, step * narrow) for step, value in enumerate(sent_weight, 1)]
+        got_weight = lax.optimization_barrier(got_weight[::-1])[::-1]
         d_proj = pl.pallas_call(
             functools.partial(total_kernel, rest),
-            in_specs=[SMEM] + [VMEM] * 2,
+            in_specs=[SMEM] + [VMEM] * wide,
             out_specs=VMEM,
             out_shape=jax.ShapeDtypeStruct((out_rows, 2 * share), F32),
             compiler_params=limit(4),
             name="weight_total",
-        )(wide_pos, own_weight, got_weight)
+        )(wide_pos, own_weight, *got_weight)
     else:
 
         def gradient_kernel(*refs):

time: 51.1 us -> 51.3 us (level)
  starting transfers between devices: 23.3 us -> 30.4 us
  waiting for transfers between devices: 14.8 us -> 8.01 us
    ppermute x18 -> x21, starting transfers between devices: 23.3 us -> 30.4 us  [swapped(): lax.ppermute(value, AXES, [(source, source ^ mask) for source in range(to...]
    ppermute x18 -> x21, waiting for transfers between devices: 14.8 us -> 8.01 us  [swapped(): lax.ppermute(value, AXES, [(source, source ^ mask) for source in range(to...]
  transfers between devices with their start and end apart: 18 -> 21, of which waited for: 6 -> 6; matrix products, arithmetic and copies ran while one was open for 1% -> 1% of each run, Pallas kernels for 7% -> 7%
where the time goes in v13:
time: 51.3 us; the launch traced here: 51.1 us
  starting transfers between devices  30.4 us (59%)
  waiting for transfers between devices  8.01 us (16%)
  Pallas kernels  7.64 us (15%)
  local copies, waits for them, and re-layouts  2.98 us (6%)
  between operations  2.07 us (4%)
    ppermute x21, starting transfers between devices, swapped(): lax.ppermute(value, AXES, [(source, source ^ mask) for source in range(to...  30.4 us
    ppermute x21, waiting for transfers between devices, swapped(): lax.ppermute(value, AXES, [(source, source ^ mask) for source in range(to...  8.01 us
    pallas_call x1, Pallas kernels, local(): pl.pallas_call(functools.partial(pair_kernel, narrow, group), in_specs=[S...  2.89 us
    unnamed x6, local copies, waits for them, and re-layouts  2.4 us
    pallas_call x1, Pallas kernels, local(): pl.pallas_call(functools.partial(caption_kernel, rows), in_specs=[VMEM] *...  1.23 us
  transfers between devices with their start and end apart: 21, of which 6 were waited for; matrix products, arithmetic and copies ran while one was open for 1% of the time, Pallas kernels for 7%

profile of v13, /device:TPU:0, one launch (start us, length us, event | category | flops | bytes accessed | tf_op | source)
XLA Modules:
  0.0 51.1 jit_solution(10509926060443642845)
XLA Ops:
  0.6 3.0 %collective-permute-start = (bf16[48,1152]{1,0:T(8,128)(2,1)}, bf16[48,1152]{1,0:T(8,128)(2,1)S(1)}, u32[]{:S(2)}, u32[]{:S(2)}) collective-permute-start(bf16[48,1152]{1,0:T(8,128)(2,1)} %refs_0_.1), channel_id=1, source_target_pairs={{0,2},{1,3},{2,0},{3,1},{4,6},{5,7},{6,4},{7,5},{8,10},{9,11},{10,... | collective-permute-start | bytes 331784 | tf_op jit(solution)/shard_map/ppermute | solution.py:31
  3.7 1.5 %collective-permute-start.1 = (bf16[48,1152]{1,0:T(8,128)(2,1)}, bf16[48,1152]{1,0:T(8,128)(2,1)S(1)}, u32[]{:S(2)}, u32[]{:S(2)}) collective-permute-start(bf16[48,1152]{1,0:T(8,128)(2,1)} %refs_0_.1), channel_id=1, source_target_pairs={{0,4},{1,5},{2,6},{3,7},{4,0},{5,1},{6,2},{7,3},{8,12},{9,13},{10,... | collective-permute-start | bytes 331784 | tf_op jit(solution)/shard_map/ppermute | solution.py:31
  5.2 4.0 %collective-permute-start.3 = (bf16[48,1152]{1,0:T(8,128)(2,1)}, bf16[48,1152]{1,0:T(8,128)(2,1)S(1)}, u32[]{:S(2)}, u32[]{:S(2)}) collective-permute-start(bf16[48,1152]{1,0:T(8,128)(2,1)} %text_ref.1), channel_id=1, source_target_pairs={{0,24},{1,25},{2,26},{3,27},{4,28},{5,29},{6,30},{7,31},{8,16},{9,... | collective-permute-start | bytes 331784 | tf_op jit(solution)/shard_map/ppermute | solution.py:31
  11.2 0.9 %copy-done.2 = bf16[48,1152]{1,0:T(8,128)(2,1)S(1)} copy-done((bf16[48,1152]{1,0:T(8,128)(2,1)S(1)}, bf16[48,1152]{1,0:T(8,128)(2,1)}, u32[]{:S(2)}) %copy-start.2) | copy-done | bytes 110616
  12.4 1.5 %copy-done = bf16[1152,1152]{1,0:T(8,128)(2,1)S(1)} copy-done((bf16[1152,1152]{1,0:T(8,128)(2,1)S(1)}, bf16[1152,1152]{1,0:T(8,128)(2,1)}, u32[]{:S(2)}) %copy-start) | copy-done | bytes 2654232
  13.9 0.8 %own_projection.1.own_proj = f32[192,1152]{1,0:T(8,128)S(1)} custom-call(bf16[192,1152]{1,0:T(8,128)(2,1)S(1)} %stack.1.feats_ref.own_half, bf16[1152,1152]{1,0:T(8,128)(2,1)S(1)} %copy-done), custom_call_target="tpu_custom_call" | custom-call | tf_op jit(solution)/shard_map/own_projection/pallas_call | solution.py:295
  14.7 3.3 %collective-permute-done.4.refs_2_ = bf16[48,1152]{1,0:T(8,128)(2,1)S(1)} collective-permute-done((bf16[48,1152]{1,0:T(8,128)(2,1)}, bf16[48,1152]{1,0:T(8,128)(2,1)S(1)}, u32[]{:S(2)}, u32[]{:S(2)}) %collective-permute-start.4) | collective-permute-done | bytes 110624 | tf_op jit(solution)/shard_map/ppermute | solution.py:31
  18.1 2.9 %pairs.1 = (bf16[384,1152]{1,0:T(8,128)(2,1)S(1)}, f32[1,384]{1,0:T(1,128)S(1)}, bf16[1152,384]{1,0:T(8,128)(2,1)S(1)}, bf16[192,384]{1,0:T(8,128)(2,1)S(1)}, f3...) custom-call(s32[1]{0:T(128)} %bitcast.1.member_ref, f32[8,128]{1,0:T(8,128)S(1)} %get-tuple-element.45.scalars_ref, ...), custom_call_target="tpu_custom_call" | custom-call | tf_op jit(solution)/shard_map/pairs/pallas_call | solution.py:314
  21.1 1.2 %captions.1 = (bf16[1152,384]{1,0:T(8,128)(2,1)S(1)}, f32[48,1152]{1,0:T(8,128)S(1)}, bf16[48,1152]{1,0:T(8,128)(2,1)S(1)}, bf16[48,1152]{1,0:T(8,128)(2,1)S(1)}, bf16[48,1152]{1,0:T(8,128)(2,1)S(1)}) custom-call(bf16[192,384]{1,0:T(8,128)(2,1)S(1)} %get-tuple-element.53.grad_ref, bf16[1152,384]{1,0:T(8,128)(2,1)S(1)} %get-tuple-element.54.emb_ref, ...), custom_call_target="tpu_custom_call" | custom-call | tf_op jit(solution)/shard_map/captions/pallas_call | solution.py:336
  23.0 1.6 %collective-permute-start.8 = (bf16[160,384]{1,0:T(8,128)(2,1)S(1)}, bf16[160,384]{1,0:T(8,128)(2,1)S(1)}, u32[]{:S(2)}, u32[]{:S(2)}) collective-permute-start(bf16[160,384]{1,0:T(8,128)(2,1)S(1)} %get-tuple-element.62), channel_id=1, source_target_pairs={{0,2},{1,3},{2,0},{3,1},{4,6},{5,7},{6,4},{7,5},{8,10},{9,11},{10,... | collective-permute-start | bytes 368648 | tf_op jit(solution)/shard_map/ppermute | solution.py:31
  24.6 1.5 %collective-permute-start.9 = (bf16[160,384]{1,0:T(8,128)(2,1)S(1)}, bf16[160,384]{1,0:T(8,128)(2,1)S(1)}, u32[]{:S(2)}, u32[]{:S(2)}) collective-permute-start(bf16[160,384]{1,0:T(8,128)(2,1)S(1)} %get-tuple-element.63), channel_id=1, source_target_pairs={{0,4},{1,5},{2,6},{3,7},{4,0},{5,1},{6,2},{7,3},{8,12},{9,13},{10,... | collective-permute-start | bytes 368648 | tf_op jit(solution)/shard_map/ppermute | solution.py:31
  26.6 2.4 %collective-permute-start.11 = (bf16[48,1152]{1,0:T(8,128)(2,1)S(1)}, bf16[48,1152]{1,0:T(8,128)(2,1)S(1)}, u32[]{:S(2)}, u32[]{:S(2)}) collective-permute-start(bf16[48,1152]{1,0:T(8,128)(2,1)S(1)} %get-tuple-element.69), channel_id=1, source_target_pairs={{0,24},{1,25},{2,26},{3,27},{4,28},{5,29},{6,30},{7,31},{8,16},{9,... | collective-permute-start | bytes 331784 | tf_op jit(solution)/shard_map/ppermute | solution.py:31
  29.0 1.9 %collective-permute-start.13 = (bf16[48,1152]{1,0:T(8,128)(2,1)S(1)}, bf16[48,1152]{1,0:T(8,128)(2,1)S(1)}, u32[]{:S(2)}, u32[]{:S(2)}) collective-permute-start(bf16[48,1152]{1,0:T(8,128)(2,1)S(1)} %get-tuple-element.71), channel_id=1, source_target_pairs={{0,8},{1,9},{2,10},{3,11},{4,12},{5,13},{6,14},{7,15},{8,0},{9,1},... | collective-permute-start | bytes 331784 | tf_op jit(solution)/shard_map/ppermute | solution.py:31
  31.0 1.3 %collective-permute-done.10.refs_4_ = bf16[160,384]{1,0:T(8,128)(2,1)S(1)} collective-permute-done((bf16[160,384]{1,0:T(8,128)(2,1)S(1)}, bf16[160,384]{1,0:T(8,128)(2,1)S(1)}, u32[]{:S(2)}, u32[]{:S(2)}) %collective-permute-start.10) | collective-permute-done | bytes 122912 | tf_op jit(solution)/shard_map/ppermute | solution.py:31
  33.0 3.4 %collective-permute-start.14 = (bf16[176,128]{1,0:T(8,128)(2,1)S(1)}, bf16[176,128]{1,0:T(8,128)(2,1)S(1)}, u32[]{:S(2)}, u32[]{:S(2)}) collective-permute-start(bf16[176,128]{1,0:T(8,128)(2,1)S(1)} %get-tuple-element.73), channel_id=1, source_target_pairs={{0,28},{1,29},{2,30},{3,31},{4,24},{5,25},{6,26},{7,27},{8,20},{9,... | collective-permute-start | bytes 135176 | tf_op jit(solution)/shard_map/ppermute | solution.py:31
  36.4 1.4 %collective-permute-start.15 = (bf16[176,128]{1,0:T(8,128)(2,1)S(1)}, bf16[176,128]{1,0:T(8,128)(2,1)S(1)}, u32[]{:S(2)}, u32[]{:S(2)}) collective-permute-start(bf16[176,128]{1,0:T(8,128)(2,1)S(1)} %get-tuple-element.74), channel_id=1, source_target_pairs={{0,24},{1,25},{2,26},{3,27},{4,28},{5,29},{6,30},{7,31},{8,16},{9,... | collective-permute-start | bytes 135176 | tf_op jit(solution)/shard_map/ppermute | solution.py:31
  37.8 1.4 %collective-permute-done.12.refs_2_ = bf16[48,1152]{1,0:T(8,128)(2,1)S(1)} collective-permute-done((bf16[48,1152]{1,0:T(8,128)(2,1)S(1)}, bf16[48,1152]{1,0:T(8,128)(2,1)S(1)}, u32[]{:S(2)}, u32[]{:S(2)}) %collective-permute-start.12) | collective-permute-done | bytes 110624 | tf_op jit(solution)/shard_map/ppermute | solution.py:31
  39.2 0.7 %caption_total.1 = f32[48,1152]{1,0:T(8,128)} custom-call(f32[48,1152]{1,0:T(8,128)S(1)} %get-tuple-element.68.refs_0_, bf16[48,1152]{1,0:T(8,128)(2,1)S(1)} %collective-permute-done.11.refs_1_, bf16[48,1152]{1,0:T(8,128)(2,1)S(1)} %collective-permute-done.12.refs_2_, bf16[48,1152]{1,0:T(8,128)(2,1)S(1)} %collective-permute-done.13.refs_3_), custom_call_target="tpu_custom_call" | custom-call | flops 5000000000 | tf_op jit(solution)/shard_map/caption_total/pallas_call | solution.py:406
  39.9 1.3 %collective-permute-start.16 = (bf16[176,128]{1,0:T(8,128)(2,1)S(1)}, bf16[176,128]{1,0:T(8,128)(2,1)S(1)}, u32[]{:S(2)}, u32[]{:S(2)}) collective-permute-start(bf16[176,128]{1,0:T(8,128)(2,1)S(1)} %get-tuple-element.75), channel_id=1, source_target_pairs={{0,20},{1,21},{2,22},{3,23},{4,16},{5,17},{6,18},{7,19},{8,28},{9,... | collective-permute-start | bytes 135176 | tf_op jit(solution)/shard_map/ppermute | solution.py:31
  41.2 3.5 %collective-permute-start.17 = (bf16[176,128]{1,0:T(8,128)(2,1)S(1)}, bf16[176,128]{1,0:T(8,128)(2,1)S(1)}, u32[]{:S(2)}, u32[]{:S(2)}) collective-permute-start(bf16[176,128]{1,0:T(8,128)(2,1)S(1)} %get-tuple-element.76), channel_id=1, source_target_pairs={{0,16},{1,17},{2,18},{3,19},{4,20},{5,21},{6,22},{7,23},{8,24},{9,... | collective-permute-start | bytes 135176 | tf_op jit(solution)/shard_map/ppermute | solution.py:31
  44.7 1.0 %collective-permute-start.19 = (bf16[176,128]{1,0:T(8,128)(2,1)S(1)}, bf16[176,128]{1,0:T(8,128)(2,1)S(1)}, u32[]{:S(2)}, u32[]{:S(2)}) collective-permute-start(bf16[176,128]{1,0:T(8,128)(2,1)S(1)} %get-tuple-element.78), channel_id=1, source_target_pairs={{0,8},{1,9},{2,10},{3,11},{4,12},{5,13},{6,14},{7,15},{8,0},{9,1},... | collective-permute-start | bytes 135176 | tf_op jit(solution)/shard_map/ppermute | solution.py:31
  45.8 2.5 %collective-permute-start.20 = (bf16[176,128]{1,0:T(8,128)(2,1)S(1)}, bf16[176,128]{1,0:T(8,128)(2,1)S(1)}, u32[]{:S(2)}, u32[]{:S(2)}) collective-permute-start(bf16[176,128]{1,0:T(8,128)(2,1)S(1)} %get-tuple-element.79), channel_id=1, source_target_pairs={{0,4},{1,5},{2,6},{3,7},{4,0},{5,1},{6,2},{7,3},{8,12},{9,13},{10,... | collective-permute-start | bytes 135176 | tf_op jit(solution)/shard_map/ppermute | solution.py:31
  48.8 0.9 %collective-permute-done.18.refs_3_ = bf16[176,128]{1,0:T(8,128)(2,1)S(1)} collective-permute-done((bf16[176,128]{1,0:T(8,128)(2,1)S(1)}, bf16[176,128]{1,0:T(8,128)(2,1)S(1)}, u32[]{:S(2)}, u32[]{:S(2)}) %collective-permute-start.18) | collective-permute-done | bytes 45088 | tf_op jit(solution)/shard_map/ppermute | solution.py:31
  50.3 0.9 %weight_total.1 = f32[144,288]{1,0:T(8,128)} custom-call(s32[1]{0:T(128)} %bitcast.refs_0_.wide_ref, f32[176,128]{1,0:T(8,128)S(1)} %get-tuple-element.72.refs_0_, bf16[176,128]{1,0:T(8,128)(2,1)S(1)} %collective-permute-done.20.refs_1_, bf16[176,128]{1,0:T(8,128)(2,1)S(1)} %collective-permute-done.19.refs_2_, ...), custom_call_target="tpu_custom_call" | custom-call | tf_op jit(solution)/shard_map/weight_total/pallas_call | solution.py:376
  (35 shorter events, 4.2 us)
Async XLA Ops:
  0.6 9.9 %collective-permute-start = (bf16[48,1152]{1,0:T(8,128)(2,1)}, bf16[48,1152]{1,0:T(8,128)(2,1)S(1)}, u32[]{:S(2)}, u32[]{:S(2)}) collective-permute-start(bf16[48,1152]{1,0:T(8,128)(2,1)} %refs_0_.1), channel_id=1, source_target_pairs={{0,2},{1,3},{2,0},{3,1},{4,6},{5,7},{6,4},{7,5},{8,10},{9,11},{10,... | collective-permute-start | bytes 331784 | tf_op jit(solution)/shard_map/ppermute | solution.py:31
  3.7 8.6 %collective-permute-start.1 = (bf16[48,1152]{1,0:T(8,128)(2,1)}, bf16[48,1152]{1,0:T(8,128)(2,1)S(1)}, u32[]{:S(2)}, u32[]{:S(2)}) collective-permute-start(bf16[48,1152]{1,0:T(8,128)(2,1)} %refs_0_.1), channel_id=1, source_target_pairs={{0,4},{1,5},{2,6},{3,7},{4,0},{5,1},{6,2},{7,3},{8,12},{9,13},{10,... | collective-permute-start | bytes 331784 | tf_op jit(solution)/shard_map/ppermute | solution.py:31
  5.2 7.1 %collective-permute-start.2 = (bf16[48,1152]{1,0:T(8,128)(2,1)}, bf16[48,1152]{1,0:T(8,128)(2,1)S(1)}, u32[]{:S(2)}, u32[]{:S(2)}) collective-permute-start(bf16[48,1152]{1,0:T(8,128)(2,1)} %refs_0_.1), channel_id=1, source_target_pairs={{0,6},{1,7},{2,4},{3,5},{4,2},{5,3},{6,0},{7,1},{8,14},{9,15},{10,... | collective-permute-start | bytes 331784 | tf_op jit(solution)/shard_map/ppermute | solution.py:31
  5.2 9.5 %collective-permute-start.3 = (bf16[48,1152]{1,0:T(8,128)(2,1)}, bf16[48,1152]{1,0:T(8,128)(2,1)S(1)}, u32[]{:S(2)}, u32[]{:S(2)}) collective-permute-start(bf16[48,1152]{1,0:T(8,128)(2,1)} %text_ref.1), channel_id=1, source_target_pairs={{0,24},{1,25},{2,26},{3,27},{4,28},{5,29},{6,30},{7,31},{8,16},{9,... | collective-permute-start | bytes 331784 | tf_op jit(solution)/shard_map/ppermute | solution.py:31
  9.2 8.7 %collective-permute-start.4 = (bf16[48,1152]{1,0:T(8,128)(2,1)}, bf16[48,1152]{1,0:T(8,128)(2,1)S(1)}, u32[]{:S(2)}, u32[]{:S(2)}) collective-permute-start(bf16[48,1152]{1,0:T(8,128)(2,1)} %text_ref.1), channel_id=1, source_target_pairs={{0,16},{1,17},{2,18},{3,19},{4,20},{5,21},{6,22},{7,23},{8,24},{9,... | collective-permute-start | bytes 331784 | tf_op jit(solution)/shard_map/ppermute | solution.py:31
  10.5 1.7 %copy-start.1 = (bf16[48,1152]{1,0:T(8,128)(2,1)S(1)}, bf16[48,1152]{1,0:T(8,128)(2,1)}, u32[]{:S(2)}) copy-start(bf16[48,1152]{1,0:T(8,128)(2,1)} %refs_0_.1) | copy-start | bytes 331780
  10.6 7.4 %collective-permute-start.5 = (bf16[48,1152]{1,0:T(8,128)(2,1)}, bf16[48,1152]{1,0:T(8,128)(2,1)S(1)}, u32[]{:S(2)}, u32[]{:S(2)}) collective-permute-start(bf16[48,1152]{1,0:T(8,128)(2,1)} %text_ref.1), channel_id=1, source_target_pairs={{0,8},{1,9},{2,10},{3,11},{4,12},{5,13},{6,14},{7,15},{8,0},{9,1},... | collective-permute-start | bytes 331784 | tf_op jit(solution)/shard_map/ppermute | solution.py:31
  11.2 0.9 %copy-start.2 = (bf16[48,1152]{1,0:T(8,128)(2,1)S(1)}, bf16[48,1152]{1,0:T(8,128)(2,1)}, u32[]{:S(2)}) copy-start(bf16[48,1152]{1,0:T(8,128)(2,1)} %text_ref.1) | copy-start | bytes 331780
  12.1 1.7 %copy-start = (bf16[1152,1152]{1,0:T(8,128)(2,1)S(1)}, bf16[1152,1152]{1,0:T(8,128)(2,1)}, u32[]{:S(2)}) copy-start(bf16[1152,1152]{1,0:T(8,128)(2,1)} %weight.1) | copy-start | bytes 7962628
  12.3 5.8 %collective-permute-start.6 = (bf16[192,1152]{1,0:T(8,128)(2,1)S(1)}, bf16[192,1152]{1,0:T(8,128)(2,1)S(1)}, u32[]{:S(2)}, u32[]{:S(2)}) collective-permute-start(bf16[192,1152]{1,0:T(8,128)(2,1)S(1)} %stack.1.feats_ref.own_half), channel_id=1, source_target_pairs={{0,1},{1,0},{2,3},{3,2},{4,5},{5,4},{6,7},{7,6},{8,9},{9,8},{10,11... | collective-permute-start | bytes 1327112 | tf_op jit(solution)/shard_map/ppermute | solution.py:31
  21.0 1.9 %collective-permute-start.7 = (bf16[4,160,384]{2,1,0:T(8,128)(2,1)S(1)}, bf16[4,160,384]{2,1,0:T(8,128)(2,1)S(1)}, u32[]{:S(2)}, u32[]{:S(2)}) collective-permute-start(bf16[4,160,384]{2,1,0:T(8,128)(2,1)S(1)} %get-tuple-element.52), channel_id=1, source_target_pairs={{0,1},{1,0},{2,3},{3,2},{4,5},{5,4},{6,7},{7,6},{8,9},{9,8},{10,11... | collective-permute-start | bytes 1474568 | tf_op jit(solution)/shard_map/ppermute | solution.py:31
  23.0 6.0 %collective-permute-start.8 = (bf16[160,384]{1,0:T(8,128)(2,1)S(1)}, bf16[160,384]{1,0:T(8,128)(2,1)S(1)}, u32[]{:S(2)}, u32[]{:S(2)}) collective-permute-start(bf16[160,384]{1,0:T(8,128)(2,1)S(1)} %get-tuple-element.62), channel_id=1, source_target_pairs={{0,2},{1,3},{2,0},{3,1},{4,6},{5,7},{6,4},{7,5},{8,10},{9,11},{10,... | collective-permute-start | bytes 368648 | tf_op jit(solution)/shard_map/ppermute | solution.py:31
  24.6 6.4 %collective-permute-start.9 = (bf16[160,384]{1,0:T(8,128)(2,1)S(1)}, bf16[160,384]{1,0:T(8,128)(2,1)S(1)}, u32[]{:S(2)}, u32[]{:S(2)}) collective-permute-start(bf16[160,384]{1,0:T(8,128)(2,1)S(1)} %get-tuple-element.63), channel_id=1, source_target_pairs={{0,4},{1,5},{2,6},{3,7},{4,0},{5,1},{6,2},{7,3},{8,12},{9,13},{10,... | collective-permute-start | bytes 368648 | tf_op jit(solution)/shard_map/ppermute | solution.py:31
  26.1 6.2 %collective-permute-start.10 = (bf16[160,384]{1,0:T(8,128)(2,1)S(1)}, bf16[160,384]{1,0:T(8,128)(2,1)S(1)}, u32[]{:S(2)}, u32[]{:S(2)}) collective-permute-start(bf16[160,384]{1,0:T(8,128)(2,1)S(1)} %get-tuple-element.64), channel_id=1, source_target_pairs={{0,6},{1,7},{2,4},{3,5},{4,2},{5,3},{6,0},{7,1},{8,14},{9,15},{10,... | collective-permute-start | bytes 368648 | tf_op jit(solution)/shard_map/ppermute | solution.py:31
  26.6 11.2 %collective-permute-start.11 = (bf16[48,1152]{1,0:T(8,128)(2,1)S(1)}, bf16[48,1152]{1,0:T(8,128)(2,1)S(1)}, u32[]{:S(2)}, u32[]{:S(2)}) collective-permute-start(bf16[48,1152]{1,0:T(8,128)(2,1)S(1)} %get-tuple-element.69), channel_id=1, source_target_pairs={{0,24},{1,25},{2,26},{3,27},{4,28},{5,29},{6,30},{7,31},{8,16},{9,... | collective-permute-start | bytes 331784 | tf_op jit(solution)/shard_map/ppermute | solution.py:31
  29.0 10.1 %collective-permute-start.12 = (bf16[48,1152]{1,0:T(8,128)(2,1)S(1)}, bf16[48,1152]{1,0:T(8,128)(2,1)S(1)}, u32[]{:S(2)}, u32[]{:S(2)}) collective-permute-start(bf16[48,1152]{1,0:T(8,128)(2,1)S(1)} %get-tuple-element.70), channel_id=1, source_target_pairs={{0,16},{1,17},{2,18},{3,19},{4,20},{5,21},{6,22},{7,23},{8,24},{9,... | collective-permute-start | bytes 331784 | tf_op jit(solution)/shard_map/ppermute | solution.py:31
  29.0 10.1 %collective-permute-start.13 = (bf16[48,1152]{1,0:T(8,128)(2,1)S(1)}, bf16[48,1152]{1,0:T(8,128)(2,1)S(1)}, u32[]{:S(2)}, u32[]{:S(2)}) collective-permute-start(bf16[48,1152]{1,0:T(8,128)(2,1)S(1)} %get-tuple-element.71), channel_id=1, source_target_pairs={{0,8},{1,9},{2,10},{3,11},{4,12},{5,13},{6,14},{7,15},{8,0},{9,1},... | collective-permute-start | bytes 331784 | tf_op jit(solution)/shard_map/ppermute | solution.py:31
  33.0 11.8 %collective-permute-start.14 = (bf16[176,128]{1,0:T(8,128)(2,1)S(1)}, bf16[176,128]{1,0:T(8,128)(2,1)S(1)}, u32[]{:S(2)}, u32[]{:S(2)}) collective-permute-start(bf16[176,128]{1,0:T(8,128)(2,1)S(1)} %get-tuple-element.73), channel_id=1, source_target_pairs={{0,28},{1,29},{2,30},{3,31},{4,24},{5,25},{6,26},{7,27},{8,20},{9,... | collective-permute-start | bytes 135176 | tf_op jit(solution)/shard_map/ppermute | solution.py:31
  36.4 9.3 %collective-permute-start.15 = (bf16[176,128]{1,0:T(8,128)(2,1)S(1)}, bf16[176,128]{1,0:T(8,128)(2,1)S(1)}, u32[]{:S(2)}, u32[]{:S(2)}) collective-permute-start(bf16[176,128]{1,0:T(8,128)(2,1)S(1)} %get-tuple-element.74), channel_id=1, source_target_pairs={{0,24},{1,25},{2,26},{3,27},{4,28},{5,29},{6,30},{7,31},{8,16},{9,... | collective-permute-start | bytes 135176 | tf_op jit(solution)/shard_map/ppermute | solution.py:31
  39.9 8.9 %collective-permute-start.16 = (bf16[176,128]{1,0:T(8,128)(2,1)S(1)}, bf16[176,128]{1,0:T(8,128)(2,1)S(1)}, u32[]{:S(2)}, u32[]{:S(2)}) collective-permute-start(bf16[176,128]{1,0:T(8,128)(2,1)S(1)} %get-tuple-element.75), channel_id=1, source_target_pairs={{0,20},{1,21},{2,22},{3,23},{4,16},{5,17},{6,18},{7,19},{8,28},{9,... | collective-permute-start | bytes 135176 | tf_op jit(solution)/shard_map/ppermute | solution.py:31
  41.2 7.6 %collective-permute-start.17 = (bf16[176,128]{1,0:T(8,128)(2,1)S(1)}, bf16[176,128]{1,0:T(8,128)(2,1)S(1)}, u32[]{:S(2)}, u32[]{:S(2)}) collective-permute-start(bf16[176,128]{1,0:T(8,128)(2,1)S(1)} %get-tuple-element.76), channel_id=1, source_target_pairs={{0,16},{1,17},{2,18},{3,19},{4,20},{5,21},{6,22},{7,23},{8,24},{9,... | collective-permute-start | bytes 135176 | tf_op jit(solution)/shard_map/ppermute | solution.py:31
  44.7 4.9 %collective-permute-start.18 = (bf16[176,128]{1,0:T(8,128)(2,1)S(1)}, bf16[176,128]{1,0:T(8,128)(2,1)S(1)}, u32[]{:S(2)}, u32[]{:S(2)}) collective-permute-start(bf16[176,128]{1,0:T(8,128)(2,1)S(1)} %get-tuple-element.77), channel_id=1, source_target_pairs={{0,12},{1,13},{2,14},{3,15},{4,8},{5,9},{6,10},{7,11},{8,4},{9,5},... | collective-permute-start | bytes 135176 | tf_op jit(solution)/shard_map/ppermute | solution.py:31
  44.7 4.9 %collective-permute-start.19 = (bf16[176,128]{1,0:T(8,128)(2,1)S(1)}, bf16[176,128]{1,0:T(8,128)(2,1)S(1)}, u32[]{:S(2)}, u32[]{:S(2)}) collective-permute-start(bf16[176,128]{1,0:T(8,128)(2,1)S(1)} %get-tuple-element.78), channel_id=1, source_target_pairs={{0,8},{1,9},{2,10},{3,11},{4,12},{5,13},{6,14},{7,15},{8,0},{9,1},... | collective-permute-start | bytes 135176 | tf_op jit(solution)/shard_map/ppermute | solution.py:31
  45.8 4.5 %collective-permute-start.20 = (bf16[176,128]{1,0:T(8,128)(2,1)S(1)}, bf16[176,128]{1,0:T(8,128)(2,1)S(1)}, u32[]{:S(2)}, u32[]{:S(2)}) collective-permute-start(bf16[176,128]{1,0:T(8,128)(2,1)S(1)} %get-tuple-element.79), channel_id=1, source_target_pairs={{0,4},{1,5},{2,6},{3,7},{4,0},{5,1},{6,2},{7,3},{8,12},{9,13},{10,... | collective-permute-start | bytes 135176 | tf_op jit(solution)/shard_map/ppermute | solution.py:31

commit v14 on v13

--- a/solution.py
+++ b/solution.py
@@ -191,11 +191,14 @@
         target[share:, :] = losses
 
 
-def caption_kernel(rows, grad_ref, emb_ref, feats_ref, feats_t, *outs):
+def caption_kernel(rows, grad_ref, emb_ref, *outs):
     for step, target in enumerate(outs):
         grad = grad_ref[step * rows : (step + 1) * rows, :]
         product = lax.dot_general(grad, emb_ref[...], NT, preferred_element_type=F32)
         target[...] = product.astype(target.dtype)
+
+
+def turn_kernel(feats_ref, feats_t):
     for start in range(0, feats_ref.shape[0], LANES):
         cols = slice(start, start + LANES)
         feats_t[:, cols] = feats_ref[cols, :].astype(F32).T.astype(BF16)
@@ -213,43 +216,31 @@
 
 
 def weight_kernel(group, wide, *refs):
-    wide_ref, own_ref = refs[:2]
-    got = refs[2 : 1 + group // 2]
-    inv_ref, feats_ref, feats_t_ref, loss_out, own_out = refs[1 + group // 2 : 6 + group // 2]
-    send_out = refs[6 + group // 2 : 5 + group // 2 + wide]
-    main_all, rest_all = refs[5 + group // 2 + wide :]
+    own_ref, got = refs[0], refs[1 : group // 2]
+    inv_ref, feats_ref, feats_t_ref, loss_out, send_out = refs[group // 2 :]
     rows = feats_t_ref.shape[0] // wide
     high, low = split_pair(gathered_gradient(own_ref, got, inv_ref, loss_out))
     rest = high.shape[0] - LANES
+    both = jnp.concatenate([high[LANES:, :], low[LANES:, :]], axis=0)
+    tail = jnp.dot(both, feats_ref[...], preferred_element_type=F32)
+    tail = (tail[:rest, :] + tail[rest:, :]).astype(BF16)
     both = jnp.concatenate([high[:LANES, :], low[:LANES, :]], axis=0)
     main = lax.dot_general(feats_t_ref[...], both, NT, preferred_element_type=F32)
-    main_all[...] = main[:, :LANES] + main[:, LANES:]
-    both = jnp.concatenate([high[LANES:, :], low[LANES:, :]], axis=0)
-    tail = jnp.dot(both, feats_ref[...], preferred_element_type=F32)
-    tail = tail[:rest, :] + tail[rest:, :]
+    main = (main[:, :LANES] + main[:, LANES:]).astype(BF16)
     for place in range(wide):
         begin = place * rows
-        rest_all[place, :rest, :] = tail[:, begin : begin + LANES]
-        rest_all[place, rest:, :] = jnp.zeros((rest, LANES), F32)
-        rest_all[place, rest:, : rows - LANES] = tail[:, begin + LANES : begin + rows]
-    for step in range(wide):
-        place = wide_ref[0] ^ step
-        target = own_out if step == 0 else send_out[step - 1]
-        target[:rows, :] = main_all[pl.ds(pl.multiple_of(place * rows, rows), rows), :].astype(target.dtype)
-        target[rows:, :] = rest_all[place].astype(target.dtype)
-
-
-def total_kernel(rest, wide_ref, *refs):
-    blocks, out = refs[:-1], refs[-1]
+        send_out[place, :rows, :] = main[begin : begin + rows, :]
+        send_out[place, rows : rows + rest, :] = tail[:, begin : begin + LANES]
+        send_out[place, rows + rest :, :] = jnp.zeros((rest, LANES), BF16)
+        send_out[place, rows + rest :, : rows - LANES] = tail[:, begin + LANES : begin + rows]
+
+
+def total_kernel(rest, got_ref, out):
     rows = out.shape[0]
-    same, other = blocks[0][...], blocks[1][...].astype(F32)
-    for block in blocks[2::2]:
-        same = same + block[...].astype(F32)
-    for block in blocks[3::2]:
-        other = other + block[...].astype(F32)
-    left_is_same = wide_ref[0] % 2 == 0
-    halves = (jnp.where(left_is_same, same, other), jnp.where(left_is_same, other, same))
-    for side, half in enumerate(halves):
+    for side in range(2):
+        half = got_ref[side].astype(F32)
+        for place in range(side + 2, got_ref.shape[0], 2):
+            half = half + got_ref[place].astype(F32)
         left = side * (LANES + rest)
         out[:, left : left + LANES] = half[:rows, :]
         out[:LANES, left + LANES : left + LANES + rest] = half[rows : rows + rest, :].T
@@ -261,6 +252,18 @@
     for block in refs[1:-1]:
         total = total + block[...].astype(F32)
     refs[-1][...] = total
+
+
+def add_text(own, parts, cost):
+    return pl.pallas_call(
+        sum_kernel,
+        in_specs=[VMEM] * (1 + len(parts)),
+        out_specs=VMEM,
+        out_shape=jax.ShapeDtypeStruct(own.shape, F32),
+        compiler_params=limit(12),
+        cost_estimate=cost,
+        name="caption_sum",
+    )(own, *parts)
 
 
 def local(wide, narrow, image_feats, proj_weight, text_embed, log_scale, logit_bias):
@@ -333,16 +336,26 @@
     )(member, scalars, proj_weight, own_half, own_proj, got_half, text_emb)
     all_feats, inv_part, img_emb, grad_tile, own_part, sent_part = results
     got_part = swapped(sent_part, total, 1)
-    feats_t, own_text, *sent_text = pl.pallas_call(
+    own_text, *sent_text = pl.pallas_call(
         functools.partial(caption_kernel, rows),
-        in_specs=[VMEM] * 3,
-        out_specs=[VMEM] * (1 + spread),
-        out_shape=[jax.ShapeDtypeStruct((width, images), BF16), jax.ShapeDtypeStruct((rows, width), F32)]
+        in_specs=[VMEM] * 2,
+        out_specs=[VMEM] * spread,
+        out_shape=[jax.ShapeDtypeStruct((rows, width), F32)]
         + [jax.ShapeDtypeStruct((rows, width), BF16)] * (spread - 1),
         compiler_params=limit(12 if spread <= 4 else 24),
         name="captions",
-    )(grad_tile, img_emb, all_feats)
-    own_part, got_part, sent_text = lax.optimization_barrier((own_part, got_part, sent_text))
+    )(grad_tile, img_emb)
+    feats_t = pl.pallas_call(
+        turn_kernel,
+        in_specs=[VMEM],
+        out_specs=VMEM,
+        out_shape=jax.ShapeDtypeStruct((width, images), BF16),
+        compiler_params=limit(8),
+        name="turn",
+    )(all_feats)
+    own_part, got_part, feats_t, sent_text[:1], sent_text[2:] = lax.optimization_barrier(
+        (own_part, got_part, feats_t, sent_text[:1], sent_text[2:])
+    )
     got_text = [swapped(value, total, step * group) for step, value in enumerate(sent_text, 1)]
     own_part, *chip_parts = pl.pallas_call(
         chip_kernel,
@@ -354,33 +367,34 @@
         name="chip_sum",
     )(own_part, got_part)
     got = [swapped(value, total, 2 * index) for index, value in enumerate(chip_parts, 1)]
+    own_text = add_text(own_text, got_text[1:2], hint(10**10))
+    own_text, got = lax.optimization_barrier((own_text, got))
 
     out_rows = width // wide
     rest = share - LANES
     packed = out_rows + 2 * rest
     direct = LANES < out_rows <= 2 * LANES and out_rows % 16 == 0 and rest % 16 == 0
     if direct:
-        wide_pos = lax.axis_index(AXES[:2]).astype(jnp.int32).reshape(1)
-        loss_line, own_weight, *sent_weight = pl.pallas_call(
+        loss_line, sent_weight = pl.pallas_call(
             functools.partial(weight_kernel, group, wide),
-            in_specs=[SMEM] + [VMEM] * (3 + group // 2),
-            out_specs=[VMEM] * (1 + wide),
-            out_shape=[jax.ShapeDtypeStruct((1, images), F32), jax.ShapeDtypeStruct((packed, LANES), F32)]
-            + [jax.ShapeDtypeStruct((packed, LANES), BF16)] * (wide - 1),
-            scratch_shapes=[pltpu.VMEM((width, LANES), F32), pltpu.VMEM((wide, 2 * rest, LANES), F32)],
+            in_specs=[VMEM] * (3 + group // 2),
+            out_specs=[VMEM] * 2,
+            out_shape=[
+                jax.ShapeDtypeStruct((1, images), F32),
+                jax.ShapeDtypeStruct((wide, packed, LANES), BF16),
+            ],
             compiler_params=limit(12),
             name="weights",
-        )(wide_pos, own_part, *got, inv_part, all_feats, feats_t)
-        got_weight = [swapped(value, total, step * narrow) for step, value in enumerate(sent_weight, 1)]
-        got_weight = lax.optimization_barrier(got_weight[::-1])[::-1]
+        )(own_part, *got, inv_part, all_feats, feats_t)
+        got_weight = lax.all_to_all(sent_weight, AXES[:2], 0, 0)
         d_proj = pl.pallas_call(
             functools.partial(total_kernel, rest),
-            in_specs=[SMEM] + [VMEM] * wide,
+            in_specs=[VMEM],
             out_specs=VMEM,
             out_shape=jax.ShapeDtypeStruct((out_rows, 2 * share), F32),
             compiler_params=limit(4),
             name="weight_total",
-        )(wide_pos, own_weight, *got_weight)
+        )(got_weight)
     else:
 
         def gradient_kernel(*refs):
@@ -403,15 +417,7 @@
         both = jnp.concatenate([jnp.where(left, partial, 0.0), jnp.where(left, 0.0, partial)], axis=1)
         d_proj = lax.psum_scatter(both, AXES[:2], scatter_dimension=0, tiled=True)
 
-    d_text_unit = pl.pallas_call(
-        sum_kernel,
-        in_specs=[VMEM] * spread,
-        out_specs=VMEM,
-        out_shape=jax.ShapeDtypeStruct((rows, width), F32),
-        compiler_params=limit(12),
-        cost_estimate=hint(5 * 10**9),
-        name="caption_total",
-    )(own_text, *got_text[::-1])
+    d_text_unit = add_text(own_text, [*got_text[:1:-1], *got_text[:1]], hint(5 * 10**9))
     image_loss = lax.dynamic_slice_in_dim(loss_line[0], first_image(member[0], rows, group), rows, 0)
     return (image_loss, d_text_unit, d_proj)
 

time: 51.3 us -> 55 us (1.072)
  waiting for transfers between devices: 8.01 us -> 19 us
  starting transfers between devices: 30.4 us -> 22 us
  Pallas kernels: 7.64 us -> 8.57 us
    ppermute x21 -> x14, starting transfers between devices: 30.4 us -> 17.4 us  [swapped(): lax.ppermute(value, AXES, [(source, source ^ mask) for source in range(to...]
    ppermute x21 -> x14, waiting for transfers between devices: 8.01 us -> 18.7 us  [swapped(): lax.ppermute(value, AXES, [(source, source ^ mask) for source in range(to...]
    all_to_all x0 -> x1, starting transfers between devices: none -> 4.69 us  [local(): got_weight = lax.all_to_all(sent_weight, AXES[:2], 0, 0)]
    pallas_call x3 -> x5, Pallas kernels: 2.33 us -> 3.3 us  [the longest x1 1.38 us: local(): pl.pallas_call(functools.partial(weight_kernel, group, wide), in_specs=[V...]
  transfers between devices with their start and end apart: 21 -> 15, of which waited for: 6 -> 6; matrix products, arithmetic and copies ran while one was open for 1% -> 1% of each run, Pallas kernels for 7% -> 6%
where the time goes in v14:
time: 55 us; the launch traced here: 54.7 us
  starting transfers between devices  22 us (40%)
  waiting for transfers between devices  19 us (35%)
  Pallas kernels  8.57 us (16%)
  local copies, waits for them, and re-layouts  2.98 us (5%)
  between operations  2.09 us (4%)
    ppermute x14, waiting for transfers between devices, swapped(): lax.ppermute(value, AXES, [(source, source ^ mask) for source in range(to...  18.7 us
    ppermute x14, starting transfers between devices, swapped(): lax.ppermute(value, AXES, [(source, source ^ mask) for source in range(to...  17.4 us
    all_to_all x1, starting transfers between devices, local(): got_weight = lax.all_to_all(sent_weight, AXES[:2], 0, 0)  4.69 us
    pallas_call x1, Pallas kernels, local(): pl.pallas_call(functools.partial(pair_kernel, narrow, group), in_specs=[S...  2.89 us
    unnamed x6, local copies, waits for them, and re-layouts  2.4 us
    pallas_call x1, Pallas kernels, local(): pl.pallas_call(functools.partial(weight_kernel, group, wide), in_specs=[V...  1.38 us
    pallas_call x1, Pallas kernels, local(): pl.pallas_call(functools.partial(caption_kernel, rows), in_specs=[VMEM] *...  1.19 us
  transfers between devices with their start and end apart: 15, of which 6 were waited for; matrix products, arithmetic and copies ran while one was open for 1% of the time, Pallas kernels for 6%

profile of v14, /device:TPU:0, one launch (start us, length us, event | category | flops | bytes accessed | tf_op | source)
XLA Modules:
  0.0 54.7 jit_solution(6934822941358252002)
XLA Ops:
  0.6 3.0 %collective-permute-start = (bf16[48,1152]{1,0:T(8,128)(2,1)}, bf16[48,1152]{1,0:T(8,128)(2,1)S(1)}, u32[]{:S(2)}, u32[]{:S(2)}) collective-permute-start(bf16[48,1152]{1,0:T(8,128)(2,1)} %refs_0_.1), channel_id=1, source_target_pairs={{0,2},{1,3},{2,0},{3,1},{4,6},{5,7},{6,4},{7,5},{8,10},{9,11},{10,... | collective-permute-start | bytes 331784 | tf_op jit(solution)/shard_map/ppermute | solution.py:31
  3.7 1.5 %collective-permute-start.1 = (bf16[48,1152]{1,0:T(8,128)(2,1)}, bf16[48,1152]{1,0:T(8,128)(2,1)S(1)}, u32[]{:S(2)}, u32[]{:S(2)}) collective-permute-start(bf16[48,1152]{1,0:T(8,128)(2,1)} %refs_0_.1), channel_id=1, source_target_pairs={{0,4},{1,5},{2,6},{3,7},{4,0},{5,1},{6,2},{7,3},{8,12},{9,13},{10,... | collective-permute-start | bytes 331784 | tf_op jit(solution)/shard_map/ppermute | solution.py:31
  5.2 4.0 %collective-permute-start.3 = (bf16[48,1152]{1,0:T(8,128)(2,1)}, bf16[48,1152]{1,0:T(8,128)(2,1)S(1)}, u32[]{:S(2)}, u32[]{:S(2)}) collective-permute-start(bf16[48,1152]{1,0:T(8,128)(2,1)} %text_ref.1), channel_id=1, source_target_pairs={{0,24},{1,25},{2,26},{3,27},{4,28},{5,29},{6,30},{7,31},{8,16},{9,... | collective-permute-start | bytes 331784 | tf_op jit(solution)/shard_map/ppermute | solution.py:31
  10.6 0.6 %collective-permute-start.5 = (bf16[48,1152]{1,0:T(8,128)(2,1)}, bf16[48,1152]{1,0:T(8,128)(2,1)S(1)}, u32[]{:S(2)}, u32[]{:S(2)}) collective-permute-start(bf16[48,1152]{1,0:T(8,128)(2,1)} %text_ref.1), channel_id=1, source_target_pairs={{0,8},{1,9},{2,10},{3,11},{4,12},{5,13},{6,14},{7,15},{8,0},{9,1},... | collective-permute-start | bytes 331784 | tf_op jit(solution)/shard_map/ppermute | solution.py:31
  11.2 0.9 %copy-done.2 = bf16[48,1152]{1,0:T(8,128)(2,1)S(1)} copy-done((bf16[48,1152]{1,0:T(8,128)(2,1)S(1)}, bf16[48,1152]{1,0:T(8,128)(2,1)}, u32[]{:S(2)}) %copy-start.2) | copy-done | bytes 110616
  12.4 1.5 %copy-done = bf16[1152,1152]{1,0:T(8,128)(2,1)S(1)} copy-done((bf16[1152,1152]{1,0:T(8,128)(2,1)S(1)}, bf16[1152,1152]{1,0:T(8,128)(2,1)}, u32[]{:S(2)}) %copy-start) | copy-done | bytes 2654232
  13.9 0.8 %own_projection.1.own_proj = f32[192,1152]{1,0:T(8,128)S(1)} custom-call(bf16[192,1152]{1,0:T(8,128)(2,1)S(1)} %stack.1.feats_ref.own_half, bf16[1152,1152]{1,0:T(8,128)(2,1)S(1)} %copy-done), custom_call_target="tpu_custom_call" | custom-call | tf_op jit(solution)/shard_map/own_projection/pallas_call | solution.py:298
  14.7 3.3 %collective-permute-done.4.refs_2_ = bf16[48,1152]{1,0:T(8,128)(2,1)S(1)} collective-permute-done((bf16[48,1152]{1,0:T(8,128)(2,1)}, bf16[48,1152]{1,0:T(8,128)(2,1)S(1)}, u32[]{:S(2)}, u32[]{:S(2)}) %collective-permute-start.4) | collective-permute-done | bytes 110624 | tf_op jit(solution)/shard_map/ppermute | solution.py:31
  18.1 2.9 %pairs.1 = (bf16[384,1152]{1,0:T(8,128)(2,1)S(1)}, f32[1,384]{1,0:T(1,128)S(1)}, bf16[1152,384]{1,0:T(8,128)(2,1)S(1)}, bf16[192,384]{1,0:T(8,128)(2,1)S(1)}, f3...) custom-call(s32[1]{0:T(128)} %bitcast.member_ref, f32[8,128]{1,0:T(8,128)S(1)} %get-tuple-element.34.scalars_ref, ...), custom_call_target="tpu_custom_call" | custom-call | tf_op jit(solution)/shard_map/pairs/pallas_call | solution.py:317
  21.1 1.2 %captions.1 = (f32[48,1152]{1,0:T(8,128)S(1)}, bf16[48,1152]{1,0:T(8,128)(2,1)S(1)}, bf16[48,1152]{1,0:T(8,128)(2,1)S(1)}, bf16[48,1152]{1,0:T(8,128)(2,1)S(1)}) custom-call(bf16[192,384]{1,0:T(8,128)(2,1)S(1)} %get-tuple-element.43.grad_ref, bf16[1152,384]{1,0:T(8,128)(2,1)S(1)} %get-tuple-element.44.emb_ref), custom_call_target="tpu_custom_call" | custom-call | tf_op jit(solution)/shard_map/captions/pallas_call | solution.py:339
  22.3 0.6 %collective-permute-start.8 = (bf16[48,1152]{1,0:T(8,128)(2,1)S(1)}, bf16[48,1152]{1,0:T(8,128)(2,1)S(1)}, u32[]{:S(2)}, u32[]{:S(2)}) collective-permute-start(bf16[48,1152]{1,0:T(8,128)(2,1)S(1)} %get-tuple-element.51), channel_id=1, source_target_pairs={{0,16},{1,17},{2,18},{3,19},{4,20},{5,21},{6,22},{7,23},{8,24},{9,... | collective-permute-start | bytes 331784 | tf_op jit(solution)/shard_map/ppermute | solution.py:31
  23.3 1.6 %collective-permute-start.10 = (bf16[160,384]{1,0:T(8,128)(2,1)S(1)}, bf16[160,384]{1,0:T(8,128)(2,1)S(1)}, u32[]{:S(2)}, u32[]{:S(2)}) collective-permute-start(bf16[160,384]{1,0:T(8,128)(2,1)S(1)} %get-tuple-element.53), channel_id=1, source_target_pairs={{0,4},{1,5},{2,6},{3,7},{4,0},{5,1},{6,2},{7,3},{8,12},{9,13},{10,... | collective-permute-start | bytes 368648 | tf_op jit(solution)/shard_map/ppermute | solution.py:31
  24.9 1.5 %collective-permute-start.11 = (bf16[160,384]{1,0:T(8,128)(2,1)S(1)}, bf16[160,384]{1,0:T(8,128)(2,1)S(1)}, u32[]{:S(2)}, u32[]{:S(2)}) collective-permute-start(bf16[160,384]{1,0:T(8,128)(2,1)S(1)} %get-tuple-element.54), channel_id=1, source_target_pairs={{0,6},{1,7},{2,4},{3,5},{4,2},{5,3},{6,0},{7,1},{8,14},{9,15},{10,... | collective-permute-start | bytes 368648 | tf_op jit(solution)/shard_map/ppermute | solution.py:31
  26.4 0.5 collective-permute-start.9
  26.9 4.0 %collective-permute-done.8.refs_1_ = bf16[48,1152]{1,0:T(8,128)(2,1)S(1)} collective-permute-done((bf16[48,1152]{1,0:T(8,128)(2,1)S(1)}, bf16[48,1152]{1,0:T(8,128)(2,1)S(1)}, u32[]{:S(2)}, u32[]{:S(2)}) %collective-permute-start.8) | collective-permute-done | bytes 110624 | tf_op jit(solution)/shard_map/ppermute | solution.py:31
  30.9 1.6 %collective-permute-done.11.refs_3_ = bf16[160,384]{1,0:T(8,128)(2,1)S(1)} collective-permute-done((bf16[160,384]{1,0:T(8,128)(2,1)S(1)}, bf16[160,384]{1,0:T(8,128)(2,1)S(1)}, u32[]{:S(2)}, u32[]{:S(2)}) %collective-permute-start.11) | collective-permute-done | bytes 122912 | tf_op jit(solution)/shard_map/ppermute | solution.py:31
  32.5 1.4 %collective-permute-done.9.refs_1_ = bf16[160,384]{1,0:T(8,128)(2,1)S(1)} collective-permute-done((bf16[160,384]{1,0:T(8,128)(2,1)S(1)}, bf16[160,384]{1,0:T(8,128)(2,1)S(1)}, u32[]{:S(2)}, u32[]{:S(2)}) %collective-permute-start.9) | collective-permute-done | bytes 122912 | tf_op jit(solution)/shard_map/ppermute | solution.py:31
  33.9 1.4 %weights.1 = (f32[1,384]{1,0:T(1,128)S(1)}, bf16[8,176,128]{2,1,0:T(8,128)(2,1)}) custom-call(f32[152,384]{1,0:T(8,128)S(1)} %get-tuple-element.49.refs_0_, bf16[160,384]{1,0:T(8,128)(2,1)S(1)} %collective-permute-done.9.refs_1_, bf16[160,384]{1,0:T(8,128)(2,1)S(1)} %collective-permute-done.10.refs_2_, bf16[160,384]{1,0:T(8,128)(2,1)S(1)} %collective-permute-done.11.refs_3_, ...), custom_call_target="tpu_custom_call" | custom-call | tf_op jit(solution)/shard_map/weights/pallas_call | solution.py:378
  35.3 4.7 %all-to-all-start = ((bf16[8,176,128]{2,1,0:T(8,128)(2,1)}), bf16[8,176,128]{2,1,0:T(8,128)(2,1)S(1)}, u32[]{:S(2)}, u32[]{:S(2)}) async-start(bf16[8,176,128]{2,1,0:T(8,128)(2,1)} %get-tuple-element.64), calls=%async_computation | async-start | bytes 720896 | tf_op jit(solution)/shard_map/all_to_all | solution.py:389
  39.9 3.8 %collective-permute-start.12 = (bf16[48,1152]{1,0:T(8,128)(2,1)S(1)}, bf16[48,1152]{1,0:T(8,128)(2,1)S(1)}, u32[]{:S(2)}, u32[]{:S(2)}) collective-permute-start(bf16[48,1152]{1,0:T(8,128)(2,1)S(1)} %get-tuple-element.62), channel_id=1, source_target_pairs={{0,24},{1,25},{2,26},{3,27},{4,28},{5,29},{6,30},{7,31},{8,16},{9,... | collective-permute-start | bytes 331784 | tf_op jit(solution)/shard_map/ppermute | solution.py:31
  43.8 0.6 %dynamic-slice_bitcast_fusion = f32[48]{0:T(128)} fusion(f32[1,384]{1,0:T(1,128)S(1)} %get-tuple-element.60, s32[]{:T(128)S(6)} %select_n.16), kind=kLoop, calls=%fused_computation | loop fusion | bytes 388 | tf_op jit(solution)/shard_map/dynamic_slice | solution.py:421
  44.3 8.4 %collective-permute-done.12.refs_1_ = bf16[48,1152]{1,0:T(8,128)(2,1)S(1)} collective-permute-done((bf16[48,1152]{1,0:T(8,128)(2,1)S(1)}, bf16[48,1152]{1,0:T(8,128)(2,1)S(1)}, u32[]{:S(2)}, u32[]{:S(2)}) %collective-permute-start.12) | collective-permute-done | bytes 110624 | tf_op jit(solution)/shard_map/ppermute | solution.py:31
  52.8 0.7 %caption_sum.3 = f32[48,1152]{1,0:T(8,128)} custom-call(f32[48,1152]{1,0:T(8,128)S(1)} %caption_sum.2.refs_0_, bf16[48,1152]{1,0:T(8,128)(2,1)S(1)} %collective-permute-done.12.refs_1_, bf16[48,1152]{1,0:T(8,128)(2,1)S(1)} %collective-permute-done.13.refs_2_), custom_call_target="tpu_custom_call" | custom-call | flops 5000000000 | tf_op jit(solution)/shard_map/caption_sum/pallas_call | solution.py:258
  53.8 0.9 %weight_total.1 = f32[144,288]{1,0:T(8,128)} custom-call(bf16[8,176,128]{2,1,0:T(8,128)(2,1)S(1)} %all-to-all-done.got_ref), custom_call_target="tpu_custom_call" | custom-call | tf_op jit(solution)/shard_map/weight_total/pallas_call | solution.py:390
  (25 shorter events, 1.2 us)
Async XLA Ops:
  0.6 9.9 %collective-permute-start = (bf16[48,1152]{1,0:T(8,128)(2,1)}, bf16[48,1152]{1,0:T(8,128)(2,1)S(1)}, u32[]{:S(2)}, u32[]{:S(2)}) collective-permute-start(bf16[48,1152]{1,0:T(8,128)(2,1)} %refs_0_.1), channel_id=1, source_target_pairs={{0,2},{1,3},{2,0},{3,1},{4,6},{5,7},{6,4},{7,5},{8,10},{9,11},{10,... | collective-permute-start | bytes 331784 | tf_op jit(solution)/shard_map/ppermute | solution.py:31
  3.7 8.6 %collective-permute-start.1 = (bf16[48,1152]{1,0:T(8,128)(2,1)}, bf16[48,1152]{1,0:T(8,128)(2,1)S(1)}, u32[]{:S(2)}, u32[]{:S(2)}) collective-permute-start(bf16[48,1152]{1,0:T(8,128)(2,1)} %refs_0_.1), channel_id=1, source_target_pairs={{0,4},{1,5},{2,6},{3,7},{4,0},{5,1},{6,2},{7,3},{8,12},{9,13},{10,... | collective-permute-start | bytes 331784 | tf_op jit(solution)/shard_map/ppermute | solution.py:31
  5.2 7.1 %collective-permute-start.2 = (bf16[48,1152]{1,0:T(8,128)(2,1)}, bf16[48,1152]{1,0:T(8,128)(2,1)S(1)}, u32[]{:S(2)}, u32[]{:S(2)}) collective-permute-start(bf16[48,1152]{1,0:T(8,128)(2,1)} %refs_0_.1), channel_id=1, source_target_pairs={{0,6},{1,7},{2,4},{3,5},{4,2},{5,3},{6,0},{7,1},{8,14},{9,15},{10,... | collective-permute-start | bytes 331784 | tf_op jit(solution)/shard_map/ppermute | solution.py:31
  5.2 9.5 %collective-permute-start.3 = (bf16[48,1152]{1,0:T(8,128)(2,1)}, bf16[48,1152]{1,0:T(8,128)(2,1)S(1)}, u32[]{:S(2)}, u32[]{:S(2)}) collective-permute-start(bf16[48,1152]{1,0:T(8,128)(2,1)} %text_ref.1), channel_id=1, source_target_pairs={{0,24},{1,25},{2,26},{3,27},{4,28},{5,29},{6,30},{7,31},{8,16},{9,... | collective-permute-start | bytes 331784 | tf_op jit(solution)/shard_map/ppermute | solution.py:31
  9.2 8.7 %collective-permute-start.4 = (bf16[48,1152]{1,0:T(8,128)(2,1)}, bf16[48,1152]{1,0:T(8,128)(2,1)S(1)}, u32[]{:S(2)}, u32[]{:S(2)}) collective-permute-start(bf16[48,1152]{1,0:T(8,128)(2,1)} %text_ref.1), channel_id=1, source_target_pairs={{0,16},{1,17},{2,18},{3,19},{4,20},{5,21},{6,22},{7,23},{8,24},{9,... | collective-permute-start | bytes 331784 | tf_op jit(solution)/shard_map/ppermute | solution.py:31
  10.5 1.7 %copy-start.1 = (bf16[48,1152]{1,0:T(8,128)(2,1)S(1)}, bf16[48,1152]{1,0:T(8,128)(2,1)}, u32[]{:S(2)}) copy-start(bf16[48,1152]{1,0:T(8,128)(2,1)} %refs_0_.1) | copy-start | bytes 331780
  10.6 7.4 %collective-permute-start.5 = (bf16[48,1152]{1,0:T(8,128)(2,1)}, bf16[48,1152]{1,0:T(8,128)(2,1)S(1)}, u32[]{:S(2)}, u32[]{:S(2)}) collective-permute-start(bf16[48,1152]{1,0:T(8,128)(2,1)} %text_ref.1), channel_id=1, source_target_pairs={{0,8},{1,9},{2,10},{3,11},{4,12},{5,13},{6,14},{7,15},{8,0},{9,1},... | collective-permute-start | bytes 331784 | tf_op jit(solution)/shard_map/ppermute | solution.py:31
  11.2 0.9 %copy-start.2 = (bf16[48,1152]{1,0:T(8,128)(2,1)S(1)}, bf16[48,1152]{1,0:T(8,128)(2,1)}, u32[]{:S(2)}) copy-start(bf16[48,1152]{1,0:T(8,128)(2,1)} %text_ref.1) | copy-start | bytes 331780
  12.1 1.7 %copy-start = (bf16[1152,1152]{1,0:T(8,128)(2,1)S(1)}, bf16[1152,1152]{1,0:T(8,128)(2,1)}, u32[]{:S(2)}) copy-start(bf16[1152,1152]{1,0:T(8,128)(2,1)} %weight.1) | copy-start | bytes 7962628
  12.3 5.8 %collective-permute-start.6 = (bf16[192,1152]{1,0:T(8,128)(2,1)S(1)}, bf16[192,1152]{1,0:T(8,128)(2,1)S(1)}, u32[]{:S(2)}, u32[]{:S(2)}) collective-permute-start(bf16[192,1152]{1,0:T(8,128)(2,1)S(1)} %stack.1.feats_ref.own_half), channel_id=1, source_target_pairs={{0,1},{1,0},{2,3},{3,2},{4,5},{5,4},{6,7},{7,6},{8,9},{9,8},{10,11... | collective-permute-start | bytes 1327112 | tf_op jit(solution)/shard_map/ppermute | solution.py:31
  21.0 2.2 %collective-permute-start.7 = (bf16[4,160,384]{2,1,0:T(8,128)(2,1)S(1)}, bf16[4,160,384]{2,1,0:T(8,128)(2,1)S(1)}, u32[]{:S(2)}, u32[]{:S(2)}) collective-permute-start(bf16[4,160,384]{2,1,0:T(8,128)(2,1)S(1)} %get-tuple-element.41), channel_id=1, source_target_pairs={{0,1},{1,0},{2,3},{3,2},{4,5},{5,4},{6,7},{7,6},{8,9},{9,8},{10,11... | collective-permute-start | bytes 1474568 | tf_op jit(solution)/shard_map/ppermute | solution.py:31
  22.3 8.6 %collective-permute-start.8 = (bf16[48,1152]{1,0:T(8,128)(2,1)S(1)}, bf16[48,1152]{1,0:T(8,128)(2,1)S(1)}, u32[]{:S(2)}, u32[]{:S(2)}) collective-permute-start(bf16[48,1152]{1,0:T(8,128)(2,1)S(1)} %get-tuple-element.51), channel_id=1, source_target_pairs={{0,16},{1,17},{2,18},{3,19},{4,20},{5,21},{6,22},{7,23},{8,24},{9,... | collective-permute-start | bytes 331784 | tf_op jit(solution)/shard_map/ppermute | solution.py:31
  23.3 7.6 %collective-permute-start.10 = (bf16[160,384]{1,0:T(8,128)(2,1)S(1)}, bf16[160,384]{1,0:T(8,128)(2,1)S(1)}, u32[]{:S(2)}, u32[]{:S(2)}) collective-permute-start(bf16[160,384]{1,0:T(8,128)(2,1)S(1)} %get-tuple-element.53), channel_id=1, source_target_pairs={{0,4},{1,5},{2,6},{3,7},{4,0},{5,1},{6,2},{7,3},{8,12},{9,13},{10,... | collective-permute-start | bytes 368648 | tf_op jit(solution)/shard_map/ppermute | solution.py:31
  24.9 7.6 %collective-permute-start.11 = (bf16[160,384]{1,0:T(8,128)(2,1)S(1)}, bf16[160,384]{1,0:T(8,128)(2,1)S(1)}, u32[]{:S(2)}, u32[]{:S(2)}) collective-permute-start(bf16[160,384]{1,0:T(8,128)(2,1)S(1)} %get-tuple-element.54), channel_id=1, source_target_pairs={{0,6},{1,7},{2,4},{3,5},{4,2},{5,3},{6,0},{7,1},{8,14},{9,15},{10,... | collective-permute-start | bytes 368648 | tf_op jit(solution)/shard_map/ppermute | solution.py:31
  26.4 7.5 %collective-permute-start.9 = (bf16[160,384]{1,0:T(8,128)(2,1)S(1)}, bf16[160,384]{1,0:T(8,128)(2,1)S(1)}, u32[]{:S(2)}, u32[]{:S(2)}) collective-permute-start(bf16[160,384]{1,0:T(8,128)(2,1)S(1)} %get-tuple-element.52), channel_id=1, source_target_pairs={{0,2},{1,3},{2,0},{3,1},{4,6},{5,7},{6,4},{7,5},{8,10},{9,11},{10,... | collective-permute-start | bytes 368648 | tf_op jit(solution)/shard_map/ppermute | solution.py:31
  35.3 18.5 %all-to-all-start = ((bf16[8,176,128]{2,1,0:T(8,128)(2,1)}), bf16[8,176,128]{2,1,0:T(8,128)(2,1)S(1)}, u32[]{:S(2)}, u32[]{:S(2)}) async-start(bf16[8,176,128]{2,1,0:T(8,128)(2,1)} %get-tuple-element.64), calls=%async_computation | async-start | bytes 720896 | tf_op jit(solution)/shard_map/all_to_all | solution.py:389
  39.9 12.8 %collective-permute-start.12 = (bf16[48,1152]{1,0:T(8,128)(2,1)S(1)}, bf16[48,1152]{1,0:T(8,128)(2,1)S(1)}, u32[]{:S(2)}, u32[]{:S(2)}) collective-permute-start(bf16[48,1152]{1,0:T(8,128)(2,1)S(1)} %get-tuple-element.62), channel_id=1, source_target_pairs={{0,24},{1,25},{2,26},{3,27},{4,28},{5,29},{6,30},{7,31},{8,16},{9,... | collective-permute-start | bytes 331784 | tf_op jit(solution)/shard_map/ppermute | solution.py:31
  43.8 9.0 %collective-permute-start.13 = (bf16[48,1152]{1,0:T(8,128)(2,1)S(1)}, bf16[48,1152]{1,0:T(8,128)(2,1)S(1)}, u32[]{:S(2)}, u32[]{:S(2)}) collective-permute-start(bf16[48,1152]{1,0:T(8,128)(2,1)S(1)} %get-tuple-element.63), channel_id=1, source_target_pairs={{0,8},{1,9},{2,10},{3,11},{4,12},{5,13},{6,14},{7,15},{8,0},{9,1},... | collective-permute-start | bytes 331784 | tf_op jit(solution)/shard_map/ppermute | solution.py:31

commit v15 on v14

--- a/solution.py
+++ b/solution.py
@@ -191,14 +191,10 @@
         target[share:, :] = losses
 
 
-def caption_kernel(rows, grad_ref, emb_ref, *outs):
+def caption_kernel(rows, grad_ref, emb_ref, feats_ref, feats_t, *outs):
+    product = lax.dot_general(grad_ref[...], emb_ref[...], NT, preferred_element_type=F32)
     for step, target in enumerate(outs):
-        grad = grad_ref[step * rows : (step + 1) * rows, :]
-        product = lax.dot_general(grad, emb_ref[...], NT, preferred_element_type=F32)
-        target[...] = product.astype(target.dtype)
-
-
-def turn_kernel(feats_ref, feats_t):
+        target[...] = product[step * rows : (step + 1) * rows, :].astype(target.dtype)
     for start in range(0, feats_ref.shape[0], LANES):
         cols = slice(start, start + LANES)
         feats_t[:, cols] = feats_ref[cols, :].astype(F32).T.astype(BF16)
@@ -252,18 +248,6 @@
     for block in refs[1:-1]:
         total = total + block[...].astype(F32)
     refs[-1][...] = total
-
-
-def add_text(own, parts, cost):
-    return pl.pallas_call(
-        sum_kernel,
-        in_specs=[VMEM] * (1 + len(parts)),
-        out_specs=VMEM,
-        out_shape=jax.ShapeDtypeStruct(own.shape, F32),
-        compiler_params=limit(12),
-        cost_estimate=cost,
-        name="caption_sum",
-    )(own, *parts)
 
 
 def local(wide, narrow, image_feats, proj_weight, text_embed, log_scale, logit_bias):
@@ -336,26 +320,16 @@
     )(member, scalars, proj_weight, own_half, own_proj, got_half, text_emb)
     all_feats, inv_part, img_emb, grad_tile, own_part, sent_part = results
     got_part = swapped(sent_part, total, 1)
-    own_text, *sent_text = pl.pallas_call(
+    feats_t, own_text, *sent_text = pl.pallas_call(
         functools.partial(caption_kernel, rows),
-        in_specs=[VMEM] * 2,
-        out_specs=[VMEM] * spread,
-        out_shape=[jax.ShapeDtypeStruct((rows, width), F32)]
+        in_specs=[VMEM] * 3,
+        out_specs=[VMEM] * (1 + spread),
+        out_shape=[jax.ShapeDtypeStruct((width, images), BF16), jax.ShapeDtypeStruct((rows, width), F32)]
         + [jax.ShapeDtypeStruct((rows, width), BF16)] * (spread - 1),
-        compiler_params=limit(12 if spread <= 4 else 24),
+        compiler_params=limit(12 if spread <= 4 else 32),
         name="captions",
-    )(grad_tile, img_emb)
-    feats_t = pl.pallas_call(
-        turn_kernel,
-        in_specs=[VMEM],
-        out_specs=VMEM,
-        out_shape=jax.ShapeDtypeStruct((width, images), BF16),
-        compiler_params=limit(8),
-        name="turn",
-    )(all_feats)
-    own_part, got_part, feats_t, sent_text[:1], sent_text[2:] = lax.optimization_barrier(
-        (own_part, got_part, feats_t, sent_text[:1], sent_text[2:])
-    )
+    )(grad_tile, img_emb, all_feats)
+    own_part, got_part, sent_text = lax.optimization_barrier((own_part, got_part, sent_text))
     got_text = [swapped(value, total, step * group) for step, value in enumerate(sent_text, 1)]
     own_part, *chip_parts = pl.pallas_call(
         chip_kernel,
@@ -367,8 +341,6 @@
         name="chip_sum",
     )(own_part, got_part)
     got = [swapped(value, total, 2 * index) for index, value in enumerate(chip_parts, 1)]
-    own_text = add_text(own_text, got_text[1:2], hint(10**10))
-    own_text, got = lax.optimization_barrier((own_text, got))
 
     out_rows = width // wide
     rest = share - LANES
@@ -417,7 +389,15 @@
         both = jnp.concatenate([jnp.where(left, partial, 0.0), jnp.where(left, 0.0, partial)], axis=1)
         d_proj = lax.psum_scatter(both, AXES[:2], scatter_dimension=0, tiled=True)
 
-    d_text_unit = add_text(own_text, [*got_text[:1:-1], *got_text[:1]], hint(5 * 10**9))
+    d_text_unit = pl.pallas_call(
+        sum_kernel,
+        in_specs=[VMEM] * spread,
+        out_specs=VMEM,
+        out_shape=jax.ShapeDtypeStruct((rows, width), F32),
+        compiler_params=limit(12),
+        cost_estimate=hint(5 * 10**9),
+        name="caption_total",
+    )(own_text, *got_text[::-1])
     image_loss = lax.dynamic_slice_in_dim(loss_line[0], first_image(member[0], rows, group), rows, 0)
     return (image_loss, d_text_unit, d_proj)
 

time: 55 us -> 50.3 us (0.915)
  waiting for transfers between devices: 19 us -> 15.9 us
  Pallas kernels: 8.57 us -> 7.58 us
    ppermute x14, waiting for transfers between devices: 18.7 us -> 6.14 us  [swapped(): lax.ppermute(value, AXES, [(source, source ^ mask) for source in range(to...]
    all_to_all x1, waiting for transfers between devices: 0.29 us -> 9.71 us  [local(): got_weight = lax.all_to_all(sent_weight, AXES[:2], 0, 0)]
    pallas_call x1, Pallas kernels: 1.19 us -> 0.51 us  [local(): pl.pallas_call(functools.partial(caption_kernel, rows), in_specs=[VMEM] *...]
  transfers between devices with their start and end apart: 15 -> 15, of which waited for: 6 -> 6; matrix products, arithmetic and copies ran while one was open for 1% -> 1% of each run, Pallas kernels for 6% -> 7%
where the time goes in v15:
time: 50.3 us; the launch traced here: 50.1 us
  starting transfers between devices  21.6 us (43%)
  waiting for transfers between devices  15.9 us (32%)
  Pallas kernels  7.58 us (15%)
  local copies, waits for them, and re-layouts  2.98 us (6%)
  between operations  2.08 us (4%)
    ppermute x14, starting transfers between devices, swapped(): lax.ppermute(value, AXES, [(source, source ^ mask) for source in range(to...  16.9 us
    all_to_all x1, waiting for transfers between devices, local(): got_weight = lax.all_to_all(sent_weight, AXES[:2], 0, 0)  9.71 us
    ppermute x14, waiting for transfers between devices, swapped(): lax.ppermute(value, AXES, [(source, source ^ mask) for source in range(to...  6.14 us
    all_to_all x1, starting transfers between devices, local(): got_weight = lax.all_to_all(sent_weight, AXES[:2], 0, 0)  4.69 us
    pallas_call x1, Pallas kernels, local(): pl.pallas_call(functools.partial(pair_kernel, narrow, group), in_specs=[S...  2.89 us
    unnamed x6, local copies, waits for them, and re-layouts  2.4 us
    pallas_call x1, Pallas kernels, local(): pl.pallas_call(functools.partial(weight_kernel, group, wide), in_specs=[V...  1.37 us
  transfers between devices with their start and end apart: 15, of which 6 were waited for; matrix products, arithmetic and copies ran while one was open for 1% of the time, Pallas kernels for 7%

profile of v15, /device:TPU:0, one launch (start us, length us, event | category | flops | bytes accessed | tf_op | source)
XLA Modules:
  0.0 50.1 jit_solution(7202627939082866556)
XLA Ops:
  0.6 3.0 %collective-permute-start = (bf16[48,1152]{1,0:T(8,128)(2,1)}, bf16[48,1152]{1,0:T(8,128)(2,1)S(1)}, u32[]{:S(2)}, u32[]{:S(2)}) collective-permute-start(bf16[48,1152]{1,0:T(8,128)(2,1)} %refs_0_.1), channel_id=1, source_target_pairs={{0,2},{1,3},{2,0},{3,1},{4,6},{5,7},{6,4},{7,5},{8,10},{9,11},{10,... | collective-permute-start | bytes 331784 | tf_op jit(solution)/shard_map/ppermute | solution.py:31
  3.7 1.5 %collective-permute-start.1 = (bf16[48,1152]{1,0:T(8,128)(2,1)}, bf16[48,1152]{1,0:T(8,128)(2,1)S(1)}, u32[]{:S(2)}, u32[]{:S(2)}) collective-permute-start(bf16[48,1152]{1,0:T(8,128)(2,1)} %refs_0_.1), channel_id=1, source_target_pairs={{0,4},{1,5},{2,6},{3,7},{4,0},{5,1},{6,2},{7,3},{8,12},{9,13},{10,... | collective-permute-start | bytes 331784 | tf_op jit(solution)/shard_map/ppermute | solution.py:31
  5.2 4.0 %collective-permute-start.3 = (bf16[48,1152]{1,0:T(8,128)(2,1)}, bf16[48,1152]{1,0:T(8,128)(2,1)S(1)}, u32[]{:S(2)}, u32[]{:S(2)}) collective-permute-start(bf16[48,1152]{1,0:T(8,128)(2,1)} %text_ref.1), channel_id=1, source_target_pairs={{0,24},{1,25},{2,26},{3,27},{4,28},{5,29},{6,30},{7,31},{8,16},{9,... | collective-permute-start | bytes 331784 | tf_op jit(solution)/shard_map/ppermute | solution.py:31
  10.6 0.6 %collective-permute-start.5 = (bf16[48,1152]{1,0:T(8,128)(2,1)}, bf16[48,1152]{1,0:T(8,128)(2,1)S(1)}, u32[]{:S(2)}, u32[]{:S(2)}) collective-permute-start(bf16[48,1152]{1,0:T(8,128)(2,1)} %text_ref.1), channel_id=1, source_target_pairs={{0,8},{1,9},{2,10},{3,11},{4,12},{5,13},{6,14},{7,15},{8,0},{9,1},... | collective-permute-start | bytes 331784 | tf_op jit(solution)/shard_map/ppermute | solution.py:31
  11.2 0.9 %copy-done.2 = bf16[48,1152]{1,0:T(8,128)(2,1)S(1)} copy-done((bf16[48,1152]{1,0:T(8,128)(2,1)S(1)}, bf16[48,1152]{1,0:T(8,128)(2,1)}, u32[]{:S(2)}) %copy-start.2) | copy-done | bytes 110616
  12.4 1.5 %copy-done = bf16[1152,1152]{1,0:T(8,128)(2,1)S(1)} copy-done((bf16[1152,1152]{1,0:T(8,128)(2,1)S(1)}, bf16[1152,1152]{1,0:T(8,128)(2,1)}, u32[]{:S(2)}) %copy-start) | copy-done | bytes 2654232
  13.9 0.8 %own_projection.1.own_proj = f32[192,1152]{1,0:T(8,128)S(1)} custom-call(bf16[192,1152]{1,0:T(8,128)(2,1)S(1)} %stack.1.feats_ref.own_half, bf16[1152,1152]{1,0:T(8,128)(2,1)S(1)} %copy-done), custom_call_target="tpu_custom_call" | custom-call | tf_op jit(solution)/shard_map/own_projection/pallas_call | solution.py:282
  14.7 3.3 %collective-permute-done.4.refs_2_ = bf16[48,1152]{1,0:T(8,128)(2,1)S(1)} collective-permute-done((bf16[48,1152]{1,0:T(8,128)(2,1)}, bf16[48,1152]{1,0:T(8,128)(2,1)S(1)}, u32[]{:S(2)}, u32[]{:S(2)}) %collective-permute-start.4) | collective-permute-done | bytes 110624 | tf_op jit(solution)/shard_map/ppermute | solution.py:31
  18.1 2.9 %pairs.1 = (bf16[384,1152]{1,0:T(8,128)(2,1)S(1)}, f32[1,384]{1,0:T(1,128)S(1)}, bf16[1152,384]{1,0:T(8,128)(2,1)S(1)}, bf16[192,384]{1,0:T(8,128)(2,1)S(1)}, f3...) custom-call(s32[1]{0:T(128)} %bitcast.member_ref, f32[8,128]{1,0:T(8,128)S(1)} %get-tuple-element.31.scalars_ref, ...), custom_call_target="tpu_custom_call" | custom-call | tf_op jit(solution)/shard_map/pairs/pallas_call | solution.py:301
  21.1 0.5 %captions.1 = (bf16[1152,384]{1,0:T(8,128)(2,1)S(1)}, f32[48,1152]{1,0:T(8,128)S(1)}, bf16[48,1152]{1,0:T(8,128)(2,1)S(1)}, bf16[48,1152]{1,0:T(8,128)(2,1)S(1)}, bf16[48,1152]{1,0:T(8,128)(2,1)S(1)}) custom-call(bf16[192,384]{1,0:T(8,128)(2,1)S(1)} %get-tuple-element.39.grad_ref, bf16[1152,384]{1,0:T(8,128)(2,1)S(1)} %get-tuple-element.40.emb_ref, ...), custom_call_target="tpu_custom_call" | custom-call | tf_op jit(solution)/shard_map/captions/pallas_call | solution.py:323
  21.6 1.3 %collective-permute-done.7.got_ref = bf16[4,160,384]{2,1,0:T(8,128)(2,1)S(1)} collective-permute-done((bf16[4,160,384]{2,1,0:T(8,128)(2,1)S(1)}, bf16[4,160,384]{2,1,0:T(8,128)(2,1)S(1)}, u32[]{:S(2)}, u32[]{:S(2)}) %collective-permute-start.7) | collective-permute-done | bytes 491552 | tf_op jit(solution)/shard_map/ppermute | solution.py:31
  23.0 2.5 %collective-permute-start.10 = (bf16[160,384]{1,0:T(8,128)(2,1)S(1)}, bf16[160,384]{1,0:T(8,128)(2,1)S(1)}, u32[]{:S(2)}, u32[]{:S(2)}) collective-permute-start(bf16[160,384]{1,0:T(8,128)(2,1)S(1)} %get-tuple-element.50), channel_id=1, source_target_pairs={{0,6},{1,7},{2,4},{3,5},{4,2},{5,3},{6,0},{7,1},{8,14},{9,15},{10,... | collective-permute-start | bytes 368648 | tf_op jit(solution)/shard_map/ppermute | solution.py:31
  25.5 0.5 %collective-permute-start.8 = (bf16[160,384]{1,0:T(8,128)(2,1)S(1)}, bf16[160,384]{1,0:T(8,128)(2,1)S(1)}, u32[]{:S(2)}, u32[]{:S(2)}) collective-permute-start(bf16[160,384]{1,0:T(8,128)(2,1)S(1)} %get-tuple-element.48), channel_id=1, source_target_pairs={{0,2},{1,3},{2,0},{3,1},{4,6},{5,7},{6,4},{7,5},{8,10},{9,11},{10,... | collective-permute-start | bytes 368648 | tf_op jit(solution)/shard_map/ppermute | solution.py:31
  26.1 0.5 %collective-permute-start.9 = (bf16[160,384]{1,0:T(8,128)(2,1)S(1)}, bf16[160,384]{1,0:T(8,128)(2,1)S(1)}, u32[]{:S(2)}, u32[]{:S(2)}) collective-permute-start(bf16[160,384]{1,0:T(8,128)(2,1)S(1)} %get-tuple-element.49), channel_id=1, source_target_pairs={{0,4},{1,5},{2,6},{3,7},{4,0},{5,1},{6,2},{7,3},{8,12},{9,13},{10,... | collective-permute-start | bytes 368648 | tf_op jit(solution)/shard_map/ppermute | solution.py:31
  26.6 2.4 %collective-permute-start.11 = (bf16[48,1152]{1,0:T(8,128)(2,1)S(1)}, bf16[48,1152]{1,0:T(8,128)(2,1)S(1)}, u32[]{:S(2)}, u32[]{:S(2)}) collective-permute-start(bf16[48,1152]{1,0:T(8,128)(2,1)S(1)} %get-tuple-element.55), channel_id=1, source_target_pairs={{0,24},{1,25},{2,26},{3,27},{4,28},{5,29},{6,30},{7,31},{8,16},{9,... | collective-permute-start | bytes 331784 | tf_op jit(solution)/shard_map/ppermute | solution.py:31
  29.0 0.4 collective-permute-done.10.refs_3_
  29.5 1.5 %collective-permute-start.13 = (bf16[48,1152]{1,0:T(8,128)(2,1)S(1)}, bf16[48,1152]{1,0:T(8,128)(2,1)S(1)}, u32[]{:S(2)}, u32[]{:S(2)}) collective-permute-start(bf16[48,1152]{1,0:T(8,128)(2,1)S(1)} %get-tuple-element.57), channel_id=1, source_target_pairs={{0,8},{1,9},{2,10},{3,11},{4,12},{5,13},{6,14},{7,15},{8,0},{9,1},... | collective-permute-start | bytes 331784 | tf_op jit(solution)/shard_map/ppermute | solution.py:31
  31.0 1.0 %collective-permute-done.8.refs_1_ = bf16[160,384]{1,0:T(8,128)(2,1)S(1)} collective-permute-done((bf16[160,384]{1,0:T(8,128)(2,1)S(1)}, bf16[160,384]{1,0:T(8,128)(2,1)S(1)}, u32[]{:S(2)}, u32[]{:S(2)}) %collective-permute-start.8) | collective-permute-done | bytes 122912 | tf_op jit(solution)/shard_map/ppermute | solution.py:31
  32.1 1.4 %weights.1 = (f32[1,384]{1,0:T(1,128)S(1)}, bf16[8,176,128]{2,1,0:T(8,128)(2,1)}) custom-call(f32[152,384]{1,0:T(8,128)S(1)} %get-tuple-element.47.refs_0_, bf16[160,384]{1,0:T(8,128)(2,1)S(1)} %collective-permute-done.8.refs_1_, bf16[160,384]{1,0:T(8,128)(2,1)S(1)} %collective-permute-done.9.refs_2_, bf16[160,384]{1,0:T(8,128)(2,1)S(1)} %collective-permute-done.10.refs_3_, ...), custom_call_target="tpu_custom_call" | custom-call | tf_op jit(solution)/shard_map/weights/pallas_call | solution.py:350
  33.4 4.7 %all-to-all-start = ((bf16[8,176,128]{2,1,0:T(8,128)(2,1)}), bf16[8,176,128]{2,1,0:T(8,128)(2,1)S(1)}, u32[]{:S(2)}, u32[]{:S(2)}) async-start(bf16[8,176,128]{2,1,0:T(8,128)(2,1)} %get-tuple-element.58), calls=%async_computation | async-start | bytes 720896 | tf_op jit(solution)/shard_map/all_to_all | solution.py:361
  38.1 0.7 %caption_total.1 = f32[48,1152]{1,0:T(8,128)} custom-call(f32[48,1152]{1,0:T(8,128)S(1)} %get-tuple-element.54.refs_0_, bf16[48,1152]{1,0:T(8,128)(2,1)S(1)} %collective-permute-done.11.refs_1_, bf16[48,1152]{1,0:T(8,128)(2,1)S(1)} %collective-permute-done.12.refs_2_, bf16[48,1152]{1,0:T(8,128)(2,1)S(1)} %collective-permute-done.13.refs_3_), custom_call_target="tpu_custom_call" | custom-call | flops 5000000000 | tf_op jit(solution)/shard_map/caption_total/pallas_call | solution.py:392
  38.9 0.6 %dynamic-slice_bitcast_fusion = f32[48]{0:T(128)} fusion(f32[1,384]{1,0:T(1,128)S(1)} %get-tuple-element.53, s32[]{:T(128)S(6)} %select_n.16), kind=kLoop, calls=%fused_computation | loop fusion | bytes 388 | tf_op jit(solution)/shard_map/dynamic_slice | solution.py:401
  39.5 9.7 %all-to-all-done.got_ref = bf16[8,176,128]{2,1,0:T(8,128)(2,1)S(1)} async-done(((bf16[8,176,128]{2,1,0:T(8,128)(2,1)}), bf16[8,176,128]{2,1,0:T(8,128)(2,1)S(1)}, u32[]{:S(2)}, u32[]{:S(2)}) %all-to-all-start) | async-done | bytes 360480 | tf_op jit(solution)/shard_map/all_to_all | solution.py:361
  49.2 0.9 %weight_total.1 = f32[144,288]{1,0:T(8,128)} custom-call(bf16[8,176,128]{2,1,0:T(8,128)(2,1)S(1)} %all-to-all-done.got_ref), custom_call_target="tpu_custom_call" | custom-call | tf_op jit(solution)/shard_map/weight_total/pallas_call | solution.py:362
  (23 shorter events, 0.7 us)
Async XLA Ops:
  0.6 9.9 %collective-permute-start = (bf16[48,1152]{1,0:T(8,128)(2,1)}, bf16[48,1152]{1,0:T(8,128)(2,1)S(1)}, u32[]{:S(2)}, u32[]{:S(2)}) collective-permute-start(bf16[48,1152]{1,0:T(8,128)(2,1)} %refs_0_.1), channel_id=1, source_target_pairs={{0,2},{1,3},{2,0},{3,1},{4,6},{5,7},{6,4},{7,5},{8,10},{9,11},{10,... | collective-permute-start | bytes 331784 | tf_op jit(solution)/shard_map/ppermute | solution.py:31
  3.7 8.6 %collective-permute-start.1 = (bf16[48,1152]{1,0:T(8,128)(2,1)}, bf16[48,1152]{1,0:T(8,128)(2,1)S(1)}, u32[]{:S(2)}, u32[]{:S(2)}) collective-permute-start(bf16[48,1152]{1,0:T(8,128)(2,1)} %refs_0_.1), channel_id=1, source_target_pairs={{0,4},{1,5},{2,6},{3,7},{4,0},{5,1},{6,2},{7,3},{8,12},{9,13},{10,... | collective-permute-start | bytes 331784 | tf_op jit(solution)/shard_map/ppermute | solution.py:31
  5.2 7.1 %collective-permute-start.2 = (bf16[48,1152]{1,0:T(8,128)(2,1)}, bf16[48,1152]{1,0:T(8,128)(2,1)S(1)}, u32[]{:S(2)}, u32[]{:S(2)}) collective-permute-start(bf16[48,1152]{1,0:T(8,128)(2,1)} %refs_0_.1), channel_id=1, source_target_pairs={{0,6},{1,7},{2,4},{3,5},{4,2},{5,3},{6,0},{7,1},{8,14},{9,15},{10,... | collective-permute-start | bytes 331784 | tf_op jit(solution)/shard_map/ppermute | solution.py:31
  5.2 9.5 %collective-permute-start.3 = (bf16[48,1152]{1,0:T(8,128)(2,1)}, bf16[48,1152]{1,0:T(8,128)(2,1)S(1)}, u32[]{:S(2)}, u32[]{:S(2)}) collective-permute-start(bf16[48,1152]{1,0:T(8,128)(2,1)} %text_ref.1), channel_id=1, source_target_pairs={{0,24},{1,25},{2,26},{3,27},{4,28},{5,29},{6,30},{7,31},{8,16},{9,... | collective-permute-start | bytes 331784 | tf_op jit(solution)/shard_map/ppermute | solution.py:31
  9.2 8.7 %collective-permute-start.4 = (bf16[48,1152]{1,0:T(8,128)(2,1)}, bf16[48,1152]{1,0:T(8,128)(2,1)S(1)}, u32[]{:S(2)}, u32[]{:S(2)}) collective-permute-start(bf16[48,1152]{1,0:T(8,128)(2,1)} %text_ref.1), channel_id=1, source_target_pairs={{0,16},{1,17},{2,18},{3,19},{4,20},{5,21},{6,22},{7,23},{8,24},{9,... | collective-permute-start | bytes 331784 | tf_op jit(solution)/shard_map/ppermute | solution.py:31
  10.5 1.7 %copy-start.1 = (bf16[48,1152]{1,0:T(8,128)(2,1)S(1)}, bf16[48,1152]{1,0:T(8,128)(2,1)}, u32[]{:S(2)}) copy-start(bf16[48,1152]{1,0:T(8,128)(2,1)} %refs_0_.1) | copy-start | bytes 331780
  10.6 7.4 %collective-permute-start.5 = (bf16[48,1152]{1,0:T(8,128)(2,1)}, bf16[48,1152]{1,0:T(8,128)(2,1)S(1)}, u32[]{:S(2)}, u32[]{:S(2)}) collective-permute-start(bf16[48,1152]{1,0:T(8,128)(2,1)} %text_ref.1), channel_id=1, source_target_pairs={{0,8},{1,9},{2,10},{3,11},{4,12},{5,13},{6,14},{7,15},{8,0},{9,1},... | collective-permute-start | bytes 331784 | tf_op jit(solution)/shard_map/ppermute | solution.py:31
  11.2 0.9 %copy-start.2 = (bf16[48,1152]{1,0:T(8,128)(2,1)S(1)}, bf16[48,1152]{1,0:T(8,128)(2,1)}, u32[]{:S(2)}) copy-start(bf16[48,1152]{1,0:T(8,128)(2,1)} %text_ref.1) | copy-start | bytes 331780
  12.1 1.7 %copy-start = (bf16[1152,1152]{1,0:T(8,128)(2,1)S(1)}, bf16[1152,1152]{1,0:T(8,128)(2,1)}, u32[]{:S(2)}) copy-start(bf16[1152,1152]{1,0:T(8,128)(2,1)} %weight.1) | copy-start | bytes 7962628
  12.3 5.8 %collective-permute-start.6 = (bf16[192,1152]{1,0:T(8,128)(2,1)S(1)}, bf16[192,1152]{1,0:T(8,128)(2,1)S(1)}, u32[]{:S(2)}, u32[]{:S(2)}) collective-permute-start(bf16[192,1152]{1,0:T(8,128)(2,1)S(1)} %stack.1.feats_ref.own_half), channel_id=1, source_target_pairs={{0,1},{1,0},{2,3},{3,2},{4,5},{5,4},{6,7},{7,6},{8,9},{9,8},{10,11... | collective-permute-start | bytes 1327112 | tf_op jit(solution)/shard_map/ppermute | solution.py:31
  21.0 1.9 %collective-permute-start.7 = (bf16[4,160,384]{2,1,0:T(8,128)(2,1)S(1)}, bf16[4,160,384]{2,1,0:T(8,128)(2,1)S(1)}, u32[]{:S(2)}, u32[]{:S(2)}) collective-permute-start(bf16[4,160,384]{2,1,0:T(8,128)(2,1)S(1)} %get-tuple-element.38), channel_id=1, source_target_pairs={{0,1},{1,0},{2,3},{3,2},{4,5},{5,4},{6,7},{7,6},{8,9},{9,8},{10,11... | collective-permute-start | bytes 1474568 | tf_op jit(solution)/shard_map/ppermute | solution.py:31
  23.0 6.4 %collective-permute-start.10 = (bf16[160,384]{1,0:T(8,128)(2,1)S(1)}, bf16[160,384]{1,0:T(8,128)(2,1)S(1)}, u32[]{:S(2)}, u32[]{:S(2)}) collective-permute-start(bf16[160,384]{1,0:T(8,128)(2,1)S(1)} %get-tuple-element.50), channel_id=1, source_target_pairs={{0,6},{1,7},{2,4},{3,5},{4,2},{5,3},{6,0},{7,1},{8,14},{9,15},{10,... | collective-permute-start | bytes 368648 | tf_op jit(solution)/shard_map/ppermute | solution.py:31
  25.5 6.4 %collective-permute-start.8 = (bf16[160,384]{1,0:T(8,128)(2,1)S(1)}, bf16[160,384]{1,0:T(8,128)(2,1)S(1)}, u32[]{:S(2)}, u32[]{:S(2)}) collective-permute-start(bf16[160,384]{1,0:T(8,128)(2,1)S(1)} %get-tuple-element.48), channel_id=1, source_target_pairs={{0,2},{1,3},{2,0},{3,1},{4,6},{5,7},{6,4},{7,5},{8,10},{9,11},{10,... | collective-permute-start | bytes 368648 | tf_op jit(solution)/shard_map/ppermute | solution.py:31
  26.1 6.0 %collective-permute-start.9 = (bf16[160,384]{1,0:T(8,128)(2,1)S(1)}, bf16[160,384]{1,0:T(8,128)(2,1)S(1)}, u32[]{:S(2)}, u32[]{:S(2)}) collective-permute-start(bf16[160,384]{1,0:T(8,128)(2,1)S(1)} %get-tuple-element.49), channel_id=1, source_target_pairs={{0,4},{1,5},{2,6},{3,7},{4,0},{5,1},{6,2},{7,3},{8,12},{9,13},{10,... | collective-permute-start | bytes 368648 | tf_op jit(solution)/shard_map/ppermute | solution.py:31
  26.6 11.5 %collective-permute-start.11 = (bf16[48,1152]{1,0:T(8,128)(2,1)S(1)}, bf16[48,1152]{1,0:T(8,128)(2,1)S(1)}, u32[]{:S(2)}, u32[]{:S(2)}) collective-permute-start(bf16[48,1152]{1,0:T(8,128)(2,1)S(1)} %get-tuple-element.55), channel_id=1, source_target_pairs={{0,24},{1,25},{2,26},{3,27},{4,28},{5,29},{6,30},{7,31},{8,16},{9,... | collective-permute-start | bytes 331784 | tf_op jit(solution)/shard_map/ppermute | solution.py:31
  29.0 9.1 %collective-permute-start.12 = (bf16[48,1152]{1,0:T(8,128)(2,1)S(1)}, bf16[48,1152]{1,0:T(8,128)(2,1)S(1)}, u32[]{:S(2)}, u32[]{:S(2)}) collective-permute-start(bf16[48,1152]{1,0:T(8,128)(2,1)S(1)} %get-tuple-element.56), channel_id=1, source_target_pairs={{0,16},{1,17},{2,18},{3,19},{4,20},{5,21},{6,22},{7,23},{8,24},{9,... | collective-permute-start | bytes 331784 | tf_op jit(solution)/shard_map/ppermute | solution.py:31
  29.5 8.7 %collective-permute-start.13 = (bf16[48,1152]{1,0:T(8,128)(2,1)S(1)}, bf16[48,1152]{1,0:T(8,128)(2,1)S(1)}, u32[]{:S(2)}, u32[]{:S(2)}) collective-permute-start(bf16[48,1152]{1,0:T(8,128)(2,1)S(1)} %get-tuple-element.57), channel_id=1, source_target_pairs={{0,8},{1,9},{2,10},{3,11},{4,12},{5,13},{6,14},{7,15},{8,0},{9,1},... | collective-permute-start | bytes 331784 | tf_op jit(solution)/shard_map/ppermute | solution.py:31
  33.4 15.8 %all-to-all-start = ((bf16[8,176,128]{2,1,0:T(8,128)(2,1)}), bf16[8,176,128]{2,1,0:T(8,128)(2,1)S(1)}, u32[]{:S(2)}, u32[]{:S(2)}) async-start(bf16[8,176,128]{2,1,0:T(8,128)(2,1)} %get-tuple-element.58), calls=%async_computation | async-start | bytes 720896 | tf_op jit(solution)/shard_map/all_to_all | solution.py:361

commit v16 on v15

--- a/solution.py
+++ b/solution.py
@@ -106,7 +106,8 @@
     emb_out,
     grad_out,
     own_out,
-    send_out,
+    near_out,
+    far_out,
     unit_all,
     d_all,
     proj_all,
@@ -175,20 +176,22 @@
     losses = loss_rows(loss_sum)
     for index in range(group // 2):
         own_out[index, :share, :] = projected(2 * index)
-        send_out[index, :share, :] = projected(2 * index + 1).astype(BF16)
-        send_out[index, share:, :] = losses
+        target = (near_out, far_out)[index * 4 // group].at[index % (group // 4)]
+        target[:share, :] = projected(2 * index + 1).astype(BF16)
+        target[share:, :] = losses
     own_out[0, share : share + 1, :] = loss_sum
 
 
-def chip_kernel(own_ref, got_ref, own_out, *send_out):
-    share = own_out.shape[0] - 8
+def chip_kernel(first, own_ref, got_ref, *outs):
+    share = own_ref.shape[1] - 8
     loss = own_ref[0, share : share + 1, :] + loss_of(got_ref[0, share:, :])
-    own_out[:share, :] = own_ref[0, :share, :] + got_ref[0, :share, :].astype(F32)
-    own_out[share : share + 1, :] = loss
-    losses = loss_rows(loss)
-    for index, target in enumerate(send_out, 1):
-        target[:share, :] = (own_ref[index, :share, :] + got_ref[index, :share, :].astype(F32)).astype(BF16)
-        target[share:, :] = losses
+    for index, target in enumerate(outs):
+        total = own_ref[first + index, :share, :] + got_ref[index, :share, :].astype(F32)
+        target[:share, :] = total.astype(target.dtype)
+        if target.dtype == BF16:
+            target[share:, :] = loss_rows(loss)
+        else:
+            target[share : share + 1, :] = loss
 
 
 def caption_kernel(rows, grad_ref, emb_ref, feats_ref, feats_t, *outs):
@@ -198,6 +201,17 @@
     for start in range(0, feats_ref.shape[0], LANES):
         cols = slice(start, start + LANES)
         feats_t[:, cols] = feats_ref[cols, :].astype(F32).T.astype(BF16)
+
+
+def far_sum_kernel(*refs):
+    own_ref, got, out = refs[0], refs[1:-1], refs[-1]
+    share = own_ref.shape[0] - 8
+    total, loss = own_ref[:share, :], own_ref[share : share + 1, :]
+    for block in got:
+        total = total + block[:share, :].astype(F32)
+        loss = loss + loss_of(block[share:, :])
+    out[:share, :] = total
+    out[share : share + 1, :] = loss
 
 
 def gathered_gradient(own_ref, got, inv_ref, loss_out):
@@ -212,8 +226,8 @@
 
 
 def weight_kernel(group, wide, *refs):
-    own_ref, got = refs[0], refs[1 : group // 2]
-    inv_ref, feats_ref, feats_t_ref, loss_out, send_out = refs[group // 2 :]
+    own_ref, got = refs[0], refs[1 : group // 4]
+    inv_ref, feats_ref, feats_t_ref, loss_out, send_out = refs[group // 4 :]
     rows = feats_t_ref.shape[0] // wide
     high, low = split_pair(gathered_gradient(own_ref, got, inv_ref, loss_out))
     rest = high.shape[0] - LANES
@@ -301,15 +315,15 @@
     results = pl.pallas_call(
         functools.partial(pair_kernel, narrow, group),
         in_specs=[SMEM] + [VMEM] * 6,
-        out_specs=[VMEM] * 6,
+        out_specs=[VMEM] * 7,
         out_shape=[
             jax.ShapeDtypeStruct((images, width), BF16),
             jax.ShapeDtypeStruct((1, images), F32),
             jax.ShapeDtypeStruct((width, images), BF16),
             jax.ShapeDtypeStruct((spread * rows, images), BF16),
             jax.ShapeDtypeStruct((group // 2, share + 8, images), F32),
-            jax.ShapeDtypeStruct((group // 2, share + STAT_ROWS, images), BF16),
-        ],
+        ]
+        + [jax.ShapeDtypeStruct((group // 4, share + STAT_ROWS, images), BF16)] * 2,
         scratch_shapes=[
             pltpu.VMEM((width, images), F32),
             pltpu.VMEM((width, images), F32),
@@ -318,8 +332,21 @@
         compiler_params=limit(24 if spread <= 4 else 40),
         name="pairs",
     )(member, scalars, proj_weight, own_half, own_proj, got_half, text_emb)
-    all_feats, inv_part, img_emb, grad_tile, own_part, sent_part = results
-    got_part = swapped(sent_part, total, 1)
+    all_feats, inv_part, img_emb, grad_tile, own_part, near_part, far_part = results
+    got_far = swapped(far_part, total, 1)
+    got_near = swapped(near_part, total, 1)
+    sent_block = jax.ShapeDtypeStruct((share + STAT_ROWS, images), BF16)
+    kept_block = jax.ShapeDtypeStruct((share + 8, images), F32)
+    half = group // 4
+    far = pl.pallas_call(
+        functools.partial(chip_kernel, half),
+        in_specs=[VMEM] * 2,
+        out_specs=[VMEM] * half,
+        out_shape=[sent_block] * half,
+        compiler_params=limit(8),
+        name="chip_far",
+    )(own_part, got_far)
+    far = [swapped(value, total, 2 * (half + index)) for index, value in enumerate(far)]
     feats_t, own_text, *sent_text = pl.pallas_call(
         functools.partial(caption_kernel, rows),
         in_specs=[VMEM] * 3,
@@ -329,18 +356,26 @@
         compiler_params=limit(12 if spread <= 4 else 32),
         name="captions",
     )(grad_tile, img_emb, all_feats)
-    own_part, got_part, sent_text = lax.optimization_barrier((own_part, got_part, sent_text))
+    own_part, got_near, sent_text = lax.optimization_barrier((own_part, got_near, sent_text))
     got_text = [swapped(value, total, step * group) for step, value in enumerate(sent_text, 1)]
-    own_part, *chip_parts = pl.pallas_call(
-        chip_kernel,
+    own_part, *near = pl.pallas_call(
+        functools.partial(chip_kernel, 0),
         in_specs=[VMEM] * 2,
-        out_specs=[VMEM] * (group // 2),
-        out_shape=[jax.ShapeDtypeStruct((share + 8, images), F32)]
-        + [jax.ShapeDtypeStruct((share + STAT_ROWS, images), BF16)] * (group // 2 - 1),
-        compiler_params=limit(12),
-        name="chip_sum",
-    )(own_part, got_part)
-    got = [swapped(value, total, 2 * index) for index, value in enumerate(chip_parts, 1)]
+        out_specs=[VMEM] * half,
+        out_shape=[kept_block] + [sent_block] * (half - 1),
+        compiler_params=limit(8),
+        name="chip_near",
+    )(own_part, got_near)
+    near = [swapped(value, total, 2 * index) for index, value in enumerate(near, 1)]
+    own_part = pl.pallas_call(
+        far_sum_kernel,
+        in_specs=[VMEM] * (1 + half),
+        out_specs=VMEM,
+        out_shape=kept_block,
+        compiler_params=limit(8),
+        cost_estimate=hint(5 * 10**8),
+        name="far_sum",
+    )(own_part, *far)
 
     out_rows = width // wide
     rest = share - LANES
@@ -349,7 +384,7 @@
     if direct:
         loss_line, sent_weight = pl.pallas_call(
             functools.partial(weight_kernel, group, wide),
-            in_specs=[VMEM] * (3 + group // 2),
+            in_specs=[VMEM] * (3 + group // 4),
             out_specs=[VMEM] * 2,
             out_shape=[
                 jax.ShapeDtypeStruct((1, images), F32),
@@ -357,7 +392,7 @@
             ],
             compiler_params=limit(12),
             name="weights",
-        )(own_part, *got, inv_part, all_feats, feats_t)
+        )(own_part, *near, inv_part, all_feats, feats_t)
         got_weight = lax.all_to_all(sent_weight, AXES[:2], 0, 0)
         d_proj = pl.pallas_call(
             functools.partial(total_kernel, rest),
@@ -370,18 +405,18 @@
     else:
 
         def gradient_kernel(*refs):
-            own_ref, blocks = refs[0], refs[1 : group // 2]
-            inv_ref, loss_out, d_out = refs[group // 2 :]
+            own_ref, blocks = refs[0], refs[1 : group // 4]
+            inv_ref, loss_out, d_out = refs[group // 4 :]
             d_out[...] = gathered_gradient(own_ref, blocks, inv_ref, loss_out)
 
         loss_line, d_zproj = pl.pallas_call(
             gradient_kernel,
-            in_specs=[VMEM] * (1 + group // 2),
+            in_specs=[VMEM] * (1 + group // 4),
             out_specs=[VMEM] * 2,
             out_shape=[jax.ShapeDtypeStruct((1, images), F32), jax.ShapeDtypeStruct((share, images), F32)],
             compiler_params=limit(12),
             name="gradient",
-        )(own_part, *got, inv_part)
+        )(own_part, *near, inv_part)
         partial = sum(
             lax.dot_general(feats_t, part, NT, preferred_element_type=F32) for part in split_pair(d_zproj)
         )

time: 50.3 us -> 49.4 us (0.982)
  waiting for transfers between devices: 15.9 us -> 14.4 us
    all_to_all x1, waiting for transfers between devices: 9.71 us -> 8.52 us  [local(): got_weight = lax.all_to_all(sent_weight, AXES[:2], 0, 0)]
    ppermute x14 -> x15, starting transfers between devices: 16.9 us -> 17.4 us  [swapped(): lax.ppermute(value, AXES, [(source, source ^ mask) for source in range(to...]
    ppermute x14 -> x15, waiting for transfers between devices: 6.14 us -> 5.84 us  [swapped(): lax.ppermute(value, AXES, [(source, source ^ mask) for source in range(to...]
  transfers between devices with their start and end apart: 15 -> 16, of which waited for: 6 -> 7; matrix products, arithmetic and copies ran while one was open for 1% -> 1% of each run, Pallas kernels for 7% -> 8%
where the time goes in v16:
time: 49.4 us; the launch traced here: 49.1 us
  starting transfers between devices  22.1 us (45%)
  waiting for transfers between devices  14.4 us (29%)
  Pallas kernels  7.64 us (15%)
  local copies, waits for them, and re-layouts  2.98 us (6%)
  between operations  2.07 us (4%)
    ppermute x15, starting transfers between devices, swapped(): lax.ppermute(value, AXES, [(source, source ^ mask) for source in range(to...  17.4 us
    all_to_all x1, waiting for transfers between devices, local(): got_weight = lax.all_to_all(sent_weight, AXES[:2], 0, 0)  8.52 us
    ppermute x15, waiting for transfers between devices, swapped(): lax.ppermute(value, AXES, [(source, source ^ mask) for source in range(to...  5.84 us
    all_to_all x1, starting transfers between devices, local(): got_weight = lax.all_to_all(sent_weight, AXES[:2], 0, 0)  4.65 us
    pallas_call x1, Pallas kernels, local(): pl.pallas_call(functools.partial(pair_kernel, narrow, group), in_specs=[S...  2.89 us
    unnamed x6, local copies, waits for them, and re-layouts  2.4 us
    pallas_call x1, Pallas kernels, local(): pl.pallas_call(functools.partial(weight_kernel, group, wide), in_specs=[V...  1.37 us
  transfers between devices with their start and end apart: 16, of which 7 were waited for; matrix products, arithmetic and copies ran while one was open for 1% of the time, Pallas kernels for 8%

profile of v16, /device:TPU:0, one launch (start us, length us, event | category | flops | bytes accessed | tf_op | source)
XLA Modules:
  0.0 49.1 jit_solution(8918182694416279939)
XLA Ops:
  0.6 3.0 %collective-permute-start = (bf16[48,1152]{1,0:T(8,128)(2,1)}, bf16[48,1152]{1,0:T(8,128)(2,1)S(1)}, u32[]{:S(2)}, u32[]{:S(2)}) collective-permute-start(bf16[48,1152]{1,0:T(8,128)(2,1)} %refs_0_.1), channel_id=1, source_target_pairs={{0,2},{1,3},{2,0},{3,1},{4,6},{5,7},{6,4},{7,5},{8,10},{9,11},{10,... | collective-permute-start | bytes 331784 | tf_op jit(solution)/shard_map/ppermute | solution.py:31
  3.7 1.5 %collective-permute-start.1 = (bf16[48,1152]{1,0:T(8,128)(2,1)}, bf16[48,1152]{1,0:T(8,128)(2,1)S(1)}, u32[]{:S(2)}, u32[]{:S(2)}) collective-permute-start(bf16[48,1152]{1,0:T(8,128)(2,1)} %refs_0_.1), channel_id=1, source_target_pairs={{0,4},{1,5},{2,6},{3,7},{4,0},{5,1},{6,2},{7,3},{8,12},{9,13},{10,... | collective-permute-start | bytes 331784 | tf_op jit(solution)/shard_map/ppermute | solution.py:31
  5.2 4.0 %collective-permute-start.3 = (bf16[48,1152]{1,0:T(8,128)(2,1)}, bf16[48,1152]{1,0:T(8,128)(2,1)S(1)}, u32[]{:S(2)}, u32[]{:S(2)}) collective-permute-start(bf16[48,1152]{1,0:T(8,128)(2,1)} %text_ref.1), channel_id=1, source_target_pairs={{0,24},{1,25},{2,26},{3,27},{4,28},{5,29},{6,30},{7,31},{8,16},{9,... | collective-permute-start | bytes 331784 | tf_op jit(solution)/shard_map/ppermute | solution.py:31
  10.6 0.6 %collective-permute-start.5 = (bf16[48,1152]{1,0:T(8,128)(2,1)}, bf16[48,1152]{1,0:T(8,128)(2,1)S(1)}, u32[]{:S(2)}, u32[]{:S(2)}) collective-permute-start(bf16[48,1152]{1,0:T(8,128)(2,1)} %text_ref.1), channel_id=1, source_target_pairs={{0,8},{1,9},{2,10},{3,11},{4,12},{5,13},{6,14},{7,15},{8,0},{9,1},... | collective-permute-start | bytes 331784 | tf_op jit(solution)/shard_map/ppermute | solution.py:31
  11.2 0.9 %copy-done.2 = bf16[48,1152]{1,0:T(8,128)(2,1)S(1)} copy-done((bf16[48,1152]{1,0:T(8,128)(2,1)S(1)}, bf16[48,1152]{1,0:T(8,128)(2,1)}, u32[]{:S(2)}) %copy-start.2) | copy-done | bytes 110616
  12.4 1.5 %copy-done = bf16[1152,1152]{1,0:T(8,128)(2,1)S(1)} copy-done((bf16[1152,1152]{1,0:T(8,128)(2,1)S(1)}, bf16[1152,1152]{1,0:T(8,128)(2,1)}, u32[]{:S(2)}) %copy-start) | copy-done | bytes 2654232
  13.9 0.8 %own_projection.1.own_proj = f32[192,1152]{1,0:T(8,128)S(1)} custom-call(bf16[192,1152]{1,0:T(8,128)(2,1)S(1)} %stack.1.feats_ref.own_half, bf16[1152,1152]{1,0:T(8,128)(2,1)S(1)} %copy-done), custom_call_target="tpu_custom_call" | custom-call | tf_op jit(solution)/shard_map/own_projection/pallas_call | solution.py:296
  14.7 3.3 %collective-permute-done.4.refs_2_ = bf16[48,1152]{1,0:T(8,128)(2,1)S(1)} collective-permute-done((bf16[48,1152]{1,0:T(8,128)(2,1)}, bf16[48,1152]{1,0:T(8,128)(2,1)S(1)}, u32[]{:S(2)}, u32[]{:S(2)}) %collective-permute-start.4) | collective-permute-done | bytes 110624 | tf_op jit(solution)/shard_map/ppermute | solution.py:31
  18.1 2.9 %pairs.1 = (bf16[384,1152]{1,0:T(8,128)(2,1)S(1)}, f32[1,384]{1,0:T(1,128)S(1)}, bf16[1152,384]{1,0:T(8,128)(2,1)S(1)}, bf16[192,384]{1,0:T(8,128)(2,1)S(1)}, f3...) custom-call(s32[1]{0:T(128)} %bitcast.member_ref, ...), custom_call_target="tpu_custom_call" | custom-call | tf_op jit(solution)/shard_map/pairs/pallas_call | solution.py:315
  21.1 0.5 %collective-permute-start.7 = (bf16[2,160,384]{2,1,0:T(8,128)(2,1)S(1)}, bf16[2,160,384]{2,1,0:T(8,128)(2,1)S(1)}, u32[]{:S(2)}, u32[]{:S(2)}) collective-permute-start(bf16[2,160,384]{2,1,0:T(8,128)(2,1)S(1)} %get-tuple-element.39), channel_id=1, source_target_pairs={{0,1},{1,0},{2,3},{3,2},{4,5},{5,4},{6,7},{7,6},{8,9},{9,8},{10,11... | collective-permute-start | bytes 737288 | tf_op jit(solution)/shard_map/ppermute | solution.py:31
  21.6 1.0 %collective-permute-done.8.got_ref = bf16[2,160,384]{2,1,0:T(8,128)(2,1)S(1)} collective-permute-done((bf16[2,160,384]{2,1,0:T(8,128)(2,1)S(1)}, bf16[2,160,384]{2,1,0:T(8,128)(2,1)S(1)}, u32[]{:S(2)}, u32[]{:S(2)}) %collective-permute-start.8) | collective-permute-done | bytes 245792 | tf_op jit(solution)/shard_map/ppermute | solution.py:31
  22.7 2.5 %collective-permute-start.10 = (bf16[160,384]{1,0:T(8,128)(2,1)S(1)}, bf16[160,384]{1,0:T(8,128)(2,1)S(1)}, u32[]{:S(2)}, u32[]{:S(2)}) collective-permute-start(bf16[160,384]{1,0:T(8,128)(2,1)S(1)} %get-tuple-element.51), channel_id=1, source_target_pairs={{0,6},{1,7},{2,4},{3,5},{4,2},{5,3},{6,0},{7,1},{8,14},{9,15},{10,... | collective-permute-start | bytes 368648 | tf_op jit(solution)/shard_map/ppermute | solution.py:31
  25.2 0.5 %collective-permute-start.9 = (bf16[160,384]{1,0:T(8,128)(2,1)S(1)}, bf16[160,384]{1,0:T(8,128)(2,1)S(1)}, u32[]{:S(2)}, u32[]{:S(2)}) collective-permute-start(bf16[160,384]{1,0:T(8,128)(2,1)S(1)} %get-tuple-element.50), channel_id=1, source_target_pairs={{0,4},{1,5},{2,6},{3,7},{4,0},{5,1},{6,2},{7,3},{8,12},{9,13},{10,... | collective-permute-start | bytes 368648 | tf_op jit(solution)/shard_map/ppermute | solution.py:31
  25.7 0.5 %captions.1 = (bf16[1152,384]{1,0:T(8,128)(2,1)S(1)}, f32[48,1152]{1,0:T(8,128)S(1)}, bf16[48,1152]{1,0:T(8,128)(2,1)S(1)}, bf16[48,1152]{1,0:T(8,128)(2,1)S(1)}, bf16[48,1152]{1,0:T(8,128)(2,1)S(1)}) custom-call(bf16[192,384]{1,0:T(8,128)(2,1)S(1)} %get-tuple-element.40.grad_ref, bf16[1152,384]{1,0:T(8,128)(2,1)S(1)} %get-tuple-element.41.emb_ref, ...), custom_call_target="tpu_custom_call" | custom-call | tf_op jit(solution)/shard_map/captions/pallas_call | solution.py:350
  26.3 0.6 %collective-permute-start.11 = (bf16[160,384]{1,0:T(8,128)(2,1)S(1)}, bf16[160,384]{1,0:T(8,128)(2,1)S(1)}, u32[]{:S(2)}, u32[]{:S(2)}) collective-permute-start(bf16[160,384]{1,0:T(8,128)(2,1)S(1)} %get-tuple-element.52), channel_id=1, source_target_pairs={{0,2},{1,3},{2,0},{3,1},{4,6},{5,7},{6,4},{7,5},{8,10},{9,11},{10,... | collective-permute-start | bytes 368648 | tf_op jit(solution)/shard_map/ppermute | solution.py:31
  26.9 2.4 %collective-permute-start.12 = (bf16[48,1152]{1,0:T(8,128)(2,1)S(1)}, bf16[48,1152]{1,0:T(8,128)(2,1)S(1)}, u32[]{:S(2)}, u32[]{:S(2)}) collective-permute-start(bf16[48,1152]{1,0:T(8,128)(2,1)S(1)} %get-tuple-element.57), channel_id=1, source_target_pairs={{0,24},{1,25},{2,26},{3,27},{4,28},{5,29},{6,30},{7,31},{8,16},{9,... | collective-permute-start | bytes 331784 | tf_op jit(solution)/shard_map/ppermute | solution.py:31
  29.8 1.5 %collective-permute-start.14 = (bf16[48,1152]{1,0:T(8,128)(2,1)S(1)}, bf16[48,1152]{1,0:T(8,128)(2,1)S(1)}, u32[]{:S(2)}, u32[]{:S(2)}) collective-permute-start(bf16[48,1152]{1,0:T(8,128)(2,1)S(1)} %get-tuple-element.59), channel_id=1, source_target_pairs={{0,8},{1,9},{2,10},{3,11},{4,12},{5,13},{6,14},{7,15},{8,0},{9,1},... | collective-permute-start | bytes 331784 | tf_op jit(solution)/shard_map/ppermute | solution.py:31
  31.8 1.4 %weights.1 = (f32[1,384]{1,0:T(1,128)S(1)}, bf16[8,176,128]{2,1,0:T(8,128)(2,1)}) custom-call(f32[152,384]{1,0:T(8,128)S(1)} %far_sum.1.refs_0_, bf16[160,384]{1,0:T(8,128)(2,1)S(1)} %collective-permute-done.11.refs_1_, f32[1,384]{1,0:T(1,128)S(1)} %get-tuple-element.53.refs_2_, bf16[384,1152]{1,0:T(8,128)(2,1)S(1)} %get-tuple-element.42.feats_ref.refs_3_, ...), custom_call_target="tpu_custom_call" | custom-call | tf_op jit(solution)/shard_map/weights/pallas_call | solution.py:385
  33.2 4.7 %all-to-all-start = ((bf16[8,176,128]{2,1,0:T(8,128)(2,1)}), bf16[8,176,128]{2,1,0:T(8,128)(2,1)S(1)}, u32[]{:S(2)}, u32[]{:S(2)}) async-start(bf16[8,176,128]{2,1,0:T(8,128)(2,1)} %get-tuple-element.60), calls=%async_computation | async-start | bytes 720896 | tf_op jit(solution)/shard_map/all_to_all | solution.py:396
  37.8 0.6 %collective-permute-done.13.refs_2_ = bf16[48,1152]{1,0:T(8,128)(2,1)S(1)} collective-permute-done((bf16[48,1152]{1,0:T(8,128)(2,1)S(1)}, bf16[48,1152]{1,0:T(8,128)(2,1)S(1)}, u32[]{:S(2)}, u32[]{:S(2)}) %collective-permute-start.13) | collective-permute-done | bytes 110624 | tf_op jit(solution)/shard_map/ppermute | solution.py:31
  38.4 0.7 %caption_total.1 = f32[48,1152]{1,0:T(8,128)} custom-call(f32[48,1152]{1,0:T(8,128)S(1)} %get-tuple-element.56.refs_0_, bf16[48,1152]{1,0:T(8,128)(2,1)S(1)} %collective-permute-done.12.refs_1_, bf16[48,1152]{1,0:T(8,128)(2,1)S(1)} %collective-permute-done.13.refs_2_, bf16[48,1152]{1,0:T(8,128)(2,1)S(1)} %collective-permute-done.14.refs_3_), custom_call_target="tpu_custom_call" | custom-call | flops 5000000000 | tf_op jit(solution)/shard_map/caption_total/pallas_call | solution.py:427
  39.1 0.6 %dynamic-slice_bitcast_fusion = f32[48]{0:T(128)} fusion(f32[1,384]{1,0:T(1,128)S(1)} %get-tuple-element.55, s32[]{:T(128)S(6)} %select_n.16), kind=kLoop, calls=%fused_computation | loop fusion | bytes 388 | tf_op jit(solution)/shard_map/dynamic_slice | solution.py:436
  39.7 8.5 %all-to-all-done.got_ref = bf16[8,176,128]{2,1,0:T(8,128)(2,1)S(1)} async-done(((bf16[8,176,128]{2,1,0:T(8,128)(2,1)}), bf16[8,176,128]{2,1,0:T(8,128)(2,1)S(1)}, u32[]{:S(2)}, u32[]{:S(2)}) %all-to-all-start) | async-done | bytes 360480 | tf_op jit(solution)/shard_map/all_to_all | solution.py:396
  48.2 0.9 %weight_total.1 = f32[144,288]{1,0:T(8,128)} custom-call(bf16[8,176,128]{2,1,0:T(8,128)(2,1)S(1)} %all-to-all-done.got_ref), custom_call_target="tpu_custom_call" | custom-call | tf_op jit(solution)/shard_map/weight_total/pallas_call | solution.py:397
  (27 shorter events, 1.7 us)
Async XLA Ops:
  0.6 9.9 %collective-permute-start = (bf16[48,1152]{1,0:T(8,128)(2,1)}, bf16[48,1152]{1,0:T(8,128)(2,1)S(1)}, u32[]{:S(2)}, u32[]{:S(2)}) collective-permute-start(bf16[48,1152]{1,0:T(8,128)(2,1)} %refs_0_.1), channel_id=1, source_target_pairs={{0,2},{1,3},{2,0},{3,1},{4,6},{5,7},{6,4},{7,5},{8,10},{9,11},{10,... | collective-permute-start | bytes 331784 | tf_op jit(solution)/shard_map/ppermute | solution.py:31
  3.7 8.6 %collective-permute-start.1 = (bf16[48,1152]{1,0:T(8,128)(2,1)}, bf16[48,1152]{1,0:T(8,128)(2,1)S(1)}, u32[]{:S(2)}, u32[]{:S(2)}) collective-permute-start(bf16[48,1152]{1,0:T(8,128)(2,1)} %refs_0_.1), channel_id=1, source_target_pairs={{0,4},{1,5},{2,6},{3,7},{4,0},{5,1},{6,2},{7,3},{8,12},{9,13},{10,... | collective-permute-start | bytes 331784 | tf_op jit(solution)/shard_map/ppermute | solution.py:31
  5.2 7.1 %collective-permute-start.2 = (bf16[48,1152]{1,0:T(8,128)(2,1)}, bf16[48,1152]{1,0:T(8,128)(2,1)S(1)}, u32[]{:S(2)}, u32[]{:S(2)}) collective-permute-start(bf16[48,1152]{1,0:T(8,128)(2,1)} %refs_0_.1), channel_id=1, source_target_pairs={{0,6},{1,7},{2,4},{3,5},{4,2},{5,3},{6,0},{7,1},{8,14},{9,15},{10,... | collective-permute-start | bytes 331784 | tf_op jit(solution)/shard_map/ppermute | solution.py:31
  5.2 9.5 %collective-permute-start.3 = (bf16[48,1152]{1,0:T(8,128)(2,1)}, bf16[48,1152]{1,0:T(8,128)(2,1)S(1)}, u32[]{:S(2)}, u32[]{:S(2)}) collective-permute-start(bf16[48,1152]{1,0:T(8,128)(2,1)} %text_ref.1), channel_id=1, source_target_pairs={{0,24},{1,25},{2,26},{3,27},{4,28},{5,29},{6,30},{7,31},{8,16},{9,... | collective-permute-start | bytes 331784 | tf_op jit(solution)/shard_map/ppermute | solution.py:31
  9.2 8.7 %collective-permute-start.4 = (bf16[48,1152]{1,0:T(8,128)(2,1)}, bf16[48,1152]{1,0:T(8,128)(2,1)S(1)}, u32[]{:S(2)}, u32[]{:S(2)}) collective-permute-start(bf16[48,1152]{1,0:T(8,128)(2,1)} %text_ref.1), channel_id=1, source_target_pairs={{0,16},{1,17},{2,18},{3,19},{4,20},{5,21},{6,22},{7,23},{8,24},{9,... | collective-permute-start | bytes 331784 | tf_op jit(solution)/shard_map/ppermute | solution.py:31
  10.5 1.7 %copy-start.1 = (bf16[48,1152]{1,0:T(8,128)(2,1)S(1)}, bf16[48,1152]{1,0:T(8,128)(2,1)}, u32[]{:S(2)}) copy-start(bf16[48,1152]{1,0:T(8,128)(2,1)} %refs_0_.1) | copy-start | bytes 331780
  10.6 7.4 %collective-permute-start.5 = (bf16[48,1152]{1,0:T(8,128)(2,1)}, bf16[48,1152]{1,0:T(8,128)(2,1)S(1)}, u32[]{:S(2)}, u32[]{:S(2)}) collective-permute-start(bf16[48,1152]{1,0:T(8,128)(2,1)} %text_ref.1), channel_id=1, source_target_pairs={{0,8},{1,9},{2,10},{3,11},{4,12},{5,13},{6,14},{7,15},{8,0},{9,1},... | collective-permute-start | bytes 331784 | tf_op jit(solution)/shard_map/ppermute | solution.py:31
  11.2 0.9 %copy-start.2 = (bf16[48,1152]{1,0:T(8,128)(2,1)S(1)}, bf16[48,1152]{1,0:T(8,128)(2,1)}, u32[]{:S(2)}) copy-start(bf16[48,1152]{1,0:T(8,128)(2,1)} %text_ref.1) | copy-start | bytes 331780
  12.1 1.7 %copy-start = (bf16[1152,1152]{1,0:T(8,128)(2,1)S(1)}, bf16[1152,1152]{1,0:T(8,128)(2,1)}, u32[]{:S(2)}) copy-start(bf16[1152,1152]{1,0:T(8,128)(2,1)} %weight.1) | copy-start | bytes 7962628
  12.3 5.8 %collective-permute-start.6 = (bf16[192,1152]{1,0:T(8,128)(2,1)S(1)}, bf16[192,1152]{1,0:T(8,128)(2,1)S(1)}, u32[]{:S(2)}, u32[]{:S(2)}) collective-permute-start(bf16[192,1152]{1,0:T(8,128)(2,1)S(1)} %stack.1.feats_ref.own_half), channel_id=1, source_target_pairs={{0,1},{1,0},{2,3},{3,2},{4,5},{5,4},{6,7},{7,6},{8,9},{9,8},{10,11... | collective-permute-start | bytes 1327112 | tf_op jit(solution)/shard_map/ppermute | solution.py:31
  21.0 1.6 %collective-permute-start.8 = (bf16[2,160,384]{2,1,0:T(8,128)(2,1)S(1)}, bf16[2,160,384]{2,1,0:T(8,128)(2,1)S(1)}, u32[]{:S(2)}, u32[]{:S(2)}) collective-permute-start(bf16[2,160,384]{2,1,0:T(8,128)(2,1)S(1)} %get-tuple-element.49), channel_id=1, source_target_pairs={{0,1},{1,0},{2,3},{3,2},{4,5},{5,4},{6,7},{7,6},{8,9},{9,8},{10,11... | collective-permute-start | bytes 737288 | tf_op jit(solution)/shard_map/ppermute | solution.py:31
  21.1 5.1 %collective-permute-start.7 = (bf16[2,160,384]{2,1,0:T(8,128)(2,1)S(1)}, bf16[2,160,384]{2,1,0:T(8,128)(2,1)S(1)}, u32[]{:S(2)}, u32[]{:S(2)}) collective-permute-start(bf16[2,160,384]{2,1,0:T(8,128)(2,1)S(1)} %get-tuple-element.39), channel_id=1, source_target_pairs={{0,1},{1,0},{2,3},{3,2},{4,5},{5,4},{6,7},{7,6},{8,9},{9,8},{10,11... | collective-permute-start | bytes 737288 | tf_op jit(solution)/shard_map/ppermute | solution.py:31
  22.7 7.1 %collective-permute-start.10 = (bf16[160,384]{1,0:T(8,128)(2,1)S(1)}, bf16[160,384]{1,0:T(8,128)(2,1)S(1)}, u32[]{:S(2)}, u32[]{:S(2)}) collective-permute-start(bf16[160,384]{1,0:T(8,128)(2,1)S(1)} %get-tuple-element.51), channel_id=1, source_target_pairs={{0,6},{1,7},{2,4},{3,5},{4,2},{5,3},{6,0},{7,1},{8,14},{9,15},{10,... | collective-permute-start | bytes 368648 | tf_op jit(solution)/shard_map/ppermute | solution.py:31
  25.2 6.5 %collective-permute-start.9 = (bf16[160,384]{1,0:T(8,128)(2,1)S(1)}, bf16[160,384]{1,0:T(8,128)(2,1)S(1)}, u32[]{:S(2)}, u32[]{:S(2)}) collective-permute-start(bf16[160,384]{1,0:T(8,128)(2,1)S(1)} %get-tuple-element.50), channel_id=1, source_target_pairs={{0,4},{1,5},{2,6},{3,7},{4,0},{5,1},{6,2},{7,3},{8,12},{9,13},{10,... | collective-permute-start | bytes 368648 | tf_op jit(solution)/shard_map/ppermute | solution.py:31
  26.3 5.5 %collective-permute-start.11 = (bf16[160,384]{1,0:T(8,128)(2,1)S(1)}, bf16[160,384]{1,0:T(8,128)(2,1)S(1)}, u32[]{:S(2)}, u32[]{:S(2)}) collective-permute-start(bf16[160,384]{1,0:T(8,128)(2,1)S(1)} %get-tuple-element.52), channel_id=1, source_target_pairs={{0,2},{1,3},{2,0},{3,1},{4,6},{5,7},{6,4},{7,5},{8,10},{9,11},{10,... | collective-permute-start | bytes 368648 | tf_op jit(solution)/shard_map/ppermute | solution.py:31
  26.9 11.0 %collective-permute-start.12 = (bf16[48,1152]{1,0:T(8,128)(2,1)S(1)}, bf16[48,1152]{1,0:T(8,128)(2,1)S(1)}, u32[]{:S(2)}, u32[]{:S(2)}) collective-permute-start(bf16[48,1152]{1,0:T(8,128)(2,1)S(1)} %get-tuple-element.57), channel_id=1, source_target_pairs={{0,24},{1,25},{2,26},{3,27},{4,28},{5,29},{6,30},{7,31},{8,16},{9,... | collective-permute-start | bytes 331784 | tf_op jit(solution)/shard_map/ppermute | solution.py:31
  29.3 9.1 %collective-permute-start.13 = (bf16[48,1152]{1,0:T(8,128)(2,1)S(1)}, bf16[48,1152]{1,0:T(8,128)(2,1)S(1)}, u32[]{:S(2)}, u32[]{:S(2)}) collective-permute-start(bf16[48,1152]{1,0:T(8,128)(2,1)S(1)} %get-tuple-element.58), channel_id=1, source_target_pairs={{0,16},{1,17},{2,18},{3,19},{4,20},{5,21},{6,22},{7,23},{8,24},{9,... | collective-permute-start | bytes 331784 | tf_op jit(solution)/shard_map/ppermute | solution.py:31
  29.8 8.6 %collective-permute-start.14 = (bf16[48,1152]{1,0:T(8,128)(2,1)S(1)}, bf16[48,1152]{1,0:T(8,128)(2,1)S(1)}, u32[]{:S(2)}, u32[]{:S(2)}) collective-permute-start(bf16[48,1152]{1,0:T(8,128)(2,1)S(1)} %get-tuple-element.59), channel_id=1, source_target_pairs={{0,8},{1,9},{2,10},{3,11},{4,12},{5,13},{6,14},{7,15},{8,0},{9,1},... | collective-permute-start | bytes 331784 | tf_op jit(solution)/shard_map/ppermute | solution.py:31
  33.2 15.1 %all-to-all-start = ((bf16[8,176,128]{2,1,0:T(8,128)(2,1)}), bf16[8,176,128]{2,1,0:T(8,128)(2,1)S(1)}, u32[]{:S(2)}, u32[]{:S(2)}) async-start(bf16[8,176,128]{2,1,0:T(8,128)(2,1)} %get-tuple-element.60), calls=%async_computation | async-start | bytes 720896 | tf_op jit(solution)/shard_map/all_to_all | solution.py:396

commit v17 on v16

--- a/solution.py
+++ b/solution.py
@@ -356,7 +356,6 @@
         compiler_params=limit(12 if spread <= 4 else 32),
         name="captions",
     )(grad_tile, img_emb, all_feats)
-    own_part, got_near, sent_text = lax.optimization_barrier((own_part, got_near, sent_text))
     got_text = [swapped(value, total, step * group) for step, value in enumerate(sent_text, 1)]
     own_part, *near = pl.pallas_call(
         functools.partial(chip_kernel, 0),

time: 49.4 us -> 49.4 us (level)
  transfers between devices with their start and end apart: 16 -> 16, of which waited for: 7 -> 6; matrix products, arithmetic and copies ran while one was open for 1% -> 1% of each run, Pallas kernels for 8% -> 8%
where the time goes in v17:
time: 49.4 us; the launch traced here: 49.1 us
  starting transfers between devices  22.2 us (45%)
  waiting for transfers between devices  14.2 us (29%)
  Pallas kernels  7.65 us (15%)
  local copies, waits for them, and re-layouts  2.98 us (6%)
  between operations  2.07 us (4%)
    ppermute x15, starting transfers between devices, swapped(): lax.ppermute(value, AXES, [(source, source ^ mask) for source in range(to...  17.5 us
    all_to_all x1, waiting for transfers between devices, local(): got_weight = lax.all_to_all(sent_weight, AXES[:2], 0, 0)  8.45 us
    ppermute x15, waiting for transfers between devices, swapped(): lax.ppermute(value, AXES, [(source, source ^ mask) for source in range(to...  5.75 us
    all_to_all x1, starting transfers between devices, local(): got_weight = lax.all_to_all(sent_weight, AXES[:2], 0, 0)  4.66 us
    pallas_call x1, Pallas kernels, local(): pl.pallas_call(functools.partial(pair_kernel, narrow, group), in_specs=[S...  2.89 us
    unnamed x6, local copies, waits for them, and re-layouts  2.4 us
    pallas_call x1, Pallas kernels, local(): pl.pallas_call(functools.partial(weight_kernel, group, wide), in_specs=[V...  1.37 us
  transfers between devices with their start and end apart: 16, of which 6 were waited for; matrix products, arithmetic and copies ran while one was open for 1% of the time, Pallas kernels for 8%

profile of v17, /device:TPU:0, one launch (start us, length us, event | category | flops | bytes accessed | tf_op | source)
XLA Modules:
  0.0 49.1 jit_solution(13320437364119085058)
XLA Ops:
  0.6 3.0 %collective-permute-start = (bf16[48,1152]{1,0:T(8,128)(2,1)}, bf16[48,1152]{1,0:T(8,128)(2,1)S(1)}, u32[]{:S(2)}, u32[]{:S(2)}) collective-permute-start(bf16[48,1152]{1,0:T(8,128)(2,1)} %refs_0_.1), channel_id=1, source_target_pairs={{0,2},{1,3},{2,0},{3,1},{4,6},{5,7},{6,4},{7,5},{8,10},{9,11},{10,... | collective-permute-start | bytes 331784 | tf_op jit(solution)/shard_map/ppermute | solution.py:31
  3.7 1.5 %collective-permute-start.1 = (bf16[48,1152]{1,0:T(8,128)(2,1)}, bf16[48,1152]{1,0:T(8,128)(2,1)S(1)}, u32[]{:S(2)}, u32[]{:S(2)}) collective-permute-start(bf16[48,1152]{1,0:T(8,128)(2,1)} %refs_0_.1), channel_id=1, source_target_pairs={{0,4},{1,5},{2,6},{3,7},{4,0},{5,1},{6,2},{7,3},{8,12},{9,13},{10,... | collective-permute-start | bytes 331784 | tf_op jit(solution)/shard_map/ppermute | solution.py:31
  5.2 4.0 %collective-permute-start.3 = (bf16[48,1152]{1,0:T(8,128)(2,1)}, bf16[48,1152]{1,0:T(8,128)(2,1)S(1)}, u32[]{:S(2)}, u32[]{:S(2)}) collective-permute-start(bf16[48,1152]{1,0:T(8,128)(2,1)} %text_ref.1), channel_id=1, source_target_pairs={{0,24},{1,25},{2,26},{3,27},{4,28},{5,29},{6,30},{7,31},{8,16},{9,... | collective-permute-start | bytes 331784 | tf_op jit(solution)/shard_map/ppermute | solution.py:31
  10.6 0.6 %collective-permute-start.5 = (bf16[48,1152]{1,0:T(8,128)(2,1)}, bf16[48,1152]{1,0:T(8,128)(2,1)S(1)}, u32[]{:S(2)}, u32[]{:S(2)}) collective-permute-start(bf16[48,1152]{1,0:T(8,128)(2,1)} %text_ref.1), channel_id=1, source_target_pairs={{0,8},{1,9},{2,10},{3,11},{4,12},{5,13},{6,14},{7,15},{8,0},{9,1},... | collective-permute-start | bytes 331784 | tf_op jit(solution)/shard_map/ppermute | solution.py:31
  11.2 0.9 %copy-done.2 = bf16[48,1152]{1,0:T(8,128)(2,1)S(1)} copy-done((bf16[48,1152]{1,0:T(8,128)(2,1)S(1)}, bf16[48,1152]{1,0:T(8,128)(2,1)}, u32[]{:S(2)}) %copy-start.2) | copy-done | bytes 110616
  12.4 1.5 %copy-done = bf16[1152,1152]{1,0:T(8,128)(2,1)S(1)} copy-done((bf16[1152,1152]{1,0:T(8,128)(2,1)S(1)}, bf16[1152,1152]{1,0:T(8,128)(2,1)}, u32[]{:S(2)}) %copy-start) | copy-done | bytes 2654232
  13.9 0.8 %own_projection.1.own_proj = f32[192,1152]{1,0:T(8,128)S(1)} custom-call(bf16[192,1152]{1,0:T(8,128)(2,1)S(1)} %stack.1.feats_ref.own_half, bf16[1152,1152]{1,0:T(8,128)(2,1)S(1)} %copy-done), custom_call_target="tpu_custom_call" | custom-call | tf_op jit(solution)/shard_map/own_projection/pallas_call | solution.py:296
  14.7 3.3 %collective-permute-done.4.refs_2_ = bf16[48,1152]{1,0:T(8,128)(2,1)S(1)} collective-permute-done((bf16[48,1152]{1,0:T(8,128)(2,1)}, bf16[48,1152]{1,0:T(8,128)(2,1)S(1)}, u32[]{:S(2)}, u32[]{:S(2)}) %collective-permute-start.4) | collective-permute-done | bytes 110624 | tf_op jit(solution)/shard_map/ppermute | solution.py:31
  18.1 2.9 %pairs.1 = (bf16[384,1152]{1,0:T(8,128)(2,1)S(1)}, f32[1,384]{1,0:T(1,128)S(1)}, bf16[1152,384]{1,0:T(8,128)(2,1)S(1)}, bf16[192,384]{1,0:T(8,128)(2,1)S(1)}, f3...) custom-call(s32[1]{0:T(128)} %bitcast.member_ref, ...), custom_call_target="tpu_custom_call" | custom-call | tf_op jit(solution)/shard_map/pairs/pallas_call | solution.py:315
  21.1 0.5 %collective-permute-start.7 = (bf16[2,160,384]{2,1,0:T(8,128)(2,1)S(1)}, bf16[2,160,384]{2,1,0:T(8,128)(2,1)S(1)}, u32[]{:S(2)}, u32[]{:S(2)}) collective-permute-start(bf16[2,160,384]{2,1,0:T(8,128)(2,1)S(1)} %get-tuple-element.34), channel_id=1, source_target_pairs={{0,1},{1,0},{2,3},{3,2},{4,5},{5,4},{6,7},{7,6},{8,9},{9,8},{10,11... | collective-permute-start | bytes 737288 | tf_op jit(solution)/shard_map/ppermute | solution.py:31
  21.6 1.0 %collective-permute-done.8.got_ref = bf16[2,160,384]{2,1,0:T(8,128)(2,1)S(1)} collective-permute-done((bf16[2,160,384]{2,1,0:T(8,128)(2,1)S(1)}, bf16[2,160,384]{2,1,0:T(8,128)(2,1)S(1)}, u32[]{:S(2)}, u32[]{:S(2)}) %collective-permute-start.8) | collective-permute-done | bytes 245792 | tf_op jit(solution)/shard_map/ppermute | solution.py:31
  22.7 2.5 %collective-permute-start.10 = (bf16[160,384]{1,0:T(8,128)(2,1)S(1)}, bf16[160,384]{1,0:T(8,128)(2,1)S(1)}, u32[]{:S(2)}, u32[]{:S(2)}) collective-permute-start(bf16[160,384]{1,0:T(8,128)(2,1)S(1)} %get-tuple-element.38), channel_id=1, source_target_pairs={{0,6},{1,7},{2,4},{3,5},{4,2},{5,3},{6,0},{7,1},{8,14},{9,15},{10,... | collective-permute-start | bytes 368648 | tf_op jit(solution)/shard_map/ppermute | solution.py:31
  25.2 0.5 %collective-permute-start.9 = (bf16[160,384]{1,0:T(8,128)(2,1)S(1)}, bf16[160,384]{1,0:T(8,128)(2,1)S(1)}, u32[]{:S(2)}, u32[]{:S(2)}) collective-permute-start(bf16[160,384]{1,0:T(8,128)(2,1)S(1)} %get-tuple-element.37), channel_id=1, source_target_pairs={{0,4},{1,5},{2,6},{3,7},{4,0},{5,1},{6,2},{7,3},{8,12},{9,13},{10,... | collective-permute-start | bytes 368648 | tf_op jit(solution)/shard_map/ppermute | solution.py:31
  25.8 0.6 %collective-permute-start.11 = (bf16[160,384]{1,0:T(8,128)(2,1)S(1)}, bf16[160,384]{1,0:T(8,128)(2,1)S(1)}, u32[]{:S(2)}, u32[]{:S(2)}) collective-permute-start(bf16[160,384]{1,0:T(8,128)(2,1)S(1)} %get-tuple-element.39), channel_id=1, source_target_pairs={{0,2},{1,3},{2,0},{3,1},{4,6},{5,7},{6,4},{7,5},{8,10},{9,11},{10,... | collective-permute-start | bytes 368648 | tf_op jit(solution)/shard_map/ppermute | solution.py:31
  26.3 0.5 %captions.1 = (bf16[1152,384]{1,0:T(8,128)(2,1)S(1)}, f32[48,1152]{1,0:T(8,128)S(1)}, bf16[48,1152]{1,0:T(8,128)(2,1)S(1)}, bf16[48,1152]{1,0:T(8,128)(2,1)S(1)}, bf16[48,1152]{1,0:T(8,128)(2,1)S(1)}) custom-call(bf16[192,384]{1,0:T(8,128)(2,1)S(1)} %get-tuple-element.42.grad_ref, bf16[1152,384]{1,0:T(8,128)(2,1)S(1)} %get-tuple-element.43.emb_ref, ...), custom_call_target="tpu_custom_call" | custom-call | tf_op jit(solution)/shard_map/captions/pallas_call | solution.py:350
  26.8 2.5 %collective-permute-start.12 = (bf16[48,1152]{1,0:T(8,128)(2,1)S(1)}, bf16[48,1152]{1,0:T(8,128)(2,1)S(1)}, u32[]{:S(2)}, u32[]{:S(2)}) collective-permute-start(bf16[48,1152]{1,0:T(8,128)(2,1)S(1)} %get-tuple-element.47), channel_id=1, source_target_pairs={{0,24},{1,25},{2,26},{3,27},{4,28},{5,29},{6,30},{7,31},{8,16},{9,... | collective-permute-start | bytes 331784 | tf_op jit(solution)/shard_map/ppermute | solution.py:31
  29.8 1.5 %collective-permute-start.14 = (bf16[48,1152]{1,0:T(8,128)(2,1)S(1)}, bf16[48,1152]{1,0:T(8,128)(2,1)S(1)}, u32[]{:S(2)}, u32[]{:S(2)}) collective-permute-start(bf16[48,1152]{1,0:T(8,128)(2,1)S(1)} %get-tuple-element.49), channel_id=1, source_target_pairs={{0,8},{1,9},{2,10},{3,11},{4,12},{5,13},{6,14},{7,15},{8,0},{9,1},... | collective-permute-start | bytes 331784 | tf_op jit(solution)/shard_map/ppermute | solution.py:31
  31.7 1.4 %weights.1 = (f32[1,384]{1,0:T(1,128)S(1)}, bf16[8,176,128]{2,1,0:T(8,128)(2,1)}) custom-call(f32[152,384]{1,0:T(8,128)S(1)} %far_sum.1.refs_0_, bf16[160,384]{1,0:T(8,128)(2,1)S(1)} %collective-permute-done.11.refs_1_, f32[1,384]{1,0:T(1,128)S(1)} %get-tuple-element.40.refs_2_, bf16[384,1152]{1,0:T(8,128)(2,1)S(1)} %get-tuple-element.41.feats_ref.refs_3_, ...), custom_call_target="tpu_custom_call" | custom-call | tf_op jit(solution)/shard_map/weights/pallas_call | solution.py:384
  33.1 4.7 %all-to-all-start = ((bf16[8,176,128]{2,1,0:T(8,128)(2,1)}), bf16[8,176,128]{2,1,0:T(8,128)(2,1)S(1)}, u32[]{:S(2)}, u32[]{:S(2)}) async-start(bf16[8,176,128]{2,1,0:T(8,128)(2,1)} %get-tuple-element.50), calls=%async_computation | async-start | bytes 720896 | tf_op jit(solution)/shard_map/all_to_all | solution.py:395
  37.8 0.7 %collective-permute-done.13.refs_2_ = bf16[48,1152]{1,0:T(8,128)(2,1)S(1)} collective-permute-done((bf16[48,1152]{1,0:T(8,128)(2,1)S(1)}, bf16[48,1152]{1,0:T(8,128)(2,1)S(1)}, u32[]{:S(2)}, u32[]{:S(2)}) %collective-permute-start.13) | collective-permute-done | bytes 110624 | tf_op jit(solution)/shard_map/ppermute | solution.py:31
  38.5 0.7 %caption_total.1 = f32[48,1152]{1,0:T(8,128)} custom-call(f32[48,1152]{1,0:T(8,128)S(1)} %get-tuple-element.46.refs_0_, bf16[48,1152]{1,0:T(8,128)(2,1)S(1)} %collective-permute-done.12.refs_1_, bf16[48,1152]{1,0:T(8,128)(2,1)S(1)} %collective-permute-done.13.refs_2_, bf16[48,1152]{1,0:T(8,128)(2,1)S(1)} %collective-permute-done.14.refs_3_), custom_call_target="tpu_custom_call" | custom-call | flops 5000000000 | tf_op jit(solution)/shard_map/caption_total/pallas_call | solution.py:426
  39.2 0.6 %dynamic-slice_bitcast_fusion = f32[48]{0:T(128)} fusion(f32[1,384]{1,0:T(1,128)S(1)} %get-tuple-element.45, s32[]{:T(128)S(6)} %select_n.16), kind=kLoop, calls=%fused_computation | loop fusion | bytes 388 | tf_op jit(solution)/shard_map/dynamic_slice | solution.py:435
  39.8 8.5 %all-to-all-done.got_ref = bf16[8,176,128]{2,1,0:T(8,128)(2,1)S(1)} async-done(((bf16[8,176,128]{2,1,0:T(8,128)(2,1)}), bf16[8,176,128]{2,1,0:T(8,128)(2,1)S(1)}, u32[]{:S(2)}, u32[]{:S(2)}) %all-to-all-start) | async-done | bytes 360480 | tf_op jit(solution)/shard_map/all_to_all | solution.py:395
  48.2 0.9 %weight_total.1 = f32[144,288]{1,0:T(8,128)} custom-call(bf16[8,176,128]{2,1,0:T(8,128)(2,1)S(1)} %all-to-all-done.got_ref), custom_call_target="tpu_custom_call" | custom-call | tf_op jit(solution)/shard_map/weight_total/pallas_call | solution.py:396
  (27 shorter events, 1.5 us)
Async XLA Ops:
  0.6 9.9 %collective-permute-start = (bf16[48,1152]{1,0:T(8,128)(2,1)}, bf16[48,1152]{1,0:T(8,128)(2,1)S(1)}, u32[]{:S(2)}, u32[]{:S(2)}) collective-permute-start(bf16[48,1152]{1,0:T(8,128)(2,1)} %refs_0_.1), channel_id=1, source_target_pairs={{0,2},{1,3},{2,0},{3,1},{4,6},{5,7},{6,4},{7,5},{8,10},{9,11},{10,... | collective-permute-start | bytes 331784 | tf_op jit(solution)/shard_map/ppermute | solution.py:31
  3.7 8.6 %collective-permute-start.1 = (bf16[48,1152]{1,0:T(8,128)(2,1)}, bf16[48,1152]{1,0:T(8,128)(2,1)S(1)}, u32[]{:S(2)}, u32[]{:S(2)}) collective-permute-start(bf16[48,1152]{1,0:T(8,128)(2,1)} %refs_0_.1), channel_id=1, source_target_pairs={{0,4},{1,5},{2,6},{3,7},{4,0},{5,1},{6,2},{7,3},{8,12},{9,13},{10,... | collective-permute-start | bytes 331784 | tf_op jit(solution)/shard_map/ppermute | solution.py:31
  5.2 7.1 %collective-permute-start.2 = (bf16[48,1152]{1,0:T(8,128)(2,1)}, bf16[48,1152]{1,0:T(8,128)(2,1)S(1)}, u32[]{:S(2)}, u32[]{:S(2)}) collective-permute-start(bf16[48,1152]{1,0:T(8,128)(2,1)} %refs_0_.1), channel_id=1, source_target_pairs={{0,6},{1,7},{2,4},{3,5},{4,2},{5,3},{6,0},{7,1},{8,14},{9,15},{10,... | collective-permute-start | bytes 331784 | tf_op jit(solution)/shard_map/ppermute | solution.py:31
  5.2 9.5 %collective-permute-start.3 = (bf16[48,1152]{1,0:T(8,128)(2,1)}, bf16[48,1152]{1,0:T(8,128)(2,1)S(1)}, u32[]{:S(2)}, u32[]{:S(2)}) collective-permute-start(bf16[48,1152]{1,0:T(8,128)(2,1)} %text_ref.1), channel_id=1, source_target_pairs={{0,24},{1,25},{2,26},{3,27},{4,28},{5,29},{6,30},{7,31},{8,16},{9,... | collective-permute-start | bytes 331784 | tf_op jit(solution)/shard_map/ppermute | solution.py:31
  9.2 8.7 %collective-permute-start.4 = (bf16[48,1152]{1,0:T(8,128)(2,1)}, bf16[48,1152]{1,0:T(8,128)(2,1)S(1)}, u32[]{:S(2)}, u32[]{:S(2)}) collective-permute-start(bf16[48,1152]{1,0:T(8,128)(2,1)} %text_ref.1), channel_id=1, source_target_pairs={{0,16},{1,17},{2,18},{3,19},{4,20},{5,21},{6,22},{7,23},{8,24},{9,... | collective-permute-start | bytes 331784 | tf_op jit(solution)/shard_map/ppermute | solution.py:31
  10.5 1.7 %copy-start.1 = (bf16[48,1152]{1,0:T(8,128)(2,1)S(1)}, bf16[48,1152]{1,0:T(8,128)(2,1)}, u32[]{:S(2)}) copy-start(bf16[48,1152]{1,0:T(8,128)(2,1)} %refs_0_.1) | copy-start | bytes 331780
  10.6 7.4 %collective-permute-start.5 = (bf16[48,1152]{1,0:T(8,128)(2,1)}, bf16[48,1152]{1,0:T(8,128)(2,1)S(1)}, u32[]{:S(2)}, u32[]{:S(2)}) collective-permute-start(bf16[48,1152]{1,0:T(8,128)(2,1)} %text_ref.1), channel_id=1, source_target_pairs={{0,8},{1,9},{2,10},{3,11},{4,12},{5,13},{6,14},{7,15},{8,0},{9,1},... | collective-permute-start | bytes 331784 | tf_op jit(solution)/shard_map/ppermute | solution.py:31
  11.2 0.9 %copy-start.2 = (bf16[48,1152]{1,0:T(8,128)(2,1)S(1)}, bf16[48,1152]{1,0:T(8,128)(2,1)}, u32[]{:S(2)}) copy-start(bf16[48,1152]{1,0:T(8,128)(2,1)} %text_ref.1) | copy-start | bytes 331780
  12.1 1.7 %copy-start = (bf16[1152,1152]{1,0:T(8,128)(2,1)S(1)}, bf16[1152,1152]{1,0:T(8,128)(2,1)}, u32[]{:S(2)}) copy-start(bf16[1152,1152]{1,0:T(8,128)(2,1)} %weight.1) | copy-start | bytes 7962628
  12.3 5.8 %collective-permute-start.6 = (bf16[192,1152]{1,0:T(8,128)(2,1)S(1)}, bf16[192,1152]{1,0:T(8,128)(2,1)S(1)}, u32[]{:S(2)}, u32[]{:S(2)}) collective-permute-start(bf16[192,1152]{1,0:T(8,128)(2,1)S(1)} %stack.1.feats_ref.own_half), channel_id=1, source_target_pairs={{0,1},{1,0},{2,3},{3,2},{4,5},{5,4},{6,7},{7,6},{8,9},{9,8},{10,11... | collective-permute-start | bytes 1327112 | tf_op jit(solution)/shard_map/ppermute | solution.py:31
  21.0 1.6 %collective-permute-start.8 = (bf16[2,160,384]{2,1,0:T(8,128)(2,1)S(1)}, bf16[2,160,384]{2,1,0:T(8,128)(2,1)S(1)}, u32[]{:S(2)}, u32[]{:S(2)}) collective-permute-start(bf16[2,160,384]{2,1,0:T(8,128)(2,1)S(1)} %get-tuple-element.36), channel_id=1, source_target_pairs={{0,1},{1,0},{2,3},{3,2},{4,5},{5,4},{6,7},{7,6},{8,9},{9,8},{10,11... | collective-permute-start | bytes 737288 | tf_op jit(solution)/shard_map/ppermute | solution.py:31
  21.1 4.6 %collective-permute-start.7 = (bf16[2,160,384]{2,1,0:T(8,128)(2,1)S(1)}, bf16[2,160,384]{2,1,0:T(8,128)(2,1)S(1)}, u32[]{:S(2)}, u32[]{:S(2)}) collective-permute-start(bf16[2,160,384]{2,1,0:T(8,128)(2,1)S(1)} %get-tuple-element.34), channel_id=1, source_target_pairs={{0,1},{1,0},{2,3},{3,2},{4,5},{5,4},{6,7},{7,6},{8,9},{9,8},{10,11... | collective-permute-start | bytes 737288 | tf_op jit(solution)/shard_map/ppermute | solution.py:31
  22.7 7.1 %collective-permute-start.10 = (bf16[160,384]{1,0:T(8,128)(2,1)S(1)}, bf16[160,384]{1,0:T(8,128)(2,1)S(1)}, u32[]{:S(2)}, u32[]{:S(2)}) collective-permute-start(bf16[160,384]{1,0:T(8,128)(2,1)S(1)} %get-tuple-element.38), channel_id=1, source_target_pairs={{0,6},{1,7},{2,4},{3,5},{4,2},{5,3},{6,0},{7,1},{8,14},{9,15},{10,... | collective-permute-start | bytes 368648 | tf_op jit(solution)/shard_map/ppermute | solution.py:31
  25.2 6.5 %collective-permute-start.9 = (bf16[160,384]{1,0:T(8,128)(2,1)S(1)}, bf16[160,384]{1,0:T(8,128)(2,1)S(1)}, u32[]{:S(2)}, u32[]{:S(2)}) collective-permute-start(bf16[160,384]{1,0:T(8,128)(2,1)S(1)} %get-tuple-element.37), channel_id=1, source_target_pairs={{0,4},{1,5},{2,6},{3,7},{4,0},{5,1},{6,2},{7,3},{8,12},{9,13},{10,... | collective-permute-start | bytes 368648 | tf_op jit(solution)/shard_map/ppermute | solution.py:31
  25.8 6.0 %collective-permute-start.11 = (bf16[160,384]{1,0:T(8,128)(2,1)S(1)}, bf16[160,384]{1,0:T(8,128)(2,1)S(1)}, u32[]{:S(2)}, u32[]{:S(2)}) collective-permute-start(bf16[160,384]{1,0:T(8,128)(2,1)S(1)} %get-tuple-element.39), channel_id=1, source_target_pairs={{0,2},{1,3},{2,0},{3,1},{4,6},{5,7},{6,4},{7,5},{8,10},{9,11},{10,... | collective-permute-start | bytes 368648 | tf_op jit(solution)/shard_map/ppermute | solution.py:31
  26.8 10.9 %collective-permute-start.12 = (bf16[48,1152]{1,0:T(8,128)(2,1)S(1)}, bf16[48,1152]{1,0:T(8,128)(2,1)S(1)}, u32[]{:S(2)}, u32[]{:S(2)}) collective-permute-start(bf16[48,1152]{1,0:T(8,128)(2,1)S(1)} %get-tuple-element.47), channel_id=1, source_target_pairs={{0,24},{1,25},{2,26},{3,27},{4,28},{5,29},{6,30},{7,31},{8,16},{9,... | collective-permute-start | bytes 331784 | tf_op jit(solution)/shard_map/ppermute | solution.py:31
  29.4 9.1 %collective-permute-start.13 = (bf16[48,1152]{1,0:T(8,128)(2,1)S(1)}, bf16[48,1152]{1,0:T(8,128)(2,1)S(1)}, u32[]{:S(2)}, u32[]{:S(2)}) collective-permute-start(bf16[48,1152]{1,0:T(8,128)(2,1)S(1)} %get-tuple-element.48), channel_id=1, source_target_pairs={{0,16},{1,17},{2,18},{3,19},{4,20},{5,21},{6,22},{7,23},{8,24},{9,... | collective-permute-start | bytes 331784 | tf_op jit(solution)/shard_map/ppermute | solution.py:31
  29.8 8.7 %collective-permute-start.14 = (bf16[48,1152]{1,0:T(8,128)(2,1)S(1)}, bf16[48,1152]{1,0:T(8,128)(2,1)S(1)}, u32[]{:S(2)}, u32[]{:S(2)}) collective-permute-start(bf16[48,1152]{1,0:T(8,128)(2,1)S(1)} %get-tuple-element.49), channel_id=1, source_target_pairs={{0,8},{1,9},{2,10},{3,11},{4,12},{5,13},{6,14},{7,15},{8,0},{9,1},... | collective-permute-start | bytes 331784 | tf_op jit(solution)/shard_map/ppermute | solution.py:31
  33.1 15.1 %all-to-all-start = ((bf16[8,176,128]{2,1,0:T(8,128)(2,1)}), bf16[8,176,128]{2,1,0:T(8,128)(2,1)S(1)}, u32[]{:S(2)}, u32[]{:S(2)}) async-start(bf16[8,176,128]{2,1,0:T(8,128)(2,1)} %get-tuple-element.50), calls=%async_computation | async-start | bytes 720896 | tf_op jit(solution)/shard_map/all_to_all | solution.py:395

commit v18 on v17

--- a/solution.py
+++ b/solution.py
@@ -262,6 +262,18 @@
     for block in refs[1:-1]:
         total = total + block[...].astype(F32)
     refs[-1][...] = total
+
+
+def added(own, parts, cost):
+    return pl.pallas_call(
+        sum_kernel,
+        in_specs=[VMEM] * (1 + len(parts)),
+        out_specs=VMEM,
+        out_shape=jax.ShapeDtypeStruct(own.shape, F32),
+        compiler_params=limit(12),
+        cost_estimate=cost,
+        name="caption_sum",
+    )(own, *parts)
 
 
 def local(wide, narrow, image_feats, proj_weight, text_embed, log_scale, logit_bias):
@@ -423,15 +435,9 @@
         both = jnp.concatenate([jnp.where(left, partial, 0.0), jnp.where(left, 0.0, partial)], axis=1)
         d_proj = lax.psum_scatter(both, AXES[:2], scatter_dimension=0, tiled=True)
 
-    d_text_unit = pl.pallas_call(
-        sum_kernel,
-        in_specs=[VMEM] * spread,
-        out_specs=VMEM,
-        out_shape=jax.ShapeDtypeStruct((rows, width), F32),
-        compiler_params=limit(12),
-        cost_estimate=hint(5 * 10**9),
-        name="caption_total",
-    )(own_text, *got_text[::-1])
+    if len(got_text) > 1:
+        own_text = added(own_text, got_text[:0:-1], hint(5 * 10**9))
+    d_text_unit = added(own_text, got_text[:1], None)
     image_loss = lax.dynamic_slice_in_dim(loss_line[0], first_image(member[0], rows, group), rows, 0)
     return (image_loss, d_text_unit, d_proj)
 

time: 49.4 us -> 50.2 us (1.016)
    ppermute x15, waiting for transfers between devices: 5.75 us -> 14.5 us  [swapped(): lax.ppermute(value, AXES, [(source, source ^ mask) for source in range(to...]
    all_to_all x1, waiting for transfers between devices: 8.45 us -> 0.01 us  [local(): got_weight = lax.all_to_all(sent_weight, AXES[:2], 0, 0)]
  transfers between devices with their start and end apart: 16 -> 16, of which waited for: 6 -> 5; matrix products, arithmetic and copies ran while one was open for 1% -> 1% of each run, Pallas kernels for 8% -> 8%
where the time goes in v18:
time: 50.2 us; the launch traced here: 49.9 us
  starting transfers between devices  22.7 us (45%)
  waiting for transfers between devices  14.5 us (29%)
  Pallas kernels  7.66 us (15%)
  local copies, waits for them, and re-layouts  2.98 us (6%)
  between operations  2.08 us (4%)
    ppermute x15, starting transfers between devices, swapped(): lax.ppermute(value, AXES, [(source, source ^ mask) for source in range(to...  18 us
    ppermute x15, waiting for transfers between devices, swapped(): lax.ppermute(value, AXES, [(source, source ^ mask) for source in range(to...  14.5 us
    all_to_all x1, starting transfers between devices, local(): got_weight = lax.all_to_all(sent_weight, AXES[:2], 0, 0)  4.65 us
    pallas_call x1, Pallas kernels, local(): pl.pallas_call(functools.partial(pair_kernel, narrow, group), in_specs=[S...  2.89 us
    unnamed x6, local copies, waits for them, and re-layouts  2.4 us
    pallas_call x1, Pallas kernels, local(): pl.pallas_call(functools.partial(weight_kernel, group, wide), in_specs=[V...  1.38 us
  transfers between devices with their start and end apart: 16, of which 5 were waited for; matrix products, arithmetic and copies ran while one was open for 1% of the time, Pallas kernels for 8%

profile of v18, /device:TPU:0, one launch (start us, length us, event | category | flops | bytes accessed | tf_op | source)
XLA Modules:
  0.0 49.9 jit_solution(8298165091490012381)
XLA Ops:
  0.6 3.0 %collective-permute-start = (bf16[48,1152]{1,0:T(8,128)(2,1)}, bf16[48,1152]{1,0:T(8,128)(2,1)S(1)}, u32[]{:S(2)}, u32[]{:S(2)}) collective-permute-start(bf16[48,1152]{1,0:T(8,128)(2,1)} %refs_0_.1), channel_id=1, source_target_pairs={{0,2},{1,3},{2,0},{3,1},{4,6},{5,7},{6,4},{7,5},{8,10},{9,11},{10,... | collective-permute-start | bytes 331784 | tf_op jit(solution)/shard_map/ppermute | solution.py:31
  3.7 1.5 %collective-permute-start.1 = (bf16[48,1152]{1,0:T(8,128)(2,1)}, bf16[48,1152]{1,0:T(8,128)(2,1)S(1)}, u32[]{:S(2)}, u32[]{:S(2)}) collective-permute-start(bf16[48,1152]{1,0:T(8,128)(2,1)} %refs_0_.1), channel_id=1, source_target_pairs={{0,4},{1,5},{2,6},{3,7},{4,0},{5,1},{6,2},{7,3},{8,12},{9,13},{10,... | collective-permute-start | bytes 331784 | tf_op jit(solution)/shard_map/ppermute | solution.py:31
  5.2 4.0 %collective-permute-start.3 = (bf16[48,1152]{1,0:T(8,128)(2,1)}, bf16[48,1152]{1,0:T(8,128)(2,1)S(1)}, u32[]{:S(2)}, u32[]{:S(2)}) collective-permute-start(bf16[48,1152]{1,0:T(8,128)(2,1)} %text_ref.1), channel_id=1, source_target_pairs={{0,24},{1,25},{2,26},{3,27},{4,28},{5,29},{6,30},{7,31},{8,16},{9,... | collective-permute-start | bytes 331784 | tf_op jit(solution)/shard_map/ppermute | solution.py:31
  10.6 0.6 %collective-permute-start.5 = (bf16[48,1152]{1,0:T(8,128)(2,1)}, bf16[48,1152]{1,0:T(8,128)(2,1)S(1)}, u32[]{:S(2)}, u32[]{:S(2)}) collective-permute-start(bf16[48,1152]{1,0:T(8,128)(2,1)} %text_ref.1), channel_id=1, source_target_pairs={{0,8},{1,9},{2,10},{3,11},{4,12},{5,13},{6,14},{7,15},{8,0},{9,1},... | collective-permute-start | bytes 331784 | tf_op jit(solution)/shard_map/ppermute | solution.py:31
  11.2 0.9 %copy-done.2 = bf16[48,1152]{1,0:T(8,128)(2,1)S(1)} copy-done((bf16[48,1152]{1,0:T(8,128)(2,1)S(1)}, bf16[48,1152]{1,0:T(8,128)(2,1)}, u32[]{:S(2)}) %copy-start.2) | copy-done | bytes 110616
  12.4 1.5 %copy-done = bf16[1152,1152]{1,0:T(8,128)(2,1)S(1)} copy-done((bf16[1152,1152]{1,0:T(8,128)(2,1)S(1)}, bf16[1152,1152]{1,0:T(8,128)(2,1)}, u32[]{:S(2)}) %copy-start) | copy-done | bytes 2654232
  13.9 0.8 %own_projection.1.own_proj = f32[192,1152]{1,0:T(8,128)S(1)} custom-call(bf16[192,1152]{1,0:T(8,128)(2,1)S(1)} %stack.1.feats_ref.own_half, bf16[1152,1152]{1,0:T(8,128)(2,1)S(1)} %copy-done), custom_call_target="tpu_custom_call" | custom-call | tf_op jit(solution)/shard_map/own_projection/pallas_call | solution.py:308
  14.7 3.3 %collective-permute-done.4.refs_2_ = bf16[48,1152]{1,0:T(8,128)(2,1)S(1)} collective-permute-done((bf16[48,1152]{1,0:T(8,128)(2,1)}, bf16[48,1152]{1,0:T(8,128)(2,1)S(1)}, u32[]{:S(2)}, u32[]{:S(2)}) %collective-permute-start.4) | collective-permute-done | bytes 110624 | tf_op jit(solution)/shard_map/ppermute | solution.py:31
  18.1 2.9 %pairs.1 = (bf16[384,1152]{1,0:T(8,128)(2,1)S(1)}, f32[1,384]{1,0:T(1,128)S(1)}, bf16[1152,384]{1,0:T(8,128)(2,1)S(1)}, bf16[192,384]{1,0:T(8,128)(2,1)S(1)}, f3...) custom-call(s32[1]{0:T(128)} %bitcast.member_ref, ...), custom_call_target="tpu_custom_call" | custom-call | tf_op jit(solution)/shard_map/pairs/pallas_call | solution.py:327
  21.1 0.5 collective-permute-start.7
  21.6 1.0 %collective-permute-done.8.got_ref = bf16[2,160,384]{2,1,0:T(8,128)(2,1)S(1)} collective-permute-done((bf16[2,160,384]{2,1,0:T(8,128)(2,1)S(1)}, bf16[2,160,384]{2,1,0:T(8,128)(2,1)S(1)}, u32[]{:S(2)}, u32[]{:S(2)}) %collective-permute-start.8) | collective-permute-done | bytes 245792 | tf_op jit(solution)/shard_map/ppermute | solution.py:31
  22.7 2.5 %collective-permute-start.10 = (bf16[160,384]{1,0:T(8,128)(2,1)S(1)}, bf16[160,384]{1,0:T(8,128)(2,1)S(1)}, u32[]{:S(2)}, u32[]{:S(2)}) collective-permute-start(bf16[160,384]{1,0:T(8,128)(2,1)S(1)} %get-tuple-element.38), channel_id=1, source_target_pairs={{0,6},{1,7},{2,4},{3,5},{4,2},{5,3},{6,0},{7,1},{8,14},{9,15},{10,... | collective-permute-start | bytes 368648 | tf_op jit(solution)/shard_map/ppermute | solution.py:31
  25.2 0.5 %collective-permute-start.9 = (bf16[160,384]{1,0:T(8,128)(2,1)S(1)}, bf16[160,384]{1,0:T(8,128)(2,1)S(1)}, u32[]{:S(2)}, u32[]{:S(2)}) collective-permute-start(bf16[160,384]{1,0:T(8,128)(2,1)S(1)} %get-tuple-element.37), channel_id=1, source_target_pairs={{0,4},{1,5},{2,6},{3,7},{4,0},{5,1},{6,2},{7,3},{8,12},{9,13},{10,... | collective-permute-start | bytes 368648 | tf_op jit(solution)/shard_map/ppermute | solution.py:31
  25.8 0.6 %collective-permute-start.11 = (bf16[160,384]{1,0:T(8,128)(2,1)S(1)}, bf16[160,384]{1,0:T(8,128)(2,1)S(1)}, u32[]{:S(2)}, u32[]{:S(2)}) collective-permute-start(bf16[160,384]{1,0:T(8,128)(2,1)S(1)} %get-tuple-element.39), channel_id=1, source_target_pairs={{0,2},{1,3},{2,0},{3,1},{4,6},{5,7},{6,4},{7,5},{8,10},{9,11},{10,... | collective-permute-start | bytes 368648 | tf_op jit(solution)/shard_map/ppermute | solution.py:31
  26.3 0.5 %captions.1 = (bf16[1152,384]{1,0:T(8,128)(2,1)S(1)}, f32[48,1152]{1,0:T(8,128)S(1)}, bf16[48,1152]{1,0:T(8,128)(2,1)S(1)}, bf16[48,1152]{1,0:T(8,128)(2,1)S(1)}, bf16[48,1152]{1,0:T(8,128)(2,1)S(1)}) custom-call(bf16[192,384]{1,0:T(8,128)(2,1)S(1)} %get-tuple-element.42.grad_ref, bf16[1152,384]{1,0:T(8,128)(2,1)S(1)} %get-tuple-element.43.emb_ref, ...), custom_call_target="tpu_custom_call" | custom-call | tf_op jit(solution)/shard_map/captions/pallas_call | solution.py:362
  26.8 2.5 %collective-permute-start.12 = (bf16[48,1152]{1,0:T(8,128)(2,1)S(1)}, bf16[48,1152]{1,0:T(8,128)(2,1)S(1)}, u32[]{:S(2)}, u32[]{:S(2)}) collective-permute-start(bf16[48,1152]{1,0:T(8,128)(2,1)S(1)} %get-tuple-element.47), channel_id=1, source_target_pairs={{0,24},{1,25},{2,26},{3,27},{4,28},{5,29},{6,30},{7,31},{8,16},{9,... | collective-permute-start | bytes 331784 | tf_op jit(solution)/shard_map/ppermute | solution.py:31
  29.8 1.9 %collective-permute-done.9.refs_1_ = bf16[160,384]{1,0:T(8,128)(2,1)S(1)} collective-permute-done((bf16[160,384]{1,0:T(8,128)(2,1)S(1)}, bf16[160,384]{1,0:T(8,128)(2,1)S(1)}, u32[]{:S(2)}, u32[]{:S(2)}) %collective-permute-start.9) | collective-permute-done | bytes 122912 | tf_op jit(solution)/shard_map/ppermute | solution.py:31
  31.7 1.4 %weights.1 = (f32[1,384]{1,0:T(1,128)S(1)}, bf16[8,176,128]{2,1,0:T(8,128)(2,1)}) custom-call(f32[152,384]{1,0:T(8,128)S(1)} %far_sum.1.refs_0_, bf16[160,384]{1,0:T(8,128)(2,1)S(1)} %collective-permute-done.11.refs_1_, f32[1,384]{1,0:T(1,128)S(1)} %get-tuple-element.40.refs_2_, bf16[384,1152]{1,0:T(8,128)(2,1)S(1)} %get-tuple-element.41.feats_ref.refs_3_, ...), custom_call_target="tpu_custom_call" | custom-call | tf_op jit(solution)/shard_map/weights/pallas_call | solution.py:396
  33.1 4.7 %all-to-all-start = ((bf16[8,176,128]{2,1,0:T(8,128)(2,1)}), bf16[8,176,128]{2,1,0:T(8,128)(2,1)S(1)}, u32[]{:S(2)}, u32[]{:S(2)}) async-start(bf16[8,176,128]{2,1,0:T(8,128)(2,1)} %get-tuple-element.50), calls=%async_computation | async-start | bytes 720896 | tf_op jit(solution)/shard_map/all_to_all | solution.py:407
  37.8 2.0 %collective-permute-start.14 = (bf16[48,1152]{1,0:T(8,128)(2,1)S(1)}, bf16[48,1152]{1,0:T(8,128)(2,1)S(1)}, u32[]{:S(2)}, u32[]{:S(2)}) collective-permute-start(bf16[48,1152]{1,0:T(8,128)(2,1)S(1)} %get-tuple-element.49), channel_id=1, source_target_pairs={{0,8},{1,9},{2,10},{3,11},{4,12},{5,13},{6,14},{7,15},{8,0},{9,1},... | collective-permute-start | bytes 331784 | tf_op jit(solution)/shard_map/ppermute | solution.py:31
  39.8 7.9 %collective-permute-done.14.refs_1_ = bf16[48,1152]{1,0:T(8,128)(2,1)S(1)} collective-permute-done((bf16[48,1152]{1,0:T(8,128)(2,1)S(1)}, bf16[48,1152]{1,0:T(8,128)(2,1)S(1)}, u32[]{:S(2)}, u32[]{:S(2)}) %collective-permute-start.14) | collective-permute-done | bytes 110624 | tf_op jit(solution)/shard_map/ppermute | solution.py:31
  47.8 0.7 %caption_sum.3 = f32[48,1152]{1,0:T(8,128)} custom-call(f32[48,1152]{1,0:T(8,128)S(1)} %caption_sum.2.refs_0_, bf16[48,1152]{1,0:T(8,128)(2,1)S(1)} %collective-permute-done.14.refs_1_), custom_call_target="tpu_custom_call" | custom-call | tf_op jit(solution)/shard_map/caption_sum/pallas_call | solution.py:268
  48.5 0.6 %dynamic-slice_bitcast_fusion = f32[48]{0:T(128)} fusion(f32[1,384]{1,0:T(1,128)S(1)} %get-tuple-element.45, s32[]{:T(128)S(6)} %select_n.16), kind=kLoop, calls=%fused_computation | loop fusion | bytes 388 | tf_op jit(solution)/shard_map/dynamic_slice | solution.py:441
  49.1 0.9 %weight_total.1 = f32[144,288]{1,0:T(8,128)} custom-call(bf16[8,176,128]{2,1,0:T(8,128)(2,1)S(1)} %all-to-all-done.got_ref), custom_call_target="tpu_custom_call" | custom-call | tf_op jit(solution)/shard_map/weight_total/pallas_call | solution.py:408
  (28 shorter events, 1.2 us)
Async XLA Ops:
  0.6 9.9 %collective-permute-start = (bf16[48,1152]{1,0:T(8,128)(2,1)}, bf16[48,1152]{1,0:T(8,128)(2,1)S(1)}, u32[]{:S(2)}, u32[]{:S(2)}) collective-permute-start(bf16[48,1152]{1,0:T(8,128)(2,1)} %refs_0_.1), channel_id=1, source_target_pairs={{0,2},{1,3},{2,0},{3,1},{4,6},{5,7},{6,4},{7,5},{8,10},{9,11},{10,... | collective-permute-start | bytes 331784 | tf_op jit(solution)/shard_map/ppermute | solution.py:31
  3.7 8.6 %collective-permute-start.1 = (bf16[48,1152]{1,0:T(8,128)(2,1)}, bf16[48,1152]{1,0:T(8,128)(2,1)S(1)}, u32[]{:S(2)}, u32[]{:S(2)}) collective-permute-start(bf16[48,1152]{1,0:T(8,128)(2,1)} %refs_0_.1), channel_id=1, source_target_pairs={{0,4},{1,5},{2,6},{3,7},{4,0},{5,1},{6,2},{7,3},{8,12},{9,13},{10,... | collective-permute-start | bytes 331784 | tf_op jit(solution)/shard_map/ppermute | solution.py:31
  5.2 7.1 %collective-permute-start.2 = (bf16[48,1152]{1,0:T(8,128)(2,1)}, bf16[48,1152]{1,0:T(8,128)(2,1)S(1)}, u32[]{:S(2)}, u32[]{:S(2)}) collective-permute-start(bf16[48,1152]{1,0:T(8,128)(2,1)} %refs_0_.1), channel_id=1, source_target_pairs={{0,6},{1,7},{2,4},{3,5},{4,2},{5,3},{6,0},{7,1},{8,14},{9,15},{10,... | collective-permute-start | bytes 331784 | tf_op jit(solution)/shard_map/ppermute | solution.py:31
  5.2 9.5 %collective-permute-start.3 = (bf16[48,1152]{1,0:T(8,128)(2,1)}, bf16[48,1152]{1,0:T(8,128)(2,1)S(1)}, u32[]{:S(2)}, u32[]{:S(2)}) collective-permute-start(bf16[48,1152]{1,0:T(8,128)(2,1)} %text_ref.1), channel_id=1, source_target_pairs={{0,24},{1,25},{2,26},{3,27},{4,28},{5,29},{6,30},{7,31},{8,16},{9,... | collective-permute-start | bytes 331784 | tf_op jit(solution)/shard_map/ppermute | solution.py:31
  9.2 8.7 %collective-permute-start.4 = (bf16[48,1152]{1,0:T(8,128)(2,1)}, bf16[48,1152]{1,0:T(8,128)(2,1)S(1)}, u32[]{:S(2)}, u32[]{:S(2)}) collective-permute-start(bf16[48,1152]{1,0:T(8,128)(2,1)} %text_ref.1), channel_id=1, source_target_pairs={{0,16},{1,17},{2,18},{3,19},{4,20},{5,21},{6,22},{7,23},{8,24},{9,... | collective-permute-start | bytes 331784 | tf_op jit(solution)/shard_map/ppermute | solution.py:31
  10.5 1.7 %copy-start.1 = (bf16[48,1152]{1,0:T(8,128)(2,1)S(1)}, bf16[48,1152]{1,0:T(8,128)(2,1)}, u32[]{:S(2)}) copy-start(bf16[48,1152]{1,0:T(8,128)(2,1)} %refs_0_.1) | copy-start | bytes 331780
  10.6 7.4 %collective-permute-start.5 = (bf16[48,1152]{1,0:T(8,128)(2,1)}, bf16[48,1152]{1,0:T(8,128)(2,1)S(1)}, u32[]{:S(2)}, u32[]{:S(2)}) collective-permute-start(bf16[48,1152]{1,0:T(8,128)(2,1)} %text_ref.1), channel_id=1, source_target_pairs={{0,8},{1,9},{2,10},{3,11},{4,12},{5,13},{6,14},{7,15},{8,0},{9,1},... | collective-permute-start | bytes 331784 | tf_op jit(solution)/shard_map/ppermute | solution.py:31
  11.2 0.9 %copy-start.2 = (bf16[48,1152]{1,0:T(8,128)(2,1)S(1)}, bf16[48,1152]{1,0:T(8,128)(2,1)}, u32[]{:S(2)}) copy-start(bf16[48,1152]{1,0:T(8,128)(2,1)} %text_ref.1) | copy-start | bytes 331780
  12.1 1.7 %copy-start = (bf16[1152,1152]{1,0:T(8,128)(2,1)S(1)}, bf16[1152,1152]{1,0:T(8,128)(2,1)}, u32[]{:S(2)}) copy-start(bf16[1152,1152]{1,0:T(8,128)(2,1)} %weight.1) | copy-start | bytes 7962628
  12.3 5.8 %collective-permute-start.6 = (bf16[192,1152]{1,0:T(8,128)(2,1)S(1)}, bf16[192,1152]{1,0:T(8,128)(2,1)S(1)}, u32[]{:S(2)}, u32[]{:S(2)}) collective-permute-start(bf16[192,1152]{1,0:T(8,128)(2,1)S(1)} %stack.1.feats_ref.own_half), channel_id=1, source_target_pairs={{0,1},{1,0},{2,3},{3,2},{4,5},{5,4},{6,7},{7,6},{8,9},{9,8},{10,11... | collective-permute-start | bytes 1327112 | tf_op jit(solution)/shard_map/ppermute | solution.py:31
  21.0 1.6 %collective-permute-start.8 = (bf16[2,160,384]{2,1,0:T(8,128)(2,1)S(1)}, bf16[2,160,384]{2,1,0:T(8,128)(2,1)S(1)}, u32[]{:S(2)}, u32[]{:S(2)}) collective-permute-start(bf16[2,160,384]{2,1,0:T(8,128)(2,1)S(1)} %get-tuple-element.36), channel_id=1, source_target_pairs={{0,1},{1,0},{2,3},{3,2},{4,5},{5,4},{6,7},{7,6},{8,9},{9,8},{10,11... | collective-permute-start | bytes 737288 | tf_op jit(solution)/shard_map/ppermute | solution.py:31
  21.1 4.6 %collective-permute-start.7 = (bf16[2,160,384]{2,1,0:T(8,128)(2,1)S(1)}, bf16[2,160,384]{2,1,0:T(8,128)(2,1)S(1)}, u32[]{:S(2)}, u32[]{:S(2)}) collective-permute-start(bf16[2,160,384]{2,1,0:T(8,128)(2,1)S(1)} %get-tuple-element.34), channel_id=1, source_target_pairs={{0,1},{1,0},{2,3},{3,2},{4,5},{5,4},{6,7},{7,6},{8,9},{9,8},{10,11... | collective-permute-start | bytes 737288 | tf_op jit(solution)/shard_map/ppermute | solution.py:31
  22.7 7.1 %collective-permute-start.10 = (bf16[160,384]{1,0:T(8,128)(2,1)S(1)}, bf16[160,384]{1,0:T(8,128)(2,1)S(1)}, u32[]{:S(2)}, u32[]{:S(2)}) collective-permute-start(bf16[160,384]{1,0:T(8,128)(2,1)S(1)} %get-tuple-element.38), channel_id=1, source_target_pairs={{0,6},{1,7},{2,4},{3,5},{4,2},{5,3},{6,0},{7,1},{8,14},{9,15},{10,... | collective-permute-start | bytes 368648 | tf_op jit(solution)/shard_map/ppermute | solution.py:31
  25.2 6.5 %collective-permute-start.9 = (bf16[160,384]{1,0:T(8,128)(2,1)S(1)}, bf16[160,384]{1,0:T(8,128)(2,1)S(1)}, u32[]{:S(2)}, u32[]{:S(2)}) collective-permute-start(bf16[160,384]{1,0:T(8,128)(2,1)S(1)} %get-tuple-element.37), channel_id=1, source_target_pairs={{0,4},{1,5},{2,6},{3,7},{4,0},{5,1},{6,2},{7,3},{8,12},{9,13},{10,... | collective-permute-start | bytes 368648 | tf_op jit(solution)/shard_map/ppermute | solution.py:31
  25.8 6.0 %collective-permute-start.11 = (bf16[160,384]{1,0:T(8,128)(2,1)S(1)}, bf16[160,384]{1,0:T(8,128)(2,1)S(1)}, u32[]{:S(2)}, u32[]{:S(2)}) collective-permute-start(bf16[160,384]{1,0:T(8,128)(2,1)S(1)} %get-tuple-element.39), channel_id=1, source_target_pairs={{0,2},{1,3},{2,0},{3,1},{4,6},{5,7},{6,4},{7,5},{8,10},{9,11},{10,... | collective-permute-start | bytes 368648 | tf_op jit(solution)/shard_map/ppermute | solution.py:31
  26.8 12.9 %collective-permute-start.12 = (bf16[48,1152]{1,0:T(8,128)(2,1)S(1)}, bf16[48,1152]{1,0:T(8,128)(2,1)S(1)}, u32[]{:S(2)}, u32[]{:S(2)}) collective-permute-start(bf16[48,1152]{1,0:T(8,128)(2,1)S(1)} %get-tuple-element.47), channel_id=1, source_target_pairs={{0,24},{1,25},{2,26},{3,27},{4,28},{5,29},{6,30},{7,31},{8,16},{9,... | collective-permute-start | bytes 331784 | tf_op jit(solution)/shard_map/ppermute | solution.py:31
  29.4 10.4 %collective-permute-start.13 = (bf16[48,1152]{1,0:T(8,128)(2,1)S(1)}, bf16[48,1152]{1,0:T(8,128)(2,1)S(1)}, u32[]{:S(2)}, u32[]{:S(2)}) collective-permute-start(bf16[48,1152]{1,0:T(8,128)(2,1)S(1)} %get-tuple-element.48), channel_id=1, source_target_pairs={{0,16},{1,17},{2,18},{3,19},{4,20},{5,21},{6,22},{7,23},{8,24},{9,... | collective-permute-start | bytes 331784 | tf_op jit(solution)/shard_map/ppermute | solution.py:31
  33.1 16.0 %all-to-all-start = ((bf16[8,176,128]{2,1,0:T(8,128)(2,1)}), bf16[8,176,128]{2,1,0:T(8,128)(2,1)S(1)}, u32[]{:S(2)}, u32[]{:S(2)}) async-start(bf16[8,176,128]{2,1,0:T(8,128)(2,1)} %get-tuple-element.50), calls=%async_computation | async-start | bytes 720896 | tf_op jit(solution)/shard_map/all_to_all | solution.py:407
  37.8 10.0 %collective-permute-start.14 = (bf16[48,1152]{1,0:T(8,128)(2,1)S(1)}, bf16[48,1152]{1,0:T(8,128)(2,1)S(1)}, u32[]{:S(2)}, u32[]{:S(2)}) collective-permute-start(bf16[48,1152]{1,0:T(8,128)(2,1)S(1)} %get-tuple-element.49), channel_id=1, source_target_pairs={{0,8},{1,9},{2,10},{3,11},{4,12},{5,13},{6,14},{7,15},{8,0},{9,1},... | collective-permute-start | bytes 331784 | tf_op jit(solution)/shard_map/ppermute | solution.py:31

commit v19 on v17

--- a/solution.py
+++ b/solution.py
@@ -335,6 +335,16 @@
     all_feats, inv_part, img_emb, grad_tile, own_part, near_part, far_part = results
     got_far = swapped(far_part, total, 1)
     got_near = swapped(near_part, total, 1)
+    feats_t, own_text, *sent_text = pl.pallas_call(
+        functools.partial(caption_kernel, rows),
+        in_specs=[VMEM] * 3,
+        out_specs=[VMEM] * (1 + spread),
+        out_shape=[jax.ShapeDtypeStruct((width, images), BF16), jax.ShapeDtypeStruct((rows, width), F32)]
+        + [jax.ShapeDtypeStruct((rows, width), BF16)] * (spread - 1),
+        compiler_params=limit(12 if spread <= 4 else 32),
+        name="captions",
+    )(grad_tile, img_emb, all_feats)
+    own_part, got_far, sent_text = lax.optimization_barrier((own_part, got_far, sent_text))
     sent_block = jax.ShapeDtypeStruct((share + STAT_ROWS, images), BF16)
     kept_block = jax.ShapeDtypeStruct((share + 8, images), F32)
     half = group // 4
@@ -347,15 +357,6 @@
         name="chip_far",
     )(own_part, got_far)
     far = [swapped(value, total, 2 * (half + index)) for index, value in enumerate(far)]
-    feats_t, own_text, *sent_text = pl.pallas_call(
-        functools.partial(caption_kernel, rows),
-        in_specs=[VMEM] * 3,
-        out_specs=[VMEM] * (1 + spread),
-        out_shape=[jax.ShapeDtypeStruct((width, images), BF16), jax.ShapeDtypeStruct((rows, width), F32)]
-        + [jax.ShapeDtypeStruct((rows, width), BF16)] * (spread - 1),
-        compiler_params=limit(12 if spread <= 4 else 32),
-        name="captions",
-    )(grad_tile, img_emb, all_feats)
     got_text = [swapped(value, total, step * group) for step, value in enumerate(sent_text, 1)]
     own_part, *near = pl.pallas_call(
         functools.partial(chip_kernel, 0),

time: 49.4 us -> 49.4 us (level)
  starting transfers between devices: 22.2 us -> 21.5 us
  waiting for transfers between devices: 14.2 us -> 14.8 us
    ppermute x15, starting transfers between devices: 17.5 us -> 16.9 us  [swapped(): lax.ppermute(value, AXES, [(source, source ^ mask) for source in range(to...]
    all_to_all x1, waiting for transfers between devices: 8.45 us -> 9.02 us  [local(): got_weight = lax.all_to_all(sent_weight, AXES[:2], 0, 0)]
where the time goes in v19:
time: 49.4 us; the launch traced here: 49.1 us
  starting transfers between devices  21.5 us (44%)
  waiting for transfers between devices  14.8 us (30%)
  Pallas kernels  7.66 us (16%)
  local copies, waits for them, and re-layouts  2.98 us (6%)
  between operations  2.07 us (4%)
    ppermute x15, starting transfers between devices, swapped(): lax.ppermute(value, AXES, [(source, source ^ mask) for source in range(to...  16.9 us
    all_to_all x1, waiting for transfers between devices, local(): got_weight = lax.all_to_all(sent_weight, AXES[:2], 0, 0)  9.02 us
    ppermute x15, waiting for transfers between devices, swapped(): lax.ppermute(value, AXES, [(source, source ^ mask) for source in range(to...  5.81 us
    all_to_all x1, starting transfers between devices, local(): got_weight = lax.all_to_all(sent_weight, AXES[:2], 0, 0)  4.65 us
    pallas_call x1, Pallas kernels, local(): pl.pallas_call(functools.partial(pair_kernel, narrow, group), in_specs=[S...  2.89 us
    unnamed x6, local copies, waits for them, and re-layouts  2.4 us
    pallas_call x1, Pallas kernels, local(): pl.pallas_call(functools.partial(weight_kernel, group, wide), in_specs=[V...  1.37 us
  transfers between devices with their start and end apart: 16, of which 6 were waited for; matrix products, arithmetic and copies ran while one was open for 1% of the time, Pallas kernels for 8%

profile of v19, /device:TPU:0, one launch (start us, length us, event | category | flops | bytes accessed | tf_op | source)
XLA Modules:
  0.0 49.1 jit_solution(6997547331322204679)
XLA Ops:
  0.6 3.0 %collective-permute-start = (bf16[48,1152]{1,0:T(8,128)(2,1)}, bf16[48,1152]{1,0:T(8,128)(2,1)S(1)}, u32[]{:S(2)}, u32[]{:S(2)}) collective-permute-start(bf16[48,1152]{1,0:T(8,128)(2,1)} %refs_0_.1), channel_id=1, source_target_pairs={{0,2},{1,3},{2,0},{3,1},{4,6},{5,7},{6,4},{7,5},{8,10},{9,11},{10,... | collective-permute-start | bytes 331784 | tf_op jit(solution)/shard_map/ppermute | solution.py:31
  3.7 1.5 %collective-permute-start.1 = (bf16[48,1152]{1,0:T(8,128)(2,1)}, bf16[48,1152]{1,0:T(8,128)(2,1)S(1)}, u32[]{:S(2)}, u32[]{:S(2)}) collective-permute-start(bf16[48,1152]{1,0:T(8,128)(2,1)} %refs_0_.1), channel_id=1, source_target_pairs={{0,4},{1,5},{2,6},{3,7},{4,0},{5,1},{6,2},{7,3},{8,12},{9,13},{10,... | collective-permute-start | bytes 331784 | tf_op jit(solution)/shard_map/ppermute | solution.py:31
  5.2 4.0 %collective-permute-start.3 = (bf16[48,1152]{1,0:T(8,128)(2,1)}, bf16[48,1152]{1,0:T(8,128)(2,1)S(1)}, u32[]{:S(2)}, u32[]{:S(2)}) collective-permute-start(bf16[48,1152]{1,0:T(8,128)(2,1)} %text_ref.1), channel_id=1, source_target_pairs={{0,24},{1,25},{2,26},{3,27},{4,28},{5,29},{6,30},{7,31},{8,16},{9,... | collective-permute-start | bytes 331784 | tf_op jit(solution)/shard_map/ppermute | solution.py:31
  10.6 0.6 %collective-permute-start.5 = (bf16[48,1152]{1,0:T(8,128)(2,1)}, bf16[48,1152]{1,0:T(8,128)(2,1)S(1)}, u32[]{:S(2)}, u32[]{:S(2)}) collective-permute-start(bf16[48,1152]{1,0:T(8,128)(2,1)} %text_ref.1), channel_id=1, source_target_pairs={{0,8},{1,9},{2,10},{3,11},{4,12},{5,13},{6,14},{7,15},{8,0},{9,1},... | collective-permute-start | bytes 331784 | tf_op jit(solution)/shard_map/ppermute | solution.py:31
  11.2 0.9 %copy-done.2 = bf16[48,1152]{1,0:T(8,128)(2,1)S(1)} copy-done((bf16[48,1152]{1,0:T(8,128)(2,1)S(1)}, bf16[48,1152]{1,0:T(8,128)(2,1)}, u32[]{:S(2)}) %copy-start.2) | copy-done | bytes 110616
  12.4 1.5 %copy-done = bf16[1152,1152]{1,0:T(8,128)(2,1)S(1)} copy-done((bf16[1152,1152]{1,0:T(8,128)(2,1)S(1)}, bf16[1152,1152]{1,0:T(8,128)(2,1)}, u32[]{:S(2)}) %copy-start) | copy-done | bytes 2654232
  13.9 0.8 %own_projection.1.own_proj = f32[192,1152]{1,0:T(8,128)S(1)} custom-call(bf16[192,1152]{1,0:T(8,128)(2,1)S(1)} %stack.1.feats_ref.own_half, bf16[1152,1152]{1,0:T(8,128)(2,1)S(1)} %copy-done), custom_call_target="tpu_custom_call" | custom-call | tf_op jit(solution)/shard_map/own_projection/pallas_call | solution.py:296
  14.7 3.3 %collective-permute-done.4.refs_2_ = bf16[48,1152]{1,0:T(8,128)(2,1)S(1)} collective-permute-done((bf16[48,1152]{1,0:T(8,128)(2,1)}, bf16[48,1152]{1,0:T(8,128)(2,1)S(1)}, u32[]{:S(2)}, u32[]{:S(2)}) %collective-permute-start.4) | collective-permute-done | bytes 110624 | tf_op jit(solution)/shard_map/ppermute | solution.py:31
  18.1 2.9 %pairs.1 = (bf16[384,1152]{1,0:T(8,128)(2,1)S(1)}, f32[1,384]{1,0:T(1,128)S(1)}, bf16[1152,384]{1,0:T(8,128)(2,1)S(1)}, bf16[192,384]{1,0:T(8,128)(2,1)S(1)}, f3...) custom-call(s32[1]{0:T(128)} %bitcast.member_ref, ...), custom_call_target="tpu_custom_call" | custom-call | tf_op jit(solution)/shard_map/pairs/pallas_call | solution.py:315
  21.1 0.5 %collective-permute-start.8 = (bf16[2,160,384]{2,1,0:T(8,128)(2,1)S(1)}, bf16[2,160,384]{2,1,0:T(8,128)(2,1)S(1)}, u32[]{:S(2)}, u32[]{:S(2)}) collective-permute-start(bf16[2,160,384]{2,1,0:T(8,128)(2,1)S(1)} %get-tuple-element.47), channel_id=1, source_target_pairs={{0,1},{1,0},{2,3},{3,2},{4,5},{5,4},{6,7},{7,6},{8,9},{9,8},{10,11... | collective-permute-start | bytes 737288 | tf_op jit(solution)/shard_map/ppermute | solution.py:31
  21.6 0.5 %captions.1 = (bf16[1152,384]{1,0:T(8,128)(2,1)S(1)}, f32[48,1152]{1,0:T(8,128)S(1)}, bf16[48,1152]{1,0:T(8,128)(2,1)S(1)}, bf16[48,1152]{1,0:T(8,128)(2,1)S(1)}, bf16[48,1152]{1,0:T(8,128)(2,1)S(1)}) custom-call(bf16[192,384]{1,0:T(8,128)(2,1)S(1)} %get-tuple-element.40.grad_ref, bf16[1152,384]{1,0:T(8,128)(2,1)S(1)} %get-tuple-element.41.emb_ref, ...), custom_call_target="tpu_custom_call" | custom-call | tf_op jit(solution)/shard_map/captions/pallas_call | solution.py:338
  22.7 2.5 %collective-permute-start.10 = (bf16[160,384]{1,0:T(8,128)(2,1)S(1)}, bf16[160,384]{1,0:T(8,128)(2,1)S(1)}, u32[]{:S(2)}, u32[]{:S(2)}) collective-permute-start(bf16[160,384]{1,0:T(8,128)(2,1)S(1)} %get-tuple-element.51), channel_id=1, source_target_pairs={{0,6},{1,7},{2,4},{3,5},{4,2},{5,3},{6,0},{7,1},{8,14},{9,15},{10,... | collective-permute-start | bytes 368648 | tf_op jit(solution)/shard_map/ppermute | solution.py:31
  25.2 0.5 %collective-permute-start.9 = (bf16[160,384]{1,0:T(8,128)(2,1)S(1)}, bf16[160,384]{1,0:T(8,128)(2,1)S(1)}, u32[]{:S(2)}, u32[]{:S(2)}) collective-permute-start(bf16[160,384]{1,0:T(8,128)(2,1)S(1)} %get-tuple-element.50), channel_id=1, source_target_pairs={{0,4},{1,5},{2,6},{3,7},{4,0},{5,1},{6,2},{7,3},{8,12},{9,13},{10,... | collective-permute-start | bytes 368648 | tf_op jit(solution)/shard_map/ppermute | solution.py:31
  25.8 0.6 %collective-permute-start.11 = (bf16[160,384]{1,0:T(8,128)(2,1)S(1)}, bf16[160,384]{1,0:T(8,128)(2,1)S(1)}, u32[]{:S(2)}, u32[]{:S(2)}) collective-permute-start(bf16[160,384]{1,0:T(8,128)(2,1)S(1)} %get-tuple-element.52), channel_id=1, source_target_pairs={{0,2},{1,3},{2,0},{3,1},{4,6},{5,7},{6,4},{7,5},{8,10},{9,11},{10,... | collective-permute-start | bytes 368648 | tf_op jit(solution)/shard_map/ppermute | solution.py:31
  26.3 2.4 %collective-permute-start.12 = (bf16[48,1152]{1,0:T(8,128)(2,1)S(1)}, bf16[48,1152]{1,0:T(8,128)(2,1)S(1)}, u32[]{:S(2)}, u32[]{:S(2)}) collective-permute-start(bf16[48,1152]{1,0:T(8,128)(2,1)S(1)} %get-tuple-element.57), channel_id=1, source_target_pairs={{0,24},{1,25},{2,26},{3,27},{4,28},{5,29},{6,30},{7,31},{8,16},{9,... | collective-permute-start | bytes 331784 | tf_op jit(solution)/shard_map/ppermute | solution.py:31
  28.8 1.0 %collective-permute-done.10.refs_2_ = bf16[160,384]{1,0:T(8,128)(2,1)S(1)} collective-permute-done((bf16[160,384]{1,0:T(8,128)(2,1)S(1)}, bf16[160,384]{1,0:T(8,128)(2,1)S(1)}, u32[]{:S(2)}, u32[]{:S(2)}) %collective-permute-start.10) | collective-permute-done | bytes 122912 | tf_op jit(solution)/shard_map/ppermute | solution.py:31
  29.8 1.0 %collective-permute-start.14 = (bf16[48,1152]{1,0:T(8,128)(2,1)S(1)}, bf16[48,1152]{1,0:T(8,128)(2,1)S(1)}, u32[]{:S(2)}, u32[]{:S(2)}) collective-permute-start(bf16[48,1152]{1,0:T(8,128)(2,1)S(1)} %get-tuple-element.59), channel_id=1, source_target_pairs={{0,8},{1,9},{2,10},{3,11},{4,12},{5,13},{6,14},{7,15},{8,0},{9,1},... | collective-permute-start | bytes 331784 | tf_op jit(solution)/shard_map/ppermute | solution.py:31
  30.7 0.9 %collective-permute-done.9.refs_1_ = bf16[160,384]{1,0:T(8,128)(2,1)S(1)} collective-permute-done((bf16[160,384]{1,0:T(8,128)(2,1)S(1)}, bf16[160,384]{1,0:T(8,128)(2,1)S(1)}, u32[]{:S(2)}, u32[]{:S(2)}) %collective-permute-start.9) | collective-permute-done | bytes 122912 | tf_op jit(solution)/shard_map/ppermute | solution.py:31
  31.7 1.4 %weights.1 = (f32[1,384]{1,0:T(1,128)S(1)}, bf16[8,176,128]{2,1,0:T(8,128)(2,1)}) custom-call(f32[152,384]{1,0:T(8,128)S(1)} %far_sum.1.refs_0_, bf16[160,384]{1,0:T(8,128)(2,1)S(1)} %collective-permute-done.11.refs_1_, f32[1,384]{1,0:T(1,128)S(1)} %get-tuple-element.53.refs_2_, bf16[384,1152]{1,0:T(8,128)(2,1)S(1)} %get-tuple-element.42.feats_ref.refs_3_, ...), custom_call_target="tpu_custom_call" | custom-call | tf_op jit(solution)/shard_map/weights/pallas_call | solution.py:385
  33.1 4.7 %all-to-all-start = ((bf16[8,176,128]{2,1,0:T(8,128)(2,1)}), bf16[8,176,128]{2,1,0:T(8,128)(2,1)S(1)}, u32[]{:S(2)}, u32[]{:S(2)}) async-start(bf16[8,176,128]{2,1,0:T(8,128)(2,1)} %get-tuple-element.60), calls=%async_computation | async-start | bytes 720896 | tf_op jit(solution)/shard_map/all_to_all | solution.py:396
  37.9 0.7 %caption_total.1 = f32[48,1152]{1,0:T(8,128)} custom-call(f32[48,1152]{1,0:T(8,128)S(1)} %get-tuple-element.56.refs_0_, bf16[48,1152]{1,0:T(8,128)(2,1)S(1)} %collective-permute-done.12.refs_1_, bf16[48,1152]{1,0:T(8,128)(2,1)S(1)} %collective-permute-done.13.refs_2_, bf16[48,1152]{1,0:T(8,128)(2,1)S(1)} %collective-permute-done.14.refs_3_), custom_call_target="tpu_custom_call" | custom-call | flops 5000000000 | tf_op jit(solution)/shard_map/caption_total/pallas_call | solution.py:427
  38.6 0.6 %dynamic-slice_bitcast_fusion = f32[48]{0:T(128)} fusion(f32[1,384]{1,0:T(1,128)S(1)} %get-tuple-element.55, s32[]{:T(128)S(6)} %select_n.16), kind=kLoop, calls=%fused_computation | loop fusion | bytes 388 | tf_op jit(solution)/shard_map/dynamic_slice | solution.py:436
  39.2 9.0 %all-to-all-done.got_ref = bf16[8,176,128]{2,1,0:T(8,128)(2,1)S(1)} async-done(((bf16[8,176,128]{2,1,0:T(8,128)(2,1)}), bf16[8,176,128]{2,1,0:T(8,128)(2,1)S(1)}, u32[]{:S(2)}, u32[]{:S(2)}) %all-to-all-start) | async-done | bytes 360480 | tf_op jit(solution)/shard_map/all_to_all | solution.py:396
  48.2 0.9 %weight_total.1 = f32[144,288]{1,0:T(8,128)} custom-call(bf16[8,176,128]{2,1,0:T(8,128)(2,1)S(1)} %all-to-all-done.got_ref), custom_call_target="tpu_custom_call" | custom-call | tf_op jit(solution)/shard_map/weight_total/pallas_call | solution.py:397
  (27 shorter events, 1.3 us)
Async XLA Ops:
  0.6 9.9 %collective-permute-start = (bf16[48,1152]{1,0:T(8,128)(2,1)}, bf16[48,1152]{1,0:T(8,128)(2,1)S(1)}, u32[]{:S(2)}, u32[]{:S(2)}) collective-permute-start(bf16[48,1152]{1,0:T(8,128)(2,1)} %refs_0_.1), channel_id=1, source_target_pairs={{0,2},{1,3},{2,0},{3,1},{4,6},{5,7},{6,4},{7,5},{8,10},{9,11},{10,... | collective-permute-start | bytes 331784 | tf_op jit(solution)/shard_map/ppermute | solution.py:31
  3.7 8.6 %collective-permute-start.1 = (bf16[48,1152]{1,0:T(8,128)(2,1)}, bf16[48,1152]{1,0:T(8,128)(2,1)S(1)}, u32[]{:S(2)}, u32[]{:S(2)}) collective-permute-start(bf16[48,1152]{1,0:T(8,128)(2,1)} %refs_0_.1), channel_id=1, source_target_pairs={{0,4},{1,5},{2,6},{3,7},{4,0},{5,1},{6,2},{7,3},{8,12},{9,13},{10,... | collective-permute-start | bytes 331784 | tf_op jit(solution)/shard_map/ppermute | solution.py:31
  5.2 7.1 %collective-permute-start.2 = (bf16[48,1152]{1,0:T(8,128)(2,1)}, bf16[48,1152]{1,0:T(8,128)(2,1)S(1)}, u32[]{:S(2)}, u32[]{:S(2)}) collective-permute-start(bf16[48,1152]{1,0:T(8,128)(2,1)} %refs_0_.1), channel_id=1, source_target_pairs={{0,6},{1,7},{2,4},{3,5},{4,2},{5,3},{6,0},{7,1},{8,14},{9,15},{10,... | collective-permute-start | bytes 331784 | tf_op jit(solution)/shard_map/ppermute | solution.py:31
  5.2 9.5 %collective-permute-start.3 = (bf16[48,1152]{1,0:T(8,128)(2,1)}, bf16[48,1152]{1,0:T(8,128)(2,1)S(1)}, u32[]{:S(2)}, u32[]{:S(2)}) collective-permute-start(bf16[48,1152]{1,0:T(8,128)(2,1)} %text_ref.1), channel_id=1, source_target_pairs={{0,24},{1,25},{2,26},{3,27},{4,28},{5,29},{6,30},{7,31},{8,16},{9,... | collective-permute-start | bytes 331784 | tf_op jit(solution)/shard_map/ppermute | solution.py:31
  9.2 8.7 %collective-permute-start.4 = (bf16[48,1152]{1,0:T(8,128)(2,1)}, bf16[48,1152]{1,0:T(8,128)(2,1)S(1)}, u32[]{:S(2)}, u32[]{:S(2)}) collective-permute-start(bf16[48,1152]{1,0:T(8,128)(2,1)} %text_ref.1), channel_id=1, source_target_pairs={{0,16},{1,17},{2,18},{3,19},{4,20},{5,21},{6,22},{7,23},{8,24},{9,... | collective-permute-start | bytes 331784 | tf_op jit(solution)/shard_map/ppermute | solution.py:31
  10.5 1.7 %copy-start.1 = (bf16[48,1152]{1,0:T(8,128)(2,1)S(1)}, bf16[48,1152]{1,0:T(8,128)(2,1)}, u32[]{:S(2)}) copy-start(bf16[48,1152]{1,0:T(8,128)(2,1)} %refs_0_.1) | copy-start | bytes 331780
  10.6 7.4 %collective-permute-start.5 = (bf16[48,1152]{1,0:T(8,128)(2,1)}, bf16[48,1152]{1,0:T(8,128)(2,1)S(1)}, u32[]{:S(2)}, u32[]{:S(2)}) collective-permute-start(bf16[48,1152]{1,0:T(8,128)(2,1)} %text_ref.1), channel_id=1, source_target_pairs={{0,8},{1,9},{2,10},{3,11},{4,12},{5,13},{6,14},{7,15},{8,0},{9,1},... | collective-permute-start | bytes 331784 | tf_op jit(solution)/shard_map/ppermute | solution.py:31
  11.2 0.9 %copy-start.2 = (bf16[48,1152]{1,0:T(8,128)(2,1)S(1)}, bf16[48,1152]{1,0:T(8,128)(2,1)}, u32[]{:S(2)}) copy-start(bf16[48,1152]{1,0:T(8,128)(2,1)} %text_ref.1) | copy-start | bytes 331780
  12.1 1.7 %copy-start = (bf16[1152,1152]{1,0:T(8,128)(2,1)S(1)}, bf16[1152,1152]{1,0:T(8,128)(2,1)}, u32[]{:S(2)}) copy-start(bf16[1152,1152]{1,0:T(8,128)(2,1)} %weight.1) | copy-start | bytes 7962628
  12.3 5.8 %collective-permute-start.6 = (bf16[192,1152]{1,0:T(8,128)(2,1)S(1)}, bf16[192,1152]{1,0:T(8,128)(2,1)S(1)}, u32[]{:S(2)}, u32[]{:S(2)}) collective-permute-start(bf16[192,1152]{1,0:T(8,128)(2,1)S(1)} %stack.1.feats_ref.own_half), channel_id=1, source_target_pairs={{0,1},{1,0},{2,3},{3,2},{4,5},{5,4},{6,7},{7,6},{8,9},{9,8},{10,11... | collective-permute-start | bytes 1327112 | tf_op jit(solution)/shard_map/ppermute | solution.py:31
  21.0 1.6 %collective-permute-start.7 = (bf16[2,160,384]{2,1,0:T(8,128)(2,1)S(1)}, bf16[2,160,384]{2,1,0:T(8,128)(2,1)S(1)}, u32[]{:S(2)}, u32[]{:S(2)}) collective-permute-start(bf16[2,160,384]{2,1,0:T(8,128)(2,1)S(1)} %get-tuple-element.39), channel_id=1, source_target_pairs={{0,1},{1,0},{2,3},{3,2},{4,5},{5,4},{6,7},{7,6},{8,9},{9,8},{10,11... | collective-permute-start | bytes 737288 | tf_op jit(solution)/shard_map/ppermute | solution.py:31
  21.1 4.6 %collective-permute-start.8 = (bf16[2,160,384]{2,1,0:T(8,128)(2,1)S(1)}, bf16[2,160,384]{2,1,0:T(8,128)(2,1)S(1)}, u32[]{:S(2)}, u32[]{:S(2)}) collective-permute-start(bf16[2,160,384]{2,1,0:T(8,128)(2,1)S(1)} %get-tuple-element.47), channel_id=1, source_target_pairs={{0,1},{1,0},{2,3},{3,2},{4,5},{5,4},{6,7},{7,6},{8,9},{9,8},{10,11... | collective-permute-start | bytes 737288 | tf_op jit(solution)/shard_map/ppermute | solution.py:31
  22.7 7.1 %collective-permute-start.10 = (bf16[160,384]{1,0:T(8,128)(2,1)S(1)}, bf16[160,384]{1,0:T(8,128)(2,1)S(1)}, u32[]{:S(2)}, u32[]{:S(2)}) collective-permute-start(bf16[160,384]{1,0:T(8,128)(2,1)S(1)} %get-tuple-element.51), channel_id=1, source_target_pairs={{0,6},{1,7},{2,4},{3,5},{4,2},{5,3},{6,0},{7,1},{8,14},{9,15},{10,... | collective-permute-start | bytes 368648 | tf_op jit(solution)/shard_map/ppermute | solution.py:31
  25.2 6.5 %collective-permute-start.9 = (bf16[160,384]{1,0:T(8,128)(2,1)S(1)}, bf16[160,384]{1,0:T(8,128)(2,1)S(1)}, u32[]{:S(2)}, u32[]{:S(2)}) collective-permute-start(bf16[160,384]{1,0:T(8,128)(2,1)S(1)} %get-tuple-element.50), channel_id=1, source_target_pairs={{0,4},{1,5},{2,6},{3,7},{4,0},{5,1},{6,2},{7,3},{8,12},{9,13},{10,... | collective-permute-start | bytes 368648 | tf_op jit(solution)/shard_map/ppermute | solution.py:31
  25.8 6.0 %collective-permute-start.11 = (bf16[160,384]{1,0:T(8,128)(2,1)S(1)}, bf16[160,384]{1,0:T(8,128)(2,1)S(1)}, u32[]{:S(2)}, u32[]{:S(2)}) collective-permute-start(bf16[160,384]{1,0:T(8,128)(2,1)S(1)} %get-tuple-element.52), channel_id=1, source_target_pairs={{0,2},{1,3},{2,0},{3,1},{4,6},{5,7},{6,4},{7,5},{8,10},{9,11},{10,... | collective-permute-start | bytes 368648 | tf_op jit(solution)/shard_map/ppermute | solution.py:31
  26.3 11.4 %collective-permute-start.12 = (bf16[48,1152]{1,0:T(8,128)(2,1)S(1)}, bf16[48,1152]{1,0:T(8,128)(2,1)S(1)}, u32[]{:S(2)}, u32[]{:S(2)}) collective-permute-start(bf16[48,1152]{1,0:T(8,128)(2,1)S(1)} %get-tuple-element.57), channel_id=1, source_target_pairs={{0,24},{1,25},{2,26},{3,27},{4,28},{5,29},{6,30},{7,31},{8,16},{9,... | collective-permute-start | bytes 331784 | tf_op jit(solution)/shard_map/ppermute | solution.py:31
  28.8 9.1 %collective-permute-start.13 = (bf16[48,1152]{1,0:T(8,128)(2,1)S(1)}, bf16[48,1152]{1,0:T(8,128)(2,1)S(1)}, u32[]{:S(2)}, u32[]{:S(2)}) collective-permute-start(bf16[48,1152]{1,0:T(8,128)(2,1)S(1)} %get-tuple-element.58), channel_id=1, source_target_pairs={{0,16},{1,17},{2,18},{3,19},{4,20},{5,21},{6,22},{7,23},{8,24},{9,... | collective-permute-start | bytes 331784 | tf_op jit(solution)/shard_map/ppermute | solution.py:31
  29.8 8.1 %collective-permute-start.14 = (bf16[48,1152]{1,0:T(8,128)(2,1)S(1)}, bf16[48,1152]{1,0:T(8,128)(2,1)S(1)}, u32[]{:S(2)}, u32[]{:S(2)}) collective-permute-start(bf16[48,1152]{1,0:T(8,128)(2,1)S(1)} %get-tuple-element.59), channel_id=1, source_target_pairs={{0,8},{1,9},{2,10},{3,11},{4,12},{5,13},{6,14},{7,15},{8,0},{9,1},... | collective-permute-start | bytes 331784 | tf_op jit(solution)/shard_map/ppermute | solution.py:31
  33.1 15.1 %all-to-all-start = ((bf16[8,176,128]{2,1,0:T(8,128)(2,1)}), bf16[8,176,128]{2,1,0:T(8,128)(2,1)S(1)}, u32[]{:S(2)}, u32[]{:S(2)}) async-start(bf16[8,176,128]{2,1,0:T(8,128)(2,1)} %get-tuple-element.60), calls=%async_computation | async-start | bytes 720896 | tf_op jit(solution)/shard_map/all_to_all | solution.py:396

commit v20 on v19

--- a/solution.py
+++ b/solution.py
@@ -178,20 +178,22 @@
         own_out[index, :share, :] = projected(2 * index)
         target = (near_out, far_out)[index * 4 // group].at[index % (group // 4)]
         target[:share, :] = projected(2 * index + 1).astype(BF16)
-        target[share:, :] = losses
+    near_out[0, share:, :] = losses
     own_out[0, share : share + 1, :] = loss_sum
 
 
 def chip_kernel(first, own_ref, got_ref, *outs):
     share = own_ref.shape[1] - 8
-    loss = own_ref[0, share : share + 1, :] + loss_of(got_ref[0, share:, :])
     for index, target in enumerate(outs):
         total = own_ref[first + index, :share, :] + got_ref[index, :share, :].astype(F32)
-        target[:share, :] = total.astype(target.dtype)
-        if target.dtype == BF16:
-            target[share:, :] = loss_rows(loss)
-        else:
-            target[share : share + 1, :] = loss
+        target[...] = total.astype(target.dtype)
+
+
+def near_kernel(own_ref, got_ref, loss_out, *outs):
+    chip_kernel(0, own_ref, got_ref, *outs)
+    share = own_ref.shape[1] - 8
+    loss = own_ref[0, share : share + 1, :] + loss_of(got_ref[0, share:, :])
+    loss_out[...] = jnp.broadcast_to(loss, loss_out.shape)
 
 
 def caption_kernel(rows, grad_ref, emb_ref, feats_ref, feats_t, *outs):
@@ -203,33 +205,18 @@
         feats_t[:, cols] = feats_ref[cols, :].astype(F32).T.astype(BF16)
 
 
-def far_sum_kernel(*refs):
-    own_ref, got, out = refs[0], refs[1:-1], refs[-1]
-    share = own_ref.shape[0] - 8
-    total, loss = own_ref[:share, :], own_ref[share : share + 1, :]
+def gathered_gradient(own_ref, got, inv_ref):
+    total = own_ref[...]
     for block in got:
-        total = total + block[:share, :].astype(F32)
-        loss = loss + loss_of(block[share:, :])
-    out[:share, :] = total
-    out[share : share + 1, :] = loss
-
-
-def gathered_gradient(own_ref, got, inv_ref, loss_out):
-    share = own_ref.shape[0] - 8
-    total = own_ref[:share, :]
-    loss = own_ref[share : share + 1, :]
-    for block in got:
-        total = total + block[:share, :].astype(F32)
-        loss = loss + loss_of(block[share:, :])
-    loss_out[...] = loss
+        total = total + block[...].astype(F32)
     return inv_ref[...] * total
 
 
 def weight_kernel(group, wide, *refs):
     own_ref, got = refs[0], refs[1 : group // 4]
-    inv_ref, feats_ref, feats_t_ref, loss_out, send_out = refs[group // 4 :]
+    inv_ref, feats_ref, feats_t_ref, send_out = refs[group // 4 :]
     rows = feats_t_ref.shape[0] // wide
-    high, low = split_pair(gathered_gradient(own_ref, got, inv_ref, loss_out))
+    high, low = split_pair(gathered_gradient(own_ref, got, inv_ref))
     rest = high.shape[0] - LANES
     both = jnp.concatenate([high[LANES:, :], low[LANES:, :]], axis=0)
     tail = jnp.dot(both, feats_ref[...], preferred_element_type=F32)
@@ -323,7 +310,7 @@
             jax.ShapeDtypeStruct((spread * rows, images), BF16),
             jax.ShapeDtypeStruct((group // 2, share + 8, images), F32),
         ]
-        + [jax.ShapeDtypeStruct((group // 4, share + STAT_ROWS, images), BF16)] * 2,
+        + [jax.ShapeDtypeStruct((group // 4, share + extra, images), BF16) for extra in (STAT_ROWS, 0)],
         scratch_shapes=[
             pltpu.VMEM((width, images), F32),
             pltpu.VMEM((width, images), F32),
@@ -345,8 +332,9 @@
         name="captions",
     )(grad_tile, img_emb, all_feats)
     own_part, got_far, sent_text = lax.optimization_barrier((own_part, got_far, sent_text))
-    sent_block = jax.ShapeDtypeStruct((share + STAT_ROWS, images), BF16)
-    kept_block = jax.ShapeDtypeStruct((share + 8, images), F32)
+    sent_block = jax.ShapeDtypeStruct((share, images), BF16)
+    kept_block = jax.ShapeDtypeStruct((share, images), F32)
+    loss_block = jax.ShapeDtypeStruct((8, images), F32)
     half = group // 4
     far = pl.pallas_call(
         functools.partial(chip_kernel, half),
@@ -358,17 +346,17 @@
     )(own_part, got_far)
     far = [swapped(value, total, 2 * (half + index)) for index, value in enumerate(far)]
     got_text = [swapped(value, total, step * group) for step, value in enumerate(sent_text, 1)]
-    own_part, *near = pl.pallas_call(
-        functools.partial(chip_kernel, 0),
+    loss, own_part, *near = pl.pallas_call(
+        near_kernel,
         in_specs=[VMEM] * 2,
-        out_specs=[VMEM] * half,
-        out_shape=[kept_block] + [sent_block] * (half - 1),
+        out_specs=[VMEM] * (1 + half),
+        out_shape=[loss_block, kept_block] + [sent_block] * (half - 1),
         compiler_params=limit(8),
         name="chip_near",
     )(own_part, got_near)
     near = [swapped(value, total, 2 * index) for index, value in enumerate(near, 1)]
     own_part = pl.pallas_call(
-        far_sum_kernel,
+        sum_kernel,
         in_specs=[VMEM] * (1 + half),
         out_specs=VMEM,
         out_shape=kept_block,
@@ -382,14 +370,11 @@
     packed = out_rows + 2 * rest
     direct = LANES < out_rows <= 2 * LANES and out_rows % 16 == 0 and rest % 16 == 0
     if direct:
-        loss_line, sent_weight = pl.pallas_call(
+        sent_weight = pl.pallas_call(
             functools.partial(weight_kernel, group, wide),
             in_specs=[VMEM] * (3 + group // 4),
-            out_specs=[VMEM] * 2,
-            out_shape=[
-                jax.ShapeDtypeStruct((1, images), F32),
-                jax.ShapeDtypeStruct((wide, packed, LANES), BF16),
-            ],
+            out_specs=VMEM,
+            out_shape=jax.ShapeDtypeStruct((wide, packed, LANES), BF16),
             compiler_params=limit(12),
             name="weights",
         )(own_part, *near, inv_part, all_feats, feats_t)
@@ -406,14 +391,14 @@
 
         def gradient_kernel(*refs):
             own_ref, blocks = refs[0], refs[1 : group // 4]
-            inv_ref, loss_out, d_out = refs[group // 4 :]
-            d_out[...] = gathered_gradient(own_ref, blocks, inv_ref, loss_out)
-
-        loss_line, d_zproj = pl.pallas_call(
+            inv_ref, d_out = refs[group // 4 :]
+            d_out[...] = gathered_gradient(own_ref, blocks, inv_ref)
+
+        d_zproj = pl.pallas_call(
             gradient_kernel,
             in_specs=[VMEM] * (1 + group // 4),
-            out_specs=[VMEM] * 2,
-            out_shape=[jax.ShapeDtypeStruct((1, images), F32), jax.ShapeDtypeStruct((share, images), F32)],
+            out_specs=VMEM,
+            out_shape=kept_block,
             compiler_params=limit(12),
             name="gradient",
         )(own_part, *near, inv_part)
@@ -432,8 +417,18 @@
         compiler_params=limit(12),
         cost_estimate=hint(5 * 10**9),
         name="caption_total",
-    )(own_text, *got_text[::-1])
-    image_loss = lax.dynamic_slice_in_dim(loss_line[0], first_image(member[0], rows, group), rows, 0)
+    )(own_text, *got_text)
+    loss, d_text_unit = lax.optimization_barrier((loss, d_text_unit))
+    losses = [swapped(loss, total, 2 * step) for step in range(1, group // 2)]
+    loss = pl.pallas_call(
+        sum_kernel,
+        in_specs=[VMEM] * (group // 2),
+        out_specs=VMEM,
+        out_shape=loss_block,
+        compiler_params=limit(4),
+        name="loss_sum",
+    )(loss, *losses)
+    image_loss = lax.dynamic_slice_in_dim(loss[0], first_image(member[0], rows, group), rows, 0)
     return (image_loss, d_text_unit, d_proj)
 
 

time: 49.4 us -> 50.4 us (1.020)
  starting transfers between devices: 21.5 us -> 25.1 us
  waiting for transfers between devices: 14.8 us -> 12.2 us
    all_to_all x1, waiting for transfers between devices: 9.02 us -> 1.97 us  [local(): got_weight = lax.all_to_all(sent_weight, AXES[:2], 0, 0)]
    ppermute x15 -> x18, waiting for transfers between devices: 5.81 us -> 10.3 us  [swapped(): lax.ppermute(value, AXES, [(source, source ^ mask) for source in range(to...]
    ppermute x15 -> x18, starting transfers between devices: 16.9 us -> 20.5 us  [swapped(): lax.ppermute(value, AXES, [(source, source ^ mask) for source in range(to...]
  transfers between devices with their start and end apart: 16 -> 19, of which waited for: 6 -> 8; matrix products, arithmetic and copies ran while one was open for 1% -> 1% of each run, Pallas kernels for 8% -> 8%
where the time goes in v20:
time: 50.4 us; the launch traced here: 50.1 us
  starting transfers between devices  25.1 us (50%)
  waiting for transfers between devices  12.2 us (24%)
  Pallas kernels  7.63 us (15%)
  local copies, waits for them, and re-layouts  2.99 us (6%)
  between operations  2.09 us (4%)
    ppermute x18, starting transfers between devices, swapped(): lax.ppermute(value, AXES, [(source, source ^ mask) for source in range(to...  20.5 us
    ppermute x18, waiting for transfers between devices, swapped(): lax.ppermute(value, AXES, [(source, source ^ mask) for source in range(to...  10.3 us
    all_to_all x1, starting transfers between devices, local(): got_weight = lax.all_to_all(sent_weight, AXES[:2], 0, 0)  4.65 us
    pallas_call x1, Pallas kernels, local(): pl.pallas_call(functools.partial(pair_kernel, narrow, group), in_specs=[S...  2.89 us
    unnamed x6, local copies, waits for them, and re-layouts  2.4 us
    all_to_all x1, waiting for transfers between devices, local(): got_weight = lax.all_to_all(sent_weight, AXES[:2], 0, 0)  1.97 us
    pallas_call x1, Pallas kernels, local(): pl.pallas_call(functools.partial(weight_kernel, group, wide), in_specs=[V...  1.36 us
  transfers between devices with their start and end apart: 19, of which 8 were waited for; matrix products, arithmetic and copies ran while one was open for 1% of the time, Pallas kernels for 8%

profile of v20, /device:TPU:0, one launch (start us, length us, event | category | flops | bytes accessed | tf_op | source)
XLA Modules:
  0.0 50.1 jit_solution(11436246907968924868)
XLA Ops:
  0.6 3.0 %collective-permute-start = (bf16[48,1152]{1,0:T(8,128)(2,1)}, bf16[48,1152]{1,0:T(8,128)(2,1)S(1)}, u32[]{:S(2)}, u32[]{:S(2)}) collective-permute-start(bf16[48,1152]{1,0:T(8,128)(2,1)} %refs_0_.1), channel_id=1, source_target_pairs={{0,2},{1,3},{2,0},{3,1},{4,6},{5,7},{6,4},{7,5},{8,10},{9,11},{10,... | collective-permute-start | bytes 331784 | tf_op jit(solution)/shard_map/ppermute | solution.py:31
  3.7 1.5 %collective-permute-start.1 = (bf16[48,1152]{1,0:T(8,128)(2,1)}, bf16[48,1152]{1,0:T(8,128)(2,1)S(1)}, u32[]{:S(2)}, u32[]{:S(2)}) collective-permute-start(bf16[48,1152]{1,0:T(8,128)(2,1)} %refs_0_.1), channel_id=1, source_target_pairs={{0,4},{1,5},{2,6},{3,7},{4,0},{5,1},{6,2},{7,3},{8,12},{9,13},{10,... | collective-permute-start | bytes 331784 | tf_op jit(solution)/shard_map/ppermute | solution.py:31
  5.2 4.0 %collective-permute-start.3 = (bf16[48,1152]{1,0:T(8,128)(2,1)}, bf16[48,1152]{1,0:T(8,128)(2,1)S(1)}, u32[]{:S(2)}, u32[]{:S(2)}) collective-permute-start(bf16[48,1152]{1,0:T(8,128)(2,1)} %text_ref.1), channel_id=1, source_target_pairs={{0,24},{1,25},{2,26},{3,27},{4,28},{5,29},{6,30},{7,31},{8,16},{9,... | collective-permute-start | bytes 331784 | tf_op jit(solution)/shard_map/ppermute | solution.py:31
  10.6 0.6 %collective-permute-start.5 = (bf16[48,1152]{1,0:T(8,128)(2,1)}, bf16[48,1152]{1,0:T(8,128)(2,1)S(1)}, u32[]{:S(2)}, u32[]{:S(2)}) collective-permute-start(bf16[48,1152]{1,0:T(8,128)(2,1)} %text_ref.1), channel_id=1, source_target_pairs={{0,8},{1,9},{2,10},{3,11},{4,12},{5,13},{6,14},{7,15},{8,0},{9,1},... | collective-permute-start | bytes 331784 | tf_op jit(solution)/shard_map/ppermute | solution.py:31
  11.2 0.9 %copy-done.2 = bf16[48,1152]{1,0:T(8,128)(2,1)S(1)} copy-done((bf16[48,1152]{1,0:T(8,128)(2,1)S(1)}, bf16[48,1152]{1,0:T(8,128)(2,1)}, u32[]{:S(2)}) %copy-start.2) | copy-done | bytes 110616
  12.4 1.5 %copy-done = bf16[1152,1152]{1,0:T(8,128)(2,1)S(1)} copy-done((bf16[1152,1152]{1,0:T(8,128)(2,1)S(1)}, bf16[1152,1152]{1,0:T(8,128)(2,1)}, u32[]{:S(2)}) %copy-start) | copy-done | bytes 2654232
  13.9 0.8 %own_projection.1.own_proj = f32[192,1152]{1,0:T(8,128)S(1)} custom-call(bf16[192,1152]{1,0:T(8,128)(2,1)S(1)} %stack.1.feats_ref.own_half, bf16[1152,1152]{1,0:T(8,128)(2,1)S(1)} %copy-done), custom_call_target="tpu_custom_call" | custom-call | tf_op jit(solution)/shard_map/own_projection/pallas_call | solution.py:283
  14.7 3.3 %collective-permute-done.4.refs_2_ = bf16[48,1152]{1,0:T(8,128)(2,1)S(1)} collective-permute-done((bf16[48,1152]{1,0:T(8,128)(2,1)}, bf16[48,1152]{1,0:T(8,128)(2,1)S(1)}, u32[]{:S(2)}, u32[]{:S(2)}) %collective-permute-start.4) | collective-permute-done | bytes 110624 | tf_op jit(solution)/shard_map/ppermute | solution.py:31
  18.1 2.9 %pairs.1 = (bf16[384,1152]{1,0:T(8,128)(2,1)S(1)}, f32[1,384]{1,0:T(1,128)S(1)}, bf16[1152,384]{1,0:T(8,128)(2,1)S(1)}, bf16[192,384]{1,0:T(8,128)(2,1)S(1)}, f3...) custom-call(s32[1]{0:T(128)} %bitcast.member_ref, ...), custom_call_target="tpu_custom_call" | custom-call | tf_op jit(solution)/shard_map/pairs/pallas_call | solution.py:302
  22.6 1.6 %collective-permute-start.15 = (bf16[144,384]{1,0:T(8,128)(2,1)S(1)}, bf16[144,384]{1,0:T(8,128)(2,1)S(1)}, u32[]{:S(2)}, u32[]{:S(2)}) collective-permute-start(bf16[144,384]{1,0:T(8,128)(2,1)S(1)} %get-tuple-element.58), channel_id=1, source_target_pairs={{0,4},{1,5},{2,6},{3,7},{4,0},{5,1},{6,2},{7,3},{8,12},{9,13},{10,... | collective-permute-start | bytes 331784 | tf_op jit(solution)/shard_map/ppermute | solution.py:31
  24.2 1.5 %collective-permute-start.16 = (bf16[144,384]{1,0:T(8,128)(2,1)S(1)}, bf16[144,384]{1,0:T(8,128)(2,1)S(1)}, u32[]{:S(2)}, u32[]{:S(2)}) collective-permute-start(bf16[144,384]{1,0:T(8,128)(2,1)S(1)} %get-tuple-element.59), channel_id=1, source_target_pairs={{0,6},{1,7},{2,4},{3,5},{4,2},{5,3},{6,0},{7,1},{8,14},{9,15},{10,... | collective-permute-start | bytes 331784 | tf_op jit(solution)/shard_map/ppermute | solution.py:31
  26.8 2.0 %collective-permute-start.11 = (bf16[48,1152]{1,0:T(8,128)(2,1)S(1)}, bf16[48,1152]{1,0:T(8,128)(2,1)S(1)}, u32[]{:S(2)}, u32[]{:S(2)}) collective-permute-start(bf16[48,1152]{1,0:T(8,128)(2,1)S(1)} %get-tuple-element.53), channel_id=1, source_target_pairs={{0,24},{1,25},{2,26},{3,27},{4,28},{5,29},{6,30},{7,31},{8,16},{9,... | collective-permute-start | bytes 331784 | tf_op jit(solution)/shard_map/ppermute | solution.py:31
  28.9 0.9 %collective-permute-start.9 = (bf16[48,1152]{1,0:T(8,128)(2,1)S(1)}, bf16[48,1152]{1,0:T(8,128)(2,1)S(1)}, u32[]{:S(2)}, u32[]{:S(2)}) collective-permute-start(bf16[48,1152]{1,0:T(8,128)(2,1)S(1)} %get-tuple-element.51), channel_id=1, source_target_pairs={{0,8},{1,9},{2,10},{3,11},{4,12},{5,13},{6,14},{7,15},{8,0},{9,1},... | collective-permute-start | bytes 331784 | tf_op jit(solution)/shard_map/ppermute | solution.py:31
  29.8 1.4 %collective-permute-done.16.refs_2_ = bf16[144,384]{1,0:T(8,128)(2,1)S(1)} collective-permute-done((bf16[144,384]{1,0:T(8,128)(2,1)S(1)}, bf16[144,384]{1,0:T(8,128)(2,1)S(1)}, u32[]{:S(2)}, u32[]{:S(2)}) %collective-permute-start.16) | collective-permute-done | bytes 110624 | tf_op jit(solution)/shard_map/ppermute | solution.py:31
  31.2 1.4 %collective-permute-done.17.refs_1_ = bf16[144,384]{1,0:T(8,128)(2,1)S(1)} collective-permute-done((bf16[144,384]{1,0:T(8,128)(2,1)S(1)}, bf16[144,384]{1,0:T(8,128)(2,1)S(1)}, u32[]{:S(2)}, u32[]{:S(2)}) %collective-permute-start.17) | collective-permute-done | bytes 110624 | tf_op jit(solution)/shard_map/ppermute | solution.py:31
  32.7 1.4 %weights.1 = bf16[8,176,128]{2,1,0:T(8,128)(2,1)} custom-call(f32[144,384]{1,0:T(8,128)S(1)} %far_sum.1.refs_0_, bf16[144,384]{1,0:T(8,128)(2,1)S(1)} %collective-permute-done.17.refs_1_, f32[1,384]{1,0:T(1,128)S(1)} %get-tuple-element.61.refs_2_, bf16[384,1152]{1,0:T(8,128)(2,1)S(1)} %get-tuple-element.43.feats_ref.refs_3_, ...), custom_call_target="tpu_custom_call" | custom-call | tf_op jit(solution)/shard_map/weights/pallas_call | solution.py:373
  34.0 4.7 %all-to-all-start = ((bf16[8,176,128]{2,1,0:T(8,128)(2,1)}), bf16[8,176,128]{2,1,0:T(8,128)(2,1)S(1)}, u32[]{:S(2)}, u32[]{:S(2)}) async-start(bf16[8,176,128]{2,1,0:T(8,128)(2,1)} %weights.1), calls=%async_computation | async-start | bytes 720896 | tf_op jit(solution)/shard_map/all_to_all | solution.py:381
  38.7 0.8 %caption_total.1 = f32[48,1152]{1,0:T(8,128)} custom-call(f32[48,1152]{1,0:T(8,128)S(1)} %get-tuple-element.50.refs_0_, bf16[48,1152]{1,0:T(8,128)(2,1)S(1)} %collective-permute-done.9.refs_1_, bf16[48,1152]{1,0:T(8,128)(2,1)S(1)} %collective-permute-done.10.refs_2_, bf16[48,1152]{1,0:T(8,128)(2,1)S(1)} %collective-permute-done.11.refs_3_), custom_call_target="tpu_custom_call" | custom-call | flops 5000000000 | tf_op jit(solution)/shard_map/caption_total/pallas_call | solution.py:412
  40.0 2.0 %collective-permute-start.13 = (f32[8,384]{1,0:T(8,128)S(1)}, f32[8,384]{1,0:T(8,128)S(1)}, u32[]{:S(2)}, u32[]{:S(2)}) collective-permute-start(f32[8,384]{1,0:T(8,128)S(1)} %get-tuple-element.54.refs_0_), channel_id=1, source_target_pairs={{0,4},{1,5},{2,6},{3,7},{4,0},{5,1},{6,2},{7,3},{8,12},{9,13},{10,... | collective-permute-start | bytes 36872 | tf_op jit(solution)/shard_map/ppermute | solution.py:31
  42.0 1.0 %collective-permute-start.14 = (f32[8,384]{1,0:T(8,128)S(1)}, f32[8,384]{1,0:T(8,128)S(1)}, u32[]{:S(2)}, u32[]{:S(2)}) collective-permute-start(f32[8,384]{1,0:T(8,128)S(1)} %get-tuple-element.54.refs_0_), channel_id=1, source_target_pairs={{0,6},{1,7},{2,4},{3,5},{4,2},{5,3},{6,0},{7,1},{8,14},{9,15},{10,... | collective-permute-start | bytes 36872 | tf_op jit(solution)/shard_map/ppermute | solution.py:31
  43.7 3.0 %collective-permute-done.14.refs_3_ = f32[8,384]{1,0:T(8,128)S(1)} collective-permute-done((f32[8,384]{1,0:T(8,128)S(1)}, f32[8,384]{1,0:T(8,128)S(1)}, u32[]{:S(2)}, u32[]{:S(2)}) %collective-permute-start.14) | collective-permute-done | bytes 12320 | tf_op jit(solution)/shard_map/ppermute | solution.py:31
  46.6 0.6 %dynamic-slice_bitcast_fusion = f32[48]{0:T(128)} fusion(f32[1,384]{1,0:T(1,128)S(1)} %slice.4, s32[]{:T(128)S(6)} %select_n.16), kind=kLoop, calls=%fused_computation | loop fusion | bytes 388 | tf_op jit(solution)/shard_map/dynamic_slice | solution.py:431
  47.2 2.0 %all-to-all-done.got_ref = bf16[8,176,128]{2,1,0:T(8,128)(2,1)S(1)} async-done(((bf16[8,176,128]{2,1,0:T(8,128)(2,1)}), bf16[8,176,128]{2,1,0:T(8,128)(2,1)S(1)}, u32[]{:S(2)}, u32[]{:S(2)}) %all-to-all-start) | async-done | bytes 360480 | tf_op jit(solution)/shard_map/all_to_all | solution.py:381
  49.2 0.9 %weight_total.1 = f32[144,288]{1,0:T(8,128)} custom-call(bf16[8,176,128]{2,1,0:T(8,128)(2,1)S(1)} %all-to-all-done.got_ref), custom_call_target="tpu_custom_call" | custom-call | tf_op jit(solution)/shard_map/weight_total/pallas_call | solution.py:382
  (35 shorter events, 4.5 us)
Async XLA Ops:
  0.6 9.9 %collective-permute-start = (bf16[48,1152]{1,0:T(8,128)(2,1)}, bf16[48,1152]{1,0:T(8,128)(2,1)S(1)}, u32[]{:S(2)}, u32[]{:S(2)}) collective-permute-start(bf16[48,1152]{1,0:T(8,128)(2,1)} %refs_0_.1), channel_id=1, source_target_pairs={{0,2},{1,3},{2,0},{3,1},{4,6},{5,7},{6,4},{7,5},{8,10},{9,11},{10,... | collective-permute-start | bytes 331784 | tf_op jit(solution)/shard_map/ppermute | solution.py:31
  3.7 8.6 %collective-permute-start.1 = (bf16[48,1152]{1,0:T(8,128)(2,1)}, bf16[48,1152]{1,0:T(8,128)(2,1)S(1)}, u32[]{:S(2)}, u32[]{:S(2)}) collective-permute-start(bf16[48,1152]{1,0:T(8,128)(2,1)} %refs_0_.1), channel_id=1, source_target_pairs={{0,4},{1,5},{2,6},{3,7},{4,0},{5,1},{6,2},{7,3},{8,12},{9,13},{10,... | collective-permute-start | bytes 331784 | tf_op jit(solution)/shard_map/ppermute | solution.py:31
  5.2 7.1 %collective-permute-start.2 = (bf16[48,1152]{1,0:T(8,128)(2,1)}, bf16[48,1152]{1,0:T(8,128)(2,1)S(1)}, u32[]{:S(2)}, u32[]{:S(2)}) collective-permute-start(bf16[48,1152]{1,0:T(8,128)(2,1)} %refs_0_.1), channel_id=1, source_target_pairs={{0,6},{1,7},{2,4},{3,5},{4,2},{5,3},{6,0},{7,1},{8,14},{9,15},{10,... | collective-permute-start | bytes 331784 | tf_op jit(solution)/shard_map/ppermute | solution.py:31
  5.2 9.5 %collective-permute-start.3 = (bf16[48,1152]{1,0:T(8,128)(2,1)}, bf16[48,1152]{1,0:T(8,128)(2,1)S(1)}, u32[]{:S(2)}, u32[]{:S(2)}) collective-permute-start(bf16[48,1152]{1,0:T(8,128)(2,1)} %text_ref.1), channel_id=1, source_target_pairs={{0,24},{1,25},{2,26},{3,27},{4,28},{5,29},{6,30},{7,31},{8,16},{9,... | collective-permute-start | bytes 331784 | tf_op jit(solution)/shard_map/ppermute | solution.py:31
  9.2 8.7 %collective-permute-start.4 = (bf16[48,1152]{1,0:T(8,128)(2,1)}, bf16[48,1152]{1,0:T(8,128)(2,1)S(1)}, u32[]{:S(2)}, u32[]{:S(2)}) collective-permute-start(bf16[48,1152]{1,0:T(8,128)(2,1)} %text_ref.1), channel_id=1, source_target_pairs={{0,16},{1,17},{2,18},{3,19},{4,20},{5,21},{6,22},{7,23},{8,24},{9,... | collective-permute-start | bytes 331784 | tf_op jit(solution)/shard_map/ppermute | solution.py:31
  10.5 1.7 %copy-start.1 = (bf16[48,1152]{1,0:T(8,128)(2,1)S(1)}, bf16[48,1152]{1,0:T(8,128)(2,1)}, u32[]{:S(2)}) copy-start(bf16[48,1152]{1,0:T(8,128)(2,1)} %refs_0_.1) | copy-start | bytes 331780
  10.6 7.4 %collective-permute-start.5 = (bf16[48,1152]{1,0:T(8,128)(2,1)}, bf16[48,1152]{1,0:T(8,128)(2,1)S(1)}, u32[]{:S(2)}, u32[]{:S(2)}) collective-permute-start(bf16[48,1152]{1,0:T(8,128)(2,1)} %text_ref.1), channel_id=1, source_target_pairs={{0,8},{1,9},{2,10},{3,11},{4,12},{5,13},{6,14},{7,15},{8,0},{9,1},... | collective-permute-start | bytes 331784 | tf_op jit(solution)/shard_map/ppermute | solution.py:31
  11.2 0.9 %copy-start.2 = (bf16[48,1152]{1,0:T(8,128)(2,1)S(1)}, bf16[48,1152]{1,0:T(8,128)(2,1)}, u32[]{:S(2)}) copy-start(bf16[48,1152]{1,0:T(8,128)(2,1)} %text_ref.1) | copy-start | bytes 331780
  12.1 1.7 %copy-start = (bf16[1152,1152]{1,0:T(8,128)(2,1)S(1)}, bf16[1152,1152]{1,0:T(8,128)(2,1)}, u32[]{:S(2)}) copy-start(bf16[1152,1152]{1,0:T(8,128)(2,1)} %weight.1) | copy-start | bytes 7962628
  12.3 5.8 %collective-permute-start.6 = (bf16[192,1152]{1,0:T(8,128)(2,1)S(1)}, bf16[192,1152]{1,0:T(8,128)(2,1)S(1)}, u32[]{:S(2)}, u32[]{:S(2)}) collective-permute-start(bf16[192,1152]{1,0:T(8,128)(2,1)S(1)} %stack.1.feats_ref.own_half), channel_id=1, source_target_pairs={{0,1},{1,0},{2,3},{3,2},{4,5},{5,4},{6,7},{7,6},{8,9},{9,8},{10,11... | collective-permute-start | bytes 1327112 | tf_op jit(solution)/shard_map/ppermute | solution.py:31
  21.0 1.5 %collective-permute-start.7 = (bf16[2,144,384]{2,1,0:T(8,128)(2,1)S(1)}, bf16[2,144,384]{2,1,0:T(8,128)(2,1)S(1)}, u32[]{:S(2)}, u32[]{:S(2)}) collective-permute-start(bf16[2,144,384]{2,1,0:T(8,128)(2,1)S(1)} %get-tuple-element.40), channel_id=1, source_target_pairs={{0,1},{1,0},{2,3},{3,2},{4,5},{5,4},{6,7},{7,6},{8,9},{9,8},{10,11... | collective-permute-start | bytes 663560 | tf_op jit(solution)/shard_map/ppermute | solution.py:31
  21.1 4.6 %collective-permute-start.8 = (bf16[2,160,384]{2,1,0:T(8,128)(2,1)S(1)}, bf16[2,160,384]{2,1,0:T(8,128)(2,1)S(1)}, u32[]{:S(2)}, u32[]{:S(2)}) collective-permute-start(bf16[2,160,384]{2,1,0:T(8,128)(2,1)S(1)} %get-tuple-element.48), channel_id=1, source_target_pairs={{0,1},{1,0},{2,3},{3,2},{4,5},{5,4},{6,7},{7,6},{8,9},{9,8},{10,11... | collective-permute-start | bytes 737288 | tf_op jit(solution)/shard_map/ppermute | solution.py:31
  22.6 6.3 %collective-permute-start.15 = (bf16[144,384]{1,0:T(8,128)(2,1)S(1)}, bf16[144,384]{1,0:T(8,128)(2,1)S(1)}, u32[]{:S(2)}, u32[]{:S(2)}) collective-permute-start(bf16[144,384]{1,0:T(8,128)(2,1)S(1)} %get-tuple-element.58), channel_id=1, source_target_pairs={{0,4},{1,5},{2,6},{3,7},{4,0},{5,1},{6,2},{7,3},{8,12},{9,13},{10,... | collective-permute-start | bytes 331784 | tf_op jit(solution)/shard_map/ppermute | solution.py:31
  24.2 7.0 %collective-permute-start.16 = (bf16[144,384]{1,0:T(8,128)(2,1)S(1)}, bf16[144,384]{1,0:T(8,128)(2,1)S(1)}, u32[]{:S(2)}, u32[]{:S(2)}) collective-permute-start(bf16[144,384]{1,0:T(8,128)(2,1)S(1)} %get-tuple-element.59), channel_id=1, source_target_pairs={{0,6},{1,7},{2,4},{3,5},{4,2},{5,3},{6,0},{7,1},{8,14},{9,15},{10,... | collective-permute-start | bytes 331784 | tf_op jit(solution)/shard_map/ppermute | solution.py:31
  25.7 7.0 %collective-permute-start.17 = (bf16[144,384]{1,0:T(8,128)(2,1)S(1)}, bf16[144,384]{1,0:T(8,128)(2,1)S(1)}, u32[]{:S(2)}, u32[]{:S(2)}) collective-permute-start(bf16[144,384]{1,0:T(8,128)(2,1)S(1)} %get-tuple-element.60), channel_id=1, source_target_pairs={{0,2},{1,3},{2,0},{3,1},{4,6},{5,7},{6,4},{7,5},{8,10},{9,11},{10,... | collective-permute-start | bytes 331784 | tf_op jit(solution)/shard_map/ppermute | solution.py:31
  26.3 12.4 %collective-permute-start.10 = (bf16[48,1152]{1,0:T(8,128)(2,1)S(1)}, bf16[48,1152]{1,0:T(8,128)(2,1)S(1)}, u32[]{:S(2)}, u32[]{:S(2)}) collective-permute-start(bf16[48,1152]{1,0:T(8,128)(2,1)S(1)} %get-tuple-element.52), channel_id=1, source_target_pairs={{0,16},{1,17},{2,18},{3,19},{4,20},{5,21},{6,22},{7,23},{8,24},{9,... | collective-permute-start | bytes 331784 | tf_op jit(solution)/shard_map/ppermute | solution.py:31
  26.8 11.9 %collective-permute-start.11 = (bf16[48,1152]{1,0:T(8,128)(2,1)S(1)}, bf16[48,1152]{1,0:T(8,128)(2,1)S(1)}, u32[]{:S(2)}, u32[]{:S(2)}) collective-permute-start(bf16[48,1152]{1,0:T(8,128)(2,1)S(1)} %get-tuple-element.53), channel_id=1, source_target_pairs={{0,24},{1,25},{2,26},{3,27},{4,28},{5,29},{6,30},{7,31},{8,16},{9,... | collective-permute-start | bytes 331784 | tf_op jit(solution)/shard_map/ppermute | solution.py:31
  28.9 9.8 %collective-permute-start.9 = (bf16[48,1152]{1,0:T(8,128)(2,1)S(1)}, bf16[48,1152]{1,0:T(8,128)(2,1)S(1)}, u32[]{:S(2)}, u32[]{:S(2)}) collective-permute-start(bf16[48,1152]{1,0:T(8,128)(2,1)S(1)} %get-tuple-element.51), channel_id=1, source_target_pairs={{0,8},{1,9},{2,10},{3,11},{4,12},{5,13},{6,14},{7,15},{8,0},{9,1},... | collective-permute-start | bytes 331784 | tf_op jit(solution)/shard_map/ppermute | solution.py:31
  34.0 15.2 %all-to-all-start = ((bf16[8,176,128]{2,1,0:T(8,128)(2,1)}), bf16[8,176,128]{2,1,0:T(8,128)(2,1)S(1)}, u32[]{:S(2)}, u32[]{:S(2)}) async-start(bf16[8,176,128]{2,1,0:T(8,128)(2,1)} %weights.1), calls=%async_computation | async-start | bytes 720896 | tf_op jit(solution)/shard_map/all_to_all | solution.py:381
  39.5 3.7 %collective-permute-start.12 = (f32[8,384]{1,0:T(8,128)S(1)}, f32[8,384]{1,0:T(8,128)S(1)}, u32[]{:S(2)}, u32[]{:S(2)}) collective-permute-start(f32[8,384]{1,0:T(8,128)S(1)} %get-tuple-element.54.refs_0_), channel_id=1, source_target_pairs={{0,2},{1,3},{2,0},{3,1},{4,6},{5,7},{6,4},{7,5},{8,10},{9,11},{10,... | collective-permute-start | bytes 36872 | tf_op jit(solution)/shard_map/ppermute | solution.py:31
  40.0 3.7 %collective-permute-start.13 = (f32[8,384]{1,0:T(8,128)S(1)}, f32[8,384]{1,0:T(8,128)S(1)}, u32[]{:S(2)}, u32[]{:S(2)}) collective-permute-start(f32[8,384]{1,0:T(8,128)S(1)} %get-tuple-element.54.refs_0_), channel_id=1, source_target_pairs={{0,4},{1,5},{2,6},{3,7},{4,0},{5,1},{6,2},{7,3},{8,12},{9,13},{10,... | collective-permute-start | bytes 36872 | tf_op jit(solution)/shard_map/ppermute | solution.py:31
  42.0 4.6 %collective-permute-start.14 = (f32[8,384]{1,0:T(8,128)S(1)}, f32[8,384]{1,0:T(8,128)S(1)}, u32[]{:S(2)}, u32[]{:S(2)}) collective-permute-start(f32[8,384]{1,0:T(8,128)S(1)} %get-tuple-element.54.refs_0_), channel_id=1, source_target_pairs={{0,6},{1,7},{2,4},{3,5},{4,2},{5,3},{6,0},{7,1},{8,14},{9,15},{10,... | collective-permute-start | bytes 36872 | tf_op jit(solution)/shard_map/ppermute | solution.py:31

commit v21 on v19

--- a/solution.py
+++ b/solution.py
@@ -225,32 +225,53 @@
     return inv_ref[...] * total
 
 
-def weight_kernel(group, wide, *refs):
-    own_ref, got = refs[0], refs[1 : group // 4]
-    inv_ref, feats_ref, feats_t_ref, loss_out, send_out = refs[group // 4 :]
+def weight_kernel(group, spread, *refs):
+    wide_ref, own_ref = refs[:2]
+    got = refs[2 : 1 + group // 4]
+    inv_ref, feats_ref, feats_t_ref, loss_out, own_out = refs[1 + group // 4 : 6 + group // 4]
+    send_out = refs[6 + group // 4 : 5 + group // 4 + spread]
+    main_all, rest_all = refs[5 + group // 4 + spread :]
+    wide = 2 * spread
     rows = feats_t_ref.shape[0] // wide
     high, low = split_pair(gathered_gradient(own_ref, got, inv_ref, loss_out))
     rest = high.shape[0] - LANES
+    both = jnp.concatenate([high[:LANES, :], low[:LANES, :]], axis=0)
+    main = lax.dot_general(feats_t_ref[...], both, NT, preferred_element_type=F32)
+    main_all[...] = main[:, :LANES] + main[:, LANES:]
     both = jnp.concatenate([high[LANES:, :], low[LANES:, :]], axis=0)
     tail = jnp.dot(both, feats_ref[...], preferred_element_type=F32)
-    tail = (tail[:rest, :] + tail[rest:, :]).astype(BF16)
-    both = jnp.concatenate([high[:LANES, :], low[:LANES, :]], axis=0)
-    main = lax.dot_general(feats_t_ref[...], both, NT, preferred_element_type=F32)
-    main = (main[:, :LANES] + main[:, LANES:]).astype(BF16)
+    tail = tail[:rest, :] + tail[rest:, :]
     for place in range(wide):
         begin = place * rows
-        send_out[place, :rows, :] = main[begin : begin + rows, :]
-        send_out[place, rows : rows + rest, :] = tail[:, begin : begin + LANES]
-        send_out[place, rows + rest :, :] = jnp.zeros((rest, LANES), BF16)
-        send_out[place, rows + rest :, : rows - LANES] = tail[:, begin + LANES : begin + rows]
-
-
-def total_kernel(rest, got_ref, out):
+        rest_all[place, :rest, :] = tail[:, begin : begin + LANES]
+        rest_all[place, rest:, :] = jnp.zeros((rest, LANES), F32)
+        rest_all[place, rest:, : rows - LANES] = tail[:, begin + LANES : begin + rows]
+    for step in range(spread):
+        target = send_out[step - 1] if step else own_out
+        for side in range(2):
+            place = wide_ref[0] ^ (2 * step + side)
+            begin = side * (rows + 2 * rest)
+            part = main_all[pl.ds(pl.multiple_of(place * rows, rows), rows), :]
+            target[begin : begin + rows, :] = part.astype(target.dtype)
+            target[begin + rows : begin + rows + 2 * rest, :] = rest_all[place].astype(target.dtype)
+
+
+def line_kernel(*refs):
+    blocks, (own_out, send_out) = refs[:-2], refs[-2:]
+    total = blocks[0][...]
+    for block in blocks[1:]:
+        total = total + block[...].astype(F32)
+    packed = own_out.shape[0]
+    own_out[...] = total[:packed, :]
+    send_out[...] = total[packed:, :].astype(BF16)
+
+
+def total_kernel(rest, wide_ref, same_ref, other_ref, out):
     rows = out.shape[0]
-    for side in range(2):
-        half = got_ref[side].astype(F32)
-        for place in range(side + 2, got_ref.shape[0], 2):
-            half = half + got_ref[place].astype(F32)
+    same, other = same_ref[...], other_ref[...].astype(F32)
+    left_is_same = wide_ref[0] % 2 == 0
+    halves = (jnp.where(left_is_same, same, other), jnp.where(left_is_same, other, same))
+    for side, half in enumerate(halves):
         left = side * (LANES + rest)
         out[:, left : left + LANES] = half[:rows, :]
         out[:LANES, left + LANES : left + LANES + rest] = half[rows : rows + rest, :].T
@@ -382,26 +403,35 @@
     packed = out_rows + 2 * rest
     direct = LANES < out_rows <= 2 * LANES and out_rows % 16 == 0 and rest % 16 == 0
     if direct:
-        loss_line, sent_weight = pl.pallas_call(
-            functools.partial(weight_kernel, group, wide),
-            in_specs=[VMEM] * (3 + group // 4),
-            out_specs=[VMEM] * 2,
-            out_shape=[
-                jax.ShapeDtypeStruct((1, images), F32),
-                jax.ShapeDtypeStruct((wide, packed, LANES), BF16),
-            ],
+        wide_pos = lax.axis_index(AXES[:2]).astype(jnp.int32).reshape(1)
+        loss_line, own_weight, *sent_weight = pl.pallas_call(
+            functools.partial(weight_kernel, group, spread),
+            in_specs=[SMEM] + [VMEM] * (3 + group // 4),
+            out_specs=[VMEM] * (1 + spread),
+            out_shape=[jax.ShapeDtypeStruct((1, images), F32), jax.ShapeDtypeStruct((2 * packed, LANES), F32)]
+            + [jax.ShapeDtypeStruct((2 * packed, LANES), BF16)] * (spread - 1),
+            scratch_shapes=[pltpu.VMEM((width, LANES), F32), pltpu.VMEM((wide, 2 * rest, LANES), F32)],
             compiler_params=limit(12),
             name="weights",
-        )(own_part, *near, inv_part, all_feats, feats_t)
-        got_weight = lax.all_to_all(sent_weight, AXES[:2], 0, 0)
+        )(wide_pos, own_part, *near, inv_part, all_feats, feats_t)
+        got_weight = [swapped(value, total, step * group) for step, value in enumerate(sent_weight, 1)]
+        own_weight, sent_weight = pl.pallas_call(
+            line_kernel,
+            in_specs=[VMEM] * spread,
+            out_specs=[VMEM] * 2,
+            out_shape=[jax.ShapeDtypeStruct((packed, LANES), kind) for kind in (F32, BF16)],
+            compiler_params=limit(4),
+            name="weight_line",
+        )(own_weight, *got_weight[::-1])
+        got_weight = swapped(sent_weight, total, narrow)
         d_proj = pl.pallas_call(
             functools.partial(total_kernel, rest),
-            in_specs=[VMEM],
+            in_specs=[SMEM] + [VMEM] * 2,
             out_specs=VMEM,
             out_shape=jax.ShapeDtypeStruct((out_rows, 2 * share), F32),
             compiler_params=limit(4),
             name="weight_total",
-        )(got_weight)
+        )(wide_pos, own_weight, got_weight)
     else:
 
         def gradient_kernel(*refs):

time: 49.4 us -> 50.8 us (1.028)
  starting transfers between devices: 21.5 us -> 23.9 us
  Pallas kernels: 7.66 us -> 7 us
    all_to_all x1 -> x0, waiting for transfers between devices: 9.02 us -> none  [local(): got_weight = lax.all_to_all(sent_weight, AXES[:2], 0, 0)]
    ppermute x15 -> x19, waiting for transfers between devices: 5.81 us -> 14.7 us  [swapped(): lax.ppermute(value, AXES, [(source, source ^ mask) for source in range(to...]
    ppermute x15 -> x19, starting transfers between devices: 16.9 us -> 23.9 us  [swapped(): lax.ppermute(value, AXES, [(source, source ^ mask) for source in range(to...]
    all_to_all x1 -> x0, starting transfers between devices: 4.65 us -> none  [local(): got_weight = lax.all_to_all(sent_weight, AXES[:2], 0, 0)]
    pallas_call x2 -> x3, Pallas kernels: 2.24 us -> 1.59 us  [the longest x1 0.87 us: local(): pl.pallas_call(functools.partial(total_kernel, rest), in_specs=[SMEM] + [...]
  transfers between devices with their start and end apart: 16 -> 19, of which waited for: 6 -> 7; matrix products, arithmetic and copies ran while one was open for 1% -> 1% of each run, Pallas kernels for 8% -> 6%
where the time goes in v21:
time: 50.8 us; the launch traced here: 50.6 us
  starting transfers between devices  23.9 us (47%)
  waiting for transfers between devices  14.7 us (29%)
  Pallas kernels  7 us (14%)
  local copies, waits for them, and re-layouts  2.98 us (6%)
  between operations  2.08 us (4%)
    ppermute x19, starting transfers between devices, swapped(): lax.ppermute(value, AXES, [(source, source ^ mask) for source in range(to...  23.9 us
    ppermute x19, waiting for transfers between devices, swapped(): lax.ppermute(value, AXES, [(source, source ^ mask) for source in range(to...  14.7 us
    pallas_call x1, Pallas kernels, local(): pl.pallas_call(functools.partial(pair_kernel, narrow, group), in_specs=[S...  2.89 us
    unnamed x6, local copies, waits for them, and re-layouts  2.4 us
  transfers between devices with their start and end apart: 19, of which 7 were waited for; matrix products, arithmetic and copies ran while one was open for 1% of the time, Pallas kernels for 6%

profile of v21, /device:TPU:0, one launch (start us, length us, event | category | flops | bytes accessed | tf_op | source)
XLA Modules:
  0.0 50.6 jit_solution(8994016198446471136)
XLA Ops:
  0.6 3.0 %collective-permute-start = (bf16[48,1152]{1,0:T(8,128)(2,1)}, bf16[48,1152]{1,0:T(8,128)(2,1)S(1)}, u32[]{:S(2)}, u32[]{:S(2)}) collective-permute-start(bf16[48,1152]{1,0:T(8,128)(2,1)} %refs_0_.1), channel_id=1, source_target_pairs={{0,2},{1,3},{2,0},{3,1},{4,6},{5,7},{6,4},{7,5},{8,10},{9,11},{10,... | collective-permute-start | bytes 331784 | tf_op jit(solution)/shard_map/ppermute | solution.py:31
  3.7 1.5 %collective-permute-start.1 = (bf16[48,1152]{1,0:T(8,128)(2,1)}, bf16[48,1152]{1,0:T(8,128)(2,1)S(1)}, u32[]{:S(2)}, u32[]{:S(2)}) collective-permute-start(bf16[48,1152]{1,0:T(8,128)(2,1)} %refs_0_.1), channel_id=1, source_target_pairs={{0,4},{1,5},{2,6},{3,7},{4,0},{5,1},{6,2},{7,3},{8,12},{9,13},{10,... | collective-permute-start | bytes 331784 | tf_op jit(solution)/shard_map/ppermute | solution.py:31
  5.2 4.0 %collective-permute-start.3 = (bf16[48,1152]{1,0:T(8,128)(2,1)}, bf16[48,1152]{1,0:T(8,128)(2,1)S(1)}, u32[]{:S(2)}, u32[]{:S(2)}) collective-permute-start(bf16[48,1152]{1,0:T(8,128)(2,1)} %text_ref.1), channel_id=1, source_target_pairs={{0,24},{1,25},{2,26},{3,27},{4,28},{5,29},{6,30},{7,31},{8,16},{9,... | collective-permute-start | bytes 331784 | tf_op jit(solution)/shard_map/ppermute | solution.py:31
  10.6 0.6 %collective-permute-start.5 = (bf16[48,1152]{1,0:T(8,128)(2,1)}, bf16[48,1152]{1,0:T(8,128)(2,1)S(1)}, u32[]{:S(2)}, u32[]{:S(2)}) collective-permute-start(bf16[48,1152]{1,0:T(8,128)(2,1)} %text_ref.1), channel_id=1, source_target_pairs={{0,8},{1,9},{2,10},{3,11},{4,12},{5,13},{6,14},{7,15},{8,0},{9,1},... | collective-permute-start | bytes 331784 | tf_op jit(solution)/shard_map/ppermute | solution.py:31
  11.2 0.9 %copy-done.2 = bf16[48,1152]{1,0:T(8,128)(2,1)S(1)} copy-done((bf16[48,1152]{1,0:T(8,128)(2,1)S(1)}, bf16[48,1152]{1,0:T(8,128)(2,1)}, u32[]{:S(2)}) %copy-start.2) | copy-done | bytes 110616
  12.4 1.5 %copy-done = bf16[1152,1152]{1,0:T(8,128)(2,1)S(1)} copy-done((bf16[1152,1152]{1,0:T(8,128)(2,1)S(1)}, bf16[1152,1152]{1,0:T(8,128)(2,1)}, u32[]{:S(2)}) %copy-start) | copy-done | bytes 2654232
  13.9 0.8 %own_projection.1.own_proj = f32[192,1152]{1,0:T(8,128)S(1)} custom-call(bf16[192,1152]{1,0:T(8,128)(2,1)S(1)} %stack.1.feats_ref.own_half, bf16[1152,1152]{1,0:T(8,128)(2,1)S(1)} %copy-done), custom_call_target="tpu_custom_call" | custom-call | tf_op jit(solution)/shard_map/own_projection/pallas_call | solution.py:317
  14.7 3.3 %collective-permute-done.4.refs_2_ = bf16[48,1152]{1,0:T(8,128)(2,1)S(1)} collective-permute-done((bf16[48,1152]{1,0:T(8,128)(2,1)}, bf16[48,1152]{1,0:T(8,128)(2,1)S(1)}, u32[]{:S(2)}, u32[]{:S(2)}) %collective-permute-start.4) | collective-permute-done | bytes 110624 | tf_op jit(solution)/shard_map/ppermute | solution.py:31
  18.1 2.9 %pairs.1 = (bf16[384,1152]{1,0:T(8,128)(2,1)S(1)}, f32[1,384]{1,0:T(1,128)S(1)}, bf16[1152,384]{1,0:T(8,128)(2,1)S(1)}, bf16[192,384]{1,0:T(8,128)(2,1)S(1)}, f3...) custom-call(s32[1]{0:T(128)} %bitcast.1.member_ref, ...), custom_call_target="tpu_custom_call" | custom-call | tf_op jit(solution)/shard_map/pairs/pallas_call | solution.py:336
  22.7 1.6 %collective-permute-start.9 = (bf16[160,384]{1,0:T(8,128)(2,1)S(1)}, bf16[160,384]{1,0:T(8,128)(2,1)S(1)}, u32[]{:S(2)}, u32[]{:S(2)}) collective-permute-start(bf16[160,384]{1,0:T(8,128)(2,1)S(1)} %get-tuple-element.55), channel_id=1, source_target_pairs={{0,4},{1,5},{2,6},{3,7},{4,0},{5,1},{6,2},{7,3},{8,12},{9,13},{10,... | collective-permute-start | bytes 368648 | tf_op jit(solution)/shard_map/ppermute | solution.py:31
  24.2 1.5 %collective-permute-start.10 = (bf16[160,384]{1,0:T(8,128)(2,1)S(1)}, bf16[160,384]{1,0:T(8,128)(2,1)S(1)}, u32[]{:S(2)}, u32[]{:S(2)}) collective-permute-start(bf16[160,384]{1,0:T(8,128)(2,1)S(1)} %get-tuple-element.56), channel_id=1, source_target_pairs={{0,6},{1,7},{2,4},{3,5},{4,2},{5,3},{6,0},{7,1},{8,14},{9,15},{10,... | collective-permute-start | bytes 368648 | tf_op jit(solution)/shard_map/ppermute | solution.py:31
  26.3 2.4 %collective-permute-start.12 = (bf16[48,1152]{1,0:T(8,128)(2,1)S(1)}, bf16[48,1152]{1,0:T(8,128)(2,1)S(1)}, u32[]{:S(2)}, u32[]{:S(2)}) collective-permute-start(bf16[48,1152]{1,0:T(8,128)(2,1)S(1)} %get-tuple-element.62), channel_id=1, source_target_pairs={{0,24},{1,25},{2,26},{3,27},{4,28},{5,29},{6,30},{7,31},{8,16},{9,... | collective-permute-start | bytes 331784 | tf_op jit(solution)/shard_map/ppermute | solution.py:31
  28.8 1.9 %collective-permute-start.14 = (bf16[48,1152]{1,0:T(8,128)(2,1)S(1)}, bf16[48,1152]{1,0:T(8,128)(2,1)S(1)}, u32[]{:S(2)}, u32[]{:S(2)}) collective-permute-start(bf16[48,1152]{1,0:T(8,128)(2,1)S(1)} %get-tuple-element.64), channel_id=1, source_target_pairs={{0,8},{1,9},{2,10},{3,11},{4,12},{5,13},{6,14},{7,15},{8,0},{9,1},... | collective-permute-start | bytes 331784 | tf_op jit(solution)/shard_map/ppermute | solution.py:31
  30.7 1.0 %collective-permute-done.10.refs_2_ = bf16[160,384]{1,0:T(8,128)(2,1)S(1)} collective-permute-done((bf16[160,384]{1,0:T(8,128)(2,1)S(1)}, bf16[160,384]{1,0:T(8,128)(2,1)S(1)}, u32[]{:S(2)}, u32[]{:S(2)}) %collective-permute-start.10) | collective-permute-done | bytes 122912 | tf_op jit(solution)/shard_map/ppermute | solution.py:31
  31.8 1.4 %collective-permute-done.11.refs_2_ = bf16[160,384]{1,0:T(8,128)(2,1)S(1)} collective-permute-done((bf16[160,384]{1,0:T(8,128)(2,1)S(1)}, bf16[160,384]{1,0:T(8,128)(2,1)S(1)}, u32[]{:S(2)}, u32[]{:S(2)}) %collective-permute-start.11) | collective-permute-done | bytes 122912 | tf_op jit(solution)/shard_map/ppermute | solution.py:31
  33.3 0.7 %weights.1 = (f32[1,384]{1,0:T(1,128)S(1)}, f32[352,128]{1,0:T(8,128)S(1)}, bf16[352,128]{1,0:T(8,128)(2,1)S(1)}, bf16[352,128]{1,0:T(8,128)(2,1)S(1)}, bf16[352,128]{1,0:T(8,128)(2,1)S(1)}) custom-call(s32[1]{0:T(128)} %bitcast.refs_0_.wide_ref, f32[152,384]{1,0:T(8,128)S(1)} %far_sum.1.refs_1_, bf16[160,384]{1,0:T(8,128)(2,1)S(1)} %collective-permute-done.11.refs_2_, ...), custom_call_target="tpu_custom_call" | custom-call | tf_op jit(solution)/shard_map/weights/pallas_call | solution.py:407
  33.9 2.5 %collective-permute-start.15 = (bf16[352,128]{1,0:T(8,128)(2,1)S(1)}, bf16[352,128]{1,0:T(8,128)(2,1)S(1)}, u32[]{:S(2)}, u32[]{:S(2)}) collective-permute-start(bf16[352,128]{1,0:T(8,128)(2,1)S(1)} %get-tuple-element.66), channel_id=1, source_target_pairs={{0,24},{1,25},{2,26},{3,27},{4,28},{5,29},{6,30},{7,31},{8,16},{9,... | collective-permute-start | bytes 270344 | tf_op jit(solution)/shard_map/ppermute | solution.py:31
  36.5 1.9 %collective-permute-start.17 = (bf16[352,128]{1,0:T(8,128)(2,1)S(1)}, bf16[352,128]{1,0:T(8,128)(2,1)S(1)}, u32[]{:S(2)}, u32[]{:S(2)}) collective-permute-start(bf16[352,128]{1,0:T(8,128)(2,1)S(1)} %get-tuple-element.68), channel_id=1, source_target_pairs={{0,8},{1,9},{2,10},{3,11},{4,12},{5,13},{6,14},{7,15},{8,0},{9,1},... | collective-permute-start | bytes 270344 | tf_op jit(solution)/shard_map/ppermute | solution.py:31
  38.4 3.1 %collective-permute-done.13.refs_2_ = bf16[48,1152]{1,0:T(8,128)(2,1)S(1)} collective-permute-done((bf16[48,1152]{1,0:T(8,128)(2,1)S(1)}, bf16[48,1152]{1,0:T(8,128)(2,1)S(1)}, u32[]{:S(2)}, u32[]{:S(2)}) %collective-permute-start.13) | collective-permute-done | bytes 110624 | tf_op jit(solution)/shard_map/ppermute | solution.py:31
  41.5 0.7 %caption_total.1 = f32[48,1152]{1,0:T(8,128)} custom-call(f32[48,1152]{1,0:T(8,128)S(1)} %get-tuple-element.61.refs_0_, bf16[48,1152]{1,0:T(8,128)(2,1)S(1)} %collective-permute-done.12.refs_1_, bf16[48,1152]{1,0:T(8,128)(2,1)S(1)} %collective-permute-done.13.refs_2_, bf16[48,1152]{1,0:T(8,128)(2,1)S(1)} %collective-permute-done.14.refs_3_), custom_call_target="tpu_custom_call" | custom-call | flops 5000000000 | tf_op jit(solution)/shard_map/caption_total/pallas_call | solution.py:457
  42.3 3.3 %collective-permute-done.16.refs_2_ = bf16[352,128]{1,0:T(8,128)(2,1)S(1)} collective-permute-done((bf16[352,128]{1,0:T(8,128)(2,1)S(1)}, bf16[352,128]{1,0:T(8,128)(2,1)S(1)}, u32[]{:S(2)}, u32[]{:S(2)}) %collective-permute-start.16) | collective-permute-done | bytes 90144 | tf_op jit(solution)/shard_map/ppermute | solution.py:31
  45.6 1.6 %collective-permute-start.18 = (bf16[176,128]{1,0:T(8,128)(2,1)S(1)}, bf16[176,128]{1,0:T(8,128)(2,1)S(1)}, u32[]{:S(2)}, u32[]{:S(2)}) collective-permute-start(bf16[176,128]{1,0:T(8,128)(2,1)S(1)} %get-tuple-element.70), channel_id=1, source_target_pairs={{0,4},{1,5},{2,6},{3,7},{4,0},{5,1},{6,2},{7,3},{8,12},{9,13},{10,... | collective-permute-start | bytes 135176 | tf_op jit(solution)/shard_map/ppermute | solution.py:31
  47.8 2.0 %collective-permute-done.18.other_ref = bf16[176,128]{1,0:T(8,128)(2,1)S(1)} collective-permute-done((bf16[176,128]{1,0:T(8,128)(2,1)S(1)}, bf16[176,128]{1,0:T(8,128)(2,1)S(1)}, u32[]{:S(2)}, u32[]{:S(2)}) %collective-permute-start.18) | collective-permute-done | bytes 45088 | tf_op jit(solution)/shard_map/ppermute | solution.py:31
  49.8 0.9 %weight_total.1 = f32[144,288]{1,0:T(8,128)} custom-call(s32[1]{0:T(128)} %bitcast.refs_0_.wide_ref, f32[176,128]{1,0:T(8,128)S(1)} %get-tuple-element.69.same_ref, bf16[176,128]{1,0:T(8,128)(2,1)S(1)} %collective-permute-done.18.other_ref), custom_call_target="tpu_custom_call" | custom-call | tf_op jit(solution)/shard_map/weight_total/pallas_call | solution.py:427
  (34 shorter events, 3.4 us)
Async XLA Ops:
  0.6 9.9 %collective-permute-start = (bf16[48,1152]{1,0:T(8,128)(2,1)}, bf16[48,1152]{1,0:T(8,128)(2,1)S(1)}, u32[]{:S(2)}, u32[]{:S(2)}) collective-permute-start(bf16[48,1152]{1,0:T(8,128)(2,1)} %refs_0_.1), channel_id=1, source_target_pairs={{0,2},{1,3},{2,0},{3,1},{4,6},{5,7},{6,4},{7,5},{8,10},{9,11},{10,... | collective-permute-start | bytes 331784 | tf_op jit(solution)/shard_map/ppermute | solution.py:31
  3.7 8.6 %collective-permute-start.1 = (bf16[48,1152]{1,0:T(8,128)(2,1)}, bf16[48,1152]{1,0:T(8,128)(2,1)S(1)}, u32[]{:S(2)}, u32[]{:S(2)}) collective-permute-start(bf16[48,1152]{1,0:T(8,128)(2,1)} %refs_0_.1), channel_id=1, source_target_pairs={{0,4},{1,5},{2,6},{3,7},{4,0},{5,1},{6,2},{7,3},{8,12},{9,13},{10,... | collective-permute-start | bytes 331784 | tf_op jit(solution)/shard_map/ppermute | solution.py:31
  5.2 7.1 %collective-permute-start.2 = (bf16[48,1152]{1,0:T(8,128)(2,1)}, bf16[48,1152]{1,0:T(8,128)(2,1)S(1)}, u32[]{:S(2)}, u32[]{:S(2)}) collective-permute-start(bf16[48,1152]{1,0:T(8,128)(2,1)} %refs_0_.1), channel_id=1, source_target_pairs={{0,6},{1,7},{2,4},{3,5},{4,2},{5,3},{6,0},{7,1},{8,14},{9,15},{10,... | collective-permute-start | bytes 331784 | tf_op jit(solution)/shard_map/ppermute | solution.py:31
  5.2 9.5 %collective-permute-start.3 = (bf16[48,1152]{1,0:T(8,128)(2,1)}, bf16[48,1152]{1,0:T(8,128)(2,1)S(1)}, u32[]{:S(2)}, u32[]{:S(2)}) collective-permute-start(bf16[48,1152]{1,0:T(8,128)(2,1)} %text_ref.1), channel_id=1, source_target_pairs={{0,24},{1,25},{2,26},{3,27},{4,28},{5,29},{6,30},{7,31},{8,16},{9,... | collective-permute-start | bytes 331784 | tf_op jit(solution)/shard_map/ppermute | solution.py:31
  9.2 8.7 %collective-permute-start.4 = (bf16[48,1152]{1,0:T(8,128)(2,1)}, bf16[48,1152]{1,0:T(8,128)(2,1)S(1)}, u32[]{:S(2)}, u32[]{:S(2)}) collective-permute-start(bf16[48,1152]{1,0:T(8,128)(2,1)} %text_ref.1), channel_id=1, source_target_pairs={{0,16},{1,17},{2,18},{3,19},{4,20},{5,21},{6,22},{7,23},{8,24},{9,... | collective-permute-start | bytes 331784 | tf_op jit(solution)/shard_map/ppermute | solution.py:31
  10.5 1.7 %copy-start.1 = (bf16[48,1152]{1,0:T(8,128)(2,1)S(1)}, bf16[48,1152]{1,0:T(8,128)(2,1)}, u32[]{:S(2)}) copy-start(bf16[48,1152]{1,0:T(8,128)(2,1)} %refs_0_.1) | copy-start | bytes 331780
  10.6 7.4 %collective-permute-start.5 = (bf16[48,1152]{1,0:T(8,128)(2,1)}, bf16[48,1152]{1,0:T(8,128)(2,1)S(1)}, u32[]{:S(2)}, u32[]{:S(2)}) collective-permute-start(bf16[48,1152]{1,0:T(8,128)(2,1)} %text_ref.1), channel_id=1, source_target_pairs={{0,8},{1,9},{2,10},{3,11},{4,12},{5,13},{6,14},{7,15},{8,0},{9,1},... | collective-permute-start | bytes 331784 | tf_op jit(solution)/shard_map/ppermute | solution.py:31
  11.2 0.9 %copy-start.2 = (bf16[48,1152]{1,0:T(8,128)(2,1)S(1)}, bf16[48,1152]{1,0:T(8,128)(2,1)}, u32[]{:S(2)}) copy-start(bf16[48,1152]{1,0:T(8,128)(2,1)} %text_ref.1) | copy-start | bytes 331780
  12.1 1.7 %copy-start = (bf16[1152,1152]{1,0:T(8,128)(2,1)S(1)}, bf16[1152,1152]{1,0:T(8,128)(2,1)}, u32[]{:S(2)}) copy-start(bf16[1152,1152]{1,0:T(8,128)(2,1)} %weight.1) | copy-start | bytes 7962628
  12.3 5.8 %collective-permute-start.6 = (bf16[192,1152]{1,0:T(8,128)(2,1)S(1)}, bf16[192,1152]{1,0:T(8,128)(2,1)S(1)}, u32[]{:S(2)}, u32[]{:S(2)}) collective-permute-start(bf16[192,1152]{1,0:T(8,128)(2,1)S(1)} %stack.1.feats_ref.own_half), channel_id=1, source_target_pairs={{0,1},{1,0},{2,3},{3,2},{4,5},{5,4},{6,7},{7,6},{8,9},{9,8},{10,11... | collective-permute-start | bytes 1327112 | tf_op jit(solution)/shard_map/ppermute | solution.py:31
  21.0 1.6 %collective-permute-start.7 = (bf16[2,160,384]{2,1,0:T(8,128)(2,1)S(1)}, bf16[2,160,384]{2,1,0:T(8,128)(2,1)S(1)}, u32[]{:S(2)}, u32[]{:S(2)}) collective-permute-start(bf16[2,160,384]{2,1,0:T(8,128)(2,1)S(1)} %get-tuple-element.44), channel_id=1, source_target_pairs={{0,1},{1,0},{2,3},{3,2},{4,5},{5,4},{6,7},{7,6},{8,9},{9,8},{10,11... | collective-permute-start | bytes 737288 | tf_op jit(solution)/shard_map/ppermute | solution.py:31
  21.1 4.6 %collective-permute-start.8 = (bf16[2,160,384]{2,1,0:T(8,128)(2,1)S(1)}, bf16[2,160,384]{2,1,0:T(8,128)(2,1)S(1)}, u32[]{:S(2)}, u32[]{:S(2)}) collective-permute-start(bf16[2,160,384]{2,1,0:T(8,128)(2,1)S(1)} %get-tuple-element.52), channel_id=1, source_target_pairs={{0,1},{1,0},{2,3},{3,2},{4,5},{5,4},{6,7},{7,6},{8,9},{9,8},{10,11... | collective-permute-start | bytes 737288 | tf_op jit(solution)/shard_map/ppermute | solution.py:31
  22.7 6.1 %collective-permute-start.9 = (bf16[160,384]{1,0:T(8,128)(2,1)S(1)}, bf16[160,384]{1,0:T(8,128)(2,1)S(1)}, u32[]{:S(2)}, u32[]{:S(2)}) collective-permute-start(bf16[160,384]{1,0:T(8,128)(2,1)S(1)} %get-tuple-element.55), channel_id=1, source_target_pairs={{0,4},{1,5},{2,6},{3,7},{4,0},{5,1},{6,2},{7,3},{8,12},{9,13},{10,... | collective-permute-start | bytes 368648 | tf_op jit(solution)/shard_map/ppermute | solution.py:31
  24.2 7.6 %collective-permute-start.10 = (bf16[160,384]{1,0:T(8,128)(2,1)S(1)}, bf16[160,384]{1,0:T(8,128)(2,1)S(1)}, u32[]{:S(2)}, u32[]{:S(2)}) collective-permute-start(bf16[160,384]{1,0:T(8,128)(2,1)S(1)} %get-tuple-element.56), channel_id=1, source_target_pairs={{0,6},{1,7},{2,4},{3,5},{4,2},{5,3},{6,0},{7,1},{8,14},{9,15},{10,... | collective-permute-start | bytes 368648 | tf_op jit(solution)/shard_map/ppermute | solution.py:31
  25.8 7.5 %collective-permute-start.11 = (bf16[160,384]{1,0:T(8,128)(2,1)S(1)}, bf16[160,384]{1,0:T(8,128)(2,1)S(1)}, u32[]{:S(2)}, u32[]{:S(2)}) collective-permute-start(bf16[160,384]{1,0:T(8,128)(2,1)S(1)} %get-tuple-element.57), channel_id=1, source_target_pairs={{0,2},{1,3},{2,0},{3,1},{4,6},{5,7},{6,4},{7,5},{8,10},{9,11},{10,... | collective-permute-start | bytes 368648 | tf_op jit(solution)/shard_map/ppermute | solution.py:31
  26.3 10.1 %collective-permute-start.12 = (bf16[48,1152]{1,0:T(8,128)(2,1)S(1)}, bf16[48,1152]{1,0:T(8,128)(2,1)S(1)}, u32[]{:S(2)}, u32[]{:S(2)}) collective-permute-start(bf16[48,1152]{1,0:T(8,128)(2,1)S(1)} %get-tuple-element.62), channel_id=1, source_target_pairs={{0,24},{1,25},{2,26},{3,27},{4,28},{5,29},{6,30},{7,31},{8,16},{9,... | collective-permute-start | bytes 331784 | tf_op jit(solution)/shard_map/ppermute | solution.py:31
  28.8 12.8 %collective-permute-start.13 = (bf16[48,1152]{1,0:T(8,128)(2,1)S(1)}, bf16[48,1152]{1,0:T(8,128)(2,1)S(1)}, u32[]{:S(2)}, u32[]{:S(2)}) collective-permute-start(bf16[48,1152]{1,0:T(8,128)(2,1)S(1)} %get-tuple-element.63), channel_id=1, source_target_pairs={{0,16},{1,17},{2,18},{3,19},{4,20},{5,21},{6,22},{7,23},{8,24},{9,... | collective-permute-start | bytes 331784 | tf_op jit(solution)/shard_map/ppermute | solution.py:31
  28.8 12.8 %collective-permute-start.14 = (bf16[48,1152]{1,0:T(8,128)(2,1)S(1)}, bf16[48,1152]{1,0:T(8,128)(2,1)S(1)}, u32[]{:S(2)}, u32[]{:S(2)}) collective-permute-start(bf16[48,1152]{1,0:T(8,128)(2,1)S(1)} %get-tuple-element.64), channel_id=1, source_target_pairs={{0,8},{1,9},{2,10},{3,11},{4,12},{5,13},{6,14},{7,15},{8,0},{9,1},... | collective-permute-start | bytes 331784 | tf_op jit(solution)/shard_map/ppermute | solution.py:31
  33.9 8.3 %collective-permute-start.15 = (bf16[352,128]{1,0:T(8,128)(2,1)S(1)}, bf16[352,128]{1,0:T(8,128)(2,1)S(1)}, u32[]{:S(2)}, u32[]{:S(2)}) collective-permute-start(bf16[352,128]{1,0:T(8,128)(2,1)S(1)} %get-tuple-element.66), channel_id=1, source_target_pairs={{0,24},{1,25},{2,26},{3,27},{4,28},{5,29},{6,30},{7,31},{8,16},{9,... | collective-permute-start | bytes 270344 | tf_op jit(solution)/shard_map/ppermute | solution.py:31
  36.5 9.1 %collective-permute-start.16 = (bf16[352,128]{1,0:T(8,128)(2,1)S(1)}, bf16[352,128]{1,0:T(8,128)(2,1)S(1)}, u32[]{:S(2)}, u32[]{:S(2)}) collective-permute-start(bf16[352,128]{1,0:T(8,128)(2,1)S(1)} %get-tuple-element.67), channel_id=1, source_target_pairs={{0,16},{1,17},{2,18},{3,19},{4,20},{5,21},{6,22},{7,23},{8,24},{9,... | collective-permute-start | bytes 270344 | tf_op jit(solution)/shard_map/ppermute | solution.py:31
  36.5 9.1 %collective-permute-start.17 = (bf16[352,128]{1,0:T(8,128)(2,1)S(1)}, bf16[352,128]{1,0:T(8,128)(2,1)S(1)}, u32[]{:S(2)}, u32[]{:S(2)}) collective-permute-start(bf16[352,128]{1,0:T(8,128)(2,1)S(1)} %get-tuple-element.68), channel_id=1, source_target_pairs={{0,8},{1,9},{2,10},{3,11},{4,12},{5,13},{6,14},{7,15},{8,0},{9,1},... | collective-permute-start | bytes 270344 | tf_op jit(solution)/shard_map/ppermute | solution.py:31
  45.6 4.1 %collective-permute-start.18 = (bf16[176,128]{1,0:T(8,128)(2,1)S(1)}, bf16[176,128]{1,0:T(8,128)(2,1)S(1)}, u32[]{:S(2)}, u32[]{:S(2)}) collective-permute-start(bf16[176,128]{1,0:T(8,128)(2,1)S(1)} %get-tuple-element.70), channel_id=1, source_target_pairs={{0,4},{1,5},{2,6},{3,7},{4,0},{5,1},{6,2},{7,3},{8,12},{9,13},{10,... | collective-permute-start | bytes 135176 | tf_op jit(solution)/shard_map/ppermute | solution.py:31

commit v22 on v19

--- a/solution.py
+++ b/solution.py
@@ -176,7 +176,7 @@
     losses = loss_rows(loss_sum)
     for index in range(group // 2):
         own_out[index, :share, :] = projected(2 * index)
-        target = (near_out, far_out)[index * 4 // group].at[index % (group // 4)]
+        target = far_out.at[0] if index == group // 2 - 1 else near_out.at[index]
         target[:share, :] = projected(2 * index + 1).astype(BF16)
         target[share:, :] = losses
     own_out[0, share : share + 1, :] = loss_sum
@@ -226,8 +226,8 @@
 
 
 def weight_kernel(group, wide, *refs):
-    own_ref, got = refs[0], refs[1 : group // 4]
-    inv_ref, feats_ref, feats_t_ref, loss_out, send_out = refs[group // 4 :]
+    own_ref, got = refs[0], refs[1 : group // 2 - 1]
+    inv_ref, feats_ref, feats_t_ref, loss_out, send_out = refs[group // 2 - 1 :]
     rows = feats_t_ref.shape[0] // wide
     high, low = split_pair(gathered_gradient(own_ref, got, inv_ref, loss_out))
     rest = high.shape[0] - LANES
@@ -323,7 +323,7 @@
             jax.ShapeDtypeStruct((spread * rows, images), BF16),
             jax.ShapeDtypeStruct((group // 2, share + 8, images), F32),
         ]
-        + [jax.ShapeDtypeStruct((group // 4, share + STAT_ROWS, images), BF16)] * 2,
+        + [jax.ShapeDtypeStruct((count, share + STAT_ROWS, images), BF16) for count in (group // 2 - 1, 1)],
         scratch_shapes=[
             pltpu.VMEM((width, images), F32),
             pltpu.VMEM((width, images), F32),
@@ -334,7 +334,6 @@
     )(member, scalars, proj_weight, own_half, own_proj, got_half, text_emb)
     all_feats, inv_part, img_emb, grad_tile, own_part, near_part, far_part = results
     got_far = swapped(far_part, total, 1)
-    got_near = swapped(near_part, total, 1)
     feats_t, own_text, *sent_text = pl.pallas_call(
         functools.partial(caption_kernel, rows),
         in_specs=[VMEM] * 3,
@@ -347,35 +346,37 @@
     own_part, got_far, sent_text = lax.optimization_barrier((own_part, got_far, sent_text))
     sent_block = jax.ShapeDtypeStruct((share + STAT_ROWS, images), BF16)
     kept_block = jax.ShapeDtypeStruct((share + 8, images), F32)
-    half = group // 4
+    last = group // 2 - 1
     far = pl.pallas_call(
-        functools.partial(chip_kernel, half),
+        functools.partial(chip_kernel, last),
         in_specs=[VMEM] * 2,
-        out_specs=[VMEM] * half,
-        out_shape=[sent_block] * half,
+        out_specs=VMEM,
+        out_shape=sent_block,
         compiler_params=limit(8),
         name="chip_far",
     )(own_part, got_far)
-    far = [swapped(value, total, 2 * (half + index)) for index, value in enumerate(far)]
+    far, near_part = lax.optimization_barrier((far, near_part))
+    far = swapped(far, total, 2 * last)
+    got_near = swapped(near_part, total, 1)
     got_text = [swapped(value, total, step * group) for step, value in enumerate(sent_text, 1)]
     own_part, *near = pl.pallas_call(
         functools.partial(chip_kernel, 0),
         in_specs=[VMEM] * 2,
-        out_specs=[VMEM] * half,
-        out_shape=[kept_block] + [sent_block] * (half - 1),
+        out_specs=[VMEM] * last,
+        out_shape=[kept_block] + [sent_block] * (last - 1),
         compiler_params=limit(8),
         name="chip_near",
     )(own_part, got_near)
     near = [swapped(value, total, 2 * index) for index, value in enumerate(near, 1)]
     own_part = pl.pallas_call(
         far_sum_kernel,
-        in_specs=[VMEM] * (1 + half),
+        in_specs=[VMEM] * 2,
         out_specs=VMEM,
         out_shape=kept_block,
         compiler_params=limit(8),
         cost_estimate=hint(5 * 10**8),
         name="far_sum",
-    )(own_part, *far)
+    )(own_part, far)
 
     out_rows = width // wide
     rest = share - LANES
@@ -384,7 +385,7 @@
     if direct:
         loss_line, sent_weight = pl.pallas_call(
             functools.partial(weight_kernel, group, wide),
-            in_specs=[VMEM] * (3 + group // 4),
+            in_specs=[VMEM] * (2 + group // 2),
             out_specs=[VMEM] * 2,
             out_shape=[
                 jax.ShapeDtypeStruct((1, images), F32),
@@ -405,13 +406,13 @@
     else:
 
         def gradient_kernel(*refs):
-            own_ref, blocks = refs[0], refs[1 : group // 4]
-            inv_ref, loss_out, d_out = refs[group // 4 :]
+            own_ref, blocks = refs[0], refs[1 : group // 2 - 1]
+            inv_ref, loss_out, d_out = refs[group // 2 - 1 :]
             d_out[...] = gathered_gradient(own_ref, blocks, inv_ref, loss_out)
 
         loss_line, d_zproj = pl.pallas_call(
             gradient_kernel,
-            in_specs=[VMEM] * (1 + group // 4),
+            in_specs=[VMEM] * (group // 2),
             out_specs=[VMEM] * 2,
             out_shape=[jax.ShapeDtypeStruct((1, images), F32), jax.ShapeDtypeStruct((share, images), F32)],
             compiler_params=limit(12),

time: 49.4 us -> 50.2 us (1.016)
  starting transfers between devices: 21.5 us -> 23.2 us
  waiting for transfers between devices: 14.8 us -> 13.9 us
    ppermute x15, starting transfers between devices: 16.9 us -> 18.6 us  [swapped(): lax.ppermute(value, AXES, [(source, source ^ mask) for source in range(to...]
    ppermute x15, waiting for transfers between devices: 5.81 us -> 5.15 us  [swapped(): lax.ppermute(value, AXES, [(source, source ^ mask) for source in range(to...]
  transfers between devices with their start and end apart: 16 -> 16, of which waited for: 6 -> 4; matrix products, arithmetic and copies ran while one was open for 1% -> 1% of each run, Pallas kernels for 8% -> 8%
where the time goes in v22:
time: 50.2 us; the launch traced here: 49.9 us
  starting transfers between devices  23.2 us (46%)
  waiting for transfers between devices  13.9 us (28%)
  Pallas kernels  7.68 us (15%)
  local copies, waits for them, and re-layouts  2.98 us (6%)
  between operations  2.07 us (4%)
    ppermute x15, starting transfers between devices, swapped(): lax.ppermute(value, AXES, [(source, source ^ mask) for source in range(to...  18.6 us
    all_to_all x1, waiting for transfers between devices, local(): got_weight = lax.all_to_all(sent_weight, AXES[:2], 0, 0)  8.77 us
    ppermute x15, waiting for transfers between devices, swapped(): lax.ppermute(value, AXES, [(source, source ^ mask) for source in range(to...  5.15 us
    all_to_all x1, starting transfers between devices, local(): got_weight = lax.all_to_all(sent_weight, AXES[:2], 0, 0)  4.65 us
    pallas_call x1, Pallas kernels, local(): pl.pallas_call(functools.partial(pair_kernel, narrow, group), in_specs=[S...  2.89 us
    unnamed x6, local copies, waits for them, and re-layouts  2.4 us
    pallas_call x1, Pallas kernels, local(): pl.pallas_call(functools.partial(weight_kernel, group, wide), in_specs=[V...  1.39 us
  transfers between devices with their start and end apart: 16, of which 4 were waited for; matrix products, arithmetic and copies ran while one was open for 1% of the time, Pallas kernels for 8%

profile of v22, /device:TPU:0, one launch (start us, length us, event | category | flops | bytes accessed | tf_op | source)
XLA Modules:
  0.0 49.9 jit_solution(3225954480494952853)
XLA Ops:
  0.6 3.0 %collective-permute-start = (bf16[48,1152]{1,0:T(8,128)(2,1)}, bf16[48,1152]{1,0:T(8,128)(2,1)S(1)}, u32[]{:S(2)}, u32[]{:S(2)}) collective-permute-start(bf16[48,1152]{1,0:T(8,128)(2,1)} %refs_0_.1), channel_id=1, source_target_pairs={{0,2},{1,3},{2,0},{3,1},{4,6},{5,7},{6,4},{7,5},{8,10},{9,11},{10,... | collective-permute-start | bytes 331784 | tf_op jit(solution)/shard_map/ppermute | solution.py:31
  3.7 1.5 %collective-permute-start.1 = (bf16[48,1152]{1,0:T(8,128)(2,1)}, bf16[48,1152]{1,0:T(8,128)(2,1)S(1)}, u32[]{:S(2)}, u32[]{:S(2)}) collective-permute-start(bf16[48,1152]{1,0:T(8,128)(2,1)} %refs_0_.1), channel_id=1, source_target_pairs={{0,4},{1,5},{2,6},{3,7},{4,0},{5,1},{6,2},{7,3},{8,12},{9,13},{10,... | collective-permute-start | bytes 331784 | tf_op jit(solution)/shard_map/ppermute | solution.py:31
  5.2 4.0 %collective-permute-start.3 = (bf16[48,1152]{1,0:T(8,128)(2,1)}, bf16[48,1152]{1,0:T(8,128)(2,1)S(1)}, u32[]{:S(2)}, u32[]{:S(2)}) collective-permute-start(bf16[48,1152]{1,0:T(8,128)(2,1)} %text_ref.1), channel_id=1, source_target_pairs={{0,24},{1,25},{2,26},{3,27},{4,28},{5,29},{6,30},{7,31},{8,16},{9,... | collective-permute-start | bytes 331784 | tf_op jit(solution)/shard_map/ppermute | solution.py:31
  10.6 0.6 %collective-permute-start.5 = (bf16[48,1152]{1,0:T(8,128)(2,1)}, bf16[48,1152]{1,0:T(8,128)(2,1)S(1)}, u32[]{:S(2)}, u32[]{:S(2)}) collective-permute-start(bf16[48,1152]{1,0:T(8,128)(2,1)} %text_ref.1), channel_id=1, source_target_pairs={{0,8},{1,9},{2,10},{3,11},{4,12},{5,13},{6,14},{7,15},{8,0},{9,1},... | collective-permute-start | bytes 331784 | tf_op jit(solution)/shard_map/ppermute | solution.py:31
  11.2 0.9 %copy-done.2 = bf16[48,1152]{1,0:T(8,128)(2,1)S(1)} copy-done((bf16[48,1152]{1,0:T(8,128)(2,1)S(1)}, bf16[48,1152]{1,0:T(8,128)(2,1)}, u32[]{:S(2)}) %copy-start.2) | copy-done | bytes 110616
  12.4 1.5 %copy-done = bf16[1152,1152]{1,0:T(8,128)(2,1)S(1)} copy-done((bf16[1152,1152]{1,0:T(8,128)(2,1)S(1)}, bf16[1152,1152]{1,0:T(8,128)(2,1)}, u32[]{:S(2)}) %copy-start) | copy-done | bytes 2654232
  13.9 0.8 %own_projection.1.own_proj = f32[192,1152]{1,0:T(8,128)S(1)} custom-call(bf16[192,1152]{1,0:T(8,128)(2,1)S(1)} %stack.1.feats_ref.own_half, bf16[1152,1152]{1,0:T(8,128)(2,1)S(1)} %copy-done), custom_call_target="tpu_custom_call" | custom-call | tf_op jit(solution)/shard_map/own_projection/pallas_call | solution.py:296
  14.7 3.3 %collective-permute-done.4.refs_2_ = bf16[48,1152]{1,0:T(8,128)(2,1)S(1)} collective-permute-done((bf16[48,1152]{1,0:T(8,128)(2,1)}, bf16[48,1152]{1,0:T(8,128)(2,1)S(1)}, u32[]{:S(2)}, u32[]{:S(2)}) %collective-permute-start.4) | collective-permute-done | bytes 110624 | tf_op jit(solution)/shard_map/ppermute | solution.py:31
  18.1 2.9 %pairs.1 = (bf16[384,1152]{1,0:T(8,128)(2,1)S(1)}, f32[1,384]{1,0:T(1,128)S(1)}, bf16[1152,384]{1,0:T(8,128)(2,1)S(1)}, bf16[192,384]{1,0:T(8,128)(2,1)S(1)}, f3...) custom-call(s32[1]{0:T(128)} %bitcast.member_ref, ...), custom_call_target="tpu_custom_call" | custom-call | tf_op jit(solution)/shard_map/pairs/pallas_call | solution.py:315
  21.1 0.5 %captions.1 = (bf16[1152,384]{1,0:T(8,128)(2,1)S(1)}, f32[48,1152]{1,0:T(8,128)S(1)}, bf16[48,1152]{1,0:T(8,128)(2,1)S(1)}, bf16[48,1152]{1,0:T(8,128)(2,1)S(1)}, bf16[48,1152]{1,0:T(8,128)(2,1)S(1)}) custom-call(bf16[192,384]{1,0:T(8,128)(2,1)S(1)} %get-tuple-element.41.grad_ref, bf16[1152,384]{1,0:T(8,128)(2,1)S(1)} %get-tuple-element.42.emb_ref, ...), custom_call_target="tpu_custom_call" | custom-call | tf_op jit(solution)/shard_map/captions/pallas_call | solution.py:337
  21.6 0.8 %collective-permute-done.7.got_ref = bf16[1,160,384]{2,1,0:T(8,128)(2,1)S(1)} collective-permute-done((bf16[1,160,384]{2,1,0:T(8,128)(2,1)S(1)}, bf16[1,160,384]{2,1,0:T(8,128)(2,1)S(1)}, u32[]{:S(2)}, u32[]{:S(2)}) %collective-permute-start.7) | collective-permute-done | bytes 122912 | tf_op jit(solution)/shard_map/ppermute | solution.py:31
  22.5 0.2 collective-permute-start.8
  22.7 2.5 %collective-permute-start.9 = (bf16[160,384]{1,0:T(8,128)(2,1)S(1)}, bf16[160,384]{1,0:T(8,128)(2,1)S(1)}, u32[]{:S(2)}, u32[]{:S(2)}) collective-permute-start(bf16[160,384]{1,0:T(8,128)(2,1)S(1)} %chip_far.1), channel_id=1, source_target_pairs={{0,6},{1,7},{2,4},{3,5},{4,2},{5,3},{6,0},{7,1},{8,14},{9,15},{10,... | collective-permute-start | bytes 368648 | tf_op jit(solution)/shard_map/ppermute | solution.py:31
  25.2 0.7 %collective-permute-start.10 = (bf16[160,384]{1,0:T(8,128)(2,1)S(1)}, bf16[160,384]{1,0:T(8,128)(2,1)S(1)}, u32[]{:S(2)}, u32[]{:S(2)}) collective-permute-start(bf16[160,384]{1,0:T(8,128)(2,1)S(1)} %get-tuple-element.53), channel_id=1, source_target_pairs={{0,2},{1,3},{2,0},{3,1},{4,6},{5,7},{6,4},{7,5},{8,10},{9,11},{10,... | collective-permute-start | bytes 368648 | tf_op jit(solution)/shard_map/ppermute | solution.py:31
  25.9 1.5 %collective-permute-start.11 = (bf16[160,384]{1,0:T(8,128)(2,1)S(1)}, bf16[160,384]{1,0:T(8,128)(2,1)S(1)}, u32[]{:S(2)}, u32[]{:S(2)}) collective-permute-start(bf16[160,384]{1,0:T(8,128)(2,1)S(1)} %get-tuple-element.54), channel_id=1, source_target_pairs={{0,4},{1,5},{2,6},{3,7},{4,0},{5,1},{6,2},{7,3},{8,12},{9,13},{10,... | collective-permute-start | bytes 368648 | tf_op jit(solution)/shard_map/ppermute | solution.py:31
  27.4 2.5 %collective-permute-start.12 = (bf16[48,1152]{1,0:T(8,128)(2,1)S(1)}, bf16[48,1152]{1,0:T(8,128)(2,1)S(1)}, u32[]{:S(2)}, u32[]{:S(2)}) collective-permute-start(bf16[48,1152]{1,0:T(8,128)(2,1)S(1)} %get-tuple-element.59), channel_id=1, source_target_pairs={{0,24},{1,25},{2,26},{3,27},{4,28},{5,29},{6,30},{7,31},{8,16},{9,... | collective-permute-start | bytes 331784 | tf_op jit(solution)/shard_map/ppermute | solution.py:31
  29.8 1.9 %collective-permute-start.14 = (bf16[48,1152]{1,0:T(8,128)(2,1)S(1)}, bf16[48,1152]{1,0:T(8,128)(2,1)S(1)}, u32[]{:S(2)}, u32[]{:S(2)}) collective-permute-start(bf16[48,1152]{1,0:T(8,128)(2,1)S(1)} %get-tuple-element.61), channel_id=1, source_target_pairs={{0,8},{1,9},{2,10},{3,11},{4,12},{5,13},{6,14},{7,15},{8,0},{9,1},... | collective-permute-start | bytes 331784 | tf_op jit(solution)/shard_map/ppermute | solution.py:31
  31.9 1.4 %weights.1 = (f32[1,384]{1,0:T(1,128)S(1)}, bf16[8,176,128]{2,1,0:T(8,128)(2,1)}) custom-call(f32[152,384]{1,0:T(8,128)S(1)} %far_sum.1.refs_0_, bf16[160,384]{1,0:T(8,128)(2,1)S(1)} %collective-permute-done.10.refs_1_, bf16[160,384]{1,0:T(8,128)(2,1)S(1)} %collective-permute-done.11.refs_2_, f32[1,384]{1,0:T(1,128)S(1)} %get-tuple-element.55.refs_3_, ...), custom_call_target="tpu_custom_call" | custom-call | tf_op jit(solution)/shard_map/weights/pallas_call | solution.py:386
  33.2 4.7 %all-to-all-start = ((bf16[8,176,128]{2,1,0:T(8,128)(2,1)}), bf16[8,176,128]{2,1,0:T(8,128)(2,1)S(1)}, u32[]{:S(2)}, u32[]{:S(2)}) async-start(bf16[8,176,128]{2,1,0:T(8,128)(2,1)} %get-tuple-element.62), calls=%async_computation | async-start | bytes 720896 | tf_op jit(solution)/shard_map/all_to_all | solution.py:397
  37.9 1.0 %collective-permute-done.13.refs_2_ = bf16[48,1152]{1,0:T(8,128)(2,1)S(1)} collective-permute-done((bf16[48,1152]{1,0:T(8,128)(2,1)S(1)}, bf16[48,1152]{1,0:T(8,128)(2,1)S(1)}, u32[]{:S(2)}, u32[]{:S(2)}) %collective-permute-start.13) | collective-permute-done | bytes 110624 | tf_op jit(solution)/shard_map/ppermute | solution.py:31
  38.9 0.7 %caption_total.1 = f32[48,1152]{1,0:T(8,128)} custom-call(f32[48,1152]{1,0:T(8,128)S(1)} %get-tuple-element.58.refs_0_, bf16[48,1152]{1,0:T(8,128)(2,1)S(1)} %collective-permute-done.12.refs_1_, bf16[48,1152]{1,0:T(8,128)(2,1)S(1)} %collective-permute-done.13.refs_2_, bf16[48,1152]{1,0:T(8,128)(2,1)S(1)} %collective-permute-done.14.refs_3_), custom_call_target="tpu_custom_call" | custom-call | flops 5000000000 | tf_op jit(solution)/shard_map/caption_total/pallas_call | solution.py:428
  39.7 0.6 %dynamic-slice_bitcast_fusion = f32[48]{0:T(128)} fusion(f32[1,384]{1,0:T(1,128)S(1)} %get-tuple-element.57, s32[]{:T(128)S(6)} %select_n.16), kind=kLoop, calls=%fused_computation | loop fusion | bytes 388 | tf_op jit(solution)/shard_map/dynamic_slice | solution.py:437
  40.2 8.8 %all-to-all-done.got_ref = bf16[8,176,128]{2,1,0:T(8,128)(2,1)S(1)} async-done(((bf16[8,176,128]{2,1,0:T(8,128)(2,1)}), bf16[8,176,128]{2,1,0:T(8,128)(2,1)S(1)}, u32[]{:S(2)}, u32[]{:S(2)}) %all-to-all-start) | async-done | bytes 360480 | tf_op jit(solution)/shard_map/all_to_all | solution.py:397
  49.0 0.9 %weight_total.1 = f32[144,288]{1,0:T(8,128)} custom-call(bf16[8,176,128]{2,1,0:T(8,128)(2,1)S(1)} %all-to-all-done.got_ref), custom_call_target="tpu_custom_call" | custom-call | tf_op jit(solution)/shard_map/weight_total/pallas_call | solution.py:398
  (27 shorter events, 0.7 us)
Async XLA Ops:
  0.6 9.9 %collective-permute-start = (bf16[48,1152]{1,0:T(8,128)(2,1)}, bf16[48,1152]{1,0:T(8,128)(2,1)S(1)}, u32[]{:S(2)}, u32[]{:S(2)}) collective-permute-start(bf16[48,1152]{1,0:T(8,128)(2,1)} %refs_0_.1), channel_id=1, source_target_pairs={{0,2},{1,3},{2,0},{3,1},{4,6},{5,7},{6,4},{7,5},{8,10},{9,11},{10,... | collective-permute-start | bytes 331784 | tf_op jit(solution)/shard_map/ppermute | solution.py:31
  3.7 8.6 %collective-permute-start.1 = (bf16[48,1152]{1,0:T(8,128)(2,1)}, bf16[48,1152]{1,0:T(8,128)(2,1)S(1)}, u32[]{:S(2)}, u32[]{:S(2)}) collective-permute-start(bf16[48,1152]{1,0:T(8,128)(2,1)} %refs_0_.1), channel_id=1, source_target_pairs={{0,4},{1,5},{2,6},{3,7},{4,0},{5,1},{6,2},{7,3},{8,12},{9,13},{10,... | collective-permute-start | bytes 331784 | tf_op jit(solution)/shard_map/ppermute | solution.py:31
  5.2 7.1 %collective-permute-start.2 = (bf16[48,1152]{1,0:T(8,128)(2,1)}, bf16[48,1152]{1,0:T(8,128)(2,1)S(1)}, u32[]{:S(2)}, u32[]{:S(2)}) collective-permute-start(bf16[48,1152]{1,0:T(8,128)(2,1)} %refs_0_.1), channel_id=1, source_target_pairs={{0,6},{1,7},{2,4},{3,5},{4,2},{5,3},{6,0},{7,1},{8,14},{9,15},{10,... | collective-permute-start | bytes 331784 | tf_op jit(solution)/shard_map/ppermute | solution.py:31
  5.2 9.5 %collective-permute-start.3 = (bf16[48,1152]{1,0:T(8,128)(2,1)}, bf16[48,1152]{1,0:T(8,128)(2,1)S(1)}, u32[]{:S(2)}, u32[]{:S(2)}) collective-permute-start(bf16[48,1152]{1,0:T(8,128)(2,1)} %text_ref.1), channel_id=1, source_target_pairs={{0,24},{1,25},{2,26},{3,27},{4,28},{5,29},{6,30},{7,31},{8,16},{9,... | collective-permute-start | bytes 331784 | tf_op jit(solution)/shard_map/ppermute | solution.py:31
  9.2 8.7 %collective-permute-start.4 = (bf16[48,1152]{1,0:T(8,128)(2,1)}, bf16[48,1152]{1,0:T(8,128)(2,1)S(1)}, u32[]{:S(2)}, u32[]{:S(2)}) collective-permute-start(bf16[48,1152]{1,0:T(8,128)(2,1)} %text_ref.1), channel_id=1, source_target_pairs={{0,16},{1,17},{2,18},{3,19},{4,20},{5,21},{6,22},{7,23},{8,24},{9,... | collective-permute-start | bytes 331784 | tf_op jit(solution)/shard_map/ppermute | solution.py:31
  10.5 1.7 %copy-start.1 = (bf16[48,1152]{1,0:T(8,128)(2,1)S(1)}, bf16[48,1152]{1,0:T(8,128)(2,1)}, u32[]{:S(2)}) copy-start(bf16[48,1152]{1,0:T(8,128)(2,1)} %refs_0_.1) | copy-start | bytes 331780
  10.6 7.4 %collective-permute-start.5 = (bf16[48,1152]{1,0:T(8,128)(2,1)}, bf16[48,1152]{1,0:T(8,128)(2,1)S(1)}, u32[]{:S(2)}, u32[]{:S(2)}) collective-permute-start(bf16[48,1152]{1,0:T(8,128)(2,1)} %text_ref.1), channel_id=1, source_target_pairs={{0,8},{1,9},{2,10},{3,11},{4,12},{5,13},{6,14},{7,15},{8,0},{9,1},... | collective-permute-start | bytes 331784 | tf_op jit(solution)/shard_map/ppermute | solution.py:31
  11.2 0.9 %copy-start.2 = (bf16[48,1152]{1,0:T(8,128)(2,1)S(1)}, bf16[48,1152]{1,0:T(8,128)(2,1)}, u32[]{:S(2)}) copy-start(bf16[48,1152]{1,0:T(8,128)(2,1)} %text_ref.1) | copy-start | bytes 331780
  12.1 1.7 %copy-start = (bf16[1152,1152]{1,0:T(8,128)(2,1)S(1)}, bf16[1152,1152]{1,0:T(8,128)(2,1)}, u32[]{:S(2)}) copy-start(bf16[1152,1152]{1,0:T(8,128)(2,1)} %weight.1) | copy-start | bytes 7962628
  12.3 5.8 %collective-permute-start.6 = (bf16[192,1152]{1,0:T(8,128)(2,1)S(1)}, bf16[192,1152]{1,0:T(8,128)(2,1)S(1)}, u32[]{:S(2)}, u32[]{:S(2)}) collective-permute-start(bf16[192,1152]{1,0:T(8,128)(2,1)S(1)} %stack.1.feats_ref.own_half), channel_id=1, source_target_pairs={{0,1},{1,0},{2,3},{3,2},{4,5},{5,4},{6,7},{7,6},{8,9},{9,8},{10,11... | collective-permute-start | bytes 1327112 | tf_op jit(solution)/shard_map/ppermute | solution.py:31
  21.0 1.4 %collective-permute-start.7 = (bf16[1,160,384]{2,1,0:T(8,128)(2,1)S(1)}, bf16[1,160,384]{2,1,0:T(8,128)(2,1)S(1)}, u32[]{:S(2)}, u32[]{:S(2)}) collective-permute-start(bf16[1,160,384]{2,1,0:T(8,128)(2,1)S(1)} %get-tuple-element.40), channel_id=1, source_target_pairs={{0,1},{1,0},{2,3},{3,2},{4,5},{5,4},{6,7},{7,6},{8,9},{9,8},{10,11... | collective-permute-start | bytes 368648 | tf_op jit(solution)/shard_map/ppermute | solution.py:31
  22.5 2.7 %collective-permute-start.8 = (bf16[3,160,384]{2,1,0:T(8,128)(2,1)S(1)}, bf16[3,160,384]{2,1,0:T(8,128)(2,1)S(1)}, u32[]{:S(2)}, u32[]{:S(2)}) collective-permute-start(bf16[3,160,384]{2,1,0:T(8,128)(2,1)S(1)} %get-tuple-element.50), channel_id=1, source_target_pairs={{0,1},{1,0},{2,3},{3,2},{4,5},{5,4},{6,7},{7,6},{8,9},{9,8},{10,11... | collective-permute-start | bytes 1105928 | tf_op jit(solution)/shard_map/ppermute | solution.py:31
  22.7 7.2 %collective-permute-start.9 = (bf16[160,384]{1,0:T(8,128)(2,1)S(1)}, bf16[160,384]{1,0:T(8,128)(2,1)S(1)}, u32[]{:S(2)}, u32[]{:S(2)}) collective-permute-start(bf16[160,384]{1,0:T(8,128)(2,1)S(1)} %chip_far.1), channel_id=1, source_target_pairs={{0,6},{1,7},{2,4},{3,5},{4,2},{5,3},{6,0},{7,1},{8,14},{9,15},{10,... | collective-permute-start | bytes 368648 | tf_op jit(solution)/shard_map/ppermute | solution.py:31
  25.2 6.6 %collective-permute-start.10 = (bf16[160,384]{1,0:T(8,128)(2,1)S(1)}, bf16[160,384]{1,0:T(8,128)(2,1)S(1)}, u32[]{:S(2)}, u32[]{:S(2)}) collective-permute-start(bf16[160,384]{1,0:T(8,128)(2,1)S(1)} %get-tuple-element.53), channel_id=1, source_target_pairs={{0,2},{1,3},{2,0},{3,1},{4,6},{5,7},{6,4},{7,5},{8,10},{9,11},{10,... | collective-permute-start | bytes 368648 | tf_op jit(solution)/shard_map/ppermute | solution.py:31
  25.9 6.0 %collective-permute-start.11 = (bf16[160,384]{1,0:T(8,128)(2,1)S(1)}, bf16[160,384]{1,0:T(8,128)(2,1)S(1)}, u32[]{:S(2)}, u32[]{:S(2)}) collective-permute-start(bf16[160,384]{1,0:T(8,128)(2,1)S(1)} %get-tuple-element.54), channel_id=1, source_target_pairs={{0,4},{1,5},{2,6},{3,7},{4,0},{5,1},{6,2},{7,3},{8,12},{9,13},{10,... | collective-permute-start | bytes 368648 | tf_op jit(solution)/shard_map/ppermute | solution.py:31
  27.4 10.5 %collective-permute-start.12 = (bf16[48,1152]{1,0:T(8,128)(2,1)S(1)}, bf16[48,1152]{1,0:T(8,128)(2,1)S(1)}, u32[]{:S(2)}, u32[]{:S(2)}) collective-permute-start(bf16[48,1152]{1,0:T(8,128)(2,1)S(1)} %get-tuple-element.59), channel_id=1, source_target_pairs={{0,24},{1,25},{2,26},{3,27},{4,28},{5,29},{6,30},{7,31},{8,16},{9,... | collective-permute-start | bytes 331784 | tf_op jit(solution)/shard_map/ppermute | solution.py:31
  29.8 9.1 %collective-permute-start.13 = (bf16[48,1152]{1,0:T(8,128)(2,1)S(1)}, bf16[48,1152]{1,0:T(8,128)(2,1)S(1)}, u32[]{:S(2)}, u32[]{:S(2)}) collective-permute-start(bf16[48,1152]{1,0:T(8,128)(2,1)S(1)} %get-tuple-element.60), channel_id=1, source_target_pairs={{0,16},{1,17},{2,18},{3,19},{4,20},{5,21},{6,22},{7,23},{8,24},{9,... | collective-permute-start | bytes 331784 | tf_op jit(solution)/shard_map/ppermute | solution.py:31
  29.8 9.1 %collective-permute-start.14 = (bf16[48,1152]{1,0:T(8,128)(2,1)S(1)}, bf16[48,1152]{1,0:T(8,128)(2,1)S(1)}, u32[]{:S(2)}, u32[]{:S(2)}) collective-permute-start(bf16[48,1152]{1,0:T(8,128)(2,1)S(1)} %get-tuple-element.61), channel_id=1, source_target_pairs={{0,8},{1,9},{2,10},{3,11},{4,12},{5,13},{6,14},{7,15},{8,0},{9,1},... | collective-permute-start | bytes 331784 | tf_op jit(solution)/shard_map/ppermute | solution.py:31
  33.2 15.8 %all-to-all-start = ((bf16[8,176,128]{2,1,0:T(8,128)(2,1)}), bf16[8,176,128]{2,1,0:T(8,128)(2,1)S(1)}, u32[]{:S(2)}, u32[]{:S(2)}) async-start(bf16[8,176,128]{2,1,0:T(8,128)(2,1)} %get-tuple-element.62), calls=%async_computation | async-start | bytes 720896 | tf_op jit(solution)/shard_map/all_to_all | solution.py:397

commit v23 on v19

--- a/solution.py
+++ b/solution.py
@@ -227,7 +227,7 @@
 
 def weight_kernel(group, wide, *refs):
     own_ref, got = refs[0], refs[1 : group // 4]
-    inv_ref, feats_ref, feats_t_ref, loss_out, send_out = refs[group // 4 :]
+    inv_ref, feats_ref, feats_t_ref, loss_out, send_out, blocks, sems = refs[group // 4 :]
     rows = feats_t_ref.shape[0] // wide
     high, low = split_pair(gathered_gradient(own_ref, got, inv_ref, loss_out))
     rest = high.shape[0] - LANES
@@ -235,14 +235,23 @@
     tail = jnp.dot(both, feats_ref[...], preferred_element_type=F32)
     tail = (tail[:rest, :] + tail[rest:, :]).astype(BF16)
     both = jnp.concatenate([high[:LANES, :], low[:LANES, :]], axis=0)
-    main = lax.dot_general(feats_t_ref[...], both, NT, preferred_element_type=F32)
-    main = (main[:, :LANES] + main[:, LANES:]).astype(BF16)
-    for place in range(wide):
-        begin = place * rows
-        send_out[place, :rows, :] = main[begin : begin + rows, :]
-        send_out[place, rows : rows + rest, :] = tail[:, begin : begin + LANES]
-        send_out[place, rows + rest :, :] = jnp.zeros((rest, LANES), BF16)
-        send_out[place, rows + rest :, : rows - LANES] = tail[:, begin + LANES : begin + rows]
+    half = wide // 2
+    copies = []
+    for part in range(2):
+        lines = slice(part * half * rows, (part + 1) * half * rows)
+        main = lax.dot_general(feats_t_ref[lines, :], both, NT, preferred_element_type=F32)
+        main = (main[:, :LANES] + main[:, LANES:]).astype(BF16)
+        for index in range(half):
+            place, begin = part * half + index, (part * half + index) * rows
+            blocks[place, :rows, :] = main[index * rows : (index + 1) * rows, :]
+            blocks[place, rows : rows + rest, :] = tail[:, begin : begin + LANES]
+            blocks[place, rows + rest :, :] = jnp.zeros((rest, LANES), BF16)
+            blocks[place, rows + rest :, : rows - LANES] = tail[:, begin + LANES : begin + rows]
+        places = pl.ds(part * half, half)
+        copies.append(pltpu.make_async_copy(blocks.at[places], send_out.at[places], sems.at[part]))
+        copies[-1].start()
+    for copy in copies:
+        copy.wait()
 
 
 def total_kernel(rest, got_ref, out):
@@ -385,11 +394,12 @@
         loss_line, sent_weight = pl.pallas_call(
             functools.partial(weight_kernel, group, wide),
             in_specs=[VMEM] * (3 + group // 4),
-            out_specs=[VMEM] * 2,
+            out_specs=[VMEM, pl.BlockSpec(memory_space=pl.ANY)],
             out_shape=[
                 jax.ShapeDtypeStruct((1, images), F32),
                 jax.ShapeDtypeStruct((wide, packed, LANES), BF16),
             ],
+            scratch_shapes=[pltpu.VMEM((wide, packed, LANES), BF16), pltpu.SemaphoreType.DMA((2,))],
             compiler_params=limit(12),
             name="weights",
         )(own_part, *near, inv_part, all_feats, feats_t)

time: 49.4 us -> 49.4 us (level)
  transfers between devices with their start and end apart: 16 -> 16, of which waited for: 6 -> 5; matrix products, arithmetic and copies ran while one was open for 1% -> 1% of each run, Pallas kernels for 8% -> 8%
where the time goes in v23:
time: 49.4 us; the launch traced here: 49.1 us
  starting transfers between devices  21.6 us (44%)
  waiting for transfers between devices  14.8 us (30%)
  Pallas kernels  7.71 us (16%)
  local copies, waits for them, and re-layouts  2.98 us (6%)
  between operations  2.08 us (4%)
    ppermute x15, starting transfers between devices, swapped(): lax.ppermute(value, AXES, [(source, source ^ mask) for source in range(to...  16.9 us
    all_to_all x1, waiting for transfers between devices, local(): got_weight = lax.all_to_all(sent_weight, AXES[:2], 0, 0)  9.08 us
    ppermute x15, waiting for transfers between devices, swapped(): lax.ppermute(value, AXES, [(source, source ^ mask) for source in range(to...  5.75 us
    all_to_all x1, starting transfers between devices, local(): got_weight = lax.all_to_all(sent_weight, AXES[:2], 0, 0)  4.67 us
    pallas_call x1, Pallas kernels, local(): pl.pallas_call(functools.partial(pair_kernel, narrow, group), in_specs=[S...  2.89 us
    unnamed x6, local copies, waits for them, and re-layouts  2.4 us
    pallas_call x1, Pallas kernels, local(): pl.pallas_call(functools.partial(weight_kernel, group, wide), in_specs=[V...  1.41 us
  transfers between devices with their start and end apart: 16, of which 5 were waited for; matrix products, arithmetic and copies ran while one was open for 1% of the time, Pallas kernels for 8%

profile of v23, /device:TPU:0, one launch (start us, length us, event | category | flops | bytes accessed | tf_op | source)
XLA Modules:
  0.0 49.1 jit_solution(15560919182388358384)
XLA Ops:
  0.6 3.0 %collective-permute-start = (bf16[48,1152]{1,0:T(8,128)(2,1)}, bf16[48,1152]{1,0:T(8,128)(2,1)S(1)}, u32[]{:S(2)}, u32[]{:S(2)}) collective-permute-start(bf16[48,1152]{1,0:T(8,128)(2,1)} %refs_0_.1), channel_id=1, source_target_pairs={{0,2},{1,3},{2,0},{3,1},{4,6},{5,7},{6,4},{7,5},{8,10},{9,11},{10,... | collective-permute-start | bytes 331784 | tf_op jit(solution)/shard_map/ppermute | solution.py:31
  3.7 1.5 %collective-permute-start.1 = (bf16[48,1152]{1,0:T(8,128)(2,1)}, bf16[48,1152]{1,0:T(8,128)(2,1)S(1)}, u32[]{:S(2)}, u32[]{:S(2)}) collective-permute-start(bf16[48,1152]{1,0:T(8,128)(2,1)} %refs_0_.1), channel_id=1, source_target_pairs={{0,4},{1,5},{2,6},{3,7},{4,0},{5,1},{6,2},{7,3},{8,12},{9,13},{10,... | collective-permute-start | bytes 331784 | tf_op jit(solution)/shard_map/ppermute | solution.py:31
  5.2 4.0 %collective-permute-start.3 = (bf16[48,1152]{1,0:T(8,128)(2,1)}, bf16[48,1152]{1,0:T(8,128)(2,1)S(1)}, u32[]{:S(2)}, u32[]{:S(2)}) collective-permute-start(bf16[48,1152]{1,0:T(8,128)(2,1)} %text_ref.1), channel_id=1, source_target_pairs={{0,24},{1,25},{2,26},{3,27},{4,28},{5,29},{6,30},{7,31},{8,16},{9,... | collective-permute-start | bytes 331784 | tf_op jit(solution)/shard_map/ppermute | solution.py:31
  10.6 0.6 %collective-permute-start.5 = (bf16[48,1152]{1,0:T(8,128)(2,1)}, bf16[48,1152]{1,0:T(8,128)(2,1)S(1)}, u32[]{:S(2)}, u32[]{:S(2)}) collective-permute-start(bf16[48,1152]{1,0:T(8,128)(2,1)} %text_ref.1), channel_id=1, source_target_pairs={{0,8},{1,9},{2,10},{3,11},{4,12},{5,13},{6,14},{7,15},{8,0},{9,1},... | collective-permute-start | bytes 331784 | tf_op jit(solution)/shard_map/ppermute | solution.py:31
  11.2 0.9 %copy-done.2 = bf16[48,1152]{1,0:T(8,128)(2,1)S(1)} copy-done((bf16[48,1152]{1,0:T(8,128)(2,1)S(1)}, bf16[48,1152]{1,0:T(8,128)(2,1)}, u32[]{:S(2)}) %copy-start.2) | copy-done | bytes 110616
  12.4 1.5 %copy-done = bf16[1152,1152]{1,0:T(8,128)(2,1)S(1)} copy-done((bf16[1152,1152]{1,0:T(8,128)(2,1)S(1)}, bf16[1152,1152]{1,0:T(8,128)(2,1)}, u32[]{:S(2)}) %copy-start) | copy-done | bytes 2654232
  13.9 0.8 %own_projection.1.own_proj = f32[192,1152]{1,0:T(8,128)S(1)} custom-call(bf16[192,1152]{1,0:T(8,128)(2,1)S(1)} %stack.1.feats_ref.own_half, bf16[1152,1152]{1,0:T(8,128)(2,1)S(1)} %copy-done), custom_call_target="tpu_custom_call" | custom-call | tf_op jit(solution)/shard_map/own_projection/pallas_call | solution.py:305
  14.7 3.3 %collective-permute-done.4.refs_2_ = bf16[48,1152]{1,0:T(8,128)(2,1)S(1)} collective-permute-done((bf16[48,1152]{1,0:T(8,128)(2,1)}, bf16[48,1152]{1,0:T(8,128)(2,1)S(1)}, u32[]{:S(2)}, u32[]{:S(2)}) %collective-permute-start.4) | collective-permute-done | bytes 110624 | tf_op jit(solution)/shard_map/ppermute | solution.py:31
  18.1 2.9 %pairs.1 = (bf16[384,1152]{1,0:T(8,128)(2,1)S(1)}, f32[1,384]{1,0:T(1,128)S(1)}, bf16[1152,384]{1,0:T(8,128)(2,1)S(1)}, bf16[192,384]{1,0:T(8,128)(2,1)S(1)}, f3...) custom-call(s32[1]{0:T(128)} %bitcast.member_ref, ...), custom_call_target="tpu_custom_call" | custom-call | tf_op jit(solution)/shard_map/pairs/pallas_call | solution.py:324
  21.1 0.5 %collective-permute-start.8 = (bf16[2,160,384]{2,1,0:T(8,128)(2,1)S(1)}, bf16[2,160,384]{2,1,0:T(8,128)(2,1)S(1)}, u32[]{:S(2)}, u32[]{:S(2)}) collective-permute-start(bf16[2,160,384]{2,1,0:T(8,128)(2,1)S(1)} %get-tuple-element.47), channel_id=1, source_target_pairs={{0,1},{1,0},{2,3},{3,2},{4,5},{5,4},{6,7},{7,6},{8,9},{9,8},{10,11... | collective-permute-start | bytes 737288 | tf_op jit(solution)/shard_map/ppermute | solution.py:31
  21.6 0.5 %captions.1 = (bf16[1152,384]{1,0:T(8,128)(2,1)S(1)}, f32[48,1152]{1,0:T(8,128)S(1)}, bf16[48,1152]{1,0:T(8,128)(2,1)S(1)}, bf16[48,1152]{1,0:T(8,128)(2,1)S(1)}, bf16[48,1152]{1,0:T(8,128)(2,1)S(1)}) custom-call(bf16[192,384]{1,0:T(8,128)(2,1)S(1)} %get-tuple-element.40.grad_ref, bf16[1152,384]{1,0:T(8,128)(2,1)S(1)} %get-tuple-element.41.emb_ref, ...), custom_call_target="tpu_custom_call" | custom-call | tf_op jit(solution)/shard_map/captions/pallas_call | solution.py:347
  22.7 2.5 %collective-permute-start.10 = (bf16[160,384]{1,0:T(8,128)(2,1)S(1)}, bf16[160,384]{1,0:T(8,128)(2,1)S(1)}, u32[]{:S(2)}, u32[]{:S(2)}) collective-permute-start(bf16[160,384]{1,0:T(8,128)(2,1)S(1)} %get-tuple-element.51), channel_id=1, source_target_pairs={{0,6},{1,7},{2,4},{3,5},{4,2},{5,3},{6,0},{7,1},{8,14},{9,15},{10,... | collective-permute-start | bytes 368648 | tf_op jit(solution)/shard_map/ppermute | solution.py:31
  25.2 0.5 %collective-permute-start.9 = (bf16[160,384]{1,0:T(8,128)(2,1)S(1)}, bf16[160,384]{1,0:T(8,128)(2,1)S(1)}, u32[]{:S(2)}, u32[]{:S(2)}) collective-permute-start(bf16[160,384]{1,0:T(8,128)(2,1)S(1)} %get-tuple-element.50), channel_id=1, source_target_pairs={{0,4},{1,5},{2,6},{3,7},{4,0},{5,1},{6,2},{7,3},{8,12},{9,13},{10,... | collective-permute-start | bytes 368648 | tf_op jit(solution)/shard_map/ppermute | solution.py:31
  25.8 0.6 %collective-permute-start.11 = (bf16[160,384]{1,0:T(8,128)(2,1)S(1)}, bf16[160,384]{1,0:T(8,128)(2,1)S(1)}, u32[]{:S(2)}, u32[]{:S(2)}) collective-permute-start(bf16[160,384]{1,0:T(8,128)(2,1)S(1)} %get-tuple-element.52), channel_id=1, source_target_pairs={{0,2},{1,3},{2,0},{3,1},{4,6},{5,7},{6,4},{7,5},{8,10},{9,11},{10,... | collective-permute-start | bytes 368648 | tf_op jit(solution)/shard_map/ppermute | solution.py:31
  26.3 2.4 %collective-permute-start.12 = (bf16[48,1152]{1,0:T(8,128)(2,1)S(1)}, bf16[48,1152]{1,0:T(8,128)(2,1)S(1)}, u32[]{:S(2)}, u32[]{:S(2)}) collective-permute-start(bf16[48,1152]{1,0:T(8,128)(2,1)S(1)} %get-tuple-element.57), channel_id=1, source_target_pairs={{0,24},{1,25},{2,26},{3,27},{4,28},{5,29},{6,30},{7,31},{8,16},{9,... | collective-permute-start | bytes 331784 | tf_op jit(solution)/shard_map/ppermute | solution.py:31
  28.8 1.0 %collective-permute-done.10.refs_2_ = bf16[160,384]{1,0:T(8,128)(2,1)S(1)} collective-permute-done((bf16[160,384]{1,0:T(8,128)(2,1)S(1)}, bf16[160,384]{1,0:T(8,128)(2,1)S(1)}, u32[]{:S(2)}, u32[]{:S(2)}) %collective-permute-start.10) | collective-permute-done | bytes 122912 | tf_op jit(solution)/shard_map/ppermute | solution.py:31
  29.8 1.0 %collective-permute-start.14 = (bf16[48,1152]{1,0:T(8,128)(2,1)S(1)}, bf16[48,1152]{1,0:T(8,128)(2,1)S(1)}, u32[]{:S(2)}, u32[]{:S(2)}) collective-permute-start(bf16[48,1152]{1,0:T(8,128)(2,1)S(1)} %get-tuple-element.59), channel_id=1, source_target_pairs={{0,8},{1,9},{2,10},{3,11},{4,12},{5,13},{6,14},{7,15},{8,0},{9,1},... | collective-permute-start | bytes 331784 | tf_op jit(solution)/shard_map/ppermute | solution.py:31
  30.7 0.9 %collective-permute-done.9.refs_1_ = bf16[160,384]{1,0:T(8,128)(2,1)S(1)} collective-permute-done((bf16[160,384]{1,0:T(8,128)(2,1)S(1)}, bf16[160,384]{1,0:T(8,128)(2,1)S(1)}, u32[]{:S(2)}, u32[]{:S(2)}) %collective-permute-start.9) | collective-permute-done | bytes 122912 | tf_op jit(solution)/shard_map/ppermute | solution.py:31
  31.7 1.4 %weights.1 = (f32[1,384]{1,0:T(1,128)S(1)}, bf16[8,176,128]{2,1,0:T(8,128)(2,1)}) custom-call(f32[152,384]{1,0:T(8,128)S(1)} %far_sum.1.refs_0_, bf16[160,384]{1,0:T(8,128)(2,1)S(1)} %collective-permute-done.11.refs_1_, f32[1,384]{1,0:T(1,128)S(1)} %get-tuple-element.53.refs_2_, bf16[384,1152]{1,0:T(8,128)(2,1)S(1)} %get-tuple-element.42.feats_ref.refs_3_, ...), custom_call_target="tpu_custom_call" | custom-call | tf_op jit(solution)/shard_map/weights/pallas_call | solution.py:394
  33.2 4.7 %all-to-all-start = ((bf16[8,176,128]{2,1,0:T(8,128)(2,1)}), bf16[8,176,128]{2,1,0:T(8,128)(2,1)S(1)}, u32[]{:S(2)}, u32[]{:S(2)}) async-start(bf16[8,176,128]{2,1,0:T(8,128)(2,1)} %get-tuple-element.60), calls=%async_computation | async-start | bytes 720896 | tf_op jit(solution)/shard_map/all_to_all | solution.py:406
  37.9 0.7 %caption_total.1 = f32[48,1152]{1,0:T(8,128)} custom-call(f32[48,1152]{1,0:T(8,128)S(1)} %get-tuple-element.56.refs_0_, bf16[48,1152]{1,0:T(8,128)(2,1)S(1)} %collective-permute-done.12.refs_1_, bf16[48,1152]{1,0:T(8,128)(2,1)S(1)} %collective-permute-done.13.refs_2_, bf16[48,1152]{1,0:T(8,128)(2,1)S(1)} %collective-permute-done.14.refs_3_), custom_call_target="tpu_custom_call" | custom-call | flops 5000000000 | tf_op jit(solution)/shard_map/caption_total/pallas_call | solution.py:437
  38.6 0.6 %dynamic-slice_bitcast_fusion = f32[48]{0:T(128)} fusion(f32[1,384]{1,0:T(1,128)S(1)} %get-tuple-element.55, s32[]{:T(128)S(6)} %select_n.16), kind=kLoop, calls=%fused_computation | loop fusion | bytes 388 | tf_op jit(solution)/shard_map/dynamic_slice | solution.py:446
  39.2 9.1 %all-to-all-done.got_ref = bf16[8,176,128]{2,1,0:T(8,128)(2,1)S(1)} async-done(((bf16[8,176,128]{2,1,0:T(8,128)(2,1)}), bf16[8,176,128]{2,1,0:T(8,128)(2,1)S(1)}, u32[]{:S(2)}, u32[]{:S(2)}) %all-to-all-start) | async-done | bytes 360480 | tf_op jit(solution)/shard_map/all_to_all | solution.py:406
  48.3 0.9 %weight_total.1 = f32[144,288]{1,0:T(8,128)} custom-call(bf16[8,176,128]{2,1,0:T(8,128)(2,1)S(1)} %all-to-all-done.got_ref), custom_call_target="tpu_custom_call" | custom-call | tf_op jit(solution)/shard_map/weight_total/pallas_call | solution.py:407
  (27 shorter events, 1.2 us)
Async XLA Ops:
  0.6 9.9 %collective-permute-start = (bf16[48,1152]{1,0:T(8,128)(2,1)}, bf16[48,1152]{1,0:T(8,128)(2,1)S(1)}, u32[]{:S(2)}, u32[]{:S(2)}) collective-permute-start(bf16[48,1152]{1,0:T(8,128)(2,1)} %refs_0_.1), channel_id=1, source_target_pairs={{0,2},{1,3},{2,0},{3,1},{4,6},{5,7},{6,4},{7,5},{8,10},{9,11},{10,... | collective-permute-start | bytes 331784 | tf_op jit(solution)/shard_map/ppermute | solution.py:31
  3.7 8.6 %collective-permute-start.1 = (bf16[48,1152]{1,0:T(8,128)(2,1)}, bf16[48,1152]{1,0:T(8,128)(2,1)S(1)}, u32[]{:S(2)}, u32[]{:S(2)}) collective-permute-start(bf16[48,1152]{1,0:T(8,128)(2,1)} %refs_0_.1), channel_id=1, source_target_pairs={{0,4},{1,5},{2,6},{3,7},{4,0},{5,1},{6,2},{7,3},{8,12},{9,13},{10,... | collective-permute-start | bytes 331784 | tf_op jit(solution)/shard_map/ppermute | solution.py:31
  5.2 7.1 %collective-permute-start.2 = (bf16[48,1152]{1,0:T(8,128)(2,1)}, bf16[48,1152]{1,0:T(8,128)(2,1)S(1)}, u32[]{:S(2)}, u32[]{:S(2)}) collective-permute-start(bf16[48,1152]{1,0:T(8,128)(2,1)} %refs_0_.1), channel_id=1, source_target_pairs={{0,6},{1,7},{2,4},{3,5},{4,2},{5,3},{6,0},{7,1},{8,14},{9,15},{10,... | collective-permute-start | bytes 331784 | tf_op jit(solution)/shard_map/ppermute | solution.py:31
  5.2 9.5 %collective-permute-start.3 = (bf16[48,1152]{1,0:T(8,128)(2,1)}, bf16[48,1152]{1,0:T(8,128)(2,1)S(1)}, u32[]{:S(2)}, u32[]{:S(2)}) collective-permute-start(bf16[48,1152]{1,0:T(8,128)(2,1)} %text_ref.1), channel_id=1, source_target_pairs={{0,24},{1,25},{2,26},{3,27},{4,28},{5,29},{6,30},{7,31},{8,16},{9,... | collective-permute-start | bytes 331784 | tf_op jit(solution)/shard_map/ppermute | solution.py:31
  9.2 8.7 %collective-permute-start.4 = (bf16[48,1152]{1,0:T(8,128)(2,1)}, bf16[48,1152]{1,0:T(8,128)(2,1)S(1)}, u32[]{:S(2)}, u32[]{:S(2)}) collective-permute-start(bf16[48,1152]{1,0:T(8,128)(2,1)} %text_ref.1), channel_id=1, source_target_pairs={{0,16},{1,17},{2,18},{3,19},{4,20},{5,21},{6,22},{7,23},{8,24},{9,... | collective-permute-start | bytes 331784 | tf_op jit(solution)/shard_map/ppermute | solution.py:31
  10.5 1.7 %copy-start.1 = (bf16[48,1152]{1,0:T(8,128)(2,1)S(1)}, bf16[48,1152]{1,0:T(8,128)(2,1)}, u32[]{:S(2)}) copy-start(bf16[48,1152]{1,0:T(8,128)(2,1)} %refs_0_.1) | copy-start | bytes 331780
  10.6 7.4 %collective-permute-start.5 = (bf16[48,1152]{1,0:T(8,128)(2,1)}, bf16[48,1152]{1,0:T(8,128)(2,1)S(1)}, u32[]{:S(2)}, u32[]{:S(2)}) collective-permute-start(bf16[48,1152]{1,0:T(8,128)(2,1)} %text_ref.1), channel_id=1, source_target_pairs={{0,8},{1,9},{2,10},{3,11},{4,12},{5,13},{6,14},{7,15},{8,0},{9,1},... | collective-permute-start | bytes 331784 | tf_op jit(solution)/shard_map/ppermute | solution.py:31
  11.2 0.9 %copy-start.2 = (bf16[48,1152]{1,0:T(8,128)(2,1)S(1)}, bf16[48,1152]{1,0:T(8,128)(2,1)}, u32[]{:S(2)}) copy-start(bf16[48,1152]{1,0:T(8,128)(2,1)} %text_ref.1) | copy-start | bytes 331780
  12.1 1.7 %copy-start = (bf16[1152,1152]{1,0:T(8,128)(2,1)S(1)}, bf16[1152,1152]{1,0:T(8,128)(2,1)}, u32[]{:S(2)}) copy-start(bf16[1152,1152]{1,0:T(8,128)(2,1)} %weight.1) | copy-start | bytes 7962628
  12.3 5.8 %collective-permute-start.6 = (bf16[192,1152]{1,0:T(8,128)(2,1)S(1)}, bf16[192,1152]{1,0:T(8,128)(2,1)S(1)}, u32[]{:S(2)}, u32[]{:S(2)}) collective-permute-start(bf16[192,1152]{1,0:T(8,128)(2,1)S(1)} %stack.1.feats_ref.own_half), channel_id=1, source_target_pairs={{0,1},{1,0},{2,3},{3,2},{4,5},{5,4},{6,7},{7,6},{8,9},{9,8},{10,11... | collective-permute-start | bytes 1327112 | tf_op jit(solution)/shard_map/ppermute | solution.py:31
  21.0 1.6 %collective-permute-start.7 = (bf16[2,160,384]{2,1,0:T(8,128)(2,1)S(1)}, bf16[2,160,384]{2,1,0:T(8,128)(2,1)S(1)}, u32[]{:S(2)}, u32[]{:S(2)}) collective-permute-start(bf16[2,160,384]{2,1,0:T(8,128)(2,1)S(1)} %get-tuple-element.39), channel_id=1, source_target_pairs={{0,1},{1,0},{2,3},{3,2},{4,5},{5,4},{6,7},{7,6},{8,9},{9,8},{10,11... | collective-permute-start | bytes 737288 | tf_op jit(solution)/shard_map/ppermute | solution.py:31
  21.1 4.6 %collective-permute-start.8 = (bf16[2,160,384]{2,1,0:T(8,128)(2,1)S(1)}, bf16[2,160,384]{2,1,0:T(8,128)(2,1)S(1)}, u32[]{:S(2)}, u32[]{:S(2)}) collective-permute-start(bf16[2,160,384]{2,1,0:T(8,128)(2,1)S(1)} %get-tuple-element.47), channel_id=1, source_target_pairs={{0,1},{1,0},{2,3},{3,2},{4,5},{5,4},{6,7},{7,6},{8,9},{9,8},{10,11... | collective-permute-start | bytes 737288 | tf_op jit(solution)/shard_map/ppermute | solution.py:31
  22.7 7.1 %collective-permute-start.10 = (bf16[160,384]{1,0:T(8,128)(2,1)S(1)}, bf16[160,384]{1,0:T(8,128)(2,1)S(1)}, u32[]{:S(2)}, u32[]{:S(2)}) collective-permute-start(bf16[160,384]{1,0:T(8,128)(2,1)S(1)} %get-tuple-element.51), channel_id=1, source_target_pairs={{0,6},{1,7},{2,4},{3,5},{4,2},{5,3},{6,0},{7,1},{8,14},{9,15},{10,... | collective-permute-start | bytes 368648 | tf_op jit(solution)/shard_map/ppermute | solution.py:31
  25.2 6.5 %collective-permute-start.9 = (bf16[160,384]{1,0:T(8,128)(2,1)S(1)}, bf16[160,384]{1,0:T(8,128)(2,1)S(1)}, u32[]{:S(2)}, u32[]{:S(2)}) collective-permute-start(bf16[160,384]{1,0:T(8,128)(2,1)S(1)} %get-tuple-element.50), channel_id=1, source_target_pairs={{0,4},{1,5},{2,6},{3,7},{4,0},{5,1},{6,2},{7,3},{8,12},{9,13},{10,... | collective-permute-start | bytes 368648 | tf_op jit(solution)/shard_map/ppermute | solution.py:31
  25.8 6.0 %collective-permute-start.11 = (bf16[160,384]{1,0:T(8,128)(2,1)S(1)}, bf16[160,384]{1,0:T(8,128)(2,1)S(1)}, u32[]{:S(2)}, u32[]{:S(2)}) collective-permute-start(bf16[160,384]{1,0:T(8,128)(2,1)S(1)} %get-tuple-element.52), channel_id=1, source_target_pairs={{0,2},{1,3},{2,0},{3,1},{4,6},{5,7},{6,4},{7,5},{8,10},{9,11},{10,... | collective-permute-start | bytes 368648 | tf_op jit(solution)/shard_map/ppermute | solution.py:31
  26.3 11.5 %collective-permute-start.12 = (bf16[48,1152]{1,0:T(8,128)(2,1)S(1)}, bf16[48,1152]{1,0:T(8,128)(2,1)S(1)}, u32[]{:S(2)}, u32[]{:S(2)}) collective-permute-start(bf16[48,1152]{1,0:T(8,128)(2,1)S(1)} %get-tuple-element.57), channel_id=1, source_target_pairs={{0,24},{1,25},{2,26},{3,27},{4,28},{5,29},{6,30},{7,31},{8,16},{9,... | collective-permute-start | bytes 331784 | tf_op jit(solution)/shard_map/ppermute | solution.py:31
  28.8 9.1 %collective-permute-start.13 = (bf16[48,1152]{1,0:T(8,128)(2,1)S(1)}, bf16[48,1152]{1,0:T(8,128)(2,1)S(1)}, u32[]{:S(2)}, u32[]{:S(2)}) collective-permute-start(bf16[48,1152]{1,0:T(8,128)(2,1)S(1)} %get-tuple-element.58), channel_id=1, source_target_pairs={{0,16},{1,17},{2,18},{3,19},{4,20},{5,21},{6,22},{7,23},{8,24},{9,... | collective-permute-start | bytes 331784 | tf_op jit(solution)/shard_map/ppermute | solution.py:31
  29.8 8.1 %collective-permute-start.14 = (bf16[48,1152]{1,0:T(8,128)(2,1)S(1)}, bf16[48,1152]{1,0:T(8,128)(2,1)S(1)}, u32[]{:S(2)}, u32[]{:S(2)}) collective-permute-start(bf16[48,1152]{1,0:T(8,128)(2,1)S(1)} %get-tuple-element.59), channel_id=1, source_target_pairs={{0,8},{1,9},{2,10},{3,11},{4,12},{5,13},{6,14},{7,15},{8,0},{9,1},... | collective-permute-start | bytes 331784 | tf_op jit(solution)/shard_map/ppermute | solution.py:31
  33.2 15.1 %all-to-all-start = ((bf16[8,176,128]{2,1,0:T(8,128)(2,1)}), bf16[8,176,128]{2,1,0:T(8,128)(2,1)S(1)}, u32[]{:S(2)}, u32[]{:S(2)}) async-start(bf16[8,176,128]{2,1,0:T(8,128)(2,1)} %get-tuple-element.60), calls=%async_computation | async-start | bytes 720896 | tf_op jit(solution)/shard_map/all_to_all | solution.py:406

commit v24 on v19

--- a/solution.py
+++ b/solution.py
@@ -432,7 +432,7 @@
         compiler_params=limit(12),
         cost_estimate=hint(5 * 10**9),
         name="caption_total",
-    )(own_text, *got_text[::-1])
+    )(own_text, *got_text[1:], got_text[0])
     image_loss = lax.dynamic_slice_in_dim(loss_line[0], first_image(member[0], rows, group), rows, 0)
     return (image_loss, d_text_unit, d_proj)
 

time: 49.4 us -> 49.4 us (level)
  waiting for transfers between devices: 14.8 us -> 15.4 us
  starting transfers between devices: 21.5 us -> 21 us
    ppermute x15, starting transfers between devices: 16.9 us -> 16.3 us  [swapped(): lax.ppermute(value, AXES, [(source, source ^ mask) for source in range(to...]
  transfers between devices with their start and end apart: 16 -> 16, of which waited for: 6 -> 5; matrix products, arithmetic and copies ran while one was open for 1% -> 1% of each run, Pallas kernels for 8% -> 8%
where the time goes in v24:
time: 49.4 us; the launch traced here: 49.1 us
  starting transfers between devices  21 us (43%)
  waiting for transfers between devices  15.4 us (31%)
  Pallas kernels  7.66 us (16%)
  local copies, waits for them, and re-layouts  2.98 us (6%)
  between operations  2.09 us (4%)
    ppermute x15, starting transfers between devices, swapped(): lax.ppermute(value, AXES, [(source, source ^ mask) for source in range(to...  16.3 us
    all_to_all x1, waiting for transfers between devices, local(): got_weight = lax.all_to_all(sent_weight, AXES[:2], 0, 0)  9.1 us
    ppermute x15, waiting for transfers between devices, swapped(): lax.ppermute(value, AXES, [(source, source ^ mask) for source in range(to...  6.28 us
    all_to_all x1, starting transfers between devices, local(): got_weight = lax.all_to_all(sent_weight, AXES[:2], 0, 0)  4.65 us
    pallas_call x1, Pallas kernels, local(): pl.pallas_call(functools.partial(pair_kernel, narrow, group), in_specs=[S...  2.89 us
    unnamed x6, local copies, waits for them, and re-layouts  2.4 us
    pallas_call x1, Pallas kernels, local(): pl.pallas_call(functools.partial(weight_kernel, group, wide), in_specs=[V...  1.37 us
  transfers between devices with their start and end apart: 16, of which 5 were waited for; matrix products, arithmetic and copies ran while one was open for 1% of the time, Pallas kernels for 8%

profile of v24, /device:TPU:0, one launch (start us, length us, event | category | flops | bytes accessed | tf_op | source)
XLA Modules:
  0.0 49.1 jit_solution(12848191434746384304)
XLA Ops:
  0.6 3.0 %collective-permute-start = (bf16[48,1152]{1,0:T(8,128)(2,1)}, bf16[48,1152]{1,0:T(8,128)(2,1)S(1)}, u32[]{:S(2)}, u32[]{:S(2)}) collective-permute-start(bf16[48,1152]{1,0:T(8,128)(2,1)} %refs_0_.1), channel_id=1, source_target_pairs={{0,2},{1,3},{2,0},{3,1},{4,6},{5,7},{6,4},{7,5},{8,10},{9,11},{10,... | collective-permute-start | bytes 331784 | tf_op jit(solution)/shard_map/ppermute | solution.py:31
  3.7 1.5 %collective-permute-start.1 = (bf16[48,1152]{1,0:T(8,128)(2,1)}, bf16[48,1152]{1,0:T(8,128)(2,1)S(1)}, u32[]{:S(2)}, u32[]{:S(2)}) collective-permute-start(bf16[48,1152]{1,0:T(8,128)(2,1)} %refs_0_.1), channel_id=1, source_target_pairs={{0,4},{1,5},{2,6},{3,7},{4,0},{5,1},{6,2},{7,3},{8,12},{9,13},{10,... | collective-permute-start | bytes 331784 | tf_op jit(solution)/shard_map/ppermute | solution.py:31
  5.2 4.0 %collective-permute-start.3 = (bf16[48,1152]{1,0:T(8,128)(2,1)}, bf16[48,1152]{1,0:T(8,128)(2,1)S(1)}, u32[]{:S(2)}, u32[]{:S(2)}) collective-permute-start(bf16[48,1152]{1,0:T(8,128)(2,1)} %text_ref.1), channel_id=1, source_target_pairs={{0,24},{1,25},{2,26},{3,27},{4,28},{5,29},{6,30},{7,31},{8,16},{9,... | collective-permute-start | bytes 331784 | tf_op jit(solution)/shard_map/ppermute | solution.py:31
  10.6 0.6 %collective-permute-start.5 = (bf16[48,1152]{1,0:T(8,128)(2,1)}, bf16[48,1152]{1,0:T(8,128)(2,1)S(1)}, u32[]{:S(2)}, u32[]{:S(2)}) collective-permute-start(bf16[48,1152]{1,0:T(8,128)(2,1)} %text_ref.1), channel_id=1, source_target_pairs={{0,8},{1,9},{2,10},{3,11},{4,12},{5,13},{6,14},{7,15},{8,0},{9,1},... | collective-permute-start | bytes 331784 | tf_op jit(solution)/shard_map/ppermute | solution.py:31
  11.2 0.9 %copy-done.2 = bf16[48,1152]{1,0:T(8,128)(2,1)S(1)} copy-done((bf16[48,1152]{1,0:T(8,128)(2,1)S(1)}, bf16[48,1152]{1,0:T(8,128)(2,1)}, u32[]{:S(2)}) %copy-start.2) | copy-done | bytes 110616
  12.4 1.5 %copy-done = bf16[1152,1152]{1,0:T(8,128)(2,1)S(1)} copy-done((bf16[1152,1152]{1,0:T(8,128)(2,1)S(1)}, bf16[1152,1152]{1,0:T(8,128)(2,1)}, u32[]{:S(2)}) %copy-start) | copy-done | bytes 2654232
  13.9 0.8 %own_projection.1.own_proj = f32[192,1152]{1,0:T(8,128)S(1)} custom-call(bf16[192,1152]{1,0:T(8,128)(2,1)S(1)} %stack.1.feats_ref.own_half, bf16[1152,1152]{1,0:T(8,128)(2,1)S(1)} %copy-done), custom_call_target="tpu_custom_call" | custom-call | tf_op jit(solution)/shard_map/own_projection/pallas_call | solution.py:296
  14.7 3.3 %collective-permute-done.4.refs_2_ = bf16[48,1152]{1,0:T(8,128)(2,1)S(1)} collective-permute-done((bf16[48,1152]{1,0:T(8,128)(2,1)}, bf16[48,1152]{1,0:T(8,128)(2,1)S(1)}, u32[]{:S(2)}, u32[]{:S(2)}) %collective-permute-start.4) | collective-permute-done | bytes 110624 | tf_op jit(solution)/shard_map/ppermute | solution.py:31
  18.1 2.9 %pairs.1 = (bf16[384,1152]{1,0:T(8,128)(2,1)S(1)}, f32[1,384]{1,0:T(1,128)S(1)}, bf16[1152,384]{1,0:T(8,128)(2,1)S(1)}, bf16[192,384]{1,0:T(8,128)(2,1)S(1)}, f3...) custom-call(s32[1]{0:T(128)} %bitcast.member_ref, ...), custom_call_target="tpu_custom_call" | custom-call | tf_op jit(solution)/shard_map/pairs/pallas_call | solution.py:315
  21.1 0.5 %collective-permute-start.8 = (bf16[2,160,384]{2,1,0:T(8,128)(2,1)S(1)}, bf16[2,160,384]{2,1,0:T(8,128)(2,1)S(1)}, u32[]{:S(2)}, u32[]{:S(2)}) collective-permute-start(bf16[2,160,384]{2,1,0:T(8,128)(2,1)S(1)} %get-tuple-element.47), channel_id=1, source_target_pairs={{0,1},{1,0},{2,3},{3,2},{4,5},{5,4},{6,7},{7,6},{8,9},{9,8},{10,11... | collective-permute-start | bytes 737288 | tf_op jit(solution)/shard_map/ppermute | solution.py:31
  21.6 0.5 %captions.1 = (bf16[1152,384]{1,0:T(8,128)(2,1)S(1)}, f32[48,1152]{1,0:T(8,128)S(1)}, bf16[48,1152]{1,0:T(8,128)(2,1)S(1)}, bf16[48,1152]{1,0:T(8,128)(2,1)S(1)}, bf16[48,1152]{1,0:T(8,128)(2,1)S(1)}) custom-call(bf16[192,384]{1,0:T(8,128)(2,1)S(1)} %get-tuple-element.40.grad_ref, bf16[1152,384]{1,0:T(8,128)(2,1)S(1)} %get-tuple-element.41.emb_ref, ...), custom_call_target="tpu_custom_call" | custom-call | tf_op jit(solution)/shard_map/captions/pallas_call | solution.py:338
  22.7 2.5 %collective-permute-start.10 = (bf16[160,384]{1,0:T(8,128)(2,1)S(1)}, bf16[160,384]{1,0:T(8,128)(2,1)S(1)}, u32[]{:S(2)}, u32[]{:S(2)}) collective-permute-start(bf16[160,384]{1,0:T(8,128)(2,1)S(1)} %get-tuple-element.51), channel_id=1, source_target_pairs={{0,6},{1,7},{2,4},{3,5},{4,2},{5,3},{6,0},{7,1},{8,14},{9,15},{10,... | collective-permute-start | bytes 368648 | tf_op jit(solution)/shard_map/ppermute | solution.py:31
  25.2 0.5 %collective-permute-start.9 = (bf16[160,384]{1,0:T(8,128)(2,1)S(1)}, bf16[160,384]{1,0:T(8,128)(2,1)S(1)}, u32[]{:S(2)}, u32[]{:S(2)}) collective-permute-start(bf16[160,384]{1,0:T(8,128)(2,1)S(1)} %get-tuple-element.50), channel_id=1, source_target_pairs={{0,4},{1,5},{2,6},{3,7},{4,0},{5,1},{6,2},{7,3},{8,12},{9,13},{10,... | collective-permute-start | bytes 368648 | tf_op jit(solution)/shard_map/ppermute | solution.py:31
  25.8 0.6 %collective-permute-start.11 = (bf16[160,384]{1,0:T(8,128)(2,1)S(1)}, bf16[160,384]{1,0:T(8,128)(2,1)S(1)}, u32[]{:S(2)}, u32[]{:S(2)}) collective-permute-start(bf16[160,384]{1,0:T(8,128)(2,1)S(1)} %get-tuple-element.52), channel_id=1, source_target_pairs={{0,2},{1,3},{2,0},{3,1},{4,6},{5,7},{6,4},{7,5},{8,10},{9,11},{10,... | collective-permute-start | bytes 368648 | tf_op jit(solution)/shard_map/ppermute | solution.py:31
  26.3 0.5 %collective-permute-start.12 = (bf16[48,1152]{1,0:T(8,128)(2,1)S(1)}, bf16[48,1152]{1,0:T(8,128)(2,1)S(1)}, u32[]{:S(2)}, u32[]{:S(2)}) collective-permute-start(bf16[48,1152]{1,0:T(8,128)(2,1)S(1)} %get-tuple-element.57), channel_id=1, source_target_pairs={{0,16},{1,17},{2,18},{3,19},{4,20},{5,21},{6,22},{7,23},{8,24},{9,... | collective-permute-start | bytes 331784 | tf_op jit(solution)/shard_map/ppermute | solution.py:31
  26.9 2.0 %collective-permute-start.13 = (bf16[48,1152]{1,0:T(8,128)(2,1)S(1)}, bf16[48,1152]{1,0:T(8,128)(2,1)S(1)}, u32[]{:S(2)}, u32[]{:S(2)}) collective-permute-start(bf16[48,1152]{1,0:T(8,128)(2,1)S(1)} %get-tuple-element.58), channel_id=1, source_target_pairs={{0,24},{1,25},{2,26},{3,27},{4,28},{5,29},{6,30},{7,31},{8,16},{9,... | collective-permute-start | bytes 331784 | tf_op jit(solution)/shard_map/ppermute | solution.py:31
  28.9 0.8 %collective-permute-done.10.refs_2_ = bf16[160,384]{1,0:T(8,128)(2,1)S(1)} collective-permute-done((bf16[160,384]{1,0:T(8,128)(2,1)S(1)}, bf16[160,384]{1,0:T(8,128)(2,1)S(1)}, u32[]{:S(2)}, u32[]{:S(2)}) %collective-permute-start.10) | collective-permute-done | bytes 122912 | tf_op jit(solution)/shard_map/ppermute | solution.py:31
  30.0 1.7 %collective-permute-done.9.refs_1_ = bf16[160,384]{1,0:T(8,128)(2,1)S(1)} collective-permute-done((bf16[160,384]{1,0:T(8,128)(2,1)S(1)}, bf16[160,384]{1,0:T(8,128)(2,1)S(1)}, u32[]{:S(2)}, u32[]{:S(2)}) %collective-permute-start.9) | collective-permute-done | bytes 122912 | tf_op jit(solution)/shard_map/ppermute | solution.py:31
  31.7 1.4 %weights.1 = (f32[1,384]{1,0:T(1,128)S(1)}, bf16[8,176,128]{2,1,0:T(8,128)(2,1)}) custom-call(f32[152,384]{1,0:T(8,128)S(1)} %far_sum.1.refs_0_, bf16[160,384]{1,0:T(8,128)(2,1)S(1)} %collective-permute-done.11.refs_1_, f32[1,384]{1,0:T(1,128)S(1)} %get-tuple-element.53.refs_2_, bf16[384,1152]{1,0:T(8,128)(2,1)S(1)} %get-tuple-element.42.feats_ref.refs_3_, ...), custom_call_target="tpu_custom_call" | custom-call | tf_op jit(solution)/shard_map/weights/pallas_call | solution.py:385
  33.1 4.7 %all-to-all-start = ((bf16[8,176,128]{2,1,0:T(8,128)(2,1)}), bf16[8,176,128]{2,1,0:T(8,128)(2,1)S(1)}, u32[]{:S(2)}, u32[]{:S(2)}) async-start(bf16[8,176,128]{2,1,0:T(8,128)(2,1)} %get-tuple-element.60), calls=%async_computation | async-start | bytes 720896 | tf_op jit(solution)/shard_map/all_to_all | solution.py:396
  37.8 0.7 %caption_total.1 = f32[48,1152]{1,0:T(8,128)} custom-call(f32[48,1152]{1,0:T(8,128)S(1)} %get-tuple-element.56.refs_0_, bf16[48,1152]{1,0:T(8,128)(2,1)S(1)} %collective-permute-done.12.refs_1_, bf16[48,1152]{1,0:T(8,128)(2,1)S(1)} %collective-permute-done.13.refs_2_, bf16[48,1152]{1,0:T(8,128)(2,1)S(1)} %collective-permute-done.14.refs_3_), custom_call_target="tpu_custom_call" | custom-call | flops 5000000000 | tf_op jit(solution)/shard_map/caption_total/pallas_call | solution.py:427
  38.5 0.6 %dynamic-slice_bitcast_fusion = f32[48]{0:T(128)} fusion(f32[1,384]{1,0:T(1,128)S(1)} %get-tuple-element.55, s32[]{:T(128)S(6)} %select_n.16), kind=kLoop, calls=%fused_computation | loop fusion | bytes 388 | tf_op jit(solution)/shard_map/dynamic_slice | solution.py:436
  39.1 9.1 %all-to-all-done.got_ref = bf16[8,176,128]{2,1,0:T(8,128)(2,1)S(1)} async-done(((bf16[8,176,128]{2,1,0:T(8,128)(2,1)}), bf16[8,176,128]{2,1,0:T(8,128)(2,1)S(1)}, u32[]{:S(2)}, u32[]{:S(2)}) %all-to-all-start) | async-done | bytes 360480 | tf_op jit(solution)/shard_map/all_to_all | solution.py:396
  48.2 0.9 %weight_total.1 = f32[144,288]{1,0:T(8,128)} custom-call(bf16[8,176,128]{2,1,0:T(8,128)(2,1)S(1)} %all-to-all-done.got_ref), custom_call_target="tpu_custom_call" | custom-call | tf_op jit(solution)/shard_map/weight_total/pallas_call | solution.py:397
  (27 shorter events, 1.4 us)
Async XLA Ops:
  0.6 9.9 %collective-permute-start = (bf16[48,1152]{1,0:T(8,128)(2,1)}, bf16[48,1152]{1,0:T(8,128)(2,1)S(1)}, u32[]{:S(2)}, u32[]{:S(2)}) collective-permute-start(bf16[48,1152]{1,0:T(8,128)(2,1)} %refs_0_.1), channel_id=1, source_target_pairs={{0,2},{1,3},{2,0},{3,1},{4,6},{5,7},{6,4},{7,5},{8,10},{9,11},{10,... | collective-permute-start | bytes 331784 | tf_op jit(solution)/shard_map/ppermute | solution.py:31
  3.7 8.6 %collective-permute-start.1 = (bf16[48,1152]{1,0:T(8,128)(2,1)}, bf16[48,1152]{1,0:T(8,128)(2,1)S(1)}, u32[]{:S(2)}, u32[]{:S(2)}) collective-permute-start(bf16[48,1152]{1,0:T(8,128)(2,1)} %refs_0_.1), channel_id=1, source_target_pairs={{0,4},{1,5},{2,6},{3,7},{4,0},{5,1},{6,2},{7,3},{8,12},{9,13},{10,... | collective-permute-start | bytes 331784 | tf_op jit(solution)/shard_map/ppermute | solution.py:31
  5.2 7.1 %collective-permute-start.2 = (bf16[48,1152]{1,0:T(8,128)(2,1)}, bf16[48,1152]{1,0:T(8,128)(2,1)S(1)}, u32[]{:S(2)}, u32[]{:S(2)}) collective-permute-start(bf16[48,1152]{1,0:T(8,128)(2,1)} %refs_0_.1), channel_id=1, source_target_pairs={{0,6},{1,7},{2,4},{3,5},{4,2},{5,3},{6,0},{7,1},{8,14},{9,15},{10,... | collective-permute-start | bytes 331784 | tf_op jit(solution)/shard_map/ppermute | solution.py:31
  5.2 9.5 %collective-permute-start.3 = (bf16[48,1152]{1,0:T(8,128)(2,1)}, bf16[48,1152]{1,0:T(8,128)(2,1)S(1)}, u32[]{:S(2)}, u32[]{:S(2)}) collective-permute-start(bf16[48,1152]{1,0:T(8,128)(2,1)} %text_ref.1), channel_id=1, source_target_pairs={{0,24},{1,25},{2,26},{3,27},{4,28},{5,29},{6,30},{7,31},{8,16},{9,... | collective-permute-start | bytes 331784 | tf_op jit(solution)/shard_map/ppermute | solution.py:31
  9.2 8.7 %collective-permute-start.4 = (bf16[48,1152]{1,0:T(8,128)(2,1)}, bf16[48,1152]{1,0:T(8,128)(2,1)S(1)}, u32[]{:S(2)}, u32[]{:S(2)}) collective-permute-start(bf16[48,1152]{1,0:T(8,128)(2,1)} %text_ref.1), channel_id=1, source_target_pairs={{0,16},{1,17},{2,18},{3,19},{4,20},{5,21},{6,22},{7,23},{8,24},{9,... | collective-permute-start | bytes 331784 | tf_op jit(solution)/shard_map/ppermute | solution.py:31
  10.5 1.7 %copy-start.1 = (bf16[48,1152]{1,0:T(8,128)(2,1)S(1)}, bf16[48,1152]{1,0:T(8,128)(2,1)}, u32[]{:S(2)}) copy-start(bf16[48,1152]{1,0:T(8,128)(2,1)} %refs_0_.1) | copy-start | bytes 331780
  10.6 7.4 %collective-permute-start.5 = (bf16[48,1152]{1,0:T(8,128)(2,1)}, bf16[48,1152]{1,0:T(8,128)(2,1)S(1)}, u32[]{:S(2)}, u32[]{:S(2)}) collective-permute-start(bf16[48,1152]{1,0:T(8,128)(2,1)} %text_ref.1), channel_id=1, source_target_pairs={{0,8},{1,9},{2,10},{3,11},{4,12},{5,13},{6,14},{7,15},{8,0},{9,1},... | collective-permute-start | bytes 331784 | tf_op jit(solution)/shard_map/ppermute | solution.py:31
  11.2 0.9 %copy-start.2 = (bf16[48,1152]{1,0:T(8,128)(2,1)S(1)}, bf16[48,1152]{1,0:T(8,128)(2,1)}, u32[]{:S(2)}) copy-start(bf16[48,1152]{1,0:T(8,128)(2,1)} %text_ref.1) | copy-start | bytes 331780
  12.1 1.7 %copy-start = (bf16[1152,1152]{1,0:T(8,128)(2,1)S(1)}, bf16[1152,1152]{1,0:T(8,128)(2,1)}, u32[]{:S(2)}) copy-start(bf16[1152,1152]{1,0:T(8,128)(2,1)} %weight.1) | copy-start | bytes 7962628
  12.3 5.8 %collective-permute-start.6 = (bf16[192,1152]{1,0:T(8,128)(2,1)S(1)}, bf16[192,1152]{1,0:T(8,128)(2,1)S(1)}, u32[]{:S(2)}, u32[]{:S(2)}) collective-permute-start(bf16[192,1152]{1,0:T(8,128)(2,1)S(1)} %stack.1.feats_ref.own_half), channel_id=1, source_target_pairs={{0,1},{1,0},{2,3},{3,2},{4,5},{5,4},{6,7},{7,6},{8,9},{9,8},{10,11... | collective-permute-start | bytes 1327112 | tf_op jit(solution)/shard_map/ppermute | solution.py:31
  21.0 1.6 %collective-permute-start.7 = (bf16[2,160,384]{2,1,0:T(8,128)(2,1)S(1)}, bf16[2,160,384]{2,1,0:T(8,128)(2,1)S(1)}, u32[]{:S(2)}, u32[]{:S(2)}) collective-permute-start(bf16[2,160,384]{2,1,0:T(8,128)(2,1)S(1)} %get-tuple-element.39), channel_id=1, source_target_pairs={{0,1},{1,0},{2,3},{3,2},{4,5},{5,4},{6,7},{7,6},{8,9},{9,8},{10,11... | collective-permute-start | bytes 737288 | tf_op jit(solution)/shard_map/ppermute | solution.py:31
  21.1 4.6 %collective-permute-start.8 = (bf16[2,160,384]{2,1,0:T(8,128)(2,1)S(1)}, bf16[2,160,384]{2,1,0:T(8,128)(2,1)S(1)}, u32[]{:S(2)}, u32[]{:S(2)}) collective-permute-start(bf16[2,160,384]{2,1,0:T(8,128)(2,1)S(1)} %get-tuple-element.47), channel_id=1, source_target_pairs={{0,1},{1,0},{2,3},{3,2},{4,5},{5,4},{6,7},{7,6},{8,9},{9,8},{10,11... | collective-permute-start | bytes 737288 | tf_op jit(solution)/shard_map/ppermute | solution.py:31
  22.7 7.1 %collective-permute-start.10 = (bf16[160,384]{1,0:T(8,128)(2,1)S(1)}, bf16[160,384]{1,0:T(8,128)(2,1)S(1)}, u32[]{:S(2)}, u32[]{:S(2)}) collective-permute-start(bf16[160,384]{1,0:T(8,128)(2,1)S(1)} %get-tuple-element.51), channel_id=1, source_target_pairs={{0,6},{1,7},{2,4},{3,5},{4,2},{5,3},{6,0},{7,1},{8,14},{9,15},{10,... | collective-permute-start | bytes 368648 | tf_op jit(solution)/shard_map/ppermute | solution.py:31
  25.2 6.5 %collective-permute-start.9 = (bf16[160,384]{1,0:T(8,128)(2,1)S(1)}, bf16[160,384]{1,0:T(8,128)(2,1)S(1)}, u32[]{:S(2)}, u32[]{:S(2)}) collective-permute-start(bf16[160,384]{1,0:T(8,128)(2,1)S(1)} %get-tuple-element.50), channel_id=1, source_target_pairs={{0,4},{1,5},{2,6},{3,7},{4,0},{5,1},{6,2},{7,3},{8,12},{9,13},{10,... | collective-permute-start | bytes 368648 | tf_op jit(solution)/shard_map/ppermute | solution.py:31
  25.8 6.0 %collective-permute-start.11 = (bf16[160,384]{1,0:T(8,128)(2,1)S(1)}, bf16[160,384]{1,0:T(8,128)(2,1)S(1)}, u32[]{:S(2)}, u32[]{:S(2)}) collective-permute-start(bf16[160,384]{1,0:T(8,128)(2,1)S(1)} %get-tuple-element.52), channel_id=1, source_target_pairs={{0,2},{1,3},{2,0},{3,1},{4,6},{5,7},{6,4},{7,5},{8,10},{9,11},{10,... | collective-permute-start | bytes 368648 | tf_op jit(solution)/shard_map/ppermute | solution.py:31
  26.3 11.4 %collective-permute-start.12 = (bf16[48,1152]{1,0:T(8,128)(2,1)S(1)}, bf16[48,1152]{1,0:T(8,128)(2,1)S(1)}, u32[]{:S(2)}, u32[]{:S(2)}) collective-permute-start(bf16[48,1152]{1,0:T(8,128)(2,1)S(1)} %get-tuple-element.57), channel_id=1, source_target_pairs={{0,16},{1,17},{2,18},{3,19},{4,20},{5,21},{6,22},{7,23},{8,24},{9,... | collective-permute-start | bytes 331784 | tf_op jit(solution)/shard_map/ppermute | solution.py:31
  26.9 10.9 %collective-permute-start.13 = (bf16[48,1152]{1,0:T(8,128)(2,1)S(1)}, bf16[48,1152]{1,0:T(8,128)(2,1)S(1)}, u32[]{:S(2)}, u32[]{:S(2)}) collective-permute-start(bf16[48,1152]{1,0:T(8,128)(2,1)S(1)} %get-tuple-element.58), channel_id=1, source_target_pairs={{0,24},{1,25},{2,26},{3,27},{4,28},{5,29},{6,30},{7,31},{8,16},{9,... | collective-permute-start | bytes 331784 | tf_op jit(solution)/shard_map/ppermute | solution.py:31
  29.8 8.0 %collective-permute-start.14 = (bf16[48,1152]{1,0:T(8,128)(2,1)S(1)}, bf16[48,1152]{1,0:T(8,128)(2,1)S(1)}, u32[]{:S(2)}, u32[]{:S(2)}) collective-permute-start(bf16[48,1152]{1,0:T(8,128)(2,1)S(1)} %get-tuple-element.59), channel_id=1, source_target_pairs={{0,8},{1,9},{2,10},{3,11},{4,12},{5,13},{6,14},{7,15},{8,0},{9,1},... | collective-permute-start | bytes 331784 | tf_op jit(solution)/shard_map/ppermute | solution.py:31
  33.1 15.1 %all-to-all-start = ((bf16[8,176,128]{2,1,0:T(8,128)(2,1)}), bf16[8,176,128]{2,1,0:T(8,128)(2,1)S(1)}, u32[]{:S(2)}, u32[]{:S(2)}) async-start(bf16[8,176,128]{2,1,0:T(8,128)(2,1)} %get-tuple-element.60), calls=%async_computation | async-start | bytes 720896 | tf_op jit(solution)/shard_map/all_to_all | solution.py:396

commit v25 on v24

--- a/solution.py
+++ b/solution.py
@@ -301,7 +301,8 @@
         compiler_params=limit(8),
         name="own_projection",
     )(own_half, proj_weight)
-    own_proj, *texts = lax.optimization_barrier((own_proj, *texts[::-1]))
+    own_proj, *texts = lax.optimization_barrier((own_proj, *texts[1:], texts[0]))
+    texts = [*texts[-2::-1], texts[-1]]
     text_emb = pl.pallas_call(
         text_kernel,
         in_specs=[VMEM] * spread,

time: 49.4 us -> 49.5 us (level)
  starting transfers between devices: 21 us -> 23.4 us
  waiting for transfers between devices: 15.4 us -> 13.1 us
    ppermute x15, waiting for transfers between devices: 6.28 us -> 3.95 us  [swapped(): lax.ppermute(value, AXES, [(source, source ^ mask) for source in range(to...]
    ppermute x15, starting transfers between devices: 16.3 us -> 18.2 us  [swapped(): lax.ppermute(value, AXES, [(source, source ^ mask) for source in range(to...]
    all_to_all x1, starting transfers between devices: 4.65 us -> 5.23 us  [local(): got_weight = lax.all_to_all(sent_weight, AXES[:2], 0, 0)]
where the time goes in v25:
time: 49.5 us; the launch traced here: 49.2 us
  starting transfers between devices  23.4 us (47%)
  waiting for transfers between devices  13.1 us (26%)
  Pallas kernels  7.66 us (15%)
  local copies, waits for them, and re-layouts  2.98 us (6%)
  between operations  2.08 us (4%)
    ppermute x15, starting transfers between devices, swapped(): lax.ppermute(value, AXES, [(source, source ^ mask) for source in range(to...  18.2 us
    all_to_all x1, waiting for transfers between devices, local(): got_weight = lax.all_to_all(sent_weight, AXES[:2], 0, 0)  9.11 us
    all_to_all x1, starting transfers between devices, local(): got_weight = lax.all_to_all(sent_weight, AXES[:2], 0, 0)  5.23 us
    ppermute x15, waiting for transfers between devices, swapped(): lax.ppermute(value, AXES, [(source, source ^ mask) for source in range(to...  3.95 us
    pallas_call x1, Pallas kernels, local(): pl.pallas_call(functools.partial(pair_kernel, narrow, group), in_specs=[S...  2.88 us
    unnamed x6, local copies, waits for them, and re-layouts  2.4 us
    pallas_call x1, Pallas kernels, local(): pl.pallas_call(functools.partial(weight_kernel, group, wide), in_specs=[V...  1.37 us
  transfers between devices with their start and end apart: 16, of which 5 were waited for; matrix products, arithmetic and copies ran while one was open for 1% of the time, Pallas kernels for 8%

profile of v25, /device:TPU:0, one launch (start us, length us, event | category | flops | bytes accessed | tf_op | source)
XLA Modules:
  0.0 49.2 jit_solution(10613121739797245030)
XLA Ops:
  0.6 3.0 %collective-permute-start = (bf16[48,1152]{1,0:T(8,128)(2,1)}, bf16[48,1152]{1,0:T(8,128)(2,1)S(1)}, u32[]{:S(2)}, u32[]{:S(2)}) collective-permute-start(bf16[48,1152]{1,0:T(8,128)(2,1)} %refs_0_.1), channel_id=1, source_target_pairs={{0,2},{1,3},{2,0},{3,1},{4,6},{5,7},{6,4},{7,5},{8,10},{9,11},{10,... | collective-permute-start | bytes 331784 | tf_op jit(solution)/shard_map/ppermute | solution.py:31
  3.7 1.5 %collective-permute-start.1 = (bf16[48,1152]{1,0:T(8,128)(2,1)}, bf16[48,1152]{1,0:T(8,128)(2,1)S(1)}, u32[]{:S(2)}, u32[]{:S(2)}) collective-permute-start(bf16[48,1152]{1,0:T(8,128)(2,1)} %refs_0_.1), channel_id=1, source_target_pairs={{0,4},{1,5},{2,6},{3,7},{4,0},{5,1},{6,2},{7,3},{8,12},{9,13},{10,... | collective-permute-start | bytes 331784 | tf_op jit(solution)/shard_map/ppermute | solution.py:31
  5.2 3.0 %collective-permute-start.3 = (bf16[48,1152]{1,0:T(8,128)(2,1)}, bf16[48,1152]{1,0:T(8,128)(2,1)S(1)}, u32[]{:S(2)}, u32[]{:S(2)}) collective-permute-start(bf16[48,1152]{1,0:T(8,128)(2,1)} %text_ref.1), channel_id=1, source_target_pairs={{0,16},{1,17},{2,18},{3,19},{4,20},{5,21},{6,22},{7,23},{8,24},{9,... | collective-permute-start | bytes 331784 | tf_op jit(solution)/shard_map/ppermute | solution.py:31
  8.2 1.3 %collective-permute-start.4 = (bf16[48,1152]{1,0:T(8,128)(2,1)}, bf16[48,1152]{1,0:T(8,128)(2,1)S(1)}, u32[]{:S(2)}, u32[]{:S(2)}) collective-permute-start(bf16[48,1152]{1,0:T(8,128)(2,1)} %text_ref.1), channel_id=1, source_target_pairs={{0,24},{1,25},{2,26},{3,27},{4,28},{5,29},{6,30},{7,31},{8,16},{9,... | collective-permute-start | bytes 331784 | tf_op jit(solution)/shard_map/ppermute | solution.py:31
  11.2 0.9 %copy-done.2 = bf16[48,1152]{1,0:T(8,128)(2,1)S(1)} copy-done((bf16[48,1152]{1,0:T(8,128)(2,1)S(1)}, bf16[48,1152]{1,0:T(8,128)(2,1)}, u32[]{:S(2)}) %copy-start.2) | copy-done | bytes 110616
  12.4 1.5 %copy-done = bf16[1152,1152]{1,0:T(8,128)(2,1)S(1)} copy-done((bf16[1152,1152]{1,0:T(8,128)(2,1)S(1)}, bf16[1152,1152]{1,0:T(8,128)(2,1)}, u32[]{:S(2)}) %copy-start) | copy-done | bytes 2654232
  13.9 0.8 %own_projection.1.own_proj = f32[192,1152]{1,0:T(8,128)S(1)} custom-call(bf16[192,1152]{1,0:T(8,128)(2,1)S(1)} %stack.1.feats_ref.own_half, bf16[1152,1152]{1,0:T(8,128)(2,1)S(1)} %copy-done), custom_call_target="tpu_custom_call" | custom-call | tf_op jit(solution)/shard_map/own_projection/pallas_call | solution.py:296
  14.7 1.8 %collective-permute-done.3.refs_2_ = bf16[48,1152]{1,0:T(8,128)(2,1)S(1)} collective-permute-done((bf16[48,1152]{1,0:T(8,128)(2,1)}, bf16[48,1152]{1,0:T(8,128)(2,1)S(1)}, u32[]{:S(2)}, u32[]{:S(2)}) %collective-permute-start.3) | collective-permute-done | bytes 110624 | tf_op jit(solution)/shard_map/ppermute | solution.py:31
  16.5 0.9 %collective-permute-done.5.refs_3_ = bf16[48,1152]{1,0:T(8,128)(2,1)S(1)} collective-permute-done((bf16[48,1152]{1,0:T(8,128)(2,1)}, bf16[48,1152]{1,0:T(8,128)(2,1)S(1)}, u32[]{:S(2)}, u32[]{:S(2)}) %collective-permute-start.5) | collective-permute-done | bytes 110624 | tf_op jit(solution)/shard_map/ppermute | solution.py:31
  17.6 2.9 %pairs.1 = (bf16[384,1152]{1,0:T(8,128)(2,1)S(1)}, f32[1,384]{1,0:T(1,128)S(1)}, bf16[1152,384]{1,0:T(8,128)(2,1)S(1)}, bf16[192,384]{1,0:T(8,128)(2,1)S(1)}, f3...) custom-call(s32[1]{0:T(128)} %bitcast.member_ref, ...), custom_call_target="tpu_custom_call" | custom-call | tf_op jit(solution)/shard_map/pairs/pallas_call | solution.py:316
  21.0 0.5 %captions.1 = (bf16[1152,384]{1,0:T(8,128)(2,1)S(1)}, f32[48,1152]{1,0:T(8,128)S(1)}, bf16[48,1152]{1,0:T(8,128)(2,1)S(1)}, bf16[48,1152]{1,0:T(8,128)(2,1)S(1)}, bf16[48,1152]{1,0:T(8,128)(2,1)S(1)}) custom-call(bf16[192,384]{1,0:T(8,128)(2,1)S(1)} %get-tuple-element.40.grad_ref, bf16[1152,384]{1,0:T(8,128)(2,1)S(1)} %get-tuple-element.41.emb_ref, ...), custom_call_target="tpu_custom_call" | custom-call | tf_op jit(solution)/shard_map/captions/pallas_call | solution.py:339
  22.1 2.6 %collective-permute-start.10 = (bf16[160,384]{1,0:T(8,128)(2,1)S(1)}, bf16[160,384]{1,0:T(8,128)(2,1)S(1)}, u32[]{:S(2)}, u32[]{:S(2)}) collective-permute-start(bf16[160,384]{1,0:T(8,128)(2,1)S(1)} %get-tuple-element.51), channel_id=1, source_target_pairs={{0,6},{1,7},{2,4},{3,5},{4,2},{5,3},{6,0},{7,1},{8,14},{9,15},{10,... | collective-permute-start | bytes 368648 | tf_op jit(solution)/shard_map/ppermute | solution.py:31
  24.7 0.5 %collective-permute-start.9 = (bf16[160,384]{1,0:T(8,128)(2,1)S(1)}, bf16[160,384]{1,0:T(8,128)(2,1)S(1)}, u32[]{:S(2)}, u32[]{:S(2)}) collective-permute-start(bf16[160,384]{1,0:T(8,128)(2,1)S(1)} %get-tuple-element.50), channel_id=1, source_target_pairs={{0,4},{1,5},{2,6},{3,7},{4,0},{5,1},{6,2},{7,3},{8,12},{9,13},{10,... | collective-permute-start | bytes 368648 | tf_op jit(solution)/shard_map/ppermute | solution.py:31
  25.3 0.5 %collective-permute-start.11 = (bf16[160,384]{1,0:T(8,128)(2,1)S(1)}, bf16[160,384]{1,0:T(8,128)(2,1)S(1)}, u32[]{:S(2)}, u32[]{:S(2)}) collective-permute-start(bf16[160,384]{1,0:T(8,128)(2,1)S(1)} %get-tuple-element.52), channel_id=1, source_target_pairs={{0,2},{1,3},{2,0},{3,1},{4,6},{5,7},{6,4},{7,5},{8,10},{9,11},{10,... | collective-permute-start | bytes 368648 | tf_op jit(solution)/shard_map/ppermute | solution.py:31
  25.8 3.0 %collective-permute-start.12 = (bf16[48,1152]{1,0:T(8,128)(2,1)S(1)}, bf16[48,1152]{1,0:T(8,128)(2,1)S(1)}, u32[]{:S(2)}, u32[]{:S(2)}) collective-permute-start(bf16[48,1152]{1,0:T(8,128)(2,1)S(1)} %get-tuple-element.57), channel_id=1, source_target_pairs={{0,16},{1,17},{2,18},{3,19},{4,20},{5,21},{6,22},{7,23},{8,24},{9,... | collective-permute-start | bytes 331784 | tf_op jit(solution)/shard_map/ppermute | solution.py:31
  28.8 0.5 %collective-permute-start.13 = (bf16[48,1152]{1,0:T(8,128)(2,1)S(1)}, bf16[48,1152]{1,0:T(8,128)(2,1)S(1)}, u32[]{:S(2)}, u32[]{:S(2)}) collective-permute-start(bf16[48,1152]{1,0:T(8,128)(2,1)S(1)} %get-tuple-element.58), channel_id=1, source_target_pairs={{0,24},{1,25},{2,26},{3,27},{4,28},{5,29},{6,30},{7,31},{8,16},{9,... | collective-permute-start | bytes 331784 | tf_op jit(solution)/shard_map/ppermute | solution.py:31
  29.4 1.1 %collective-permute-start.14 = (bf16[48,1152]{1,0:T(8,128)(2,1)S(1)}, bf16[48,1152]{1,0:T(8,128)(2,1)S(1)}, u32[]{:S(2)}, u32[]{:S(2)}) collective-permute-start(bf16[48,1152]{1,0:T(8,128)(2,1)S(1)} %get-tuple-element.59), channel_id=1, source_target_pairs={{0,8},{1,9},{2,10},{3,11},{4,12},{5,13},{6,14},{7,15},{8,0},{9,1},... | collective-permute-start | bytes 331784 | tf_op jit(solution)/shard_map/ppermute | solution.py:31
  30.5 0.7 %collective-permute-done.9.refs_1_ = bf16[160,384]{1,0:T(8,128)(2,1)S(1)} collective-permute-done((bf16[160,384]{1,0:T(8,128)(2,1)S(1)}, bf16[160,384]{1,0:T(8,128)(2,1)S(1)}, u32[]{:S(2)}, u32[]{:S(2)}) %collective-permute-start.9) | collective-permute-done | bytes 122912 | tf_op jit(solution)/shard_map/ppermute | solution.py:31
  31.2 1.4 %weights.1 = (f32[1,384]{1,0:T(1,128)S(1)}, bf16[8,176,128]{2,1,0:T(8,128)(2,1)}) custom-call(f32[152,384]{1,0:T(8,128)S(1)} %far_sum.1.refs_0_, bf16[160,384]{1,0:T(8,128)(2,1)S(1)} %collective-permute-done.11.refs_1_, f32[1,384]{1,0:T(1,128)S(1)} %get-tuple-element.53.refs_2_, bf16[384,1152]{1,0:T(8,128)(2,1)S(1)} %get-tuple-element.42.feats_ref.refs_3_, ...), custom_call_target="tpu_custom_call" | custom-call | tf_op jit(solution)/shard_map/weights/pallas_call | solution.py:386
  32.6 5.2 %all-to-all-start = ((bf16[8,176,128]{2,1,0:T(8,128)(2,1)}), bf16[8,176,128]{2,1,0:T(8,128)(2,1)S(1)}, u32[]{:S(2)}, u32[]{:S(2)}) async-start(bf16[8,176,128]{2,1,0:T(8,128)(2,1)} %get-tuple-element.60), calls=%async_computation | async-start | bytes 720896 | tf_op jit(solution)/shard_map/all_to_all | solution.py:397
  37.9 0.7 %caption_total.1 = f32[48,1152]{1,0:T(8,128)} custom-call(f32[48,1152]{1,0:T(8,128)S(1)} %get-tuple-element.56.refs_0_, bf16[48,1152]{1,0:T(8,128)(2,1)S(1)} %collective-permute-done.12.refs_1_, bf16[48,1152]{1,0:T(8,128)(2,1)S(1)} %collective-permute-done.13.refs_2_, bf16[48,1152]{1,0:T(8,128)(2,1)S(1)} %collective-permute-done.14.refs_3_), custom_call_target="tpu_custom_call" | custom-call | flops 5000000000 | tf_op jit(solution)/shard_map/caption_total/pallas_call | solution.py:428
  38.6 0.6 %dynamic-slice_bitcast_fusion = f32[48]{0:T(128)} fusion(f32[1,384]{1,0:T(1,128)S(1)} %get-tuple-element.55, s32[]{:T(128)S(6)} %select_n.16), kind=kLoop, calls=%fused_computation | loop fusion | bytes 388 | tf_op jit(solution)/shard_map/dynamic_slice | solution.py:437
  39.2 9.1 %all-to-all-done.got_ref = bf16[8,176,128]{2,1,0:T(8,128)(2,1)S(1)} async-done(((bf16[8,176,128]{2,1,0:T(8,128)(2,1)}), bf16[8,176,128]{2,1,0:T(8,128)(2,1)S(1)}, u32[]{:S(2)}, u32[]{:S(2)}) %all-to-all-start) | async-done | bytes 360480 | tf_op jit(solution)/shard_map/all_to_all | solution.py:397
  48.3 0.9 %weight_total.1 = f32[144,288]{1,0:T(8,128)} custom-call(bf16[8,176,128]{2,1,0:T(8,128)(2,1)S(1)} %all-to-all-done.got_ref), custom_call_target="tpu_custom_call" | custom-call | tf_op jit(solution)/shard_map/weight_total/pallas_call | solution.py:398
  (27 shorter events, 2.0 us)
Async XLA Ops:
  0.6 10.2 %collective-permute-start = (bf16[48,1152]{1,0:T(8,128)(2,1)}, bf16[48,1152]{1,0:T(8,128)(2,1)S(1)}, u32[]{:S(2)}, u32[]{:S(2)}) collective-permute-start(bf16[48,1152]{1,0:T(8,128)(2,1)} %refs_0_.1), channel_id=1, source_target_pairs={{0,2},{1,3},{2,0},{3,1},{4,6},{5,7},{6,4},{7,5},{8,10},{9,11},{10,... | collective-permute-start | bytes 331784 | tf_op jit(solution)/shard_map/ppermute | solution.py:31
  3.7 8.6 %collective-permute-start.1 = (bf16[48,1152]{1,0:T(8,128)(2,1)}, bf16[48,1152]{1,0:T(8,128)(2,1)S(1)}, u32[]{:S(2)}, u32[]{:S(2)}) collective-permute-start(bf16[48,1152]{1,0:T(8,128)(2,1)} %refs_0_.1), channel_id=1, source_target_pairs={{0,4},{1,5},{2,6},{3,7},{4,0},{5,1},{6,2},{7,3},{8,12},{9,13},{10,... | collective-permute-start | bytes 331784 | tf_op jit(solution)/shard_map/ppermute | solution.py:31
  5.2 7.1 %collective-permute-start.2 = (bf16[48,1152]{1,0:T(8,128)(2,1)}, bf16[48,1152]{1,0:T(8,128)(2,1)S(1)}, u32[]{:S(2)}, u32[]{:S(2)}) collective-permute-start(bf16[48,1152]{1,0:T(8,128)(2,1)} %refs_0_.1), channel_id=1, source_target_pairs={{0,6},{1,7},{2,4},{3,5},{4,2},{5,3},{6,0},{7,1},{8,14},{9,15},{10,... | collective-permute-start | bytes 331784 | tf_op jit(solution)/shard_map/ppermute | solution.py:31
  5.2 11.3 %collective-permute-start.3 = (bf16[48,1152]{1,0:T(8,128)(2,1)}, bf16[48,1152]{1,0:T(8,128)(2,1)S(1)}, u32[]{:S(2)}, u32[]{:S(2)}) collective-permute-start(bf16[48,1152]{1,0:T(8,128)(2,1)} %text_ref.1), channel_id=1, source_target_pairs={{0,16},{1,17},{2,18},{3,19},{4,20},{5,21},{6,22},{7,23},{8,24},{9,... | collective-permute-start | bytes 331784 | tf_op jit(solution)/shard_map/ppermute | solution.py:31
  8.2 8.2 %collective-permute-start.4 = (bf16[48,1152]{1,0:T(8,128)(2,1)}, bf16[48,1152]{1,0:T(8,128)(2,1)S(1)}, u32[]{:S(2)}, u32[]{:S(2)}) collective-permute-start(bf16[48,1152]{1,0:T(8,128)(2,1)} %text_ref.1), channel_id=1, source_target_pairs={{0,24},{1,25},{2,26},{3,27},{4,28},{5,29},{6,30},{7,31},{8,16},{9,... | collective-permute-start | bytes 331784 | tf_op jit(solution)/shard_map/ppermute | solution.py:31
  10.9 1.4 %copy-start.1 = (bf16[48,1152]{1,0:T(8,128)(2,1)S(1)}, bf16[48,1152]{1,0:T(8,128)(2,1)}, u32[]{:S(2)}) copy-start(bf16[48,1152]{1,0:T(8,128)(2,1)} %refs_0_.1) | copy-start | bytes 331780
  10.9 6.5 %collective-permute-start.5 = (bf16[48,1152]{1,0:T(8,128)(2,1)}, bf16[48,1152]{1,0:T(8,128)(2,1)S(1)}, u32[]{:S(2)}, u32[]{:S(2)}) collective-permute-start(bf16[48,1152]{1,0:T(8,128)(2,1)} %text_ref.1), channel_id=1, source_target_pairs={{0,8},{1,9},{2,10},{3,11},{4,12},{5,13},{6,14},{7,15},{8,0},{9,1},... | collective-permute-start | bytes 331784 | tf_op jit(solution)/shard_map/ppermute | solution.py:31
  11.2 0.9 %copy-start.2 = (bf16[48,1152]{1,0:T(8,128)(2,1)S(1)}, bf16[48,1152]{1,0:T(8,128)(2,1)}, u32[]{:S(2)}) copy-start(bf16[48,1152]{1,0:T(8,128)(2,1)} %text_ref.1) | copy-start | bytes 331780
  12.1 1.7 %copy-start = (bf16[1152,1152]{1,0:T(8,128)(2,1)S(1)}, bf16[1152,1152]{1,0:T(8,128)(2,1)}, u32[]{:S(2)}) copy-start(bf16[1152,1152]{1,0:T(8,128)(2,1)} %weight.1) | copy-start | bytes 7962628
  12.3 5.2 %collective-permute-start.6 = (bf16[192,1152]{1,0:T(8,128)(2,1)S(1)}, bf16[192,1152]{1,0:T(8,128)(2,1)S(1)}, u32[]{:S(2)}, u32[]{:S(2)}) collective-permute-start(bf16[192,1152]{1,0:T(8,128)(2,1)S(1)} %stack.1.feats_ref.own_half), channel_id=1, source_target_pairs={{0,1},{1,0},{2,3},{3,2},{4,5},{5,4},{6,7},{7,6},{8,9},{9,8},{10,11... | collective-permute-start | bytes 1327112 | tf_op jit(solution)/shard_map/ppermute | solution.py:31
  20.5 1.6 %collective-permute-start.7 = (bf16[2,160,384]{2,1,0:T(8,128)(2,1)S(1)}, bf16[2,160,384]{2,1,0:T(8,128)(2,1)S(1)}, u32[]{:S(2)}, u32[]{:S(2)}) collective-permute-start(bf16[2,160,384]{2,1,0:T(8,128)(2,1)S(1)} %get-tuple-element.39), channel_id=1, source_target_pairs={{0,1},{1,0},{2,3},{3,2},{4,5},{5,4},{6,7},{7,6},{8,9},{9,8},{10,11... | collective-permute-start | bytes 737288 | tf_op jit(solution)/shard_map/ppermute | solution.py:31
  20.5 4.7 %collective-permute-start.8 = (bf16[2,160,384]{2,1,0:T(8,128)(2,1)S(1)}, bf16[2,160,384]{2,1,0:T(8,128)(2,1)S(1)}, u32[]{:S(2)}, u32[]{:S(2)}) collective-permute-start(bf16[2,160,384]{2,1,0:T(8,128)(2,1)S(1)} %get-tuple-element.47), channel_id=1, source_target_pairs={{0,1},{1,0},{2,3},{3,2},{4,5},{5,4},{6,7},{7,6},{8,9},{9,8},{10,11... | collective-permute-start | bytes 737288 | tf_op jit(solution)/shard_map/ppermute | solution.py:31
  22.1 7.3 %collective-permute-start.10 = (bf16[160,384]{1,0:T(8,128)(2,1)S(1)}, bf16[160,384]{1,0:T(8,128)(2,1)S(1)}, u32[]{:S(2)}, u32[]{:S(2)}) collective-permute-start(bf16[160,384]{1,0:T(8,128)(2,1)S(1)} %get-tuple-element.51), channel_id=1, source_target_pairs={{0,6},{1,7},{2,4},{3,5},{4,2},{5,3},{6,0},{7,1},{8,14},{9,15},{10,... | collective-permute-start | bytes 368648 | tf_op jit(solution)/shard_map/ppermute | solution.py:31
  24.7 6.5 %collective-permute-start.9 = (bf16[160,384]{1,0:T(8,128)(2,1)S(1)}, bf16[160,384]{1,0:T(8,128)(2,1)S(1)}, u32[]{:S(2)}, u32[]{:S(2)}) collective-permute-start(bf16[160,384]{1,0:T(8,128)(2,1)S(1)} %get-tuple-element.50), channel_id=1, source_target_pairs={{0,4},{1,5},{2,6},{3,7},{4,0},{5,1},{6,2},{7,3},{8,12},{9,13},{10,... | collective-permute-start | bytes 368648 | tf_op jit(solution)/shard_map/ppermute | solution.py:31
  25.3 6.0 %collective-permute-start.11 = (bf16[160,384]{1,0:T(8,128)(2,1)S(1)}, bf16[160,384]{1,0:T(8,128)(2,1)S(1)}, u32[]{:S(2)}, u32[]{:S(2)}) collective-permute-start(bf16[160,384]{1,0:T(8,128)(2,1)S(1)} %get-tuple-element.52), channel_id=1, source_target_pairs={{0,2},{1,3},{2,0},{3,1},{4,6},{5,7},{6,4},{7,5},{8,10},{9,11},{10,... | collective-permute-start | bytes 368648 | tf_op jit(solution)/shard_map/ppermute | solution.py:31
  25.8 12.1 %collective-permute-start.12 = (bf16[48,1152]{1,0:T(8,128)(2,1)S(1)}, bf16[48,1152]{1,0:T(8,128)(2,1)S(1)}, u32[]{:S(2)}, u32[]{:S(2)}) collective-permute-start(bf16[48,1152]{1,0:T(8,128)(2,1)S(1)} %get-tuple-element.57), channel_id=1, source_target_pairs={{0,16},{1,17},{2,18},{3,19},{4,20},{5,21},{6,22},{7,23},{8,24},{9,... | collective-permute-start | bytes 331784 | tf_op jit(solution)/shard_map/ppermute | solution.py:31
  28.8 9.0 %collective-permute-start.13 = (bf16[48,1152]{1,0:T(8,128)(2,1)S(1)}, bf16[48,1152]{1,0:T(8,128)(2,1)S(1)}, u32[]{:S(2)}, u32[]{:S(2)}) collective-permute-start(bf16[48,1152]{1,0:T(8,128)(2,1)S(1)} %get-tuple-element.58), channel_id=1, source_target_pairs={{0,24},{1,25},{2,26},{3,27},{4,28},{5,29},{6,30},{7,31},{8,16},{9,... | collective-permute-start | bytes 331784 | tf_op jit(solution)/shard_map/ppermute | solution.py:31
  29.4 8.5 %collective-permute-start.14 = (bf16[48,1152]{1,0:T(8,128)(2,1)S(1)}, bf16[48,1152]{1,0:T(8,128)(2,1)S(1)}, u32[]{:S(2)}, u32[]{:S(2)}) collective-permute-start(bf16[48,1152]{1,0:T(8,128)(2,1)S(1)} %get-tuple-element.59), channel_id=1, source_target_pairs={{0,8},{1,9},{2,10},{3,11},{4,12},{5,13},{6,14},{7,15},{8,0},{9,1},... | collective-permute-start | bytes 331784 | tf_op jit(solution)/shard_map/ppermute | solution.py:31
  32.6 15.7 %all-to-all-start = ((bf16[8,176,128]{2,1,0:T(8,128)(2,1)}), bf16[8,176,128]{2,1,0:T(8,128)(2,1)S(1)}, u32[]{:S(2)}, u32[]{:S(2)}) async-start(bf16[8,176,128]{2,1,0:T(8,128)(2,1)} %get-tuple-element.60), calls=%async_computation | async-start | bytes 720896 | tf_op jit(solution)/shard_map/all_to_all | solution.py:397
